TPU v7x, 32 devices: a whole 2x2x4 slice. The times are simulated.
32 devices in a mesh: replica: 8 (over y, x, core), tensor: 4 (over z).
Axes of the slice: x: 2, y: 2, z: 4, core: 2. Of those that a mesh axis runs over, the one named last changes fastest.
Arguments:
- projection_inputs: bfloat16 [1024, 5120], P('replica', 'tensor'), may hold values from -6 to 6
- switch_logits_raw: bfloat16 [1024, 256], P('replica', 'tensor'), may hold values from -6 to 6
- inner_neuron_slope: bfloat16 [1024, 256], P('replica', 'tensor'), may hold values from -0.59765625 to 0.59765625
- expansion_matrix: bfloat16 [256, 5120], P('tensor'), may hold values from -3 to 3
- velocity_buffer: float32 [8, 256, 5120], P('replica', 'tensor'), may hold values from -6 to 6
- sent_spectral_lines: int32 [8, 4, 80, 8], P('replica', 'tensor'), may hold values from 0 to 63, as said below
- participant_mask: int32 [8], replicated, may hold values from 0 to 1, as said below
- token_tallies: int32 [8], replicated, may hold values from 64 to 256
Outputs:
- input_grad: bfloat16 [1024, 5120], P('replica', 'tensor')
- new_momentum: float32 [8, 256, 5120], P('replica', 'tensor')
- update: float32 [256, 5120], P('tensor')
Inputs may be any that keep to these rules, and one draw needn't show every extreme that they name: `sent_spectral_lines`: the 8 rows of one replica and block are distinct. `participant_mask`: at least one replica survives.
All inputs are finite; a program needn't handle non-finite values.
Results may differ from a plain program's by a relative error of at most 0.005.
Values may be sent and summed in bfloat16 or wider, within the bound.
No kernel may reach another device: no remote copies, remote signals or barrier semaphores. Data moves between devices by JAX's collectives and lax.ppermute only.
A program may use at most 64 MiB of HBM per device.

v0:
```python
import jax
import jax.numpy as jnp
from jax import lax
from jax.sharding import PartitionSpec as P

momentum_decay = 0.9


def cosine_table():
    freqs = jnp.arange(64, dtype=jnp.float32)[:, None]
    places = jnp.arange(64, dtype=jnp.float32)[None, :]
    cosines = jnp.cos(jnp.pi * (places + 0.5) * freqs / 64.0) * jnp.sqrt(2.0 / 64.0)
    return cosines.at[0].multiply(jnp.sqrt(0.5))


def per_device(
    projection_inputs,
    switch_logits_raw,
    inner_neuron_slope,
    expansion_matrix,
    velocity_buffer,
    sent_spectral_lines,
    participant_mask,
    token_tallies,
):
    highest = lax.Precision.HIGHEST
    up_grad = (
        inner_neuron_slope.astype(jnp.float32) * jax.nn.silu(switch_logits_raw.astype(jnp.float32))
    ).astype(jnp.bfloat16)
    partial_terms = jnp.dot(up_grad, expansion_matrix, preferred_element_type=jnp.float32)
    input_grad = lax.psum_scatter(partial_terms, "tensor", scatter_dimension=1, tiled=True).astype(
        jnp.bfloat16
    )
    grad_w = lax.dot_general(
        up_grad,
        lax.all_gather(projection_inputs, "tensor", axis=1, tiled=True),
        (((0,), (0,)), ((), ())),
        preferred_element_type=jnp.float32,
    )
    row_total_count = expansion_matrix.shape[0] // 64
    col_count = expansion_matrix.shape[1] // 64
    moment = momentum_decay * velocity_buffer[0] + grad_w
    cosines = cosine_table()
    blocks = moment.reshape(row_total_count, 64, col_count, 64).transpose(0, 2, 1, 3)
    coefficients = jnp.einsum("fa,ijab,gb->ijfg", cosines, blocks, cosines, precision=highest)
    freq_ids = jnp.arange(64, dtype=jnp.int32)
    own_rows = sent_spectral_lines[0]
    chosen = (own_rows[..., None] == freq_ids).astype(jnp.float32)
    shipped = jnp.einsum("ijkf,ijfg->ijkg", chosen, coefficients, precision=highest).astype(
        jnp.bfloat16
    )
    spectrum = jnp.einsum("ijkf,ijkg->ijfg", chosen, shipped.astype(jnp.float32), precision=highest)
    returned = jnp.einsum("fa,ijfg,gb->ijab", cosines, spectrum, cosines, precision=highest)
    new_moment = moment - returned.transpose(0, 2, 1, 3).reshape(moment.shape)
    worker_burdens = participant_mask.astype(jnp.float32) * token_tallies.astype(jnp.float32)
    worker_fractions = worker_burdens * (
        jnp.sum(participant_mask.astype(jnp.float32)) / jnp.sum(worker_burdens)
    )
    myself = lax.axis_index("replica")
    combined = lax.psum(worker_fractions[myself] * spectrum, "replica")
    update = jnp.einsum("fa,ijfg,gb->ijab", cosines, combined, cosines, precision=highest)
    update = update.transpose(0, 2, 1, 3).reshape(moment.shape)
    return (input_grad, new_moment[None], update)


def solution(mesh):
    return jax.shard_map(
        per_device,
        mesh=mesh,
        in_specs=(
            P("replica", "tensor"),
            P("replica", "tensor"),
            P("replica", "tensor"),
            P("tensor", None),
            P("replica", "tensor", None),
            P("replica", "tensor", None, None),
            P(),
            P(),
        ),
        out_specs=(P("replica", "tensor"), P("replica", "tensor", None), P("tensor", None)),
        check_vma=False,
    )
```

profile of v0, /device:TPU:0, one launch (start us, length us, event | category | flops | bytes accessed | tf_op | source)
XLA Modules:
  0.0 191.7 jit_solution(14874963681324859862)
XLA Ops:
  7.2 0.0 copy-start
  7.2 0.0 all-gather.2.cloned.1.call-start
  7.2 0.7 all-gather.2.cloned.1.call-update
  7.9 0.0 all-reduce.2.cloned.1.call-start
  8.0 0.8 copy.13
  8.8 0.2 cosine_multiply_fusion
  9.0 0.2 scatter-mul.4
  9.1 1.3 fusion.19
  11.8 0.7 broadcast_multiply_fusion.1
  12.4 0.6 dynamic_slice.3
  13.0 32.0 %all-gather.2.cloned.1.call-done = bf16[128,5120]{1,0:T(8,128)(2,1)} async-done(((bf16[128,1280]{1,0:T(8,128)(2,1)}), bf16[128,5120]{1,0:T(8,128)(2,1)}) %all-gather.2.cloned.1.call-update) | async-done | bytes 1310736 | tf_op jit(solution)/shard_map/all_gather | solution.py:36
  45.0 2.1 %convolution_add_fusion = f32[64,5120]{1,0:T(8,128)S(1)} fusion(bf16[128,5120]{1,0:T(8,128)(2,1)} %all-gather.2.cloned.1.call-done, f32[1,64,5120]{2,1,0:T(8,128)} %param.14, bf16[128,64]{0,1:T(8,128)(2,1)} %param.11, bf16[128,64]{0,1:T(8,128)(2,1)} %param.12), kind=kOutput, calls=%fused_computation | convolution fusion | flops 84606976 | bytes 3964928 | tf_op jit(solution)/shard_map/dot_general | solution.py:34
  47.1 2.2 %reshape.81 = f32[1,64,80,64]{3,2,1,0:T(8,128)} reshape(f32[64,5120]{1,0:T(8,128)S(1)} %convolution_add_fusion) | data formatting | bytes 2621440 | tf_op jit(solution)/shard_map/reshape | solution.py:44
  49.3 6.4 %fusion = f32[80,64,64]{2,1,0:T(8,128)S(1)} fusion(f32[80,64,64]{2,0,1:T(8,128)} %bitcast.43, f32[64,64]{0,1:T(8,128)S(1)} %scatter-mul.4), kind=kOutput, calls=%fused_computation.1 | convolution fusion | flops 251658240 | bytes 2637824 | tf_op jit(solution)/shard_map/fa,ijab,gb->ijfg/dot_general | solution.py:45
  55.7 4.2 %fusion.15 = f32[80,64,64]{2,1,0:T(8,128)S(1)} fusion(f32[80,64,64]{2,1,0:T(8,128)S(1)} %fusion, f32[64,64]{0,1:T(8,128)S(1)} %scatter-mul.4), kind=kOutput, calls=%fused_computation.25 | convolution fusion | flops 251658240 | bytes 2637824 | tf_op jit(solution)/shard_map/fa,ijab,gb->ijfg/dot_general | solution.py:45
  60.0 1.4 convolution_convert_fusion
  61.3 4.1 %broadcast_multiply_fusion = (f32[80,64,64]{2,1,0:T(8,128)}, f32[80,64,64]{2,1,0:T(8,128)}) fusion(f32[]{:T(128)} %bitcast.8, bf16[80,8,64]{2,1,0:T(8,128)(2,1)S(1)} %convolution_convert_fusion, s32[80,8]{1,0:T(8,128)S(1)} %copy.13), kind=kOutput, calls=%fused_computation.5 | convolution fusion | flops 5611520 | bytes 2705924 | tf_op jit(solution)/shard_map/ijkf,ijkg->ijfg/dot_general | solution.py:52
  65.5 0.0 copy-start.1
  65.5 0.0 copy-start.2
  65.5 0.0 all-reduce.2.cloned.1.call-update
  65.5 0.0 reduce-scatter.2.cloned.1.call-start
  65.6 0.0 copy-done
  65.6 0.6 copy-done.1
  66.2 0.0 copy-done.2
  66.2 2.0 %fusion.21 = f32[128,5120]{1,0:T(8,128)} fusion(bf16[64,5120]{1,0:T(8,128)(2,1)S(1)} %copy-done, bf16[128,64]{0,1:T(8,128)(2,1)S(1)} %copy-done.1, bf16[128,64]{0,1:T(8,128)(2,1)S(1)} %copy-done.2), kind=kOutput, calls=%fused_computation.35 | convolution fusion | flops 83951616 | bytes 3309568 | tf_op jit(solution)/shard_map/dot_general | solution.py:30
  68.3 0.0 reduce-scatter.2.cloned.1.call-update
  68.3 7.5 %fusion.13 = f32[80,64,64]{2,1,0:T(8,128)} fusion(f32[80,64,64]{2,1,0:T(8,128)} %get-tuple-element.18, f32[64,64]{0,1:T(8,128)S(1)} %scatter-mul.4), kind=kOutput, calls=%fused_computation.23 | convolution fusion | flops 251658240 | bytes 2637824 | tf_op jit(solution)/shard_map/fa,ijfg,gb->ijab/dot_general | solution.py:53
  75.8 4.4 %copy.17 = f32[80,64,64]{0,1,2:T(8,128)} copy(f32[80,64,64]{2,1,0:T(8,128)} %fusion.13) | data formatting | bytes 2621440 | tf_op jit(solution)/shard_map/fa,ijfg,gb->ijab/dot_general | solution.py:53
  80.2 4.9 %convolution_bitcast_fusion.1 = f32[1,64,80,64]{2,3,1,0:T(8,128)} fusion(f32[80,64,64]{0,1,2:T(8,128)} %copy.17, f32[64,64]{0,1:T(8,128)S(1)} %scatter-mul.4), kind=kOutput, calls=%fused_computation.4 | convolution fusion | flops 251658240 | bytes 2637824 | tf_op jit(solution)/shard_map/fa,ijfg,gb->ijab/dot_general | solution.py:53
  85.1 3.2 %copy.14 = f32[1,64,80,64]{3,2,1,0:T(8,128)} copy(f32[1,64,80,64]{2,3,1,0:T(8,128)} %convolution_bitcast_fusion.1) | data formatting | bytes 2621440 | tf_op jit(solution)/shard_map/transpose | solution.py:54
  88.3 2.3 %reshape.83 = f32[64,5120]{1,0:T(8,128)S(1)} reshape(f32[1,64,80,64]{3,2,1,0:T(8,128)} %copy.14) | data formatting | bytes 2621440 | tf_op jit(solution)/shard_map/reshape | solution.py:54
  90.6 1.2 subtract_bitcast_fusion
  91.8 37.4 %all-reduce.2.cloned.1.call-done = f32[80,64,64]{2,1,0:T(8,128)} async-done(((f32[80,64,64]{2,1,0:T(8,128)}), f32[80,64,64]{2,1,0:T(8,128)}) %all-reduce.2.cloned.1.call-update) | async-done | bytes 1310736 | tf_op jit(solution)/shard_map/psum | solution.py:60
  129.2 6.0 %fusion.10 = f32[80,64,64]{2,1,0:T(8,128)S(1)} fusion(f32[80,64,64]{2,1,0:T(8,128)} %all-reduce.2.cloned.1.call-done, f32[64,64]{0,1:T(8,128)S(1)} %scatter-mul.4), kind=kOutput, calls=%fused_computation.20 | convolution fusion | flops 251658240 | bytes 2637824 | tf_op jit(solution)/shard_map/fa,ijfg,gb->ijab/dot_general | solution.py:61
  135.2 3.2 %copy.18 = f32[80,64,64]{0,1,2:T(8,128)} copy(f32[80,64,64]{2,1,0:T(8,128)S(1)} %fusion.10) | data formatting | bytes 2621440 | tf_op jit(solution)/shard_map/fa,ijfg,gb->ijab/dot_general | solution.py:61
  138.4 4.9 %convolution_bitcast_fusion = f32[1,64,80,64]{2,3,1,0:T(8,128)} fusion(f32[80,64,64]{0,1,2:T(8,128)} %copy.18, f32[64,64]{0,1:T(8,128)S(1)} %scatter-mul.4), kind=kOutput, calls=%fused_computation.3 | convolution fusion | flops 251658240 | bytes 2637824 | tf_op jit(solution)/shard_map/fa,ijfg,gb->ijab/dot_general | solution.py:61
  143.4 2.1 %copy.15 = f32[1,64,80,64]{3,2,1,0:T(8,128)S(1)} copy(f32[1,64,80,64]{2,3,1,0:T(8,128)} %convolution_bitcast_fusion) | data formatting | bytes 2621440 | tf_op jit(solution)/shard_map/transpose | solution.py:62
  145.5 1.7 reshape.85
  147.2 36.0 %reduce-scatter.2.cloned.1.call-done = f32[128,1280]{1,0:T(8,128)} async-done(((f32[128,5120]{1,0:T(8,128)}), f32[128,1280]{1,0:T(8,128)}) %reduce-scatter.2.cloned.1.call-update) | async-done | bytes 655376 | tf_op jit(solution)/shard_map/reduce_scatter | solution.py:31
  183.3 1.8 convert_element_type.28
  (2 shorter events, 0.0 us)
Async XLA Ops:
  7.2 58.4 %copy-start = (bf16[64,5120]{1,0:T(8,128)(2,1)S(1)}, bf16[64,5120]{1,0:T(8,128)(2,1)}, u32[]{:S(2)}) copy-start(bf16[64,5120]{1,0:T(8,128)(2,1)} %param.13) | copy-start | bytes 1966084
  7.2 37.8 %all-gather.2.cloned.1.call-start = ((), (), s32[]{:S(2)}) async-start(), calls=%async_computation.2 | async-start | bytes 1638400 | tf_op jit(solution)/shard_map/all_gather | solution.py:36
  7.9 121.3 %all-reduce.2.cloned.1.call-start = ((), (), s32[]{:S(2)}) async-start(), calls=%async_computation.3 | async-start | bytes 5242880 | tf_op jit(solution)/shard_map/psum | solution.py:60
  65.5 0.7 copy-start.1
  65.5 0.7 copy-start.2
  65.5 117.8 %reduce-scatter.2.cloned.1.call-start = ((), (), s32[]{:S(2)}) async-start(), calls=%async_computation.1 | async-start | bytes 3276800 | tf_op jit(solution)/shard_map/reduce_scatter | solution.py:31
Sparse Core Ops, SparseCore 0:
  9.6 35.3 all-gather.1
  65.6 63.5 all-reduce.1
  131.5 51.7 reduce-scatter.1
where the time goes:
time: 192 us
  waiting for transfers between devices  106 us (55%)
  matrix products  43.6 us (23%)
  local copies, waits for them, and re-layouts  21.4 us (11%)
  between operations  15.2 us (8%)
  other arithmetic  5.2 us (3%)
    psum x1, waiting for transfers between devices, per_device(): combined = lax.psum(worker_fractions[myself] * spectrum, 'replica')  37.4 us
    reduce_scatter x1, waiting for transfers between devices, per_device(): lax.psum_scatter(partial_terms, 'tensor', scatter_dimension=1, tiled=True)  36 us
    all_gather x1, waiting for transfers between devices, per_device(): lax.all_gather(projection_inputs, 'tensor', axis=1, tiled=True)  32 us
    dot_general x2, matrix products, per_device(): jnp.einsum('fa,ijfg,gb->ijab', cosines, spectrum, cosines, precision=high...  12.4 us
    dot_general x2, matrix products, per_device(): jnp.einsum('fa,ijfg,gb->ijab', cosines, combined, cosines, precision=high...  10.9 us
    dot_general x2, matrix products, per_device(): jnp.einsum('fa,ijab,gb->ijfg', cosines, blocks, cosines, precision=highest)  10.6 us
    dot_general x1, local copies, waits for them, and re-layouts, per_device(): jnp.einsum('fa,ijfg,gb->ijab', cosines, spectrum, cosines, precision=high...  4.4 us
    dot_general x1, matrix products, per_device(): jnp.einsum('ijkf,ijkg->ijfg', chosen, shipped.astype(jnp.float32), precis...  4.15 us
  transfers between devices with their start and end apart: 3, of which 3 were waited for; matrix products, arithmetic and copies ran while one was open for 25% of the time, Pallas kernels for 0%

commit v1 on v0

--- a/solution.py
+++ b/solution.py
@@ -1,9 +1,22 @@
+import functools
+
 import jax
 import jax.numpy as jnp
+import numpy as np
 from jax import lax
+from jax.experimental import pallas as pl
+from jax.experimental.pallas import tpu as pltpu
 from jax.sharding import PartitionSpec as P
 
 momentum_decay = 0.9
+B = 64
+G = 256
+F32 = jnp.float32
+BF16 = jnp.bfloat16
+VMEM_LIMIT = 48 * 1024 * 1024
+
+VM = pl.BlockSpec(memory_space=pltpu.VMEM)
+SM = pl.BlockSpec(memory_space=pltpu.SMEM)
 
 
 def cosine_table():
@@ -13,7 +26,280 @@
     return cosines.at[0].multiply(jnp.sqrt(0.5))
 
 
-def per_device(
+def cosine_np():
+    f = np.arange(B)[:, None]
+    a = np.arange(B)[None, :]
+    c = np.cos(np.pi * (a + 0.5) * f / B) * np.sqrt(2.0 / B)
+    c[0] *= np.sqrt(0.5)
+    return c
+
+
+def halves(c):
+    hi = np.asarray(c, dtype=np.float32).astype(jnp.bfloat16)
+    lo = (np.asarray(c, np.float64) - hi.astype(np.float64)).astype(np.float32).astype(jnp.bfloat16)
+    return hi, lo
+
+
+def constants():
+    c = cosine_np()
+    hi, lo = halves(c)
+    stack = lambda h, l: np.block([[h, h], [l, l]])
+    left = stack(hi, lo)
+    left_t = stack(hi.T, lo.T)
+    eye = np.eye(G // B)
+    fwd = np.stack([np.kron(eye, np.asarray(x.T, np.float32)).astype(jnp.bfloat16) for x in (hi, lo)])
+    inv = np.stack([np.kron(eye, np.asarray(x, np.float32)).astype(jnp.bfloat16) for x in (hi, lo)])
+    tall = np.concatenate([hi.T, lo.T], axis=0)
+    return [jnp.asarray(x) for x in (left, left_t, fwd, inv, tall)]
+
+
+def dot(a, b):
+    return jnp.dot(a, b, preferred_element_type=F32)
+
+
+def split(x):
+    hi = x.astype(BF16)
+    return hi, (x - hi.astype(F32)).astype(BF16)
+
+
+def left_mul(stacked, x):
+    hi, lo = split(x)
+    y = dot(stacked, jnp.concatenate([hi, lo], axis=0))
+    return y[:B] + y[B:]
+
+
+def call(body, out_shape, ins, in_specs, out_specs, scratch=(), flops=0, nbytes=0, name=None):
+    return pl.pallas_call(
+        body,
+        out_shape=out_shape,
+        in_specs=in_specs,
+        out_specs=out_specs,
+        scratch_shapes=scratch,
+        compiler_params=pltpu.CompilerParams(vmem_limit_bytes=VMEM_LIMIT),
+        cost_estimate=pl.CostEstimate(flops=flops, bytes_accessed=nbytes, transcendentals=0),
+        name=name,
+    )(*ins)
+
+
+def cut_body(n_t, rp, cp, cols, pos, exp_ref, *outs):
+    rep, ten = pos[0], pos[1]
+    nr, nc = B // rp, cols // cp
+    r0 = pl.multiple_of((rep // cp) * nr, nr)
+    for k in range(n_t):
+        dest = lax.rem(ten + k, n_t)
+        c0 = pl.multiple_of(dest * cols + lax.rem(rep, cp) * nc, 128)
+        outs[k][...] = exp_ref[pl.ds(r0, nr), pl.ds(c0, nc)]
+
+
+def grads_body(n_t, *refs):
+    ups, act, outs = refs[:n_t], refs[n_t], refs[n_t + 1 :]
+    up = jnp.concatenate([u[...] for u in ups], axis=0)
+    cols = act.shape[1]
+    for c in range(0, cols, G):
+        g = dot(up, act[:, c : c + G])
+        for k in range(n_t):
+            outs[k][:, c : c + G] = g[k * B : (k + 1) * B].astype(outs[k].dtype)
+
+
+def moment_body(n_t, pos, vel, idx, left, left_t, fwd, inv, *refs):
+    grads, (new_ref, ship_ref) = refs[:n_t], refs[n_t:]
+    ten = pos[1]
+    cols = grads[0].shape[1]
+    keep = idx.shape[0]
+    ng = cols // G
+    blocks = idx.shape[1]
+    idx_f = idx[...].astype(F32).astype(BF16)
+    for k in range(n_t):
+        c0 = pl.multiple_of(lax.rem(ten + k, n_t) * cols, 128)
+        block = lax.broadcasted_iota(jnp.int32, (blocks, cols), 0)
+        lane = lax.broadcasted_iota(jnp.int32, (blocks, cols), 1) + c0
+        spread = jnp.where(lane // B == block, 1.0, 0.0).astype(BF16)
+        rows = dot(idx_f, spread).astype(jnp.int32)
+        moments = momentum_decay * vel[:, pl.ds(c0, cols)] + grads[k][...].astype(F32)
+        sel = []
+        for g in range(ng):
+            coef = left_mul(left[...], moments[:, g * G : (g + 1) * G])
+            num = rows[:, g * G : (g + 1) * G]
+            got = jnp.zeros((keep, G), F32)
+            for f in range(B):
+                got = jnp.where(num == f, coef[f : f + 1], got)
+            sel.append(got)
+        sel = jnp.concatenate(sel, axis=0)
+        hi, lo = split(sel)
+        n = ng * keep
+        y = dot(jnp.concatenate([hi, lo], axis=0), fwd[0])
+        ship = (y[:n] + y[n:] + dot(hi, fwd[1])).astype(BF16)
+        q = dot(ship, inv[0]) + dot(ship, inv[1])
+        shipf = ship.astype(F32)
+        freq = lax.broadcasted_iota(jnp.int32, (B, G), 0)
+        ship_ref[:, pl.ds(c0, cols)] = jnp.concatenate(
+            [shipf[g * keep : (g + 1) * keep] for g in range(ng)], axis=1
+        ).astype(BF16)
+        for g in range(ng):
+            num = rows[:, g * G : (g + 1) * G]
+            spec = jnp.zeros((B, G), F32)
+            for s in range(keep):
+                r = g * keep + s
+                spec = jnp.where(freq == num[s : s + 1], q[r : r + 1], spec)
+            back = left_mul(left_t[...], spec)
+            at = pl.multiple_of(c0 + g * G, 128)
+            new_ref[:, pl.ds(at, G)] = moments[:, g * G : (g + 1) * G] - back
+
+
+def places_body(n_r, keep, mask, tally, idx_row, tall, hi_ref, lo_ref):
+    total, alive = jnp.float32(0), jnp.float32(0)
+    burdens = []
+    for r in range(n_r):
+        m = mask[r].astype(F32)
+        burdens.append(m * tally[r].astype(F32))
+        total = total + burdens[r]
+        alive = alive + m
+    rep = (lax.broadcasted_iota(jnp.int32, (1, G), 1) // keep) % n_r
+    w = jnp.zeros((1, G), F32)
+    for r in range(n_r):
+        w = jnp.where(rep == r, burdens[r], w)
+    w = w * (jnp.full((1, G), alive) / jnp.full((1, G), total))
+    freq = lax.broadcasted_iota(jnp.int32, (B, G), 0)
+    for c in range(0, idx_row.shape[1], G):
+        hot = jnp.where(freq == idx_row[:, c : c + G], 1.0, 0.0).astype(BF16)
+        y = dot(tall[...], hot)
+        hi, lo = split((y[:B] + y[B:]) * w)
+        hi_ref[:, c : c + G] = hi
+        lo_ref[:, c : c + G] = lo
+
+
+def update_body(n_r, keep, pos, p_hi, p_lo, inv, *refs):
+    ships, out, held = refs[:n_r], refs[n_r], refs[n_r + 1]
+    rep = pos[0]
+    for m in range(n_r):
+        q = pl.multiple_of((rep ^ m) * keep, keep)
+        held[pl.ds(q, keep), :] = ships[m][...].astype(F32)
+    per = n_r * keep
+    nb = G // B
+    width = nb * per
+    lane_block = lax.broadcasted_iota(jnp.int32, (per, G), 1) // B
+    for g in range(out.shape[1] // G):
+        s = held[:, g * G : (g + 1) * G]
+        w = jnp.concatenate(
+            [jnp.where(lane_block == j, s, 0.0).astype(BF16) for j in range(nb)], axis=0
+        )
+        cut = slice(g * width, (g + 1) * width)
+        y = dot(jnp.concatenate([p_hi[:, cut], p_lo[:, cut]], axis=0), w)
+        hi, lo = split(y[:B] + y[B:])
+        z = dot(jnp.concatenate([hi, lo], axis=0), inv[0])
+        out[:, g * G : (g + 1) * G] = z[:B] + z[B:] + dot(hi, inv[1])
+
+
+def input_grad_body(n_t, rp, cp, exp_ref, *refs):
+    ups, out, held = refs[:n_t], refs[n_t], refs[n_t + 1]
+    nr = B // rp
+    nc = out.shape[1] // cp
+    for i in range(rp):
+        for j in range(cp):
+            for k in range(n_t):
+                held[k * B + i * nr : k * B + (i + 1) * nr, j * nc : (j + 1) * nc] = exp_ref[i * cp + j, k]
+    up = jnp.concatenate([u[...] for u in ups], axis=0).T
+    for c in range(0, out.shape[1], G):
+        out[:, c : c + G] = dot(up, held[:, c : c + G]).astype(BF16)
+
+
+def per_device(n_t, n_r, act, switch, slope, exp, vel, lines, mask, tally):
+    cols = act.shape[1]
+    width = exp.shape[1]
+    tok = act.shape[0]
+    keep = lines.shape[3]
+    blocks = width // B
+    cp = 2
+    rp = n_r // cp
+    left, left_t, fwd, inv, tall = constants()
+    rep = lax.axis_index("replica")
+    ten = lax.axis_index("tensor")
+    pos = jnp.stack([rep, ten]).astype(jnp.int32)
+
+    shift = lambda x, k: lax.ppermute(x, "tensor", [(i, (i + k) % n_t) for i in range(n_t)]) if k % n_t else x
+    swap = lambda x, m: lax.ppermute(x, "replica", [(i, i ^ m) for i in range(n_r)]) if m else x
+
+    up = (slope.astype(F32) * jax.nn.silu(switch.astype(F32))).astype(BF16).T
+    ups = [shift(up, k) for k in range(n_t)]
+
+    pieces = call(
+        functools.partial(cut_body, n_t, rp, cp, cols),
+        [jax.ShapeDtypeStruct((B // rp, cols // cp), BF16)] * n_t,
+        (pos, exp),
+        [SM, VM],
+        [VM] * n_t,
+        nbytes=exp.size * 2,
+        name="cut_expansion",
+    )
+    pieces = jnp.stack([shift(pieces[k], k) for k in range(n_t)])
+    exp_all = lax.all_gather(pieces, "replica", axis=0)
+
+    own = lines[0, 0].T
+    idx_all = lax.all_gather(own, "replica", axis=0)
+    idx_row = idx_all.reshape(n_r * keep, blocks).T.reshape(1, blocks * n_r * keep)
+
+    grads = call(
+        functools.partial(grads_body, n_t),
+        [jax.ShapeDtypeStruct((B, cols), F32)] + [jax.ShapeDtypeStruct((B, cols), BF16)] * (n_t - 1),
+        (*ups, act),
+        [VM] * (n_t + 1),
+        [VM] * n_t,
+        flops=2 * n_t * B * tok * cols,
+        nbytes=act.size * 2 + n_t * B * cols * 2,
+        name="weight_grads",
+    )
+    grads = [shift(grads[k], -k) for k in range(n_t)]
+
+    p_hi, p_lo = call(
+        functools.partial(places_body, n_r, keep),
+        [jax.ShapeDtypeStruct((B, blocks * n_r * keep), BF16)] * 2,
+        (mask, tally, idx_row, tall),
+        [SM, SM, VM, VM],
+        [VM, VM],
+        flops=4 * B * B * blocks * n_r * keep,
+        nbytes=4 * B * blocks * n_r * keep,
+        name="places",
+    )
+
+    new, ship = call(
+        functools.partial(moment_body, n_t),
+        [jax.ShapeDtypeStruct((B, width), F32), jax.ShapeDtypeStruct((keep, width), BF16)],
+        (pos, vel[0], own, left, left_t, fwd, inv, *grads),
+        [SM] + [VM] * (6 + n_t),
+        [VM, VM],
+        flops=12 * B * B * width,
+        nbytes=B * width * 12,
+        name="moments",
+    )
+    ships = [swap(ship, m) for m in range(n_r)]
+
+    input_grad = call(
+        functools.partial(input_grad_body, n_t, rp, cp),
+        jax.ShapeDtypeStruct((tok, cols), BF16),
+        (exp_all, *ups),
+        [VM] * (1 + n_t),
+        VM,
+        scratch=[pltpu.VMEM((n_t * B, cols), BF16)],
+        flops=2 * tok * n_t * B * cols,
+        nbytes=(n_t * B * cols + tok * cols) * 2,
+        name="input_grads",
+    )
+
+    update = call(
+        functools.partial(update_body, n_r, keep),
+        jax.ShapeDtypeStruct((B, width), F32),
+        (pos, p_hi, p_lo, inv, *ships),
+        [SM] + [VM] * (3 + n_r),
+        VM,
+        scratch=[pltpu.VMEM((n_r * keep, width), F32)],
+        flops=8 * B * G * width,
+        nbytes=B * width * 8,
+        name="updates",
+    )
+    return input_grad, new[None], update
+
+
+def per_device_plain(
     projection_inputs,
     switch_logits_raw,
     inner_neuron_slope,
@@ -64,8 +350,23 @@
 
 
 def solution(mesh):
+    n_t, n_r = mesh.shape["tensor"], mesh.shape["replica"]
+
+    def device(*args):
+        act, exp, lines = args[0], args[3], args[5]
+        fits = (
+            act.shape[1] % G == 0
+            and act.shape[0] % 128 == 0
+            and exp.shape[0] == B
+            and lines.shape[3] == 8
+            and n_r == 8
+        )
+        if not fits:
+            return per_device_plain(*args)
+        return per_device(n_t, n_r, *args)
+
     return jax.shard_map(
-        per_device,
+        device,
         mesh=mesh,
         in_specs=(
             P("replica", "tensor"),

time: 192 us -> 68.4 us (0.36)
  waiting for transfers between devices: 106 us -> 2.59 us
  matrix products: 43.6 us -> 0 us
  starting transfers between devices: 0.12 us -> 22.7 us
  blocking collectives: 0 us -> 20 us
  between operations: 15.2 us -> 0.78 us
  local copies, waits for them, and re-layouts: 21.4 us -> 7.45 us
  Pallas kernels: 0 us -> 13.4 us
  other arithmetic: 5.2 us -> 0.96 us
    dot_general x10 -> x0, matrix products: 43.6 us -> none  [the longest x2 12.4 us: per_device(): jnp.einsum('fa,ijfg,gb->ijab', cosines, spectrum, cosines, precision=high...]
    psum x1 -> x0, waiting for transfers between devices: 37.4 us -> none  [per_device(): combined = lax.psum(worker_fractions[myself] * spectrum, 'replica')]
    reduce_scatter x1 -> x0, waiting for transfers between devices: 36 us -> none  [per_device(): lax.psum_scatter(partial_terms, 'tensor', scatter_dimension=1, tiled=True)]
    all_gather x1 -> x0, waiting for transfers between devices: 32 us -> none  [per_device(): lax.all_gather(projection_inputs, 'tensor', axis=1, tiled=True)]
    ppermute x0 -> x16, starting transfers between devices: none -> 22.7 us  [the longest x9 16.2 us: per_device(): lax.ppermute(x, 'tensor', [(i, (i + k) % n_t) for i in range(n_t)])]
    all_gather x0 -> x2, blocking collectives: none -> 20 us  [the longest x1 10.8 us: per_device(): exp_all = lax.all_gather(pieces, 'replica', axis=0)]
    pallas_call x0 -> x6, Pallas kernels: none -> 13.4 us  [call(): pl.pallas_call(body, out_shape=out_shape, in_specs=in_specs, out_specs=ou...]
    dot_general x2 -> x0, local copies, waits for them, and re-layouts: 7.63 us -> none  [the longest x1 4.4 us: per_device(): jnp.einsum('fa,ijfg,gb->ijab', cosines, spectrum, cosines, precision=high...]
  transfers between devices with their start and end apart: 3 -> 16, of which waited for: 3 -> 3; matrix products, arithmetic and copies ran while one was open for 25% -> 0% of each run, Pallas kernels for 0% -> 13%
where the time goes in v1:
time: 68.4 us; the launch traced here: 67.8 us
  starting transfers between devices  22.7 us (33%)
  blocking collectives  20 us (29%)
  Pallas kernels  13.4 us (20%)
  local copies, waits for them, and re-layouts  7.45 us (11%)
  waiting for transfers between devices  2.59 us (4%)
  other arithmetic  0.96 us (1%)
  between operations  0.78 us (1%)
    ppermute x9, starting transfers between devices, per_device(): lax.ppermute(x, 'tensor', [(i, (i + k) % n_t) for i in range(n_t)])  16.2 us
    pallas_call x6, Pallas kernels, call(): pl.pallas_call(body, out_shape=out_shape, in_specs=in_specs, out_specs=ou...  13.4 us
    all_gather x1, blocking collectives, per_device(): exp_all = lax.all_gather(pieces, 'replica', axis=0)  10.8 us
    all_gather x1, blocking collectives, per_device(): idx_all = lax.all_gather(own, 'replica', axis=0)  9.2 us
    unnamed x22, local copies, waits for them, and re-layouts  7.28 us
    ppermute x7, starting transfers between devices, per_device(): lax.ppermute(x, 'replica', [(i, i ^ m) for i in range(n_r)])  6.43 us
    ppermute x9, waiting for transfers between devices, per_device(): lax.ppermute(x, 'tensor', [(i, (i + k) % n_t) for i in range(n_t)])  2.4 us
  transfers between devices with their start and end apart: 16, of which 3 were waited for; matrix products, arithmetic and copies ran while one was open for 0% of the time, Pallas kernels for 13%

profile of v1, /device:TPU:0, one launch (start us, length us, event | category | flops | bytes accessed | tf_op | source)
XLA Modules:
  0.0 67.8 jit_solution(9572975880792908461)
XLA Ops:
  0.6 0.0 copy-start.1
  0.6 0.0 copy-start
  0.7 0.9 %fusion.5.refs_0_ = bf16[64,128]{1,0:T(8,128)(2,1)S(1)} fusion(bf16[128,64]{0,1:T(8,128)(2,1)} %param.14, bf16[128,64]{0,1:T(8,128)(2,1)} %param.15), kind=kLoop, calls=%fused_computation.8 | loop fusion | flops 65536 | bytes 49152 | tf_op jit(solution)/shard_map/transpose | solution.py:222
  1.5 3.1 %collective-permute-start.3 = (bf16[64,128]{1,0:T(8,128)(2,1)S(1)}, bf16[64,128]{1,0:T(8,128)(2,1)S(1)}, u32[]{:S(2)}, u32[]{:S(2)}) collective-permute-start(bf16[64,128]{1,0:T(8,128)(2,1)S(1)} %fusion.5.refs_0_), channel_id=1, source_target_pairs={{0,1},{1,2},{2,3},{3,0},{4,5},{5,6},{6,7},{7,4},{8,9},{9,10},{10,1... | collective-permute-start | bytes 49160 | tf_op jit(solution)/shard_map/ppermute | solution.py:219
  4.6 2.6 %collective-permute-start.4 = (bf16[64,128]{1,0:T(8,128)(2,1)S(1)}, bf16[64,128]{1,0:T(8,128)(2,1)S(1)}, u32[]{:S(2)}, u32[]{:S(2)}) collective-permute-start(bf16[64,128]{1,0:T(8,128)(2,1)S(1)} %fusion.5.refs_0_), channel_id=1, source_target_pairs={{0,2},{1,3},{2,0},{3,1},{4,6},{5,7},{6,4},{7,5},{8,10},{9,11},{10,... | collective-permute-start | bytes 49160 | tf_op jit(solution)/shard_map/ppermute | solution.py:219
  7.2 1.3 %collective-permute-start.5 = (bf16[64,128]{1,0:T(8,128)(2,1)S(1)}, bf16[64,128]{1,0:T(8,128)(2,1)S(1)}, u32[]{:S(2)}, u32[]{:S(2)}) collective-permute-start(bf16[64,128]{1,0:T(8,128)(2,1)S(1)} %fusion.5.refs_0_), channel_id=1, source_target_pairs={{0,3},{1,0},{2,1},{3,2},{4,7},{5,4},{6,5},{7,6},{8,11},{9,8},{10,9... | collective-permute-start | bytes 49160 | tf_op jit(solution)/shard_map/ppermute | solution.py:219
  8.5 0.0 collective-permute-done.3.refs_1_
  8.5 0.8 %collective-permute-done.4.refs_2_ = bf16[64,128]{1,0:T(8,128)(2,1)S(1)} collective-permute-done((bf16[64,128]{1,0:T(8,128)(2,1)S(1)}, bf16[64,128]{1,0:T(8,128)(2,1)S(1)}, u32[]{:S(2)}, u32[]{:S(2)}) %collective-permute-start.4) | collective-permute-done | bytes 16416 | tf_op jit(solution)/shard_map/ppermute | solution.py:219
  9.3 1.6 %collective-permute-done.5.refs_3_ = bf16[64,128]{1,0:T(8,128)(2,1)S(1)} collective-permute-done((bf16[64,128]{1,0:T(8,128)(2,1)S(1)}, bf16[64,128]{1,0:T(8,128)(2,1)S(1)}, u32[]{:S(2)}, u32[]{:S(2)}) %collective-permute-start.5) | collective-permute-done | bytes 16416 | tf_op jit(solution)/shard_map/ppermute | solution.py:219
  10.9 0.0 copy-start.3
  10.9 1.0 %copy-done.3 = bf16[128,1280]{1,0:T(8,128)(2,1)S(1)} copy-done((bf16[128,1280]{1,0:T(8,128)(2,1)S(1)}, bf16[128,1280]{1,0:T(8,128)(2,1)}, u32[]{:S(2)}) %copy-start.3) | copy-done | bytes 327704
  11.9 0.3 weight_grads.1
  12.2 3.2 %collective-permute-start.6 = (bf16[64,1280]{1,0:T(8,128)(2,1)S(1)}, bf16[64,1280]{1,0:T(8,128)(2,1)S(1)}, u32[]{:S(2)}, u32[]{:S(2)}) collective-permute-start(bf16[64,1280]{1,0:T(8,128)(2,1)S(1)} %get-tuple-element.20), channel_id=1, source_target_pairs={{0,3},{1,0},{2,1},{3,2},{4,7},{5,4},{6,5},{7,6},{8,11},{9,8},{10,9... | collective-permute-start | bytes 491528 | tf_op jit(solution)/shard_map/ppermute | solution.py:219
  15.4 0.0 collective-permute-start.7
  15.4 0.6 collective-permute-start.8
  16.1 0.1 pad_add_fusion.pos
  16.1 0.0 copy-start.2
  16.1 1.1 %copy-done.2 = bf16[64,5120]{1,0:T(8,128)(2,1)S(1)} copy-done((bf16[64,5120]{1,0:T(8,128)(2,1)S(1)}, bf16[64,5120]{1,0:T(8,128)(2,1)}, u32[]{:S(2)}) %copy-start.2) | copy-done | bytes 655384
  17.2 0.6 cut_expansion.1
  17.8 2.9 %collective-permute-start = (bf16[16,640]{1,0:T(8,128)(2,1)S(1)}, bf16[16,640]{1,0:T(8,128)(2,1)S(1)}, u32[]{:S(2)}, u32[]{:S(2)}) collective-permute-start(bf16[16,640]{1,0:T(8,128)(2,1)S(1)} %get-tuple-element.16), channel_id=1, source_target_pairs={{0,1},{1,2},{2,3},{3,0},{4,5},{5,6},{6,7},{7,4},{8,9},{9,10},{10,1... | collective-permute-start | bytes 61448 | tf_op jit(solution)/shard_map/ppermute | solution.py:219
  20.7 0.9 %collective-permute-start.1 = (bf16[16,640]{1,0:T(8,128)(2,1)S(1)}, bf16[16,640]{1,0:T(8,128)(2,1)S(1)}, u32[]{:S(2)}, u32[]{:S(2)}) collective-permute-start(bf16[16,640]{1,0:T(8,128)(2,1)S(1)} %get-tuple-element.17), channel_id=1, source_target_pairs={{0,2},{1,3},{2,0},{3,1},{4,6},{5,7},{6,4},{7,5},{8,10},{9,11},{10,... | collective-permute-start | bytes 61448 | tf_op jit(solution)/shard_map/ppermute | solution.py:219
  21.6 9.2 %all-gather.1 = s32[64,80]{1,0:T(8,128)S(1)} all-gather(s32[8,80]{1,0:T(8,128)} %bitcast.18), channel_id=3, replica_groups=mesh['replica'=8,'tensor'=4] {'replica'}, dimensions={0}, use_global_device_ids=true | all-gather | bytes 23040 | tf_op jit(solution)/shard_map/all_gather | solution.py:238
  30.8 0.1 copy.18
  30.9 0.1 reshape.13.idx_row
  31.0 0.0 copy-start.8
  31.0 0.6 copy-done.8
  31.6 0.0 copy-start.9
  31.7 0.7 copy-done.9
  32.3 0.0 copy-start.10
  32.3 0.8 %copy-done.10 = bf16[128,64]{1,0:T(8,128)(2,1)S(1)} copy-done((bf16[128,64]{1,0:T(8,128)(2,1)S(1)}, bf16[128,64]{1,0:T(8,128)(2,1)}, u32[]{:S(2)}) %copy-start.10) | copy-done | bytes 16408
  33.1 1.0 %places.1 = (bf16[64,5120]{1,0:T(8,128)(2,1)S(1)}, bf16[64,5120]{1,0:T(8,128)(2,1)S(1)}) custom-call(s32[8]{0:T(128)S(1)} %copy-done.8, s32[8]{0:T(128)S(1)} %copy-done.9, s32[1,5120]{1,0:T(1,128)S(1)} %reshape.13.idx_row, bf16[128,64]{1,0:T(8,128)(2,1)S(1)} %copy-done.10), custom_call_target="tpu_custom_call" | custom-call | flops 83886080 | bytes 1310720 | tf_op jit(solution)/shard_map/places/pallas_call | solution.py:72
  34.1 0.0 collective-permute-done.6.refs_1_
  34.1 1.6 %collective-permute-start.2 = (bf16[16,640]{1,0:T(8,128)(2,1)S(1)}, bf16[16,640]{1,0:T(8,128)(2,1)S(1)}, u32[]{:S(2)}, u32[]{:S(2)}) collective-permute-start(bf16[16,640]{1,0:T(8,128)(2,1)S(1)} %get-tuple-element.18), channel_id=1, source_target_pairs={{0,3},{1,0},{2,1},{3,2},{4,7},{5,4},{6,5},{7,6},{8,11},{9,8},{10,9... | collective-permute-start | bytes 61448 | tf_op jit(solution)/shard_map/ppermute | solution.py:219
  35.7 0.0 collective-permute-done.7.refs_2_
  35.7 0.0 collective-permute-done.8.refs_3_
  35.7 0.0 copy-done.1
  35.7 0.0 copy-done
  35.7 0.0 copy-start.4
  35.7 0.9 %copy-done.4 = bf16[2,256,256]{2,1,0:T(8,128)(2,1)S(1)} copy-done((bf16[2,256,256]{2,1,0:T(8,128)(2,1)S(1)}, bf16[2,256,256]{2,1,0:T(8,128)(2,1)}, u32[]{:S(2)}) %copy-start.4) | copy-done | bytes 262168
  36.7 0.0 copy-start.5
  36.7 0.8 %copy-done.5 = bf16[128,128]{1,0:T(8,128)(2,1)S(1)} copy-done((bf16[128,128]{1,0:T(8,128)(2,1)S(1)}, bf16[128,128]{1,0:T(8,128)(2,1)}, u32[]{:S(2)}) %copy-start.5) | copy-done | bytes 32792
  37.5 0.8 %copy-done.6 = bf16[128,128]{1,0:T(8,128)(2,1)S(1)} copy-done((bf16[128,128]{1,0:T(8,128)(2,1)S(1)}, bf16[128,128]{1,0:T(8,128)(2,1)}, u32[]{:S(2)}) %copy-start.6) | copy-done | bytes 32792
  38.2 0.7 %copy-done.7 = s32[1,1,80,8]{2,3,1,0:T(8,128)S(1)} copy-done((s32[1,1,80,8]{2,3,1,0:T(8,128)S(1)}, s32[1,1,80,8]{2,3,1,0:T(8,128)}, u32[]{:S(2)}) %copy-start.7) | copy-done | bytes 2584
  38.9 6.3 %moments.1 = (f32[64,5120]{1,0:T(8,128)}, bf16[8,5120]{1,0:T(8,128)(2,1)S(1)}) custom-call(s32[2]{0:T(128)S(1)} %pad_add_fusion.pos, f32[64,5120]{1,0:T(8,128)S(1)} %bitcast.16, s32[8,80]{1,0:T(8,128)S(1)} %bitcast.19, bf16[128,128]{1,0:T(8,128)(2,1)S(1)} %copy-done.5, bf16[128,128]{1,0:T(8,128)(2,1)S(1)} %copy-done.6, bf16[2,256,256]{2,1,0:T(8,128)(2,1)S(1)} %copy-done.4, ...), custom_call_target="tpu_custom_call" | custom-call | flops 251658240 | bytes 3932160 | tf_op jit(solution)/shard_map/moments/pallas_call | solution.py:72
  45.2 1.4 %collective-permute-start.10 = (bf16[8,5120]{1,0:T(8,128)(2,1)S(1)}, bf16[8,5120]{1,0:T(8,128)(2,1)S(1)}, u32[]{:S(2)}, u32[]{:S(2)}) collective-permute-start(bf16[8,5120]{1,0:T(8,128)(2,1)S(1)} %get-tuple-element.26.refs_0_), channel_id=1, source_target_pairs={{0,8},{4,12},{8,0},{12,4},{16,24},{20,28},{24,16},{28,20},{1,9},{5... | collective-permute-start | bytes 245768 | tf_op jit(solution)/shard_map/ppermute | solution.py:220
  46.5 0.0 collective-permute-start.11
  46.6 0.0 collective-permute-done
  46.6 0.0 collective-permute-done.1
  46.6 0.0 collective-permute-done.2
  46.6 1.4 %collective-permute-start.12 = (bf16[8,5120]{1,0:T(8,128)(2,1)S(1)}, bf16[8,5120]{1,0:T(8,128)(2,1)S(1)}, u32[]{:S(2)}, u32[]{:S(2)}) collective-permute-start(bf16[8,5120]{1,0:T(8,128)(2,1)S(1)} %get-tuple-element.26.refs_0_), channel_id=1, source_target_pairs={{0,16},{4,20},{8,24},{12,28},{16,0},{20,4},{24,8},{28,12},{1,17},{... | collective-permute-start | bytes 245768 | tf_op jit(solution)/shard_map/ppermute | solution.py:220
  48.0 0.7 %collective-permute-start.13 = (bf16[8,5120]{1,0:T(8,128)(2,1)S(1)}, bf16[8,5120]{1,0:T(8,128)(2,1)S(1)}, u32[]{:S(2)}, u32[]{:S(2)}) collective-permute-start(bf16[8,5120]{1,0:T(8,128)(2,1)S(1)} %get-tuple-element.26.refs_0_), channel_id=1, source_target_pairs={{0,20},{4,16},{8,28},{12,24},{16,4},{20,0},{24,12},{28,8},{1,21},{... | collective-permute-start | bytes 245768 | tf_op jit(solution)/shard_map/ppermute | solution.py:220
  48.8 1.3 %collective-permute-start.14 = (bf16[8,5120]{1,0:T(8,128)(2,1)S(1)}, bf16[8,5120]{1,0:T(8,128)(2,1)S(1)}, u32[]{:S(2)}, u32[]{:S(2)}) collective-permute-start(bf16[8,5120]{1,0:T(8,128)(2,1)S(1)} %get-tuple-element.26.refs_0_), channel_id=1, source_target_pairs={{0,24},{4,28},{8,16},{12,20},{16,8},{20,12},{24,0},{28,4},{1,25},{... | collective-permute-start | bytes 245768 | tf_op jit(solution)/shard_map/ppermute | solution.py:220
  50.1 0.0 collective-permute-done.10.refs_2_
  50.1 1.0 %collective-permute-start.15 = (bf16[8,5120]{1,0:T(8,128)(2,1)S(1)}, bf16[8,5120]{1,0:T(8,128)(2,1)S(1)}, u32[]{:S(2)}, u32[]{:S(2)}) collective-permute-start(bf16[8,5120]{1,0:T(8,128)(2,1)S(1)} %get-tuple-element.26.refs_0_), channel_id=1, source_target_pairs={{0,28},{4,24},{8,20},{12,16},{16,12},{20,8},{24,4},{28,0},{1,29},{... | collective-permute-start | bytes 245768 | tf_op jit(solution)/shard_map/ppermute | solution.py:220
  51.1 0.2 collective-permute-done.11.refs_3_
  51.2 0.6 collective-permute-start.9
  51.8 10.8 %all-gather = bf16[32,16,640]{2,1,0:T(8,128)(2,1)S(1)} all-gather(bf16[4,16,640]{2,1,0:T(8,128)(2,1)S(1)} %pad_maximum_fusion), channel_id=2, replica_groups=mesh['replica'=8,'tensor'=4] {'replica'}, dimensions={0}, use_global_device_ids=true | all-gather | bytes 737280 | tf_op jit(solution)/shard_map/all_gather | solution.py:235
  62.6 1.0 %input_grads.1 = bf16[128,1280]{1,0:T(8,128)(2,1)} custom-call(bf16[8,4,16,640]{3,2,1,0:T(8,128)(2,1)S(1)} %bitcast.15, bf16[64,128]{1,0:T(8,128)(2,1)S(1)} %fusion.5.refs_0_, bf16[64,128]{1,0:T(8,128)(2,1)S(1)} %collective-permute-done.3.refs_1_, bf16[64,128]{1,0:T(8,128)(2,1)S(1)} %collective-permute-done.4.refs_2_, ...), custom_call_target="tpu_custom_call" | custom-call | flops 83886080 | bytes 983040 | tf_op jit(solution)/shard_map/input_grads/pallas_call | solution.py:72
  63.6 0.0 collective-permute-done.12.refs_4_
  63.6 0.0 collective-permute-done.13.refs_5_
  63.6 0.0 collective-permute-done.14.refs_6_
  63.6 0.0 collective-permute-done.15.refs_7_
  63.7 0.0 collective-permute-done.9.refs_1_
  63.7 4.2 %updates.1 = f32[64,5120]{1,0:T(8,128)} custom-call(s32[2]{0:T(128)S(1)} %pad_add_fusion.pos, bf16[64,5120]{1,0:T(8,128)(2,1)S(1)} %get-tuple-element.24.p_hi, bf16[64,5120]{1,0:T(8,128)(2,1)S(1)} %get-tuple-element.25.p_lo, bf16[2,256,256]{2,1,0:T(8,128)(2,1)S(1)} %copy-done.1, bf16[8,5120]{1,0:T(8,128)(2,1)S(1)} %get-tuple-element.26.refs_0_, ...), custom_call_target="tpu_custom_call" | custom-call | flops 671088640 | bytes 2621440 | tf_op jit(solution)/shard_map/updates/pallas_call | solution.py:72
  (3 shorter events, 0.0 us)
Async XLA Ops:
  0.6 35.1 %copy-start.1 = (bf16[2,256,256]{2,1,0:T(8,128)(2,1)S(1)}, bf16[2,256,256]{2,1,0:T(8,128)(2,1)}, u32[]{:S(2)}) copy-start(bf16[2,256,256]{2,1,0:T(8,128)(2,1)} %constant.25.clone.inv) | copy-start | bytes 786436
  0.6 35.1 %copy-start = (f32[1,64,5120]{2,1,0:T(8,128)S(1)}, f32[1,64,5120]{2,1,0:T(8,128)}, u32[]{:S(2)}) copy-start(f32[1,64,5120]{2,1,0:T(8,128)} %param.17) | copy-start | bytes 3932164
  1.5 7.0 %collective-permute-start.3 = (bf16[64,128]{1,0:T(8,128)(2,1)S(1)}, bf16[64,128]{1,0:T(8,128)(2,1)S(1)}, u32[]{:S(2)}, u32[]{:S(2)}) collective-permute-start(bf16[64,128]{1,0:T(8,128)(2,1)S(1)} %fusion.5.refs_0_), channel_id=1, source_target_pairs={{0,1},{1,2},{2,3},{3,0},{4,5},{5,6},{6,7},{7,4},{8,9},{9,10},{10,1... | collective-permute-start | bytes 49160 | tf_op jit(solution)/shard_map/ppermute | solution.py:219
  4.6 4.7 %collective-permute-start.4 = (bf16[64,128]{1,0:T(8,128)(2,1)S(1)}, bf16[64,128]{1,0:T(8,128)(2,1)S(1)}, u32[]{:S(2)}, u32[]{:S(2)}) collective-permute-start(bf16[64,128]{1,0:T(8,128)(2,1)S(1)} %fusion.5.refs_0_), channel_id=1, source_target_pairs={{0,2},{1,3},{2,0},{3,1},{4,6},{5,7},{6,4},{7,5},{8,10},{9,11},{10,... | collective-permute-start | bytes 49160 | tf_op jit(solution)/shard_map/ppermute | solution.py:219
  7.2 3.7 %collective-permute-start.5 = (bf16[64,128]{1,0:T(8,128)(2,1)S(1)}, bf16[64,128]{1,0:T(8,128)(2,1)S(1)}, u32[]{:S(2)}, u32[]{:S(2)}) collective-permute-start(bf16[64,128]{1,0:T(8,128)(2,1)S(1)} %fusion.5.refs_0_), channel_id=1, source_target_pairs={{0,3},{1,0},{2,1},{3,2},{4,7},{5,4},{6,5},{7,6},{8,11},{9,8},{10,9... | collective-permute-start | bytes 49160 | tf_op jit(solution)/shard_map/ppermute | solution.py:219
  10.9 1.0 %copy-start.3 = (bf16[128,1280]{1,0:T(8,128)(2,1)S(1)}, bf16[128,1280]{1,0:T(8,128)(2,1)}, u32[]{:S(2)}) copy-start(bf16[128,1280]{1,0:T(8,128)(2,1)} %refs_4_.1) | copy-start | bytes 983044
  12.2 21.9 %collective-permute-start.6 = (bf16[64,1280]{1,0:T(8,128)(2,1)S(1)}, bf16[64,1280]{1,0:T(8,128)(2,1)S(1)}, u32[]{:S(2)}, u32[]{:S(2)}) collective-permute-start(bf16[64,1280]{1,0:T(8,128)(2,1)S(1)} %get-tuple-element.20), channel_id=1, source_target_pairs={{0,3},{1,0},{2,1},{3,2},{4,7},{5,4},{6,5},{7,6},{8,11},{9,8},{10,9... | collective-permute-start | bytes 491528 | tf_op jit(solution)/shard_map/ppermute | solution.py:219
  15.4 20.3 %collective-permute-start.7 = (bf16[64,1280]{1,0:T(8,128)(2,1)S(1)}, bf16[64,1280]{1,0:T(8,128)(2,1)S(1)}, u32[]{:S(2)}, u32[]{:S(2)}) collective-permute-start(bf16[64,1280]{1,0:T(8,128)(2,1)S(1)} %get-tuple-element.21), channel_id=1, source_target_pairs={{0,2},{1,3},{2,0},{3,1},{4,6},{5,7},{6,4},{7,5},{8,10},{9,11},{10,... | collective-permute-start | bytes 491528 | tf_op jit(solution)/shard_map/ppermute | solution.py:219
  15.4 20.3 %collective-permute-start.8 = (bf16[64,1280]{1,0:T(8,128)(2,1)S(1)}, bf16[64,1280]{1,0:T(8,128)(2,1)S(1)}, u32[]{:S(2)}, u32[]{:S(2)}) collective-permute-start(bf16[64,1280]{1,0:T(8,128)(2,1)S(1)} %get-tuple-element.22), channel_id=1, source_target_pairs={{0,1},{1,2},{2,3},{3,0},{4,5},{5,6},{6,7},{7,4},{8,9},{9,10},{10,1... | collective-permute-start | bytes 491528 | tf_op jit(solution)/shard_map/ppermute | solution.py:219
  16.1 1.1 %copy-start.2 = (bf16[64,5120]{1,0:T(8,128)(2,1)S(1)}, bf16[64,5120]{1,0:T(8,128)(2,1)}, u32[]{:S(2)}) copy-start(bf16[64,5120]{1,0:T(8,128)(2,1)} %exp_ref.1) | copy-start | bytes 1966084
  17.8 28.8 %collective-permute-start = (bf16[16,640]{1,0:T(8,128)(2,1)S(1)}, bf16[16,640]{1,0:T(8,128)(2,1)S(1)}, u32[]{:S(2)}, u32[]{:S(2)}) collective-permute-start(bf16[16,640]{1,0:T(8,128)(2,1)S(1)} %get-tuple-element.16), channel_id=1, source_target_pairs={{0,1},{1,2},{2,3},{3,0},{4,5},{5,6},{6,7},{7,4},{8,9},{9,10},{10,1... | collective-permute-start | bytes 61448 | tf_op jit(solution)/shard_map/ppermute | solution.py:219
  20.7 25.9 %collective-permute-start.1 = (bf16[16,640]{1,0:T(8,128)(2,1)S(1)}, bf16[16,640]{1,0:T(8,128)(2,1)S(1)}, u32[]{:S(2)}, u32[]{:S(2)}) collective-permute-start(bf16[16,640]{1,0:T(8,128)(2,1)S(1)} %get-tuple-element.17), channel_id=1, source_target_pairs={{0,2},{1,3},{2,0},{3,1},{4,6},{5,7},{6,4},{7,5},{8,10},{9,11},{10,... | collective-permute-start | bytes 61448 | tf_op jit(solution)/shard_map/ppermute | solution.py:219
  31.0 0.7 copy-start.8
  31.6 0.7 copy-start.9
  32.3 0.8 %copy-start.10 = (bf16[128,64]{1,0:T(8,128)(2,1)S(1)}, bf16[128,64]{1,0:T(8,128)(2,1)}, u32[]{:S(2)}) copy-start(bf16[128,64]{1,0:T(8,128)(2,1)} %constant.26.clone.tall) | copy-start | bytes 49156
  34.1 12.4 %collective-permute-start.2 = (bf16[16,640]{1,0:T(8,128)(2,1)S(1)}, bf16[16,640]{1,0:T(8,128)(2,1)S(1)}, u32[]{:S(2)}, u32[]{:S(2)}) collective-permute-start(bf16[16,640]{1,0:T(8,128)(2,1)S(1)} %get-tuple-element.18), channel_id=1, source_target_pairs={{0,3},{1,0},{2,1},{3,2},{4,7},{5,4},{6,5},{7,6},{8,11},{9,8},{10,9... | collective-permute-start | bytes 61448 | tf_op jit(solution)/shard_map/ppermute | solution.py:219
  35.7 1.0 %copy-start.4 = (bf16[2,256,256]{2,1,0:T(8,128)(2,1)S(1)}, bf16[2,256,256]{2,1,0:T(8,128)(2,1)}, u32[]{:S(2)}) copy-start(bf16[2,256,256]{2,1,0:T(8,128)(2,1)} %constant.24.clone.fwd) | copy-start | bytes 786436
  36.7 0.8 %copy-start.5 = (bf16[128,128]{1,0:T(8,128)(2,1)S(1)}, bf16[128,128]{1,0:T(8,128)(2,1)}, u32[]{:S(2)}) copy-start(bf16[128,128]{1,0:T(8,128)(2,1)} %constant.22.clone.left) | copy-start | bytes 98308
  37.4 0.8 %copy-start.6 = (bf16[128,128]{1,0:T(8,128)(2,1)S(1)}, bf16[128,128]{1,0:T(8,128)(2,1)}, u32[]{:S(2)}) copy-start(bf16[128,128]{1,0:T(8,128)(2,1)} %constant.23.clone.left_t) | copy-start | bytes 98308
  38.2 0.7 %copy-start.7 = (s32[1,1,80,8]{2,3,1,0:T(8,128)S(1)}, s32[1,1,80,8]{2,3,1,0:T(8,128)}, u32[]{:S(2)}) copy-start(s32[1,1,80,8]{2,3,1,0:T(8,128)} %param.18) | copy-start | bytes 7684
  45.2 4.9 %collective-permute-start.10 = (bf16[8,5120]{1,0:T(8,128)(2,1)S(1)}, bf16[8,5120]{1,0:T(8,128)(2,1)S(1)}, u32[]{:S(2)}, u32[]{:S(2)}) collective-permute-start(bf16[8,5120]{1,0:T(8,128)(2,1)S(1)} %get-tuple-element.26.refs_0_), channel_id=1, source_target_pairs={{0,8},{4,12},{8,0},{12,4},{16,24},{20,28},{24,16},{28,20},{1,9},{5... | collective-permute-start | bytes 245768 | tf_op jit(solution)/shard_map/ppermute | solution.py:220
  46.5 4.7 %collective-permute-start.11 = (bf16[8,5120]{1,0:T(8,128)(2,1)S(1)}, bf16[8,5120]{1,0:T(8,128)(2,1)S(1)}, u32[]{:S(2)}, u32[]{:S(2)}) collective-permute-start(bf16[8,5120]{1,0:T(8,128)(2,1)S(1)} %get-tuple-element.26.refs_0_), channel_id=1, source_target_pairs={{0,12},{4,8},{8,4},{12,0},{16,28},{20,24},{24,20},{28,16},{1,13},{... | collective-permute-start | bytes 245768 | tf_op jit(solution)/shard_map/ppermute | solution.py:220
  46.6 17.0 %collective-permute-start.12 = (bf16[8,5120]{1,0:T(8,128)(2,1)S(1)}, bf16[8,5120]{1,0:T(8,128)(2,1)S(1)}, u32[]{:S(2)}, u32[]{:S(2)}) collective-permute-start(bf16[8,5120]{1,0:T(8,128)(2,1)S(1)} %get-tuple-element.26.refs_0_), channel_id=1, source_target_pairs={{0,16},{4,20},{8,24},{12,28},{16,0},{20,4},{24,8},{28,12},{1,17},{... | collective-permute-start | bytes 245768 | tf_op jit(solution)/shard_map/ppermute | solution.py:220
  48.0 15.6 %collective-permute-start.13 = (bf16[8,5120]{1,0:T(8,128)(2,1)S(1)}, bf16[8,5120]{1,0:T(8,128)(2,1)S(1)}, u32[]{:S(2)}, u32[]{:S(2)}) collective-permute-start(bf16[8,5120]{1,0:T(8,128)(2,1)S(1)} %get-tuple-element.26.refs_0_), channel_id=1, source_target_pairs={{0,20},{4,16},{8,28},{12,24},{16,4},{20,0},{24,12},{28,8},{1,21},{... | collective-permute-start | bytes 245768 | tf_op jit(solution)/shard_map/ppermute | solution.py:220
  48.8 14.9 %collective-permute-start.14 = (bf16[8,5120]{1,0:T(8,128)(2,1)S(1)}, bf16[8,5120]{1,0:T(8,128)(2,1)S(1)}, u32[]{:S(2)}, u32[]{:S(2)}) collective-permute-start(bf16[8,5120]{1,0:T(8,128)(2,1)S(1)} %get-tuple-element.26.refs_0_), channel_id=1, source_target_pairs={{0,24},{4,28},{8,16},{12,20},{16,8},{20,12},{24,0},{28,4},{1,25},{... | collective-permute-start | bytes 245768 | tf_op jit(solution)/shard_map/ppermute | solution.py:220
  50.1 13.6 %collective-permute-start.15 = (bf16[8,5120]{1,0:T(8,128)(2,1)S(1)}, bf16[8,5120]{1,0:T(8,128)(2,1)S(1)}, u32[]{:S(2)}, u32[]{:S(2)}) collective-permute-start(bf16[8,5120]{1,0:T(8,128)(2,1)S(1)} %get-tuple-element.26.refs_0_), channel_id=1, source_target_pairs={{0,28},{4,24},{8,20},{12,16},{16,12},{20,8},{24,4},{28,0},{1,29},{... | collective-permute-start | bytes 245768 | tf_op jit(solution)/shard_map/ppermute | solution.py:220
  51.2 12.4 %collective-permute-start.9 = (bf16[8,5120]{1,0:T(8,128)(2,1)S(1)}, bf16[8,5120]{1,0:T(8,128)(2,1)S(1)}, u32[]{:S(2)}, u32[]{:S(2)}) collective-permute-start(bf16[8,5120]{1,0:T(8,128)(2,1)S(1)} %get-tuple-element.26.refs_0_), channel_id=1, source_target_pairs={{0,4},{4,0},{8,12},{12,8},{16,20},{20,16},{24,28},{28,24},{1,5},{5... | collective-permute-start | bytes 245768 | tf_op jit(solution)/shard_map/ppermute | solution.py:220

commit v2 on v1

v2 whole, which is shorter than its diff:
```python
import functools

import jax
import jax.numpy as jnp
import numpy as np
from jax import lax
from jax.experimental import pallas as pl
from jax.experimental.pallas import tpu as pltpu
from jax.sharding import PartitionSpec as P

momentum_decay = 0.9
B = 64
G = 256
F32 = jnp.float32
BF16 = jnp.bfloat16
VMEM_LIMIT = 48 * 1024 * 1024

VM = pl.BlockSpec(memory_space=pltpu.VMEM)
SM = pl.BlockSpec(memory_space=pltpu.SMEM)


def cosine_table():
    freqs = jnp.arange(64, dtype=jnp.float32)[:, None]
    places = jnp.arange(64, dtype=jnp.float32)[None, :]
    cosines = jnp.cos(jnp.pi * (places + 0.5) * freqs / 64.0) * jnp.sqrt(2.0 / 64.0)
    return cosines.at[0].multiply(jnp.sqrt(0.5))


def cosine_np():
    f = np.arange(B)[:, None]
    a = np.arange(B)[None, :]
    c = np.cos(np.pi * (a + 0.5) * f / B) * np.sqrt(2.0 / B)
    c[0] *= np.sqrt(0.5)
    return c


def halves(c):
    hi = np.asarray(c, dtype=np.float32).astype(jnp.bfloat16)
    lo = (np.asarray(c, np.float64) - hi.astype(np.float64)).astype(np.float32).astype(jnp.bfloat16)
    return hi, lo


def constants():
    hi, lo = halves(cosine_np())
    eye = np.eye(G // B)
    kron = lambda x: np.kron(eye, np.asarray(x, np.float32)).astype(jnp.bfloat16)
    tall = np.zeros((2 * B, G), jnp.bfloat16)
    tall[:B, :B], tall[B:, :B] = hi.T, lo.T
    return jnp.asarray(np.concatenate([kron(hi.T), kron(lo.T), kron(hi), kron(lo), tall], axis=0))


def fwd(tab, i):
    return tab[i * G : (i + 1) * G, :]


def inv(tab, i):
    return tab[(2 + i) * G : (3 + i) * G, :]


def tall(tab):
    return tab[4 * G : 4 * G + 2 * B, :B]


def dot(a, b):
    return jnp.dot(a, b, preferred_element_type=F32)


def split(x):
    hi = x.astype(BF16)
    return hi, (x - hi.astype(F32)).astype(BF16)


def call(body, out_shape, ins, in_specs, out_specs, scratch=(), flops=0, nbytes=0, name=None):
    return pl.pallas_call(
        body,
        out_shape=out_shape,
        in_specs=in_specs,
        out_specs=out_specs,
        scratch_shapes=scratch,
        compiler_params=pltpu.CompilerParams(vmem_limit_bytes=VMEM_LIMIT),
        cost_estimate=pl.CostEstimate(flops=flops, bytes_accessed=nbytes, transcendentals=0),
        name=name,
    )(*ins)


def cut_body(n_t, rp, cp, cols, pos, exp_ref, out):
    rep = pos[0]
    nr, nc = B // rp, cols // cp
    r0 = pl.multiple_of((rep // cp) * nr, nr)
    for k in range(n_t):
        c0 = pl.multiple_of(k * cols + lax.rem(rep, cp) * nc, 128)
        out[k] = exp_ref[pl.ds(r0, nr), pl.ds(c0, nc)]


def grads_body(n_t, ups, act, out):
    up = ups[...].reshape(n_t * B, ups.shape[2])
    for c in range(0, act.shape[1], G):
        g = dot(up, act[:, c : c + G]).astype(BF16)
        for k in range(n_t):
            out[k, :, c : c + G] = g[k * B : (k + 1) * B]


def own_body(rows, tab, p_ref, a_ref):
    freq = lax.broadcasted_iota(jnp.int32, (B, 2 * B), 0)
    term = lax.broadcasted_iota(jnp.int32, (B, 2 * B), 1) // (B // 2)
    for g in range(rows.shape[0]):
        hot = jnp.where(freq == rows[g : g + 1, :], 1.0, 0.0).astype(BF16)
        y = dot(tall(tab), hot)
        p = jnp.where(term == 3, 0.0, jnp.where(term == 1, y[B:], y[:B]))
        p_ref[:, g * 2 * B : (g + 1) * 2 * B] = p.astype(BF16)
        a_ref[g * B : (g + 1) * B, :] = jnp.concatenate([p, p], axis=0).T[:B].astype(BF16)


def kept_body(keep, vel, a_ref, tab, grads, ship_ref):
    cols = grads.shape[2]
    ng = vel.shape[1] // G
    lane_block = lax.broadcasted_iota(jnp.int32, (keep, G), 1) // B
    sel = []
    for g in range(ng):
        k, c = divmod(g * G, cols)
        cut = slice(g * G, (g + 1) * G)
        hi, lo = split(momentum_decay * vel[:, cut] + grads[k, :, c : c + G].astype(F32))
        y = dot(a_ref[g * B : (g + 1) * B, :], jnp.concatenate([hi, lo], axis=0))
        y = y[: B // 2] + y[B // 2 :]
        got = y[:keep]
        for j in range(1, G // B):
            got = jnp.where(lane_block == j, y[j * keep : (j + 1) * keep], got)
        sel.append(got)
    hi, lo = split(jnp.concatenate(sel, axis=0))
    n = ng * keep
    y = dot(jnp.concatenate([hi, lo], axis=0), fwd(tab, 0))
    y = y[:n] + y[n:] + dot(hi, fwd(tab, 1))
    ship_ref[...] = jnp.concatenate(
        [y[g * keep : (g + 1) * keep] for g in range(ng)], axis=1
    ).astype(BF16)


def return_body(keep, vel, p_ref, tab, grads, ship, new_ref):
    cols = grads.shape[2]
    ng = vel.shape[1] // G
    lane_block = lax.broadcasted_iota(jnp.int32, (keep, G), 1) // B
    kept = ship[...].astype(F32)
    kept = jnp.concatenate([kept[:, g * G : (g + 1) * G] for g in range(ng)], axis=0).astype(BF16)
    q = dot(kept, inv(tab, 0)) + dot(kept, inv(tab, 1))
    for g in range(ng):
        k, c = divmod(g * G, cols)
        cut = slice(g * G, (g + 1) * G)
        own = q[g * keep : (g + 1) * keep]
        spread = jnp.concatenate(
            [jnp.where(lane_block == j, own, 0.0) for j in range(G // B)], axis=0
        )
        hi, lo = split(spread)
        w = jnp.concatenate([hi, hi, lo, jnp.zeros_like(lo)], axis=0)
        back = dot(p_ref[:, g * 2 * B : (g + 1) * 2 * B], w)
        new_ref[:, cut] = momentum_decay * vel[:, cut] + grads[k, :, c : c + G].astype(F32) - back


def places_body(n_r, keep, mask, tally, idx_row, tab, hi_ref, lo_ref):
    total, alive = jnp.float32(0), jnp.float32(0)
    burdens = []
    for r in range(n_r):
        m = mask[r].astype(F32)
        burdens.append(m * tally[r].astype(F32))
        total = total + burdens[r]
        alive = alive + m
    rep = (lax.broadcasted_iota(jnp.int32, (1, G), 1) // keep) % n_r
    w = jnp.zeros((1, G), F32)
    for r in range(n_r):
        w = jnp.where(rep == r, burdens[r], w)
    w = w * (jnp.full((1, G), alive) / jnp.full((1, G), total))
    freq = lax.broadcasted_iota(jnp.int32, (B, G), 0)
    for c in range(0, idx_row.shape[1], G):
        hot = jnp.where(freq == idx_row[:, c : c + G], 1.0, 0.0).astype(BF16)
        y = dot(tall(tab), hot)
        hi, lo = split((y[:B] + y[B:]) * w)
        hi_ref[:, c : c + G] = hi
        lo_ref[:, c : c + G] = lo


def update_body(n_r, keep, p_hi, p_lo, tab, ships, out):
    per = n_r * keep
    nb = G // B
    width = nb * per
    lane_block = lax.broadcasted_iota(jnp.int32, (per, G), 1) // B
    for g in range(out.shape[1] // G):
        cut = slice(g * G, (g + 1) * G)
        s = jnp.concatenate([ships[r, :, cut].astype(F32) for r in range(n_r)], axis=0)
        w = jnp.concatenate(
            [jnp.where(lane_block == j, s, 0.0).astype(BF16) for j in range(nb)], axis=0
        )
        wide = slice(g * width, (g + 1) * width)
        y = dot(jnp.concatenate([p_hi[:, wide], p_lo[:, wide]], axis=0), w)
        hi, lo = split(y[:B] + y[B:])
        z = dot(jnp.concatenate([hi, lo], axis=0), inv(tab, 0))
        out[:, cut] = z[:B] + z[B:] + dot(hi, inv(tab, 1))


def input_grad_body(n_t, rp, cp, exp_ref, ups, out, held):
    nr = B // rp
    nc = out.shape[1] // cp
    for i in range(rp):
        for j in range(cp):
            for k in range(n_t):
                held[k * B + i * nr : k * B + (i + 1) * nr, j * nc : (j + 1) * nc] = exp_ref[
                    i * cp + j, k * nr : (k + 1) * nr, :
                ]
    up = ups[...].reshape(n_t * B, ups.shape[2]).T
    for c in range(0, out.shape[1], G):
        out[:, c : c + G] = dot(up, held[:, c : c + G]).astype(BF16)


def per_device(n_t, n_r, act, switch, slope, exp, vel, lines, mask, tally):
    cols = act.shape[1]
    width = exp.shape[1]
    tok = act.shape[0]
    keep = lines.shape[3]
    blocks = width // B
    groups = width // G
    cp = 2
    rp = n_r // cp
    tab = constants()
    pos = lax.axis_index("replica").astype(jnp.int32).reshape(1)

    def trade(x, axis):
        return lax.all_to_all(x, axis, split_axis=0, concat_axis=0)

    def spread(x, axis, n):
        return trade(jnp.broadcast_to(x[None], (n,) + x.shape), axis)

    up = (slope.astype(F32) * jax.nn.silu(switch.astype(F32))).astype(BF16).T
    ups = spread(up, "tensor", n_t)

    grads = call(
        functools.partial(grads_body, n_t),
        jax.ShapeDtypeStruct((n_t, B, cols), BF16),
        (ups, act),
        [VM] * 2,
        VM,
        flops=2 * n_t * B * tok * cols,
        nbytes=act.size * 2 + n_t * B * cols * 2,
        name="weight_grads",
    )
    grads = trade(grads, "tensor")

    pieces = call(
        functools.partial(cut_body, n_t, rp, cp, cols),
        jax.ShapeDtypeStruct((n_t, B // rp, cols // cp), BF16),
        (pos, exp),
        [SM, VM],
        VM,
        nbytes=exp.size * 2,
        name="cut_expansion",
    )
    pieces = trade(pieces, "tensor").reshape(n_t * (B // rp), cols // cp)
    own = lines[0, 0].T
    lines_bf = jnp.pad(own.astype(BF16), ((0, 16 - keep), (0, cols // cp - blocks)))
    shared = spread(jnp.concatenate([pieces, lines_bf], axis=0), "replica", n_r)
    idx_all = shared[:, n_t * (B // rp) :][:, :keep, :blocks].astype(jnp.int32)
    idx_row = idx_all.reshape(n_r * keep, blocks).T.reshape(1, blocks * n_r * keep)

    own_rows = jnp.concatenate([lines[0, 0].reshape(groups, B // 2)] * 4, axis=1)
    p_own, a_own = call(
        own_body,
        [
            jax.ShapeDtypeStruct((B, groups * 2 * B), BF16),
            jax.ShapeDtypeStruct((groups * B, 2 * B), BF16),
        ],
        (own_rows, tab),
        [VM, VM],
        [VM, VM],
        flops=groups * 4 * B**3 * 4,
        nbytes=groups * B * B * 8,
        name="own_places",
    )
    p_hi, p_lo = call(
        functools.partial(places_body, n_r, keep),
        [jax.ShapeDtypeStruct((B, blocks * n_r * keep), BF16)] * 2,
        (mask, tally, idx_row, tab),
        [SM, SM, VM, VM],
        [VM, VM],
        flops=4 * B * B * blocks * n_r * keep,
        nbytes=4 * B * blocks * n_r * keep,
        name="places",
    )

    ship = call(
        functools.partial(kept_body, keep),
        jax.ShapeDtypeStruct((keep, width), BF16),
        (vel[0], a_own, tab, grads),
        [VM] * 4,
        VM,
        flops=6 * B * B * width,
        nbytes=B * width * 6,
        name="kept_rows",
    )
    ships = spread(ship, "replica", n_r)
    new = call(
        functools.partial(return_body, keep),
        jax.ShapeDtypeStruct((B, width), F32),
        (vel[0], p_own, tab, grads, ship),
        [VM] * 5,
        VM,
        flops=6 * B * B * width,
        nbytes=B * width * 10,
        name="new_momentums",
    )

    input_grad = call(
        functools.partial(input_grad_body, n_t, rp, cp),
        jax.ShapeDtypeStruct((tok, cols), BF16),
        (shared, ups),
        [VM] * 2,
        VM,
        scratch=[pltpu.VMEM((n_t * B, cols), BF16)],
        flops=2 * tok * n_t * B * cols,
        nbytes=(n_t * B * cols + tok * cols) * 2,
        name="input_grads",
    )

    update = call(
        functools.partial(update_body, n_r, keep),
        jax.ShapeDtypeStruct((B, width), F32),
        (p_hi, p_lo, tab, ships),
        [VM] * 4,
        VM,
        flops=8 * B * G * width,
        nbytes=B * width * 8,
        name="updates",
    )
    return input_grad, new[None], update


def per_device_plain(
    projection_inputs,
    switch_logits_raw,
    inner_neuron_slope,
    expansion_matrix,
    velocity_buffer,
    sent_spectral_lines,
    participant_mask,
    token_tallies,
):
    highest = lax.Precision.HIGHEST
    up_grad = (
        inner_neuron_slope.astype(jnp.float32) * jax.nn.silu(switch_logits_raw.astype(jnp.float32))
    ).astype(jnp.bfloat16)
    partial_terms = jnp.dot(up_grad, expansion_matrix, preferred_element_type=jnp.float32)
    input_grad = lax.psum_scatter(partial_terms, "tensor", scatter_dimension=1, tiled=True).astype(
        jnp.bfloat16
    )
    grad_w = lax.dot_general(
        up_grad,
        lax.all_gather(projection_inputs, "tensor", axis=1, tiled=True),
        (((0,), (0,)), ((), ())),
        preferred_element_type=jnp.float32,
    )
    row_total_count = expansion_matrix.shape[0] // 64
    col_count = expansion_matrix.shape[1] // 64
    moment = momentum_decay * velocity_buffer[0] + grad_w
    cosines = cosine_table()
    blocks = moment.reshape(row_total_count, 64, col_count, 64).transpose(0, 2, 1, 3)
    coefficients = jnp.einsum("fa,ijab,gb->ijfg", cosines, blocks, cosines, precision=highest)
    freq_ids = jnp.arange(64, dtype=jnp.int32)
    own_rows = sent_spectral_lines[0]
    chosen = (own_rows[..., None] == freq_ids).astype(jnp.float32)
    shipped = jnp.einsum("ijkf,ijfg->ijkg", chosen, coefficients, precision=highest).astype(
        jnp.bfloat16
    )
    spectrum = jnp.einsum("ijkf,ijkg->ijfg", chosen, shipped.astype(jnp.float32), precision=highest)
    returned = jnp.einsum("fa,ijfg,gb->ijab", cosines, spectrum, cosines, precision=highest)
    new_moment = moment - returned.transpose(0, 2, 1, 3).reshape(moment.shape)
    worker_burdens = participant_mask.astype(jnp.float32) * token_tallies.astype(jnp.float32)
    worker_fractions = worker_burdens * (
        jnp.sum(participant_mask.astype(jnp.float32)) / jnp.sum(worker_burdens)
    )
    myself = lax.axis_index("replica")
    combined = lax.psum(worker_fractions[myself] * spectrum, "replica")
    update = jnp.einsum("fa,ijfg,gb->ijab", cosines, combined, cosines, precision=highest)
    update = update.transpose(0, 2, 1, 3).reshape(moment.shape)
    return (input_grad, new_moment[None], update)


def solution(mesh):
    n_t, n_r = mesh.shape["tensor"], mesh.shape["replica"]

    def device(*args):
        act, exp, lines = args[0], args[3], args[5]
        fits = (
            act.shape[1] % G == 0
            and act.shape[0] % 128 == 0
            and exp.shape[0] == B
            and lines.shape[3] == 8
            and n_r == 8
        )
        if not fits:
            return per_device_plain(*args)
        return per_device(n_t, n_r, *args)

    return jax.shard_map(
        device,
        mesh=mesh,
        in_specs=(
            P("replica", "tensor"),
            P("replica", "tensor"),
            P("replica", "tensor"),
            P("tensor", None),
            P("replica", "tensor", None),
            P("replica", "tensor", None, None),
            P(),
            P(),
        ),
        out_specs=(P("replica", "tensor"), P("replica", "tensor", None), P("tensor", None)),
        check_vma=False,
    )
```

time: 68.4 us -> 82.2 us (1.20)
  waiting for transfers between devices: 2.59 us -> 37.1 us
  blocking collectives: 20 us -> 0 us
  local copies, waits for them, and re-layouts: 7.45 us -> 9.71 us
  Pallas kernels: 13.4 us -> 11.2 us
  starting transfers between devices: 22.7 us -> 21.1 us
    all_to_all x0 -> x5, waiting for transfers between devices: none -> 37.1 us  [trade(): return lax.all_to_all(x, axis, split_axis=0, concat_axis=0)]
    ppermute x16 -> x0, starting transfers between devices: 22.7 us -> none  [the longest x9 16.2 us: per_device(): lax.ppermute(x, 'tensor', [(i, (i + k) % n_t) for i in range(n_t)])]
    all_to_all x0 -> x5, starting transfers between devices: none -> 21.1 us  [trade(): return lax.all_to_all(x, axis, split_axis=0, concat_axis=0)]
    all_gather x2 -> x0, blocking collectives: 20 us -> none  [the longest x1 10.8 us: per_device(): exp_all = lax.all_gather(pieces, 'replica', axis=0)]
    ppermute x16 -> x0, waiting for transfers between devices: 2.59 us -> none  [the longest x9 2.4 us: per_device(): lax.ppermute(x, 'tensor', [(i, (i + k) % n_t) for i in range(n_t)])]
    broadcast_in_dim x0 -> x3, local copies, waits for them, and re-layouts: none -> 2.49 us  [spread(): return trade(jnp.broadcast_to(x[None], (n,) + x.shape), axis)]
    unnamed x22 -> x27, local copies, waits for them, and re-layouts: 7.28 us -> 4.82 us
    reshape x1 -> x2, local copies, waits for them, and re-layouts: 0.09 us -> 2.33 us  [per_device(): idx_all.reshape(n_r * keep, blocks).T.reshape(1, blocks * n_r * keep)]
  transfers between devices with their start and end apart: 16 -> 5, of which waited for: 3 -> 5; matrix products, arithmetic and copies ran while one was open for 0% -> 4% of each run, Pallas kernels for 13% -> 8%
where the time goes in v2:
time: 82.2 us; the launch traced here: 81.4 us
  waiting for transfers between devices  37.1 us (45%)
  starting transfers between devices  21.1 us (26%)
  Pallas kernels  11.2 us (14%)
  local copies, waits for them, and re-layouts  9.71 us (12%)
  other arithmetic  1.47 us (2%)
    all_to_all x5, waiting for transfers between devices, trade(): return lax.all_to_all(x, axis, split_axis=0, concat_axis=0)  37.1 us
    all_to_all x5, starting transfers between devices, trade(): return lax.all_to_all(x, axis, split_axis=0, concat_axis=0)  21.1 us
    pallas_call x8, Pallas kernels, call(): pl.pallas_call(body, out_shape=out_shape, in_specs=in_specs, out_specs=ou...  11.2 us
    unnamed x27, local copies, waits for them, and re-layouts  4.82 us
    broadcast_in_dim x3, local copies, waits for them, and re-layouts, spread(): return trade(jnp.broadcast_to(x[None], (n,) + x.shape), axis)  2.49 us
    reshape x2, local copies, waits for them, and re-layouts, per_device(): idx_all.reshape(n_r * keep, blocks).T.reshape(1, blocks * n_r * keep)  2.33 us
  transfers between devices with their start and end apart: 5, of which 5 were waited for; matrix products, arithmetic and copies ran while one was open for 4% of the time, Pallas kernels for 8%

profile of v2, /device:TPU:0, one launch (start us, length us, event | category | flops | bytes accessed | tf_op | source)
XLA Modules:
  0.0 81.4 jit_solution(9616654293347703076)
XLA Ops:
  0.6 0.8 fusion.8
  1.4 0.6 broadcast_in_dim.9
  2.0 6.3 %all-to-all-start.2 = ((bf16[4,64,128]{2,1,0:T(8,128)(2,1)}), bf16[4,64,128]{2,1,0:T(8,128)(2,1)S(1)}, u32[]{:S(2)}, u32[]{:S(2)}) async-start(bf16[4,64,128]{2,1,0:T(8,128)(2,1)} %broadcast_in_dim.9), calls=%async_computation.2 | async-start | bytes 131072 | tf_op jit(solution)/shard_map/all_to_all | solution.py:225
  8.3 0.0 copy-start.2
  8.4 1.1 %copy-done.2 = bf16[64,5120]{1,0:T(8,128)(2,1)S(1)} copy-done((bf16[64,5120]{1,0:T(8,128)(2,1)S(1)}, bf16[64,5120]{1,0:T(8,128)(2,1)}, u32[]{:S(2)}) %copy-start.2) | copy-done | bytes 655384
  9.4 0.6 cut_expansion.1
  10.1 0.0 copy-start.12
  10.1 4.0 %all-to-all-done.2.ups = bf16[4,64,128]{2,1,0:T(8,128)(2,1)S(1)} async-done(((bf16[4,64,128]{2,1,0:T(8,128)(2,1)}), bf16[4,64,128]{2,1,0:T(8,128)(2,1)S(1)}, u32[]{:S(2)}, u32[]{:S(2)}) %all-to-all-start.2) | async-done | bytes 65568 | tf_op jit(solution)/shard_map/all_to_all | solution.py:225
  14.1 3.3 %all-to-all-start = ((bf16[4,16,640]{2,1,0:T(8,128)(2,1)}), bf16[4,16,640]{2,1,0:T(8,128)(2,1)S(1)}, u32[]{:S(2)}, u32[]{:S(2)}) async-start(bf16[4,16,640]{2,1,0:T(8,128)(2,1)} %cut_expansion.1), calls=%async_computation | async-start | bytes 163840 | tf_op jit(solution)/shard_map/all_to_all | solution.py:225
  17.4 0.0 copy-start.9
  17.4 1.0 %copy-done.9 = bf16[128,1280]{1,0:T(8,128)(2,1)S(1)} copy-done((bf16[128,1280]{1,0:T(8,128)(2,1)S(1)}, bf16[128,1280]{1,0:T(8,128)(2,1)}, u32[]{:S(2)}) %copy-start.9) | copy-done | bytes 327704
  18.4 1.2 %weight_grads.1 = bf16[4,64,1280]{2,1,0:T(8,128)(2,1)} custom-call(bf16[4,64,128]{2,1,0:T(8,128)(2,1)S(1)} %all-to-all-done.2.ups, bf16[128,1280]{1,0:T(8,128)(2,1)S(1)} %copy-done.9), custom_call_target="tpu_custom_call" | custom-call | flops 83886080 | bytes 983040 | tf_op jit(solution)/shard_map/weight_grads/pallas_call | solution.py:74
  19.5 3.6 %all-to-all-done = bf16[4,16,640]{2,1,0:T(8,128)(2,1)S(1)} async-done(((bf16[4,16,640]{2,1,0:T(8,128)(2,1)}), bf16[4,16,640]{2,1,0:T(8,128)(2,1)S(1)}, u32[]{:S(2)}, u32[]{:S(2)}) %all-to-all-start) | async-done | bytes 81952 | tf_op jit(solution)/shard_map/all_to_all | solution.py:225
  23.2 3.5 %all-to-all-start.3 = ((bf16[4,64,1280]{2,1,0:T(8,128)(2,1)}), bf16[4,64,1280]{2,1,0:T(8,128)(2,1)S(1)}, u32[]{:S(2)}, u32[]{:S(2)}) async-start(bf16[4,64,1280]{2,1,0:T(8,128)(2,1)} %weight_grads.1), calls=%async_computation.3 | async-start | bytes 1310720 | tf_op jit(solution)/shard_map/all_to_all | solution.py:225
  26.6 0.0 copy-done.12
  26.7 0.0 copy-start
  26.7 14.9 %all-to-all-done.3.grads = bf16[4,64,1280]{2,1,0:T(8,128)(2,1)S(1)} async-done(((bf16[4,64,1280]{2,1,0:T(8,128)(2,1)}), bf16[4,64,1280]{2,1,0:T(8,128)(2,1)S(1)}, u32[]{:S(2)}, u32[]{:S(2)}) %all-to-all-start.3) | async-done | bytes 655392 | tf_op jit(solution)/shard_map/all_to_all | solution.py:225
  41.6 1.0 %broadcast_in_dim.8 = bf16[8,80,640]{2,1,0:T(8,128)(2,1)} broadcast(bf16[80,640]{1,0:T(8,128)(2,1)S(1)} %fusion.1), dimensions={1,2} | broadcast | bytes 921600 | tf_op jit(solution)/shard_map/broadcast_in_dim | solution.py:228
  42.6 0.0 copy-start.1
  42.6 3.9 %all-to-all-start.1 = ((bf16[8,80,640]{2,1,0:T(8,128)(2,1)}), bf16[8,80,640]{2,1,0:T(8,128)(2,1)S(1)}, u32[]{:S(2)}, u32[]{:S(2)}) async-start(bf16[8,80,640]{2,1,0:T(8,128)(2,1)} %broadcast_in_dim.8), calls=%async_computation.1 | async-start | bytes 1638400 | tf_op jit(solution)/shard_map/all_to_all | solution.py:225
  46.4 0.1 copy.14
  46.5 0.1 reshape_squeeze.3
  46.6 0.1 pad_add_fusion.rows
  46.7 0.0 copy-done
  46.7 0.4 own_places.1
  47.1 0.0 copy-start.7
  47.1 0.7 copy-done.7
  47.8 0.0 copy-done.1
  47.8 0.7 kept_rows.1.ship
  48.5 0.0 copy-start.10
  48.5 0.0 copy-start.11
  48.5 10.9 %all-to-all-done.1.exp_ref = bf16[8,80,640]{2,1,0:T(8,128)(2,1)S(1)} async-done(((bf16[8,80,640]{2,1,0:T(8,128)(2,1)}), bf16[8,80,640]{2,1,0:T(8,128)(2,1)S(1)}, u32[]{:S(2)}, u32[]{:S(2)}) %all-to-all-start.1) | async-done | bytes 819232 | tf_op jit(solution)/shard_map/all_to_all | solution.py:225
  59.4 0.9 %broadcast_in_dim.11 = bf16[8,8,5120]{2,1,0:T(8,128)(2,1)} broadcast(bf16[8,5120]{1,0:T(8,128)(2,1)S(1)} %kept_rows.1.ship), dimensions={1,2} | broadcast | bytes 737280 | tf_op jit(solution)/shard_map/broadcast_in_dim | solution.py:228
  60.3 4.2 %all-to-all-start.4 = ((bf16[8,8,5120]{2,1,0:T(8,128)(2,1)}), bf16[8,8,5120]{2,1,0:T(8,128)(2,1)}, u32[]{:S(2)}, u32[]{:S(2)}) async-start(bf16[8,8,5120]{2,1,0:T(8,128)(2,1)} %broadcast_in_dim.11), calls=%async_computation.4 | async-start | bytes 1310720 | tf_op jit(solution)/shard_map/all_to_all | solution.py:225
  64.5 0.6 fusion.7
  65.1 1.5 %copy.15 = s32[64,80]{0,1:T(8,128)} copy(s32[64,80]{1,0:T(8,128)} %fusion.7) | data formatting | bytes 40960 | tf_op jit(solution)/shard_map/reshape | solution.py:259
  66.6 0.9 %reshape.31.idx_row = s32[1,5120]{1,0:T(1,128)S(1)} reshape(s32[80,64]{1,0:T(8,128)} %bitcast.22) | data formatting | bytes 40960 | tf_op jit(solution)/shard_map/reshape | solution.py:259
  67.4 0.0 copy-done.10
  67.4 0.0 copy-done.11
  67.4 0.0 copy-start.8
  67.5 1.0 %places.1 = (bf16[64,5120]{1,0:T(8,128)(2,1)S(1)}, bf16[64,5120]{1,0:T(8,128)(2,1)S(1)}) custom-call(s32[8]{0:T(128)S(1)} %copy-done.10, s32[8]{0:T(128)S(1)} %copy-done.11, s32[1,5120]{1,0:T(1,128)S(1)} %reshape.31.idx_row, bf16[1152,256]{1,0:T(8,128)(2,1)S(1)} %copy-done), custom_call_target="tpu_custom_call" | custom-call | flops 83886080 | bytes 1310720 | tf_op jit(solution)/shard_map/places/pallas_call | solution.py:74
  68.5 0.0 copy-start.3
  68.5 0.8 %copy-done.3 = bf16[64,5120]{1,0:T(8,128)(2,1)} copy-done((bf16[64,5120]{1,0:T(8,128)(2,1)}, bf16[64,5120]{1,0:T(8,128)(2,1)S(1)}, u32[]{:S(2)}) %copy-start.3) | copy-done | bytes 655384
  69.3 0.0 copy-start.5
  69.3 1.0 %input_grads.1 = bf16[128,1280]{1,0:T(8,128)(2,1)} custom-call(bf16[8,80,640]{2,1,0:T(8,128)(2,1)S(1)} %all-to-all-done.1.exp_ref, bf16[4,64,128]{2,1,0:T(8,128)(2,1)S(1)} %all-to-all-done.2.ups), custom_call_target="tpu_custom_call" | custom-call | flops 83886080 | bytes 983040 | tf_op jit(solution)/shard_map/input_grads/pallas_call | solution.py:74
  70.4 0.0 copy-done.5
  70.4 0.0 copy-done.8
  70.4 0.0 copy-start.4
  70.4 1.6 %new_momentums.1 = f32[64,5120]{1,0:T(8,128)} custom-call(f32[64,5120]{1,0:T(8,128)S(1)} %bitcast.19, bf16[64,2560]{1,0:T(8,128)(2,1)S(1)} %copy-done.8, bf16[1152,256]{1,0:T(8,128)(2,1)S(1)} %copy-done, bf16[4,64,1280]{2,1,0:T(8,128)(2,1)S(1)} %all-to-all-done.3.grads, bf16[8,5120]{1,0:T(8,128)(2,1)S(1)} %kept_rows.1.ship), custom_call_target="tpu_custom_call" | custom-call | flops 125829120 | bytes 3276800 | tf_op jit(solution)/shard_map/new_momentums/pallas_call | solution.py:74
  72.0 3.7 %all-to-all-done.4.ships = bf16[8,8,5120]{2,1,0:T(8,128)(2,1)} async-done(((bf16[8,8,5120]{2,1,0:T(8,128)(2,1)}), bf16[8,8,5120]{2,1,0:T(8,128)(2,1)}, u32[]{:S(2)}, u32[]{:S(2)}) %all-to-all-start.4) | async-done | bytes 655392 | tf_op jit(solution)/shard_map/all_to_all | solution.py:225
  75.6 0.0 copy-done.4
  75.6 0.0 copy-start.6
  75.6 1.1 %copy-done.6 = bf16[64,5120]{1,0:T(8,128)(2,1)S(1)} copy-done((bf16[64,5120]{1,0:T(8,128)(2,1)S(1)}, bf16[64,5120]{1,0:T(8,128)(2,1)}, u32[]{:S(2)}) %copy-start.6) | copy-done | bytes 655384
  76.7 4.6 %updates.1 = f32[64,5120]{1,0:T(8,128)} custom-call(bf16[64,5120]{1,0:T(8,128)(2,1)S(1)} %copy-done.4, bf16[64,5120]{1,0:T(8,128)(2,1)S(1)} %copy-done.6, bf16[1152,256]{1,0:T(8,128)(2,1)S(1)} %copy-done, bf16[8,8,5120]{2,1,0:T(8,128)(2,1)} %all-to-all-done.4.ships), custom_call_target="tpu_custom_call" | custom-call | flops 671088640 | bytes 2621440 | tf_op jit(solution)/shard_map/updates/pallas_call | solution.py:74
  (2 shorter events, 0.0 us)
Async XLA Ops:
  2.0 12.1 %all-to-all-start.2 = ((bf16[4,64,128]{2,1,0:T(8,128)(2,1)}), bf16[4,64,128]{2,1,0:T(8,128)(2,1)S(1)}, u32[]{:S(2)}, u32[]{:S(2)}) async-start(bf16[4,64,128]{2,1,0:T(8,128)(2,1)} %broadcast_in_dim.9), calls=%async_computation.2 | async-start | bytes 131072 | tf_op jit(solution)/shard_map/all_to_all | solution.py:225
  8.3 1.1 %copy-start.2 = (bf16[64,5120]{1,0:T(8,128)(2,1)S(1)}, bf16[64,5120]{1,0:T(8,128)(2,1)}, u32[]{:S(2)}) copy-start(bf16[64,5120]{1,0:T(8,128)(2,1)} %exp_ref.1) | copy-start | bytes 1966084
  10.1 16.6 %copy-start.12 = (s32[1,1,80,8]{2,3,1,0:T(8,128)S(1)}, s32[1,1,80,8]{2,3,1,0:T(8,128)}, u32[]{:S(2)}) copy-start(s32[1,1,80,8]{2,3,1,0:T(8,128)} %param.14) | copy-start | bytes 7684
  14.1 9.1 %all-to-all-start = ((bf16[4,16,640]{2,1,0:T(8,128)(2,1)}), bf16[4,16,640]{2,1,0:T(8,128)(2,1)S(1)}, u32[]{:S(2)}, u32[]{:S(2)}) async-start(bf16[4,16,640]{2,1,0:T(8,128)(2,1)} %cut_expansion.1), calls=%async_computation | async-start | bytes 163840 | tf_op jit(solution)/shard_map/all_to_all | solution.py:225
  17.4 1.0 %copy-start.9 = (bf16[128,1280]{1,0:T(8,128)(2,1)S(1)}, bf16[128,1280]{1,0:T(8,128)(2,1)}, u32[]{:S(2)}) copy-start(bf16[128,1280]{1,0:T(8,128)(2,1)} %act.1) | copy-start | bytes 983044
  23.2 18.5 %all-to-all-start.3 = ((bf16[4,64,1280]{2,1,0:T(8,128)(2,1)}), bf16[4,64,1280]{2,1,0:T(8,128)(2,1)S(1)}, u32[]{:S(2)}, u32[]{:S(2)}) async-start(bf16[4,64,1280]{2,1,0:T(8,128)(2,1)} %weight_grads.1), calls=%async_computation.3 | async-start | bytes 1310720 | tf_op jit(solution)/shard_map/all_to_all | solution.py:225
  26.7 20.0 %copy-start = (bf16[1152,256]{1,0:T(8,128)(2,1)S(1)}, bf16[1152,256]{1,0:T(8,128)(2,1)}, u32[]{:S(2)}) copy-start(bf16[1152,256]{1,0:T(8,128)(2,1)} %constant.14.clone.tab) | copy-start | bytes 1769476
  42.6 5.3 %copy-start.1 = (f32[1,64,5120]{2,1,0:T(8,128)S(1)}, f32[1,64,5120]{2,1,0:T(8,128)}, u32[]{:S(2)}) copy-start(f32[1,64,5120]{2,1,0:T(8,128)} %param.13) | copy-start | bytes 3932164
  42.6 16.8 %all-to-all-start.1 = ((bf16[8,80,640]{2,1,0:T(8,128)(2,1)}), bf16[8,80,640]{2,1,0:T(8,128)(2,1)S(1)}, u32[]{:S(2)}, u32[]{:S(2)}) async-start(bf16[8,80,640]{2,1,0:T(8,128)(2,1)} %broadcast_in_dim.8), calls=%async_computation.1 | async-start | bytes 1638400 | tf_op jit(solution)/shard_map/all_to_all | solution.py:225
  47.1 0.7 copy-start.7
  48.5 18.9 %copy-start.10 = (s32[8]{0:T(128)S(1)}, s32[8]{0:T(128)}, u32[]{:S(2)}) copy-start(s32[8]{0:T(128)} %mask.1) | copy-start | bytes 100
  48.5 18.9 %copy-start.11 = (s32[8]{0:T(128)S(1)}, s32[8]{0:T(128)}, u32[]{:S(2)}) copy-start(s32[8]{0:T(128)} %tally.1) | copy-start | bytes 100
  60.3 15.4 %all-to-all-start.4 = ((bf16[8,8,5120]{2,1,0:T(8,128)(2,1)}), bf16[8,8,5120]{2,1,0:T(8,128)(2,1)}, u32[]{:S(2)}, u32[]{:S(2)}) async-start(bf16[8,8,5120]{2,1,0:T(8,128)(2,1)} %broadcast_in_dim.11), calls=%async_computation.4 | async-start | bytes 1310720 | tf_op jit(solution)/shard_map/all_to_all | solution.py:225
  67.4 2.9 %copy-start.8 = (bf16[64,2560]{1,0:T(8,128)(2,1)S(1)}, bf16[64,2560]{1,0:T(8,128)(2,1)}, u32[]{:S(2)}) copy-start(bf16[64,2560]{1,0:T(8,128)(2,1)} %copy-done.7) | copy-start | bytes 983044
  68.5 0.8 %copy-start.3 = (bf16[64,5120]{1,0:T(8,128)(2,1)}, bf16[64,5120]{1,0:T(8,128)(2,1)S(1)}, u32[]{:S(2)}) copy-start(bf16[64,5120]{1,0:T(8,128)(2,1)S(1)} %get-tuple-element.9.p_hi) | copy-start | bytes 1966084
  69.3 1.0 %copy-start.5 = (bf16[64,5120]{1,0:T(8,128)(2,1)}, bf16[64,5120]{1,0:T(8,128)(2,1)S(1)}, u32[]{:S(2)}) copy-start(bf16[64,5120]{1,0:T(8,128)(2,1)S(1)} %get-tuple-element.10.p_lo) | copy-start | bytes 1966084
  70.4 5.3 %copy-start.4 = (bf16[64,5120]{1,0:T(8,128)(2,1)S(1)}, bf16[64,5120]{1,0:T(8,128)(2,1)}, u32[]{:S(2)}) copy-start(bf16[64,5120]{1,0:T(8,128)(2,1)} %copy-done.3) | copy-start | bytes 1966084
  75.6 1.1 %copy-start.6 = (bf16[64,5120]{1,0:T(8,128)(2,1)S(1)}, bf16[64,5120]{1,0:T(8,128)(2,1)}, u32[]{:S(2)}) copy-start(bf16[64,5120]{1,0:T(8,128)(2,1)} %copy-done.5) | copy-start | bytes 1966084

commit v3 on v2

v3 whole, which is shorter than its diff:
```python
import functools

import jax
import jax.numpy as jnp
import numpy as np
from jax import lax
from jax.experimental import pallas as pl
from jax.experimental.pallas import tpu as pltpu
from jax.sharding import PartitionSpec as P

momentum_decay = 0.9
B = 64
G = 256
F32 = jnp.float32
BF16 = jnp.bfloat16
VMEM_LIMIT = 24 * 1024 * 1024
FIRST_LIMIT = 63 * 1024 * 1024

VM = pl.BlockSpec(memory_space=pltpu.VMEM)
SM = pl.BlockSpec(memory_space=pltpu.SMEM)
ANY = pl.BlockSpec(memory_space=pl.ANY)


def cosine_table():
    freqs = jnp.arange(64, dtype=jnp.float32)[:, None]
    places = jnp.arange(64, dtype=jnp.float32)[None, :]
    cosines = jnp.cos(jnp.pi * (places + 0.5) * freqs / 64.0) * jnp.sqrt(2.0 / 64.0)
    return cosines.at[0].multiply(jnp.sqrt(0.5))


def cosine_np():
    f = np.arange(B)[:, None]
    a = np.arange(B)[None, :]
    c = np.cos(np.pi * (a + 0.5) * f / B) * np.sqrt(2.0 / B)
    c[0] *= np.sqrt(0.5)
    return c


def halves(c):
    hi = np.asarray(c, dtype=np.float32).astype(jnp.bfloat16)
    lo = (np.asarray(c, np.float64) - hi.astype(np.float64)).astype(np.float32).astype(jnp.bfloat16)
    return hi, lo


def constants():
    hi, lo = halves(cosine_np())
    eye = np.eye(G // B)
    kron = lambda x: np.kron(eye, np.asarray(x, np.float32)).astype(jnp.bfloat16)
    tall = np.zeros((2 * B, G), jnp.bfloat16)
    tall[:B, :B], tall[B:, :B] = hi.T, lo.T
    return jnp.asarray(np.concatenate([kron(hi.T), kron(lo.T), kron(hi), kron(lo), tall], axis=0))


def fwd(tab, i):
    return tab[i * G : (i + 1) * G, :]


def inv(tab, i):
    return tab[(2 + i) * G : (3 + i) * G, :]


def tall(tab):
    return tab[4 * G : 4 * G + 2 * B, :B]


def dot(a, b):
    return jnp.dot(a, b, preferred_element_type=F32)


def split(x):
    hi = x.astype(BF16)
    return hi, (x - hi.astype(F32)).astype(BF16)


def call(body, out_shape, ins, in_specs, out_specs, scratch=(), flops=0, nbytes=0, name=None, limit=VMEM_LIMIT):
    return pl.pallas_call(
        body,
        out_shape=out_shape,
        in_specs=in_specs,
        out_specs=out_specs,
        scratch_shapes=scratch,
        compiler_params=pltpu.CompilerParams(vmem_limit_bytes=limit),
        cost_estimate=pl.CostEstimate(flops=flops, bytes_accessed=nbytes, transcendentals=0),
        name=name,
    )(*ins)


def up_grad(switch, slope):
    v = switch.astype(F32)
    return (slope.astype(F32) * (v * jax.nn.sigmoid(v))).astype(BF16)


def first_body(n_t, cp, cols, nr, pos, switch, slope, exp_ref, *refs):
    outs = refs[:n_t]
    switch_v, slope_v, exp_v, sems = refs[n_t:]
    rep, ten = pos[0], pos[1]
    r0 = pl.multiple_of((rep // cp) * nr, nr)
    copies = [
        pltpu.make_async_copy(src, dst, sems.at[i])
        for i, (src, dst) in enumerate(
            [(switch, switch_v), (slope, slope_v), (exp_ref.at[pl.ds(r0, nr), :], exp_v)]
        )
    ]
    for copy in copies:
        copy.start()
    copies[0].wait()
    copies[1].wait()
    up = up_grad(switch_v[...], slope_v[...])
    for k in range(n_t):
        outs[k][:B, :] = up
    copies[2].wait()
    nc = cols // cp
    for k in range(n_t):
        c0 = lax.rem(ten + k, n_t) * cols + lax.rem(rep, cp) * nc
        for j in range(nc // 128):
            at = pl.multiple_of(c0 + j * 128, 128)
            outs[k][B + j * nr : B + (j + 1) * nr, :] = exp_v[:, pl.ds(at, 128)]


def grads_body(n_t, switch, slope, act, *refs):
    ups, outs = refs[: n_t - 1], refs[n_t - 1 :]
    up = jnp.concatenate([up_grad(switch[...], slope[...])] + [u[:B, :] for u in ups], axis=0)
    for c in range(0, act.shape[1], G):
        g = dot(up, act[:, c : c + G])
        for k in range(n_t):
            outs[k][:, c : c + G] = g[k * B : (k + 1) * B].astype(outs[k].dtype)


def bundle_body(n_t, keep, after, lines, *refs):
    parts, out = refs[:n_t], refs[n_t]
    n = parts[0].shape[0] - B
    for k in range(n_t):
        out[k * n : (k + 1) * n, :] = parts[k][B:, :]
    blocks = lines.shape[1]
    rows = jnp.concatenate([lines[...].astype(F32), jnp.zeros((keep, 128 - blocks), F32)], axis=1)
    out[n_t * n :, :] = jnp.concatenate([rows, jnp.zeros((16 - keep, 128), F32)], axis=0).astype(BF16)


def join_body(*refs):
    for i, ref in enumerate(refs[:-1]):
        refs[-1][i] = ref[...]


def own_body(n_r, keep, pos, mask, tally, rows, tab, p_ref, a_ref, tab_ref, w_ref, mask_s, tally_s, sems):
    copies = [pltpu.make_async_copy(mask, mask_s, sems.at[0]), pltpu.make_async_copy(tally, tally_s, sems.at[1])]
    for copy in copies:
        copy.start()
    tab_ref[...] = tab[...]
    freq = lax.broadcasted_iota(jnp.int32, (B, 2 * B), 0)
    term = lax.broadcasted_iota(jnp.int32, (B, 2 * B), 1) // (B // 2)
    for g in range(rows.shape[0]):
        hot = jnp.where(freq == rows[g : g + 1, :], 1.0, 0.0).astype(BF16)
        y = dot(tall(tab), hot)
        p = jnp.where(term == 3, 0.0, jnp.where(term == 1, y[B:], y[:B]))
        p_ref[:, g * 2 * B : (g + 1) * 2 * B] = p.astype(BF16)
        a_ref[g * B : (g + 1) * B, :] = jnp.concatenate([p, p], axis=0).T[:B].astype(BF16)
    for copy in copies:
        copy.wait()
    total, alive = jnp.float32(0), jnp.float32(0)
    for r in range(n_r):
        m = mask_s[r].astype(F32)
        total = total + m * tally_s[r].astype(F32)
        alive = alive + m
    half = n_r // 2
    place = (lax.broadcasted_iota(jnp.int32, (8, 2 * B), 1) // keep) % n_r
    w = jnp.zeros((8, 2 * B), F32)
    for i in range(n_r):
        r = pos[0] ^ (2 * (i % half) + i // half)
        w = jnp.where(place == i, mask_s[r].astype(F32) * tally_s[r].astype(F32), w)
    w_ref[...] = w * (jnp.full((8, 2 * B), alive) / jnp.full((8, 2 * B), total))


def kept_body(n_t, keep, pos, vel, a_ref, tab, after, *refs):
    grads, ship_ref = refs[:n_t], refs[n_t]
    cols = grads[0].shape[1]
    ng = cols // G
    lane_block = lax.broadcasted_iota(jnp.int32, (keep, G), 1) // B
    sel = []
    for k in range(n_t):
        c0 = lax.rem(pos[1] + k, n_t) * cols
        for i in range(ng):
            at = pl.multiple_of(c0 + i * G, G)
            moment = momentum_decay * vel[:, pl.ds(at, G)] + grads[k][:, i * G : (i + 1) * G].astype(F32)
            hi, lo = split(moment)
            y = dot(a_ref[pl.ds(pl.multiple_of(at // (G // B), B), B), :], jnp.concatenate([hi, lo], axis=0))
            y = y[: B // 2] + y[B // 2 :]
            got = y[:keep]
            for j in range(1, G // B):
                got = jnp.where(lane_block == j, y[j * keep : (j + 1) * keep], got)
            sel.append(got)
    hi, lo = split(jnp.concatenate(sel, axis=0))
    n = n_t * ng * keep
    y = dot(jnp.concatenate([hi, lo], axis=0), fwd(tab, 0))
    y = y[:n] + y[n:] + dot(hi, fwd(tab, 1))
    for k in range(n_t):
        c0 = pl.multiple_of(lax.rem(pos[1] + k, n_t) * cols, G)
        ship_ref[:, pl.ds(c0, cols)] = jnp.concatenate(
            [y[(k * ng + i) * keep : (k * ng + i + 1) * keep] for i in range(ng)], axis=1
        ).astype(BF16)


def return_body(n_t, keep, pos, vel, p_ref, tab, ship, *refs):
    grads, new_ref = refs[:n_t], refs[n_t]
    cols = grads[0].shape[1]
    ng = cols // G
    lane_block = lax.broadcasted_iota(jnp.int32, (keep, G), 1) // B
    kept = ship[...].astype(F32)
    total = kept.shape[1] // G
    kept = jnp.concatenate([kept[:, g * G : (g + 1) * G] for g in range(total)], axis=0).astype(BF16)
    q = dot(kept, inv(tab, 0)) + dot(kept, inv(tab, 1))
    for g in range(total):
        own = q[g * keep : (g + 1) * keep]
        spread = jnp.concatenate(
            [jnp.where(lane_block == j, own, 0.0) for j in range(G // B)], axis=0
        )
        hi, lo = split(spread)
        w = jnp.concatenate([hi, hi, lo, jnp.zeros_like(lo)], axis=0)
        back = dot(p_ref[:, g * 2 * B : (g + 1) * 2 * B], w)
        cut = slice(g * G, (g + 1) * G)
        new_ref[:, cut] = momentum_decay * vel[:, cut] - back
    for k in range(n_t):
        c0 = lax.rem(pos[1] + k, n_t) * cols
        for i in range(ng):
            at = pl.multiple_of(c0 + i * G, G)
            new_ref[:, pl.ds(at, G)] += grads[k][:, i * G : (i + 1) * G].astype(F32)


def places_body(n_r, keep, w_ref, mine, other, tab, hi_ref, lo_ref):
    half = n_r // 2
    w = w_ref[:1, :]
    last = mine.shape[1] - 16
    rows = [ref[i, last:, :].astype(F32)[:keep] for ref in (mine, other) for i in range(half)]
    rows = jnp.concatenate(rows + rows, axis=0).T
    freq = lax.broadcasted_iota(jnp.int32, (B, 2 * B), 0).astype(F32)
    first = lax.broadcasted_iota(jnp.int32, (1, 2 * B), 1) < B
    for c in range(hi_ref.shape[1] // (2 * B)):
        num = jnp.where(first, rows[2 * c : 2 * c + 1], rows[2 * c + 1 : 2 * c + 2])
        hot = jnp.where(freq == num, 1.0, 0.0).astype(BF16)
        y = dot(tall(tab), hot)
        hi, lo = split((y[:B] + y[B:]) * w)
        hi_ref[:, c * 2 * B : (c + 1) * 2 * B] = hi
        lo_ref[:, c * 2 * B : (c + 1) * 2 * B] = lo


def update_body(n_r, keep, p_hi, p_lo, tab, mine, other, out, hi_ref, lo_ref):
    per = n_r * keep
    nb = G // B
    width = nb * per
    half = n_r // 2
    ng = out.shape[1] // G
    lane_block = lax.broadcasted_iota(jnp.int32, (per, G), 1) // B
    for g in range(ng):
        cut = slice(g * G, (g + 1) * G)
        s = jnp.concatenate(
            [ref[i, :, cut].astype(F32) for ref in (mine, other) for i in range(half)], axis=0
        )
        w = jnp.concatenate(
            [jnp.where(lane_block == j, s, 0.0).astype(BF16) for j in range(nb)], axis=0
        )
        wide = slice(g * width, (g + 1) * width)
        y = dot(jnp.concatenate([p_hi[:, wide], p_lo[:, wide]], axis=0), w)
        hi, lo = split(y[:B] + y[B:])
        hi_ref[g * B : (g + 1) * B, :] = hi
        lo_ref[g * B : (g + 1) * B, :] = lo
    z = dot(hi_ref[...], inv(tab, 0)) + dot(lo_ref[...], inv(tab, 0)) + dot(hi_ref[...], inv(tab, 1))
    for g in range(ng):
        out[:, g * G : (g + 1) * G] = z[g * B : (g + 1) * B]


def input_grad_body(n_t, n_r, cp, pos, mine, other, *refs):
    ups, out, held = refs[:n_t], refs[n_t], refs[n_t + 1]
    nc = out.shape[1] // cp
    nr = B // (n_r // cp)
    tiles = nc // 128
    for h, ref in enumerate((mine, other)):
        for i in range(n_r // 2):
            src = pos[0] ^ (2 * i + h)
            r0 = (src // cp) * nr
            c0 = lax.rem(src, cp) * nc
            for k in range(n_t):
                for j in range(tiles):
                    at = (k * tiles + j) * nr
                    held[
                        pl.ds(pl.multiple_of(k * B + r0, nr), nr), pl.ds(pl.multiple_of(c0 + j * 128, 128), 128)
                    ] = ref[i, at : at + nr, :]
    up = jnp.concatenate([u[:B, :] for u in ups], axis=0).T
    for c in range(0, out.shape[1], G):
        out[:, c : c + G] = dot(up, held[:, c : c + G]).astype(BF16)


def per_device(n_t, n_r, act, switch, slope, exp, vel, lines, mask, tally):
    cols = act.shape[1]
    width = exp.shape[1]
    tok = act.shape[0]
    keep = lines.shape[3]
    blocks = width // B
    groups = width // G
    cp = 2
    rp = n_r // cp
    half = n_r // 2
    tab = constants()
    rep = lax.axis_index("replica").astype(jnp.int32)
    ten = lax.axis_index("tensor").astype(jnp.int32)
    pos = jnp.stack([rep, ten])

    def shift(x, k):
        return lax.ppermute(x, "tensor", [(i, (i + k) % n_t) for i in range(n_t)])

    def shifts(xs, sign):
        order = sorted(range(1, n_t), key=lambda k: -min(k, n_t - k))
        got = {0: xs[0]}
        for k in order:
            got[k] = shift(xs[k], sign * k)
        return [got[k] for k in range(n_t)]

    def swap(x, m):
        return lax.ppermute(x, "replica", [(i, i ^ m) for i in range(n_r)])

    def share(x, name):
        parts = [x] + [swap(x, 2 * i) for i in range(1, half)]
        mine = call(
            join_body,
            jax.ShapeDtypeStruct((half,) + x.shape, x.dtype),
            parts,
            [VM] * half,
            VM,
            name=name,
        )
        return mine, swap(mine, 1)

    tiles = cols // cp // 128
    nr = B // rp
    outs = call(
        functools.partial(first_body, n_t, cp, cols, nr),
        [jax.ShapeDtypeStruct((B + tiles * nr, 128), BF16)] * n_t,
        (pos, switch.T, slope.T, exp),
        [SM, ANY, ANY, ANY],
        [VM] * n_t,
        scratch=[
            pltpu.VMEM((B, tok), BF16),
            pltpu.VMEM((B, tok), BF16),
            pltpu.VMEM((nr, width), BF16),
            pltpu.SemaphoreType.DMA((3,)),
        ],
        flops=1 << 32,
        name="up_grads",
        limit=FIRST_LIMIT,
    )
    parts = shifts(outs, 1)

    grads = call(
        functools.partial(grads_body, n_t),
        [jax.ShapeDtypeStruct((B, cols), F32)] + [jax.ShapeDtypeStruct((B, cols), BF16)] * (n_t - 1),
        (switch.T, slope.T, act, *parts[1:]),
        [VM] * (n_t + 2),
        [VM] * n_t,
        flops=2 * n_t * B * tok * cols,
        nbytes=act.size * 2 + n_t * B * cols * 2,
        name="weight_grads",
    )
    made = grads[1]
    grads = shifts(grads, -1)

    own = lines[0, 0].T
    bundle = call(
        functools.partial(bundle_body, n_t, keep),
        jax.ShapeDtypeStruct((n_t * tiles * nr + 16, 128), BF16),
        (made, own, *parts),
        [ANY] + [VM] * (n_t + 1),
        VM,
        name="bundle",
    )
    mine, other = share(bundle, "join_bundles")

    own_rows = jnp.concatenate([lines[0, 0].reshape(groups, B // 2)] * 4, axis=1)
    p_own, a_own, tab, shares = call(
        functools.partial(own_body, n_r, keep),
        [
            jax.ShapeDtypeStruct((B, groups * 2 * B), BF16),
            jax.ShapeDtypeStruct((groups * B, 2 * B), BF16),
            jax.ShapeDtypeStruct(tab.shape, BF16),
            jax.ShapeDtypeStruct((8, 2 * B), F32),
        ],
        (pos, mask, tally, own_rows, tab),
        [SM, ANY, ANY, VM, VM],
        [VM] * 4,
        scratch=[pltpu.SMEM((n_r,), jnp.int32)] * 2 + [pltpu.SemaphoreType.DMA((2,))],
        name="own_places",
    )
    p_hi, p_lo = call(
        functools.partial(places_body, n_r, keep),
        [jax.ShapeDtypeStruct((B, blocks * n_r * keep), BF16)] * 2,
        (shares, mine, other, tab),
        [VM] * 4,
        [VM, VM],
        name="places",
    )
    input_grad = call(
        functools.partial(input_grad_body, n_t, n_r, cp),
        jax.ShapeDtypeStruct((tok, cols), BF16),
        (pos, mine, other, *parts),
        [SM] + [VM] * (2 + n_t),
        VM,
        scratch=[pltpu.VMEM((n_t * B, cols), BF16)],
        flops=2 * tok * n_t * B * cols,
        nbytes=(n_t * B * cols + tok * cols) * 2,
        name="input_grads",
    )

    ship = call(
        functools.partial(kept_body, n_t, keep),
        jax.ShapeDtypeStruct((keep, width), BF16),
        (pos, vel[0], a_own, tab, p_hi, *grads),
        [SM] + [VM] * 3 + [ANY] + [VM] * n_t,
        VM,
        flops=6 * B * B * width,
        nbytes=B * width * 6,
        name="kept_rows",
    )
    mine, other = share(ship, "join_kept")
    new = call(
        functools.partial(return_body, n_t, keep),
        jax.ShapeDtypeStruct((B, width), F32),
        (pos, vel[0], p_own, tab, ship, *grads),
        [SM] + [VM] * (4 + n_t),
        VM,
        flops=6 * B * B * width,
        nbytes=B * width * 10,
        name="new_momentums",
    )
    update = call(
        functools.partial(update_body, n_r, keep),
        jax.ShapeDtypeStruct((B, width), F32),
        (p_hi, p_lo, tab, mine, other),
        [VM] * 5,
        VM,
        scratch=[pltpu.VMEM((groups * B, G), BF16)] * 2,
        flops=8 * B * G * width,
        nbytes=B * width * 8,
        name="updates",
    )
    return input_grad, new[None], update


def per_device_plain(
    projection_inputs,
    switch_logits_raw,
    inner_neuron_slope,
    expansion_matrix,
    velocity_buffer,
    sent_spectral_lines,
    participant_mask,
    token_tallies,
):
    highest = lax.Precision.HIGHEST
    up_grad = (
        inner_neuron_slope.astype(jnp.float32) * jax.nn.silu(switch_logits_raw.astype(jnp.float32))
    ).astype(jnp.bfloat16)
    partial_terms = jnp.dot(up_grad, expansion_matrix, preferred_element_type=jnp.float32)
    input_grad = lax.psum_scatter(partial_terms, "tensor", scatter_dimension=1, tiled=True).astype(
        jnp.bfloat16
    )
    grad_w = lax.dot_general(
        up_grad,
        lax.all_gather(projection_inputs, "tensor", axis=1, tiled=True),
        (((0,), (0,)), ((), ())),
        preferred_element_type=jnp.float32,
    )
    row_total_count = expansion_matrix.shape[0] // 64
    col_count = expansion_matrix.shape[1] // 64
    moment = momentum_decay * velocity_buffer[0] + grad_w
    cosines = cosine_table()
    blocks = moment.reshape(row_total_count, 64, col_count, 64).transpose(0, 2, 1, 3)
    coefficients = jnp.einsum("fa,ijab,gb->ijfg", cosines, blocks, cosines, precision=highest)
    freq_ids = jnp.arange(64, dtype=jnp.int32)
    own_rows = sent_spectral_lines[0]
    chosen = (own_rows[..., None] == freq_ids).astype(jnp.float32)
    shipped = jnp.einsum("ijkf,ijfg->ijkg", chosen, coefficients, precision=highest).astype(
        jnp.bfloat16
    )
    spectrum = jnp.einsum("ijkf,ijkg->ijfg", chosen, shipped.astype(jnp.float32), precision=highest)
    returned = jnp.einsum("fa,ijfg,gb->ijab", cosines, spectrum, cosines, precision=highest)
    new_moment = moment - returned.transpose(0, 2, 1, 3).reshape(moment.shape)
    worker_burdens = participant_mask.astype(jnp.float32) * token_tallies.astype(jnp.float32)
    worker_fractions = worker_burdens * (
        jnp.sum(participant_mask.astype(jnp.float32)) / jnp.sum(worker_burdens)
    )
    myself = lax.axis_index("replica")
    combined = lax.psum(worker_fractions[myself] * spectrum, "replica")
    update = jnp.einsum("fa,ijfg,gb->ijab", cosines, combined, cosines, precision=highest)
    update = update.transpose(0, 2, 1, 3).reshape(moment.shape)
    return (input_grad, new_moment[None], update)


def solution(mesh):
    n_t, n_r = mesh.shape["tensor"], mesh.shape["replica"]

    def device(*args):
        act, exp, lines = args[0], args[3], args[5]
        fits = (
            act.shape[1] % G == 0
            and act.shape[0] % 128 == 0
            and exp.shape[0] == B
            and lines.shape[3] == 8
            and n_r == 8
        )
        if not fits:
            return per_device_plain(*args)
        return per_device(n_t, n_r, *args)

    return jax.shard_map(
        device,
        mesh=mesh,
        in_specs=(
            P("replica", "tensor"),
            P("replica", "tensor"),
            P("replica", "tensor"),
            P("tensor", None),
            P("replica", "tensor", None),
            P("replica", "tensor", None, None),
            P(),
            P(),
        ),
        out_specs=(P("replica", "tensor"), P("replica", "tensor", None), P("tensor", None)),
        check_vma=False,
    )
```

time: 82.2 us -> 55.3 us (0.67)
  waiting for transfers between devices: 37.1 us -> 17.9 us
  local copies, waits for them, and re-layouts: 9.71 us -> 3.34 us
  starting transfers between devices: 21.1 us -> 19.1 us
  Pallas kernels: 11.2 us -> 12.7 us
    all_to_all x5 -> x0, waiting for transfers between devices: 37.1 us -> none  [trade(): return lax.all_to_all(x, axis, split_axis=0, concat_axis=0)]
    all_to_all x5 -> x0, starting transfers between devices: 21.1 us -> none  [trade(): return lax.all_to_all(x, axis, split_axis=0, concat_axis=0)]
    ppermute x0 -> x14, starting transfers between devices: none -> 19.1 us  [the longest x6 11.9 us: shift(): return lax.ppermute(x, 'tensor', [(i, (i + k) % n_t) for i in range(n_t)])]
    ppermute x0 -> x14, waiting for transfers between devices: none -> 17.9 us  [the longest x6 11 us: shift(): return lax.ppermute(x, 'tensor', [(i, (i + k) % n_t) for i in range(n_t)])]
    broadcast_in_dim x3 -> x0, local copies, waits for them, and re-layouts: 2.49 us -> none  [spread(): return trade(jnp.broadcast_to(x[None], (n,) + x.shape), axis)]
    unnamed x27 -> x23, local copies, waits for them, and re-layouts: 4.82 us -> 2.48 us
    reshape x2 -> x0, local copies, waits for them, and re-layouts: 2.33 us -> none  [per_device(): idx_all.reshape(n_r * keep, blocks).T.reshape(1, blocks * n_r * keep)]
    pallas_call x8 -> x11, Pallas kernels: 11.2 us -> 12.7 us  [call(): pl.pallas_call(body, out_shape=out_shape, in_specs=in_specs, out_specs=ou...]
  transfers between devices with their start and end apart: 5 -> 14, of which waited for: 5 -> 10; matrix products, arithmetic and copies ran while one was open for 4% -> 3% of each run, Pallas kernels for 8% -> 11%
where the time goes in v3:
time: 55.3 us; the launch traced here: 54.6 us
  starting transfers between devices  19.1 us (35%)
  waiting for transfers between devices  17.9 us (32%)
  Pallas kernels  12.7 us (23%)
  local copies, waits for them, and re-layouts  3.34 us (6%)
  between operations  0.79 us (1%)
  other arithmetic  0.7 us (1%)
    pallas_call x11, Pallas kernels, call(): pl.pallas_call(body, out_shape=out_shape, in_specs=in_specs, out_specs=ou...  12.7 us
    ppermute x6, starting transfers between devices, shift(): return lax.ppermute(x, 'tensor', [(i, (i + k) % n_t) for i in range(n_t)])  11.9 us
    ppermute x6, waiting for transfers between devices, shift(): return lax.ppermute(x, 'tensor', [(i, (i + k) % n_t) for i in range(n_t)])  11 us
    ppermute x8, starting transfers between devices, swap(): return lax.ppermute(x, 'replica', [(i, i ^ m) for i in range(n_r)])  7.25 us
    ppermute x8, waiting for transfers between devices, swap(): return lax.ppermute(x, 'replica', [(i, i ^ m) for i in range(n_r)])  6.94 us
    unnamed x23, local copies, waits for them, and re-layouts  2.48 us
  transfers between devices with their start and end apart: 14, of which 10 were waited for; matrix products, arithmetic and copies ran while one was open for 3% of the time, Pallas kernels for 11%

profile of v3, /device:TPU:0, one launch (start us, length us, event | category | flops | bytes accessed | tf_op | source)
XLA Modules:
  0.0 54.6 jit_solution(1165977672661440437)
XLA Ops:
  0.6 0.6 %pad_add_fusion.1.pos = s32[2]{0:T(128)} fusion(s32[1]{0:T(128)} %bitcast.1, s32[1]{0:T(128)} %bitcast), kind=kLoop, calls=%fused_computation.1 | loop fusion | flops 2 | bytes 16 | tf_op jit(solution)/shard_map/stack | solution.py:304
  1.3 0.0 copy-start.6
  1.3 0.0 copy-start.7
  1.3 0.0 copy-start.5
  1.3 0.0 copy-start.8
  1.3 0.0 copy-start.9
  1.3 0.0 copy-start.10
  1.3 2.4 %up_grads.1 = (bf16[144,128]{1,0:T(8,128)(2,1)}, bf16[144,128]{1,0:T(8,128)(2,1)}, bf16[144,128]{1,0:T(8,128)(2,1)}, bf16[144,128]{1,0:T(8,128)(2,1)}) custom-call(s32[2]{0:T(128)} %pad_add_fusion.1.pos, bf16[64,128]{1,0:T(8,128)(2,1)} %bitcast.14, bf16[64,128]{1,0:T(8,128)(2,1)} %bitcast.16, bf16[64,5120]{1,0:T(8,128)(2,1)} %exp_ref.1), custom_call_target="tpu_custom_call" | custom-call | flops 4294967296 | tf_op jit(solution)/shard_map/up_grads/pallas_call | solution.py:76
  3.7 0.0 copy-start.1
  3.8 3.1 %collective-permute-start = (bf16[144,128]{1,0:T(8,128)(2,1)}, bf16[144,128]{1,0:T(8,128)(2,1)S(1)}, u32[]{:S(2)}, u32[]{:S(2)}) collective-permute-start(bf16[144,128]{1,0:T(8,128)(2,1)} %get-tuple-element.17), channel_id=1, source_target_pairs={{0,1},{1,2},{2,3},{3,0},{4,5},{5,6},{6,7},{7,4},{8,9},{9,10},{10,1... | collective-permute-start | bytes 110600 | tf_op jit(solution)/shard_map/ppermute | solution.py:307
  6.8 2.6 %collective-permute-start.1 = (bf16[144,128]{1,0:T(8,128)(2,1)}, bf16[144,128]{1,0:T(8,128)(2,1)S(1)}, u32[]{:S(2)}, u32[]{:S(2)}) collective-permute-start(bf16[144,128]{1,0:T(8,128)(2,1)} %get-tuple-element.18), channel_id=1, source_target_pairs={{0,2},{1,3},{2,0},{3,1},{4,6},{5,7},{6,4},{7,5},{8,10},{9,11},{10,... | collective-permute-start | bytes 110600 | tf_op jit(solution)/shard_map/ppermute | solution.py:307
  9.4 1.3 %collective-permute-start.2 = (bf16[144,128]{1,0:T(8,128)(2,1)}, bf16[144,128]{1,0:T(8,128)(2,1)S(1)}, u32[]{:S(2)}, u32[]{:S(2)}) collective-permute-start(bf16[144,128]{1,0:T(8,128)(2,1)} %get-tuple-element.19), channel_id=1, source_target_pairs={{0,3},{1,0},{2,1},{3,2},{4,7},{5,4},{6,5},{7,6},{8,11},{9,8},{10,9... | collective-permute-start | bytes 110600 | tf_op jit(solution)/shard_map/ppermute | solution.py:307
  10.8 0.2 collective-permute-done.refs_0_.refs_1_
  11.0 1.3 %collective-permute-done.1.refs_1_.refs_2_ = bf16[144,128]{1,0:T(8,128)(2,1)S(1)} collective-permute-done((bf16[144,128]{1,0:T(8,128)(2,1)}, bf16[144,128]{1,0:T(8,128)(2,1)S(1)}, u32[]{:S(2)}, u32[]{:S(2)}) %collective-permute-start.1) | collective-permute-done | bytes 36896 | tf_op jit(solution)/shard_map/ppermute | solution.py:307
  12.3 1.3 %collective-permute-done.2.refs_2_.refs_3_ = bf16[144,128]{1,0:T(8,128)(2,1)S(1)} collective-permute-done((bf16[144,128]{1,0:T(8,128)(2,1)}, bf16[144,128]{1,0:T(8,128)(2,1)S(1)}, u32[]{:S(2)}, u32[]{:S(2)}) %collective-permute-start.2) | collective-permute-done | bytes 36896 | tf_op jit(solution)/shard_map/ppermute | solution.py:307
  13.6 0.0 copy-done.6
  13.6 0.0 copy-done.7
  13.6 0.0 copy-start.2
  13.6 1.0 %copy-done.2 = bf16[128,1280]{1,0:T(8,128)(2,1)S(1)} copy-done((bf16[128,1280]{1,0:T(8,128)(2,1)S(1)}, bf16[128,1280]{1,0:T(8,128)(2,1)}, u32[]{:S(2)}) %copy-start.2) | copy-done | bytes 327704
  14.6 1.1 %weight_grads.1 = (f32[64,1280]{1,0:T(8,128)S(1)}, bf16[64,1280]{1,0:T(8,128)(2,1)}, bf16[64,1280]{1,0:T(8,128)(2,1)}, bf16[64,1280]{1,0:T(8,128)(2,1)}) custom-call(bf16[64,128]{1,0:T(8,128)(2,1)S(1)} %bitcast.15, bf16[64,128]{1,0:T(8,128)(2,1)S(1)} %bitcast.17, bf16[128,1280]{1,0:T(8,128)(2,1)S(1)} %copy-done.2, ...), custom_call_target="tpu_custom_call" | custom-call | flops 83886080 | bytes 983040 | tf_op jit(solution)/shard_map/weight_grads/pallas_call | solution.py:76
  15.6 0.0 copy-done.5
  15.6 0.0 copy-start.3
  15.6 0.8 %copy-done.3 = bf16[144,128]{1,0:T(8,128)(2,1)S(1)} copy-done((bf16[144,128]{1,0:T(8,128)(2,1)S(1)}, bf16[144,128]{1,0:T(8,128)(2,1)}, u32[]{:S(2)}) %copy-start.3) | copy-done | bytes 36888
  16.4 0.0 copy-start
  16.4 2.5 %collective-permute-start.5 = (bf16[336,128]{1,0:T(8,128)(2,1)S(1)}, bf16[336,128]{1,0:T(8,128)(2,1)S(1)}, u32[]{:S(2)}, u32[]{:S(2)}) collective-permute-start(bf16[336,128]{1,0:T(8,128)(2,1)S(1)} %bundle.1.refs_0_), channel_id=1, source_target_pairs={{0,24},{4,28},{8,16},{12,20},{16,8},{20,12},{24,0},{28,4},{1,25},{... | collective-permute-start | bytes 258056 | tf_op jit(solution)/shard_map/ppermute | solution.py:317
  18.9 0.5 collective-permute-start.4
  19.4 0.5 collective-permute-start.3
  20.0 2.7 %collective-permute-done.5.refs_3_ = bf16[336,128]{1,0:T(8,128)(2,1)S(1)} collective-permute-done((bf16[336,128]{1,0:T(8,128)(2,1)S(1)}, bf16[336,128]{1,0:T(8,128)(2,1)S(1)}, u32[]{:S(2)}, u32[]{:S(2)}) %collective-permute-start.5) | collective-permute-done | bytes 86048 | tf_op jit(solution)/shard_map/ppermute | solution.py:317
  22.6 0.9 %collective-permute-done.4.refs_2_ = bf16[336,128]{1,0:T(8,128)(2,1)S(1)} collective-permute-done((bf16[336,128]{1,0:T(8,128)(2,1)S(1)}, bf16[336,128]{1,0:T(8,128)(2,1)S(1)}, u32[]{:S(2)}, u32[]{:S(2)}) %collective-permute-start.4) | collective-permute-done | bytes 86048 | tf_op jit(solution)/shard_map/ppermute | solution.py:317
  23.5 0.4 collective-permute-done.3.refs_1_
  24.0 0.1 collective-permute-start.6
  24.0 1.0 %collective-permute-start.8 = (bf16[64,1280]{1,0:T(8,128)(2,1)}, bf16[64,1280]{1,0:T(8,128)(2,1)S(1)}, u32[]{:S(2)}, u32[]{:S(2)}) collective-permute-start(bf16[64,1280]{1,0:T(8,128)(2,1)} %get-tuple-element.28), channel_id=1, source_target_pairs={{0,2},{1,3},{2,0},{3,1},{4,6},{5,7},{6,4},{7,5},{8,10},{9,11},{10,... | collective-permute-start | bytes 491528 | tf_op jit(solution)/shard_map/ppermute | solution.py:307
  25.1 2.8 %collective-permute-start.9 = (bf16[64,1280]{1,0:T(8,128)(2,1)}, bf16[64,1280]{1,0:T(8,128)(2,1)S(1)}, u32[]{:S(2)}, u32[]{:S(2)}) collective-permute-start(bf16[64,1280]{1,0:T(8,128)(2,1)} %get-tuple-element.29), channel_id=1, source_target_pairs={{0,1},{1,2},{2,3},{3,0},{4,5},{5,6},{6,7},{7,4},{8,9},{9,10},{10,1... | collective-permute-start | bytes 491528 | tf_op jit(solution)/shard_map/ppermute | solution.py:307
  27.8 1.1 %collective-permute-start.7 = (bf16[64,1280]{1,0:T(8,128)(2,1)}, bf16[64,1280]{1,0:T(8,128)(2,1)S(1)}, u32[]{:S(2)}, u32[]{:S(2)}) collective-permute-start(bf16[64,1280]{1,0:T(8,128)(2,1)} %get-tuple-element.20.after), channel_id=1, source_target_pairs={{0,3},{1,0},{2,1},{3,2},{4,7},{5,4},{6,5},{7,6},{8,11},{9,8},{10,9... | collective-permute-start | bytes 491528 | tf_op jit(solution)/shard_map/ppermute | solution.py:307
  28.9 0.7 %copy.13 = s32[1,1,80,8]{3,2,1,0:T(8,128)} copy(s32[1,1,80,8]{2,3,1,0:T(8,128)S(1)} %copy-done.5) | data formatting | bytes 5120 | tf_op args[5]
  29.6 0.9 %reshape_squeeze.3 = s32[20,32]{1,0:T(8,128)S(1)} reshape(s32[1,1,80,8]{3,2,1,0:T(8,128)} %copy.13) | data formatting | bytes 5120 | tf_op jit(solution)/shard_map/reshape;squeeze | solution.py:375
  30.4 0.1 pad_add_fusion.rows
  30.5 0.0 copy-done.8
  30.5 0.0 copy-done.9
  30.5 0.0 copy-done.10
  30.5 0.0 copy-done.1
  30.5 1.1 %own_places.1 = (bf16[64,2560]{1,0:T(8,128)(2,1)S(1)}, bf16[1280,128]{1,0:T(8,128)(2,1)S(1)}, bf16[1152,256]{1,0:T(8,128)(2,1)S(1)}, f32[8,128]{1,0:T(8,128)S(1)}) custom-call(s32[2]{0:T(128)S(1)} %copy-done.8, s32[8]{0:T(128)S(1)} %copy-done.9, s32[8]{0:T(128)S(1)} %copy-done.10, s32[20,128]{1,0:T(8,128)S(1)} %pad_add_fusion.rows, ...), custom_call_target="tpu_custom_call" | custom-call | tf_op jit(solution)/shard_map/own_places/pallas_call | solution.py:76
  31.7 0.0 collective-permute-done.6.other
  31.7 0.6 %places.1 = (bf16[64,5120]{1,0:T(8,128)(2,1)S(1)}, bf16[64,5120]{1,0:T(8,128)(2,1)S(1)}) custom-call(f32[8,128]{1,0:T(8,128)S(1)} %get-tuple-element.25.w_ref, bf16[4,336,128]{2,1,0:T(8,128)(2,1)S(1)} %join_bundles.1.mine, bf16[4,336,128]{2,1,0:T(8,128)(2,1)S(1)} %collective-permute-done.6.other, bf16[1152,256]{1,0:T(8,128)(2,1)S(1)} %get-tuple-element.23.tab), custom_call_target="tpu_custom_call" | custom-call | tf_op jit(solution)/shard_map/places/pallas_call | solution.py:76
  32.3 7.0 %collective-permute-done.8.refs_2_ = bf16[64,1280]{1,0:T(8,128)(2,1)S(1)} collective-permute-done((bf16[64,1280]{1,0:T(8,128)(2,1)}, bf16[64,1280]{1,0:T(8,128)(2,1)S(1)}, u32[]{:S(2)}, u32[]{:S(2)}) %collective-permute-start.8) | collective-permute-done | bytes 163872 | tf_op jit(solution)/shard_map/ppermute | solution.py:307
  39.3 0.0 collective-permute-done.9.refs_3_
  39.3 1.2 %collective-permute-done.7.refs_1_ = bf16[64,1280]{1,0:T(8,128)(2,1)S(1)} collective-permute-done((bf16[64,1280]{1,0:T(8,128)(2,1)}, bf16[64,1280]{1,0:T(8,128)(2,1)S(1)}, u32[]{:S(2)}, u32[]{:S(2)}) %collective-permute-start.7) | collective-permute-done | bytes 163872 | tf_op jit(solution)/shard_map/ppermute | solution.py:307
  40.4 0.0 copy-done
  40.4 0.0 copy-start.4
  40.4 1.2 %kept_rows.1.ship.refs_0_ = bf16[8,5120]{1,0:T(8,128)(2,1)S(1)} custom-call(s32[2]{0:T(128)S(1)} %copy-done.8, f32[64,5120]{1,0:T(8,128)S(1)} %bitcast.11, bf16[1280,128]{1,0:T(8,128)(2,1)S(1)} %get-tuple-element.24.a_ref, bf16[1152,256]{1,0:T(8,128)(2,1)S(1)} %get-tuple-element.23.tab, bf16[64,5120]{1,0:T(8,128)(2,1)S(1)} %get-tuple-element.26.after.p_hi, ...), custom_call_target="tpu_custom_call" | custom-call | flops 125829120 | bytes 1966080 | tf_op jit(solution)/shard_map/kept_rows/pallas_call | solution.py:76
  41.7 1.6 %collective-permute-start.12 = (bf16[8,5120]{1,0:T(8,128)(2,1)S(1)}, bf16[8,5120]{1,0:T(8,128)(2,1)S(1)}, u32[]{:S(2)}, u32[]{:S(2)}) collective-permute-start(bf16[8,5120]{1,0:T(8,128)(2,1)S(1)} %kept_rows.1.ship.refs_0_), channel_id=1, source_target_pairs={{0,24},{4,28},{8,16},{12,20},{16,8},{20,12},{24,0},{28,4},{1,25},{... | collective-permute-start | bytes 245768 | tf_op jit(solution)/shard_map/ppermute | solution.py:317
  43.2 0.5 collective-permute-start.11
  43.7 1.5 %collective-permute-start.10 = (bf16[8,5120]{1,0:T(8,128)(2,1)S(1)}, bf16[8,5120]{1,0:T(8,128)(2,1)S(1)}, u32[]{:S(2)}, u32[]{:S(2)}) collective-permute-start(bf16[8,5120]{1,0:T(8,128)(2,1)S(1)} %kept_rows.1.ship.refs_0_), channel_id=1, source_target_pairs={{0,8},{4,12},{8,0},{12,4},{16,24},{20,28},{24,16},{28,20},{1,9},{5... | collective-permute-start | bytes 245768 | tf_op jit(solution)/shard_map/ppermute | solution.py:317
  45.2 2.4 %collective-permute-done.12.refs_3_ = bf16[8,5120]{1,0:T(8,128)(2,1)S(1)} collective-permute-done((bf16[8,5120]{1,0:T(8,128)(2,1)S(1)}, bf16[8,5120]{1,0:T(8,128)(2,1)S(1)}, u32[]{:S(2)}, u32[]{:S(2)}) %collective-permute-start.12) | collective-permute-done | bytes 81952 | tf_op jit(solution)/shard_map/ppermute | solution.py:317
  47.6 0.6 %collective-permute-done.11.refs_2_ = bf16[8,5120]{1,0:T(8,128)(2,1)S(1)} collective-permute-done((bf16[8,5120]{1,0:T(8,128)(2,1)S(1)}, bf16[8,5120]{1,0:T(8,128)(2,1)S(1)}, u32[]{:S(2)}, u32[]{:S(2)}) %collective-permute-start.11) | collective-permute-done | bytes 81952 | tf_op jit(solution)/shard_map/ppermute | solution.py:317
  48.2 0.0 collective-permute-done.10.refs_1_
  48.2 0.1 collective-permute-start.13
  48.3 0.0 copy-done.4
  48.3 1.7 %input_grads.1 = bf16[128,1280]{1,0:T(8,128)(2,1)} custom-call(s32[2]{0:T(128)S(1)} %copy-done.8, bf16[4,336,128]{2,1,0:T(8,128)(2,1)S(1)} %join_bundles.1.mine, bf16[4,336,128]{2,1,0:T(8,128)(2,1)S(1)} %collective-permute-done.6.other, bf16[144,128]{1,0:T(8,128)(2,1)S(1)} %copy-done.4, bf16[144,128]{1,0:T(8,128)(2,1)S(1)} %collective-permute-done.refs_0_.refs_1_, ...), custom_call_target="tpu_custom_call" | custom-call | flops 83886080 | bytes 983040 | tf_op jit(solution)/shard_map/input_grads/pallas_call | solution.py:76
  50.1 2.4 %new_momentums.1 = f32[64,5120]{1,0:T(8,128)} custom-call(s32[2]{0:T(128)S(1)} %copy-done.8, f32[64,5120]{1,0:T(8,128)S(1)} %bitcast.12, bf16[64,2560]{1,0:T(8,128)(2,1)S(1)} %get-tuple-element.22.p_ref, bf16[1152,256]{1,0:T(8,128)(2,1)S(1)} %get-tuple-element.23.tab, bf16[8,5120]{1,0:T(8,128)(2,1)S(1)} %kept_rows.1.ship.refs_0_, ...), custom_call_target="tpu_custom_call" | custom-call | flops 125829120 | bytes 3276800 | tf_op jit(solution)/shard_map/new_momentums/pallas_call | solution.py:76
  52.5 0.0 collective-permute-done.13.other
  52.5 2.1 %updates.1 = f32[64,5120]{1,0:T(8,128)} custom-call(bf16[64,5120]{1,0:T(8,128)(2,1)S(1)} %get-tuple-element.26.after.p_hi, bf16[64,5120]{1,0:T(8,128)(2,1)S(1)} %get-tuple-element.30.p_lo, bf16[1152,256]{1,0:T(8,128)(2,1)S(1)} %get-tuple-element.23.tab, bf16[4,8,5120]{2,1,0:T(8,128)(2,1)S(1)} %join_kept.1.mine, ...), custom_call_target="tpu_custom_call" | custom-call | flops 671088640 | bytes 2621440 | tf_op jit(solution)/shard_map/updates/pallas_call | solution.py:76
  (3 shorter events, 0.1 us)
Async XLA Ops:
  1.3 12.3 %copy-start.6 = (bf16[128,64]{0,1:T(8,128)(2,1)S(1)}, bf16[128,64]{0,1:T(8,128)(2,1)}, u32[]{:S(2)}) copy-start(bf16[128,64]{0,1:T(8,128)(2,1)} %param.10) | copy-start | bytes 49156
  1.3 12.3 %copy-start.7 = (bf16[128,64]{0,1:T(8,128)(2,1)S(1)}, bf16[128,64]{0,1:T(8,128)(2,1)}, u32[]{:S(2)}) copy-start(bf16[128,64]{0,1:T(8,128)(2,1)} %param.11) | copy-start | bytes 49156
  1.3 14.4 %copy-start.5 = (s32[1,1,80,8]{2,3,1,0:T(8,128)S(1)}, s32[1,1,80,8]{2,3,1,0:T(8,128)}, u32[]{:S(2)}) copy-start(s32[1,1,80,8]{2,3,1,0:T(8,128)} %param.14) | copy-start | bytes 7684
  1.3 29.3 %copy-start.8 = (s32[2]{0:T(128)S(1)}, s32[2]{0:T(128)}, u32[]{:S(2)}) copy-start(s32[2]{0:T(128)} %pad_add_fusion.1.pos) | copy-start | bytes 28
  1.3 29.3 %copy-start.9 = (s32[8]{0:T(128)S(1)}, s32[8]{0:T(128)}, u32[]{:S(2)}) copy-start(s32[8]{0:T(128)} %mask.1) | copy-start | bytes 100
  1.3 29.3 %copy-start.10 = (s32[8]{0:T(128)S(1)}, s32[8]{0:T(128)}, u32[]{:S(2)}) copy-start(s32[8]{0:T(128)} %tally.1) | copy-start | bytes 100
  3.7 26.8 %copy-start.1 = (bf16[1152,256]{1,0:T(8,128)(2,1)S(1)}, bf16[1152,256]{1,0:T(8,128)(2,1)}, u32[]{:S(2)}) copy-start(bf16[1152,256]{1,0:T(8,128)(2,1)} %constant.11.clone.tab) | copy-start | bytes 1769476
  3.8 7.2 %collective-permute-start = (bf16[144,128]{1,0:T(8,128)(2,1)}, bf16[144,128]{1,0:T(8,128)(2,1)S(1)}, u32[]{:S(2)}, u32[]{:S(2)}) collective-permute-start(bf16[144,128]{1,0:T(8,128)(2,1)} %get-tuple-element.17), channel_id=1, source_target_pairs={{0,1},{1,2},{2,3},{3,0},{4,5},{5,6},{6,7},{7,4},{8,9},{9,10},{10,1... | collective-permute-start | bytes 110600 | tf_op jit(solution)/shard_map/ppermute | solution.py:307
  6.8 5.5 %collective-permute-start.1 = (bf16[144,128]{1,0:T(8,128)(2,1)}, bf16[144,128]{1,0:T(8,128)(2,1)S(1)}, u32[]{:S(2)}, u32[]{:S(2)}) collective-permute-start(bf16[144,128]{1,0:T(8,128)(2,1)} %get-tuple-element.18), channel_id=1, source_target_pairs={{0,2},{1,3},{2,0},{3,1},{4,6},{5,7},{6,4},{7,5},{8,10},{9,11},{10,... | collective-permute-start | bytes 110600 | tf_op jit(solution)/shard_map/ppermute | solution.py:307
  9.4 4.2 %collective-permute-start.2 = (bf16[144,128]{1,0:T(8,128)(2,1)}, bf16[144,128]{1,0:T(8,128)(2,1)S(1)}, u32[]{:S(2)}, u32[]{:S(2)}) collective-permute-start(bf16[144,128]{1,0:T(8,128)(2,1)} %get-tuple-element.19), channel_id=1, source_target_pairs={{0,3},{1,0},{2,1},{3,2},{4,7},{5,4},{6,5},{7,6},{8,11},{9,8},{10,9... | collective-permute-start | bytes 110600 | tf_op jit(solution)/shard_map/ppermute | solution.py:307
  13.6 1.0 %copy-start.2 = (bf16[128,1280]{1,0:T(8,128)(2,1)S(1)}, bf16[128,1280]{1,0:T(8,128)(2,1)}, u32[]{:S(2)}) copy-start(bf16[128,1280]{1,0:T(8,128)(2,1)} %act.1) | copy-start | bytes 983044
  15.6 0.8 %copy-start.3 = (bf16[144,128]{1,0:T(8,128)(2,1)S(1)}, bf16[144,128]{1,0:T(8,128)(2,1)}, u32[]{:S(2)}) copy-start(bf16[144,128]{1,0:T(8,128)(2,1)} %get-tuple-element.21.refs_0_) | copy-start | bytes 110596
  16.4 24.0 %copy-start = (f32[1,64,5120]{2,1,0:T(8,128)S(1)}, f32[1,64,5120]{2,1,0:T(8,128)}, u32[]{:S(2)}) copy-start(f32[1,64,5120]{2,1,0:T(8,128)} %param.13) | copy-start | bytes 3932164
  16.4 6.2 %collective-permute-start.5 = (bf16[336,128]{1,0:T(8,128)(2,1)S(1)}, bf16[336,128]{1,0:T(8,128)(2,1)S(1)}, u32[]{:S(2)}, u32[]{:S(2)}) collective-permute-start(bf16[336,128]{1,0:T(8,128)(2,1)S(1)} %bundle.1.refs_0_), channel_id=1, source_target_pairs={{0,24},{4,28},{8,16},{12,20},{16,8},{20,12},{24,0},{28,4},{1,25},{... | collective-permute-start | bytes 258056 | tf_op jit(solution)/shard_map/ppermute | solution.py:317
  18.9 4.6 %collective-permute-start.4 = (bf16[336,128]{1,0:T(8,128)(2,1)S(1)}, bf16[336,128]{1,0:T(8,128)(2,1)S(1)}, u32[]{:S(2)}, u32[]{:S(2)}) collective-permute-start(bf16[336,128]{1,0:T(8,128)(2,1)S(1)} %bundle.1.refs_0_), channel_id=1, source_target_pairs={{0,16},{4,20},{8,24},{12,28},{16,0},{20,4},{24,8},{28,12},{1,17},{... | collective-permute-start | bytes 258056 | tf_op jit(solution)/shard_map/ppermute | solution.py:317
  19.4 4.5 %collective-permute-start.3 = (bf16[336,128]{1,0:T(8,128)(2,1)S(1)}, bf16[336,128]{1,0:T(8,128)(2,1)S(1)}, u32[]{:S(2)}, u32[]{:S(2)}) collective-permute-start(bf16[336,128]{1,0:T(8,128)(2,1)S(1)} %bundle.1.refs_0_), channel_id=1, source_target_pairs={{0,8},{4,12},{8,0},{12,4},{16,24},{20,28},{24,16},{28,20},{1,9},{5... | collective-permute-start | bytes 258056 | tf_op jit(solution)/shard_map/ppermute | solution.py:317
  24.0 7.7 %collective-permute-start.6 = (bf16[4,336,128]{2,1,0:T(8,128)(2,1)S(1)}, bf16[4,336,128]{2,1,0:T(8,128)(2,1)S(1)}, u32[]{:S(2)}, u32[]{:S(2)}) collective-permute-start(bf16[4,336,128]{2,1,0:T(8,128)(2,1)S(1)} %join_bundles.1.mine), channel_id=1, source_target_pairs={{0,4},{4,0},{8,12},{12,8},{16,20},{20,16},{24,28},{28,24},{1,5},{5... | collective-permute-start | bytes 1032200 | tf_op jit(solution)/shard_map/ppermute | solution.py:317
  24.0 15.2 %collective-permute-start.8 = (bf16[64,1280]{1,0:T(8,128)(2,1)}, bf16[64,1280]{1,0:T(8,128)(2,1)S(1)}, u32[]{:S(2)}, u32[]{:S(2)}) collective-permute-start(bf16[64,1280]{1,0:T(8,128)(2,1)} %get-tuple-element.28), channel_id=1, source_target_pairs={{0,2},{1,3},{2,0},{3,1},{4,6},{5,7},{6,4},{7,5},{8,10},{9,11},{10,... | collective-permute-start | bytes 491528 | tf_op jit(solution)/shard_map/ppermute | solution.py:307
  25.1 14.2 %collective-permute-start.9 = (bf16[64,1280]{1,0:T(8,128)(2,1)}, bf16[64,1280]{1,0:T(8,128)(2,1)S(1)}, u32[]{:S(2)}, u32[]{:S(2)}) collective-permute-start(bf16[64,1280]{1,0:T(8,128)(2,1)} %get-tuple-element.29), channel_id=1, source_target_pairs={{0,1},{1,2},{2,3},{3,0},{4,5},{5,6},{6,7},{7,4},{8,9},{9,10},{10,1... | collective-permute-start | bytes 491528 | tf_op jit(solution)/shard_map/ppermute | solution.py:307
  27.8 12.6 %collective-permute-start.7 = (bf16[64,1280]{1,0:T(8,128)(2,1)}, bf16[64,1280]{1,0:T(8,128)(2,1)S(1)}, u32[]{:S(2)}, u32[]{:S(2)}) collective-permute-start(bf16[64,1280]{1,0:T(8,128)(2,1)} %get-tuple-element.20.after), channel_id=1, source_target_pairs={{0,3},{1,0},{2,1},{3,2},{4,7},{5,4},{6,5},{7,6},{8,11},{9,8},{10,9... | collective-permute-start | bytes 491528 | tf_op jit(solution)/shard_map/ppermute | solution.py:307
  40.4 7.9 %copy-start.4 = (bf16[144,128]{1,0:T(8,128)(2,1)S(1)}, bf16[144,128]{1,0:T(8,128)(2,1)}, u32[]{:S(2)}) copy-start(bf16[144,128]{1,0:T(8,128)(2,1)} %get-tuple-element.21.refs_0_) | copy-start | bytes 110596
  41.7 5.9 %collective-permute-start.12 = (bf16[8,5120]{1,0:T(8,128)(2,1)S(1)}, bf16[8,5120]{1,0:T(8,128)(2,1)S(1)}, u32[]{:S(2)}, u32[]{:S(2)}) collective-permute-start(bf16[8,5120]{1,0:T(8,128)(2,1)S(1)} %kept_rows.1.ship.refs_0_), channel_id=1, source_target_pairs={{0,24},{4,28},{8,16},{12,20},{16,8},{20,12},{24,0},{28,4},{1,25},{... | collective-permute-start | bytes 245768 | tf_op jit(solution)/shard_map/ppermute | solution.py:317
  43.2 5.0 %collective-permute-start.11 = (bf16[8,5120]{1,0:T(8,128)(2,1)S(1)}, bf16[8,5120]{1,0:T(8,128)(2,1)S(1)}, u32[]{:S(2)}, u32[]{:S(2)}) collective-permute-start(bf16[8,5120]{1,0:T(8,128)(2,1)S(1)} %kept_rows.1.ship.refs_0_), channel_id=1, source_target_pairs={{0,16},{4,20},{8,24},{12,28},{16,0},{20,4},{24,8},{28,12},{1,17},{... | collective-permute-start | bytes 245768 | tf_op jit(solution)/shard_map/ppermute | solution.py:317
  43.7 4.5 %collective-permute-start.10 = (bf16[8,5120]{1,0:T(8,128)(2,1)S(1)}, bf16[8,5120]{1,0:T(8,128)(2,1)S(1)}, u32[]{:S(2)}, u32[]{:S(2)}) collective-permute-start(bf16[8,5120]{1,0:T(8,128)(2,1)S(1)} %kept_rows.1.ship.refs_0_), channel_id=1, source_target_pairs={{0,8},{4,12},{8,0},{12,4},{16,24},{20,28},{24,16},{28,20},{1,9},{5... | collective-permute-start | bytes 245768 | tf_op jit(solution)/shard_map/ppermute | solution.py:317
  48.2 4.2 %collective-permute-start.13 = (bf16[4,8,5120]{2,1,0:T(8,128)(2,1)S(1)}, bf16[4,8,5120]{2,1,0:T(8,128)(2,1)S(1)}, u32[]{:S(2)}, u32[]{:S(2)}) collective-permute-start(bf16[4,8,5120]{2,1,0:T(8,128)(2,1)S(1)} %join_kept.1.mine), channel_id=1, source_target_pairs={{0,4},{4,0},{8,12},{12,8},{16,20},{20,16},{24,28},{28,24},{1,5},{5... | collective-permute-start | bytes 983048 | tf_op jit(solution)/shard_map/ppermute | solution.py:317

commit v4 on v3

--- a/solution.py
+++ b/solution.py
@@ -14,7 +14,6 @@
 F32 = jnp.float32
 BF16 = jnp.bfloat16
 VMEM_LIMIT = 24 * 1024 * 1024
-FIRST_LIMIT = 63 * 1024 * 1024
 
 VM = pl.BlockSpec(memory_space=pltpu.VMEM)
 SM = pl.BlockSpec(memory_space=pltpu.SMEM)
@@ -72,40 +71,44 @@
     return hi, (x - hi.astype(F32)).astype(BF16)
 
 
-def call(body, out_shape, ins, in_specs, out_specs, scratch=(), flops=0, nbytes=0, name=None, limit=VMEM_LIMIT):
+def near(shape, dtype=BF16):
+    return pltpu.VMEM(shape, dtype)
+
+
+def far(x):
+    return pltpu.with_memory_space_constraint(x, pltpu.HBM)
+
+
+def call(body, out_shape, ins, in_specs, out_specs, scratch=(), flops=0, nbytes=0, name=None):
     return pl.pallas_call(
         body,
         out_shape=out_shape,
         in_specs=in_specs,
         out_specs=out_specs,
         scratch_shapes=scratch,
-        compiler_params=pltpu.CompilerParams(vmem_limit_bytes=limit),
+        compiler_params=pltpu.CompilerParams(vmem_limit_bytes=VMEM_LIMIT),
         cost_estimate=pl.CostEstimate(flops=flops, bytes_accessed=nbytes, transcendentals=0),
         name=name,
     )(*ins)
 
 
-def up_grad(switch, slope):
-    v = switch.astype(F32)
-    return (slope.astype(F32) * (v * jax.nn.sigmoid(v))).astype(BF16)
-
-
-def first_body(n_t, cp, cols, nr, pos, switch, slope, exp_ref, *refs):
-    outs = refs[:n_t]
-    switch_v, slope_v, exp_v, sems = refs[n_t:]
-    rep, ten = pos[0], pos[1]
+def first_body(n_t, cp, cols, nr, switch, slope, exp_ref, act, *refs):
+    outs, act_out = refs[:n_t], refs[n_t]
+    switch_v, slope_v, exp_v, sems = refs[n_t + 1 :]
+    rep, ten = lax.axis_index("replica"), lax.axis_index("tensor")
     r0 = pl.multiple_of((rep // cp) * nr, nr)
     copies = [
         pltpu.make_async_copy(src, dst, sems.at[i])
         for i, (src, dst) in enumerate(
-            [(switch, switch_v), (slope, slope_v), (exp_ref.at[pl.ds(r0, nr), :], exp_v)]
+            [(switch, switch_v), (slope, slope_v), (exp_ref.at[pl.ds(r0, nr), :], exp_v), (act, act_out)]
         )
     ]
     for copy in copies:
         copy.start()
     copies[0].wait()
     copies[1].wait()
-    up = up_grad(switch_v[...], slope_v[...])
+    v = switch_v[...].astype(F32)
+    up = (slope_v[...].astype(F32) * (v * jax.nn.sigmoid(v))).astype(BF16)
     for k in range(n_t):
         outs[k][:B, :] = up
     copies[2].wait()
@@ -115,11 +118,12 @@
         for j in range(nc // 128):
             at = pl.multiple_of(c0 + j * 128, 128)
             outs[k][B + j * nr : B + (j + 1) * nr, :] = exp_v[:, pl.ds(at, 128)]
-
-
-def grads_body(n_t, switch, slope, act, *refs):
-    ups, outs = refs[: n_t - 1], refs[n_t - 1 :]
-    up = jnp.concatenate([up_grad(switch[...], slope[...])] + [u[:B, :] for u in ups], axis=0)
+    copies[3].wait()
+
+
+def grads_body(n_t, act, *refs):
+    ups, outs = refs[:n_t], refs[n_t:]
+    up = jnp.concatenate([u[:B, :] for u in ups], axis=0)
     for c in range(0, act.shape[1], G):
         g = dot(up, act[:, c : c + G])
         for k in range(n_t):
@@ -136,48 +140,56 @@
     out[n_t * n :, :] = jnp.concatenate([rows, jnp.zeros((16 - keep, 128), F32)], axis=0).astype(BF16)
 
 
-def join_body(*refs):
+def join_body(after, *refs):
     for i, ref in enumerate(refs[:-1]):
         refs[-1][i] = ref[...]
 
 
-def own_body(n_r, keep, pos, mask, tally, rows, tab, p_ref, a_ref, tab_ref, w_ref, mask_s, tally_s, sems):
-    copies = [pltpu.make_async_copy(mask, mask_s, sems.at[0]), pltpu.make_async_copy(tally, tally_s, sems.at[1])]
+def own_body(n_r, keep, after, mask, tally, lines, tab, p_ref, a_ref, tab_ref, w_ref, mask_s, tally_s, sems):
+    copies = [
+        pltpu.make_async_copy(src, dst, sems.at[i])
+        for i, (src, dst) in enumerate([(mask, mask_s), (tally, tally_s), (tab, tab_ref)])
+    ]
     for copy in copies:
         copy.start()
-    tab_ref[...] = tab[...]
-    freq = lax.broadcasted_iota(jnp.int32, (B, 2 * B), 0)
+    blocks = lines.shape[1]
+    rows = jnp.concatenate([lines[...].astype(F32), jnp.zeros((keep, 128 - blocks), F32)], axis=1)
+    rows = jnp.concatenate([rows] * (2 * B // keep), axis=0).T
+    freq = lax.broadcasted_iota(jnp.int32, (B, 2 * B), 0).astype(F32)
+    block = (lax.broadcasted_iota(jnp.int32, (1, 2 * B), 1) // keep) % (G // B)
     term = lax.broadcasted_iota(jnp.int32, (B, 2 * B), 1) // (B // 2)
-    for g in range(rows.shape[0]):
-        hot = jnp.where(freq == rows[g : g + 1, :], 1.0, 0.0).astype(BF16)
-        y = dot(tall(tab), hot)
+    for copy in copies:
+        copy.wait()
+    for g in range(blocks // (G // B)):
+        num = rows[g * (G // B) : g * (G // B) + 1]
+        for j in range(1, G // B):
+            num = jnp.where(block == j, rows[g * (G // B) + j : g * (G // B) + j + 1], num)
+        hot = jnp.where(freq == num, 1.0, 0.0).astype(BF16)
+        y = dot(tall(tab_ref), hot)
         p = jnp.where(term == 3, 0.0, jnp.where(term == 1, y[B:], y[:B]))
         p_ref[:, g * 2 * B : (g + 1) * 2 * B] = p.astype(BF16)
         a_ref[g * B : (g + 1) * B, :] = jnp.concatenate([p, p], axis=0).T[:B].astype(BF16)
-    for copy in copies:
-        copy.wait()
     total, alive = jnp.float32(0), jnp.float32(0)
     for r in range(n_r):
         m = mask_s[r].astype(F32)
         total = total + m * tally_s[r].astype(F32)
         alive = alive + m
-    half = n_r // 2
     place = (lax.broadcasted_iota(jnp.int32, (8, 2 * B), 1) // keep) % n_r
     w = jnp.zeros((8, 2 * B), F32)
-    for i in range(n_r):
-        r = pos[0] ^ (2 * (i % half) + i // half)
-        w = jnp.where(place == i, mask_s[r].astype(F32) * tally_s[r].astype(F32), w)
+    for m in range(n_r):
+        r = lax.axis_index("replica") ^ m
+        w = jnp.where(place == m, mask_s[r].astype(F32) * tally_s[r].astype(F32), w)
     w_ref[...] = w * (jnp.full((8, 2 * B), alive) / jnp.full((8, 2 * B), total))
 
 
-def kept_body(n_t, keep, pos, vel, a_ref, tab, after, *refs):
+def kept_body(n_t, keep, vel, a_ref, tab, after, *refs):
     grads, ship_ref = refs[:n_t], refs[n_t]
     cols = grads[0].shape[1]
     ng = cols // G
     lane_block = lax.broadcasted_iota(jnp.int32, (keep, G), 1) // B
     sel = []
     for k in range(n_t):
-        c0 = lax.rem(pos[1] + k, n_t) * cols
+        c0 = lax.rem(lax.axis_index("tensor") + k, n_t) * cols
         for i in range(ng):
             at = pl.multiple_of(c0 + i * G, G)
             moment = momentum_decay * vel[:, pl.ds(at, G)] + grads[k][:, i * G : (i + 1) * G].astype(F32)
@@ -193,13 +205,13 @@
     y = dot(jnp.concatenate([hi, lo], axis=0), fwd(tab, 0))
     y = y[:n] + y[n:] + dot(hi, fwd(tab, 1))
     for k in range(n_t):
-        c0 = pl.multiple_of(lax.rem(pos[1] + k, n_t) * cols, G)
+        c0 = pl.multiple_of(lax.rem(lax.axis_index("tensor") + k, n_t) * cols, G)
         ship_ref[:, pl.ds(c0, cols)] = jnp.concatenate(
             [y[(k * ng + i) * keep : (k * ng + i + 1) * keep] for i in range(ng)], axis=1
         ).astype(BF16)
 
 
-def return_body(n_t, keep, pos, vel, p_ref, tab, ship, *refs):
+def return_body(n_t, keep, vel, p_ref, tab, ship, *refs):
     grads, new_ref = refs[:n_t], refs[n_t]
     cols = grads[0].shape[1]
     ng = cols // G
@@ -219,17 +231,17 @@
         cut = slice(g * G, (g + 1) * G)
         new_ref[:, cut] = momentum_decay * vel[:, cut] - back
     for k in range(n_t):
-        c0 = lax.rem(pos[1] + k, n_t) * cols
+        c0 = lax.rem(lax.axis_index("tensor") + k, n_t) * cols
         for i in range(ng):
             at = pl.multiple_of(c0 + i * G, G)
             new_ref[:, pl.ds(at, G)] += grads[k][:, i * G : (i + 1) * G].astype(F32)
 
 
-def places_body(n_r, keep, w_ref, mine, other, tab, hi_ref, lo_ref):
-    half = n_r // 2
+def places_body(keep, w_ref, tab, bundles, hi_ref, lo_ref):
     w = w_ref[:1, :]
-    last = mine.shape[1] - 16
-    rows = [ref[i, last:, :].astype(F32)[:keep] for ref in (mine, other) for i in range(half)]
+    n_r, last = bundles.shape[0], bundles.shape[1] - 16
+    rep = lax.axis_index("replica")
+    rows = [bundles[rep ^ m, last:, :].astype(F32)[:keep] for m in range(n_r)]
     rows = jnp.concatenate(rows + rows, axis=0).T
     freq = lax.broadcasted_iota(jnp.int32, (B, 2 * B), 0).astype(F32)
     first = lax.broadcasted_iota(jnp.int32, (1, 2 * B), 1) < B
@@ -252,7 +264,7 @@
     for g in range(ng):
         cut = slice(g * G, (g + 1) * G)
         s = jnp.concatenate(
-            [ref[i, :, cut].astype(F32) for ref in (mine, other) for i in range(half)], axis=0
+            [ref[i, :, cut].astype(F32) for i in range(half) for ref in (mine, other)], axis=0
         )
         w = jnp.concatenate(
             [jnp.where(lane_block == j, s, 0.0).astype(BF16) for j in range(nb)], axis=0
@@ -267,22 +279,17 @@
         out[:, g * G : (g + 1) * G] = z[g * B : (g + 1) * B]
 
 
-def input_grad_body(n_t, n_r, cp, pos, mine, other, *refs):
+def input_grad_body(n_t, n_r, cp, bundles, *refs):
     ups, out, held = refs[:n_t], refs[n_t], refs[n_t + 1]
     nc = out.shape[1] // cp
     nr = B // (n_r // cp)
     tiles = nc // 128
-    for h, ref in enumerate((mine, other)):
-        for i in range(n_r // 2):
-            src = pos[0] ^ (2 * i + h)
-            r0 = (src // cp) * nr
-            c0 = lax.rem(src, cp) * nc
-            for k in range(n_t):
-                for j in range(tiles):
-                    at = (k * tiles + j) * nr
-                    held[
-                        pl.ds(pl.multiple_of(k * B + r0, nr), nr), pl.ds(pl.multiple_of(c0 + j * 128, 128), 128)
-                    ] = ref[i, at : at + nr, :]
+    for r in range(n_r):
+        r0, c0 = (r // cp) * nr, (r % cp) * nc
+        for k in range(n_t):
+            for j in range(tiles):
+                at = (k * tiles + j) * nr
+                held[k * B + r0 : k * B + r0 + nr, c0 + j * 128 : c0 + (j + 1) * 128] = bundles[r, at : at + nr, :]
     up = jnp.concatenate([u[:B, :] for u in ups], axis=0).T
     for c in range(0, out.shape[1], G):
         out[:, c : c + G] = dot(up, held[:, c : c + G]).astype(BF16)
@@ -299,10 +306,6 @@
     rp = n_r // cp
     half = n_r // 2
     tab = constants()
-    rep = lax.axis_index("replica").astype(jnp.int32)
-    ten = lax.axis_index("tensor").astype(jnp.int32)
-    pos = jnp.stack([rep, ten])
-
     def shift(x, k):
         return lax.ppermute(x, "tensor", [(i, (i + k) % n_t) for i in range(n_t)])
 
@@ -316,45 +319,31 @@
     def swap(x, m):
         return lax.ppermute(x, "replica", [(i, i ^ m) for i in range(n_r)])
 
-    def share(x, name):
-        parts = [x] + [swap(x, 2 * i) for i in range(1, half)]
-        mine = call(
-            join_body,
-            jax.ShapeDtypeStruct((half,) + x.shape, x.dtype),
-            parts,
-            [VM] * half,
-            VM,
-            name=name,
-        )
-        return mine, swap(mine, 1)
-
     tiles = cols // cp // 128
     nr = B // rp
-    outs = call(
+    *parts, act = call(
         functools.partial(first_body, n_t, cp, cols, nr),
-        [jax.ShapeDtypeStruct((B + tiles * nr, 128), BF16)] * n_t,
-        (pos, switch.T, slope.T, exp),
-        [SM, ANY, ANY, ANY],
-        [VM] * n_t,
+        [near((B + tiles * nr, 128))] * n_t + [near(act.shape)],
+        (far(switch.T), far(slope.T), far(exp), far(act)),
+        [ANY] * 4,
+        [VM] * (n_t + 1),
         scratch=[
             pltpu.VMEM((B, tok), BF16),
             pltpu.VMEM((B, tok), BF16),
             pltpu.VMEM((nr, width), BF16),
-            pltpu.SemaphoreType.DMA((3,)),
+            pltpu.SemaphoreType.DMA((4,)),
         ],
-        flops=1 << 32,
+        nbytes=act.size * 4 + nr * width * 2,
         name="up_grads",
-        limit=FIRST_LIMIT,
-    )
-    parts = shifts(outs, 1)
+    )
+    parts = shifts(parts, 1)
 
     grads = call(
         functools.partial(grads_body, n_t),
-        [jax.ShapeDtypeStruct((B, cols), F32)] + [jax.ShapeDtypeStruct((B, cols), BF16)] * (n_t - 1),
-        (switch.T, slope.T, act, *parts[1:]),
-        [VM] * (n_t + 2),
+        [near((B, cols), F32)] + [near((B, cols))] * (n_t - 1),
+        (act, *parts),
+        [VM] * (n_t + 1),
         [VM] * n_t,
-        flops=2 * n_t * B * tok * cols,
         nbytes=act.size * 2 + n_t * B * cols * 2,
         name="weight_grads",
     )
@@ -364,42 +353,41 @@
     own = lines[0, 0].T
     bundle = call(
         functools.partial(bundle_body, n_t, keep),
-        jax.ShapeDtypeStruct((n_t * tiles * nr + 16, 128), BF16),
+        near((n_t * tiles * nr + 16, 128)),
         (made, own, *parts),
         [ANY] + [VM] * (n_t + 1),
         VM,
         name="bundle",
     )
-    mine, other = share(bundle, "join_bundles")
-
-    own_rows = jnp.concatenate([lines[0, 0].reshape(groups, B // 2)] * 4, axis=1)
+    bundles = lax.all_gather(bundle, "replica", axis=0)
+
     p_own, a_own, tab, shares = call(
         functools.partial(own_body, n_r, keep),
         [
-            jax.ShapeDtypeStruct((B, groups * 2 * B), BF16),
-            jax.ShapeDtypeStruct((groups * B, 2 * B), BF16),
-            jax.ShapeDtypeStruct(tab.shape, BF16),
-            jax.ShapeDtypeStruct((8, 2 * B), F32),
+            near((B, groups * 2 * B)),
+            near((groups * B, 2 * B)),
+            near(tab.shape),
+            near((8, 2 * B), F32),
         ],
-        (pos, mask, tally, own_rows, tab),
-        [SM, ANY, ANY, VM, VM],
+        (made, far(mask), far(tally), own, far(tab)),
+        [ANY, ANY, ANY, VM, ANY],
         [VM] * 4,
-        scratch=[pltpu.SMEM((n_r,), jnp.int32)] * 2 + [pltpu.SemaphoreType.DMA((2,))],
+        scratch=[pltpu.SMEM((n_r,), jnp.int32)] * 2 + [pltpu.SemaphoreType.DMA((3,))],
         name="own_places",
     )
     p_hi, p_lo = call(
-        functools.partial(places_body, n_r, keep),
-        [jax.ShapeDtypeStruct((B, blocks * n_r * keep), BF16)] * 2,
-        (shares, mine, other, tab),
-        [VM] * 4,
+        functools.partial(places_body, keep),
+        [near((B, blocks * n_r * keep))] * 2,
+        (shares, tab, bundles),
+        [VM] * 3,
         [VM, VM],
         name="places",
     )
     input_grad = call(
         functools.partial(input_grad_body, n_t, n_r, cp),
         jax.ShapeDtypeStruct((tok, cols), BF16),
-        (pos, mine, other, *parts),
-        [SM] + [VM] * (2 + n_t),
+        (bundles, *parts),
+        [VM] * (1 + n_t),
         VM,
         scratch=[pltpu.VMEM((n_t * B, cols), BF16)],
         flops=2 * tok * n_t * B * cols,
@@ -409,25 +397,34 @@
 
     ship = call(
         functools.partial(kept_body, n_t, keep),
-        jax.ShapeDtypeStruct((keep, width), BF16),
-        (pos, vel[0], a_own, tab, p_hi, *grads),
-        [SM] + [VM] * 3 + [ANY] + [VM] * n_t,
+        near((keep, width)),
+        (vel[0], a_own, tab, p_hi, *grads),
+        [VM] * 3 + [ANY] + [VM] * n_t,
         VM,
         flops=6 * B * B * width,
         nbytes=B * width * 6,
         name="kept_rows",
     )
-    mine, other = share(ship, "join_kept")
+    ships = [ship] + [swap(ship, 2 * i) for i in range(1, half)]
     new = call(
         functools.partial(return_body, n_t, keep),
         jax.ShapeDtypeStruct((B, width), F32),
-        (pos, vel[0], p_own, tab, ship, *grads),
-        [SM] + [VM] * (4 + n_t),
+        (vel[0], p_own, tab, ship, *grads),
+        [VM] * (4 + n_t),
         VM,
         flops=6 * B * B * width,
         nbytes=B * width * 10,
         name="new_momentums",
     )
+    mine = call(
+        join_body,
+        near((half, keep, width)),
+        (far(new), *ships),
+        [ANY] + [VM] * half,
+        VM,
+        name="join_kept",
+    )
+    other = swap(mine, 1)
     update = call(
         functools.partial(update_body, n_r, keep),
         jax.ShapeDtypeStruct((B, width), F32),

time: 55.3 us -> 41.3 us (0.75)
  waiting for transfers between devices: 17.9 us -> 5.19 us
  blocking collectives: 0 us -> 10.4 us
  starting transfers between devices: 19.1 us -> 15.5 us
  Pallas kernels: 12.7 us -> 9.27 us
  local copies, waits for them, and re-layouts: 3.34 us -> 0.01 us
  other arithmetic: 0.7 us -> 0 us
    all_gather x0 -> x1, blocking collectives: none -> 10.4 us  [per_device(): bundles = lax.all_gather(bundle, 'replica', axis=0)]
    ppermute x6, waiting for transfers between devices: 11 us -> 2.62 us  [shift(): return lax.ppermute(x, 'tensor', [(i, (i + k) % n_t) for i in range(n_t)])]
    ppermute x8 -> x4, waiting for transfers between devices: 6.94 us -> 2.57 us  [swap(): return lax.ppermute(x, 'replica', [(i, i ^ m) for i in range(n_r)])]
    ppermute x8 -> x4, starting transfers between devices: 7.25 us -> 3.62 us  [swap(): return lax.ppermute(x, 'replica', [(i, i ^ m) for i in range(n_r)])]
    pallas_call x11 -> x10, Pallas kernels: 12.7 us -> 9.27 us  [call(): pl.pallas_call(body, out_shape=out_shape, in_specs=in_specs, out_specs=ou...]
    unnamed x23 -> x4, local copies, waits for them, and re-layouts: 2.48 us -> 0.01 us
    another operation x1 -> x0, local copies, waits for them, and re-layouts: 0.85 us -> none  [per_device(): lines[0, 0].reshape(groups, B // 2)]
    another operation x1 -> x0, other arithmetic: 0.62 us -> none  [per_device(): pos = jnp.stack([rep, ten])]
  transfers between devices with their start and end apart: 14 -> 10, of which waited for: 10 -> 5; matrix products, arithmetic and copies ran while one was open for 3% -> 0% of each run, Pallas kernels for 11% -> 12%
where the time goes in v4:
time: 41.3 us; the launch traced here: 41.1 us
  starting transfers between devices  15.5 us (38%)
  blocking collectives  10.4 us (25%)
  Pallas kernels  9.27 us (22%)
  waiting for transfers between devices  5.19 us (13%)
  between operations  0.74 us (2%)
    ppermute x6, starting transfers between devices, shift(): return lax.ppermute(x, 'tensor', [(i, (i + k) % n_t) for i in range(n_t)])  11.9 us
    all_gather x1, blocking collectives, per_device(): bundles = lax.all_gather(bundle, 'replica', axis=0)  10.4 us
    pallas_call x10, Pallas kernels, call(): pl.pallas_call(body, out_shape=out_shape, in_specs=in_specs, out_specs=ou...  9.27 us
    ppermute x4, starting transfers between devices, swap(): return lax.ppermute(x, 'replica', [(i, i ^ m) for i in range(n_r)])  3.62 us
    ppermute x6, waiting for transfers between devices, shift(): return lax.ppermute(x, 'tensor', [(i, (i + k) % n_t) for i in range(n_t)])  2.62 us
    ppermute x4, waiting for transfers between devices, swap(): return lax.ppermute(x, 'replica', [(i, i ^ m) for i in range(n_r)])  2.57 us
  transfers between devices with their start and end apart: 10, of which 5 were waited for; matrix products, arithmetic and copies ran while one was open for 0% of the time, Pallas kernels for 12%

profile of v4, /device:TPU:0, one launch (start us, length us, event | category | flops | bytes accessed | tf_op | source)
XLA Modules:
  0.0 41.1 jit_solution(15506498525435742766)
XLA Ops:
  0.6 0.0 copy-start.1
  0.6 1.1 %up_grads.1 = (bf16[144,128]{1,0:T(8,128)(2,1)S(1)}, bf16[144,128]{1,0:T(8,128)(2,1)S(1)}, bf16[144,128]{1,0:T(8,128)(2,1)S(1)}, bf16[144,128]{1,0:T(8,128)(2,1)S(1)}, bf16[128,1280]{1,0:T(8,128)(2,1)S(1)}) custom-call(bf16[64,128]{1,0:T(8,128)(2,1)} %bitcast.15, bf16[64,128]{1,0:T(8,128)(2,1)} %bitcast.16, bf16[64,5120]{1,0:T(8,128)(2,1)} %exp_ref.1, ...), custom_call_target="tpu_custom_call" | custom-call | bytes 819200 | tf_op jit(solution)/shard_map/up_grads/pallas_call | solution.py:83
  1.8 3.1 %collective-permute-start = (bf16[144,128]{1,0:T(8,128)(2,1)S(1)}, bf16[144,128]{1,0:T(8,128)(2,1)S(1)}, u32[]{:S(2)}, u32[]{:S(2)}) collective-permute-start(bf16[144,128]{1,0:T(8,128)(2,1)S(1)} %get-tuple-element.20), channel_id=1, source_target_pairs={{0,1},{1,2},{2,3},{3,0},{4,5},{5,6},{6,7},{7,4},{8,9},{9,10},{10,1... | collective-permute-start | bytes 110600 | tf_op jit(solution)/shard_map/ppermute | solution.py:310
  4.9 2.6 %collective-permute-start.1 = (bf16[144,128]{1,0:T(8,128)(2,1)S(1)}, bf16[144,128]{1,0:T(8,128)(2,1)S(1)}, u32[]{:S(2)}, u32[]{:S(2)}) collective-permute-start(bf16[144,128]{1,0:T(8,128)(2,1)S(1)} %get-tuple-element.21), channel_id=1, source_target_pairs={{0,2},{1,3},{2,0},{3,1},{4,6},{5,7},{6,4},{7,5},{8,10},{9,11},{10,... | collective-permute-start | bytes 110600 | tf_op jit(solution)/shard_map/ppermute | solution.py:310
  7.4 1.3 %collective-permute-start.2 = (bf16[144,128]{1,0:T(8,128)(2,1)S(1)}, bf16[144,128]{1,0:T(8,128)(2,1)S(1)}, u32[]{:S(2)}, u32[]{:S(2)}) collective-permute-start(bf16[144,128]{1,0:T(8,128)(2,1)S(1)} %get-tuple-element.22), channel_id=1, source_target_pairs={{0,3},{1,0},{2,1},{3,2},{4,7},{5,4},{6,5},{7,6},{8,11},{9,8},{10,9... | collective-permute-start | bytes 110600 | tf_op jit(solution)/shard_map/ppermute | solution.py:310
  8.8 0.0 collective-permute-done.refs_1_
  8.8 1.3 %collective-permute-done.1.refs_2_ = bf16[144,128]{1,0:T(8,128)(2,1)S(1)} collective-permute-done((bf16[144,128]{1,0:T(8,128)(2,1)S(1)}, bf16[144,128]{1,0:T(8,128)(2,1)S(1)}, u32[]{:S(2)}, u32[]{:S(2)}) %collective-permute-start.1) | collective-permute-done | bytes 36896 | tf_op jit(solution)/shard_map/ppermute | solution.py:310
  10.1 1.3 %collective-permute-done.2.refs_3_ = bf16[144,128]{1,0:T(8,128)(2,1)S(1)} collective-permute-done((bf16[144,128]{1,0:T(8,128)(2,1)S(1)}, bf16[144,128]{1,0:T(8,128)(2,1)S(1)}, u32[]{:S(2)}, u32[]{:S(2)}) %collective-permute-start.2) | collective-permute-done | bytes 36896 | tf_op jit(solution)/shard_map/ppermute | solution.py:310
  11.4 0.3 weight_grads.1
  11.7 1.0 %collective-permute-start.4 = (bf16[64,1280]{1,0:T(8,128)(2,1)S(1)}, bf16[64,1280]{1,0:T(8,128)(2,1)S(1)}, u32[]{:S(2)}, u32[]{:S(2)}) collective-permute-start(bf16[64,1280]{1,0:T(8,128)(2,1)S(1)} %get-tuple-element.30), channel_id=1, source_target_pairs={{0,2},{1,3},{2,0},{3,1},{4,6},{5,7},{6,4},{7,5},{8,10},{9,11},{10,... | collective-permute-start | bytes 491528 | tf_op jit(solution)/shard_map/ppermute | solution.py:310
  12.7 2.8 %collective-permute-start.5 = (bf16[64,1280]{1,0:T(8,128)(2,1)S(1)}, bf16[64,1280]{1,0:T(8,128)(2,1)S(1)}, u32[]{:S(2)}, u32[]{:S(2)}) collective-permute-start(bf16[64,1280]{1,0:T(8,128)(2,1)S(1)} %get-tuple-element.31), channel_id=1, source_target_pairs={{0,1},{1,2},{2,3},{3,0},{4,5},{5,6},{6,7},{7,4},{8,9},{9,10},{10,1... | collective-permute-start | bytes 491528 | tf_op jit(solution)/shard_map/ppermute | solution.py:310
  15.5 1.1 %collective-permute-start.3 = (bf16[64,1280]{1,0:T(8,128)(2,1)S(1)}, bf16[64,1280]{1,0:T(8,128)(2,1)S(1)}, u32[]{:S(2)}, u32[]{:S(2)}) collective-permute-start(bf16[64,1280]{1,0:T(8,128)(2,1)S(1)} %get-tuple-element.23.after), channel_id=1, source_target_pairs={{0,3},{1,0},{2,1},{3,2},{4,7},{5,4},{6,5},{7,6},{8,11},{9,8},{10,9... | collective-permute-start | bytes 491528 | tf_op jit(solution)/shard_map/ppermute | solution.py:310
  16.6 0.0 copy-done.1
  16.6 1.5 %own_places.1 = (bf16[64,2560]{1,0:T(8,128)(2,1)S(1)}, bf16[1280,128]{1,0:T(8,128)(2,1)S(1)}, bf16[1152,256]{1,0:T(8,128)(2,1)S(1)}, f32[8,128]{1,0:T(8,128)S(1)}) custom-call(bf16[64,1280]{1,0:T(8,128)(2,1)S(1)} %get-tuple-element.23.after, s32[8]{0:T(128)} %mask.1, s32[8]{0:T(128)} %tally.1, s32[8,80]{1,0:T(8,128)S(1)} %bitcast.12, ...), custom_call_target="tpu_custom_call" | custom-call | tf_op jit(solution)/shard_map/own_places/pallas_call | solution.py:83
  18.1 0.0 copy-start
  18.1 10.4 %all-gather = bf16[2688,128]{1,0:T(8,128)(2,1)S(1)} all-gather(bf16[336,128]{1,0:T(8,128)(2,1)S(1)} %bundle.1), channel_id=2, replica_groups=mesh['replica'=8,'tensor'=4] {'replica'}, dimensions={0}, use_global_device_ids=true | all-gather | bytes 774144 | tf_op jit(solution)/shard_map/all_gather | solution.py:362
  28.5 0.6 %places.1 = (bf16[64,5120]{1,0:T(8,128)(2,1)S(1)}, bf16[64,5120]{1,0:T(8,128)(2,1)S(1)}) custom-call(f32[8,128]{1,0:T(8,128)S(1)} %get-tuple-element.27.w_ref, bf16[1152,256]{1,0:T(8,128)(2,1)S(1)} %get-tuple-element.25.tab, bf16[8,336,128]{2,1,0:T(8,128)(2,1)S(1)} %bitcast.8), custom_call_target="tpu_custom_call" | custom-call | tf_op jit(solution)/shard_map/places/pallas_call | solution.py:83
  29.1 0.0 collective-permute-done.4.refs_2_
  29.1 0.0 collective-permute-done.5.refs_3_
  29.1 0.0 collective-permute-done.3.refs_1_
  29.1 0.0 copy-done
  29.1 0.7 %kept_rows.1.ship.refs_0_ = bf16[8,5120]{1,0:T(8,128)(2,1)S(1)} custom-call(f32[64,5120]{1,0:T(8,128)S(1)} %bitcast.10, bf16[1280,128]{1,0:T(8,128)(2,1)S(1)} %get-tuple-element.26.a_ref, bf16[1152,256]{1,0:T(8,128)(2,1)S(1)} %get-tuple-element.25.tab, bf16[64,5120]{1,0:T(8,128)(2,1)S(1)} %get-tuple-element.28.after.p_hi, ...), custom_call_target="tpu_custom_call" | custom-call | flops 125829120 | bytes 1966080 | tf_op jit(solution)/shard_map/kept_rows/pallas_call | solution.py:83
  29.8 1.5 %collective-permute-start.8 = (bf16[8,5120]{1,0:T(8,128)(2,1)S(1)}, bf16[8,5120]{1,0:T(8,128)(2,1)S(1)}, u32[]{:S(2)}, u32[]{:S(2)}) collective-permute-start(bf16[8,5120]{1,0:T(8,128)(2,1)S(1)} %kept_rows.1.ship.refs_0_), channel_id=1, source_target_pairs={{0,24},{4,28},{8,16},{12,20},{16,8},{20,12},{24,0},{28,4},{1,25},{... | collective-permute-start | bytes 245768 | tf_op jit(solution)/shard_map/ppermute | solution.py:320
  31.4 1.5 %collective-permute-start.7 = (bf16[8,5120]{1,0:T(8,128)(2,1)S(1)}, bf16[8,5120]{1,0:T(8,128)(2,1)S(1)}, u32[]{:S(2)}, u32[]{:S(2)}) collective-permute-start(bf16[8,5120]{1,0:T(8,128)(2,1)S(1)} %kept_rows.1.ship.refs_0_), channel_id=1, source_target_pairs={{0,16},{4,20},{8,24},{12,28},{16,0},{20,4},{24,8},{28,12},{1,17},{... | collective-permute-start | bytes 245768 | tf_op jit(solution)/shard_map/ppermute | solution.py:320
  32.8 0.5 %collective-permute-start.6 = (bf16[8,5120]{1,0:T(8,128)(2,1)S(1)}, bf16[8,5120]{1,0:T(8,128)(2,1)S(1)}, u32[]{:S(2)}, u32[]{:S(2)}) collective-permute-start(bf16[8,5120]{1,0:T(8,128)(2,1)S(1)} %kept_rows.1.ship.refs_0_), channel_id=1, source_target_pairs={{0,8},{4,12},{8,0},{12,4},{16,24},{20,28},{24,16},{28,20},{1,9},{5... | collective-permute-start | bytes 245768 | tf_op jit(solution)/shard_map/ppermute | solution.py:320
  33.4 1.9 %new_momentums.1.after = f32[64,5120]{1,0:T(8,128)} custom-call(f32[64,5120]{1,0:T(8,128)S(1)} %bitcast.11, bf16[64,2560]{1,0:T(8,128)(2,1)S(1)} %get-tuple-element.24.p_ref, bf16[1152,256]{1,0:T(8,128)(2,1)S(1)} %get-tuple-element.25.tab, bf16[8,5120]{1,0:T(8,128)(2,1)S(1)} %kept_rows.1.ship.refs_0_, f32[64,1280]{1,0:T(8,128)S(1)} %get-tuple-element.29.refs_0_, ...), custom_call_target="tpu_custom_call" | custom-call | flops 125829120 | bytes 3276800 | tf_op jit(solution)/shard_map/new_momentums/pallas_call | solution.py:83
  35.2 0.5 %collective-permute-done.8.refs_3_ = bf16[8,5120]{1,0:T(8,128)(2,1)S(1)} collective-permute-done((bf16[8,5120]{1,0:T(8,128)(2,1)S(1)}, bf16[8,5120]{1,0:T(8,128)(2,1)S(1)}, u32[]{:S(2)}, u32[]{:S(2)}) %collective-permute-start.8) | collective-permute-done | bytes 81952 | tf_op jit(solution)/shard_map/ppermute | solution.py:320
  35.8 1.4 %collective-permute-done.7.refs_2_ = bf16[8,5120]{1,0:T(8,128)(2,1)S(1)} collective-permute-done((bf16[8,5120]{1,0:T(8,128)(2,1)S(1)}, bf16[8,5120]{1,0:T(8,128)(2,1)S(1)}, u32[]{:S(2)}, u32[]{:S(2)}) %collective-permute-start.7) | collective-permute-done | bytes 81952 | tf_op jit(solution)/shard_map/ppermute | solution.py:320
  37.2 0.0 collective-permute-done.6.refs_1_
  37.3 0.1 collective-permute-start.9
  37.4 1.1 %input_grads.1 = bf16[128,1280]{1,0:T(8,128)(2,1)} custom-call(bf16[8,336,128]{2,1,0:T(8,128)(2,1)S(1)} %bitcast.9, bf16[144,128]{1,0:T(8,128)(2,1)S(1)} %get-tuple-element.19.refs_0_, bf16[144,128]{1,0:T(8,128)(2,1)S(1)} %collective-permute-done.refs_1_, bf16[144,128]{1,0:T(8,128)(2,1)S(1)} %collective-permute-done.1.refs_2_, ...), custom_call_target="tpu_custom_call" | custom-call | flops 83886080 | bytes 983040 | tf_op jit(solution)/shard_map/input_grads/pallas_call | solution.py:83
  38.5 0.5 %collective-permute-done.9.other = bf16[4,8,5120]{2,1,0:T(8,128)(2,1)S(1)} collective-permute-done((bf16[4,8,5120]{2,1,0:T(8,128)(2,1)S(1)}, bf16[4,8,5120]{2,1,0:T(8,128)(2,1)S(1)}, u32[]{:S(2)}, u32[]{:S(2)}) %collective-permute-start.9) | collective-permute-done | bytes 327712 | tf_op jit(solution)/shard_map/ppermute | solution.py:320
  39.0 2.1 %updates.1 = f32[64,5120]{1,0:T(8,128)} custom-call(bf16[64,5120]{1,0:T(8,128)(2,1)S(1)} %get-tuple-element.28.after.p_hi, bf16[64,5120]{1,0:T(8,128)(2,1)S(1)} %get-tuple-element.32.p_lo, bf16[1152,256]{1,0:T(8,128)(2,1)S(1)} %get-tuple-element.25.tab, bf16[4,8,5120]{2,1,0:T(8,128)(2,1)S(1)} %join_kept.1.mine, ...), custom_call_target="tpu_custom_call" | custom-call | flops 671088640 | bytes 2621440 | tf_op jit(solution)/shard_map/updates/pallas_call | solution.py:83
  (2 shorter events, 0.0 us)
Async XLA Ops:
  0.6 15.9 %copy-start.1 = (s32[1,1,80,8]{2,3,1,0:T(8,128)S(1)}, s32[1,1,80,8]{2,3,1,0:T(8,128)}, u32[]{:S(2)}) copy-start(s32[1,1,80,8]{2,3,1,0:T(8,128)} %param.14) | copy-start | bytes 7684
  1.8 7.0 %collective-permute-start = (bf16[144,128]{1,0:T(8,128)(2,1)S(1)}, bf16[144,128]{1,0:T(8,128)(2,1)S(1)}, u32[]{:S(2)}, u32[]{:S(2)}) collective-permute-start(bf16[144,128]{1,0:T(8,128)(2,1)S(1)} %get-tuple-element.20), channel_id=1, source_target_pairs={{0,1},{1,2},{2,3},{3,0},{4,5},{5,6},{6,7},{7,4},{8,9},{9,10},{10,1... | collective-permute-start | bytes 110600 | tf_op jit(solution)/shard_map/ppermute | solution.py:310
  4.9 5.2 %collective-permute-start.1 = (bf16[144,128]{1,0:T(8,128)(2,1)S(1)}, bf16[144,128]{1,0:T(8,128)(2,1)S(1)}, u32[]{:S(2)}, u32[]{:S(2)}) collective-permute-start(bf16[144,128]{1,0:T(8,128)(2,1)S(1)} %get-tuple-element.21), channel_id=1, source_target_pairs={{0,2},{1,3},{2,0},{3,1},{4,6},{5,7},{6,4},{7,5},{8,10},{9,11},{10,... | collective-permute-start | bytes 110600 | tf_op jit(solution)/shard_map/ppermute | solution.py:310
  7.4 4.0 %collective-permute-start.2 = (bf16[144,128]{1,0:T(8,128)(2,1)S(1)}, bf16[144,128]{1,0:T(8,128)(2,1)S(1)}, u32[]{:S(2)}, u32[]{:S(2)}) collective-permute-start(bf16[144,128]{1,0:T(8,128)(2,1)S(1)} %get-tuple-element.22), channel_id=1, source_target_pairs={{0,3},{1,0},{2,1},{3,2},{4,7},{5,4},{6,5},{7,6},{8,11},{9,8},{10,9... | collective-permute-start | bytes 110600 | tf_op jit(solution)/shard_map/ppermute | solution.py:310
  11.7 17.4 %collective-permute-start.4 = (bf16[64,1280]{1,0:T(8,128)(2,1)S(1)}, bf16[64,1280]{1,0:T(8,128)(2,1)S(1)}, u32[]{:S(2)}, u32[]{:S(2)}) collective-permute-start(bf16[64,1280]{1,0:T(8,128)(2,1)S(1)} %get-tuple-element.30), channel_id=1, source_target_pairs={{0,2},{1,3},{2,0},{3,1},{4,6},{5,7},{6,4},{7,5},{8,10},{9,11},{10,... | collective-permute-start | bytes 491528 | tf_op jit(solution)/shard_map/ppermute | solution.py:310
  12.7 16.4 %collective-permute-start.5 = (bf16[64,1280]{1,0:T(8,128)(2,1)S(1)}, bf16[64,1280]{1,0:T(8,128)(2,1)S(1)}, u32[]{:S(2)}, u32[]{:S(2)}) collective-permute-start(bf16[64,1280]{1,0:T(8,128)(2,1)S(1)} %get-tuple-element.31), channel_id=1, source_target_pairs={{0,1},{1,2},{2,3},{3,0},{4,5},{5,6},{6,7},{7,4},{8,9},{9,10},{10,1... | collective-permute-start | bytes 491528 | tf_op jit(solution)/shard_map/ppermute | solution.py:310
  15.5 13.6 %collective-permute-start.3 = (bf16[64,1280]{1,0:T(8,128)(2,1)S(1)}, bf16[64,1280]{1,0:T(8,128)(2,1)S(1)}, u32[]{:S(2)}, u32[]{:S(2)}) collective-permute-start(bf16[64,1280]{1,0:T(8,128)(2,1)S(1)} %get-tuple-element.23.after), channel_id=1, source_target_pairs={{0,3},{1,0},{2,1},{3,2},{4,7},{5,4},{6,5},{7,6},{8,11},{9,8},{10,9... | collective-permute-start | bytes 491528 | tf_op jit(solution)/shard_map/ppermute | solution.py:310
  18.1 11.1 %copy-start = (f32[1,64,5120]{2,1,0:T(8,128)S(1)}, f32[1,64,5120]{2,1,0:T(8,128)}, u32[]{:S(2)}) copy-start(f32[1,64,5120]{2,1,0:T(8,128)} %param.13) | copy-start | bytes 3932164
  29.8 6.0 %collective-permute-start.8 = (bf16[8,5120]{1,0:T(8,128)(2,1)S(1)}, bf16[8,5120]{1,0:T(8,128)(2,1)S(1)}, u32[]{:S(2)}, u32[]{:S(2)}) collective-permute-start(bf16[8,5120]{1,0:T(8,128)(2,1)S(1)} %kept_rows.1.ship.refs_0_), channel_id=1, source_target_pairs={{0,24},{4,28},{8,16},{12,20},{16,8},{20,12},{24,0},{28,4},{1,25},{... | collective-permute-start | bytes 245768 | tf_op jit(solution)/shard_map/ppermute | solution.py:320
  31.4 5.9 %collective-permute-start.7 = (bf16[8,5120]{1,0:T(8,128)(2,1)S(1)}, bf16[8,5120]{1,0:T(8,128)(2,1)S(1)}, u32[]{:S(2)}, u32[]{:S(2)}) collective-permute-start(bf16[8,5120]{1,0:T(8,128)(2,1)S(1)} %kept_rows.1.ship.refs_0_), channel_id=1, source_target_pairs={{0,16},{4,20},{8,24},{12,28},{16,0},{20,4},{24,8},{28,12},{1,17},{... | collective-permute-start | bytes 245768 | tf_op jit(solution)/shard_map/ppermute | solution.py:320
  32.8 4.4 %collective-permute-start.6 = (bf16[8,5120]{1,0:T(8,128)(2,1)S(1)}, bf16[8,5120]{1,0:T(8,128)(2,1)S(1)}, u32[]{:S(2)}, u32[]{:S(2)}) collective-permute-start(bf16[8,5120]{1,0:T(8,128)(2,1)S(1)} %kept_rows.1.ship.refs_0_), channel_id=1, source_target_pairs={{0,8},{4,12},{8,0},{12,4},{16,24},{20,28},{24,16},{28,20},{1,9},{5... | collective-permute-start | bytes 245768 | tf_op jit(solution)/shard_map/ppermute | solution.py:320
  37.3 1.7 %collective-permute-start.9 = (bf16[4,8,5120]{2,1,0:T(8,128)(2,1)S(1)}, bf16[4,8,5120]{2,1,0:T(8,128)(2,1)S(1)}, u32[]{:S(2)}, u32[]{:S(2)}) collective-permute-start(bf16[4,8,5120]{2,1,0:T(8,128)(2,1)S(1)} %join_kept.1.mine), channel_id=1, source_target_pairs={{0,4},{4,0},{8,12},{12,8},{16,20},{20,16},{24,28},{28,24},{1,5},{5... | collective-permute-start | bytes 983048 | tf_op jit(solution)/shard_map/ppermute | solution.py:320

commit v5 on v4

--- a/solution.py
+++ b/solution.py
@@ -121,12 +121,12 @@
     copies[3].wait()
 
 
-def grads_body(n_t, act, *refs):
-    ups, outs = refs[:n_t], refs[n_t:]
+def grads_body(n, act, after, *refs):
+    ups, outs = refs[:n], refs[n:]
     up = jnp.concatenate([u[:B, :] for u in ups], axis=0)
     for c in range(0, act.shape[1], G):
         g = dot(up, act[:, c : c + G])
-        for k in range(n_t):
+        for k in range(n):
             outs[k][:, c : c + G] = g[k * B : (k + 1) * B].astype(outs[k].dtype)
 
 
@@ -140,12 +140,12 @@
     out[n_t * n :, :] = jnp.concatenate([rows, jnp.zeros((16 - keep, 128), F32)], axis=0).astype(BF16)
 
 
-def join_body(after, *refs):
+def join_body(after, after_too, *refs):
     for i, ref in enumerate(refs[:-1]):
         refs[-1][i] = ref[...]
 
 
-def own_body(n_r, keep, after, mask, tally, lines, tab, p_ref, a_ref, tab_ref, w_ref, mask_s, tally_s, sems):
+def own_body(n_r, keep, mask, tally, lines, tab, p_ref, a_ref, tab_ref, w_ref, mask_s, tally_s, sems):
     copies = [
         pltpu.make_async_copy(src, dst, sems.at[i])
         for i, (src, dst) in enumerate([(mask, mask_s), (tally, tally_s), (tab, tab_ref)])
@@ -309,16 +309,12 @@
     def shift(x, k):
         return lax.ppermute(x, "tensor", [(i, (i + k) % n_t) for i in range(n_t)])
 
-    def shifts(xs, sign):
-        order = sorted(range(1, n_t), key=lambda k: -min(k, n_t - k))
-        got = {0: xs[0]}
-        for k in order:
-            got[k] = shift(xs[k], sign * k)
-        return [got[k] for k in range(n_t)]
+    order = sorted(range(1, n_t), key=lambda k: -min(k, n_t - k))
 
     def swap(x, m):
         return lax.ppermute(x, "replica", [(i, i ^ m) for i in range(n_r)])
 
+    own = lines[0, 0].T
     tiles = cols // cp // 128
     nr = B // rp
     *parts, act = call(
@@ -336,30 +332,7 @@
         nbytes=act.size * 4 + nr * width * 2,
         name="up_grads",
     )
-    parts = shifts(parts, 1)
-
-    grads = call(
-        functools.partial(grads_body, n_t),
-        [near((B, cols), F32)] + [near((B, cols))] * (n_t - 1),
-        (act, *parts),
-        [VM] * (n_t + 1),
-        [VM] * n_t,
-        nbytes=act.size * 2 + n_t * B * cols * 2,
-        name="weight_grads",
-    )
-    made = grads[1]
-    grads = shifts(grads, -1)
-
-    own = lines[0, 0].T
-    bundle = call(
-        functools.partial(bundle_body, n_t, keep),
-        near((n_t * tiles * nr + 16, 128)),
-        (made, own, *parts),
-        [ANY] + [VM] * (n_t + 1),
-        VM,
-        name="bundle",
-    )
-    bundles = lax.all_gather(bundle, "replica", axis=0)
+    parts = [parts[0]] + [shift(parts[k], k) for k in range(1, n_t)]
 
     p_own, a_own, tab, shares = call(
         functools.partial(own_body, n_r, keep),
@@ -369,12 +342,40 @@
             near(tab.shape),
             near((8, 2 * B), F32),
         ],
-        (made, far(mask), far(tally), own, far(tab)),
-        [ANY, ANY, ANY, VM, ANY],
+        (far(mask), far(tally), own, far(tab)),
+        [ANY, ANY, VM, ANY],
         [VM] * 4,
         scratch=[pltpu.SMEM((n_r,), jnp.int32)] * 2 + [pltpu.SemaphoreType.DMA((3,))],
         name="own_places",
     )
+
+    def grads_of(ks, after):
+        return call(
+            functools.partial(grads_body, len(ks)),
+            [near((B, cols), BF16 if k else F32) for k in ks],
+            (act, after, *[parts[k] for k in ks]),
+            [VM, ANY] + [VM] * len(ks),
+            [VM] * len(ks),
+            name="weight_grads",
+        )
+
+    grads = {}
+    for k in order[:-1]:
+        (grads[k],) = grads_of([k], act)
+    made, grads[0] = grads_of([order[-1], 0], shares)
+    grads[order[-1]] = made
+    grads = [grads[0]] + [shift(grads[k], -k) for k in range(1, n_t)]
+
+    bundle = call(
+        functools.partial(bundle_body, n_t, keep),
+        near((n_t * tiles * nr + 16, 128)),
+        (made, own, *parts),
+        [ANY] + [VM] * (n_t + 1),
+        VM,
+        name="bundle",
+    )
+    bundles = lax.all_gather(bundle, "replica", axis=0)
+
     p_hi, p_lo = call(
         functools.partial(places_body, keep),
         [near((B, blocks * n_r * keep))] * 2,
@@ -398,7 +399,7 @@
     ship = call(
         functools.partial(kept_body, n_t, keep),
         near((keep, width)),
-        (vel[0], a_own, tab, p_hi, *grads),
+        (vel[0], a_own, tab, bundles, *grads),
         [VM] * 3 + [ANY] + [VM] * n_t,
         VM,
         flops=6 * B * B * width,
@@ -419,8 +420,8 @@
     mine = call(
         join_body,
         near((half, keep, width)),
-        (far(new), *ships),
-        [ANY] + [VM] * half,
+        (far(new), p_hi, *ships),
+        [ANY, ANY] + [VM] * half,
         VM,
         name="join_kept",
     )

time: 41.3 us -> 39.2 us (0.949)
  starting transfers between devices: 15.5 us -> 13 us
  local copies, waits for them, and re-layouts: 0.01 us -> 0.69 us
  waiting for transfers between devices: 5.19 us -> 4.54 us
    ppermute x6, starting transfers between devices: 11.9 us -> 9.4 us  [shift(): return lax.ppermute(x, 'tensor', [(i, (i + k) % n_t) for i in range(n_t)])]
    unnamed x4, local copies, waits for them, and re-layouts: 0.01 us -> 0.69 us
    ppermute x4, waiting for transfers between devices: 2.57 us -> 1.99 us  [swap(): return lax.ppermute(x, 'replica', [(i, i ^ m) for i in range(n_r)])]
    pallas_call x10 -> x12, Pallas kernels: 9.27 us -> 9.55 us  [call(): pl.pallas_call(body, out_shape=out_shape, in_specs=in_specs, out_specs=ou...]
  transfers between devices with their start and end apart: 10 -> 10, of which waited for: 5 -> 4; matrix products, arithmetic and copies ran while one was open for 0% -> 0% of each run, Pallas kernels for 12% -> 14%
where the time goes in v5:
time: 39.2 us; the launch traced here: 38.9 us
  starting transfers between devices  13 us (33%)
  blocking collectives  10.4 us (27%)
  Pallas kernels  9.55 us (24%)
  waiting for transfers between devices  4.54 us (12%)
  between operations  0.71 us (2%)
  local copies, waits for them, and re-layouts  0.69 us (2%)
    all_gather x1, blocking collectives, per_device(): bundles = lax.all_gather(bundle, 'replica', axis=0)  10.4 us
    pallas_call x12, Pallas kernels, call(): pl.pallas_call(body, out_shape=out_shape, in_specs=in_specs, out_specs=ou...  9.55 us
    ppermute x6, starting transfers between devices, shift(): return lax.ppermute(x, 'tensor', [(i, (i + k) % n_t) for i in range(n_t)])  9.4 us
    ppermute x4, starting transfers between devices, swap(): return lax.ppermute(x, 'replica', [(i, i ^ m) for i in range(n_r)])  3.62 us
    ppermute x6, waiting for transfers between devices, shift(): return lax.ppermute(x, 'tensor', [(i, (i + k) % n_t) for i in range(n_t)])  2.54 us
    ppermute x4, waiting for transfers between devices, swap(): return lax.ppermute(x, 'replica', [(i, i ^ m) for i in range(n_r)])  1.99 us
  transfers between devices with their start and end apart: 10, of which 4 were waited for; matrix products, arithmetic and copies ran while one was open for 0% of the time, Pallas kernels for 14%

profile of v5, /device:TPU:0, one launch (start us, length us, event | category | flops | bytes accessed | tf_op | source)
XLA Modules:
  0.0 38.9 jit_solution(15748546136972125671)
XLA Ops:
  0.6 1.1 %up_grads.1 = (bf16[144,128]{1,0:T(8,128)(2,1)S(1)}, bf16[144,128]{1,0:T(8,128)(2,1)S(1)}, bf16[144,128]{1,0:T(8,128)(2,1)S(1)}, bf16[144,128]{1,0:T(8,128)(2,1)S(1)}, bf16[128,1280]{1,0:T(8,128)(2,1)S(1)}) custom-call(bf16[64,128]{1,0:T(8,128)(2,1)} %bitcast.16, bf16[64,128]{1,0:T(8,128)(2,1)} %bitcast.17, bf16[64,5120]{1,0:T(8,128)(2,1)} %exp_ref.1, ...), custom_call_target="tpu_custom_call" | custom-call | bytes 819200 | tf_op jit(solution)/shard_map/up_grads/pallas_call | solution.py:83
  1.8 3.1 %collective-permute-start.1 = (bf16[144,128]{1,0:T(8,128)(2,1)S(1)}, bf16[144,128]{1,0:T(8,128)(2,1)S(1)}, u32[]{:S(2)}, u32[]{:S(2)}) collective-permute-start(bf16[144,128]{1,0:T(8,128)(2,1)S(1)} %get-tuple-element.21), channel_id=1, source_target_pairs={{0,1},{1,2},{2,3},{3,0},{4,5},{5,6},{6,7},{7,4},{8,9},{9,10},{10,1... | collective-permute-start | bytes 110600 | tf_op jit(solution)/shard_map/ppermute | solution.py:310
  4.8 2.6 %collective-permute-start.2 = (bf16[144,128]{1,0:T(8,128)(2,1)S(1)}, bf16[144,128]{1,0:T(8,128)(2,1)S(1)}, u32[]{:S(2)}, u32[]{:S(2)}) collective-permute-start(bf16[144,128]{1,0:T(8,128)(2,1)S(1)} %get-tuple-element.22), channel_id=1, source_target_pairs={{0,2},{1,3},{2,0},{3,1},{4,6},{5,7},{6,4},{7,5},{8,10},{9,11},{10,... | collective-permute-start | bytes 110600 | tf_op jit(solution)/shard_map/ppermute | solution.py:310
  7.4 1.3 %collective-permute-start = (bf16[144,128]{1,0:T(8,128)(2,1)S(1)}, bf16[144,128]{1,0:T(8,128)(2,1)S(1)}, u32[]{:S(2)}, u32[]{:S(2)}) collective-permute-start(bf16[144,128]{1,0:T(8,128)(2,1)S(1)} %get-tuple-element.18), channel_id=1, source_target_pairs={{0,3},{1,0},{2,1},{3,2},{4,7},{5,4},{6,5},{7,6},{8,11},{9,8},{10,9... | collective-permute-start | bytes 110600 | tf_op jit(solution)/shard_map/ppermute | solution.py:310
  8.8 0.0 copy-start.1
  8.8 0.7 %copy-done.1 = s32[1,1,80,8]{2,3,1,0:T(8,128)S(1)} copy-done((s32[1,1,80,8]{2,3,1,0:T(8,128)S(1)}, s32[1,1,80,8]{2,3,1,0:T(8,128)}, u32[]{:S(2)}) %copy-start.1) | copy-done | bytes 2584
  9.5 1.5 %own_places.1 = (bf16[64,2560]{1,0:T(8,128)(2,1)S(1)}, bf16[1280,128]{1,0:T(8,128)(2,1)S(1)}, bf16[1152,256]{1,0:T(8,128)(2,1)S(1)}, f32[8,128]{1,0:T(8,128)S(1)}) custom-call(s32[8]{0:T(128)} %mask.1, s32[8]{0:T(128)} %tally.1, s32[8,80]{1,0:T(8,128)S(1)} %bitcast.13, bf16[1152,256]{1,0:T(8,128)(2,1)} %constant.2.clone.tab), custom_call_target="tpu_custom_call" | custom-call | tf_op jit(solution)/shard_map/own_places/pallas_call | solution.py:83
  11.0 0.0 collective-permute-done.1.refs_1_.refs_0_
  11.0 0.2 weight_grads.4
  11.2 0.0 copy-start
  11.2 0.5 %collective-permute-start.3 = (bf16[64,1280]{1,0:T(8,128)(2,1)S(1)}, bf16[64,1280]{1,0:T(8,128)(2,1)S(1)}, u32[]{:S(2)}, u32[]{:S(2)}) collective-permute-start(bf16[64,1280]{1,0:T(8,128)(2,1)S(1)} %weight_grads.4), channel_id=1, source_target_pairs={{0,3},{1,0},{2,1},{3,2},{4,7},{5,4},{6,5},{7,6},{8,11},{9,8},{10,9... | collective-permute-start | bytes 491528 | tf_op jit(solution)/shard_map/ppermute | solution.py:310
  11.7 0.0 collective-permute-done.2.refs_2_.refs_0_
  11.7 0.2 weight_grads.5
  11.9 1.7 %collective-permute-start.4 = (bf16[64,1280]{1,0:T(8,128)(2,1)S(1)}, bf16[64,1280]{1,0:T(8,128)(2,1)S(1)}, u32[]{:S(2)}, u32[]{:S(2)}) collective-permute-start(bf16[64,1280]{1,0:T(8,128)(2,1)S(1)} %weight_grads.5), channel_id=1, source_target_pairs={{0,2},{1,3},{2,0},{3,1},{4,6},{5,7},{6,4},{7,5},{8,10},{9,11},{10,... | collective-permute-start | bytes 491528 | tf_op jit(solution)/shard_map/ppermute | solution.py:310
  13.6 0.0 collective-permute-done.refs_0_.refs_3_
  13.6 0.2 weight_grads.3
  13.9 0.1 collective-permute-start.5
  14.0 10.4 %all-gather = bf16[2688,128]{1,0:T(8,128)(2,1)S(1)} all-gather(bf16[336,128]{1,0:T(8,128)(2,1)S(1)} %bundle.1), channel_id=2, replica_groups=mesh['replica'=8,'tensor'=4] {'replica'}, dimensions={0}, use_global_device_ids=true | all-gather | bytes 774144 | tf_op jit(solution)/shard_map/all_gather | solution.py:377
  24.4 0.0 collective-permute-done.3.refs_1_
  24.4 2.5 %collective-permute-done.4.refs_2_ = bf16[64,1280]{1,0:T(8,128)(2,1)S(1)} collective-permute-done((bf16[64,1280]{1,0:T(8,128)(2,1)S(1)}, bf16[64,1280]{1,0:T(8,128)(2,1)S(1)}, u32[]{:S(2)}, u32[]{:S(2)}) %collective-permute-start.4) | collective-permute-done | bytes 163872 | tf_op jit(solution)/shard_map/ppermute | solution.py:310
  27.0 0.0 collective-permute-done.5.refs_3_
  27.0 0.0 copy-done
  27.0 0.7 %kept_rows.1.ship.refs_0_ = bf16[8,5120]{1,0:T(8,128)(2,1)S(1)} custom-call(f32[64,5120]{1,0:T(8,128)S(1)} %bitcast.11, bf16[1280,128]{1,0:T(8,128)(2,1)S(1)} %get-tuple-element.25.a_ref, bf16[1152,256]{1,0:T(8,128)(2,1)S(1)} %get-tuple-element.24.tab, bf16[8,336,128]{2,1,0:T(8,128)(2,1)S(1)} %bitcast.8, f32[64,1280]{1,0:T(8,128)S(1)} %get-tuple-element.26.refs_0_, ...), custom_call_target="tpu_custom_call" | custom-call | flops 125829120 | bytes 1966080 | tf_op jit(solution)/shard_map/kept_rows/pallas_call | solution.py:83
  27.7 2.5 %collective-permute-start.8 = (bf16[8,5120]{1,0:T(8,128)(2,1)S(1)}, bf16[8,5120]{1,0:T(8,128)(2,1)S(1)}, u32[]{:S(2)}, u32[]{:S(2)}) collective-permute-start(bf16[8,5120]{1,0:T(8,128)(2,1)S(1)} %kept_rows.1.ship.refs_0_), channel_id=1, source_target_pairs={{0,24},{4,28},{8,16},{12,20},{16,8},{20,12},{24,0},{28,4},{1,25},{... | collective-permute-start | bytes 245768 | tf_op jit(solution)/shard_map/ppermute | solution.py:315
  30.2 0.5 %collective-permute-start.7 = (bf16[8,5120]{1,0:T(8,128)(2,1)S(1)}, bf16[8,5120]{1,0:T(8,128)(2,1)S(1)}, u32[]{:S(2)}, u32[]{:S(2)}) collective-permute-start(bf16[8,5120]{1,0:T(8,128)(2,1)S(1)} %kept_rows.1.ship.refs_0_), channel_id=1, source_target_pairs={{0,16},{4,20},{8,24},{12,28},{16,0},{20,4},{24,8},{28,12},{1,17},{... | collective-permute-start | bytes 245768 | tf_op jit(solution)/shard_map/ppermute | solution.py:315
  30.7 0.5 %collective-permute-start.6 = (bf16[8,5120]{1,0:T(8,128)(2,1)S(1)}, bf16[8,5120]{1,0:T(8,128)(2,1)S(1)}, u32[]{:S(2)}, u32[]{:S(2)}) collective-permute-start(bf16[8,5120]{1,0:T(8,128)(2,1)S(1)} %kept_rows.1.ship.refs_0_), channel_id=1, source_target_pairs={{0,8},{4,12},{8,0},{12,4},{16,24},{20,28},{24,16},{28,20},{1,9},{5... | collective-permute-start | bytes 245768 | tf_op jit(solution)/shard_map/ppermute | solution.py:315
  31.2 0.6 %places.1 = (bf16[64,5120]{1,0:T(8,128)(2,1)S(1)}, bf16[64,5120]{1,0:T(8,128)(2,1)S(1)}) custom-call(f32[8,128]{1,0:T(8,128)S(1)} %get-tuple-element.17.after.w_ref, bf16[1152,256]{1,0:T(8,128)(2,1)S(1)} %get-tuple-element.24.tab, bf16[8,336,128]{2,1,0:T(8,128)(2,1)S(1)} %bitcast.9), custom_call_target="tpu_custom_call" | custom-call | tf_op jit(solution)/shard_map/places/pallas_call | solution.py:83
  31.8 1.9 %new_momentums.1.after = f32[64,5120]{1,0:T(8,128)} custom-call(f32[64,5120]{1,0:T(8,128)S(1)} %bitcast.12, bf16[64,2560]{1,0:T(8,128)(2,1)S(1)} %get-tuple-element.23.p_ref, bf16[1152,256]{1,0:T(8,128)(2,1)S(1)} %get-tuple-element.24.tab, bf16[8,5120]{1,0:T(8,128)(2,1)S(1)} %kept_rows.1.ship.refs_0_, f32[64,1280]{1,0:T(8,128)S(1)} %get-tuple-element.26.refs_0_, ...), custom_call_target="tpu_custom_call" | custom-call | flops 125829120 | bytes 3276800 | tf_op jit(solution)/shard_map/new_momentums/pallas_call | solution.py:83
  33.7 0.0 collective-permute-done.8.refs_3_
  33.7 0.9 %collective-permute-done.7.refs_2_ = bf16[8,5120]{1,0:T(8,128)(2,1)S(1)} collective-permute-done((bf16[8,5120]{1,0:T(8,128)(2,1)S(1)}, bf16[8,5120]{1,0:T(8,128)(2,1)S(1)}, u32[]{:S(2)}, u32[]{:S(2)}) %collective-permute-start.7) | collective-permute-done | bytes 81952 | tf_op jit(solution)/shard_map/ppermute | solution.py:315
  34.6 0.5 %collective-permute-done.6.refs_1_ = bf16[8,5120]{1,0:T(8,128)(2,1)S(1)} collective-permute-done((bf16[8,5120]{1,0:T(8,128)(2,1)S(1)}, bf16[8,5120]{1,0:T(8,128)(2,1)S(1)}, u32[]{:S(2)}, u32[]{:S(2)}) %collective-permute-start.6) | collective-permute-done | bytes 81952 | tf_op jit(solution)/shard_map/ppermute | solution.py:315
  35.1 0.1 collective-permute-start.9
  35.2 1.1 %input_grads.1 = bf16[128,1280]{1,0:T(8,128)(2,1)} custom-call(bf16[8,336,128]{2,1,0:T(8,128)(2,1)S(1)} %bitcast.10, bf16[144,128]{1,0:T(8,128)(2,1)S(1)} %get-tuple-element.19.refs_1_.refs_0_, bf16[144,128]{1,0:T(8,128)(2,1)S(1)} %collective-permute-done.1.refs_1_.refs_0_, bf16[144,128]{1,0:T(8,128)(2,1)S(1)} %collective-permute-done.2.refs_2_.refs_0_, ...), custom_call_target="tpu_custom_call" | custom-call | flops 83886080 | bytes 983040 | tf_op jit(solution)/shard_map/input_grads/pallas_call | solution.py:83
  36.3 0.5 %collective-permute-done.9.other = bf16[4,8,5120]{2,1,0:T(8,128)(2,1)S(1)} collective-permute-done((bf16[4,8,5120]{2,1,0:T(8,128)(2,1)S(1)}, bf16[4,8,5120]{2,1,0:T(8,128)(2,1)S(1)}, u32[]{:S(2)}, u32[]{:S(2)}) %collective-permute-start.9) | collective-permute-done | bytes 327712 | tf_op jit(solution)/shard_map/ppermute | solution.py:315
  36.8 2.1 %updates.1 = f32[64,5120]{1,0:T(8,128)} custom-call(bf16[64,5120]{1,0:T(8,128)(2,1)S(1)} %get-tuple-element.27.after_too.p_hi, bf16[64,5120]{1,0:T(8,128)(2,1)S(1)} %get-tuple-element.28.p_lo, bf16[1152,256]{1,0:T(8,128)(2,1)S(1)} %get-tuple-element.24.tab, bf16[4,8,5120]{2,1,0:T(8,128)(2,1)S(1)} %join_kept.1.mine, ...), custom_call_target="tpu_custom_call" | custom-call | flops 671088640 | bytes 2621440 | tf_op jit(solution)/shard_map/updates/pallas_call | solution.py:83
  (2 shorter events, 0.0 us)
Async XLA Ops:
  1.8 9.2 %collective-permute-start.1 = (bf16[144,128]{1,0:T(8,128)(2,1)S(1)}, bf16[144,128]{1,0:T(8,128)(2,1)S(1)}, u32[]{:S(2)}, u32[]{:S(2)}) collective-permute-start(bf16[144,128]{1,0:T(8,128)(2,1)S(1)} %get-tuple-element.21), channel_id=1, source_target_pairs={{0,1},{1,2},{2,3},{3,0},{4,5},{5,6},{6,7},{7,4},{8,9},{9,10},{10,1... | collective-permute-start | bytes 110600 | tf_op jit(solution)/shard_map/ppermute | solution.py:310
  4.8 6.9 %collective-permute-start.2 = (bf16[144,128]{1,0:T(8,128)(2,1)S(1)}, bf16[144,128]{1,0:T(8,128)(2,1)S(1)}, u32[]{:S(2)}, u32[]{:S(2)}) collective-permute-start(bf16[144,128]{1,0:T(8,128)(2,1)S(1)} %get-tuple-element.22), channel_id=1, source_target_pairs={{0,2},{1,3},{2,0},{3,1},{4,6},{5,7},{6,4},{7,5},{8,10},{9,11},{10,... | collective-permute-start | bytes 110600 | tf_op jit(solution)/shard_map/ppermute | solution.py:310
  7.4 6.2 %collective-permute-start = (bf16[144,128]{1,0:T(8,128)(2,1)S(1)}, bf16[144,128]{1,0:T(8,128)(2,1)S(1)}, u32[]{:S(2)}, u32[]{:S(2)}) collective-permute-start(bf16[144,128]{1,0:T(8,128)(2,1)S(1)} %get-tuple-element.18), channel_id=1, source_target_pairs={{0,3},{1,0},{2,1},{3,2},{4,7},{5,4},{6,5},{7,6},{8,11},{9,8},{10,9... | collective-permute-start | bytes 110600 | tf_op jit(solution)/shard_map/ppermute | solution.py:310
  8.8 0.7 %copy-start.1 = (s32[1,1,80,8]{2,3,1,0:T(8,128)S(1)}, s32[1,1,80,8]{2,3,1,0:T(8,128)}, u32[]{:S(2)}) copy-start(s32[1,1,80,8]{2,3,1,0:T(8,128)} %param.14) | copy-start | bytes 7684
  11.2 15.8 %copy-start = (f32[1,64,5120]{2,1,0:T(8,128)S(1)}, f32[1,64,5120]{2,1,0:T(8,128)}, u32[]{:S(2)}) copy-start(f32[1,64,5120]{2,1,0:T(8,128)} %param.13) | copy-start | bytes 3932164
  11.2 13.3 %collective-permute-start.3 = (bf16[64,1280]{1,0:T(8,128)(2,1)S(1)}, bf16[64,1280]{1,0:T(8,128)(2,1)S(1)}, u32[]{:S(2)}, u32[]{:S(2)}) collective-permute-start(bf16[64,1280]{1,0:T(8,128)(2,1)S(1)} %weight_grads.4), channel_id=1, source_target_pairs={{0,3},{1,0},{2,1},{3,2},{4,7},{5,4},{6,5},{7,6},{8,11},{9,8},{10,9... | collective-permute-start | bytes 491528 | tf_op jit(solution)/shard_map/ppermute | solution.py:310
  11.9 15.1 %collective-permute-start.4 = (bf16[64,1280]{1,0:T(8,128)(2,1)S(1)}, bf16[64,1280]{1,0:T(8,128)(2,1)S(1)}, u32[]{:S(2)}, u32[]{:S(2)}) collective-permute-start(bf16[64,1280]{1,0:T(8,128)(2,1)S(1)} %weight_grads.5), channel_id=1, source_target_pairs={{0,2},{1,3},{2,0},{3,1},{4,6},{5,7},{6,4},{7,5},{8,10},{9,11},{10,... | collective-permute-start | bytes 491528 | tf_op jit(solution)/shard_map/ppermute | solution.py:310
  13.9 13.1 %collective-permute-start.5 = (bf16[64,1280]{1,0:T(8,128)(2,1)S(1)}, bf16[64,1280]{1,0:T(8,128)(2,1)S(1)}, u32[]{:S(2)}, u32[]{:S(2)}) collective-permute-start(bf16[64,1280]{1,0:T(8,128)(2,1)S(1)} %get-tuple-element.20.after), channel_id=1, source_target_pairs={{0,1},{1,2},{2,3},{3,0},{4,5},{5,6},{6,7},{7,4},{8,9},{9,10},{10,1... | collective-permute-start | bytes 491528 | tf_op jit(solution)/shard_map/ppermute | solution.py:310
  27.7 6.0 %collective-permute-start.8 = (bf16[8,5120]{1,0:T(8,128)(2,1)S(1)}, bf16[8,5120]{1,0:T(8,128)(2,1)S(1)}, u32[]{:S(2)}, u32[]{:S(2)}) collective-permute-start(bf16[8,5120]{1,0:T(8,128)(2,1)S(1)} %kept_rows.1.ship.refs_0_), channel_id=1, source_target_pairs={{0,24},{4,28},{8,16},{12,20},{16,8},{20,12},{24,0},{28,4},{1,25},{... | collective-permute-start | bytes 245768 | tf_op jit(solution)/shard_map/ppermute | solution.py:315
  30.2 4.4 %collective-permute-start.7 = (bf16[8,5120]{1,0:T(8,128)(2,1)S(1)}, bf16[8,5120]{1,0:T(8,128)(2,1)S(1)}, u32[]{:S(2)}, u32[]{:S(2)}) collective-permute-start(bf16[8,5120]{1,0:T(8,128)(2,1)S(1)} %kept_rows.1.ship.refs_0_), channel_id=1, source_target_pairs={{0,16},{4,20},{8,24},{12,28},{16,0},{20,4},{24,8},{28,12},{1,17},{... | collective-permute-start | bytes 245768 | tf_op jit(solution)/shard_map/ppermute | solution.py:315
  30.7 4.4 %collective-permute-start.6 = (bf16[8,5120]{1,0:T(8,128)(2,1)S(1)}, bf16[8,5120]{1,0:T(8,128)(2,1)S(1)}, u32[]{:S(2)}, u32[]{:S(2)}) collective-permute-start(bf16[8,5120]{1,0:T(8,128)(2,1)S(1)} %kept_rows.1.ship.refs_0_), channel_id=1, source_target_pairs={{0,8},{4,12},{8,0},{12,4},{16,24},{20,28},{24,16},{28,20},{1,9},{5... | collective-permute-start | bytes 245768 | tf_op jit(solution)/shard_map/ppermute | solution.py:315
  35.1 1.7 %collective-permute-start.9 = (bf16[4,8,5120]{2,1,0:T(8,128)(2,1)S(1)}, bf16[4,8,5120]{2,1,0:T(8,128)(2,1)S(1)}, u32[]{:S(2)}, u32[]{:S(2)}) collective-permute-start(bf16[4,8,5120]{2,1,0:T(8,128)(2,1)S(1)} %join_kept.1.mine), channel_id=1, source_target_pairs={{0,4},{4,0},{8,12},{12,8},{16,20},{20,16},{24,28},{28,24},{1,5},{5... | collective-permute-start | bytes 983048 | tf_op jit(solution)/shard_map/ppermute | solution.py:315

commit v6 on v5

--- a/solution.py
+++ b/solution.py
@@ -92,15 +92,22 @@
     )(*ins)
 
 
-def first_body(n_t, cp, cols, nr, switch, slope, exp_ref, act, *refs):
-    outs, act_out = refs[:n_t], refs[n_t]
-    switch_v, slope_v, exp_v, sems = refs[n_t + 1 :]
+def first_body(n_t, cp, cols, nr, switch, slope, exp_ref, act, lines, tab, *refs):
+    outs, (act_out, lines_out, tab_out) = refs[:n_t], refs[n_t : n_t + 3]
+    switch_v, slope_v, exp_v, sems = refs[n_t + 3 :]
     rep, ten = lax.axis_index("replica"), lax.axis_index("tensor")
     r0 = pl.multiple_of((rep // cp) * nr, nr)
     copies = [
         pltpu.make_async_copy(src, dst, sems.at[i])
         for i, (src, dst) in enumerate(
-            [(switch, switch_v), (slope, slope_v), (exp_ref.at[pl.ds(r0, nr), :], exp_v), (act, act_out)]
+            [
+                (switch, switch_v),
+                (slope, slope_v),
+                (exp_ref.at[pl.ds(r0, nr), :], exp_v),
+                (act, act_out),
+                (lines, lines_out),
+                (tab, tab_out),
+            ]
         )
     ]
     for copy in copies:
@@ -118,7 +125,8 @@
         for j in range(nc // 128):
             at = pl.multiple_of(c0 + j * 128, 128)
             outs[k][B + j * nr : B + (j + 1) * nr, :] = exp_v[:, pl.ds(at, 128)]
-    copies[3].wait()
+    for copy in copies[3:]:
+        copy.wait()
 
 
 def grads_body(n, act, after, *refs):
@@ -140,15 +148,15 @@
     out[n_t * n :, :] = jnp.concatenate([rows, jnp.zeros((16 - keep, 128), F32)], axis=0).astype(BF16)
 
 
-def join_body(after, after_too, *refs):
+def join_body(after, *refs):
     for i, ref in enumerate(refs[:-1]):
         refs[-1][i] = ref[...]
 
 
-def own_body(n_r, keep, mask, tally, lines, tab, p_ref, a_ref, tab_ref, w_ref, mask_s, tally_s, sems):
+def own_body(n_r, keep, mask, tally, lines, tab, p_ref, a_ref, w_ref, mask_s, tally_s, sems):
     copies = [
         pltpu.make_async_copy(src, dst, sems.at[i])
-        for i, (src, dst) in enumerate([(mask, mask_s), (tally, tally_s), (tab, tab_ref)])
+        for i, (src, dst) in enumerate([(mask, mask_s), (tally, tally_s)])
     ]
     for copy in copies:
         copy.start()
@@ -158,31 +166,34 @@
     freq = lax.broadcasted_iota(jnp.int32, (B, 2 * B), 0).astype(F32)
     block = (lax.broadcasted_iota(jnp.int32, (1, 2 * B), 1) // keep) % (G // B)
     term = lax.broadcasted_iota(jnp.int32, (B, 2 * B), 1) // (B // 2)
-    for copy in copies:
-        copy.wait()
     for g in range(blocks // (G // B)):
         num = rows[g * (G // B) : g * (G // B) + 1]
         for j in range(1, G // B):
             num = jnp.where(block == j, rows[g * (G // B) + j : g * (G // B) + j + 1], num)
         hot = jnp.where(freq == num, 1.0, 0.0).astype(BF16)
-        y = dot(tall(tab_ref), hot)
+        y = dot(tall(tab), hot)
         p = jnp.where(term == 3, 0.0, jnp.where(term == 1, y[B:], y[:B]))
         p_ref[:, g * 2 * B : (g + 1) * 2 * B] = p.astype(BF16)
         a_ref[g * B : (g + 1) * B, :] = jnp.concatenate([p, p], axis=0).T[:B].astype(BF16)
+    for copy in copies:
+        copy.wait()
     total, alive = jnp.float32(0), jnp.float32(0)
     for r in range(n_r):
         m = mask_s[r].astype(F32)
         total = total + m * tally_s[r].astype(F32)
         alive = alive + m
-    place = (lax.broadcasted_iota(jnp.int32, (8, 2 * B), 1) // keep) % n_r
-    w = jnp.zeros((8, 2 * B), F32)
-    for m in range(n_r):
-        r = lax.axis_index("replica") ^ m
-        w = jnp.where(place == m, mask_s[r].astype(F32) * tally_s[r].astype(F32), w)
-    w_ref[...] = w * (jnp.full((8, 2 * B), alive) / jnp.full((8, 2 * B), total))
-
-
-def kept_body(n_t, keep, vel, a_ref, tab, after, *refs):
+    half = n_r // 2
+    place = (lax.broadcasted_iota(jnp.int32, (8, 2 * B), 1) // keep) % half
+    scale = jnp.full((8, 2 * B), alive) / jnp.full((8, 2 * B), total)
+    for h in range(2):
+        w = jnp.zeros((8, 2 * B), F32)
+        for i in range(half):
+            r = lax.axis_index("replica") ^ (2 * i + h)
+            w = jnp.where(place == i, mask_s[r].astype(F32) * tally_s[r].astype(F32), w)
+        w_ref[h] = w * scale
+
+
+def kept_body(n_t, keep, vel, a_ref, tab, after, after_too, *refs):
     grads, ship_ref = refs[:n_t], refs[n_t]
     cols = grads[0].shape[1]
     ng = cols // G
@@ -212,71 +223,93 @@
 
 
 def return_body(n_t, keep, vel, p_ref, tab, ship, *refs):
-    grads, new_ref = refs[:n_t], refs[n_t]
+    grads, (new_ref, held, sems) = refs[:n_t], refs[n_t:]
     cols = grads[0].shape[1]
     ng = cols // G
     lane_block = lax.broadcasted_iota(jnp.int32, (keep, G), 1) // B
-    kept = ship[...].astype(F32)
-    total = kept.shape[1] // G
-    kept = jnp.concatenate([kept[:, g * G : (g + 1) * G] for g in range(total)], axis=0).astype(BF16)
-    q = dot(kept, inv(tab, 0)) + dot(kept, inv(tab, 1))
-    for g in range(total):
-        own = q[g * keep : (g + 1) * keep]
-        spread = jnp.concatenate(
-            [jnp.where(lane_block == j, own, 0.0) for j in range(G // B)], axis=0
-        )
-        hi, lo = split(spread)
-        w = jnp.concatenate([hi, hi, lo, jnp.zeros_like(lo)], axis=0)
-        back = dot(p_ref[:, g * 2 * B : (g + 1) * 2 * B], w)
-        cut = slice(g * G, (g + 1) * G)
-        new_ref[:, cut] = momentum_decay * vel[:, cut] - back
-    for k in range(n_t):
-        c0 = lax.rem(lax.axis_index("tensor") + k, n_t) * cols
+    q = []
+    for k in range(n_t):
+        c0 = pl.multiple_of(lax.rem(lax.axis_index("tensor") + k, n_t) * cols, G)
+        kept = ship[:, pl.ds(c0, cols)].astype(F32)
+        q += [kept[:, i * G : (i + 1) * G] for i in range(ng)]
+    q = jnp.concatenate(q, axis=0).astype(BF16)
+    q = dot(q, inv(tab, 0)) + dot(q, inv(tab, 1))
+    copies = []
+    for k in range(n_t):
+        c0 = pl.multiple_of(lax.rem(lax.axis_index("tensor") + k, n_t) * cols, G)
         for i in range(ng):
             at = pl.multiple_of(c0 + i * G, G)
-            new_ref[:, pl.ds(at, G)] += grads[k][:, i * G : (i + 1) * G].astype(F32)
-
-
-def places_body(keep, w_ref, tab, bundles, hi_ref, lo_ref):
-    w = w_ref[:1, :]
+            own = q[(k * ng + i) * keep : (k * ng + i + 1) * keep]
+            spread = jnp.concatenate(
+                [jnp.where(lane_block == j, own, 0.0) for j in range(G // B)], axis=0
+            )
+            hi, lo = split(spread)
+            w = jnp.concatenate([hi, hi, lo, jnp.zeros_like(lo)], axis=0)
+            back = dot(p_ref[:, pl.ds(pl.multiple_of(at // 2, 2 * B), 2 * B)], w)
+            moment = momentum_decay * vel[:, pl.ds(at, G)] + grads[k][:, i * G : (i + 1) * G].astype(F32)
+            held[:, pl.ds(at, G)] = moment - back
+        cut = pl.ds(c0, cols)
+        copies.append(pltpu.make_async_copy(held.at[:, cut], new_ref.at[:, cut], sems.at[k]))
+        copies[-1].start()
+    for copy in copies:
+        copy.wait()
+
+
+def places_body(keep, w_ref, tab, bundles, *p_refs):
     n_r, last = bundles.shape[0], bundles.shape[1] - 16
+    half, nb = n_r // 2, G // B
     rep = lax.axis_index("replica")
-    rows = [bundles[rep ^ m, last:, :].astype(F32)[:keep] for m in range(n_r)]
-    rows = jnp.concatenate(rows + rows, axis=0).T
     freq = lax.broadcasted_iota(jnp.int32, (B, 2 * B), 0).astype(F32)
-    first = lax.broadcasted_iota(jnp.int32, (1, 2 * B), 1) < B
-    for c in range(hi_ref.shape[1] // (2 * B)):
-        num = jnp.where(first, rows[2 * c : 2 * c + 1], rows[2 * c + 1 : 2 * c + 2])
-        hot = jnp.where(freq == num, 1.0, 0.0).astype(BF16)
-        y = dot(tall(tab), hot)
-        hi, lo = split((y[:B] + y[B:]) * w)
-        hi_ref[:, c * 2 * B : (c + 1) * 2 * B] = hi
-        lo_ref[:, c * 2 * B : (c + 1) * 2 * B] = lo
-
-
-def update_body(n_r, keep, p_hi, p_lo, tab, mine, other, out, hi_ref, lo_ref):
-    per = n_r * keep
-    nb = G // B
-    width = nb * per
-    half = n_r // 2
-    ng = out.shape[1] // G
-    lane_block = lax.broadcasted_iota(jnp.int32, (per, G), 1) // B
-    for g in range(ng):
-        cut = slice(g * G, (g + 1) * G)
-        s = jnp.concatenate(
-            [ref[i, :, cut].astype(F32) for i in range(half) for ref in (mine, other)], axis=0
-        )
-        w = jnp.concatenate(
-            [jnp.where(lane_block == j, s, 0.0).astype(BF16) for j in range(nb)], axis=0
-        )
-        wide = slice(g * width, (g + 1) * width)
-        y = dot(jnp.concatenate([p_hi[:, wide], p_lo[:, wide]], axis=0), w)
-        hi, lo = split(y[:B] + y[B:])
-        hi_ref[g * B : (g + 1) * B, :] = hi
-        lo_ref[g * B : (g + 1) * B, :] = lo
-    z = dot(hi_ref[...], inv(tab, 0)) + dot(lo_ref[...], inv(tab, 0)) + dot(hi_ref[...], inv(tab, 1))
-    for g in range(ng):
-        out[:, g * G : (g + 1) * G] = z[g * B : (g + 1) * B]
+    block = lax.broadcasted_iota(jnp.int32, (1, 2 * B), 1) // (half * keep)
+    for h in range(2):
+        hi_ref, lo_ref = p_refs[2 * h : 2 * h + 2]
+        w = w_ref[h, :1, :]
+        rows = [bundles[rep ^ (2 * i + h), last:, :].astype(F32)[:keep] for i in range(half)]
+        rows = jnp.concatenate(rows * nb, axis=0).T
+        for g in range(hi_ref.shape[1] // (2 * B)):
+            num = rows[g * nb : g * nb + 1]
+            for j in range(1, nb):
+                num = jnp.where(block == j, rows[g * nb + j : g * nb + j + 1], num)
+            hot = jnp.where(freq == num, 1.0, 0.0).astype(BF16)
+            y = dot(tall(tab), hot)
+            hi, lo = split((y[:B] + y[B:]) * w)
+            hi_ref[:, g * 2 * B : (g + 1) * 2 * B] = hi
+            lo_ref[:, g * 2 * B : (g + 1) * 2 * B] = lo
+
+
+def spread_rows(p_hi, p_lo, ships, g):
+    half, keep = ships.shape[0], ships.shape[1]
+    lane_block = lax.broadcasted_iota(jnp.int32, (half * keep, G), 1) // B
+    s = jnp.concatenate([ships[i, :, g * G : (g + 1) * G].astype(F32) for i in range(half)], axis=0)
+    w = jnp.concatenate(
+        [jnp.where(lane_block == j, s, 0.0).astype(BF16) for j in range(G // B)], axis=0
+    )
+    cut = slice(g * 2 * B, (g + 1) * 2 * B)
+    y = dot(jnp.concatenate([p_hi[:, cut], p_lo[:, cut]], axis=0), w)
+    return y[:B] + y[B:]
+
+
+def half_update_body(p_hi, p_lo, mine, out):
+    for g in range(out.shape[0] // B):
+        out[g * B : (g + 1) * B, :] = spread_rows(p_hi, p_lo, mine, g)
+
+
+def update_body(chunk, half_sum, p_hi, p_lo, tab, other, out, hi_ref, lo_ref, held, sems):
+    ng = half_sum.shape[0] // B
+    copies = []
+    for c in range(0, ng, chunk):
+        for g in range(c, c + chunk):
+            at = slice(g * B, (g + 1) * B)
+            hi_ref[at, :], lo_ref[at, :] = split(half_sum[at, :] + spread_rows(p_hi, p_lo, other, g))
+        rows = slice(c * B, (c + chunk) * B)
+        z = dot(hi_ref[rows, :], inv(tab, 0)) + dot(lo_ref[rows, :], inv(tab, 0)) + dot(hi_ref[rows, :], inv(tab, 1))
+        for g in range(chunk):
+            held[:, (c + g) * G : (c + g + 1) * G] = z[g * B : (g + 1) * B]
+        cut = pl.ds(c * G, chunk * G)
+        copies.append(pltpu.make_async_copy(held.at[:, cut], out.at[:, cut], sems.at[c // chunk]))
+        copies[-1].start()
+    for copy in copies:
+        copy.wait()
 
 
 def input_grad_body(n_t, n_r, cp, bundles, *refs):
@@ -317,35 +350,35 @@
     own = lines[0, 0].T
     tiles = cols // cp // 128
     nr = B // rp
-    *parts, act = call(
+    *parts, act, own, tab = call(
         functools.partial(first_body, n_t, cp, cols, nr),
-        [near((B + tiles * nr, 128))] * n_t + [near(act.shape)],
-        (far(switch.T), far(slope.T), far(exp), far(act)),
-        [ANY] * 4,
-        [VM] * (n_t + 1),
+        [near((B + tiles * nr, 128))] * n_t
+        + [near(act.shape), near(own.shape, jnp.int32), near(tab.shape)],
+        (far(switch.T), far(slope.T), far(exp), far(act), far(own), far(tab)),
+        [ANY] * 6,
+        [VM] * (n_t + 3),
         scratch=[
             pltpu.VMEM((B, tok), BF16),
             pltpu.VMEM((B, tok), BF16),
             pltpu.VMEM((nr, width), BF16),
-            pltpu.SemaphoreType.DMA((4,)),
+            pltpu.SemaphoreType.DMA((6,)),
         ],
         nbytes=act.size * 4 + nr * width * 2,
         name="up_grads",
     )
     parts = [parts[0]] + [shift(parts[k], k) for k in range(1, n_t)]
 
-    p_own, a_own, tab, shares = call(
+    p_own, a_own, shares = call(
         functools.partial(own_body, n_r, keep),
         [
             near((B, groups * 2 * B)),
             near((groups * B, 2 * B)),
-            near(tab.shape),
-            near((8, 2 * B), F32),
+            near((2, 8, 2 * B), F32),
         ],
-        (far(mask), far(tally), own, far(tab)),
-        [ANY, ANY, VM, ANY],
-        [VM] * 4,
-        scratch=[pltpu.SMEM((n_r,), jnp.int32)] * 2 + [pltpu.SemaphoreType.DMA((3,))],
+        (far(mask), far(tally), own, tab),
+        [ANY, ANY, VM, VM],
+        [VM] * 3,
+        scratch=[pltpu.SMEM((n_r,), jnp.int32)] * 2 + [pltpu.SemaphoreType.DMA((2,))],
         name="own_places",
     )
 
@@ -376,12 +409,12 @@
     )
     bundles = lax.all_gather(bundle, "replica", axis=0)
 
-    p_hi, p_lo = call(
+    places = call(
         functools.partial(places_body, keep),
-        [near((B, blocks * n_r * keep))] * 2,
+        [near((B, blocks * half * keep))] * 4,
         (shares, tab, bundles),
         [VM] * 3,
-        [VM, VM],
+        [VM] * 4,
         name="places",
     )
     input_grad = call(
@@ -399,8 +432,8 @@
     ship = call(
         functools.partial(kept_body, n_t, keep),
         near((keep, width)),
-        (vel[0], a_own, tab, bundles, *grads),
-        [VM] * 3 + [ANY] + [VM] * n_t,
+        (vel[0], a_own, tab, places[0], far(input_grad), *grads),
+        [VM] * 3 + [ANY, ANY] + [VM] * n_t,
         VM,
         flops=6 * B * B * width,
         nbytes=B * width * 6,
@@ -412,7 +445,8 @@
         jax.ShapeDtypeStruct((B, width), F32),
         (vel[0], p_own, tab, ship, *grads),
         [VM] * (4 + n_t),
-        VM,
+        ANY,
+        scratch=[pltpu.VMEM((B, width), F32), pltpu.SemaphoreType.DMA((n_t,))],
         flops=6 * B * B * width,
         nbytes=B * width * 10,
         name="new_momentums",
@@ -420,19 +454,33 @@
     mine = call(
         join_body,
         near((half, keep, width)),
-        (far(new), p_hi, *ships),
-        [ANY, ANY] + [VM] * half,
+        (far(new), *ships),
+        [ANY] + [VM] * half,
         VM,
         name="join_kept",
     )
     other = swap(mine, 1)
+    half_sum = call(
+        half_update_body,
+        near((groups * B, G), F32),
+        (*places[:2], mine),
+        [VM] * 3,
+        VM,
+        name="half_updates",
+    )
+    chunk = next(c for c in (5, 4, 3, 2, 1) if groups % c == 0)
     update = call(
-        functools.partial(update_body, n_r, keep),
+        functools.partial(update_body, chunk),
         jax.ShapeDtypeStruct((B, width), F32),
-        (p_hi, p_lo, tab, mine, other),
+        (half_sum, *places[2:], tab, other),
         [VM] * 5,
-        VM,
-        scratch=[pltpu.VMEM((groups * B, G), BF16)] * 2,
+        ANY,
+        scratch=[
+            pltpu.VMEM((groups * B, G), BF16),
+            pltpu.VMEM((groups * B, G), BF16),
+            pltpu.VMEM((B, width), F32),
+            pltpu.SemaphoreType.DMA((groups // chunk,)),
+        ],
         flops=8 * B * G * width,
         nbytes=B * width * 8,
         name="updates",

time: 39.2 us -> 37.9 us (0.967)
  starting transfers between devices: 13 us -> 13.8 us
  waiting for transfers between devices: 4.54 us -> 3.8 us
  local copies, waits for them, and re-layouts: 0.69 us -> 0.01 us
  Pallas kernels: 9.55 us -> 9.05 us
    ppermute x6, waiting for transfers between devices: 2.54 us -> 0.29 us  [shift(): return lax.ppermute(x, 'tensor', [(i, (i + k) % n_t) for i in range(n_t)])]
    ppermute x4, waiting for transfers between devices: 1.99 us -> 3.51 us  [swap(): return lax.ppermute(x, 'replica', [(i, i ^ m) for i in range(n_r)])]
    ppermute x6, starting transfers between devices: 9.4 us -> 10.1 us  [shift(): return lax.ppermute(x, 'tensor', [(i, (i + k) % n_t) for i in range(n_t)])]
    unnamed x4 -> x2, local copies, waits for them, and re-layouts: 0.69 us -> 0.01 us
    pallas_call x12 -> x13, Pallas kernels: 9.55 us -> 9.05 us  [call(): pl.pallas_call(body, out_shape=out_shape, in_specs=in_specs, out_specs=ou...]
  transfers between devices with their start and end apart: 10 -> 10, of which waited for: 4 -> 5; matrix products, arithmetic and copies ran while one was open for 0% -> 0% of each run, Pallas kernels for 14% -> 13%
where the time goes in v6:
time: 37.9 us; the launch traced here: 37.6 us
  starting transfers between devices  13.8 us (36%)
  blocking collectives  10.3 us (27%)
  Pallas kernels  9.05 us (24%)
  waiting for transfers between devices  3.8 us (10%)
  between operations  0.71 us (2%)
    all_gather x1, blocking collectives, per_device(): bundles = lax.all_gather(bundle, 'replica', axis=0)  10.3 us
    ppermute x6, starting transfers between devices, shift(): return lax.ppermute(x, 'tensor', [(i, (i + k) % n_t) for i in range(n_t)])  10.1 us
    pallas_call x13, Pallas kernels, call(): pl.pallas_call(body, out_shape=out_shape, in_specs=in_specs, out_specs=ou...  9.05 us
    ppermute x4, starting transfers between devices, swap(): return lax.ppermute(x, 'replica', [(i, i ^ m) for i in range(n_r)])  3.62 us
    ppermute x4, waiting for transfers between devices, swap(): return lax.ppermute(x, 'replica', [(i, i ^ m) for i in range(n_r)])  3.51 us
  transfers between devices with their start and end apart: 10, of which 5 were waited for; matrix products, arithmetic and copies ran while one was open for 0% of the time, Pallas kernels for 13%

profile of v6, /device:TPU:0, one launch (start us, length us, event | category | flops | bytes accessed | tf_op | source)
XLA Modules:
  0.0 37.6 jit_solution(1239881353315331144)
XLA Ops:
  0.6 1.4 %up_grads.1 = (bf16[144,128]{1,0:T(8,128)(2,1)S(1)}, bf16[144,128]{1,0:T(8,128)(2,1)S(1)}, bf16[144,128]{1,0:T(8,128)(2,1)S(1)}, bf16[144,128]{1,0:T(8,128)(2,1)...) custom-call(bf16[64,128]{1,0:T(8,128)(2,1)} %bitcast.13, ...), custom_call_target="tpu_custom_call" | custom-call | bytes 819200 | tf_op jit(solution)/shard_map/up_grads/pallas_call | solution.py:83
  2.0 3.1 %collective-permute-start.1 = (bf16[144,128]{1,0:T(8,128)(2,1)S(1)}, bf16[144,128]{1,0:T(8,128)(2,1)S(1)}, u32[]{:S(2)}, u32[]{:S(2)}) collective-permute-start(bf16[144,128]{1,0:T(8,128)(2,1)S(1)} %get-tuple-element.26), channel_id=1, source_target_pairs={{0,1},{1,2},{2,3},{3,0},{4,5},{5,6},{6,7},{7,4},{8,9},{9,10},{10,1... | collective-permute-start | bytes 110600 | tf_op jit(solution)/shard_map/ppermute | solution.py:343
  5.1 2.6 %collective-permute-start.2 = (bf16[144,128]{1,0:T(8,128)(2,1)S(1)}, bf16[144,128]{1,0:T(8,128)(2,1)S(1)}, u32[]{:S(2)}, u32[]{:S(2)}) collective-permute-start(bf16[144,128]{1,0:T(8,128)(2,1)S(1)} %get-tuple-element.27), channel_id=1, source_target_pairs={{0,2},{1,3},{2,0},{3,1},{4,6},{5,7},{6,4},{7,5},{8,10},{9,11},{10,... | collective-permute-start | bytes 110600 | tf_op jit(solution)/shard_map/ppermute | solution.py:343
  7.7 1.3 %collective-permute-start = (bf16[144,128]{1,0:T(8,128)(2,1)S(1)}, bf16[144,128]{1,0:T(8,128)(2,1)S(1)}, u32[]{:S(2)}, u32[]{:S(2)}) collective-permute-start(bf16[144,128]{1,0:T(8,128)(2,1)S(1)} %get-tuple-element.23), channel_id=1, source_target_pairs={{0,3},{1,0},{2,1},{3,2},{4,7},{5,4},{6,5},{7,6},{8,11},{9,8},{10,9... | collective-permute-start | bytes 110600 | tf_op jit(solution)/shard_map/ppermute | solution.py:343
  9.0 0.7 %own_places.1 = (bf16[64,2560]{1,0:T(8,128)(2,1)S(1)}, bf16[1280,128]{1,0:T(8,128)(2,1)S(1)}, f32[2,8,128]{2,1,0:T(8,128)S(1)}) custom-call(s32[8]{0:T(128)} %mask.1, s32[8]{0:T(128)} %tally.1, s32[8,80]{1,0:T(8,128)S(1)} %get-tuple-element.20.lines, bf16[1152,256]{1,0:T(8,128)(2,1)S(1)} %get-tuple-element.21.tab), custom_call_target="tpu_custom_call" | custom-call | tf_op jit(solution)/shard_map/own_places/pallas_call | solution.py:83
  9.7 0.0 collective-permute-done.1.refs_1_.refs_0_
  9.8 0.2 weight_grads.4
  9.9 1.6 %collective-permute-start.3 = (bf16[64,1280]{1,0:T(8,128)(2,1)S(1)}, bf16[64,1280]{1,0:T(8,128)(2,1)S(1)}, u32[]{:S(2)}, u32[]{:S(2)}) collective-permute-start(bf16[64,1280]{1,0:T(8,128)(2,1)S(1)} %weight_grads.4), channel_id=1, source_target_pairs={{0,3},{1,0},{2,1},{3,2},{4,7},{5,4},{6,5},{7,6},{8,11},{9,8},{10,9... | collective-permute-start | bytes 491528 | tf_op jit(solution)/shard_map/ppermute | solution.py:343
  11.6 0.0 collective-permute-done.2.refs_2_.refs_0_
  11.6 0.2 weight_grads.5
  11.8 1.0 %collective-permute-start.4 = (bf16[64,1280]{1,0:T(8,128)(2,1)S(1)}, bf16[64,1280]{1,0:T(8,128)(2,1)S(1)}, u32[]{:S(2)}, u32[]{:S(2)}) collective-permute-start(bf16[64,1280]{1,0:T(8,128)(2,1)S(1)} %weight_grads.5), channel_id=1, source_target_pairs={{0,2},{1,3},{2,0},{3,1},{4,6},{5,7},{6,4},{7,5},{8,10},{9,11},{10,... | collective-permute-start | bytes 491528 | tf_op jit(solution)/shard_map/ppermute | solution.py:343
  12.8 0.0 collective-permute-done.refs_0_.refs_3_
  12.8 0.2 weight_grads.3
  13.1 0.4 %collective-permute-start.5 = (bf16[64,1280]{1,0:T(8,128)(2,1)S(1)}, bf16[64,1280]{1,0:T(8,128)(2,1)S(1)}, u32[]{:S(2)}, u32[]{:S(2)}) collective-permute-start(bf16[64,1280]{1,0:T(8,128)(2,1)S(1)} %get-tuple-element.25.after), channel_id=1, source_target_pairs={{0,1},{1,2},{2,3},{3,0},{4,5},{5,6},{6,7},{7,4},{8,9},{9,10},{10,1... | collective-permute-start | bytes 491528 | tf_op jit(solution)/shard_map/ppermute | solution.py:343
  13.5 10.3 %all-gather = bf16[2688,128]{1,0:T(8,128)(2,1)S(1)} all-gather(bf16[336,128]{1,0:T(8,128)(2,1)S(1)} %bundle.1), channel_id=2, replica_groups=mesh['replica'=8,'tensor'=4] {'replica'}, dimensions={0}, use_global_device_ids=true | all-gather | bytes 774144 | tf_op jit(solution)/shard_map/all_gather | solution.py:410
  23.8 0.0 copy-start
  23.8 0.6 %places.1 = (bf16[64,2560]{1,0:T(8,128)(2,1)S(1)}, bf16[64,2560]{1,0:T(8,128)(2,1)S(1)}, bf16[64,2560]{1,0:T(8,128)(2,1)S(1)}, bf16[64,2560]{1,0:T(8,128)(2,1)S(1)}) custom-call(f32[2,8,128]{2,1,0:T(8,128)S(1)} %get-tuple-element.22.after.w_ref, bf16[1152,256]{1,0:T(8,128)(2,1)S(1)} %get-tuple-element.21.tab, bf16[8,336,128]{2,1,0:T(8,128)(2,1)S(1)} %bitcast.8), custom_call_target="tpu_custom_call" | custom-call | tf_op jit(solution)/shard_map/places/pallas_call | solution.py:83
  24.4 1.1 %input_grads.1.after_too = bf16[128,1280]{1,0:T(8,128)(2,1)} custom-call(bf16[8,336,128]{2,1,0:T(8,128)(2,1)S(1)} %bitcast.9, bf16[144,128]{1,0:T(8,128)(2,1)S(1)} %get-tuple-element.24.refs_1_.refs_0_, bf16[144,128]{1,0:T(8,128)(2,1)S(1)} %collective-permute-done.1.refs_1_.refs_0_, bf16[144,128]{1,0:T(8,128)(2,1)S(1)} %collective-permute-done.2.refs_2_.refs_0_, ...), custom_call_target="tpu_custom_call" | custom-call | flops 83886080 | bytes 983040 | tf_op jit(solution)/shard_map/input_grads/pallas_call | solution.py:83
  25.5 0.0 collective-permute-done.3.refs_1_
  25.5 0.3 collective-permute-done.4.refs_2_
  25.7 0.0 collective-permute-done.5.refs_3_
  25.7 0.0 copy-done
  25.8 0.7 %kept_rows.1.ship.refs_0_ = bf16[8,5120]{1,0:T(8,128)(2,1)S(1)} custom-call(f32[64,5120]{1,0:T(8,128)S(1)} %bitcast.10, bf16[1280,128]{1,0:T(8,128)(2,1)S(1)} %get-tuple-element.29.a_ref, bf16[1152,256]{1,0:T(8,128)(2,1)S(1)} %get-tuple-element.21.tab, bf16[64,2560]{1,0:T(8,128)(2,1)S(1)} %get-tuple-element.30.after.p_hi, ...), custom_call_target="tpu_custom_call" | custom-call | flops 125829120 | bytes 1966080 | tf_op jit(solution)/shard_map/kept_rows/pallas_call | solution.py:83
  26.4 2.5 %collective-permute-start.8 = (bf16[8,5120]{1,0:T(8,128)(2,1)S(1)}, bf16[8,5120]{1,0:T(8,128)(2,1)S(1)}, u32[]{:S(2)}, u32[]{:S(2)}) collective-permute-start(bf16[8,5120]{1,0:T(8,128)(2,1)S(1)} %kept_rows.1.ship.refs_0_), channel_id=1, source_target_pairs={{0,24},{4,28},{8,16},{12,20},{16,8},{20,12},{24,0},{28,4},{1,25},{... | collective-permute-start | bytes 245768 | tf_op jit(solution)/shard_map/ppermute | solution.py:348
  28.9 0.5 %collective-permute-start.7 = (bf16[8,5120]{1,0:T(8,128)(2,1)S(1)}, bf16[8,5120]{1,0:T(8,128)(2,1)S(1)}, u32[]{:S(2)}, u32[]{:S(2)}) collective-permute-start(bf16[8,5120]{1,0:T(8,128)(2,1)S(1)} %kept_rows.1.ship.refs_0_), channel_id=1, source_target_pairs={{0,16},{4,20},{8,24},{12,28},{16,0},{20,4},{24,8},{28,12},{1,17},{... | collective-permute-start | bytes 245768 | tf_op jit(solution)/shard_map/ppermute | solution.py:348
  29.5 0.5 %collective-permute-start.6 = (bf16[8,5120]{1,0:T(8,128)(2,1)S(1)}, bf16[8,5120]{1,0:T(8,128)(2,1)S(1)}, u32[]{:S(2)}, u32[]{:S(2)}) collective-permute-start(bf16[8,5120]{1,0:T(8,128)(2,1)S(1)} %kept_rows.1.ship.refs_0_), channel_id=1, source_target_pairs={{0,8},{4,12},{8,0},{12,4},{16,24},{20,28},{24,16},{28,20},{1,9},{5... | collective-permute-start | bytes 245768 | tf_op jit(solution)/shard_map/ppermute | solution.py:348
  30.0 1.5 %new_momentums.1.after = f32[64,5120]{1,0:T(8,128)} custom-call(f32[64,5120]{1,0:T(8,128)S(1)} %bitcast.11, bf16[64,2560]{1,0:T(8,128)(2,1)S(1)} %get-tuple-element.28.p_ref, bf16[1152,256]{1,0:T(8,128)(2,1)S(1)} %get-tuple-element.21.tab, bf16[8,5120]{1,0:T(8,128)(2,1)S(1)} %kept_rows.1.ship.refs_0_, f32[64,1280]{1,0:T(8,128)S(1)} %get-tuple-element.31.refs_0_, ...), custom_call_target="tpu_custom_call" | custom-call | flops 125829120 | bytes 3276800 | tf_op jit(solution)/shard_map/new_momentums/pallas_call | solution.py:83
  31.5 0.7 %collective-permute-done.8.refs_3_ = bf16[8,5120]{1,0:T(8,128)(2,1)S(1)} collective-permute-done((bf16[8,5120]{1,0:T(8,128)(2,1)S(1)}, bf16[8,5120]{1,0:T(8,128)(2,1)S(1)}, u32[]{:S(2)}, u32[]{:S(2)}) %collective-permute-start.8) | collective-permute-done | bytes 81952 | tf_op jit(solution)/shard_map/ppermute | solution.py:348
  32.2 1.4 %collective-permute-done.7.refs_2_ = bf16[8,5120]{1,0:T(8,128)(2,1)S(1)} collective-permute-done((bf16[8,5120]{1,0:T(8,128)(2,1)S(1)}, bf16[8,5120]{1,0:T(8,128)(2,1)S(1)}, u32[]{:S(2)}, u32[]{:S(2)}) %collective-permute-start.7) | collective-permute-done | bytes 81952 | tf_op jit(solution)/shard_map/ppermute | solution.py:348
  33.6 0.3 collective-permute-done.6.refs_1_
  33.9 0.1 collective-permute-start.9
  34.0 0.5 %half_updates.1.half_sum = f32[1280,256]{1,0:T(8,128)S(1)} custom-call(bf16[64,2560]{1,0:T(8,128)(2,1)S(1)} %get-tuple-element.30.after.p_hi, bf16[64,2560]{1,0:T(8,128)(2,1)S(1)} %get-tuple-element.32.p_lo, bf16[4,8,5120]{2,1,0:T(8,128)(2,1)S(1)} %join_kept.1.mine), custom_call_target="tpu_custom_call" | custom-call | tf_op jit(solution)/shard_map/half_updates/pallas_call | solution.py:83
  34.5 1.1 %collective-permute-done.9.other = bf16[4,8,5120]{2,1,0:T(8,128)(2,1)S(1)} collective-permute-done((bf16[4,8,5120]{2,1,0:T(8,128)(2,1)S(1)}, bf16[4,8,5120]{2,1,0:T(8,128)(2,1)S(1)}, u32[]{:S(2)}, u32[]{:S(2)}) %collective-permute-start.9) | collective-permute-done | bytes 327712 | tf_op jit(solution)/shard_map/ppermute | solution.py:348
  35.6 2.0 %updates.1 = f32[64,5120]{1,0:T(8,128)} custom-call(f32[1280,256]{1,0:T(8,128)S(1)} %half_updates.1.half_sum, bf16[64,2560]{1,0:T(8,128)(2,1)S(1)} %get-tuple-element.33.p_hi, bf16[64,2560]{1,0:T(8,128)(2,1)S(1)} %get-tuple-element.34.p_lo, bf16[1152,256]{1,0:T(8,128)(2,1)S(1)} %get-tuple-element.21.tab, bf16[4,8,5120]{2,1,0:T(8,128)(2,1)S(1)} %collective-permute-done.9.other), custom_call_target="tpu_custom_call" | custom-call | flops 671088640 | bytes 2621440 | tf_op jit(solution)/shard_map/updates/pallas_call | solution.py:83
  (2 shorter events, 0.0 us)
Async XLA Ops:
  2.0 7.8 %collective-permute-start.1 = (bf16[144,128]{1,0:T(8,128)(2,1)S(1)}, bf16[144,128]{1,0:T(8,128)(2,1)S(1)}, u32[]{:S(2)}, u32[]{:S(2)}) collective-permute-start(bf16[144,128]{1,0:T(8,128)(2,1)S(1)} %get-tuple-element.26), channel_id=1, source_target_pairs={{0,1},{1,2},{2,3},{3,0},{4,5},{5,6},{6,7},{7,4},{8,9},{9,10},{10,1... | collective-permute-start | bytes 110600 | tf_op jit(solution)/shard_map/ppermute | solution.py:343
  5.1 6.5 %collective-permute-start.2 = (bf16[144,128]{1,0:T(8,128)(2,1)S(1)}, bf16[144,128]{1,0:T(8,128)(2,1)S(1)}, u32[]{:S(2)}, u32[]{:S(2)}) collective-permute-start(bf16[144,128]{1,0:T(8,128)(2,1)S(1)} %get-tuple-element.27), channel_id=1, source_target_pairs={{0,2},{1,3},{2,0},{3,1},{4,6},{5,7},{6,4},{7,5},{8,10},{9,11},{10,... | collective-permute-start | bytes 110600 | tf_op jit(solution)/shard_map/ppermute | solution.py:343
  7.7 5.2 %collective-permute-start = (bf16[144,128]{1,0:T(8,128)(2,1)S(1)}, bf16[144,128]{1,0:T(8,128)(2,1)S(1)}, u32[]{:S(2)}, u32[]{:S(2)}) collective-permute-start(bf16[144,128]{1,0:T(8,128)(2,1)S(1)} %get-tuple-element.23), channel_id=1, source_target_pairs={{0,3},{1,0},{2,1},{3,2},{4,7},{5,4},{6,5},{7,6},{8,11},{9,8},{10,9... | collective-permute-start | bytes 110600 | tf_op jit(solution)/shard_map/ppermute | solution.py:343
  9.9 15.5 %collective-permute-start.3 = (bf16[64,1280]{1,0:T(8,128)(2,1)S(1)}, bf16[64,1280]{1,0:T(8,128)(2,1)S(1)}, u32[]{:S(2)}, u32[]{:S(2)}) collective-permute-start(bf16[64,1280]{1,0:T(8,128)(2,1)S(1)} %weight_grads.4), channel_id=1, source_target_pairs={{0,3},{1,0},{2,1},{3,2},{4,7},{5,4},{6,5},{7,6},{8,11},{9,8},{10,9... | collective-permute-start | bytes 491528 | tf_op jit(solution)/shard_map/ppermute | solution.py:343
  11.8 14.0 %collective-permute-start.4 = (bf16[64,1280]{1,0:T(8,128)(2,1)S(1)}, bf16[64,1280]{1,0:T(8,128)(2,1)S(1)}, u32[]{:S(2)}, u32[]{:S(2)}) collective-permute-start(bf16[64,1280]{1,0:T(8,128)(2,1)S(1)} %weight_grads.5), channel_id=1, source_target_pairs={{0,2},{1,3},{2,0},{3,1},{4,6},{5,7},{6,4},{7,5},{8,10},{9,11},{10,... | collective-permute-start | bytes 491528 | tf_op jit(solution)/shard_map/ppermute | solution.py:343
  13.1 12.7 %collective-permute-start.5 = (bf16[64,1280]{1,0:T(8,128)(2,1)S(1)}, bf16[64,1280]{1,0:T(8,128)(2,1)S(1)}, u32[]{:S(2)}, u32[]{:S(2)}) collective-permute-start(bf16[64,1280]{1,0:T(8,128)(2,1)S(1)} %get-tuple-element.25.after), channel_id=1, source_target_pairs={{0,1},{1,2},{2,3},{3,0},{4,5},{5,6},{6,7},{7,4},{8,9},{9,10},{10,1... | collective-permute-start | bytes 491528 | tf_op jit(solution)/shard_map/ppermute | solution.py:343
  23.8 2.0 %copy-start = (f32[1,64,5120]{2,1,0:T(8,128)S(1)}, f32[1,64,5120]{2,1,0:T(8,128)}, u32[]{:S(2)}) copy-start(f32[1,64,5120]{2,1,0:T(8,128)} %param.13) | copy-start | bytes 3932164
  26.4 5.8 %collective-permute-start.8 = (bf16[8,5120]{1,0:T(8,128)(2,1)S(1)}, bf16[8,5120]{1,0:T(8,128)(2,1)S(1)}, u32[]{:S(2)}, u32[]{:S(2)}) collective-permute-start(bf16[8,5120]{1,0:T(8,128)(2,1)S(1)} %kept_rows.1.ship.refs_0_), channel_id=1, source_target_pairs={{0,24},{4,28},{8,16},{12,20},{16,8},{20,12},{24,0},{28,4},{1,25},{... | collective-permute-start | bytes 245768 | tf_op jit(solution)/shard_map/ppermute | solution.py:348
  28.9 4.7 %collective-permute-start.7 = (bf16[8,5120]{1,0:T(8,128)(2,1)S(1)}, bf16[8,5120]{1,0:T(8,128)(2,1)S(1)}, u32[]{:S(2)}, u32[]{:S(2)}) collective-permute-start(bf16[8,5120]{1,0:T(8,128)(2,1)S(1)} %kept_rows.1.ship.refs_0_), channel_id=1, source_target_pairs={{0,16},{4,20},{8,24},{12,28},{16,0},{20,4},{24,8},{28,12},{1,17},{... | collective-permute-start | bytes 245768 | tf_op jit(solution)/shard_map/ppermute | solution.py:348
  29.5 4.4 %collective-permute-start.6 = (bf16[8,5120]{1,0:T(8,128)(2,1)S(1)}, bf16[8,5120]{1,0:T(8,128)(2,1)S(1)}, u32[]{:S(2)}, u32[]{:S(2)}) collective-permute-start(bf16[8,5120]{1,0:T(8,128)(2,1)S(1)} %kept_rows.1.ship.refs_0_), channel_id=1, source_target_pairs={{0,8},{4,12},{8,0},{12,4},{16,24},{20,28},{24,16},{28,20},{1,9},{5... | collective-permute-start | bytes 245768 | tf_op jit(solution)/shard_map/ppermute | solution.py:348
  33.9 1.7 %collective-permute-start.9 = (bf16[4,8,5120]{2,1,0:T(8,128)(2,1)S(1)}, bf16[4,8,5120]{2,1,0:T(8,128)(2,1)S(1)}, u32[]{:S(2)}, u32[]{:S(2)}) collective-permute-start(bf16[4,8,5120]{2,1,0:T(8,128)(2,1)S(1)} %join_kept.1.mine), channel_id=1, source_target_pairs={{0,4},{4,0},{8,12},{12,8},{16,20},{20,16},{24,28},{28,24},{1,5},{5... | collective-permute-start | bytes 983048 | tf_op jit(solution)/shard_map/ppermute | solution.py:348

commit v7 on v6

--- a/solution.py
+++ b/solution.py
@@ -45,9 +45,9 @@
     hi, lo = halves(cosine_np())
     eye = np.eye(G // B)
     kron = lambda x: np.kron(eye, np.asarray(x, np.float32)).astype(jnp.bfloat16)
-    tall = np.zeros((2 * B, G), jnp.bfloat16)
+    tall = np.zeros((2 * B, 2 * B), jnp.bfloat16)
     tall[:B, :B], tall[B:, :B] = hi.T, lo.T
-    return jnp.asarray(np.concatenate([kron(hi.T), kron(lo.T), kron(hi), kron(lo), tall], axis=0))
+    return jnp.asarray(np.concatenate([kron(x) for x in (hi.T, lo.T, hi, lo)], axis=0)), jnp.asarray(tall)
 
 
 def fwd(tab, i):
@@ -56,10 +56,6 @@
 
 def inv(tab, i):
     return tab[(2 + i) * G : (3 + i) * G, :]
-
-
-def tall(tab):
-    return tab[4 * G : 4 * G + 2 * B, :B]
 
 
 def dot(a, b):
@@ -92,8 +88,8 @@
     )(*ins)
 
 
-def first_body(n_t, cp, cols, nr, switch, slope, exp_ref, act, lines, tab, *refs):
-    outs, (act_out, lines_out, tab_out) = refs[:n_t], refs[n_t : n_t + 3]
+def first_body(n_t, cp, cols, nr, switch, slope, exp_ref, act, lines, tall, *refs):
+    outs, (act_out, lines_out, tall_out) = refs[:n_t], refs[n_t : n_t + 3]
     switch_v, slope_v, exp_v, sems = refs[n_t + 3 :]
     rep, ten = lax.axis_index("replica"), lax.axis_index("tensor")
     r0 = pl.multiple_of((rep // cp) * nr, nr)
@@ -106,7 +102,7 @@
                 (exp_ref.at[pl.ds(r0, nr), :], exp_v),
                 (act, act_out),
                 (lines, lines_out),
-                (tab, tab_out),
+                (tall, tall_out),
             ]
         )
     ]
@@ -129,7 +125,7 @@
         copy.wait()
 
 
-def grads_body(n, act, after, *refs):
+def grads_body(n, act, *refs):
     ups, outs = refs[:n], refs[n:]
     up = jnp.concatenate([u[:B, :] for u in ups], axis=0)
     for c in range(0, act.shape[1], G):
@@ -148,15 +144,15 @@
     out[n_t * n :, :] = jnp.concatenate([rows, jnp.zeros((16 - keep, 128), F32)], axis=0).astype(BF16)
 
 
-def join_body(after, *refs):
-    for i, ref in enumerate(refs[:-1]):
+def join_body(n, *refs):
+    for i, ref in enumerate(refs[:n]):
         refs[-1][i] = ref[...]
 
 
-def own_body(n_r, keep, mask, tally, lines, tab, p_ref, a_ref, w_ref, mask_s, tally_s, sems):
+def own_body(n_r, keep, mask, tally, tab, lines, tall, p_ref, a_ref, w_ref, tab_ref, mask_s, tally_s, sems):
     copies = [
         pltpu.make_async_copy(src, dst, sems.at[i])
-        for i, (src, dst) in enumerate([(mask, mask_s), (tally, tally_s)])
+        for i, (src, dst) in enumerate([(mask, mask_s), (tally, tally_s), (tab, tab_ref)])
     ]
     for copy in copies:
         copy.start()
@@ -171,7 +167,7 @@
         for j in range(1, G // B):
             num = jnp.where(block == j, rows[g * (G // B) + j : g * (G // B) + j + 1], num)
         hot = jnp.where(freq == num, 1.0, 0.0).astype(BF16)
-        y = dot(tall(tab), hot)
+        y = dot(tall[:, :B], hot)
         p = jnp.where(term == 3, 0.0, jnp.where(term == 1, y[B:], y[:B]))
         p_ref[:, g * 2 * B : (g + 1) * 2 * B] = p.astype(BF16)
         a_ref[g * B : (g + 1) * B, :] = jnp.concatenate([p, p], axis=0).T[:B].astype(BF16)
@@ -193,8 +189,8 @@
         w_ref[h] = w * scale
 
 
-def kept_body(n_t, keep, vel, a_ref, tab, after, after_too, *refs):
-    grads, ship_ref = refs[:n_t], refs[n_t]
+def kept_body(n_t, keep, vel, a_ref, tab, after, *refs):
+    grads, (send_ref, own_ref) = refs[:n_t], refs[n_t:]
     cols = grads[0].shape[1]
     ng = cols // G
     lane_block = lax.broadcasted_iota(jnp.int32, (keep, G), 1) // B
@@ -214,32 +210,26 @@
     hi, lo = split(jnp.concatenate(sel, axis=0))
     n = n_t * ng * keep
     y = dot(jnp.concatenate([hi, lo], axis=0), fwd(tab, 0))
-    y = y[:n] + y[n:] + dot(hi, fwd(tab, 1))
+    kept = (y[:n] + y[n:] + dot(hi, fwd(tab, 1))).astype(BF16)
+    q = dot(kept, inv(tab, 0)) + dot(kept, inv(tab, 1))
     for k in range(n_t):
         c0 = pl.multiple_of(lax.rem(lax.axis_index("tensor") + k, n_t) * cols, G)
-        ship_ref[:, pl.ds(c0, cols)] = jnp.concatenate(
-            [y[(k * ng + i) * keep : (k * ng + i + 1) * keep] for i in range(ng)], axis=1
-        ).astype(BF16)
-
-
-def return_body(n_t, keep, vel, p_ref, tab, ship, *refs):
+        part = jnp.concatenate([q[(k * ng + i) * keep : (k * ng + i + 1) * keep] for i in range(ng)], axis=1)
+        own_ref[:, pl.ds(c0, cols)] = part
+        send_ref[:, pl.ds(c0, cols)] = part.astype(BF16)
+
+
+def return_body(n_t, keep, vel, p_ref, q, *refs):
     grads, (new_ref, held, sems) = refs[:n_t], refs[n_t:]
     cols = grads[0].shape[1]
     ng = cols // G
     lane_block = lax.broadcasted_iota(jnp.int32, (keep, G), 1) // B
-    q = []
-    for k in range(n_t):
-        c0 = pl.multiple_of(lax.rem(lax.axis_index("tensor") + k, n_t) * cols, G)
-        kept = ship[:, pl.ds(c0, cols)].astype(F32)
-        q += [kept[:, i * G : (i + 1) * G] for i in range(ng)]
-    q = jnp.concatenate(q, axis=0).astype(BF16)
-    q = dot(q, inv(tab, 0)) + dot(q, inv(tab, 1))
     copies = []
     for k in range(n_t):
         c0 = pl.multiple_of(lax.rem(lax.axis_index("tensor") + k, n_t) * cols, G)
         for i in range(ng):
             at = pl.multiple_of(c0 + i * G, G)
-            own = q[(k * ng + i) * keep : (k * ng + i + 1) * keep]
+            own = q[:, pl.ds(at, G)]
             spread = jnp.concatenate(
                 [jnp.where(lane_block == j, own, 0.0) for j in range(G // B)], axis=0
             )
@@ -255,7 +245,7 @@
         copy.wait()
 
 
-def places_body(keep, w_ref, tab, bundles, *p_refs):
+def places_body(keep, w_ref, tall, bundles, *p_refs):
     n_r, last = bundles.shape[0], bundles.shape[1] - 16
     half, nb = n_r // 2, G // B
     rep = lax.axis_index("replica")
@@ -271,7 +261,7 @@
             for j in range(1, nb):
                 num = jnp.where(block == j, rows[g * nb + j : g * nb + j + 1], num)
             hot = jnp.where(freq == num, 1.0, 0.0).astype(BF16)
-            y = dot(tall(tab), hot)
+            y = dot(tall[:, :B], hot)
             hi, lo = split((y[:B] + y[B:]) * w)
             hi_ref[:, g * 2 * B : (g + 1) * 2 * B] = hi
             lo_ref[:, g * 2 * B : (g + 1) * 2 * B] = lo
@@ -294,17 +284,12 @@
         out[g * B : (g + 1) * B, :] = spread_rows(p_hi, p_lo, mine, g)
 
 
-def update_body(chunk, half_sum, p_hi, p_lo, tab, other, out, hi_ref, lo_ref, held, sems):
+def update_body(chunk, half_sum, p_hi, p_lo, other, out, held, sems):
     ng = half_sum.shape[0] // B
     copies = []
     for c in range(0, ng, chunk):
         for g in range(c, c + chunk):
-            at = slice(g * B, (g + 1) * B)
-            hi_ref[at, :], lo_ref[at, :] = split(half_sum[at, :] + spread_rows(p_hi, p_lo, other, g))
-        rows = slice(c * B, (c + chunk) * B)
-        z = dot(hi_ref[rows, :], inv(tab, 0)) + dot(lo_ref[rows, :], inv(tab, 0)) + dot(hi_ref[rows, :], inv(tab, 1))
-        for g in range(chunk):
-            held[:, (c + g) * G : (c + g + 1) * G] = z[g * B : (g + 1) * B]
+            held[:, g * G : (g + 1) * G] = half_sum[g * B : (g + 1) * B, :] + spread_rows(p_hi, p_lo, other, g)
         cut = pl.ds(c * G, chunk * G)
         copies.append(pltpu.make_async_copy(held.at[:, cut], out.at[:, cut], sems.at[c // chunk]))
         copies[-1].start()
@@ -338,7 +323,7 @@
     cp = 2
     rp = n_r // cp
     half = n_r // 2
-    tab = constants()
+    tab, tall = constants()
     def shift(x, k):
         return lax.ppermute(x, "tensor", [(i, (i + k) % n_t) for i in range(n_t)])
 
@@ -350,11 +335,11 @@
     own = lines[0, 0].T
     tiles = cols // cp // 128
     nr = B // rp
-    *parts, act, own, tab = call(
+    *parts, act, own, tall = call(
         functools.partial(first_body, n_t, cp, cols, nr),
         [near((B + tiles * nr, 128))] * n_t
-        + [near(act.shape), near(own.shape, jnp.int32), near(tab.shape)],
-        (far(switch.T), far(slope.T), far(exp), far(act), far(own), far(tab)),
+        + [near(act.shape), near(own.shape, jnp.int32), near(tall.shape)],
+        (far(switch.T), far(slope.T), far(exp), far(act), far(own), far(tall)),
         [ANY] * 6,
         [VM] * (n_t + 3),
         scratch=[
@@ -368,34 +353,35 @@
     )
     parts = [parts[0]] + [shift(parts[k], k) for k in range(1, n_t)]
 
-    p_own, a_own, shares = call(
+    p_own, a_own, shares, tab = call(
         functools.partial(own_body, n_r, keep),
         [
             near((B, groups * 2 * B)),
             near((groups * B, 2 * B)),
             near((2, 8, 2 * B), F32),
+            near(tab.shape),
         ],
-        (far(mask), far(tally), own, tab),
-        [ANY, ANY, VM, VM],
-        [VM] * 3,
-        scratch=[pltpu.SMEM((n_r,), jnp.int32)] * 2 + [pltpu.SemaphoreType.DMA((2,))],
+        (far(mask), far(tally), far(tab), own, tall),
+        [ANY, ANY, ANY, VM, VM],
+        [VM] * 4,
+        scratch=[pltpu.SMEM((n_r,), jnp.int32)] * 2 + [pltpu.SemaphoreType.DMA((3,))],
         name="own_places",
     )
 
-    def grads_of(ks, after):
+    def grads_of(ks):
         return call(
             functools.partial(grads_body, len(ks)),
             [near((B, cols), BF16 if k else F32) for k in ks],
-            (act, after, *[parts[k] for k in ks]),
-            [VM, ANY] + [VM] * len(ks),
+            (act, *[parts[k] for k in ks]),
+            [VM] * (1 + len(ks)),
             [VM] * len(ks),
             name="weight_grads",
         )
 
     grads = {}
     for k in order[:-1]:
-        (grads[k],) = grads_of([k], act)
-    made, grads[0] = grads_of([order[-1], 0], shares)
+        (grads[k],) = grads_of([k])
+    made, grads[0] = grads_of([order[-1], 0])
     grads[order[-1]] = made
     grads = [grads[0]] + [shift(grads[k], -k) for k in range(1, n_t)]
 
@@ -412,7 +398,7 @@
     places = call(
         functools.partial(places_body, keep),
         [near((B, blocks * half * keep))] * 4,
-        (shares, tab, bundles),
+        (shares, tall, bundles),
         [VM] * 3,
         [VM] * 4,
         name="places",
@@ -429,12 +415,12 @@
         name="input_grads",
     )
 
-    ship = call(
+    ship, q_own = call(
         functools.partial(kept_body, n_t, keep),
-        near((keep, width)),
-        (vel[0], a_own, tab, places[0], far(input_grad), *grads),
-        [VM] * 3 + [ANY, ANY] + [VM] * n_t,
-        VM,
+        [near((keep, width)), near((keep, width), F32)],
+        (vel[0], a_own, tab, bundles, *grads),
+        [VM] * 3 + [ANY] + [VM] * n_t,
+        [VM] * 2,
         flops=6 * B * B * width,
         nbytes=B * width * 6,
         name="kept_rows",
@@ -443,8 +429,8 @@
     new = call(
         functools.partial(return_body, n_t, keep),
         jax.ShapeDtypeStruct((B, width), F32),
-        (vel[0], p_own, tab, ship, *grads),
-        [VM] * (4 + n_t),
+        (vel[0], p_own, q_own, *grads),
+        [VM] * (3 + n_t),
         ANY,
         scratch=[pltpu.VMEM((B, width), F32), pltpu.SemaphoreType.DMA((n_t,))],
         flops=6 * B * B * width,
@@ -452,10 +438,10 @@
         name="new_momentums",
     )
     mine = call(
-        join_body,
+        functools.partial(join_body, half),
         near((half, keep, width)),
-        (far(new), *ships),
-        [ANY] + [VM] * half,
+        (*ships, far(new), far(input_grad), places[0]),
+        [VM] * half + [ANY] * 3,
         VM,
         name="join_kept",
     )
@@ -472,12 +458,10 @@
     update = call(
         functools.partial(update_body, chunk),
         jax.ShapeDtypeStruct((B, width), F32),
-        (half_sum, *places[2:], tab, other),
-        [VM] * 5,
+        (half_sum, *places[2:], other),
+        [VM] * 4,
         ANY,
         scratch=[
-            pltpu.VMEM((groups * B, G), BF16),
-            pltpu.VMEM((groups * B, G), BF16),
             pltpu.VMEM((B, width), F32),
             pltpu.SemaphoreType.DMA((groups // chunk,)),
         ],

time: 37.9 us -> 38.7 us (1.021)
  waiting for transfers between devices: 3.8 us -> 5.48 us
  Pallas kernels: 9.05 us -> 8.51 us
    ppermute x6, waiting for transfers between devices: 0.29 us -> 3.42 us  [shift(): return lax.ppermute(x, 'tensor', [(i, (i + k) % n_t) for i in range(n_t)])]
    ppermute x4, waiting for transfers between devices: 3.51 us -> 2.06 us  [swap(): return lax.ppermute(x, 'replica', [(i, i ^ m) for i in range(n_r)])]
    pallas_call x13, Pallas kernels: 9.05 us -> 8.51 us  [call(): pl.pallas_call(body, out_shape=out_shape, in_specs=in_specs, out_specs=ou...]
  transfers between devices with their start and end apart: 10 -> 10, of which waited for: 5 -> 6; matrix products, arithmetic and copies ran while one was open for 0% -> 0% of each run, Pallas kernels for 13% -> 13%
where the time goes in v7:
time: 38.7 us; the launch traced here: 38.5 us
  starting transfers between devices  13.5 us (35%)
  blocking collectives  10.3 us (27%)
  Pallas kernels  8.51 us (22%)
  waiting for transfers between devices  5.48 us (14%)
  between operations  0.73 us (2%)
    all_gather x1, blocking collectives, per_device(): bundles = lax.all_gather(bundle, 'replica', axis=0)  10.3 us
    ppermute x6, starting transfers between devices, shift(): return lax.ppermute(x, 'tensor', [(i, (i + k) % n_t) for i in range(n_t)])  9.85 us
    pallas_call x13, Pallas kernels, call(): pl.pallas_call(body, out_shape=out_shape, in_specs=in_specs, out_specs=ou...  8.51 us
    ppermute x4, starting transfers between devices, swap(): return lax.ppermute(x, 'replica', [(i, i ^ m) for i in range(n_r)])  3.62 us
    ppermute x6, waiting for transfers between devices, shift(): return lax.ppermute(x, 'tensor', [(i, (i + k) % n_t) for i in range(n_t)])  3.42 us
    ppermute x4, waiting for transfers between devices, swap(): return lax.ppermute(x, 'replica', [(i, i ^ m) for i in range(n_r)])  2.06 us
  transfers between devices with their start and end apart: 10, of which 6 were waited for; matrix products, arithmetic and copies ran while one was open for 0% of the time, Pallas kernels for 13%

profile of v7, /device:TPU:0, one launch (start us, length us, event | category | flops | bytes accessed | tf_op | source)
XLA Modules:
  0.0 38.5 jit_solution(13539252615094436031)
XLA Ops:
  0.6 1.2 %up_grads.1 = (bf16[144,128]{1,0:T(8,128)(2,1)S(1)}, bf16[144,128]{1,0:T(8,128)(2,1)S(1)}, bf16[144,128]{1,0:T(8,128)(2,1)S(1)}, bf16[144,128]{1,0:T(8,128)(2,1)...) custom-call(bf16[64,128]{1,0:T(8,128)(2,1)} %bitcast.14, ...), custom_call_target="tpu_custom_call" | custom-call | bytes 819200 | tf_op jit(solution)/shard_map/up_grads/pallas_call | solution.py:79
  1.8 5.1 %collective-permute-start = (bf16[144,128]{1,0:T(8,128)(2,1)S(1)}, bf16[144,128]{1,0:T(8,128)(2,1)S(1)}, u32[]{:S(2)}, u32[]{:S(2)}) collective-permute-start(bf16[144,128]{1,0:T(8,128)(2,1)S(1)} %get-tuple-element.23), channel_id=1, source_target_pairs={{0,3},{1,0},{2,1},{3,2},{4,7},{5,4},{6,5},{7,6},{8,11},{9,8},{10,9... | collective-permute-start | bytes 110600 | tf_op jit(solution)/shard_map/ppermute | solution.py:328
  6.9 0.0 collective-permute-start.1
  6.9 1.0 %collective-permute-start.2 = (bf16[144,128]{1,0:T(8,128)(2,1)S(1)}, bf16[144,128]{1,0:T(8,128)(2,1)S(1)}, u32[]{:S(2)}, u32[]{:S(2)}) collective-permute-start(bf16[144,128]{1,0:T(8,128)(2,1)S(1)} %get-tuple-element.28), channel_id=1, source_target_pairs={{0,2},{1,3},{2,0},{3,1},{4,6},{5,7},{6,4},{7,5},{8,10},{9,11},{10,... | collective-permute-start | bytes 110600 | tf_op jit(solution)/shard_map/ppermute | solution.py:328
  7.9 0.6 %collective-permute-done.refs_0_.refs_3_ = bf16[144,128]{1,0:T(8,128)(2,1)S(1)} collective-permute-done((bf16[144,128]{1,0:T(8,128)(2,1)S(1)}, bf16[144,128]{1,0:T(8,128)(2,1)S(1)}, u32[]{:S(2)}, u32[]{:S(2)}) %collective-permute-start) | collective-permute-done | bytes 36896 | tf_op jit(solution)/shard_map/ppermute | solution.py:328
  8.5 0.2 weight_grads.3
  8.8 0.0 copy-start
  8.8 2.8 %collective-permute-start.5 = (bf16[64,1280]{1,0:T(8,128)(2,1)S(1)}, bf16[64,1280]{1,0:T(8,128)(2,1)S(1)}, u32[]{:S(2)}, u32[]{:S(2)}) collective-permute-start(bf16[64,1280]{1,0:T(8,128)(2,1)S(1)} %get-tuple-element.25.after), channel_id=1, source_target_pairs={{0,1},{1,2},{2,3},{3,0},{4,5},{5,6},{6,7},{7,4},{8,9},{9,10},{10,1... | collective-permute-start | bytes 491528 | tf_op jit(solution)/shard_map/ppermute | solution.py:328
  11.6 1.2 %collective-permute-done.1.refs_1_.refs_0_ = bf16[144,128]{1,0:T(8,128)(2,1)S(1)} collective-permute-done((bf16[144,128]{1,0:T(8,128)(2,1)S(1)}, bf16[144,128]{1,0:T(8,128)(2,1)S(1)}, u32[]{:S(2)}, u32[]{:S(2)}) %collective-permute-start.1) | collective-permute-done | bytes 36896 | tf_op jit(solution)/shard_map/ppermute | solution.py:328
  12.8 0.2 weight_grads.4
  13.0 0.3 collective-permute-start.3
  13.3 0.0 collective-permute-done.2.refs_2_.refs_0_
  13.3 0.2 weight_grads.5
  13.5 0.6 %collective-permute-start.4 = (bf16[64,1280]{1,0:T(8,128)(2,1)S(1)}, bf16[64,1280]{1,0:T(8,128)(2,1)S(1)}, u32[]{:S(2)}, u32[]{:S(2)}) collective-permute-start(bf16[64,1280]{1,0:T(8,128)(2,1)S(1)} %weight_grads.5), channel_id=1, source_target_pairs={{0,2},{1,3},{2,0},{3,1},{4,6},{5,7},{6,4},{7,5},{8,10},{9,11},{10,... | collective-permute-start | bytes 491528 | tf_op jit(solution)/shard_map/ppermute | solution.py:328
  14.1 1.1 %own_places.1 = (bf16[64,2560]{1,0:T(8,128)(2,1)S(1)}, bf16[1280,128]{1,0:T(8,128)(2,1)S(1)}, f32[2,8,128]{2,1,0:T(8,128)S(1)}, bf16[1024,256]{1,0:T(8,128)(2,1)S(1)}) custom-call(s32[8]{0:T(128)} %mask.1, s32[8]{0:T(128)} %tally.1, bf16[1024,256]{1,0:T(8,128)(2,1)} %constant.4.clone.tab, s32[8,80]{1,0:T(8,128)S(1)} %get-tuple-element.26.lines, ...), custom_call_target="tpu_custom_call" | custom-call | tf_op jit(solution)/shard_map/own_places/pallas_call | solution.py:79
  15.2 10.3 %all-gather = bf16[2688,128]{1,0:T(8,128)(2,1)S(1)} all-gather(bf16[336,128]{1,0:T(8,128)(2,1)S(1)} %bundle.1), channel_id=2, replica_groups=mesh['replica'=8,'tensor'=4] {'replica'}, dimensions={0}, use_global_device_ids=true | all-gather | bytes 774144 | tf_op jit(solution)/shard_map/all_gather | solution.py:396
  25.5 0.0 collective-permute-done.5.refs_3_
  25.5 0.0 collective-permute-done.3.refs_1_
  25.5 1.6 %collective-permute-done.4.refs_2_ = bf16[64,1280]{1,0:T(8,128)(2,1)S(1)} collective-permute-done((bf16[64,1280]{1,0:T(8,128)(2,1)S(1)}, bf16[64,1280]{1,0:T(8,128)(2,1)S(1)}, u32[]{:S(2)}, u32[]{:S(2)}) %collective-permute-start.4) | collective-permute-done | bytes 163872 | tf_op jit(solution)/shard_map/ppermute | solution.py:328
  27.1 0.0 copy-done
  27.1 0.9 %kept_rows.1 = (bf16[8,5120]{1,0:T(8,128)(2,1)S(1)}, f32[8,5120]{1,0:T(8,128)S(1)}) custom-call(f32[64,5120]{1,0:T(8,128)S(1)} %bitcast.11, bf16[1280,128]{1,0:T(8,128)(2,1)S(1)} %get-tuple-element.31.a_ref, bf16[1024,256]{1,0:T(8,128)(2,1)S(1)} %get-tuple-element.32.tab, bf16[8,336,128]{2,1,0:T(8,128)(2,1)S(1)} %bitcast.8, ...), custom_call_target="tpu_custom_call" | custom-call | flops 125829120 | bytes 1966080 | tf_op jit(solution)/shard_map/kept_rows/pallas_call | solution.py:79
  28.0 2.5 %collective-permute-start.8 = (bf16[8,5120]{1,0:T(8,128)(2,1)S(1)}, bf16[8,5120]{1,0:T(8,128)(2,1)S(1)}, u32[]{:S(2)}, u32[]{:S(2)}) collective-permute-start(bf16[8,5120]{1,0:T(8,128)(2,1)S(1)} %get-tuple-element.38.refs_0_), channel_id=1, source_target_pairs={{0,24},{4,28},{8,16},{12,20},{16,8},{20,12},{24,0},{28,4},{1,25},{... | collective-permute-start | bytes 245768 | tf_op jit(solution)/shard_map/ppermute | solution.py:333
  30.5 0.5 %collective-permute-start.7 = (bf16[8,5120]{1,0:T(8,128)(2,1)S(1)}, bf16[8,5120]{1,0:T(8,128)(2,1)S(1)}, u32[]{:S(2)}, u32[]{:S(2)}) collective-permute-start(bf16[8,5120]{1,0:T(8,128)(2,1)S(1)} %get-tuple-element.38.refs_0_), channel_id=1, source_target_pairs={{0,16},{4,20},{8,24},{12,28},{16,0},{20,4},{24,8},{28,12},{1,17},{... | collective-permute-start | bytes 245768 | tf_op jit(solution)/shard_map/ppermute | solution.py:333
  31.0 0.5 %collective-permute-start.6 = (bf16[8,5120]{1,0:T(8,128)(2,1)S(1)}, bf16[8,5120]{1,0:T(8,128)(2,1)S(1)}, u32[]{:S(2)}, u32[]{:S(2)}) collective-permute-start(bf16[8,5120]{1,0:T(8,128)(2,1)S(1)} %get-tuple-element.38.refs_0_), channel_id=1, source_target_pairs={{0,8},{4,12},{8,0},{12,4},{16,24},{20,28},{24,16},{28,20},{1,9},{5... | collective-permute-start | bytes 245768 | tf_op jit(solution)/shard_map/ppermute | solution.py:333
  31.5 0.6 %places.1 = (bf16[64,2560]{1,0:T(8,128)(2,1)S(1)}, bf16[64,2560]{1,0:T(8,128)(2,1)S(1)}, bf16[64,2560]{1,0:T(8,128)(2,1)S(1)}, bf16[64,2560]{1,0:T(8,128)(2,1)S(1)}) custom-call(f32[2,8,128]{2,1,0:T(8,128)S(1)} %get-tuple-element.35.w_ref, bf16[128,128]{1,0:T(8,128)(2,1)S(1)} %get-tuple-element.29.tall, bf16[8,336,128]{2,1,0:T(8,128)(2,1)S(1)} %bitcast.9), custom_call_target="tpu_custom_call" | custom-call | tf_op jit(solution)/shard_map/places/pallas_call | solution.py:79
  32.1 1.1 %input_grads.1.refs_5_ = bf16[128,1280]{1,0:T(8,128)(2,1)} custom-call(bf16[8,336,128]{2,1,0:T(8,128)(2,1)S(1)} %bitcast.10, bf16[144,128]{1,0:T(8,128)(2,1)S(1)} %get-tuple-element.24.refs_1_.refs_0_, bf16[144,128]{1,0:T(8,128)(2,1)S(1)} %collective-permute-done.1.refs_1_.refs_0_, bf16[144,128]{1,0:T(8,128)(2,1)S(1)} %collective-permute-done.2.refs_2_.refs_0_, ...), custom_call_target="tpu_custom_call" | custom-call | flops 83886080 | bytes 983040 | tf_op jit(solution)/shard_map/input_grads/pallas_call | solution.py:79
  33.2 1.3 %new_momentums.1.refs_4_ = f32[64,5120]{1,0:T(8,128)} custom-call(f32[64,5120]{1,0:T(8,128)S(1)} %bitcast.12, bf16[64,2560]{1,0:T(8,128)(2,1)S(1)} %get-tuple-element.30.p_ref, f32[8,5120]{1,0:T(8,128)S(1)} %get-tuple-element.34.q, f32[64,1280]{1,0:T(8,128)S(1)} %get-tuple-element.33.refs_0_, bf16[64,1280]{1,0:T(8,128)(2,1)S(1)} %collective-permute-done.3.refs_1_, ...), custom_call_target="tpu_custom_call" | custom-call | flops 125829120 | bytes 3276800 | tf_op jit(solution)/shard_map/new_momentums/pallas_call | solution.py:79
  34.5 0.0 collective-permute-done.8.refs_3_
  34.5 0.6 %collective-permute-done.7.refs_2_ = bf16[8,5120]{1,0:T(8,128)(2,1)S(1)} collective-permute-done((bf16[8,5120]{1,0:T(8,128)(2,1)S(1)}, bf16[8,5120]{1,0:T(8,128)(2,1)S(1)}, u32[]{:S(2)}, u32[]{:S(2)}) %collective-permute-start.7) | collective-permute-done | bytes 81952 | tf_op jit(solution)/shard_map/ppermute | solution.py:333
  35.1 0.3 collective-permute-done.6.refs_1_
  35.5 0.1 collective-permute-start.9
  35.5 0.5 %half_updates.1.half_sum = f32[1280,256]{1,0:T(8,128)S(1)} custom-call(bf16[64,2560]{1,0:T(8,128)(2,1)S(1)} %get-tuple-element.36.refs_6_.p_hi, bf16[64,2560]{1,0:T(8,128)(2,1)S(1)} %get-tuple-element.37.p_lo, bf16[4,8,5120]{2,1,0:T(8,128)(2,1)S(1)} %join_kept.1.mine), custom_call_target="tpu_custom_call" | custom-call | tf_op jit(solution)/shard_map/half_updates/pallas_call | solution.py:79
  36.0 1.1 %collective-permute-done.9.other = bf16[4,8,5120]{2,1,0:T(8,128)(2,1)S(1)} collective-permute-done((bf16[4,8,5120]{2,1,0:T(8,128)(2,1)S(1)}, bf16[4,8,5120]{2,1,0:T(8,128)(2,1)S(1)}, u32[]{:S(2)}, u32[]{:S(2)}) %collective-permute-start.9) | collective-permute-done | bytes 327712 | tf_op jit(solution)/shard_map/ppermute | solution.py:333
  37.2 1.3 %updates.1 = f32[64,5120]{1,0:T(8,128)} custom-call(f32[1280,256]{1,0:T(8,128)S(1)} %half_updates.1.half_sum, bf16[64,2560]{1,0:T(8,128)(2,1)S(1)} %get-tuple-element.39.p_hi, bf16[64,2560]{1,0:T(8,128)(2,1)S(1)} %get-tuple-element.40.p_lo, bf16[4,8,5120]{2,1,0:T(8,128)(2,1)S(1)} %collective-permute-done.9.other), custom_call_target="tpu_custom_call" | custom-call | flops 671088640 | bytes 2621440 | tf_op jit(solution)/shard_map/updates/pallas_call | solution.py:79
  (2 shorter events, 0.0 us)
Async XLA Ops:
  1.8 6.7 %collective-permute-start = (bf16[144,128]{1,0:T(8,128)(2,1)S(1)}, bf16[144,128]{1,0:T(8,128)(2,1)S(1)}, u32[]{:S(2)}, u32[]{:S(2)}) collective-permute-start(bf16[144,128]{1,0:T(8,128)(2,1)S(1)} %get-tuple-element.23), channel_id=1, source_target_pairs={{0,3},{1,0},{2,1},{3,2},{4,7},{5,4},{6,5},{7,6},{8,11},{9,8},{10,9... | collective-permute-start | bytes 110600 | tf_op jit(solution)/shard_map/ppermute | solution.py:328
  6.9 5.9 %collective-permute-start.1 = (bf16[144,128]{1,0:T(8,128)(2,1)S(1)}, bf16[144,128]{1,0:T(8,128)(2,1)S(1)}, u32[]{:S(2)}, u32[]{:S(2)}) collective-permute-start(bf16[144,128]{1,0:T(8,128)(2,1)S(1)} %get-tuple-element.27), channel_id=1, source_target_pairs={{0,1},{1,2},{2,3},{3,0},{4,5},{5,6},{6,7},{7,4},{8,9},{9,10},{10,1... | collective-permute-start | bytes 110600 | tf_op jit(solution)/shard_map/ppermute | solution.py:328
  6.9 6.4 %collective-permute-start.2 = (bf16[144,128]{1,0:T(8,128)(2,1)S(1)}, bf16[144,128]{1,0:T(8,128)(2,1)S(1)}, u32[]{:S(2)}, u32[]{:S(2)}) collective-permute-start(bf16[144,128]{1,0:T(8,128)(2,1)S(1)} %get-tuple-element.28), channel_id=1, source_target_pairs={{0,2},{1,3},{2,0},{3,1},{4,6},{5,7},{6,4},{7,5},{8,10},{9,11},{10,... | collective-permute-start | bytes 110600 | tf_op jit(solution)/shard_map/ppermute | solution.py:328
  8.8 18.3 %copy-start = (f32[1,64,5120]{2,1,0:T(8,128)S(1)}, f32[1,64,5120]{2,1,0:T(8,128)}, u32[]{:S(2)}) copy-start(f32[1,64,5120]{2,1,0:T(8,128)} %param.14) | copy-start | bytes 3932164
  8.8 16.7 %collective-permute-start.5 = (bf16[64,1280]{1,0:T(8,128)(2,1)S(1)}, bf16[64,1280]{1,0:T(8,128)(2,1)S(1)}, u32[]{:S(2)}, u32[]{:S(2)}) collective-permute-start(bf16[64,1280]{1,0:T(8,128)(2,1)S(1)} %get-tuple-element.25.after), channel_id=1, source_target_pairs={{0,1},{1,2},{2,3},{3,0},{4,5},{5,6},{6,7},{7,4},{8,9},{9,10},{10,1... | collective-permute-start | bytes 491528 | tf_op jit(solution)/shard_map/ppermute | solution.py:328
  13.0 12.5 %collective-permute-start.3 = (bf16[64,1280]{1,0:T(8,128)(2,1)S(1)}, bf16[64,1280]{1,0:T(8,128)(2,1)S(1)}, u32[]{:S(2)}, u32[]{:S(2)}) collective-permute-start(bf16[64,1280]{1,0:T(8,128)(2,1)S(1)} %weight_grads.4), channel_id=1, source_target_pairs={{0,3},{1,0},{2,1},{3,2},{4,7},{5,4},{6,5},{7,6},{8,11},{9,8},{10,9... | collective-permute-start | bytes 491528 | tf_op jit(solution)/shard_map/ppermute | solution.py:328
  13.5 13.6 %collective-permute-start.4 = (bf16[64,1280]{1,0:T(8,128)(2,1)S(1)}, bf16[64,1280]{1,0:T(8,128)(2,1)S(1)}, u32[]{:S(2)}, u32[]{:S(2)}) collective-permute-start(bf16[64,1280]{1,0:T(8,128)(2,1)S(1)} %weight_grads.5), channel_id=1, source_target_pairs={{0,2},{1,3},{2,0},{3,1},{4,6},{5,7},{6,4},{7,5},{8,10},{9,11},{10,... | collective-permute-start | bytes 491528 | tf_op jit(solution)/shard_map/ppermute | solution.py:328
  28.0 6.5 %collective-permute-start.8 = (bf16[8,5120]{1,0:T(8,128)(2,1)S(1)}, bf16[8,5120]{1,0:T(8,128)(2,1)S(1)}, u32[]{:S(2)}, u32[]{:S(2)}) collective-permute-start(bf16[8,5120]{1,0:T(8,128)(2,1)S(1)} %get-tuple-element.38.refs_0_), channel_id=1, source_target_pairs={{0,24},{4,28},{8,16},{12,20},{16,8},{20,12},{24,0},{28,4},{1,25},{... | collective-permute-start | bytes 245768 | tf_op jit(solution)/shard_map/ppermute | solution.py:333
  30.5 4.6 %collective-permute-start.7 = (bf16[8,5120]{1,0:T(8,128)(2,1)S(1)}, bf16[8,5120]{1,0:T(8,128)(2,1)S(1)}, u32[]{:S(2)}, u32[]{:S(2)}) collective-permute-start(bf16[8,5120]{1,0:T(8,128)(2,1)S(1)} %get-tuple-element.38.refs_0_), channel_id=1, source_target_pairs={{0,16},{4,20},{8,24},{12,28},{16,0},{20,4},{24,8},{28,12},{1,17},{... | collective-permute-start | bytes 245768 | tf_op jit(solution)/shard_map/ppermute | solution.py:333
  31.0 4.4 %collective-permute-start.6 = (bf16[8,5120]{1,0:T(8,128)(2,1)S(1)}, bf16[8,5120]{1,0:T(8,128)(2,1)S(1)}, u32[]{:S(2)}, u32[]{:S(2)}) collective-permute-start(bf16[8,5120]{1,0:T(8,128)(2,1)S(1)} %get-tuple-element.38.refs_0_), channel_id=1, source_target_pairs={{0,8},{4,12},{8,0},{12,4},{16,24},{20,28},{24,16},{28,20},{1,9},{5... | collective-permute-start | bytes 245768 | tf_op jit(solution)/shard_map/ppermute | solution.py:333
  35.5 1.7 %collective-permute-start.9 = (bf16[4,8,5120]{2,1,0:T(8,128)(2,1)S(1)}, bf16[4,8,5120]{2,1,0:T(8,128)(2,1)S(1)}, u32[]{:S(2)}, u32[]{:S(2)}) collective-permute-start(bf16[4,8,5120]{2,1,0:T(8,128)(2,1)S(1)} %join_kept.1.mine), channel_id=1, source_target_pairs={{0,4},{4,0},{8,12},{12,8},{16,20},{20,16},{24,28},{28,24},{1,5},{5... | collective-permute-start | bytes 983048 | tf_op jit(solution)/shard_map/ppermute | solution.py:333

commit v8 on v7

--- a/solution.py
+++ b/solution.py
@@ -75,13 +75,14 @@
     return pltpu.with_memory_space_constraint(x, pltpu.HBM)
 
 
-def call(body, out_shape, ins, in_specs, out_specs, scratch=(), flops=0, nbytes=0, name=None):
+def call(body, out_shape, ins, in_specs, out_specs, scratch=(), flops=0, nbytes=0, name=None, alias={}):
     return pl.pallas_call(
         body,
         out_shape=out_shape,
         in_specs=in_specs,
         out_specs=out_specs,
         scratch_shapes=scratch,
+        input_output_aliases=alias,
         compiler_params=pltpu.CompilerParams(vmem_limit_bytes=VMEM_LIMIT),
         cost_estimate=pl.CostEstimate(flops=flops, bytes_accessed=nbytes, transcendentals=0),
         name=name,
@@ -125,7 +126,7 @@
         copy.wait()
 
 
-def grads_body(n, act, *refs):
+def grads_body(n, act, after, *refs):
     ups, outs = refs[:n], refs[n:]
     up = jnp.concatenate([u[:B, :] for u in ups], axis=0)
     for c in range(0, act.shape[1], G):
@@ -149,7 +150,7 @@
         refs[-1][i] = ref[...]
 
 
-def own_body(n_r, keep, mask, tally, tab, lines, tall, p_ref, a_ref, w_ref, tab_ref, mask_s, tally_s, sems):
+def own_body(n_r, keep, after, mask, tally, tab, lines, tall, p_ref, a_ref, w_ref, tab_ref, mask_s, tally_s, sems):
     copies = [
         pltpu.make_async_copy(src, dst, sems.at[i])
         for i, (src, dst) in enumerate([(mask, mask_s), (tally, tally_s), (tab, tab_ref)])
@@ -189,17 +190,17 @@
         w_ref[h] = w * scale
 
 
-def kept_body(n_t, keep, vel, a_ref, tab, after, *refs):
-    grads, (send_ref, own_ref) = refs[:n_t], refs[n_t:]
+def kept_body(ks, n_t, keep, vel, a_ref, tab, *refs):
+    grads, (send_ref, own_ref) = refs[: len(ks)], refs[-2:]
     cols = grads[0].shape[1]
     ng = cols // G
     lane_block = lax.broadcasted_iota(jnp.int32, (keep, G), 1) // B
     sel = []
-    for k in range(n_t):
+    for n, k in enumerate(ks):
         c0 = lax.rem(lax.axis_index("tensor") + k, n_t) * cols
         for i in range(ng):
             at = pl.multiple_of(c0 + i * G, G)
-            moment = momentum_decay * vel[:, pl.ds(at, G)] + grads[k][:, i * G : (i + 1) * G].astype(F32)
+            moment = momentum_decay * vel[:, pl.ds(at, G)] + grads[n][:, i * G : (i + 1) * G].astype(F32)
             hi, lo = split(moment)
             y = dot(a_ref[pl.ds(pl.multiple_of(at // (G // B), B), B), :], jnp.concatenate([hi, lo], axis=0))
             y = y[: B // 2] + y[B // 2 :]
@@ -208,13 +209,13 @@
                 got = jnp.where(lane_block == j, y[j * keep : (j + 1) * keep], got)
             sel.append(got)
     hi, lo = split(jnp.concatenate(sel, axis=0))
-    n = n_t * ng * keep
+    n = len(ks) * ng * keep
     y = dot(jnp.concatenate([hi, lo], axis=0), fwd(tab, 0))
     kept = (y[:n] + y[n:] + dot(hi, fwd(tab, 1))).astype(BF16)
     q = dot(kept, inv(tab, 0)) + dot(kept, inv(tab, 1))
-    for k in range(n_t):
+    for n, k in enumerate(ks):
         c0 = pl.multiple_of(lax.rem(lax.axis_index("tensor") + k, n_t) * cols, G)
-        part = jnp.concatenate([q[(k * ng + i) * keep : (k * ng + i + 1) * keep] for i in range(ng)], axis=1)
+        part = jnp.concatenate([q[(n * ng + i) * keep : (n * ng + i + 1) * keep] for i in range(ng)], axis=1)
         own_ref[:, pl.ds(c0, cols)] = part
         send_ref[:, pl.ds(c0, cols)] = part.astype(BF16)
 
@@ -327,8 +328,6 @@
     def shift(x, k):
         return lax.ppermute(x, "tensor", [(i, (i + k) % n_t) for i in range(n_t)])
 
-    order = sorted(range(1, n_t), key=lambda k: -min(k, n_t - k))
-
     def swap(x, m):
         return lax.ppermute(x, "replica", [(i, i ^ m) for i in range(n_r)])
 
@@ -353,6 +352,35 @@
     )
     parts = [parts[0]] + [shift(parts[k], k) for k in range(1, n_t)]
 
+    def grads_of(ks, after):
+        return call(
+            functools.partial(grads_body, len(ks)),
+            [near((B, cols), BF16 if k else F32) for k in ks],
+            (act, after, *[parts[k] for k in ks]),
+            [VM, ANY] + [VM] * len(ks),
+            [VM] * len(ks),
+            name="weight_grads",
+        )
+
+    grads = {}
+    made = act
+    for k in range(1, n_t - 1):
+        (made,) = grads_of([k], made)
+        grads[k] = made
+    made, grads[0] = grads_of([n_t - 1, 0], made)
+    grads[n_t - 1] = made
+    grads = [grads[0]] + [shift(grads[k], -k) for k in range(1, n_t)]
+
+    bundle = call(
+        functools.partial(bundle_body, n_t, keep),
+        near((n_t * tiles * nr + 16, 128)),
+        (made, own, *parts),
+        [ANY] + [VM] * (n_t + 1),
+        VM,
+        name="bundle",
+    )
+    bundles = lax.all_gather(bundle, "replica", axis=0)
+
     p_own, a_own, shares, tab = call(
         functools.partial(own_body, n_r, keep),
         [
@@ -361,40 +389,12 @@
             near((2, 8, 2 * B), F32),
             near(tab.shape),
         ],
-        (far(mask), far(tally), far(tab), own, tall),
-        [ANY, ANY, ANY, VM, VM],
+        (bundles, far(mask), far(tally), far(tab), own, tall),
+        [ANY, ANY, ANY, ANY, VM, VM],
         [VM] * 4,
         scratch=[pltpu.SMEM((n_r,), jnp.int32)] * 2 + [pltpu.SemaphoreType.DMA((3,))],
         name="own_places",
     )
-
-    def grads_of(ks):
-        return call(
-            functools.partial(grads_body, len(ks)),
-            [near((B, cols), BF16 if k else F32) for k in ks],
-            (act, *[parts[k] for k in ks]),
-            [VM] * (1 + len(ks)),
-            [VM] * len(ks),
-            name="weight_grads",
-        )
-
-    grads = {}
-    for k in order[:-1]:
-        (grads[k],) = grads_of([k])
-    made, grads[0] = grads_of([order[-1], 0])
-    grads[order[-1]] = made
-    grads = [grads[0]] + [shift(grads[k], -k) for k in range(1, n_t)]
-
-    bundle = call(
-        functools.partial(bundle_body, n_t, keep),
-        near((n_t * tiles * nr + 16, 128)),
-        (made, own, *parts),
-        [ANY] + [VM] * (n_t + 1),
-        VM,
-        name="bundle",
-    )
-    bundles = lax.all_gather(bundle, "replica", axis=0)
-
     places = call(
         functools.partial(places_body, keep),
         [near((B, blocks * half * keep))] * 4,
@@ -415,16 +415,20 @@
         name="input_grads",
     )
 
-    ship, q_own = call(
-        functools.partial(kept_body, n_t, keep),
-        [near((keep, width)), near((keep, width), F32)],
-        (vel[0], a_own, tab, bundles, *grads),
-        [VM] * 3 + [ANY] + [VM] * n_t,
-        [VM] * 2,
-        flops=6 * B * B * width,
-        nbytes=B * width * 6,
-        name="kept_rows",
-    )
+    rows = []
+    for ks in (list(range(n_t - 1)), [n_t - 1]):
+        rows = call(
+            functools.partial(kept_body, ks, n_t, keep),
+            [near((keep, width)), near((keep, width), F32)],
+            (vel[0], a_own, tab, *[grads[k] for k in ks], *rows),
+            [VM] * (3 + len(ks) + len(rows)),
+            [VM] * 2,
+            flops=6 * B * B * cols * len(ks),
+            nbytes=B * cols * 6 * len(ks),
+            name="kept_rows",
+            alias={3 + len(ks): 0, 4 + len(ks): 1} if rows else {},
+        )
+    ship, q_own = rows
     ships = [ship] + [swap(ship, 2 * i) for i in range(1, half)]
     new = call(
         functools.partial(return_body, n_t, keep),

time: 38.7 us -> 38.3 us (0.990)
  waiting for transfers between devices: 5.48 us -> 3.18 us
  starting transfers between devices: 13.5 us -> 15 us
    ppermute x6, waiting for transfers between devices: 3.42 us -> 1.13 us  [shift(): return lax.ppermute(x, 'tensor', [(i, (i + k) % n_t) for i in range(n_t)])]
    ppermute x6, starting transfers between devices: 9.85 us -> 11.4 us  [shift(): return lax.ppermute(x, 'tensor', [(i, (i + k) % n_t) for i in range(n_t)])]
    pallas_call x13 -> x14, Pallas kernels: 8.51 us -> 8.85 us  [call(): pl.pallas_call(body, out_shape=out_shape, in_specs=in_specs, out_specs=ou...]
  transfers between devices with their start and end apart: 10 -> 10, of which waited for: 6 -> 3; matrix products, arithmetic and copies ran while one was open for 0% -> 0% of each run, Pallas kernels for 13% -> 15%
where the time goes in v8:
time: 38.3 us; the launch traced here: 38.1 us
  starting transfers between devices  15 us (39%)
  blocking collectives  10.3 us (27%)
  Pallas kernels  8.85 us (23%)
  waiting for transfers between devices  3.18 us (8%)
  between operations  0.76 us (2%)
    ppermute x6, starting transfers between devices, shift(): return lax.ppermute(x, 'tensor', [(i, (i + k) % n_t) for i in range(n_t)])  11.4 us
    all_gather x1, blocking collectives, per_device(): bundles = lax.all_gather(bundle, 'replica', axis=0)  10.3 us
    pallas_call x14, Pallas kernels, call(): pl.pallas_call(body, out_shape=out_shape, in_specs=in_specs, out_specs=ou...  8.85 us
    ppermute x4, starting transfers between devices, swap(): return lax.ppermute(x, 'replica', [(i, i ^ m) for i in range(n_r)])  3.61 us
    ppermute x4, waiting for transfers between devices, swap(): return lax.ppermute(x, 'replica', [(i, i ^ m) for i in range(n_r)])  2.05 us
    ppermute x6, waiting for transfers between devices, shift(): return lax.ppermute(x, 'tensor', [(i, (i + k) % n_t) for i in range(n_t)])  1.13 us
  transfers between devices with their start and end apart: 10, of which 3 were waited for; matrix products, arithmetic and copies ran while one was open for 0% of the time, Pallas kernels for 15%

profile of v8, /device:TPU:0, one launch (start us, length us, event | category | flops | bytes accessed | tf_op | source)
XLA Modules:
  0.0 38.1 jit_solution(9963277918615409570)
XLA Ops:
  0.6 1.2 %up_grads.1 = (bf16[144,128]{1,0:T(8,128)(2,1)S(1)}, bf16[144,128]{1,0:T(8,128)(2,1)S(1)}, bf16[144,128]{1,0:T(8,128)(2,1)S(1)}, bf16[144,128]{1,0:T(8,128)(2,1)...) custom-call(bf16[64,128]{1,0:T(8,128)(2,1)} %bitcast.15, ...), custom_call_target="tpu_custom_call" | custom-call | bytes 819200 | tf_op jit(solution)/shard_map/up_grads/pallas_call | solution.py:79
  1.8 3.1 %collective-permute-start = (bf16[144,128]{1,0:T(8,128)(2,1)S(1)}, bf16[144,128]{1,0:T(8,128)(2,1)S(1)}, u32[]{:S(2)}, u32[]{:S(2)}) collective-permute-start(bf16[144,128]{1,0:T(8,128)(2,1)S(1)} %get-tuple-element.25), channel_id=1, source_target_pairs={{0,1},{1,2},{2,3},{3,0},{4,5},{5,6},{6,7},{7,4},{8,9},{9,10},{10,1... | collective-permute-start | bytes 110600 | tf_op jit(solution)/shard_map/ppermute | solution.py:329
  4.9 2.6 %collective-permute-start.1 = (bf16[144,128]{1,0:T(8,128)(2,1)S(1)}, bf16[144,128]{1,0:T(8,128)(2,1)S(1)}, u32[]{:S(2)}, u32[]{:S(2)}) collective-permute-start(bf16[144,128]{1,0:T(8,128)(2,1)S(1)} %get-tuple-element.26), channel_id=1, source_target_pairs={{0,2},{1,3},{2,0},{3,1},{4,6},{5,7},{6,4},{7,5},{8,10},{9,11},{10,... | collective-permute-start | bytes 110600 | tf_op jit(solution)/shard_map/ppermute | solution.py:329
  7.5 1.3 %collective-permute-start.2 = (bf16[144,128]{1,0:T(8,128)(2,1)S(1)}, bf16[144,128]{1,0:T(8,128)(2,1)S(1)}, u32[]{:S(2)}, u32[]{:S(2)}) collective-permute-start(bf16[144,128]{1,0:T(8,128)(2,1)S(1)} %get-tuple-element.27), channel_id=1, source_target_pairs={{0,3},{1,0},{2,1},{3,2},{4,7},{5,4},{6,5},{7,6},{8,11},{9,8},{10,9... | collective-permute-start | bytes 110600 | tf_op jit(solution)/shard_map/ppermute | solution.py:329
  8.8 0.0 collective-permute-done.refs_0_.refs_1_
  8.8 0.2 weight_grads.3.after
  9.0 1.1 %collective-permute-done.1.refs_0_.refs_2_ = bf16[144,128]{1,0:T(8,128)(2,1)S(1)} collective-permute-done((bf16[144,128]{1,0:T(8,128)(2,1)S(1)}, bf16[144,128]{1,0:T(8,128)(2,1)S(1)}, u32[]{:S(2)}, u32[]{:S(2)}) %collective-permute-start.1) | collective-permute-done | bytes 36896 | tf_op jit(solution)/shard_map/ppermute | solution.py:329
  10.1 0.2 weight_grads.4.after
  10.3 2.3 %collective-permute-start.5 = (bf16[64,1280]{1,0:T(8,128)(2,1)S(1)}, bf16[64,1280]{1,0:T(8,128)(2,1)S(1)}, u32[]{:S(2)}, u32[]{:S(2)}) collective-permute-start(bf16[64,1280]{1,0:T(8,128)(2,1)S(1)} %weight_grads.4.after), channel_id=1, source_target_pairs={{0,2},{1,3},{2,0},{3,1},{4,6},{5,7},{6,4},{7,5},{8,10},{9,11},{10,... | collective-permute-start | bytes 491528 | tf_op jit(solution)/shard_map/ppermute | solution.py:329
  12.6 1.3 %collective-permute-start.4 = (bf16[64,1280]{1,0:T(8,128)(2,1)S(1)}, bf16[64,1280]{1,0:T(8,128)(2,1)S(1)}, u32[]{:S(2)}, u32[]{:S(2)}) collective-permute-start(bf16[64,1280]{1,0:T(8,128)(2,1)S(1)} %weight_grads.3.after), channel_id=1, source_target_pairs={{0,3},{1,0},{2,1},{3,2},{4,7},{5,4},{6,5},{7,6},{8,11},{9,8},{10,9... | collective-permute-start | bytes 491528 | tf_op jit(solution)/shard_map/ppermute | solution.py:329
  13.9 0.0 collective-permute-done.2.refs_0_.refs_3_
  13.9 0.2 weight_grads.5
  14.2 0.0 copy-start
  14.2 0.8 %collective-permute-start.3 = (bf16[64,1280]{1,0:T(8,128)(2,1)S(1)}, bf16[64,1280]{1,0:T(8,128)(2,1)S(1)}, u32[]{:S(2)}, u32[]{:S(2)}) collective-permute-start(bf16[64,1280]{1,0:T(8,128)(2,1)S(1)} %get-tuple-element.29.after), channel_id=1, source_target_pairs={{0,1},{1,2},{2,3},{3,0},{4,5},{5,6},{6,7},{7,4},{8,9},{9,10},{10,1... | collective-permute-start | bytes 491528 | tf_op jit(solution)/shard_map/ppermute | solution.py:329
  15.0 10.3 %all-gather = bf16[2688,128]{1,0:T(8,128)(2,1)S(1)} all-gather(bf16[336,128]{1,0:T(8,128)(2,1)S(1)} %bundle.1), channel_id=2, replica_groups=mesh['replica'=8,'tensor'=4] {'replica'}, dimensions={0}, use_global_device_ids=true | all-gather | bytes 774144 | tf_op jit(solution)/shard_map/all_gather | solution.py:382
  25.2 1.1 %own_places.1 = (bf16[64,2560]{1,0:T(8,128)(2,1)S(1)}, bf16[1280,128]{1,0:T(8,128)(2,1)S(1)}, f32[2,8,128]{2,1,0:T(8,128)S(1)}, bf16[1024,256]{1,0:T(8,128)(2,1)S(1)}) custom-call(bf16[8,336,128]{2,1,0:T(8,128)(2,1)S(1)} %bitcast.11, s32[8]{0:T(128)} %mask.1, s32[8]{0:T(128)} %tally.1, bf16[1024,256]{1,0:T(8,128)(2,1)} %constant.4.clone.tab, ...), custom_call_target="tpu_custom_call" | custom-call | tf_op jit(solution)/shard_map/own_places/pallas_call | solution.py:79
  26.3 0.0 collective-permute-done.5.refs_2_
  26.3 0.0 collective-permute-done.4.refs_1_
  26.4 0.0 copy-done
  26.4 0.7 %kept_rows.2 = (bf16[8,5120]{1,0:T(8,128)(2,1)S(1)}, f32[8,5120]{1,0:T(8,128)S(1)}) custom-call(f32[64,5120]{1,0:T(8,128)S(1)} %bitcast.8, bf16[1280,128]{1,0:T(8,128)(2,1)S(1)} %get-tuple-element.33.a_ref, bf16[1024,256]{1,0:T(8,128)(2,1)S(1)} %get-tuple-element.34.tab, f32[64,1280]{1,0:T(8,128)S(1)} %get-tuple-element.35.refs_0_, ...), custom_call_target="tpu_custom_call" | custom-call | flops 94371840 | bytes 1474560 | tf_op jit(solution)/shard_map/kept_rows/pallas_call | solution.py:79
  27.1 0.0 collective-permute-done.3.refs_0_.refs_3_
  27.1 0.5 %kept_rows.3 = (bf16[8,5120]{1,0:T(8,128)(2,1)S(1)}, f32[8,5120]{1,0:T(8,128)S(1)}) custom-call(f32[64,5120]{1,0:T(8,128)S(1)} %bitcast.9, bf16[1280,128]{1,0:T(8,128)(2,1)S(1)} %get-tuple-element.33.a_ref, bf16[1024,256]{1,0:T(8,128)(2,1)S(1)} %get-tuple-element.34.tab, ...), custom_call_target="tpu_custom_call", output_to_operand_aliasing={{0}: (4, {}), {1}: (5, {})} | custom-call | flops 31457280 | bytes 491520 | tf_op jit(solution)/shard_map/kept_rows/pallas_call | solution.py:79
  27.6 1.5 %collective-permute-start.8 = (bf16[8,5120]{1,0:T(8,128)(2,1)S(1)}, bf16[8,5120]{1,0:T(8,128)(2,1)S(1)}, u32[]{:S(2)}, u32[]{:S(2)}) collective-permute-start(bf16[8,5120]{1,0:T(8,128)(2,1)S(1)} %get-tuple-element.42.refs_0_), channel_id=1, source_target_pairs={{0,24},{4,28},{8,16},{12,20},{16,8},{20,12},{24,0},{28,4},{1,25},{... | collective-permute-start | bytes 245768 | tf_op jit(solution)/shard_map/ppermute | solution.py:332
  29.1 1.5 %collective-permute-start.7 = (bf16[8,5120]{1,0:T(8,128)(2,1)S(1)}, bf16[8,5120]{1,0:T(8,128)(2,1)S(1)}, u32[]{:S(2)}, u32[]{:S(2)}) collective-permute-start(bf16[8,5120]{1,0:T(8,128)(2,1)S(1)} %get-tuple-element.42.refs_0_), channel_id=1, source_target_pairs={{0,16},{4,20},{8,24},{12,28},{16,0},{20,4},{24,8},{28,12},{1,17},{... | collective-permute-start | bytes 245768 | tf_op jit(solution)/shard_map/ppermute | solution.py:332
  30.6 0.5 %collective-permute-start.6 = (bf16[8,5120]{1,0:T(8,128)(2,1)S(1)}, bf16[8,5120]{1,0:T(8,128)(2,1)S(1)}, u32[]{:S(2)}, u32[]{:S(2)}) collective-permute-start(bf16[8,5120]{1,0:T(8,128)(2,1)S(1)} %get-tuple-element.42.refs_0_), channel_id=1, source_target_pairs={{0,8},{4,12},{8,0},{12,4},{16,24},{20,28},{24,16},{28,20},{1,9},{5... | collective-permute-start | bytes 245768 | tf_op jit(solution)/shard_map/ppermute | solution.py:332
  31.1 0.6 %places.1 = (bf16[64,2560]{1,0:T(8,128)(2,1)S(1)}, bf16[64,2560]{1,0:T(8,128)(2,1)S(1)}, bf16[64,2560]{1,0:T(8,128)(2,1)S(1)}, bf16[64,2560]{1,0:T(8,128)(2,1)S(1)}) custom-call(f32[2,8,128]{2,1,0:T(8,128)S(1)} %get-tuple-element.39.w_ref, bf16[128,128]{1,0:T(8,128)(2,1)S(1)} %get-tuple-element.31.tall, bf16[8,336,128]{2,1,0:T(8,128)(2,1)S(1)} %bitcast.12), custom_call_target="tpu_custom_call" | custom-call | tf_op jit(solution)/shard_map/places/pallas_call | solution.py:79
  31.7 1.1 %input_grads.1.refs_5_ = bf16[128,1280]{1,0:T(8,128)(2,1)} custom-call(bf16[8,336,128]{2,1,0:T(8,128)(2,1)S(1)} %bitcast.13, bf16[144,128]{1,0:T(8,128)(2,1)S(1)} %get-tuple-element.28.refs_1_.refs_0_, bf16[144,128]{1,0:T(8,128)(2,1)S(1)} %collective-permute-done.refs_0_.refs_1_, bf16[144,128]{1,0:T(8,128)(2,1)S(1)} %collective-permute-done.1.refs_0_.refs_2_, ...), custom_call_target="tpu_custom_call" | custom-call | flops 83886080 | bytes 983040 | tf_op jit(solution)/shard_map/input_grads/pallas_call | solution.py:79
  32.8 1.3 %new_momentums.1.refs_4_ = f32[64,5120]{1,0:T(8,128)} custom-call(f32[64,5120]{1,0:T(8,128)S(1)} %bitcast.10, bf16[64,2560]{1,0:T(8,128)(2,1)S(1)} %get-tuple-element.32.p_ref, f32[8,5120]{1,0:T(8,128)S(1)} %get-tuple-element.38.q, f32[64,1280]{1,0:T(8,128)S(1)} %get-tuple-element.35.refs_0_, bf16[64,1280]{1,0:T(8,128)(2,1)S(1)} %collective-permute-done.4.refs_1_, ...), custom_call_target="tpu_custom_call" | custom-call | flops 125829120 | bytes 3276800 | tf_op jit(solution)/shard_map/new_momentums/pallas_call | solution.py:79
  34.1 0.0 collective-permute-done.8.refs_3_
  34.1 0.9 %collective-permute-done.7.refs_2_ = bf16[8,5120]{1,0:T(8,128)(2,1)S(1)} collective-permute-done((bf16[8,5120]{1,0:T(8,128)(2,1)S(1)}, bf16[8,5120]{1,0:T(8,128)(2,1)S(1)}, u32[]{:S(2)}, u32[]{:S(2)}) %collective-permute-start.7) | collective-permute-done | bytes 81952 | tf_op jit(solution)/shard_map/ppermute | solution.py:332
  35.0 0.0 collective-permute-done.6.refs_1_
  35.1 0.1 collective-permute-start.9
  35.1 0.5 %half_updates.1.half_sum = f32[1280,256]{1,0:T(8,128)S(1)} custom-call(bf16[64,2560]{1,0:T(8,128)(2,1)S(1)} %get-tuple-element.40.refs_6_.p_hi, bf16[64,2560]{1,0:T(8,128)(2,1)S(1)} %get-tuple-element.41.p_lo, bf16[4,8,5120]{2,1,0:T(8,128)(2,1)S(1)} %join_kept.1.mine), custom_call_target="tpu_custom_call" | custom-call | tf_op jit(solution)/shard_map/half_updates/pallas_call | solution.py:79
  35.6 1.1 %collective-permute-done.9.other = bf16[4,8,5120]{2,1,0:T(8,128)(2,1)S(1)} collective-permute-done((bf16[4,8,5120]{2,1,0:T(8,128)(2,1)S(1)}, bf16[4,8,5120]{2,1,0:T(8,128)(2,1)S(1)}, u32[]{:S(2)}, u32[]{:S(2)}) %collective-permute-start.9) | collective-permute-done | bytes 327712 | tf_op jit(solution)/shard_map/ppermute | solution.py:332
  36.8 1.3 %updates.1 = f32[64,5120]{1,0:T(8,128)} custom-call(f32[1280,256]{1,0:T(8,128)S(1)} %half_updates.1.half_sum, bf16[64,2560]{1,0:T(8,128)(2,1)S(1)} %get-tuple-element.43.p_hi, bf16[64,2560]{1,0:T(8,128)(2,1)S(1)} %get-tuple-element.44.p_lo, bf16[4,8,5120]{2,1,0:T(8,128)(2,1)S(1)} %collective-permute-done.9.other), custom_call_target="tpu_custom_call" | custom-call | flops 671088640 | bytes 2621440 | tf_op jit(solution)/shard_map/updates/pallas_call | solution.py:79
  (2 shorter events, 0.0 us)
Async XLA Ops:
  1.8 7.0 %collective-permute-start = (bf16[144,128]{1,0:T(8,128)(2,1)S(1)}, bf16[144,128]{1,0:T(8,128)(2,1)S(1)}, u32[]{:S(2)}, u32[]{:S(2)}) collective-permute-start(bf16[144,128]{1,0:T(8,128)(2,1)S(1)} %get-tuple-element.25), channel_id=1, source_target_pairs={{0,1},{1,2},{2,3},{3,0},{4,5},{5,6},{6,7},{7,4},{8,9},{9,10},{10,1... | collective-permute-start | bytes 110600 | tf_op jit(solution)/shard_map/ppermute | solution.py:329
  4.9 5.2 %collective-permute-start.1 = (bf16[144,128]{1,0:T(8,128)(2,1)S(1)}, bf16[144,128]{1,0:T(8,128)(2,1)S(1)}, u32[]{:S(2)}, u32[]{:S(2)}) collective-permute-start(bf16[144,128]{1,0:T(8,128)(2,1)S(1)} %get-tuple-element.26), channel_id=1, source_target_pairs={{0,2},{1,3},{2,0},{3,1},{4,6},{5,7},{6,4},{7,5},{8,10},{9,11},{10,... | collective-permute-start | bytes 110600 | tf_op jit(solution)/shard_map/ppermute | solution.py:329
  7.5 6.5 %collective-permute-start.2 = (bf16[144,128]{1,0:T(8,128)(2,1)S(1)}, bf16[144,128]{1,0:T(8,128)(2,1)S(1)}, u32[]{:S(2)}, u32[]{:S(2)}) collective-permute-start(bf16[144,128]{1,0:T(8,128)(2,1)S(1)} %get-tuple-element.27), channel_id=1, source_target_pairs={{0,3},{1,0},{2,1},{3,2},{4,7},{5,4},{6,5},{7,6},{8,11},{9,8},{10,9... | collective-permute-start | bytes 110600 | tf_op jit(solution)/shard_map/ppermute | solution.py:329
  10.3 16.0 %collective-permute-start.5 = (bf16[64,1280]{1,0:T(8,128)(2,1)S(1)}, bf16[64,1280]{1,0:T(8,128)(2,1)S(1)}, u32[]{:S(2)}, u32[]{:S(2)}) collective-permute-start(bf16[64,1280]{1,0:T(8,128)(2,1)S(1)} %weight_grads.4.after), channel_id=1, source_target_pairs={{0,2},{1,3},{2,0},{3,1},{4,6},{5,7},{6,4},{7,5},{8,10},{9,11},{10,... | collective-permute-start | bytes 491528 | tf_op jit(solution)/shard_map/ppermute | solution.py:329
  12.6 13.7 %collective-permute-start.4 = (bf16[64,1280]{1,0:T(8,128)(2,1)S(1)}, bf16[64,1280]{1,0:T(8,128)(2,1)S(1)}, u32[]{:S(2)}, u32[]{:S(2)}) collective-permute-start(bf16[64,1280]{1,0:T(8,128)(2,1)S(1)} %weight_grads.3.after), channel_id=1, source_target_pairs={{0,3},{1,0},{2,1},{3,2},{4,7},{5,4},{6,5},{7,6},{8,11},{9,8},{10,9... | collective-permute-start | bytes 491528 | tf_op jit(solution)/shard_map/ppermute | solution.py:329
  14.2 12.2 %copy-start = (f32[1,64,5120]{2,1,0:T(8,128)S(1)}, f32[1,64,5120]{2,1,0:T(8,128)}, u32[]{:S(2)}) copy-start(f32[1,64,5120]{2,1,0:T(8,128)} %param.14) | copy-start | bytes 3932164
  14.2 12.9 %collective-permute-start.3 = (bf16[64,1280]{1,0:T(8,128)(2,1)S(1)}, bf16[64,1280]{1,0:T(8,128)(2,1)S(1)}, u32[]{:S(2)}, u32[]{:S(2)}) collective-permute-start(bf16[64,1280]{1,0:T(8,128)(2,1)S(1)} %get-tuple-element.29.after), channel_id=1, source_target_pairs={{0,1},{1,2},{2,3},{3,0},{4,5},{5,6},{6,7},{7,4},{8,9},{9,10},{10,1... | collective-permute-start | bytes 491528 | tf_op jit(solution)/shard_map/ppermute | solution.py:329
  27.6 6.5 %collective-permute-start.8 = (bf16[8,5120]{1,0:T(8,128)(2,1)S(1)}, bf16[8,5120]{1,0:T(8,128)(2,1)S(1)}, u32[]{:S(2)}, u32[]{:S(2)}) collective-permute-start(bf16[8,5120]{1,0:T(8,128)(2,1)S(1)} %get-tuple-element.42.refs_0_), channel_id=1, source_target_pairs={{0,24},{4,28},{8,16},{12,20},{16,8},{20,12},{24,0},{28,4},{1,25},{... | collective-permute-start | bytes 245768 | tf_op jit(solution)/shard_map/ppermute | solution.py:332
  29.1 5.9 %collective-permute-start.7 = (bf16[8,5120]{1,0:T(8,128)(2,1)S(1)}, bf16[8,5120]{1,0:T(8,128)(2,1)S(1)}, u32[]{:S(2)}, u32[]{:S(2)}) collective-permute-start(bf16[8,5120]{1,0:T(8,128)(2,1)S(1)} %get-tuple-element.42.refs_0_), channel_id=1, source_target_pairs={{0,16},{4,20},{8,24},{12,28},{16,0},{20,4},{24,8},{28,12},{1,17},{... | collective-permute-start | bytes 245768 | tf_op jit(solution)/shard_map/ppermute | solution.py:332
  30.6 4.4 %collective-permute-start.6 = (bf16[8,5120]{1,0:T(8,128)(2,1)S(1)}, bf16[8,5120]{1,0:T(8,128)(2,1)S(1)}, u32[]{:S(2)}, u32[]{:S(2)}) collective-permute-start(bf16[8,5120]{1,0:T(8,128)(2,1)S(1)} %get-tuple-element.42.refs_0_), channel_id=1, source_target_pairs={{0,8},{4,12},{8,0},{12,4},{16,24},{20,28},{24,16},{28,20},{1,9},{5... | collective-permute-start | bytes 245768 | tf_op jit(solution)/shard_map/ppermute | solution.py:332
  35.1 1.7 %collective-permute-start.9 = (bf16[4,8,5120]{2,1,0:T(8,128)(2,1)S(1)}, bf16[4,8,5120]{2,1,0:T(8,128)(2,1)S(1)}, u32[]{:S(2)}, u32[]{:S(2)}) collective-permute-start(bf16[4,8,5120]{2,1,0:T(8,128)(2,1)S(1)} %join_kept.1.mine), channel_id=1, source_target_pairs={{0,4},{4,0},{8,12},{12,8},{16,20},{20,16},{24,28},{28,24},{1,5},{5... | collective-permute-start | bytes 983048 | tf_op jit(solution)/shard_map/ppermute | solution.py:332

commit v9 on v8

--- a/solution.py
+++ b/solution.py
@@ -150,7 +150,7 @@
         refs[-1][i] = ref[...]
 
 
-def own_body(n_r, keep, after, mask, tally, tab, lines, tall, p_ref, a_ref, w_ref, tab_ref, mask_s, tally_s, sems):
+def own_body(n_r, keep, mask, tally, tab, lines, tall, p_ref, a_ref, w_ref, tab_ref, mask_s, tally_s, sems):
     copies = [
         pltpu.make_async_copy(src, dst, sems.at[i])
         for i, (src, dst) in enumerate([(mask, mask_s), (tally, tally_s), (tab, tab_ref)])
@@ -246,26 +246,22 @@
         copy.wait()
 
 
-def places_body(keep, w_ref, tall, bundles, *p_refs):
-    n_r, last = bundles.shape[0], bundles.shape[1] - 16
-    half, nb = n_r // 2, G // B
-    rep = lax.axis_index("replica")
+def places_body(keep, h, w_ref, tall, bundles, hi_ref, lo_ref):
+    half, last, nb = bundles.shape[0], bundles.shape[1] - 16, G // B
     freq = lax.broadcasted_iota(jnp.int32, (B, 2 * B), 0).astype(F32)
     block = lax.broadcasted_iota(jnp.int32, (1, 2 * B), 1) // (half * keep)
-    for h in range(2):
-        hi_ref, lo_ref = p_refs[2 * h : 2 * h + 2]
-        w = w_ref[h, :1, :]
-        rows = [bundles[rep ^ (2 * i + h), last:, :].astype(F32)[:keep] for i in range(half)]
-        rows = jnp.concatenate(rows * nb, axis=0).T
-        for g in range(hi_ref.shape[1] // (2 * B)):
-            num = rows[g * nb : g * nb + 1]
-            for j in range(1, nb):
-                num = jnp.where(block == j, rows[g * nb + j : g * nb + j + 1], num)
-            hot = jnp.where(freq == num, 1.0, 0.0).astype(BF16)
-            y = dot(tall[:, :B], hot)
-            hi, lo = split((y[:B] + y[B:]) * w)
-            hi_ref[:, g * 2 * B : (g + 1) * 2 * B] = hi
-            lo_ref[:, g * 2 * B : (g + 1) * 2 * B] = lo
+    w = w_ref[h, :1, :]
+    rows = [bundles[i, last:, :].astype(F32)[:keep] for i in range(half)]
+    rows = jnp.concatenate(rows * nb, axis=0).T
+    for g in range(hi_ref.shape[1] // (2 * B)):
+        num = rows[g * nb : g * nb + 1]
+        for j in range(1, nb):
+            num = jnp.where(block == j, rows[g * nb + j : g * nb + j + 1], num)
+        hot = jnp.where(freq == num, 1.0, 0.0).astype(BF16)
+        y = dot(tall[:, :B], hot)
+        hi, lo = split((y[:B] + y[B:]) * w)
+        hi_ref[:, g * 2 * B : (g + 1) * 2 * B] = hi
+        lo_ref[:, g * 2 * B : (g + 1) * 2 * B] = lo
 
 
 def spread_rows(p_hi, p_lo, ships, g):
@@ -298,17 +294,20 @@
         copy.wait()
 
 
-def input_grad_body(n_t, n_r, cp, bundles, *refs):
+def input_grad_body(n_t, n_r, cp, mine, other, *refs):
     ups, out, held = refs[:n_t], refs[n_t], refs[n_t + 1]
     nc = out.shape[1] // cp
     nr = B // (n_r // cp)
     tiles = nc // 128
-    for r in range(n_r):
-        r0, c0 = (r // cp) * nr, (r % cp) * nc
+    for m in range(n_r):
+        src = lax.axis_index("replica") ^ m
+        r0, c0 = (src // cp) * nr, lax.rem(src, cp) * nc
+        ref = (mine, other)[m % 2]
         for k in range(n_t):
+            row = pl.multiple_of(k * B + r0, nr)
             for j in range(tiles):
                 at = (k * tiles + j) * nr
-                held[k * B + r0 : k * B + r0 + nr, c0 + j * 128 : c0 + (j + 1) * 128] = bundles[r, at : at + nr, :]
+                held[pl.ds(row, nr), pl.ds(pl.multiple_of(c0 + j * 128, 128), 128)] = ref[m // 2, at : at + nr, :]
     up = jnp.concatenate([u[:B, :] for u in ups], axis=0).T
     for c in range(0, out.shape[1], G):
         out[:, c : c + G] = dot(up, held[:, c : c + G]).astype(BF16)
@@ -330,6 +329,17 @@
 
     def swap(x, m):
         return lax.ppermute(x, "replica", [(i, i ^ m) for i in range(n_r)])
+
+    def share(x, name, after=()):
+        mine = call(
+            functools.partial(join_body, half),
+            near((half,) + x.shape),
+            (x, *[swap(x, 2 * i) for i in range(1, half)], *after),
+            [VM] * half + [ANY] * len(after),
+            VM,
+            name=name,
+        )
+        return mine, swap(mine, 1)
 
     own = lines[0, 0].T
     tiles = cols // cp // 128
@@ -379,7 +389,7 @@
         VM,
         name="bundle",
     )
-    bundles = lax.all_gather(bundle, "replica", axis=0)
+    bundles = share(bundle, "join_bundles")
 
     p_own, a_own, shares, tab = call(
         functools.partial(own_body, n_r, keep),
@@ -389,25 +399,28 @@
             near((2, 8, 2 * B), F32),
             near(tab.shape),
         ],
-        (bundles, far(mask), far(tally), far(tab), own, tall),
-        [ANY, ANY, ANY, ANY, VM, VM],
+        (far(mask), far(tally), far(tab), own, tall),
+        [ANY, ANY, ANY, VM, VM],
         [VM] * 4,
         scratch=[pltpu.SMEM((n_r,), jnp.int32)] * 2 + [pltpu.SemaphoreType.DMA((3,))],
         name="own_places",
     )
-    places = call(
-        functools.partial(places_body, keep),
-        [near((B, blocks * half * keep))] * 4,
-        (shares, tall, bundles),
-        [VM] * 3,
-        [VM] * 4,
-        name="places",
-    )
+    places = [
+        call(
+            functools.partial(places_body, keep, h),
+            [near((B, blocks * half * keep))] * 2,
+            (shares, tall, bundles[h]),
+            [VM] * 3,
+            [VM] * 2,
+            name="places",
+        )
+        for h in range(2)
+    ]
     input_grad = call(
         functools.partial(input_grad_body, n_t, n_r, cp),
         jax.ShapeDtypeStruct((tok, cols), BF16),
-        (bundles, *parts),
-        [VM] * (1 + n_t),
+        (*bundles, *parts),
+        [VM] * (2 + n_t),
         VM,
         scratch=[pltpu.VMEM((n_t * B, cols), BF16)],
         flops=2 * tok * n_t * B * cols,
@@ -429,7 +442,6 @@
             alias={3 + len(ks): 0, 4 + len(ks): 1} if rows else {},
         )
     ship, q_own = rows
-    ships = [ship] + [swap(ship, 2 * i) for i in range(1, half)]
     new = call(
         functools.partial(return_body, n_t, keep),
         jax.ShapeDtypeStruct((B, width), F32),
@@ -441,19 +453,11 @@
         nbytes=B * width * 10,
         name="new_momentums",
     )
-    mine = call(
-        functools.partial(join_body, half),
-        near((half, keep, width)),
-        (*ships, far(new), far(input_grad), places[0]),
-        [VM] * half + [ANY] * 3,
-        VM,
-        name="join_kept",
-    )
-    other = swap(mine, 1)
+    mine, other = share(ship, "join_kept", (far(new),))
     half_sum = call(
         half_update_body,
         near((groups * B, G), F32),
-        (*places[:2], mine),
+        (*places[0], mine),
         [VM] * 3,
         VM,
         name="half_updates",
@@ -462,7 +466,7 @@
     update = call(
         functools.partial(update_body, chunk),
         jax.ShapeDtypeStruct((B, width), F32),
-        (half_sum, *places[2:], other),
+        (half_sum, *places[1], other),
         [VM] * 4,
         ANY,
         scratch=[

time: 38.3 us -> 38.2 us (level)
  blocking collectives: 10.3 us -> 0 us
  waiting for transfers between devices: 3.18 us -> 8.23 us
  starting transfers between devices: 15 us -> 19.7 us
    all_gather x1 -> x0, blocking collectives: 10.3 us -> none  [per_device(): bundles = lax.all_gather(bundle, 'replica', axis=0)]
    ppermute x6, waiting for transfers between devices: 1.13 us -> 6.82 us  [shift(): return lax.ppermute(x, 'tensor', [(i, (i + k) % n_t) for i in range(n_t)])]
    ppermute x4 -> x8, starting transfers between devices: 3.61 us -> 8.31 us  [swap(): return lax.ppermute(x, 'replica', [(i, i ^ m) for i in range(n_r)])]
    ppermute x4 -> x8, waiting for transfers between devices: 2.05 us -> 1.41 us  [swap(): return lax.ppermute(x, 'replica', [(i, i ^ m) for i in range(n_r)])]
    pallas_call x14 -> x16, Pallas kernels: 8.85 us -> 9.22 us  [call(): pl.pallas_call(body, out_shape=out_shape, in_specs=in_specs, out_specs=ou...]
  transfers between devices with their start and end apart: 10 -> 14, of which waited for: 3 -> 5; matrix products, arithmetic and copies ran while one was open for 0% -> 0% of each run, Pallas kernels for 15% -> 18%
where the time goes in v9:
time: 38.2 us; the launch traced here: 37.9 us
  starting transfers between devices  19.7 us (52%)
  Pallas kernels  9.22 us (24%)
  waiting for transfers between devices  8.23 us (22%)
  between operations  0.77 us (2%)
    ppermute x6, starting transfers between devices, shift(): return lax.ppermute(x, 'tensor', [(i, (i + k) % n_t) for i in range(n_t)])  11.4 us
    pallas_call x16, Pallas kernels, call(): pl.pallas_call(body, out_shape=out_shape, in_specs=in_specs, out_specs=ou...  9.22 us
    ppermute x8, starting transfers between devices, swap(): return lax.ppermute(x, 'replica', [(i, i ^ m) for i in range(n_r)])  8.31 us
    ppermute x6, waiting for transfers between devices, shift(): return lax.ppermute(x, 'tensor', [(i, (i + k) % n_t) for i in range(n_t)])  6.82 us
    ppermute x8, waiting for transfers between devices, swap(): return lax.ppermute(x, 'replica', [(i, i ^ m) for i in range(n_r)])  1.41 us
  transfers between devices with their start and end apart: 14, of which 5 were waited for; matrix products, arithmetic and copies ran while one was open for 0% of the time, Pallas kernels for 18%

profile of v9, /device:TPU:0, one launch (start us, length us, event | category | flops | bytes accessed | tf_op | source)
XLA Modules:
  0.0 37.9 jit_solution(1964708735046066490)
XLA Ops:
  0.6 1.2 %up_grads.1 = (bf16[144,128]{1,0:T(8,128)(2,1)S(1)}, bf16[144,128]{1,0:T(8,128)(2,1)S(1)}, bf16[144,128]{1,0:T(8,128)(2,1)S(1)}, bf16[144,128]{1,0:T(8,128)(2,1)...) custom-call(bf16[64,128]{1,0:T(8,128)(2,1)} %bitcast.11, ...), custom_call_target="tpu_custom_call" | custom-call | bytes 819200 | tf_op jit(solution)/shard_map/up_grads/pallas_call | solution.py:79
  1.8 3.1 %collective-permute-start = (bf16[144,128]{1,0:T(8,128)(2,1)S(1)}, bf16[144,128]{1,0:T(8,128)(2,1)S(1)}, u32[]{:S(2)}, u32[]{:S(2)}) collective-permute-start(bf16[144,128]{1,0:T(8,128)(2,1)S(1)} %get-tuple-element.25), channel_id=1, source_target_pairs={{0,1},{1,2},{2,3},{3,0},{4,5},{5,6},{6,7},{7,4},{8,9},{9,10},{10,1... | collective-permute-start | bytes 110600 | tf_op jit(solution)/shard_map/ppermute | solution.py:328
  4.9 2.6 %collective-permute-start.1 = (bf16[144,128]{1,0:T(8,128)(2,1)S(1)}, bf16[144,128]{1,0:T(8,128)(2,1)S(1)}, u32[]{:S(2)}, u32[]{:S(2)}) collective-permute-start(bf16[144,128]{1,0:T(8,128)(2,1)S(1)} %get-tuple-element.26), channel_id=1, source_target_pairs={{0,2},{1,3},{2,0},{3,1},{4,6},{5,7},{6,4},{7,5},{8,10},{9,11},{10,... | collective-permute-start | bytes 110600 | tf_op jit(solution)/shard_map/ppermute | solution.py:328
  7.5 1.3 %collective-permute-start.2 = (bf16[144,128]{1,0:T(8,128)(2,1)S(1)}, bf16[144,128]{1,0:T(8,128)(2,1)S(1)}, u32[]{:S(2)}, u32[]{:S(2)}) collective-permute-start(bf16[144,128]{1,0:T(8,128)(2,1)S(1)} %get-tuple-element.27), channel_id=1, source_target_pairs={{0,3},{1,0},{2,1},{3,2},{4,7},{5,4},{6,5},{7,6},{8,11},{9,8},{10,9... | collective-permute-start | bytes 110600 | tf_op jit(solution)/shard_map/ppermute | solution.py:328
  8.8 0.0 collective-permute-done.refs_0_.refs_1_
  8.8 0.2 weight_grads.3.after
  9.0 0.0 copy-start
  9.0 1.1 %collective-permute-done.1.refs_0_.refs_2_ = bf16[144,128]{1,0:T(8,128)(2,1)S(1)} collective-permute-done((bf16[144,128]{1,0:T(8,128)(2,1)S(1)}, bf16[144,128]{1,0:T(8,128)(2,1)S(1)}, u32[]{:S(2)}, u32[]{:S(2)}) %collective-permute-start.1) | collective-permute-done | bytes 36896 | tf_op jit(solution)/shard_map/ppermute | solution.py:328
  10.1 0.2 weight_grads.4.after
  10.3 2.3 %collective-permute-start.9 = (bf16[64,1280]{1,0:T(8,128)(2,1)S(1)}, bf16[64,1280]{1,0:T(8,128)(2,1)S(1)}, u32[]{:S(2)}, u32[]{:S(2)}) collective-permute-start(bf16[64,1280]{1,0:T(8,128)(2,1)S(1)} %weight_grads.4.after), channel_id=1, source_target_pairs={{0,2},{1,3},{2,0},{3,1},{4,6},{5,7},{6,4},{7,5},{8,10},{9,11},{10,... | collective-permute-start | bytes 491528 | tf_op jit(solution)/shard_map/ppermute | solution.py:328
  12.6 1.3 %collective-permute-start.8 = (bf16[64,1280]{1,0:T(8,128)(2,1)S(1)}, bf16[64,1280]{1,0:T(8,128)(2,1)S(1)}, u32[]{:S(2)}, u32[]{:S(2)}) collective-permute-start(bf16[64,1280]{1,0:T(8,128)(2,1)S(1)} %weight_grads.3.after), channel_id=1, source_target_pairs={{0,3},{1,0},{2,1},{3,2},{4,7},{5,4},{6,5},{7,6},{8,11},{9,8},{10,9... | collective-permute-start | bytes 491528 | tf_op jit(solution)/shard_map/ppermute | solution.py:328
  13.9 0.0 collective-permute-done.2.refs_0_.refs_3_
  13.9 0.2 weight_grads.5
  14.2 0.8 %collective-permute-start.7 = (bf16[64,1280]{1,0:T(8,128)(2,1)S(1)}, bf16[64,1280]{1,0:T(8,128)(2,1)S(1)}, u32[]{:S(2)}, u32[]{:S(2)}) collective-permute-start(bf16[64,1280]{1,0:T(8,128)(2,1)S(1)} %get-tuple-element.29.after), channel_id=1, source_target_pairs={{0,1},{1,2},{2,3},{3,0},{4,5},{5,6},{6,7},{7,4},{8,9},{9,10},{10,1... | collective-permute-start | bytes 491528 | tf_op jit(solution)/shard_map/ppermute | solution.py:328
  14.9 2.5 %collective-permute-start.5 = (bf16[336,128]{1,0:T(8,128)(2,1)S(1)}, bf16[336,128]{1,0:T(8,128)(2,1)S(1)}, u32[]{:S(2)}, u32[]{:S(2)}) collective-permute-start(bf16[336,128]{1,0:T(8,128)(2,1)S(1)} %bundle.1.refs_0_), channel_id=1, source_target_pairs={{0,24},{4,28},{8,16},{12,20},{16,8},{20,12},{24,0},{28,4},{1,25},{... | collective-permute-start | bytes 258056 | tf_op jit(solution)/shard_map/ppermute | solution.py:331
  17.5 0.5 %collective-permute-start.4 = (bf16[336,128]{1,0:T(8,128)(2,1)S(1)}, bf16[336,128]{1,0:T(8,128)(2,1)S(1)}, u32[]{:S(2)}, u32[]{:S(2)}) collective-permute-start(bf16[336,128]{1,0:T(8,128)(2,1)S(1)} %bundle.1.refs_0_), channel_id=1, source_target_pairs={{0,16},{4,20},{8,24},{12,28},{16,0},{20,4},{24,8},{28,12},{1,17},{... | collective-permute-start | bytes 258056 | tf_op jit(solution)/shard_map/ppermute | solution.py:331
  18.0 5.7 %collective-permute-done.9.refs_2_ = bf16[64,1280]{1,0:T(8,128)(2,1)S(1)} collective-permute-done((bf16[64,1280]{1,0:T(8,128)(2,1)S(1)}, bf16[64,1280]{1,0:T(8,128)(2,1)S(1)}, u32[]{:S(2)}, u32[]{:S(2)}) %collective-permute-start.9) | collective-permute-done | bytes 163872 | tf_op jit(solution)/shard_map/ppermute | solution.py:328
  23.7 1.6 %collective-permute-start.3 = (bf16[336,128]{1,0:T(8,128)(2,1)S(1)}, bf16[336,128]{1,0:T(8,128)(2,1)S(1)}, u32[]{:S(2)}, u32[]{:S(2)}) collective-permute-start(bf16[336,128]{1,0:T(8,128)(2,1)S(1)} %bundle.1.refs_0_), channel_id=1, source_target_pairs={{0,8},{4,12},{8,0},{12,4},{16,24},{20,28},{24,16},{28,20},{1,9},{5... | collective-permute-start | bytes 258056 | tf_op jit(solution)/shard_map/ppermute | solution.py:331
  25.3 1.1 %own_places.1 = (bf16[64,2560]{1,0:T(8,128)(2,1)S(1)}, bf16[1280,128]{1,0:T(8,128)(2,1)S(1)}, f32[2,8,128]{2,1,0:T(8,128)S(1)}, bf16[1024,256]{1,0:T(8,128)(2,1)S(1)}) custom-call(s32[8]{0:T(128)} %mask.1, s32[8]{0:T(128)} %tally.1, bf16[1024,256]{1,0:T(8,128)(2,1)} %constant.4.clone.tab, s32[8,80]{1,0:T(8,128)S(1)} %get-tuple-element.30.lines, ...), custom_call_target="tpu_custom_call" | custom-call | tf_op jit(solution)/shard_map/own_places/pallas_call | solution.py:79
  26.4 0.0 collective-permute-done.8.refs_1_
  26.4 0.0 copy-done
  26.4 0.7 %kept_rows.2 = (bf16[8,5120]{1,0:T(8,128)(2,1)S(1)}, f32[8,5120]{1,0:T(8,128)S(1)}) custom-call(f32[64,5120]{1,0:T(8,128)S(1)} %bitcast.7, bf16[1280,128]{1,0:T(8,128)(2,1)S(1)} %get-tuple-element.33.a_ref, bf16[1024,256]{1,0:T(8,128)(2,1)S(1)} %get-tuple-element.34.tab, f32[64,1280]{1,0:T(8,128)S(1)} %get-tuple-element.35.refs_0_, ...), custom_call_target="tpu_custom_call" | custom-call | flops 94371840 | bytes 1474560 | tf_op jit(solution)/shard_map/kept_rows/pallas_call | solution.py:79
  27.1 0.0 collective-permute-done.7.refs_0_.refs_3_
  27.1 0.5 %kept_rows.3 = (bf16[8,5120]{1,0:T(8,128)(2,1)S(1)}, f32[8,5120]{1,0:T(8,128)S(1)}) custom-call(f32[64,5120]{1,0:T(8,128)S(1)} %bitcast.8, bf16[1280,128]{1,0:T(8,128)(2,1)S(1)} %get-tuple-element.33.a_ref, bf16[1024,256]{1,0:T(8,128)(2,1)S(1)} %get-tuple-element.34.tab, ...), custom_call_target="tpu_custom_call", output_to_operand_aliasing={{0}: (4, {}), {1}: (5, {})} | custom-call | flops 31457280 | bytes 491520 | tf_op jit(solution)/shard_map/kept_rows/pallas_call | solution.py:79
  27.6 1.5 %collective-permute-start.12 = (bf16[8,5120]{1,0:T(8,128)(2,1)S(1)}, bf16[8,5120]{1,0:T(8,128)(2,1)S(1)}, u32[]{:S(2)}, u32[]{:S(2)}) collective-permute-start(bf16[8,5120]{1,0:T(8,128)(2,1)S(1)} %get-tuple-element.42.refs_0_), channel_id=1, source_target_pairs={{0,24},{4,28},{8,16},{12,20},{16,8},{20,12},{24,0},{28,4},{1,25},{... | collective-permute-start | bytes 245768 | tf_op jit(solution)/shard_map/ppermute | solution.py:331
  29.2 0.4 %collective-permute-start.11 = (bf16[8,5120]{1,0:T(8,128)(2,1)S(1)}, bf16[8,5120]{1,0:T(8,128)(2,1)S(1)}, u32[]{:S(2)}, u32[]{:S(2)}) collective-permute-start(bf16[8,5120]{1,0:T(8,128)(2,1)S(1)} %get-tuple-element.42.refs_0_), channel_id=1, source_target_pairs={{0,16},{4,20},{8,24},{12,28},{16,0},{20,4},{24,8},{28,12},{1,17},{... | collective-permute-start | bytes 245768 | tf_op jit(solution)/shard_map/ppermute | solution.py:331
  29.5 0.0 collective-permute-done.5.refs_3_
  29.6 1.6 %collective-permute-start.10 = (bf16[8,5120]{1,0:T(8,128)(2,1)S(1)}, bf16[8,5120]{1,0:T(8,128)(2,1)S(1)}, u32[]{:S(2)}, u32[]{:S(2)}) collective-permute-start(bf16[8,5120]{1,0:T(8,128)(2,1)S(1)} %get-tuple-element.42.refs_0_), channel_id=1, source_target_pairs={{0,8},{4,12},{8,0},{12,4},{16,24},{20,28},{24,16},{28,20},{1,9},{5... | collective-permute-start | bytes 245768 | tf_op jit(solution)/shard_map/ppermute | solution.py:331
  31.2 0.0 collective-permute-done.4.refs_2_
  31.2 0.0 collective-permute-done.3.refs_1_
  31.2 0.1 collective-permute-start.6
  31.3 1.3 %new_momentums.1.refs_4_ = f32[64,5120]{1,0:T(8,128)} custom-call(f32[64,5120]{1,0:T(8,128)S(1)} %bitcast.9, bf16[64,2560]{1,0:T(8,128)(2,1)S(1)} %get-tuple-element.32.p_ref, f32[8,5120]{1,0:T(8,128)S(1)} %get-tuple-element.38.q, f32[64,1280]{1,0:T(8,128)S(1)} %get-tuple-element.35.refs_0_, bf16[64,1280]{1,0:T(8,128)(2,1)S(1)} %collective-permute-done.8.refs_1_, ...), custom_call_target="tpu_custom_call" | custom-call | flops 125829120 | bytes 3276800 | tf_op jit(solution)/shard_map/new_momentums/pallas_call | solution.py:79
  32.6 0.4 %collective-permute-done.12.refs_3_ = bf16[8,5120]{1,0:T(8,128)(2,1)S(1)} collective-permute-done((bf16[8,5120]{1,0:T(8,128)(2,1)S(1)}, bf16[8,5120]{1,0:T(8,128)(2,1)S(1)}, u32[]{:S(2)}, u32[]{:S(2)}) %collective-permute-start.12) | collective-permute-done | bytes 81952 | tf_op jit(solution)/shard_map/ppermute | solution.py:331
  33.0 0.8 %collective-permute-done.11.refs_2_ = bf16[8,5120]{1,0:T(8,128)(2,1)S(1)} collective-permute-done((bf16[8,5120]{1,0:T(8,128)(2,1)S(1)}, bf16[8,5120]{1,0:T(8,128)(2,1)S(1)}, u32[]{:S(2)}, u32[]{:S(2)}) %collective-permute-start.11) | collective-permute-done | bytes 81952 | tf_op jit(solution)/shard_map/ppermute | solution.py:331
  33.9 0.1 collective-permute-done.10.refs_1_
  34.0 0.1 collective-permute-start.13
  34.1 0.4 %places.2 = (bf16[64,2560]{1,0:T(8,128)(2,1)S(1)}, bf16[64,2560]{1,0:T(8,128)(2,1)S(1)}) custom-call(f32[2,8,128]{2,1,0:T(8,128)S(1)} %get-tuple-element.39.w_ref, bf16[128,128]{1,0:T(8,128)(2,1)S(1)} %get-tuple-element.31.tall, bf16[4,336,128]{2,1,0:T(8,128)(2,1)S(1)} %join_bundles.1.mine.bundles), custom_call_target="tpu_custom_call" | custom-call | tf_op jit(solution)/shard_map/places/pallas_call | solution.py:79
  34.5 0.5 %half_updates.1.half_sum = f32[1280,256]{1,0:T(8,128)S(1)} custom-call(bf16[64,2560]{1,0:T(8,128)(2,1)S(1)} %get-tuple-element.40.p_hi, bf16[64,2560]{1,0:T(8,128)(2,1)S(1)} %get-tuple-element.41.p_lo, bf16[4,8,5120]{2,1,0:T(8,128)(2,1)S(1)} %join_kept.1.mine), custom_call_target="tpu_custom_call" | custom-call | tf_op jit(solution)/shard_map/half_updates/pallas_call | solution.py:79
  35.0 0.0 collective-permute-done.6.other.bundles
  35.0 0.4 %places.3 = (bf16[64,2560]{1,0:T(8,128)(2,1)S(1)}, bf16[64,2560]{1,0:T(8,128)(2,1)S(1)}) custom-call(f32[2,8,128]{2,1,0:T(8,128)S(1)} %get-tuple-element.39.w_ref, bf16[128,128]{1,0:T(8,128)(2,1)S(1)} %get-tuple-element.31.tall, bf16[4,336,128]{2,1,0:T(8,128)(2,1)S(1)} %collective-permute-done.6.other.bundles), custom_call_target="tpu_custom_call" | custom-call | tf_op jit(solution)/shard_map/places/pallas_call | solution.py:79
  35.4 1.2 %input_grads.1 = bf16[128,1280]{1,0:T(8,128)(2,1)} custom-call(bf16[4,336,128]{2,1,0:T(8,128)(2,1)S(1)} %join_bundles.1.mine.bundles, bf16[4,336,128]{2,1,0:T(8,128)(2,1)S(1)} %collective-permute-done.6.other.bundles, bf16[144,128]{1,0:T(8,128)(2,1)S(1)} %get-tuple-element.28.refs_1_.refs_0_, bf16[144,128]{1,0:T(8,128)(2,1)S(1)} %collective-permute-done.refs_0_.refs_1_, ...), custom_call_target="tpu_custom_call" | custom-call | flops 83886080 | bytes 983040 | tf_op jit(solution)/shard_map/input_grads/pallas_call | solution.py:79
  36.6 0.0 collective-permute-done.13.other
  36.6 1.3 %updates.1 = f32[64,5120]{1,0:T(8,128)} custom-call(f32[1280,256]{1,0:T(8,128)S(1)} %half_updates.1.half_sum, bf16[64,2560]{1,0:T(8,128)(2,1)S(1)} %get-tuple-element.43.p_hi, bf16[64,2560]{1,0:T(8,128)(2,1)S(1)} %get-tuple-element.44.p_lo, bf16[4,8,5120]{2,1,0:T(8,128)(2,1)S(1)} %collective-permute-done.13.other), custom_call_target="tpu_custom_call" | custom-call | flops 671088640 | bytes 2621440 | tf_op jit(solution)/shard_map/updates/pallas_call | solution.py:79
  (3 shorter events, 0.1 us)
Async XLA Ops:
  1.8 7.0 %collective-permute-start = (bf16[144,128]{1,0:T(8,128)(2,1)S(1)}, bf16[144,128]{1,0:T(8,128)(2,1)S(1)}, u32[]{:S(2)}, u32[]{:S(2)}) collective-permute-start(bf16[144,128]{1,0:T(8,128)(2,1)S(1)} %get-tuple-element.25), channel_id=1, source_target_pairs={{0,1},{1,2},{2,3},{3,0},{4,5},{5,6},{6,7},{7,4},{8,9},{9,10},{10,1... | collective-permute-start | bytes 110600 | tf_op jit(solution)/shard_map/ppermute | solution.py:328
  4.9 5.2 %collective-permute-start.1 = (bf16[144,128]{1,0:T(8,128)(2,1)S(1)}, bf16[144,128]{1,0:T(8,128)(2,1)S(1)}, u32[]{:S(2)}, u32[]{:S(2)}) collective-permute-start(bf16[144,128]{1,0:T(8,128)(2,1)S(1)} %get-tuple-element.26), channel_id=1, source_target_pairs={{0,2},{1,3},{2,0},{3,1},{4,6},{5,7},{6,4},{7,5},{8,10},{9,11},{10,... | collective-permute-start | bytes 110600 | tf_op jit(solution)/shard_map/ppermute | solution.py:328
  7.5 6.5 %collective-permute-start.2 = (bf16[144,128]{1,0:T(8,128)(2,1)S(1)}, bf16[144,128]{1,0:T(8,128)(2,1)S(1)}, u32[]{:S(2)}, u32[]{:S(2)}) collective-permute-start(bf16[144,128]{1,0:T(8,128)(2,1)S(1)} %get-tuple-element.27), channel_id=1, source_target_pairs={{0,3},{1,0},{2,1},{3,2},{4,7},{5,4},{6,5},{7,6},{8,11},{9,8},{10,9... | collective-permute-start | bytes 110600 | tf_op jit(solution)/shard_map/ppermute | solution.py:328
  9.0 17.4 %copy-start = (f32[1,64,5120]{2,1,0:T(8,128)S(1)}, f32[1,64,5120]{2,1,0:T(8,128)}, u32[]{:S(2)}) copy-start(f32[1,64,5120]{2,1,0:T(8,128)} %param.14) | copy-start | bytes 3932164
  10.3 13.4 %collective-permute-start.9 = (bf16[64,1280]{1,0:T(8,128)(2,1)S(1)}, bf16[64,1280]{1,0:T(8,128)(2,1)S(1)}, u32[]{:S(2)}, u32[]{:S(2)}) collective-permute-start(bf16[64,1280]{1,0:T(8,128)(2,1)S(1)} %weight_grads.4.after), channel_id=1, source_target_pairs={{0,2},{1,3},{2,0},{3,1},{4,6},{5,7},{6,4},{7,5},{8,10},{9,11},{10,... | collective-permute-start | bytes 491528 | tf_op jit(solution)/shard_map/ppermute | solution.py:328
  12.6 13.8 %collective-permute-start.8 = (bf16[64,1280]{1,0:T(8,128)(2,1)S(1)}, bf16[64,1280]{1,0:T(8,128)(2,1)S(1)}, u32[]{:S(2)}, u32[]{:S(2)}) collective-permute-start(bf16[64,1280]{1,0:T(8,128)(2,1)S(1)} %weight_grads.3.after), channel_id=1, source_target_pairs={{0,3},{1,0},{2,1},{3,2},{4,7},{5,4},{6,5},{7,6},{8,11},{9,8},{10,9... | collective-permute-start | bytes 491528 | tf_op jit(solution)/shard_map/ppermute | solution.py:328
  14.2 12.9 %collective-permute-start.7 = (bf16[64,1280]{1,0:T(8,128)(2,1)S(1)}, bf16[64,1280]{1,0:T(8,128)(2,1)S(1)}, u32[]{:S(2)}, u32[]{:S(2)}) collective-permute-start(bf16[64,1280]{1,0:T(8,128)(2,1)S(1)} %get-tuple-element.29.after), channel_id=1, source_target_pairs={{0,1},{1,2},{2,3},{3,0},{4,5},{5,6},{6,7},{7,4},{8,9},{9,10},{10,1... | collective-permute-start | bytes 491528 | tf_op jit(solution)/shard_map/ppermute | solution.py:328
  14.9 14.6 %collective-permute-start.5 = (bf16[336,128]{1,0:T(8,128)(2,1)S(1)}, bf16[336,128]{1,0:T(8,128)(2,1)S(1)}, u32[]{:S(2)}, u32[]{:S(2)}) collective-permute-start(bf16[336,128]{1,0:T(8,128)(2,1)S(1)} %bundle.1.refs_0_), channel_id=1, source_target_pairs={{0,24},{4,28},{8,16},{12,20},{16,8},{20,12},{24,0},{28,4},{1,25},{... | collective-permute-start | bytes 258056 | tf_op jit(solution)/shard_map/ppermute | solution.py:331
  17.5 13.7 %collective-permute-start.4 = (bf16[336,128]{1,0:T(8,128)(2,1)S(1)}, bf16[336,128]{1,0:T(8,128)(2,1)S(1)}, u32[]{:S(2)}, u32[]{:S(2)}) collective-permute-start(bf16[336,128]{1,0:T(8,128)(2,1)S(1)} %bundle.1.refs_0_), channel_id=1, source_target_pairs={{0,16},{4,20},{8,24},{12,28},{16,0},{20,4},{24,8},{28,12},{1,17},{... | collective-permute-start | bytes 258056 | tf_op jit(solution)/shard_map/ppermute | solution.py:331
  23.7 7.5 %collective-permute-start.3 = (bf16[336,128]{1,0:T(8,128)(2,1)S(1)}, bf16[336,128]{1,0:T(8,128)(2,1)S(1)}, u32[]{:S(2)}, u32[]{:S(2)}) collective-permute-start(bf16[336,128]{1,0:T(8,128)(2,1)S(1)} %bundle.1.refs_0_), channel_id=1, source_target_pairs={{0,8},{4,12},{8,0},{12,4},{16,24},{20,28},{24,16},{28,20},{1,9},{5... | collective-permute-start | bytes 258056 | tf_op jit(solution)/shard_map/ppermute | solution.py:331
  27.6 5.4 %collective-permute-start.12 = (bf16[8,5120]{1,0:T(8,128)(2,1)S(1)}, bf16[8,5120]{1,0:T(8,128)(2,1)S(1)}, u32[]{:S(2)}, u32[]{:S(2)}) collective-permute-start(bf16[8,5120]{1,0:T(8,128)(2,1)S(1)} %get-tuple-element.42.refs_0_), channel_id=1, source_target_pairs={{0,24},{4,28},{8,16},{12,20},{16,8},{20,12},{24,0},{28,4},{1,25},{... | collective-permute-start | bytes 245768 | tf_op jit(solution)/shard_map/ppermute | solution.py:331
  29.2 4.7 %collective-permute-start.11 = (bf16[8,5120]{1,0:T(8,128)(2,1)S(1)}, bf16[8,5120]{1,0:T(8,128)(2,1)S(1)}, u32[]{:S(2)}, u32[]{:S(2)}) collective-permute-start(bf16[8,5120]{1,0:T(8,128)(2,1)S(1)} %get-tuple-element.42.refs_0_), channel_id=1, source_target_pairs={{0,16},{4,20},{8,24},{12,28},{16,0},{20,4},{24,8},{28,12},{1,17},{... | collective-permute-start | bytes 245768 | tf_op jit(solution)/shard_map/ppermute | solution.py:331
  29.6 4.4 %collective-permute-start.10 = (bf16[8,5120]{1,0:T(8,128)(2,1)S(1)}, bf16[8,5120]{1,0:T(8,128)(2,1)S(1)}, u32[]{:S(2)}, u32[]{:S(2)}) collective-permute-start(bf16[8,5120]{1,0:T(8,128)(2,1)S(1)} %get-tuple-element.42.refs_0_), channel_id=1, source_target_pairs={{0,8},{4,12},{8,0},{12,4},{16,24},{20,28},{24,16},{28,20},{1,9},{5... | collective-permute-start | bytes 245768 | tf_op jit(solution)/shard_map/ppermute | solution.py:331
  31.2 3.8 %collective-permute-start.6 = (bf16[4,336,128]{2,1,0:T(8,128)(2,1)S(1)}, bf16[4,336,128]{2,1,0:T(8,128)(2,1)S(1)}, u32[]{:S(2)}, u32[]{:S(2)}) collective-permute-start(bf16[4,336,128]{2,1,0:T(8,128)(2,1)S(1)} %join_bundles.1.mine.bundles), channel_id=1, source_target_pairs={{0,4},{4,0},{8,12},{12,8},{16,20},{20,16},{24,28},{28,24},{1,5},{5... | collective-permute-start | bytes 1032200 | tf_op jit(solution)/shard_map/ppermute | solution.py:331
  34.0 2.6 %collective-permute-start.13 = (bf16[4,8,5120]{2,1,0:T(8,128)(2,1)S(1)}, bf16[4,8,5120]{2,1,0:T(8,128)(2,1)S(1)}, u32[]{:S(2)}, u32[]{:S(2)}) collective-permute-start(bf16[4,8,5120]{2,1,0:T(8,128)(2,1)S(1)} %join_kept.1.mine), channel_id=1, source_target_pairs={{0,4},{4,0},{8,12},{12,8},{16,20},{20,16},{24,28},{28,24},{1,5},{5... | collective-permute-start | bytes 983048 | tf_op jit(solution)/shard_map/ppermute | solution.py:331

commit v10 on v8

--- a/solution.py
+++ b/solution.py
@@ -150,10 +150,10 @@
         refs[-1][i] = ref[...]
 
 
-def own_body(n_r, keep, after, mask, tally, tab, lines, tall, p_ref, a_ref, w_ref, tab_ref, mask_s, tally_s, sems):
+def own_body(n_r, keep, mask, tally, lines, tall, p_ref, a_ref, w_ref, mask_s, tally_s, sems):
     copies = [
         pltpu.make_async_copy(src, dst, sems.at[i])
-        for i, (src, dst) in enumerate([(mask, mask_s), (tally, tally_s), (tab, tab_ref)])
+        for i, (src, dst) in enumerate([(mask, mask_s), (tally, tally_s)])
     ]
     for copy in copies:
         copy.start()
@@ -190,7 +190,7 @@
         w_ref[h] = w * scale
 
 
-def kept_body(ks, n_t, keep, vel, a_ref, tab, *refs):
+def kept_body(ks, n_t, keep, vel, a_ref, tab, after, *refs):
     grads, (send_ref, own_ref) = refs[: len(ks)], refs[-2:]
     cols = grads[0].shape[1]
     ng = cols // G
@@ -352,6 +352,20 @@
     )
     parts = [parts[0]] + [shift(parts[k], k) for k in range(1, n_t)]
 
+    p_own, a_own, shares = call(
+        functools.partial(own_body, n_r, keep),
+        [
+            near((B, groups * 2 * B)),
+            near((groups * B, 2 * B)),
+            near((2, 8, 2 * B), F32),
+        ],
+        (far(mask), far(tally), own, tall),
+        [ANY, ANY, VM, VM],
+        [VM] * 3,
+        scratch=[pltpu.SMEM((n_r,), jnp.int32)] * 2 + [pltpu.SemaphoreType.DMA((2,))],
+        name="own_places",
+    )
+
     def grads_of(ks, after):
         return call(
             functools.partial(grads_body, len(ks)),
@@ -363,11 +377,9 @@
         )
 
     grads = {}
-    made = act
     for k in range(1, n_t - 1):
-        (made,) = grads_of([k], made)
-        grads[k] = made
-    made, grads[0] = grads_of([n_t - 1, 0], made)
+        (grads[k],) = grads_of([k], act)
+    made, grads[0] = grads_of([n_t - 1, 0], shares)
     grads[n_t - 1] = made
     grads = [grads[0]] + [shift(grads[k], -k) for k in range(1, n_t)]
 
@@ -381,20 +393,6 @@
     )
     bundles = lax.all_gather(bundle, "replica", axis=0)
 
-    p_own, a_own, shares, tab = call(
-        functools.partial(own_body, n_r, keep),
-        [
-            near((B, groups * 2 * B)),
-            near((groups * B, 2 * B)),
-            near((2, 8, 2 * B), F32),
-            near(tab.shape),
-        ],
-        (bundles, far(mask), far(tally), far(tab), own, tall),
-        [ANY, ANY, ANY, ANY, VM, VM],
-        [VM] * 4,
-        scratch=[pltpu.SMEM((n_r,), jnp.int32)] * 2 + [pltpu.SemaphoreType.DMA((3,))],
-        name="own_places",
-    )
     places = call(
         functools.partial(places_body, keep),
         [near((B, blocks * half * keep))] * 4,
@@ -420,13 +418,13 @@
         rows = call(
             functools.partial(kept_body, ks, n_t, keep),
             [near((keep, width)), near((keep, width), F32)],
-            (vel[0], a_own, tab, *[grads[k] for k in ks], *rows),
-            [VM] * (3 + len(ks) + len(rows)),
+            (vel[0], a_own, tab, bundles, *[grads[k] for k in ks], *rows),
+            [VM] * 3 + [ANY] + [VM] * (len(ks) + len(rows)),
             [VM] * 2,
             flops=6 * B * B * cols * len(ks),
             nbytes=B * cols * 6 * len(ks),
             name="kept_rows",
-            alias={3 + len(ks): 0, 4 + len(ks): 1} if rows else {},
+            alias={4 + len(ks): 0, 5 + len(ks): 1} if rows else {},
         )
     ship, q_own = rows
     ships = [ship] + [swap(ship, 2 * i) for i in range(1, half)]

time: 38.3 us -> 37.2 us (0.971)
  starting transfers between devices: 15 us -> 14.4 us
    ppermute x6, starting transfers between devices: 11.4 us -> 10.8 us  [shift(): return lax.ppermute(x, 'tensor', [(i, (i + k) % n_t) for i in range(n_t)])]
  transfers between devices with their start and end apart: 10 -> 10, of which waited for: 3 -> 4; matrix products, arithmetic and copies ran while one was open for 0% -> 0% of each run, Pallas kernels for 15% -> 15%
where the time goes in v10:
time: 37.2 us; the launch traced here: 36.9 us
  starting transfers between devices  14.4 us (39%)
  blocking collectives  10.3 us (28%)
  Pallas kernels  8.48 us (23%)
  waiting for transfers between devices  2.93 us (8%)
  between operations  0.75 us (2%)
    ppermute x6, starting transfers between devices, shift(): return lax.ppermute(x, 'tensor', [(i, (i + k) % n_t) for i in range(n_t)])  10.8 us
    all_gather x1, blocking collectives, per_device(): bundles = lax.all_gather(bundle, 'replica', axis=0)  10.3 us
    pallas_call x14, Pallas kernels, call(): pl.pallas_call(body, out_shape=out_shape, in_specs=in_specs, out_specs=ou...  8.48 us
    ppermute x4, starting transfers between devices, swap(): return lax.ppermute(x, 'replica', [(i, i ^ m) for i in range(n_r)])  3.61 us
    ppermute x4, waiting for transfers between devices, swap(): return lax.ppermute(x, 'replica', [(i, i ^ m) for i in range(n_r)])  2.06 us
    ppermute x6, waiting for transfers between devices, shift(): return lax.ppermute(x, 'tensor', [(i, (i + k) % n_t) for i in range(n_t)])  0.88 us
  transfers between devices with their start and end apart: 10, of which 4 were waited for; matrix products, arithmetic and copies ran while one was open for 0% of the time, Pallas kernels for 15%

profile of v10, /device:TPU:0, one launch (start us, length us, event | category | flops | bytes accessed | tf_op | source)
XLA Modules:
  0.0 36.9 jit_solution(8628941883175524542)
XLA Ops:
  0.6 1.2 %up_grads.1 = (bf16[144,128]{1,0:T(8,128)(2,1)S(1)}, bf16[144,128]{1,0:T(8,128)(2,1)S(1)}, bf16[144,128]{1,0:T(8,128)(2,1)S(1)}, bf16[144,128]{1,0:T(8,128)(2,1)...) custom-call(bf16[64,128]{1,0:T(8,128)(2,1)} %bitcast.16, ...), custom_call_target="tpu_custom_call" | custom-call | bytes 819200 | tf_op jit(solution)/shard_map/up_grads/pallas_call | solution.py:79
  1.8 3.1 %collective-permute-start.1 = (bf16[144,128]{1,0:T(8,128)(2,1)S(1)}, bf16[144,128]{1,0:T(8,128)(2,1)S(1)}, u32[]{:S(2)}, u32[]{:S(2)}) collective-permute-start(bf16[144,128]{1,0:T(8,128)(2,1)S(1)} %get-tuple-element.30), channel_id=1, source_target_pairs={{0,1},{1,2},{2,3},{3,0},{4,5},{5,6},{6,7},{7,4},{8,9},{9,10},{10,1... | collective-permute-start | bytes 110600 | tf_op jit(solution)/shard_map/ppermute | solution.py:329
  4.9 2.6 %collective-permute-start.2 = (bf16[144,128]{1,0:T(8,128)(2,1)S(1)}, bf16[144,128]{1,0:T(8,128)(2,1)S(1)}, u32[]{:S(2)}, u32[]{:S(2)}) collective-permute-start(bf16[144,128]{1,0:T(8,128)(2,1)S(1)} %get-tuple-element.31), channel_id=1, source_target_pairs={{0,2},{1,3},{2,0},{3,1},{4,6},{5,7},{6,4},{7,5},{8,10},{9,11},{10,... | collective-permute-start | bytes 110600 | tf_op jit(solution)/shard_map/ppermute | solution.py:329
  7.5 1.3 %collective-permute-start = (bf16[144,128]{1,0:T(8,128)(2,1)S(1)}, bf16[144,128]{1,0:T(8,128)(2,1)S(1)}, u32[]{:S(2)}, u32[]{:S(2)}) collective-permute-start(bf16[144,128]{1,0:T(8,128)(2,1)S(1)} %get-tuple-element.27), channel_id=1, source_target_pairs={{0,3},{1,0},{2,1},{3,2},{4,7},{5,4},{6,5},{7,6},{8,11},{9,8},{10,9... | collective-permute-start | bytes 110600 | tf_op jit(solution)/shard_map/ppermute | solution.py:329
  8.8 0.0 collective-permute-done.1.refs_1_.refs_0_
  8.8 0.2 weight_grads.4
  9.0 0.0 copy-start
  9.0 0.0 copy-start.1
  9.0 2.4 %collective-permute-start.4 = (bf16[64,1280]{1,0:T(8,128)(2,1)S(1)}, bf16[64,1280]{1,0:T(8,128)(2,1)S(1)}, u32[]{:S(2)}, u32[]{:S(2)}) collective-permute-start(bf16[64,1280]{1,0:T(8,128)(2,1)S(1)} %weight_grads.4), channel_id=1, source_target_pairs={{0,3},{1,0},{2,1},{3,2},{4,7},{5,4},{6,5},{7,6},{8,11},{9,8},{10,9... | collective-permute-start | bytes 491528 | tf_op jit(solution)/shard_map/ppermute | solution.py:329
  11.4 0.0 collective-permute-done.2.refs_2_.refs_0_
  11.4 0.2 weight_grads.5
  11.6 1.0 %collective-permute-start.5 = (bf16[64,1280]{1,0:T(8,128)(2,1)S(1)}, bf16[64,1280]{1,0:T(8,128)(2,1)S(1)}, u32[]{:S(2)}, u32[]{:S(2)}) collective-permute-start(bf16[64,1280]{1,0:T(8,128)(2,1)S(1)} %weight_grads.5), channel_id=1, source_target_pairs={{0,2},{1,3},{2,0},{3,1},{4,6},{5,7},{6,4},{7,5},{8,10},{9,11},{10,... | collective-permute-start | bytes 491528 | tf_op jit(solution)/shard_map/ppermute | solution.py:329
  12.6 0.7 %own_places.1 = (bf16[64,2560]{1,0:T(8,128)(2,1)S(1)}, bf16[1280,128]{1,0:T(8,128)(2,1)S(1)}, f32[2,8,128]{2,1,0:T(8,128)S(1)}) custom-call(s32[8]{0:T(128)} %mask.1, s32[8]{0:T(128)} %tally.1, s32[8,80]{1,0:T(8,128)S(1)} %get-tuple-element.24.lines, bf16[128,128]{1,0:T(8,128)(2,1)S(1)} %get-tuple-element.25.tall), custom_call_target="tpu_custom_call" | custom-call | tf_op jit(solution)/shard_map/own_places/pallas_call | solution.py:79
  13.4 0.0 collective-permute-done.refs_0_.refs_3_
  13.4 0.2 weight_grads.3
  13.6 0.4 %collective-permute-start.3 = (bf16[64,1280]{1,0:T(8,128)(2,1)S(1)}, bf16[64,1280]{1,0:T(8,128)(2,1)S(1)}, u32[]{:S(2)}, u32[]{:S(2)}) collective-permute-start(bf16[64,1280]{1,0:T(8,128)(2,1)S(1)} %get-tuple-element.29.after), channel_id=1, source_target_pairs={{0,1},{1,2},{2,3},{3,0},{4,5},{5,6},{6,7},{7,4},{8,9},{9,10},{10,1... | collective-permute-start | bytes 491528 | tf_op jit(solution)/shard_map/ppermute | solution.py:329
  14.1 10.3 %all-gather = bf16[2688,128]{1,0:T(8,128)(2,1)S(1)} all-gather(bf16[336,128]{1,0:T(8,128)(2,1)S(1)} %bundle.1), channel_id=2, replica_groups=mesh['replica'=8,'tensor'=4] {'replica'}, dimensions={0}, use_global_device_ids=true | all-gather | bytes 774144 | tf_op jit(solution)/shard_map/all_gather | solution.py:394
  24.3 0.0 collective-permute-done.4.refs_1_
  24.3 0.8 %collective-permute-done.5.refs_2_ = bf16[64,1280]{1,0:T(8,128)(2,1)S(1)} collective-permute-done((bf16[64,1280]{1,0:T(8,128)(2,1)S(1)}, bf16[64,1280]{1,0:T(8,128)(2,1)S(1)}, u32[]{:S(2)}, u32[]{:S(2)}) %collective-permute-start.5) | collective-permute-done | bytes 163872 | tf_op jit(solution)/shard_map/ppermute | solution.py:329
  25.2 0.0 copy-done
  25.2 0.0 copy-done.1
  25.2 0.7 %kept_rows.2 = (bf16[8,5120]{1,0:T(8,128)(2,1)S(1)}, f32[8,5120]{1,0:T(8,128)S(1)}) custom-call(f32[64,5120]{1,0:T(8,128)S(1)} %bitcast.12, bf16[1280,128]{1,0:T(8,128)(2,1)S(1)} %get-tuple-element.33.a_ref, bf16[1024,256]{1,0:T(8,128)(2,1)S(1)} %copy-done.1, bf16[8,336,128]{2,1,0:T(8,128)(2,1)S(1)} %bitcast.8, f32[64,1280]{1,0:T(8,128)S(1)} %get-tuple-element.34.refs_0_, ...), custom_call_target="tpu_custom_call" | custom-call | flops 94371840 | bytes 1474560 | tf_op jit(solution)/shard_map/kept_rows/pallas_call | solution.py:79
  25.9 0.0 collective-permute-done.3.refs_0_.refs_3_
  25.9 0.5 %kept_rows.3 = (bf16[8,5120]{1,0:T(8,128)(2,1)S(1)}, f32[8,5120]{1,0:T(8,128)S(1)}) custom-call(f32[64,5120]{1,0:T(8,128)S(1)} %bitcast.13, bf16[1280,128]{1,0:T(8,128)(2,1)S(1)} %get-tuple-element.33.a_ref, bf16[1024,256]{1,0:T(8,128)(2,1)S(1)} %copy-done.1, bf16[8,336,128]{2,1,0:T(8,128)(2,1)S(1)} %bitcast.9, ...), custom_call_target="tpu_custom_call", output_to_operand_aliasing={{0}: (5, {}), {1}: (6, {})} | custom-call | flops 31457280 | bytes 491520 | tf_op jit(solution)/shard_map/kept_rows/pallas_call | solution.py:79
  26.4 2.5 %collective-permute-start.8 = (bf16[8,5120]{1,0:T(8,128)(2,1)S(1)}, bf16[8,5120]{1,0:T(8,128)(2,1)S(1)}, u32[]{:S(2)}, u32[]{:S(2)}) collective-permute-start(bf16[8,5120]{1,0:T(8,128)(2,1)S(1)} %get-tuple-element.40.refs_0_), channel_id=1, source_target_pairs={{0,24},{4,28},{8,16},{12,20},{16,8},{20,12},{24,0},{28,4},{1,25},{... | collective-permute-start | bytes 245768 | tf_op jit(solution)/shard_map/ppermute | solution.py:332
  28.9 0.5 %collective-permute-start.7 = (bf16[8,5120]{1,0:T(8,128)(2,1)S(1)}, bf16[8,5120]{1,0:T(8,128)(2,1)S(1)}, u32[]{:S(2)}, u32[]{:S(2)}) collective-permute-start(bf16[8,5120]{1,0:T(8,128)(2,1)S(1)} %get-tuple-element.40.refs_0_), channel_id=1, source_target_pairs={{0,16},{4,20},{8,24},{12,28},{16,0},{20,4},{24,8},{28,12},{1,17},{... | collective-permute-start | bytes 245768 | tf_op jit(solution)/shard_map/ppermute | solution.py:332
  29.4 0.5 %collective-permute-start.6 = (bf16[8,5120]{1,0:T(8,128)(2,1)S(1)}, bf16[8,5120]{1,0:T(8,128)(2,1)S(1)}, u32[]{:S(2)}, u32[]{:S(2)}) collective-permute-start(bf16[8,5120]{1,0:T(8,128)(2,1)S(1)} %get-tuple-element.40.refs_0_), channel_id=1, source_target_pairs={{0,8},{4,12},{8,0},{12,4},{16,24},{20,28},{24,16},{28,20},{1,9},{5... | collective-permute-start | bytes 245768 | tf_op jit(solution)/shard_map/ppermute | solution.py:332
  29.9 0.6 %places.1 = (bf16[64,2560]{1,0:T(8,128)(2,1)S(1)}, bf16[64,2560]{1,0:T(8,128)(2,1)S(1)}, bf16[64,2560]{1,0:T(8,128)(2,1)S(1)}, bf16[64,2560]{1,0:T(8,128)(2,1)S(1)}) custom-call(f32[2,8,128]{2,1,0:T(8,128)S(1)} %get-tuple-element.26.after.w_ref, bf16[128,128]{1,0:T(8,128)(2,1)S(1)} %get-tuple-element.25.tall, bf16[8,336,128]{2,1,0:T(8,128)(2,1)S(1)} %bitcast.10), custom_call_target="tpu_custom_call" | custom-call | tf_op jit(solution)/shard_map/places/pallas_call | solution.py:79
  30.5 1.1 %input_grads.1.refs_5_ = bf16[128,1280]{1,0:T(8,128)(2,1)} custom-call(bf16[8,336,128]{2,1,0:T(8,128)(2,1)S(1)} %bitcast.11, bf16[144,128]{1,0:T(8,128)(2,1)S(1)} %get-tuple-element.28.refs_1_.refs_0_, bf16[144,128]{1,0:T(8,128)(2,1)S(1)} %collective-permute-done.1.refs_1_.refs_0_, bf16[144,128]{1,0:T(8,128)(2,1)S(1)} %collective-permute-done.2.refs_2_.refs_0_, ...), custom_call_target="tpu_custom_call" | custom-call | flops 83886080 | bytes 983040 | tf_op jit(solution)/shard_map/input_grads/pallas_call | solution.py:79
  31.6 1.3 %new_momentums.1.refs_4_ = f32[64,5120]{1,0:T(8,128)} custom-call(f32[64,5120]{1,0:T(8,128)S(1)} %bitcast.14, bf16[64,2560]{1,0:T(8,128)(2,1)S(1)} %get-tuple-element.32.p_ref, f32[8,5120]{1,0:T(8,128)S(1)} %get-tuple-element.37.q, f32[64,1280]{1,0:T(8,128)S(1)} %get-tuple-element.34.refs_0_, bf16[64,1280]{1,0:T(8,128)(2,1)S(1)} %collective-permute-done.4.refs_1_, ...), custom_call_target="tpu_custom_call" | custom-call | flops 125829120 | bytes 3276800 | tf_op jit(solution)/shard_map/new_momentums/pallas_call | solution.py:79
  32.9 0.0 collective-permute-done.8.refs_3_
  32.9 0.5 %collective-permute-done.7.refs_2_ = bf16[8,5120]{1,0:T(8,128)(2,1)S(1)} collective-permute-done((bf16[8,5120]{1,0:T(8,128)(2,1)S(1)}, bf16[8,5120]{1,0:T(8,128)(2,1)S(1)}, u32[]{:S(2)}, u32[]{:S(2)}) %collective-permute-start.7) | collective-permute-done | bytes 81952 | tf_op jit(solution)/shard_map/ppermute | solution.py:332
  33.4 0.4 %collective-permute-done.6.refs_1_ = bf16[8,5120]{1,0:T(8,128)(2,1)S(1)} collective-permute-done((bf16[8,5120]{1,0:T(8,128)(2,1)S(1)}, bf16[8,5120]{1,0:T(8,128)(2,1)S(1)}, u32[]{:S(2)}, u32[]{:S(2)}) %collective-permute-start.6) | collective-permute-done | bytes 81952 | tf_op jit(solution)/shard_map/ppermute | solution.py:332
  33.9 0.1 collective-permute-start.9
  33.9 0.5 %half_updates.1.half_sum = f32[1280,256]{1,0:T(8,128)S(1)} custom-call(bf16[64,2560]{1,0:T(8,128)(2,1)S(1)} %get-tuple-element.38.refs_6_.p_hi, bf16[64,2560]{1,0:T(8,128)(2,1)S(1)} %get-tuple-element.39.p_lo, bf16[4,8,5120]{2,1,0:T(8,128)(2,1)S(1)} %join_kept.1.mine), custom_call_target="tpu_custom_call" | custom-call | tf_op jit(solution)/shard_map/half_updates/pallas_call | solution.py:79
  34.4 1.1 %collective-permute-done.9.other = bf16[4,8,5120]{2,1,0:T(8,128)(2,1)S(1)} collective-permute-done((bf16[4,8,5120]{2,1,0:T(8,128)(2,1)S(1)}, bf16[4,8,5120]{2,1,0:T(8,128)(2,1)S(1)}, u32[]{:S(2)}, u32[]{:S(2)}) %collective-permute-start.9) | collective-permute-done | bytes 327712 | tf_op jit(solution)/shard_map/ppermute | solution.py:332
  35.6 1.3 %updates.1 = f32[64,5120]{1,0:T(8,128)} custom-call(f32[1280,256]{1,0:T(8,128)S(1)} %half_updates.1.half_sum, bf16[64,2560]{1,0:T(8,128)(2,1)S(1)} %get-tuple-element.41.p_hi, bf16[64,2560]{1,0:T(8,128)(2,1)S(1)} %get-tuple-element.42.p_lo, bf16[4,8,5120]{2,1,0:T(8,128)(2,1)S(1)} %collective-permute-done.9.other), custom_call_target="tpu_custom_call" | custom-call | flops 671088640 | bytes 2621440 | tf_op jit(solution)/shard_map/updates/pallas_call | solution.py:79
  (2 shorter events, 0.0 us)
Async XLA Ops:
  1.8 7.0 %collective-permute-start.1 = (bf16[144,128]{1,0:T(8,128)(2,1)S(1)}, bf16[144,128]{1,0:T(8,128)(2,1)S(1)}, u32[]{:S(2)}, u32[]{:S(2)}) collective-permute-start(bf16[144,128]{1,0:T(8,128)(2,1)S(1)} %get-tuple-element.30), channel_id=1, source_target_pairs={{0,1},{1,2},{2,3},{3,0},{4,5},{5,6},{6,7},{7,4},{8,9},{9,10},{10,1... | collective-permute-start | bytes 110600 | tf_op jit(solution)/shard_map/ppermute | solution.py:329
  4.9 6.6 %collective-permute-start.2 = (bf16[144,128]{1,0:T(8,128)(2,1)S(1)}, bf16[144,128]{1,0:T(8,128)(2,1)S(1)}, u32[]{:S(2)}, u32[]{:S(2)}) collective-permute-start(bf16[144,128]{1,0:T(8,128)(2,1)S(1)} %get-tuple-element.31), channel_id=1, source_target_pairs={{0,2},{1,3},{2,0},{3,1},{4,6},{5,7},{6,4},{7,5},{8,10},{9,11},{10,... | collective-permute-start | bytes 110600 | tf_op jit(solution)/shard_map/ppermute | solution.py:329
  7.5 5.9 %collective-permute-start = (bf16[144,128]{1,0:T(8,128)(2,1)S(1)}, bf16[144,128]{1,0:T(8,128)(2,1)S(1)}, u32[]{:S(2)}, u32[]{:S(2)}) collective-permute-start(bf16[144,128]{1,0:T(8,128)(2,1)S(1)} %get-tuple-element.27), channel_id=1, source_target_pairs={{0,3},{1,0},{2,1},{3,2},{4,7},{5,4},{6,5},{7,6},{8,11},{9,8},{10,9... | collective-permute-start | bytes 110600 | tf_op jit(solution)/shard_map/ppermute | solution.py:329
  9.0 16.2 %copy-start = (f32[1,64,5120]{2,1,0:T(8,128)S(1)}, f32[1,64,5120]{2,1,0:T(8,128)}, u32[]{:S(2)}) copy-start(f32[1,64,5120]{2,1,0:T(8,128)} %param.14) | copy-start | bytes 3932164
  9.0 16.1 %copy-start.1 = (bf16[1024,256]{1,0:T(8,128)(2,1)S(1)}, bf16[1024,256]{1,0:T(8,128)(2,1)}, u32[]{:S(2)}) copy-start(bf16[1024,256]{1,0:T(8,128)(2,1)} %constant.4.clone.tab) | copy-start | bytes 1572868
  9.0 15.3 %collective-permute-start.4 = (bf16[64,1280]{1,0:T(8,128)(2,1)S(1)}, bf16[64,1280]{1,0:T(8,128)(2,1)S(1)}, u32[]{:S(2)}, u32[]{:S(2)}) collective-permute-start(bf16[64,1280]{1,0:T(8,128)(2,1)S(1)} %weight_grads.4), channel_id=1, source_target_pairs={{0,3},{1,0},{2,1},{3,2},{4,7},{5,4},{6,5},{7,6},{8,11},{9,8},{10,9... | collective-permute-start | bytes 491528 | tf_op jit(solution)/shard_map/ppermute | solution.py:329
  11.6 13.6 %collective-permute-start.5 = (bf16[64,1280]{1,0:T(8,128)(2,1)S(1)}, bf16[64,1280]{1,0:T(8,128)(2,1)S(1)}, u32[]{:S(2)}, u32[]{:S(2)}) collective-permute-start(bf16[64,1280]{1,0:T(8,128)(2,1)S(1)} %weight_grads.5), channel_id=1, source_target_pairs={{0,2},{1,3},{2,0},{3,1},{4,6},{5,7},{6,4},{7,5},{8,10},{9,11},{10,... | collective-permute-start | bytes 491528 | tf_op jit(solution)/shard_map/ppermute | solution.py:329
  13.6 12.3 %collective-permute-start.3 = (bf16[64,1280]{1,0:T(8,128)(2,1)S(1)}, bf16[64,1280]{1,0:T(8,128)(2,1)S(1)}, u32[]{:S(2)}, u32[]{:S(2)}) collective-permute-start(bf16[64,1280]{1,0:T(8,128)(2,1)S(1)} %get-tuple-element.29.after), channel_id=1, source_target_pairs={{0,1},{1,2},{2,3},{3,0},{4,5},{5,6},{6,7},{7,4},{8,9},{9,10},{10,1... | collective-permute-start | bytes 491528 | tf_op jit(solution)/shard_map/ppermute | solution.py:329
  26.4 6.5 %collective-permute-start.8 = (bf16[8,5120]{1,0:T(8,128)(2,1)S(1)}, bf16[8,5120]{1,0:T(8,128)(2,1)S(1)}, u32[]{:S(2)}, u32[]{:S(2)}) collective-permute-start(bf16[8,5120]{1,0:T(8,128)(2,1)S(1)} %get-tuple-element.40.refs_0_), channel_id=1, source_target_pairs={{0,24},{4,28},{8,16},{12,20},{16,8},{20,12},{24,0},{28,4},{1,25},{... | collective-permute-start | bytes 245768 | tf_op jit(solution)/shard_map/ppermute | solution.py:332
  28.9 4.5 %collective-permute-start.7 = (bf16[8,5120]{1,0:T(8,128)(2,1)S(1)}, bf16[8,5120]{1,0:T(8,128)(2,1)S(1)}, u32[]{:S(2)}, u32[]{:S(2)}) collective-permute-start(bf16[8,5120]{1,0:T(8,128)(2,1)S(1)} %get-tuple-element.40.refs_0_), channel_id=1, source_target_pairs={{0,16},{4,20},{8,24},{12,28},{16,0},{20,4},{24,8},{28,12},{1,17},{... | collective-permute-start | bytes 245768 | tf_op jit(solution)/shard_map/ppermute | solution.py:332
  29.4 4.4 %collective-permute-start.6 = (bf16[8,5120]{1,0:T(8,128)(2,1)S(1)}, bf16[8,5120]{1,0:T(8,128)(2,1)S(1)}, u32[]{:S(2)}, u32[]{:S(2)}) collective-permute-start(bf16[8,5120]{1,0:T(8,128)(2,1)S(1)} %get-tuple-element.40.refs_0_), channel_id=1, source_target_pairs={{0,8},{4,12},{8,0},{12,4},{16,24},{20,28},{24,16},{28,20},{1,9},{5... | collective-permute-start | bytes 245768 | tf_op jit(solution)/shard_map/ppermute | solution.py:332
  33.9 1.7 %collective-permute-start.9 = (bf16[4,8,5120]{2,1,0:T(8,128)(2,1)S(1)}, bf16[4,8,5120]{2,1,0:T(8,128)(2,1)S(1)}, u32[]{:S(2)}, u32[]{:S(2)}) collective-permute-start(bf16[4,8,5120]{2,1,0:T(8,128)(2,1)S(1)} %join_kept.1.mine), channel_id=1, source_target_pairs={{0,4},{4,0},{8,12},{12,8},{16,20},{20,16},{24,28},{28,24},{1,5},{5... | collective-permute-start | bytes 983048 | tf_op jit(solution)/shard_map/ppermute | solution.py:332

commit v11 on v10

--- a/solution.py
+++ b/solution.py
@@ -118,7 +118,7 @@
     copies[2].wait()
     nc = cols // cp
     for k in range(n_t):
-        c0 = lax.rem(ten + k, n_t) * cols + lax.rem(rep, cp) * nc
+        c0 = (ten ^ k) * cols + lax.rem(rep, cp) * nc
         for j in range(nc // 128):
             at = pl.multiple_of(c0 + j * 128, 128)
             outs[k][B + j * nr : B + (j + 1) * nr, :] = exp_v[:, pl.ds(at, 128)]
@@ -197,7 +197,7 @@
     lane_block = lax.broadcasted_iota(jnp.int32, (keep, G), 1) // B
     sel = []
     for n, k in enumerate(ks):
-        c0 = lax.rem(lax.axis_index("tensor") + k, n_t) * cols
+        c0 = (lax.axis_index("tensor") ^ k) * cols
         for i in range(ng):
             at = pl.multiple_of(c0 + i * G, G)
             moment = momentum_decay * vel[:, pl.ds(at, G)] + grads[n][:, i * G : (i + 1) * G].astype(F32)
@@ -214,7 +214,7 @@
     kept = (y[:n] + y[n:] + dot(hi, fwd(tab, 1))).astype(BF16)
     q = dot(kept, inv(tab, 0)) + dot(kept, inv(tab, 1))
     for n, k in enumerate(ks):
-        c0 = pl.multiple_of(lax.rem(lax.axis_index("tensor") + k, n_t) * cols, G)
+        c0 = pl.multiple_of((lax.axis_index("tensor") ^ k) * cols, G)
         part = jnp.concatenate([q[(n * ng + i) * keep : (n * ng + i + 1) * keep] for i in range(ng)], axis=1)
         own_ref[:, pl.ds(c0, cols)] = part
         send_ref[:, pl.ds(c0, cols)] = part.astype(BF16)
@@ -227,7 +227,7 @@
     lane_block = lax.broadcasted_iota(jnp.int32, (keep, G), 1) // B
     copies = []
     for k in range(n_t):
-        c0 = pl.multiple_of(lax.rem(lax.axis_index("tensor") + k, n_t) * cols, G)
+        c0 = pl.multiple_of((lax.axis_index("tensor") ^ k) * cols, G)
         for i in range(ng):
             at = pl.multiple_of(c0 + i * G, G)
             own = q[:, pl.ds(at, G)]
@@ -325,8 +325,10 @@
     rp = n_r // cp
     half = n_r // 2
     tab, tall = constants()
-    def shift(x, k):
-        return lax.ppermute(x, "tensor", [(i, (i + k) % n_t) for i in range(n_t)])
+    def trade(x, k):
+        return lax.ppermute(x, "tensor", [(i, i ^ k) for i in range(n_t)])
+
+    order = [*range(2, n_t), 1]
 
     def swap(x, m):
         return lax.ppermute(x, "replica", [(i, i ^ m) for i in range(n_r)])
@@ -350,7 +352,8 @@
         nbytes=act.size * 4 + nr * width * 2,
         name="up_grads",
     )
-    parts = [parts[0]] + [shift(parts[k], k) for k in range(1, n_t)]
+    got = {k: trade(parts[k], k) for k in order}
+    parts = [parts[0]] + [got[k] for k in range(1, n_t)]
 
     p_own, a_own, shares = call(
         functools.partial(own_body, n_r, keep),
@@ -377,11 +380,11 @@
         )
 
     grads = {}
-    for k in range(1, n_t - 1):
+    for k in order[:-1]:
         (grads[k],) = grads_of([k], act)
-    made, grads[0] = grads_of([n_t - 1, 0], shares)
-    grads[n_t - 1] = made
-    grads = [grads[0]] + [shift(grads[k], -k) for k in range(1, n_t)]
+    made, grads[0] = grads_of([order[-1], 0], shares)
+    grads[order[-1]] = made
+    grads.update({k: trade(grads[k], k) for k in order})
 
     bundle = call(
         functools.partial(bundle_body, n_t, keep),
@@ -414,7 +417,7 @@
     )
 
     rows = []
-    for ks in (list(range(n_t - 1)), [n_t - 1]):
+    for ks in ([k for k in range(n_t) if k != n_t - 1], [n_t - 1]):
         rows = call(
             functools.partial(kept_body, ks, n_t, keep),
             [near((keep, width)), near((keep, width), F32)],
@@ -431,7 +434,7 @@
     new = call(
         functools.partial(return_body, n_t, keep),
         jax.ShapeDtypeStruct((B, width), F32),
-        (vel[0], p_own, q_own, *grads),
+        (vel[0], p_own, q_own, *[grads[k] for k in range(n_t)]),
         [VM] * (3 + n_t),
         ANY,
         scratch=[pltpu.VMEM((B, width), F32), pltpu.SemaphoreType.DMA((n_t,))],
@@ -535,6 +538,8 @@
             and exp.shape[0] == B
             and lines.shape[3] == 8
             and n_r == 8
+            and n_t >= 2
+            and n_t & (n_t - 1) == 0
         )
         if not fits:
             return per_device_plain(*args)

time: 37.2 us -> 36.3 us (0.976)
  waiting for transfers between devices: 2.93 us -> 2.22 us
    ppermute x6, waiting for transfers between devices: 0.88 us -> 0.18 us  [trade(): return lax.ppermute(x, 'tensor', [(i, i ^ k) for i in range(n_t)])]
  transfers between devices with their start and end apart: 10 -> 10, of which waited for: 4 -> 3; matrix products, arithmetic and copies ran while one was open for 0% -> 0% of each run, Pallas kernels for 15% -> 15%
where the time goes in v11:
time: 36.3 us; the launch traced here: 36 us
  starting transfers between devices  14.2 us (39%)
  blocking collectives  10.3 us (28%)
  Pallas kernels  8.49 us (23%)
  waiting for transfers between devices  2.22 us (6%)
  between operations  0.76 us (2%)
    ppermute x6, starting transfers between devices, trade(): return lax.ppermute(x, 'tensor', [(i, i ^ k) for i in range(n_t)])  10.6 us
    all_gather x1, blocking collectives, per_device(): bundles = lax.all_gather(bundle, 'replica', axis=0)  10.3 us
    pallas_call x14, Pallas kernels, call(): pl.pallas_call(body, out_shape=out_shape, in_specs=in_specs, out_specs=ou...  8.49 us
    ppermute x4, starting transfers between devices, swap(): return lax.ppermute(x, 'replica', [(i, i ^ m) for i in range(n_r)])  3.62 us
    ppermute x4, waiting for transfers between devices, swap(): return lax.ppermute(x, 'replica', [(i, i ^ m) for i in range(n_r)])  2.04 us
  transfers between devices with their start and end apart: 10, of which 3 were waited for; matrix products, arithmetic and copies ran while one was open for 0% of the time, Pallas kernels for 15%

profile of v11, /device:TPU:0, one launch (start us, length us, event | category | flops | bytes accessed | tf_op | source)
XLA Modules:
  0.0 36.0 jit_solution(13500831035915199163)
XLA Ops:
  0.6 1.2 %up_grads.1 = (bf16[144,128]{1,0:T(8,128)(2,1)S(1)}, bf16[144,128]{1,0:T(8,128)(2,1)S(1)}, bf16[144,128]{1,0:T(8,128)(2,1)S(1)}, bf16[144,128]{1,0:T(8,128)(2,1)...) custom-call(bf16[64,128]{1,0:T(8,128)(2,1)} %bitcast.16, ...), custom_call_target="tpu_custom_call" | custom-call | bytes 819200 | tf_op jit(solution)/shard_map/up_grads/pallas_call | solution.py:79
  1.8 4.1 %collective-permute-start.1 = (bf16[144,128]{1,0:T(8,128)(2,1)S(1)}, bf16[144,128]{1,0:T(8,128)(2,1)S(1)}, u32[]{:S(2)}, u32[]{:S(2)}) collective-permute-start(bf16[144,128]{1,0:T(8,128)(2,1)S(1)} %get-tuple-element.30), channel_id=1, source_target_pairs={{0,2},{1,3},{2,0},{3,1},{4,6},{5,7},{6,4},{7,5},{8,10},{9,11},{10,... | collective-permute-start | bytes 110600 | tf_op jit(solution)/shard_map/ppermute | solution.py:329
  5.9 1.6 %collective-permute-start = (bf16[144,128]{1,0:T(8,128)(2,1)S(1)}, bf16[144,128]{1,0:T(8,128)(2,1)S(1)}, u32[]{:S(2)}, u32[]{:S(2)}) collective-permute-start(bf16[144,128]{1,0:T(8,128)(2,1)S(1)} %get-tuple-element.27), channel_id=1, source_target_pairs={{0,1},{1,0},{2,3},{3,2},{4,5},{5,4},{6,7},{7,6},{8,9},{9,8},{10,11... | collective-permute-start | bytes 110600 | tf_op jit(solution)/shard_map/ppermute | solution.py:329
  7.5 0.0 collective-permute-start.2
  7.5 0.7 %own_places.1 = (bf16[64,2560]{1,0:T(8,128)(2,1)S(1)}, bf16[1280,128]{1,0:T(8,128)(2,1)S(1)}, f32[2,8,128]{2,1,0:T(8,128)S(1)}) custom-call(s32[8]{0:T(128)} %mask.1, s32[8]{0:T(128)} %tally.1, s32[8,80]{1,0:T(8,128)S(1)} %get-tuple-element.24.lines, bf16[128,128]{1,0:T(8,128)(2,1)S(1)} %get-tuple-element.25.tall), custom_call_target="tpu_custom_call" | custom-call | tf_op jit(solution)/shard_map/own_places/pallas_call | solution.py:79
  8.2 0.1 collective-permute-done.1.refs_2_.refs_0_
  8.3 0.2 weight_grads.5
  8.5 0.0 copy-start
  8.5 0.0 copy-start.1
  8.5 2.7 %collective-permute-start.5 = (bf16[64,1280]{1,0:T(8,128)(2,1)S(1)}, bf16[64,1280]{1,0:T(8,128)(2,1)S(1)}, u32[]{:S(2)}, u32[]{:S(2)}) collective-permute-start(bf16[64,1280]{1,0:T(8,128)(2,1)S(1)} %weight_grads.5), channel_id=1, source_target_pairs={{0,2},{1,3},{2,0},{3,1},{4,6},{5,7},{6,4},{7,5},{8,10},{9,11},{10,... | collective-permute-start | bytes 491528 | tf_op jit(solution)/shard_map/ppermute | solution.py:329
  11.3 0.0 collective-permute-done.refs_0_.refs_1_
  11.3 0.2 weight_grads.3
  11.5 2.1 %collective-permute-start.4 = (bf16[64,1280]{1,0:T(8,128)(2,1)S(1)}, bf16[64,1280]{1,0:T(8,128)(2,1)S(1)}, u32[]{:S(2)}, u32[]{:S(2)}) collective-permute-start(bf16[64,1280]{1,0:T(8,128)(2,1)S(1)} %get-tuple-element.29.after), channel_id=1, source_target_pairs={{0,1},{1,0},{2,3},{3,2},{4,5},{5,4},{6,7},{7,6},{8,9},{9,8},{10,11... | collective-permute-start | bytes 491528 | tf_op jit(solution)/shard_map/ppermute | solution.py:329
  13.6 0.0 collective-permute-done.2.refs_3_.refs_0_
  13.7 0.2 weight_grads.4
  13.9 0.1 collective-permute-start.3
  14.0 10.3 %all-gather = bf16[2688,128]{1,0:T(8,128)(2,1)S(1)} all-gather(bf16[336,128]{1,0:T(8,128)(2,1)S(1)} %bundle.1), channel_id=2, replica_groups=mesh['replica'=8,'tensor'=4] {'replica'}, dimensions={0}, use_global_device_ids=true | all-gather | bytes 774144 | tf_op jit(solution)/shard_map/all_gather | solution.py:397
  24.2 0.0 collective-permute-done.5.refs_2_
  24.2 0.0 collective-permute-done.4.refs_1_
  24.2 0.0 copy-done
  24.3 0.0 copy-done.1
  24.3 0.7 %kept_rows.2 = (bf16[8,5120]{1,0:T(8,128)(2,1)S(1)}, f32[8,5120]{1,0:T(8,128)S(1)}) custom-call(f32[64,5120]{1,0:T(8,128)S(1)} %bitcast.12, bf16[1280,128]{1,0:T(8,128)(2,1)S(1)} %get-tuple-element.33.a_ref, bf16[1024,256]{1,0:T(8,128)(2,1)S(1)} %copy-done.1, bf16[8,336,128]{2,1,0:T(8,128)(2,1)S(1)} %bitcast.8, f32[64,1280]{1,0:T(8,128)S(1)} %get-tuple-element.34.refs_0_, ...), custom_call_target="tpu_custom_call" | custom-call | flops 94371840 | bytes 1474560 | tf_op jit(solution)/shard_map/kept_rows/pallas_call | solution.py:79
  25.0 0.0 collective-permute-done.3.refs_0_.refs_3_
  25.0 0.5 %kept_rows.3 = (bf16[8,5120]{1,0:T(8,128)(2,1)S(1)}, f32[8,5120]{1,0:T(8,128)S(1)}) custom-call(f32[64,5120]{1,0:T(8,128)S(1)} %bitcast.13, bf16[1280,128]{1,0:T(8,128)(2,1)S(1)} %get-tuple-element.33.a_ref, bf16[1024,256]{1,0:T(8,128)(2,1)S(1)} %copy-done.1, bf16[8,336,128]{2,1,0:T(8,128)(2,1)S(1)} %bitcast.9, ...), custom_call_target="tpu_custom_call", output_to_operand_aliasing={{0}: (5, {}), {1}: (6, {})} | custom-call | flops 31457280 | bytes 491520 | tf_op jit(solution)/shard_map/kept_rows/pallas_call | solution.py:79
  25.5 1.5 %collective-permute-start.8 = (bf16[8,5120]{1,0:T(8,128)(2,1)S(1)}, bf16[8,5120]{1,0:T(8,128)(2,1)S(1)}, u32[]{:S(2)}, u32[]{:S(2)}) collective-permute-start(bf16[8,5120]{1,0:T(8,128)(2,1)S(1)} %get-tuple-element.40.refs_0_), channel_id=1, source_target_pairs={{0,24},{4,28},{8,16},{12,20},{16,8},{20,12},{24,0},{28,4},{1,25},{... | collective-permute-start | bytes 245768 | tf_op jit(solution)/shard_map/ppermute | solution.py:334
  27.0 1.5 %collective-permute-start.7 = (bf16[8,5120]{1,0:T(8,128)(2,1)S(1)}, bf16[8,5120]{1,0:T(8,128)(2,1)S(1)}, u32[]{:S(2)}, u32[]{:S(2)}) collective-permute-start(bf16[8,5120]{1,0:T(8,128)(2,1)S(1)} %get-tuple-element.40.refs_0_), channel_id=1, source_target_pairs={{0,16},{4,20},{8,24},{12,28},{16,0},{20,4},{24,8},{28,12},{1,17},{... | collective-permute-start | bytes 245768 | tf_op jit(solution)/shard_map/ppermute | solution.py:334
  28.5 0.5 %collective-permute-start.6 = (bf16[8,5120]{1,0:T(8,128)(2,1)S(1)}, bf16[8,5120]{1,0:T(8,128)(2,1)S(1)}, u32[]{:S(2)}, u32[]{:S(2)}) collective-permute-start(bf16[8,5120]{1,0:T(8,128)(2,1)S(1)} %get-tuple-element.40.refs_0_), channel_id=1, source_target_pairs={{0,8},{4,12},{8,0},{12,4},{16,24},{20,28},{24,16},{28,20},{1,9},{5... | collective-permute-start | bytes 245768 | tf_op jit(solution)/shard_map/ppermute | solution.py:334
  29.0 0.6 %places.1 = (bf16[64,2560]{1,0:T(8,128)(2,1)S(1)}, bf16[64,2560]{1,0:T(8,128)(2,1)S(1)}, bf16[64,2560]{1,0:T(8,128)(2,1)S(1)}, bf16[64,2560]{1,0:T(8,128)(2,1)S(1)}) custom-call(f32[2,8,128]{2,1,0:T(8,128)S(1)} %get-tuple-element.26.after.w_ref, bf16[128,128]{1,0:T(8,128)(2,1)S(1)} %get-tuple-element.25.tall, bf16[8,336,128]{2,1,0:T(8,128)(2,1)S(1)} %bitcast.10), custom_call_target="tpu_custom_call" | custom-call | tf_op jit(solution)/shard_map/places/pallas_call | solution.py:79
  29.6 1.1 %input_grads.1.refs_5_ = bf16[128,1280]{1,0:T(8,128)(2,1)} custom-call(bf16[8,336,128]{2,1,0:T(8,128)(2,1)S(1)} %bitcast.11, bf16[144,128]{1,0:T(8,128)(2,1)S(1)} %get-tuple-element.28.refs_1_.refs_0_, bf16[144,128]{1,0:T(8,128)(2,1)S(1)} %collective-permute-done.refs_0_.refs_1_, bf16[144,128]{1,0:T(8,128)(2,1)S(1)} %collective-permute-done.1.refs_2_.refs_0_, ...), custom_call_target="tpu_custom_call" | custom-call | flops 83886080 | bytes 983040 | tf_op jit(solution)/shard_map/input_grads/pallas_call | solution.py:79
  30.7 1.3 %new_momentums.1.refs_4_ = f32[64,5120]{1,0:T(8,128)} custom-call(f32[64,5120]{1,0:T(8,128)S(1)} %bitcast.14, bf16[64,2560]{1,0:T(8,128)(2,1)S(1)} %get-tuple-element.32.p_ref, f32[8,5120]{1,0:T(8,128)S(1)} %get-tuple-element.37.q, f32[64,1280]{1,0:T(8,128)S(1)} %get-tuple-element.34.refs_0_, bf16[64,1280]{1,0:T(8,128)(2,1)S(1)} %collective-permute-done.4.refs_1_, ...), custom_call_target="tpu_custom_call" | custom-call | flops 125829120 | bytes 3276800 | tf_op jit(solution)/shard_map/new_momentums/pallas_call | solution.py:79
  32.0 0.0 collective-permute-done.8.refs_3_
  32.0 0.9 %collective-permute-done.7.refs_2_ = bf16[8,5120]{1,0:T(8,128)(2,1)S(1)} collective-permute-done((bf16[8,5120]{1,0:T(8,128)(2,1)S(1)}, bf16[8,5120]{1,0:T(8,128)(2,1)S(1)}, u32[]{:S(2)}, u32[]{:S(2)}) %collective-permute-start.7) | collective-permute-done | bytes 81952 | tf_op jit(solution)/shard_map/ppermute | solution.py:334
  32.9 0.0 collective-permute-done.6.refs_1_
  33.0 0.1 collective-permute-start.9
  33.0 0.5 %half_updates.1.half_sum = f32[1280,256]{1,0:T(8,128)S(1)} custom-call(bf16[64,2560]{1,0:T(8,128)(2,1)S(1)} %get-tuple-element.38.refs_6_.p_hi, bf16[64,2560]{1,0:T(8,128)(2,1)S(1)} %get-tuple-element.39.p_lo, bf16[4,8,5120]{2,1,0:T(8,128)(2,1)S(1)} %join_kept.1.mine), custom_call_target="tpu_custom_call" | custom-call | tf_op jit(solution)/shard_map/half_updates/pallas_call | solution.py:79
  33.5 1.1 %collective-permute-done.9.other = bf16[4,8,5120]{2,1,0:T(8,128)(2,1)S(1)} collective-permute-done((bf16[4,8,5120]{2,1,0:T(8,128)(2,1)S(1)}, bf16[4,8,5120]{2,1,0:T(8,128)(2,1)S(1)}, u32[]{:S(2)}, u32[]{:S(2)}) %collective-permute-start.9) | collective-permute-done | bytes 327712 | tf_op jit(solution)/shard_map/ppermute | solution.py:334
  34.7 1.3 %updates.1 = f32[64,5120]{1,0:T(8,128)} custom-call(f32[1280,256]{1,0:T(8,128)S(1)} %half_updates.1.half_sum, bf16[64,2560]{1,0:T(8,128)(2,1)S(1)} %get-tuple-element.41.p_hi, bf16[64,2560]{1,0:T(8,128)(2,1)S(1)} %get-tuple-element.42.p_lo, bf16[4,8,5120]{2,1,0:T(8,128)(2,1)S(1)} %collective-permute-done.9.other), custom_call_target="tpu_custom_call" | custom-call | flops 671088640 | bytes 2621440 | tf_op jit(solution)/shard_map/updates/pallas_call | solution.py:79
  (2 shorter events, 0.0 us)
Async XLA Ops:
  1.8 6.5 %collective-permute-start.1 = (bf16[144,128]{1,0:T(8,128)(2,1)S(1)}, bf16[144,128]{1,0:T(8,128)(2,1)S(1)}, u32[]{:S(2)}, u32[]{:S(2)}) collective-permute-start(bf16[144,128]{1,0:T(8,128)(2,1)S(1)} %get-tuple-element.30), channel_id=1, source_target_pairs={{0,2},{1,3},{2,0},{3,1},{4,6},{5,7},{6,4},{7,5},{8,10},{9,11},{10,... | collective-permute-start | bytes 110600 | tf_op jit(solution)/shard_map/ppermute | solution.py:329
  5.9 5.4 %collective-permute-start = (bf16[144,128]{1,0:T(8,128)(2,1)S(1)}, bf16[144,128]{1,0:T(8,128)(2,1)S(1)}, u32[]{:S(2)}, u32[]{:S(2)}) collective-permute-start(bf16[144,128]{1,0:T(8,128)(2,1)S(1)} %get-tuple-element.27), channel_id=1, source_target_pairs={{0,1},{1,0},{2,3},{3,2},{4,5},{5,4},{6,7},{7,6},{8,9},{9,8},{10,11... | collective-permute-start | bytes 110600 | tf_op jit(solution)/shard_map/ppermute | solution.py:329
  7.5 6.2 %collective-permute-start.2 = (bf16[144,128]{1,0:T(8,128)(2,1)S(1)}, bf16[144,128]{1,0:T(8,128)(2,1)S(1)}, u32[]{:S(2)}, u32[]{:S(2)}) collective-permute-start(bf16[144,128]{1,0:T(8,128)(2,1)S(1)} %get-tuple-element.31), channel_id=1, source_target_pairs={{0,3},{1,2},{2,1},{3,0},{4,7},{5,6},{6,5},{7,4},{8,11},{9,10},{10,... | collective-permute-start | bytes 110600 | tf_op jit(solution)/shard_map/ppermute | solution.py:329
  8.5 15.7 %copy-start = (f32[1,64,5120]{2,1,0:T(8,128)S(1)}, f32[1,64,5120]{2,1,0:T(8,128)}, u32[]{:S(2)}) copy-start(f32[1,64,5120]{2,1,0:T(8,128)} %param.14) | copy-start | bytes 3932164
  8.5 15.7 %copy-start.1 = (bf16[1024,256]{1,0:T(8,128)(2,1)S(1)}, bf16[1024,256]{1,0:T(8,128)(2,1)}, u32[]{:S(2)}) copy-start(bf16[1024,256]{1,0:T(8,128)(2,1)} %constant.4.clone.tab) | copy-start | bytes 1572868
  8.5 15.7 %collective-permute-start.5 = (bf16[64,1280]{1,0:T(8,128)(2,1)S(1)}, bf16[64,1280]{1,0:T(8,128)(2,1)S(1)}, u32[]{:S(2)}, u32[]{:S(2)}) collective-permute-start(bf16[64,1280]{1,0:T(8,128)(2,1)S(1)} %weight_grads.5), channel_id=1, source_target_pairs={{0,2},{1,3},{2,0},{3,1},{4,6},{5,7},{6,4},{7,5},{8,10},{9,11},{10,... | collective-permute-start | bytes 491528 | tf_op jit(solution)/shard_map/ppermute | solution.py:329
  11.5 12.8 %collective-permute-start.4 = (bf16[64,1280]{1,0:T(8,128)(2,1)S(1)}, bf16[64,1280]{1,0:T(8,128)(2,1)S(1)}, u32[]{:S(2)}, u32[]{:S(2)}) collective-permute-start(bf16[64,1280]{1,0:T(8,128)(2,1)S(1)} %get-tuple-element.29.after), channel_id=1, source_target_pairs={{0,1},{1,0},{2,3},{3,2},{4,5},{5,4},{6,7},{7,6},{8,9},{9,8},{10,11... | collective-permute-start | bytes 491528 | tf_op jit(solution)/shard_map/ppermute | solution.py:329
  13.9 11.1 %collective-permute-start.3 = (bf16[64,1280]{1,0:T(8,128)(2,1)S(1)}, bf16[64,1280]{1,0:T(8,128)(2,1)S(1)}, u32[]{:S(2)}, u32[]{:S(2)}) collective-permute-start(bf16[64,1280]{1,0:T(8,128)(2,1)S(1)} %weight_grads.4), channel_id=1, source_target_pairs={{0,3},{1,2},{2,1},{3,0},{4,7},{5,6},{6,5},{7,4},{8,11},{9,10},{10,... | collective-permute-start | bytes 491528 | tf_op jit(solution)/shard_map/ppermute | solution.py:329
  25.5 6.5 %collective-permute-start.8 = (bf16[8,5120]{1,0:T(8,128)(2,1)S(1)}, bf16[8,5120]{1,0:T(8,128)(2,1)S(1)}, u32[]{:S(2)}, u32[]{:S(2)}) collective-permute-start(bf16[8,5120]{1,0:T(8,128)(2,1)S(1)} %get-tuple-element.40.refs_0_), channel_id=1, source_target_pairs={{0,24},{4,28},{8,16},{12,20},{16,8},{20,12},{24,0},{28,4},{1,25},{... | collective-permute-start | bytes 245768 | tf_op jit(solution)/shard_map/ppermute | solution.py:334
  27.0 5.9 %collective-permute-start.7 = (bf16[8,5120]{1,0:T(8,128)(2,1)S(1)}, bf16[8,5120]{1,0:T(8,128)(2,1)S(1)}, u32[]{:S(2)}, u32[]{:S(2)}) collective-permute-start(bf16[8,5120]{1,0:T(8,128)(2,1)S(1)} %get-tuple-element.40.refs_0_), channel_id=1, source_target_pairs={{0,16},{4,20},{8,24},{12,28},{16,0},{20,4},{24,8},{28,12},{1,17},{... | collective-permute-start | bytes 245768 | tf_op jit(solution)/shard_map/ppermute | solution.py:334
  28.5 4.4 %collective-permute-start.6 = (bf16[8,5120]{1,0:T(8,128)(2,1)S(1)}, bf16[8,5120]{1,0:T(8,128)(2,1)S(1)}, u32[]{:S(2)}, u32[]{:S(2)}) collective-permute-start(bf16[8,5120]{1,0:T(8,128)(2,1)S(1)} %get-tuple-element.40.refs_0_), channel_id=1, source_target_pairs={{0,8},{4,12},{8,0},{12,4},{16,24},{20,28},{24,16},{28,20},{1,9},{5... | collective-permute-start | bytes 245768 | tf_op jit(solution)/shard_map/ppermute | solution.py:334
  33.0 1.7 %collective-permute-start.9 = (bf16[4,8,5120]{2,1,0:T(8,128)(2,1)S(1)}, bf16[4,8,5120]{2,1,0:T(8,128)(2,1)S(1)}, u32[]{:S(2)}, u32[]{:S(2)}) collective-permute-start(bf16[4,8,5120]{2,1,0:T(8,128)(2,1)S(1)} %join_kept.1.mine), channel_id=1, source_target_pairs={{0,4},{4,0},{8,12},{12,8},{16,20},{20,16},{24,28},{28,24},{1,5},{5... | collective-permute-start | bytes 983048 | tf_op jit(solution)/shard_map/ppermute | solution.py:334

commit v12 on v11

--- a/solution.py
+++ b/solution.py
@@ -417,7 +417,7 @@
     )
 
     rows = []
-    for ks in ([k for k in range(n_t) if k != n_t - 1], [n_t - 1]):
+    for ks in ([0, *order[:-1]], order[-1:]):
         rows = call(
             functools.partial(kept_body, ks, n_t, keep),
             [near((keep, width)), near((keep, width), F32)],

time: 36.3 us -> 37.1 us (1.022)
  waiting for transfers between devices: 2.22 us -> 3.18 us
    ppermute x6, waiting for transfers between devices: 0.18 us -> 1.14 us  [trade(): return lax.ppermute(x, 'tensor', [(i, i ^ k) for i in range(n_t)])]
  transfers between devices with their start and end apart: 10 -> 10, of which waited for: 3 -> 4; matrix products, arithmetic and copies ran while one was open for 0% -> 0% of each run, Pallas kernels for 15% -> 15%
where the time goes in v12:
time: 37.1 us; the launch traced here: 36.8 us
  starting transfers between devices  14.1 us (38%)
  blocking collectives  10.3 us (28%)
  Pallas kernels  8.49 us (23%)
  waiting for transfers between devices  3.18 us (9%)
  between operations  0.76 us (2%)
    ppermute x6, starting transfers between devices, trade(): return lax.ppermute(x, 'tensor', [(i, i ^ k) for i in range(n_t)])  10.5 us
    all_gather x1, blocking collectives, per_device(): bundles = lax.all_gather(bundle, 'replica', axis=0)  10.3 us
    pallas_call x14, Pallas kernels, call(): pl.pallas_call(body, out_shape=out_shape, in_specs=in_specs, out_specs=ou...  8.49 us
    ppermute x4, starting transfers between devices, swap(): return lax.ppermute(x, 'replica', [(i, i ^ m) for i in range(n_r)])  3.62 us
    ppermute x4, waiting for transfers between devices, swap(): return lax.ppermute(x, 'replica', [(i, i ^ m) for i in range(n_r)])  2.05 us
    ppermute x6, waiting for transfers between devices, trade(): return lax.ppermute(x, 'tensor', [(i, i ^ k) for i in range(n_t)])  1.14 us
  transfers between devices with their start and end apart: 10, of which 4 were waited for; matrix products, arithmetic and copies ran while one was open for 0% of the time, Pallas kernels for 15%

profile of v12, /device:TPU:0, one launch (start us, length us, event | category | flops | bytes accessed | tf_op | source)
XLA Modules:
  0.0 36.8 jit_solution(11551795705504890801)
XLA Ops:
  0.6 1.2 %up_grads.1 = (bf16[144,128]{1,0:T(8,128)(2,1)S(1)}, bf16[144,128]{1,0:T(8,128)(2,1)S(1)}, bf16[144,128]{1,0:T(8,128)(2,1)S(1)}, bf16[144,128]{1,0:T(8,128)(2,1)...) custom-call(bf16[64,128]{1,0:T(8,128)(2,1)} %bitcast.16, ...), custom_call_target="tpu_custom_call" | custom-call | bytes 819200 | tf_op jit(solution)/shard_map/up_grads/pallas_call | solution.py:79
  1.8 4.1 %collective-permute-start.1 = (bf16[144,128]{1,0:T(8,128)(2,1)S(1)}, bf16[144,128]{1,0:T(8,128)(2,1)S(1)}, u32[]{:S(2)}, u32[]{:S(2)}) collective-permute-start(bf16[144,128]{1,0:T(8,128)(2,1)S(1)} %get-tuple-element.30), channel_id=1, source_target_pairs={{0,2},{1,3},{2,0},{3,1},{4,6},{5,7},{6,4},{7,5},{8,10},{9,11},{10,... | collective-permute-start | bytes 110600 | tf_op jit(solution)/shard_map/ppermute | solution.py:329
  5.9 1.3 %collective-permute-start.2 = (bf16[144,128]{1,0:T(8,128)(2,1)S(1)}, bf16[144,128]{1,0:T(8,128)(2,1)S(1)}, u32[]{:S(2)}, u32[]{:S(2)}) collective-permute-start(bf16[144,128]{1,0:T(8,128)(2,1)S(1)} %get-tuple-element.31), channel_id=1, source_target_pairs={{0,3},{1,2},{2,1},{3,0},{4,7},{5,6},{6,5},{7,4},{8,11},{9,10},{10,... | collective-permute-start | bytes 110600 | tf_op jit(solution)/shard_map/ppermute | solution.py:329
  7.2 0.2 collective-permute-start
  7.5 0.8 %collective-permute-done.1.refs_2_.refs_0_ = bf16[144,128]{1,0:T(8,128)(2,1)S(1)} collective-permute-done((bf16[144,128]{1,0:T(8,128)(2,1)S(1)}, bf16[144,128]{1,0:T(8,128)(2,1)S(1)}, u32[]{:S(2)}, u32[]{:S(2)}) %collective-permute-start.1) | collective-permute-done | bytes 36896 | tf_op jit(solution)/shard_map/ppermute | solution.py:329
  8.2 0.2 weight_grads.4
  8.4 0.0 copy-start
  8.4 0.0 copy-start.1
  8.4 3.0 %collective-permute-start.4 = (bf16[64,1280]{1,0:T(8,128)(2,1)S(1)}, bf16[64,1280]{1,0:T(8,128)(2,1)S(1)}, u32[]{:S(2)}, u32[]{:S(2)}) collective-permute-start(bf16[64,1280]{1,0:T(8,128)(2,1)S(1)} %weight_grads.4), channel_id=1, source_target_pairs={{0,2},{1,3},{2,0},{3,1},{4,6},{5,7},{6,4},{7,5},{8,10},{9,11},{10,... | collective-permute-start | bytes 491528 | tf_op jit(solution)/shard_map/ppermute | solution.py:329
  11.5 0.4 %collective-permute-done.2.refs_3_.refs_0_ = bf16[144,128]{1,0:T(8,128)(2,1)S(1)} collective-permute-done((bf16[144,128]{1,0:T(8,128)(2,1)S(1)}, bf16[144,128]{1,0:T(8,128)(2,1)S(1)}, u32[]{:S(2)}, u32[]{:S(2)}) %collective-permute-start.2) | collective-permute-done | bytes 36896 | tf_op jit(solution)/shard_map/ppermute | solution.py:329
  11.9 0.2 weight_grads.5
  12.0 1.3 %collective-permute-start.5 = (bf16[64,1280]{1,0:T(8,128)(2,1)S(1)}, bf16[64,1280]{1,0:T(8,128)(2,1)S(1)}, u32[]{:S(2)}, u32[]{:S(2)}) collective-permute-start(bf16[64,1280]{1,0:T(8,128)(2,1)S(1)} %weight_grads.5), channel_id=1, source_target_pairs={{0,3},{1,2},{2,1},{3,0},{4,7},{5,6},{6,5},{7,4},{8,11},{9,10},{10,... | collective-permute-start | bytes 491528 | tf_op jit(solution)/shard_map/ppermute | solution.py:329
  13.4 0.7 %own_places.1 = (bf16[64,2560]{1,0:T(8,128)(2,1)S(1)}, bf16[1280,128]{1,0:T(8,128)(2,1)S(1)}, f32[2,8,128]{2,1,0:T(8,128)S(1)}) custom-call(s32[8]{0:T(128)} %mask.1, s32[8]{0:T(128)} %tally.1, s32[8,80]{1,0:T(8,128)S(1)} %get-tuple-element.24.lines, bf16[128,128]{1,0:T(8,128)(2,1)S(1)} %get-tuple-element.25.tall), custom_call_target="tpu_custom_call" | custom-call | tf_op jit(solution)/shard_map/own_places/pallas_call | solution.py:79
  14.1 0.0 collective-permute-done.refs_0_.refs_1_
  14.1 0.2 weight_grads.3
  14.3 0.4 %collective-permute-start.3 = (bf16[64,1280]{1,0:T(8,128)(2,1)S(1)}, bf16[64,1280]{1,0:T(8,128)(2,1)S(1)}, u32[]{:S(2)}, u32[]{:S(2)}) collective-permute-start(bf16[64,1280]{1,0:T(8,128)(2,1)S(1)} %get-tuple-element.29.after), channel_id=1, source_target_pairs={{0,1},{1,0},{2,3},{3,2},{4,5},{5,4},{6,7},{7,6},{8,9},{9,8},{10,11... | collective-permute-start | bytes 491528 | tf_op jit(solution)/shard_map/ppermute | solution.py:329
  14.8 10.3 %all-gather = bf16[2688,128]{1,0:T(8,128)(2,1)S(1)} all-gather(bf16[336,128]{1,0:T(8,128)(2,1)S(1)} %bundle.1), channel_id=2, replica_groups=mesh['replica'=8,'tensor'=4] {'replica'}, dimensions={0}, use_global_device_ids=true | all-gather | bytes 774144 | tf_op jit(solution)/shard_map/all_gather | solution.py:397
  25.0 0.0 collective-permute-done.4.refs_1_.refs_2_
  25.1 0.0 collective-permute-done.5.refs_2_.refs_3_
  25.1 0.0 copy-done
  25.1 0.0 copy-done.1
  25.1 0.7 %kept_rows.2 = (bf16[8,5120]{1,0:T(8,128)(2,1)S(1)}, f32[8,5120]{1,0:T(8,128)S(1)}) custom-call(f32[64,5120]{1,0:T(8,128)S(1)} %bitcast.12, bf16[1280,128]{1,0:T(8,128)(2,1)S(1)} %get-tuple-element.33.a_ref, bf16[1024,256]{1,0:T(8,128)(2,1)S(1)} %copy-done.1, bf16[8,336,128]{2,1,0:T(8,128)(2,1)S(1)} %bitcast.8, f32[64,1280]{1,0:T(8,128)S(1)} %get-tuple-element.34.refs_0_, ...), custom_call_target="tpu_custom_call" | custom-call | flops 94371840 | bytes 1474560 | tf_op jit(solution)/shard_map/kept_rows/pallas_call | solution.py:79
  25.8 0.0 collective-permute-done.3.refs_0_.refs_1_
  25.8 0.5 %kept_rows.3 = (bf16[8,5120]{1,0:T(8,128)(2,1)S(1)}, f32[8,5120]{1,0:T(8,128)S(1)}) custom-call(f32[64,5120]{1,0:T(8,128)S(1)} %bitcast.13, bf16[1280,128]{1,0:T(8,128)(2,1)S(1)} %get-tuple-element.33.a_ref, bf16[1024,256]{1,0:T(8,128)(2,1)S(1)} %copy-done.1, bf16[8,336,128]{2,1,0:T(8,128)(2,1)S(1)} %bitcast.9, ...), custom_call_target="tpu_custom_call", output_to_operand_aliasing={{0}: (5, {}), {1}: (6, {})} | custom-call | flops 31457280 | bytes 491520 | tf_op jit(solution)/shard_map/kept_rows/pallas_call | solution.py:79
  26.3 1.5 %collective-permute-start.8 = (bf16[8,5120]{1,0:T(8,128)(2,1)S(1)}, bf16[8,5120]{1,0:T(8,128)(2,1)S(1)}, u32[]{:S(2)}, u32[]{:S(2)}) collective-permute-start(bf16[8,5120]{1,0:T(8,128)(2,1)S(1)} %get-tuple-element.40.refs_0_), channel_id=1, source_target_pairs={{0,24},{4,28},{8,16},{12,20},{16,8},{20,12},{24,0},{28,4},{1,25},{... | collective-permute-start | bytes 245768 | tf_op jit(solution)/shard_map/ppermute | solution.py:334
  27.8 1.5 %collective-permute-start.7 = (bf16[8,5120]{1,0:T(8,128)(2,1)S(1)}, bf16[8,5120]{1,0:T(8,128)(2,1)S(1)}, u32[]{:S(2)}, u32[]{:S(2)}) collective-permute-start(bf16[8,5120]{1,0:T(8,128)(2,1)S(1)} %get-tuple-element.40.refs_0_), channel_id=1, source_target_pairs={{0,16},{4,20},{8,24},{12,28},{16,0},{20,4},{24,8},{28,12},{1,17},{... | collective-permute-start | bytes 245768 | tf_op jit(solution)/shard_map/ppermute | solution.py:334
  29.3 0.5 %collective-permute-start.6 = (bf16[8,5120]{1,0:T(8,128)(2,1)S(1)}, bf16[8,5120]{1,0:T(8,128)(2,1)S(1)}, u32[]{:S(2)}, u32[]{:S(2)}) collective-permute-start(bf16[8,5120]{1,0:T(8,128)(2,1)S(1)} %get-tuple-element.40.refs_0_), channel_id=1, source_target_pairs={{0,8},{4,12},{8,0},{12,4},{16,24},{20,28},{24,16},{28,20},{1,9},{5... | collective-permute-start | bytes 245768 | tf_op jit(solution)/shard_map/ppermute | solution.py:334
  29.8 0.6 %places.1 = (bf16[64,2560]{1,0:T(8,128)(2,1)S(1)}, bf16[64,2560]{1,0:T(8,128)(2,1)S(1)}, bf16[64,2560]{1,0:T(8,128)(2,1)S(1)}, bf16[64,2560]{1,0:T(8,128)(2,1)S(1)}) custom-call(f32[2,8,128]{2,1,0:T(8,128)S(1)} %get-tuple-element.26.after.w_ref, bf16[128,128]{1,0:T(8,128)(2,1)S(1)} %get-tuple-element.25.tall, bf16[8,336,128]{2,1,0:T(8,128)(2,1)S(1)} %bitcast.10), custom_call_target="tpu_custom_call" | custom-call | tf_op jit(solution)/shard_map/places/pallas_call | solution.py:79
  30.4 1.1 %input_grads.1.refs_5_ = bf16[128,1280]{1,0:T(8,128)(2,1)} custom-call(bf16[8,336,128]{2,1,0:T(8,128)(2,1)S(1)} %bitcast.11, bf16[144,128]{1,0:T(8,128)(2,1)S(1)} %get-tuple-element.28.refs_1_.refs_0_, bf16[144,128]{1,0:T(8,128)(2,1)S(1)} %collective-permute-done.refs_0_.refs_1_, bf16[144,128]{1,0:T(8,128)(2,1)S(1)} %collective-permute-done.1.refs_2_.refs_0_, ...), custom_call_target="tpu_custom_call" | custom-call | flops 83886080 | bytes 983040 | tf_op jit(solution)/shard_map/input_grads/pallas_call | solution.py:79
  31.5 1.3 %new_momentums.1.refs_4_ = f32[64,5120]{1,0:T(8,128)} custom-call(f32[64,5120]{1,0:T(8,128)S(1)} %bitcast.14, bf16[64,2560]{1,0:T(8,128)(2,1)S(1)} %get-tuple-element.32.p_ref, f32[8,5120]{1,0:T(8,128)S(1)} %get-tuple-element.37.q, f32[64,1280]{1,0:T(8,128)S(1)} %get-tuple-element.34.refs_0_, bf16[64,1280]{1,0:T(8,128)(2,1)S(1)} %collective-permute-done.3.refs_0_.refs_1_, ...), custom_call_target="tpu_custom_call" | custom-call | flops 125829120 | bytes 3276800 | tf_op jit(solution)/shard_map/new_momentums/pallas_call | solution.py:79
  32.8 0.0 collective-permute-done.8.refs_3_
  32.8 0.9 %collective-permute-done.7.refs_2_ = bf16[8,5120]{1,0:T(8,128)(2,1)S(1)} collective-permute-done((bf16[8,5120]{1,0:T(8,128)(2,1)S(1)}, bf16[8,5120]{1,0:T(8,128)(2,1)S(1)}, u32[]{:S(2)}, u32[]{:S(2)}) %collective-permute-start.7) | collective-permute-done | bytes 81952 | tf_op jit(solution)/shard_map/ppermute | solution.py:334
  33.7 0.0 collective-permute-done.6.refs_1_
  33.8 0.1 collective-permute-start.9
  33.8 0.5 %half_updates.1.half_sum = f32[1280,256]{1,0:T(8,128)S(1)} custom-call(bf16[64,2560]{1,0:T(8,128)(2,1)S(1)} %get-tuple-element.38.refs_6_.p_hi, bf16[64,2560]{1,0:T(8,128)(2,1)S(1)} %get-tuple-element.39.p_lo, bf16[4,8,5120]{2,1,0:T(8,128)(2,1)S(1)} %join_kept.1.mine), custom_call_target="tpu_custom_call" | custom-call | tf_op jit(solution)/shard_map/half_updates/pallas_call | solution.py:79
  34.3 1.1 %collective-permute-done.9.other = bf16[4,8,5120]{2,1,0:T(8,128)(2,1)S(1)} collective-permute-done((bf16[4,8,5120]{2,1,0:T(8,128)(2,1)S(1)}, bf16[4,8,5120]{2,1,0:T(8,128)(2,1)S(1)}, u32[]{:S(2)}, u32[]{:S(2)}) %collective-permute-start.9) | collective-permute-done | bytes 327712 | tf_op jit(solution)/shard_map/ppermute | solution.py:334
  35.5 1.3 %updates.1 = f32[64,5120]{1,0:T(8,128)} custom-call(f32[1280,256]{1,0:T(8,128)S(1)} %half_updates.1.half_sum, bf16[64,2560]{1,0:T(8,128)(2,1)S(1)} %get-tuple-element.41.p_hi, bf16[64,2560]{1,0:T(8,128)(2,1)S(1)} %get-tuple-element.42.p_lo, bf16[4,8,5120]{2,1,0:T(8,128)(2,1)S(1)} %collective-permute-done.9.other), custom_call_target="tpu_custom_call" | custom-call | flops 671088640 | bytes 2621440 | tf_op jit(solution)/shard_map/updates/pallas_call | solution.py:79
  (2 shorter events, 0.0 us)
Async XLA Ops:
  1.8 6.4 %collective-permute-start.1 = (bf16[144,128]{1,0:T(8,128)(2,1)S(1)}, bf16[144,128]{1,0:T(8,128)(2,1)S(1)}, u32[]{:S(2)}, u32[]{:S(2)}) collective-permute-start(bf16[144,128]{1,0:T(8,128)(2,1)S(1)} %get-tuple-element.30), channel_id=1, source_target_pairs={{0,2},{1,3},{2,0},{3,1},{4,6},{5,7},{6,4},{7,5},{8,10},{9,11},{10,... | collective-permute-start | bytes 110600 | tf_op jit(solution)/shard_map/ppermute | solution.py:329
  5.9 6.0 %collective-permute-start.2 = (bf16[144,128]{1,0:T(8,128)(2,1)S(1)}, bf16[144,128]{1,0:T(8,128)(2,1)S(1)}, u32[]{:S(2)}, u32[]{:S(2)}) collective-permute-start(bf16[144,128]{1,0:T(8,128)(2,1)S(1)} %get-tuple-element.31), channel_id=1, source_target_pairs={{0,3},{1,2},{2,1},{3,0},{4,7},{5,6},{6,5},{7,4},{8,11},{9,10},{10,... | collective-permute-start | bytes 110600 | tf_op jit(solution)/shard_map/ppermute | solution.py:329
  7.2 6.9 %collective-permute-start = (bf16[144,128]{1,0:T(8,128)(2,1)S(1)}, bf16[144,128]{1,0:T(8,128)(2,1)S(1)}, u32[]{:S(2)}, u32[]{:S(2)}) collective-permute-start(bf16[144,128]{1,0:T(8,128)(2,1)S(1)} %get-tuple-element.27), channel_id=1, source_target_pairs={{0,1},{1,0},{2,3},{3,2},{4,5},{5,4},{6,7},{7,6},{8,9},{9,8},{10,11... | collective-permute-start | bytes 110600 | tf_op jit(solution)/shard_map/ppermute | solution.py:329
  8.4 16.6 %copy-start = (f32[1,64,5120]{2,1,0:T(8,128)S(1)}, f32[1,64,5120]{2,1,0:T(8,128)}, u32[]{:S(2)}) copy-start(f32[1,64,5120]{2,1,0:T(8,128)} %param.14) | copy-start | bytes 3932164
  8.4 16.6 %copy-start.1 = (bf16[1024,256]{1,0:T(8,128)(2,1)S(1)}, bf16[1024,256]{1,0:T(8,128)(2,1)}, u32[]{:S(2)}) copy-start(bf16[1024,256]{1,0:T(8,128)(2,1)} %constant.4.clone.tab) | copy-start | bytes 1572868
  8.4 16.6 %collective-permute-start.4 = (bf16[64,1280]{1,0:T(8,128)(2,1)S(1)}, bf16[64,1280]{1,0:T(8,128)(2,1)S(1)}, u32[]{:S(2)}, u32[]{:S(2)}) collective-permute-start(bf16[64,1280]{1,0:T(8,128)(2,1)S(1)} %weight_grads.4), channel_id=1, source_target_pairs={{0,2},{1,3},{2,0},{3,1},{4,6},{5,7},{6,4},{7,5},{8,10},{9,11},{10,... | collective-permute-start | bytes 491528 | tf_op jit(solution)/shard_map/ppermute | solution.py:329
  12.0 13.0 %collective-permute-start.5 = (bf16[64,1280]{1,0:T(8,128)(2,1)S(1)}, bf16[64,1280]{1,0:T(8,128)(2,1)S(1)}, u32[]{:S(2)}, u32[]{:S(2)}) collective-permute-start(bf16[64,1280]{1,0:T(8,128)(2,1)S(1)} %weight_grads.5), channel_id=1, source_target_pairs={{0,3},{1,2},{2,1},{3,0},{4,7},{5,6},{6,5},{7,4},{8,11},{9,10},{10,... | collective-permute-start | bytes 491528 | tf_op jit(solution)/shard_map/ppermute | solution.py:329
  14.3 11.4 %collective-permute-start.3 = (bf16[64,1280]{1,0:T(8,128)(2,1)S(1)}, bf16[64,1280]{1,0:T(8,128)(2,1)S(1)}, u32[]{:S(2)}, u32[]{:S(2)}) collective-permute-start(bf16[64,1280]{1,0:T(8,128)(2,1)S(1)} %get-tuple-element.29.after), channel_id=1, source_target_pairs={{0,1},{1,0},{2,3},{3,2},{4,5},{5,4},{6,7},{7,6},{8,9},{9,8},{10,11... | collective-permute-start | bytes 491528 | tf_op jit(solution)/shard_map/ppermute | solution.py:329
  26.3 6.5 %collective-permute-start.8 = (bf16[8,5120]{1,0:T(8,128)(2,1)S(1)}, bf16[8,5120]{1,0:T(8,128)(2,1)S(1)}, u32[]{:S(2)}, u32[]{:S(2)}) collective-permute-start(bf16[8,5120]{1,0:T(8,128)(2,1)S(1)} %get-tuple-element.40.refs_0_), channel_id=1, source_target_pairs={{0,24},{4,28},{8,16},{12,20},{16,8},{20,12},{24,0},{28,4},{1,25},{... | collective-permute-start | bytes 245768 | tf_op jit(solution)/shard_map/ppermute | solution.py:334
  27.8 5.9 %collective-permute-start.7 = (bf16[8,5120]{1,0:T(8,128)(2,1)S(1)}, bf16[8,5120]{1,0:T(8,128)(2,1)S(1)}, u32[]{:S(2)}, u32[]{:S(2)}) collective-permute-start(bf16[8,5120]{1,0:T(8,128)(2,1)S(1)} %get-tuple-element.40.refs_0_), channel_id=1, source_target_pairs={{0,16},{4,20},{8,24},{12,28},{16,0},{20,4},{24,8},{28,12},{1,17},{... | collective-permute-start | bytes 245768 | tf_op jit(solution)/shard_map/ppermute | solution.py:334
  29.3 4.4 %collective-permute-start.6 = (bf16[8,5120]{1,0:T(8,128)(2,1)S(1)}, bf16[8,5120]{1,0:T(8,128)(2,1)S(1)}, u32[]{:S(2)}, u32[]{:S(2)}) collective-permute-start(bf16[8,5120]{1,0:T(8,128)(2,1)S(1)} %get-tuple-element.40.refs_0_), channel_id=1, source_target_pairs={{0,8},{4,12},{8,0},{12,4},{16,24},{20,28},{24,16},{28,20},{1,9},{5... | collective-permute-start | bytes 245768 | tf_op jit(solution)/shard_map/ppermute | solution.py:334
  33.8 1.7 %collective-permute-start.9 = (bf16[4,8,5120]{2,1,0:T(8,128)(2,1)S(1)}, bf16[4,8,5120]{2,1,0:T(8,128)(2,1)S(1)}, u32[]{:S(2)}, u32[]{:S(2)}) collective-permute-start(bf16[4,8,5120]{2,1,0:T(8,128)(2,1)S(1)} %join_kept.1.mine), channel_id=1, source_target_pairs={{0,4},{4,0},{8,12},{12,8},{16,20},{20,16},{24,28},{28,24},{1,5},{5... | collective-permute-start | bytes 983048 | tf_op jit(solution)/shard_map/ppermute | solution.py:334

commit v13 on v9

--- a/solution.py
+++ b/solution.py
@@ -118,7 +118,7 @@
     copies[2].wait()
     nc = cols // cp
     for k in range(n_t):
-        c0 = lax.rem(ten + k, n_t) * cols + lax.rem(rep, cp) * nc
+        c0 = (ten ^ k) * cols + lax.rem(rep, cp) * nc
         for j in range(nc // 128):
             at = pl.multiple_of(c0 + j * 128, 128)
             outs[k][B + j * nr : B + (j + 1) * nr, :] = exp_v[:, pl.ds(at, 128)]
@@ -126,7 +126,7 @@
         copy.wait()
 
 
-def grads_body(n, act, after, *refs):
+def grads_body(n, act, *refs):
     ups, outs = refs[:n], refs[n:]
     up = jnp.concatenate([u[:B, :] for u in ups], axis=0)
     for c in range(0, act.shape[1], G):
@@ -197,7 +197,7 @@
     lane_block = lax.broadcasted_iota(jnp.int32, (keep, G), 1) // B
     sel = []
     for n, k in enumerate(ks):
-        c0 = lax.rem(lax.axis_index("tensor") + k, n_t) * cols
+        c0 = (lax.axis_index("tensor") ^ k) * cols
         for i in range(ng):
             at = pl.multiple_of(c0 + i * G, G)
             moment = momentum_decay * vel[:, pl.ds(at, G)] + grads[n][:, i * G : (i + 1) * G].astype(F32)
@@ -214,7 +214,7 @@
     kept = (y[:n] + y[n:] + dot(hi, fwd(tab, 1))).astype(BF16)
     q = dot(kept, inv(tab, 0)) + dot(kept, inv(tab, 1))
     for n, k in enumerate(ks):
-        c0 = pl.multiple_of(lax.rem(lax.axis_index("tensor") + k, n_t) * cols, G)
+        c0 = pl.multiple_of((lax.axis_index("tensor") ^ k) * cols, G)
         part = jnp.concatenate([q[(n * ng + i) * keep : (n * ng + i + 1) * keep] for i in range(ng)], axis=1)
         own_ref[:, pl.ds(c0, cols)] = part
         send_ref[:, pl.ds(c0, cols)] = part.astype(BF16)
@@ -227,7 +227,7 @@
     lane_block = lax.broadcasted_iota(jnp.int32, (keep, G), 1) // B
     copies = []
     for k in range(n_t):
-        c0 = pl.multiple_of(lax.rem(lax.axis_index("tensor") + k, n_t) * cols, G)
+        c0 = pl.multiple_of((lax.axis_index("tensor") ^ k) * cols, G)
         for i in range(ng):
             at = pl.multiple_of(c0 + i * G, G)
             own = q[:, pl.ds(at, G)]
@@ -294,23 +294,26 @@
         copy.wait()
 
 
-def input_grad_body(n_t, n_r, cp, mine, other, *refs):
-    ups, out, held = refs[:n_t], refs[n_t], refs[n_t + 1]
-    nc = out.shape[1] // cp
-    nr = B // (n_r // cp)
+def input_grad_body(n_t, h, bundles, *refs):
+    ups, (out, held, ready, sem) = refs[:n_t], refs[-4:]
+    half = bundles.shape[0]
+    nc, nr = held.shape[1], B // half
     tiles = nc // 128
-    for m in range(n_r):
-        src = lax.axis_index("replica") ^ m
-        r0, c0 = (src // cp) * nr, lax.rem(src, cp) * nc
-        ref = (mine, other)[m % 2]
+    rep = lax.axis_index("replica")
+    for i in range(half):
+        r0 = ((rep ^ (2 * i + h)) // 2) * nr
         for k in range(n_t):
             row = pl.multiple_of(k * B + r0, nr)
             for j in range(tiles):
                 at = (k * tiles + j) * nr
-                held[pl.ds(row, nr), pl.ds(pl.multiple_of(c0 + j * 128, 128), 128)] = ref[m // 2, at : at + nr, :]
+                held[pl.ds(row, nr), j * 128 : (j + 1) * 128] = bundles[i, at : at + nr, :]
     up = jnp.concatenate([u[:B, :] for u in ups], axis=0).T
-    for c in range(0, out.shape[1], G):
-        out[:, c : c + G] = dot(up, held[:, c : c + G]).astype(BF16)
+    for c in range(0, nc, 128):
+        ready[:, c : c + 128] = dot(up, held[:, c : c + 128]).astype(BF16)
+    c0 = pl.multiple_of(lax.rem(rep ^ h, 2) * nc, 128)
+    copy = pltpu.make_async_copy(ready, out.at[:, pl.ds(c0, nc)], sem)
+    copy.start()
+    copy.wait()
 
 
 def per_device(n_t, n_r, act, switch, slope, exp, vel, lines, mask, tally):
@@ -324,8 +327,10 @@
     rp = n_r // cp
     half = n_r // 2
     tab, tall = constants()
-    def shift(x, k):
-        return lax.ppermute(x, "tensor", [(i, (i + k) % n_t) for i in range(n_t)])
+    def trade(x, k):
+        return lax.ppermute(x, "tensor", [(i, i ^ k) for i in range(n_t)])
+
+    order = [*range(2, n_t), 1]
 
     def swap(x, m):
         return lax.ppermute(x, "replica", [(i, i ^ m) for i in range(n_r)])
@@ -360,26 +365,25 @@
         nbytes=act.size * 4 + nr * width * 2,
         name="up_grads",
     )
-    parts = [parts[0]] + [shift(parts[k], k) for k in range(1, n_t)]
-
-    def grads_of(ks, after):
+    got = {k: trade(parts[k], k) for k in order}
+    parts = [parts[0]] + [got[k] for k in range(1, n_t)]
+
+    def grads_of(ks):
         return call(
             functools.partial(grads_body, len(ks)),
             [near((B, cols), BF16 if k else F32) for k in ks],
-            (act, after, *[parts[k] for k in ks]),
-            [VM, ANY] + [VM] * len(ks),
+            (act, *[parts[k] for k in ks]),
+            [VM] * (1 + len(ks)),
             [VM] * len(ks),
             name="weight_grads",
         )
 
     grads = {}
-    made = act
-    for k in range(1, n_t - 1):
-        (made,) = grads_of([k], made)
-        grads[k] = made
-    made, grads[0] = grads_of([n_t - 1, 0], made)
-    grads[n_t - 1] = made
-    grads = [grads[0]] + [shift(grads[k], -k) for k in range(1, n_t)]
+    for k in order[:-1]:
+        (grads[k],) = grads_of([k])
+    made, grads[0] = grads_of([order[-1], 0])
+    grads[order[-1]] = made
+    grads.update({k: trade(grads[k], k) for k in order})
 
     bundle = call(
         functools.partial(bundle_body, n_t, keep),
@@ -416,17 +420,26 @@
         )
         for h in range(2)
     ]
-    input_grad = call(
-        functools.partial(input_grad_body, n_t, n_r, cp),
-        jax.ShapeDtypeStruct((tok, cols), BF16),
-        (*bundles, *parts),
-        [VM] * (2 + n_t),
-        VM,
-        scratch=[pltpu.VMEM((n_t * B, cols), BF16)],
-        flops=2 * tok * n_t * B * cols,
-        nbytes=(n_t * B * cols + tok * cols) * 2,
-        name="input_grads",
-    )
+    input_grad = []
+    for h in range(2):
+        input_grad = [
+            call(
+                functools.partial(input_grad_body, n_t, h),
+                jax.ShapeDtypeStruct((tok, cols), BF16),
+                (bundles[h], *parts, *[far(x) for x in input_grad]),
+                [VM] * (1 + n_t) + [ANY] * len(input_grad),
+                ANY,
+                scratch=[
+                    pltpu.VMEM((n_t * B, cols // cp), BF16),
+                    pltpu.VMEM((tok, cols // cp), BF16),
+                    pltpu.SemaphoreType.DMA,
+                ],
+                name="input_grads",
+                alias={1 + n_t: 0} if input_grad else {},
+            )
+        ]
+        first_half = input_grad[0] if h == 0 else first_half
+    input_grad = input_grad[0]
 
     rows = []
     for ks in (list(range(n_t - 1)), [n_t - 1]):
@@ -445,7 +458,7 @@
     new = call(
         functools.partial(return_body, n_t, keep),
         jax.ShapeDtypeStruct((B, width), F32),
-        (vel[0], p_own, q_own, *grads),
+        (vel[0], p_own, q_own, *[grads[k] for k in range(n_t)]),
         [VM] * (3 + n_t),
         ANY,
         scratch=[pltpu.VMEM((B, width), F32), pltpu.SemaphoreType.DMA((n_t,))],
@@ -453,7 +466,7 @@
         nbytes=B * width * 10,
         name="new_momentums",
     )
-    mine, other = share(ship, "join_kept", (far(new),))
+    mine, other = share(ship, "join_kept", (far(new), places[0][0], far(first_half)))
     half_sum = call(
         half_update_body,
         near((groups * B, G), F32),
@@ -541,6 +554,8 @@
             and exp.shape[0] == B
             and lines.shape[3] == 8
             and n_r == 8
+            and n_t >= 2
+            and n_t & (n_t - 1) == 0
         )
         if not fits:
             return per_device_plain(*args)

time: 38.2 us -> 37.3 us (0.976)
  starting transfers between devices: 19.7 us -> 17.2 us
  Pallas kernels: 9.22 us -> 10 us
  waiting for transfers between devices: 8.23 us -> 9.01 us
    ppermute x6, starting transfers between devices: 11.4 us -> 10 us  [trade(): return lax.ppermute(x, 'tensor', [(i, i ^ k) for i in range(n_t)])]
    ppermute x6, waiting for transfers between devices: 6.82 us -> 7.94 us  [trade(): return lax.ppermute(x, 'tensor', [(i, i ^ k) for i in range(n_t)])]
    ppermute x8, starting transfers between devices: 8.31 us -> 7.24 us  [swap(): return lax.ppermute(x, 'replica', [(i, i ^ m) for i in range(n_r)])]
    pallas_call x16 -> x17, Pallas kernels: 9.22 us -> 10 us  [call(): pl.pallas_call(body, out_shape=out_shape, in_specs=in_specs, out_specs=ou...]
  transfers between devices with their start and end apart: 14 -> 14, of which waited for: 5 -> 5; matrix products, arithmetic and copies ran while one was open for 0% -> 0% of each run, Pallas kernels for 18% -> 20%
where the time goes in v13:
time: 37.3 us; the launch traced here: 37.1 us
  starting transfers between devices  17.2 us (46%)
  Pallas kernels  10 us (27%)
  waiting for transfers between devices  9.01 us (24%)
  between operations  0.79 us (2%)
    pallas_call x17, Pallas kernels, call(): pl.pallas_call(body, out_shape=out_shape, in_specs=in_specs, out_specs=ou...  10 us
    ppermute x6, starting transfers between devices, trade(): return lax.ppermute(x, 'tensor', [(i, i ^ k) for i in range(n_t)])  10 us
    ppermute x6, waiting for transfers between devices, trade(): return lax.ppermute(x, 'tensor', [(i, i ^ k) for i in range(n_t)])  7.94 us
    ppermute x8, starting transfers between devices, swap(): return lax.ppermute(x, 'replica', [(i, i ^ m) for i in range(n_r)])  7.24 us
    ppermute x8, waiting for transfers between devices, swap(): return lax.ppermute(x, 'replica', [(i, i ^ m) for i in range(n_r)])  1.07 us
  transfers between devices with their start and end apart: 14, of which 5 were waited for; matrix products, arithmetic and copies ran while one was open for 0% of the time, Pallas kernels for 20%

profile of v13, /device:TPU:0, one launch (start us, length us, event | category | flops | bytes accessed | tf_op | source)
XLA Modules:
  0.0 37.1 jit_solution(10829492476277873930)
XLA Ops:
  0.6 1.2 %up_grads.1 = (bf16[144,128]{1,0:T(8,128)(2,1)S(1)}, bf16[144,128]{1,0:T(8,128)(2,1)S(1)}, bf16[144,128]{1,0:T(8,128)(2,1)S(1)}, bf16[144,128]{1,0:T(8,128)(2,1)...) custom-call(bf16[64,128]{1,0:T(8,128)(2,1)} %bitcast.11, ...), custom_call_target="tpu_custom_call" | custom-call | bytes 819200 | tf_op jit(solution)/shard_map/up_grads/pallas_call | solution.py:79
  1.8 0.0 copy-start
  1.8 3.1 %collective-permute-start = (bf16[144,128]{1,0:T(8,128)(2,1)S(1)}, bf16[144,128]{1,0:T(8,128)(2,1)S(1)}, u32[]{:S(2)}, u32[]{:S(2)}) collective-permute-start(bf16[144,128]{1,0:T(8,128)(2,1)S(1)} %get-tuple-element.25), channel_id=1, source_target_pairs={{0,1},{1,0},{2,3},{3,2},{4,5},{5,4},{6,7},{7,6},{8,9},{9,8},{10,11... | collective-permute-start | bytes 110600 | tf_op jit(solution)/shard_map/ppermute | solution.py:331
  4.9 2.6 %collective-permute-start.1 = (bf16[144,128]{1,0:T(8,128)(2,1)S(1)}, bf16[144,128]{1,0:T(8,128)(2,1)S(1)}, u32[]{:S(2)}, u32[]{:S(2)}) collective-permute-start(bf16[144,128]{1,0:T(8,128)(2,1)S(1)} %get-tuple-element.29), channel_id=1, source_target_pairs={{0,2},{1,3},{2,0},{3,1},{4,6},{5,7},{6,4},{7,5},{8,10},{9,11},{10,... | collective-permute-start | bytes 110600 | tf_op jit(solution)/shard_map/ppermute | solution.py:331
  7.5 0.0 collective-permute-start.2
  7.5 0.0 collective-permute-done.refs_0_.refs_1_
  7.5 0.2 weight_grads.3
  7.7 1.4 %collective-permute-start.8 = (bf16[64,1280]{1,0:T(8,128)(2,1)S(1)}, bf16[64,1280]{1,0:T(8,128)(2,1)S(1)}, u32[]{:S(2)}, u32[]{:S(2)}) collective-permute-start(bf16[64,1280]{1,0:T(8,128)(2,1)S(1)} %get-tuple-element.27.after), channel_id=1, source_target_pairs={{0,1},{1,0},{2,3},{3,2},{4,5},{5,4},{6,7},{7,6},{8,9},{9,8},{10,11... | collective-permute-start | bytes 491528 | tf_op jit(solution)/shard_map/ppermute | solution.py:331
  9.2 1.4 %collective-permute-done.1.refs_2_.refs_0_ = bf16[144,128]{1,0:T(8,128)(2,1)S(1)} collective-permute-done((bf16[144,128]{1,0:T(8,128)(2,1)S(1)}, bf16[144,128]{1,0:T(8,128)(2,1)S(1)}, u32[]{:S(2)}, u32[]{:S(2)}) %collective-permute-start.1) | collective-permute-done | bytes 36896 | tf_op jit(solution)/shard_map/ppermute | solution.py:331
  10.5 0.2 weight_grads.5
  10.7 2.2 %collective-permute-start.9 = (bf16[64,1280]{1,0:T(8,128)(2,1)S(1)}, bf16[64,1280]{1,0:T(8,128)(2,1)S(1)}, u32[]{:S(2)}, u32[]{:S(2)}) collective-permute-start(bf16[64,1280]{1,0:T(8,128)(2,1)S(1)} %weight_grads.5), channel_id=1, source_target_pairs={{0,2},{1,3},{2,0},{3,1},{4,6},{5,7},{6,4},{7,5},{8,10},{9,11},{10,... | collective-permute-start | bytes 491528 | tf_op jit(solution)/shard_map/ppermute | solution.py:331
  12.9 0.8 %collective-permute-done.2.refs_3_.refs_0_ = bf16[144,128]{1,0:T(8,128)(2,1)S(1)} collective-permute-done((bf16[144,128]{1,0:T(8,128)(2,1)S(1)}, bf16[144,128]{1,0:T(8,128)(2,1)S(1)}, u32[]{:S(2)}, u32[]{:S(2)}) %collective-permute-start.2) | collective-permute-done | bytes 36896 | tf_op jit(solution)/shard_map/ppermute | solution.py:331
  13.8 0.2 weight_grads.4
  13.9 0.7 %collective-permute-start.7 = (bf16[64,1280]{1,0:T(8,128)(2,1)S(1)}, bf16[64,1280]{1,0:T(8,128)(2,1)S(1)}, u32[]{:S(2)}, u32[]{:S(2)}) collective-permute-start(bf16[64,1280]{1,0:T(8,128)(2,1)S(1)} %weight_grads.4), channel_id=1, source_target_pairs={{0,3},{1,2},{2,1},{3,0},{4,7},{5,6},{6,5},{7,4},{8,11},{9,10},{10,... | collective-permute-start | bytes 491528 | tf_op jit(solution)/shard_map/ppermute | solution.py:331
  14.6 2.5 %collective-permute-start.5 = (bf16[336,128]{1,0:T(8,128)(2,1)S(1)}, bf16[336,128]{1,0:T(8,128)(2,1)S(1)}, u32[]{:S(2)}, u32[]{:S(2)}) collective-permute-start(bf16[336,128]{1,0:T(8,128)(2,1)S(1)} %bundle.1.refs_0_), channel_id=1, source_target_pairs={{0,24},{4,28},{8,16},{12,20},{16,8},{20,12},{24,0},{28,4},{1,25},{... | collective-permute-start | bytes 258056 | tf_op jit(solution)/shard_map/ppermute | solution.py:336
  17.2 0.5 %collective-permute-start.4 = (bf16[336,128]{1,0:T(8,128)(2,1)S(1)}, bf16[336,128]{1,0:T(8,128)(2,1)S(1)}, u32[]{:S(2)}, u32[]{:S(2)}) collective-permute-start(bf16[336,128]{1,0:T(8,128)(2,1)S(1)} %bundle.1.refs_0_), channel_id=1, source_target_pairs={{0,16},{4,20},{8,24},{12,28},{16,0},{20,4},{24,8},{28,12},{1,17},{... | collective-permute-start | bytes 258056 | tf_op jit(solution)/shard_map/ppermute | solution.py:336
  17.7 0.0 collective-permute-done.8.refs_1_
  17.7 0.5 %collective-permute-start.3 = (bf16[336,128]{1,0:T(8,128)(2,1)S(1)}, bf16[336,128]{1,0:T(8,128)(2,1)S(1)}, u32[]{:S(2)}, u32[]{:S(2)}) collective-permute-start(bf16[336,128]{1,0:T(8,128)(2,1)S(1)} %bundle.1.refs_0_), channel_id=1, source_target_pairs={{0,8},{4,12},{8,0},{12,4},{16,24},{20,28},{24,16},{28,20},{1,9},{5... | collective-permute-start | bytes 258056 | tf_op jit(solution)/shard_map/ppermute | solution.py:336
  18.2 1.1 %own_places.1 = (bf16[64,2560]{1,0:T(8,128)(2,1)S(1)}, bf16[1280,128]{1,0:T(8,128)(2,1)S(1)}, f32[2,8,128]{2,1,0:T(8,128)S(1)}, bf16[1024,256]{1,0:T(8,128)(2,1)S(1)}) custom-call(s32[8]{0:T(128)} %mask.1, s32[8]{0:T(128)} %tally.1, bf16[1024,256]{1,0:T(8,128)(2,1)} %constant.4.clone.tab, s32[8,80]{1,0:T(8,128)S(1)} %get-tuple-element.28.lines, ...), custom_call_target="tpu_custom_call" | custom-call | tf_op jit(solution)/shard_map/own_places/pallas_call | solution.py:79
  19.3 5.7 %collective-permute-done.9.refs_2_ = bf16[64,1280]{1,0:T(8,128)(2,1)S(1)} collective-permute-done((bf16[64,1280]{1,0:T(8,128)(2,1)S(1)}, bf16[64,1280]{1,0:T(8,128)(2,1)S(1)}, u32[]{:S(2)}, u32[]{:S(2)}) %collective-permute-start.9) | collective-permute-done | bytes 163872 | tf_op jit(solution)/shard_map/ppermute | solution.py:331
  25.0 0.0 copy-done
  25.0 0.7 %kept_rows.2 = (bf16[8,5120]{1,0:T(8,128)(2,1)S(1)}, f32[8,5120]{1,0:T(8,128)S(1)}) custom-call(f32[64,5120]{1,0:T(8,128)S(1)} %bitcast.7, bf16[1280,128]{1,0:T(8,128)(2,1)S(1)} %get-tuple-element.33.a_ref, bf16[1024,256]{1,0:T(8,128)(2,1)S(1)} %get-tuple-element.34.tab, f32[64,1280]{1,0:T(8,128)S(1)} %get-tuple-element.35.refs_0_, ...), custom_call_target="tpu_custom_call" | custom-call | flops 94371840 | bytes 1474560 | tf_op jit(solution)/shard_map/kept_rows/pallas_call | solution.py:79
  25.7 0.0 collective-permute-done.7.refs_0_.refs_3_
  25.7 0.5 %kept_rows.3 = (bf16[8,5120]{1,0:T(8,128)(2,1)S(1)}, f32[8,5120]{1,0:T(8,128)S(1)}) custom-call(f32[64,5120]{1,0:T(8,128)S(1)} %bitcast.8, bf16[1280,128]{1,0:T(8,128)(2,1)S(1)} %get-tuple-element.33.a_ref, bf16[1024,256]{1,0:T(8,128)(2,1)S(1)} %get-tuple-element.34.tab, ...), custom_call_target="tpu_custom_call", output_to_operand_aliasing={{0}: (4, {}), {1}: (5, {})} | custom-call | flops 31457280 | bytes 491520 | tf_op jit(solution)/shard_map/kept_rows/pallas_call | solution.py:79
  26.2 2.5 %collective-permute-start.12 = (bf16[8,5120]{1,0:T(8,128)(2,1)S(1)}, bf16[8,5120]{1,0:T(8,128)(2,1)S(1)}, u32[]{:S(2)}, u32[]{:S(2)}) collective-permute-start(bf16[8,5120]{1,0:T(8,128)(2,1)S(1)} %get-tuple-element.42.refs_0_), channel_id=1, source_target_pairs={{0,24},{4,28},{8,16},{12,20},{16,8},{20,12},{24,0},{28,4},{1,25},{... | collective-permute-start | bytes 245768 | tf_op jit(solution)/shard_map/ppermute | solution.py:336
  28.7 0.5 %collective-permute-start.11 = (bf16[8,5120]{1,0:T(8,128)(2,1)S(1)}, bf16[8,5120]{1,0:T(8,128)(2,1)S(1)}, u32[]{:S(2)}, u32[]{:S(2)}) collective-permute-start(bf16[8,5120]{1,0:T(8,128)(2,1)S(1)} %get-tuple-element.42.refs_0_), channel_id=1, source_target_pairs={{0,16},{4,20},{8,24},{12,28},{16,0},{20,4},{24,8},{28,12},{1,17},{... | collective-permute-start | bytes 245768 | tf_op jit(solution)/shard_map/ppermute | solution.py:336
  29.2 0.0 collective-permute-done.5.refs_3_
  29.2 0.5 %collective-permute-start.10 = (bf16[8,5120]{1,0:T(8,128)(2,1)S(1)}, bf16[8,5120]{1,0:T(8,128)(2,1)S(1)}, u32[]{:S(2)}, u32[]{:S(2)}) collective-permute-start(bf16[8,5120]{1,0:T(8,128)(2,1)S(1)} %get-tuple-element.42.refs_0_), channel_id=1, source_target_pairs={{0,8},{4,12},{8,0},{12,4},{16,24},{20,28},{24,16},{28,20},{1,9},{5... | collective-permute-start | bytes 245768 | tf_op jit(solution)/shard_map/ppermute | solution.py:336
  29.8 0.0 collective-permute-done.4.refs_2_
  29.8 0.0 collective-permute-done.3.refs_1_
  29.8 0.1 collective-permute-start.6
  29.9 0.4 %places.2 = (bf16[64,2560]{1,0:T(8,128)(2,1)S(1)}, bf16[64,2560]{1,0:T(8,128)(2,1)S(1)}) custom-call(f32[2,8,128]{2,1,0:T(8,128)S(1)} %get-tuple-element.39.w_ref, bf16[128,128]{1,0:T(8,128)(2,1)S(1)} %get-tuple-element.31.tall, bf16[4,336,128]{2,1,0:T(8,128)(2,1)S(1)} %join_bundles.1.bundles), custom_call_target="tpu_custom_call" | custom-call | tf_op jit(solution)/shard_map/places/pallas_call | solution.py:79
  30.3 1.0 %input_grads.2.refs_4_.refs_6_ = bf16[128,1280]{1,0:T(8,128)(2,1)} custom-call(bf16[4,336,128]{2,1,0:T(8,128)(2,1)S(1)} %join_bundles.1.bundles, bf16[144,128]{1,0:T(8,128)(2,1)S(1)} %get-tuple-element.26.refs_1_.refs_0_, bf16[144,128]{1,0:T(8,128)(2,1)S(1)} %collective-permute-done.refs_0_.refs_1_, ...), custom_call_target="tpu_custom_call" | custom-call | tf_op jit(solution)/shard_map/input_grads/pallas_call | solution.py:79
  31.3 1.3 %new_momentums.1.refs_4_ = f32[64,5120]{1,0:T(8,128)} custom-call(f32[64,5120]{1,0:T(8,128)S(1)} %bitcast.9, bf16[64,2560]{1,0:T(8,128)(2,1)S(1)} %get-tuple-element.32.p_ref, f32[8,5120]{1,0:T(8,128)S(1)} %get-tuple-element.38.q, f32[64,1280]{1,0:T(8,128)S(1)} %get-tuple-element.35.refs_0_, bf16[64,1280]{1,0:T(8,128)(2,1)S(1)} %collective-permute-done.8.refs_1_, ...), custom_call_target="tpu_custom_call" | custom-call | flops 125829120 | bytes 3276800 | tf_op jit(solution)/shard_map/new_momentums/pallas_call | solution.py:79
  32.6 0.0 collective-permute-done.12.refs_3_
  32.6 0.6 %collective-permute-done.11.refs_2_ = bf16[8,5120]{1,0:T(8,128)(2,1)S(1)} collective-permute-done((bf16[8,5120]{1,0:T(8,128)(2,1)S(1)}, bf16[8,5120]{1,0:T(8,128)(2,1)S(1)}, u32[]{:S(2)}, u32[]{:S(2)}) %collective-permute-start.11) | collective-permute-done | bytes 81952 | tf_op jit(solution)/shard_map/ppermute | solution.py:336
  33.2 0.5 %collective-permute-done.10.refs_1_ = bf16[8,5120]{1,0:T(8,128)(2,1)S(1)} collective-permute-done((bf16[8,5120]{1,0:T(8,128)(2,1)S(1)}, bf16[8,5120]{1,0:T(8,128)(2,1)S(1)}, u32[]{:S(2)}, u32[]{:S(2)}) %collective-permute-start.10) | collective-permute-done | bytes 81952 | tf_op jit(solution)/shard_map/ppermute | solution.py:336
  33.7 0.1 collective-permute-start.13
  33.8 0.5 %half_updates.1.half_sum = f32[1280,256]{1,0:T(8,128)S(1)} custom-call(bf16[64,2560]{1,0:T(8,128)(2,1)S(1)} %get-tuple-element.40.refs_5_.p_hi, bf16[64,2560]{1,0:T(8,128)(2,1)S(1)} %get-tuple-element.41.p_lo, bf16[4,8,5120]{2,1,0:T(8,128)(2,1)S(1)} %join_kept.1.mine), custom_call_target="tpu_custom_call" | custom-call | tf_op jit(solution)/shard_map/half_updates/pallas_call | solution.py:79
  34.3 0.0 collective-permute-done.6.bundles
  34.3 1.0 %input_grads.3 = bf16[128,1280]{1,0:T(8,128)(2,1)} custom-call(bf16[4,336,128]{2,1,0:T(8,128)(2,1)S(1)} %collective-permute-done.6.bundles, bf16[144,128]{1,0:T(8,128)(2,1)S(1)} %get-tuple-element.26.refs_1_.refs_0_, bf16[144,128]{1,0:T(8,128)(2,1)S(1)} %collective-permute-done.refs_0_.refs_1_, ...), custom_call_target="tpu_custom_call", output_to_operand_aliasing={{}: (5, {})} | custom-call | tf_op jit(solution)/shard_map/input_grads/pallas_call | solution.py:79
  35.3 0.4 %places.3 = (bf16[64,2560]{1,0:T(8,128)(2,1)S(1)}, bf16[64,2560]{1,0:T(8,128)(2,1)S(1)}) custom-call(f32[2,8,128]{2,1,0:T(8,128)S(1)} %get-tuple-element.39.w_ref, bf16[128,128]{1,0:T(8,128)(2,1)S(1)} %get-tuple-element.31.tall, bf16[4,336,128]{2,1,0:T(8,128)(2,1)S(1)} %collective-permute-done.6.bundles), custom_call_target="tpu_custom_call" | custom-call | tf_op jit(solution)/shard_map/places/pallas_call | solution.py:79
  35.7 0.0 collective-permute-done.13.other
  35.7 1.3 %updates.1 = f32[64,5120]{1,0:T(8,128)} custom-call(f32[1280,256]{1,0:T(8,128)S(1)} %half_updates.1.half_sum, bf16[64,2560]{1,0:T(8,128)(2,1)S(1)} %get-tuple-element.43.p_hi, bf16[64,2560]{1,0:T(8,128)(2,1)S(1)} %get-tuple-element.44.p_lo, bf16[4,8,5120]{2,1,0:T(8,128)(2,1)S(1)} %collective-permute-done.13.other), custom_call_target="tpu_custom_call" | custom-call | flops 671088640 | bytes 2621440 | tf_op jit(solution)/shard_map/updates/pallas_call | solution.py:79
  (3 shorter events, 0.1 us)
Async XLA Ops:
  1.8 23.2 %copy-start = (f32[1,64,5120]{2,1,0:T(8,128)S(1)}, f32[1,64,5120]{2,1,0:T(8,128)}, u32[]{:S(2)}) copy-start(f32[1,64,5120]{2,1,0:T(8,128)} %param.14) | copy-start | bytes 3932164
  1.8 5.7 %collective-permute-start = (bf16[144,128]{1,0:T(8,128)(2,1)S(1)}, bf16[144,128]{1,0:T(8,128)(2,1)S(1)}, u32[]{:S(2)}, u32[]{:S(2)}) collective-permute-start(bf16[144,128]{1,0:T(8,128)(2,1)S(1)} %get-tuple-element.25), channel_id=1, source_target_pairs={{0,1},{1,0},{2,3},{3,2},{4,5},{5,4},{6,7},{7,6},{8,9},{9,8},{10,11... | collective-permute-start | bytes 110600 | tf_op jit(solution)/shard_map/ppermute | solution.py:331
  4.9 5.6 %collective-permute-start.1 = (bf16[144,128]{1,0:T(8,128)(2,1)S(1)}, bf16[144,128]{1,0:T(8,128)(2,1)S(1)}, u32[]{:S(2)}, u32[]{:S(2)}) collective-permute-start(bf16[144,128]{1,0:T(8,128)(2,1)S(1)} %get-tuple-element.29), channel_id=1, source_target_pairs={{0,2},{1,3},{2,0},{3,1},{4,6},{5,7},{6,4},{7,5},{8,10},{9,11},{10,... | collective-permute-start | bytes 110600 | tf_op jit(solution)/shard_map/ppermute | solution.py:331
  7.5 6.3 %collective-permute-start.2 = (bf16[144,128]{1,0:T(8,128)(2,1)S(1)}, bf16[144,128]{1,0:T(8,128)(2,1)S(1)}, u32[]{:S(2)}, u32[]{:S(2)}) collective-permute-start(bf16[144,128]{1,0:T(8,128)(2,1)S(1)} %get-tuple-element.30), channel_id=1, source_target_pairs={{0,3},{1,2},{2,1},{3,0},{4,7},{5,6},{6,5},{7,4},{8,11},{9,10},{10,... | collective-permute-start | bytes 110600 | tf_op jit(solution)/shard_map/ppermute | solution.py:331
  7.7 9.9 %collective-permute-start.8 = (bf16[64,1280]{1,0:T(8,128)(2,1)S(1)}, bf16[64,1280]{1,0:T(8,128)(2,1)S(1)}, u32[]{:S(2)}, u32[]{:S(2)}) collective-permute-start(bf16[64,1280]{1,0:T(8,128)(2,1)S(1)} %get-tuple-element.27.after), channel_id=1, source_target_pairs={{0,1},{1,0},{2,3},{3,2},{4,5},{5,4},{6,7},{7,6},{8,9},{9,8},{10,11... | collective-permute-start | bytes 491528 | tf_op jit(solution)/shard_map/ppermute | solution.py:331
  10.7 14.3 %collective-permute-start.9 = (bf16[64,1280]{1,0:T(8,128)(2,1)S(1)}, bf16[64,1280]{1,0:T(8,128)(2,1)S(1)}, u32[]{:S(2)}, u32[]{:S(2)}) collective-permute-start(bf16[64,1280]{1,0:T(8,128)(2,1)S(1)} %weight_grads.5), channel_id=1, source_target_pairs={{0,2},{1,3},{2,0},{3,1},{4,6},{5,7},{6,4},{7,5},{8,10},{9,11},{10,... | collective-permute-start | bytes 491528 | tf_op jit(solution)/shard_map/ppermute | solution.py:331
  13.9 11.8 %collective-permute-start.7 = (bf16[64,1280]{1,0:T(8,128)(2,1)S(1)}, bf16[64,1280]{1,0:T(8,128)(2,1)S(1)}, u32[]{:S(2)}, u32[]{:S(2)}) collective-permute-start(bf16[64,1280]{1,0:T(8,128)(2,1)S(1)} %weight_grads.4), channel_id=1, source_target_pairs={{0,3},{1,2},{2,1},{3,0},{4,7},{5,6},{6,5},{7,4},{8,11},{9,10},{10,... | collective-permute-start | bytes 491528 | tf_op jit(solution)/shard_map/ppermute | solution.py:331
  14.6 14.6 %collective-permute-start.5 = (bf16[336,128]{1,0:T(8,128)(2,1)S(1)}, bf16[336,128]{1,0:T(8,128)(2,1)S(1)}, u32[]{:S(2)}, u32[]{:S(2)}) collective-permute-start(bf16[336,128]{1,0:T(8,128)(2,1)S(1)} %bundle.1.refs_0_), channel_id=1, source_target_pairs={{0,24},{4,28},{8,16},{12,20},{16,8},{20,12},{24,0},{28,4},{1,25},{... | collective-permute-start | bytes 258056 | tf_op jit(solution)/shard_map/ppermute | solution.py:336
  17.2 12.6 %collective-permute-start.4 = (bf16[336,128]{1,0:T(8,128)(2,1)S(1)}, bf16[336,128]{1,0:T(8,128)(2,1)S(1)}, u32[]{:S(2)}, u32[]{:S(2)}) collective-permute-start(bf16[336,128]{1,0:T(8,128)(2,1)S(1)} %bundle.1.refs_0_), channel_id=1, source_target_pairs={{0,16},{4,20},{8,24},{12,28},{16,0},{20,4},{24,8},{28,12},{1,17},{... | collective-permute-start | bytes 258056 | tf_op jit(solution)/shard_map/ppermute | solution.py:336
  17.7 12.1 %collective-permute-start.3 = (bf16[336,128]{1,0:T(8,128)(2,1)S(1)}, bf16[336,128]{1,0:T(8,128)(2,1)S(1)}, u32[]{:S(2)}, u32[]{:S(2)}) collective-permute-start(bf16[336,128]{1,0:T(8,128)(2,1)S(1)} %bundle.1.refs_0_), channel_id=1, source_target_pairs={{0,8},{4,12},{8,0},{12,4},{16,24},{20,28},{24,16},{28,20},{1,9},{5... | collective-permute-start | bytes 258056 | tf_op jit(solution)/shard_map/ppermute | solution.py:336
  26.2 6.4 %collective-permute-start.12 = (bf16[8,5120]{1,0:T(8,128)(2,1)S(1)}, bf16[8,5120]{1,0:T(8,128)(2,1)S(1)}, u32[]{:S(2)}, u32[]{:S(2)}) collective-permute-start(bf16[8,5120]{1,0:T(8,128)(2,1)S(1)} %get-tuple-element.42.refs_0_), channel_id=1, source_target_pairs={{0,24},{4,28},{8,16},{12,20},{16,8},{20,12},{24,0},{28,4},{1,25},{... | collective-permute-start | bytes 245768 | tf_op jit(solution)/shard_map/ppermute | solution.py:336
  28.7 4.4 %collective-permute-start.11 = (bf16[8,5120]{1,0:T(8,128)(2,1)S(1)}, bf16[8,5120]{1,0:T(8,128)(2,1)S(1)}, u32[]{:S(2)}, u32[]{:S(2)}) collective-permute-start(bf16[8,5120]{1,0:T(8,128)(2,1)S(1)} %get-tuple-element.42.refs_0_), channel_id=1, source_target_pairs={{0,16},{4,20},{8,24},{12,28},{16,0},{20,4},{24,8},{28,12},{1,17},{... | collective-permute-start | bytes 245768 | tf_op jit(solution)/shard_map/ppermute | solution.py:336
  29.2 4.4 %collective-permute-start.10 = (bf16[8,5120]{1,0:T(8,128)(2,1)S(1)}, bf16[8,5120]{1,0:T(8,128)(2,1)S(1)}, u32[]{:S(2)}, u32[]{:S(2)}) collective-permute-start(bf16[8,5120]{1,0:T(8,128)(2,1)S(1)} %get-tuple-element.42.refs_0_), channel_id=1, source_target_pairs={{0,8},{4,12},{8,0},{12,4},{16,24},{20,28},{24,16},{28,20},{1,9},{5... | collective-permute-start | bytes 245768 | tf_op jit(solution)/shard_map/ppermute | solution.py:336
  29.8 4.5 %collective-permute-start.6 = (bf16[4,336,128]{2,1,0:T(8,128)(2,1)S(1)}, bf16[4,336,128]{2,1,0:T(8,128)(2,1)S(1)}, u32[]{:S(2)}, u32[]{:S(2)}) collective-permute-start(bf16[4,336,128]{2,1,0:T(8,128)(2,1)S(1)} %join_bundles.1.bundles), channel_id=1, source_target_pairs={{0,4},{4,0},{8,12},{12,8},{16,20},{20,16},{24,28},{28,24},{1,5},{5... | collective-permute-start | bytes 1032200 | tf_op jit(solution)/shard_map/ppermute | solution.py:336
  33.7 2.0 %collective-permute-start.13 = (bf16[4,8,5120]{2,1,0:T(8,128)(2,1)S(1)}, bf16[4,8,5120]{2,1,0:T(8,128)(2,1)S(1)}, u32[]{:S(2)}, u32[]{:S(2)}) collective-permute-start(bf16[4,8,5120]{2,1,0:T(8,128)(2,1)S(1)} %join_kept.1.mine), channel_id=1, source_target_pairs={{0,4},{4,0},{8,12},{12,8},{16,20},{20,16},{24,28},{28,24},{1,5},{5... | collective-permute-start | bytes 983048 | tf_op jit(solution)/shard_map/ppermute | solution.py:336

commit v14 on v11

--- a/solution.py
+++ b/solution.py
@@ -45,9 +45,11 @@
     hi, lo = halves(cosine_np())
     eye = np.eye(G // B)
     kron = lambda x: np.kron(eye, np.asarray(x, np.float32)).astype(jnp.bfloat16)
-    tall = np.zeros((2 * B, 2 * B), jnp.bfloat16)
-    tall[:B, :B], tall[B:, :B] = hi.T, lo.T
-    return jnp.asarray(np.concatenate([kron(x) for x in (hi.T, lo.T, hi, lo)], axis=0)), jnp.asarray(tall)
+    small = np.zeros((2 * B, 4 * B), jnp.bfloat16)
+    for i, x in enumerate((hi, lo)):
+        rows = slice(i * B, (i + 1) * B)
+        small[rows, :B], small[rows, B : 2 * B], small[rows, 2 * B : 3 * B] = x, x, x.T
+    return jnp.asarray(np.concatenate([kron(x) for x in (hi.T, lo.T, hi, lo)], axis=0)), jnp.asarray(small)
 
 
 def fwd(tab, i):
@@ -89,8 +91,8 @@
     )(*ins)
 
 
-def first_body(n_t, cp, cols, nr, switch, slope, exp_ref, act, lines, tall, *refs):
-    outs, (act_out, lines_out, tall_out) = refs[:n_t], refs[n_t : n_t + 3]
+def first_body(n_t, cp, cols, nr, switch, slope, exp_ref, act, lines, small, *refs):
+    outs, (act_out, lines_out, small_out) = refs[:n_t], refs[n_t : n_t + 3]
     switch_v, slope_v, exp_v, sems = refs[n_t + 3 :]
     rep, ten = lax.axis_index("replica"), lax.axis_index("tensor")
     r0 = pl.multiple_of((rep // cp) * nr, nr)
@@ -103,7 +105,7 @@
                 (exp_ref.at[pl.ds(r0, nr), :], exp_v),
                 (act, act_out),
                 (lines, lines_out),
-                (tall, tall_out),
+                (small, small_out),
             ]
         )
     ]
@@ -117,7 +119,7 @@
         outs[k][:B, :] = up
     copies[2].wait()
     nc = cols // cp
-    for k in range(n_t):
+    for k in range(1, n_t):
         c0 = (ten ^ k) * cols + lax.rem(rep, cp) * nc
         for j in range(nc // 128):
             at = pl.multiple_of(c0 + j * 128, 128)
@@ -136,13 +138,13 @@
 
 
 def bundle_body(n_t, keep, after, lines, *refs):
-    parts, out = refs[:n_t], refs[n_t]
+    parts, out = refs[: n_t - 1], refs[n_t - 1]
     n = parts[0].shape[0] - B
-    for k in range(n_t):
+    for k in range(n_t - 1):
         out[k * n : (k + 1) * n, :] = parts[k][B:, :]
     blocks = lines.shape[1]
     rows = jnp.concatenate([lines[...].astype(F32), jnp.zeros((keep, 128 - blocks), F32)], axis=1)
-    out[n_t * n :, :] = jnp.concatenate([rows, jnp.zeros((16 - keep, 128), F32)], axis=0).astype(BF16)
+    out[(n_t - 1) * n :, :] = jnp.concatenate([rows, jnp.zeros((16 - keep, 128), F32)], axis=0).astype(BF16)
 
 
 def join_body(n, *refs):
@@ -150,44 +152,30 @@
         refs[-1][i] = ref[...]
 
 
-def own_body(n_r, keep, mask, tally, lines, tall, p_ref, a_ref, w_ref, mask_s, tally_s, sems):
-    copies = [
-        pltpu.make_async_copy(src, dst, sems.at[i])
-        for i, (src, dst) in enumerate([(mask, mask_s), (tally, tally_s)])
-    ]
-    for copy in copies:
-        copy.start()
-    blocks = lines.shape[1]
+def own_body(keep, lines, small, p_ref, a_ref):
+    blocks, nb = lines.shape[1], G // B
     rows = jnp.concatenate([lines[...].astype(F32), jnp.zeros((keep, 128 - blocks), F32)], axis=1)
+    lane = lax.broadcasted_iota(jnp.int32, (nb * keep, 2 * B), 1).astype(F32)
+    for g in range(blocks // nb):
+        num = jnp.concatenate(
+            [jnp.broadcast_to(rows[:, g * nb + j : g * nb + j + 1], (keep, 2 * B)) for j in range(nb)], axis=0
+        )
+        hot = jnp.concatenate(
+            [jnp.where(lane == num, 1.0, 0.0), jnp.where(lane - B == num, 1.0, 0.0)], axis=0
+        ).astype(BF16)
+        a_ref[g * B : (g + 1) * B, :] = dot(hot, small[:, : 2 * B]).astype(BF16)
     rows = jnp.concatenate([rows] * (2 * B // keep), axis=0).T
     freq = lax.broadcasted_iota(jnp.int32, (B, 2 * B), 0).astype(F32)
-    block = (lax.broadcasted_iota(jnp.int32, (1, 2 * B), 1) // keep) % (G // B)
+    block = (lax.broadcasted_iota(jnp.int32, (1, 2 * B), 1) // keep) % nb
     term = lax.broadcasted_iota(jnp.int32, (B, 2 * B), 1) // (B // 2)
-    for g in range(blocks // (G // B)):
-        num = rows[g * (G // B) : g * (G // B) + 1]
-        for j in range(1, G // B):
-            num = jnp.where(block == j, rows[g * (G // B) + j : g * (G // B) + j + 1], num)
+    for g in range(blocks // nb):
+        num = rows[g * nb : g * nb + 1]
+        for j in range(1, nb):
+            num = jnp.where(block == j, rows[g * nb + j : g * nb + j + 1], num)
         hot = jnp.where(freq == num, 1.0, 0.0).astype(BF16)
-        y = dot(tall[:, :B], hot)
+        y = dot(small[:, 2 * B : 3 * B], hot)
         p = jnp.where(term == 3, 0.0, jnp.where(term == 1, y[B:], y[:B]))
         p_ref[:, g * 2 * B : (g + 1) * 2 * B] = p.astype(BF16)
-        a_ref[g * B : (g + 1) * B, :] = jnp.concatenate([p, p], axis=0).T[:B].astype(BF16)
-    for copy in copies:
-        copy.wait()
-    total, alive = jnp.float32(0), jnp.float32(0)
-    for r in range(n_r):
-        m = mask_s[r].astype(F32)
-        total = total + m * tally_s[r].astype(F32)
-        alive = alive + m
-    half = n_r // 2
-    place = (lax.broadcasted_iota(jnp.int32, (8, 2 * B), 1) // keep) % half
-    scale = jnp.full((8, 2 * B), alive) / jnp.full((8, 2 * B), total)
-    for h in range(2):
-        w = jnp.zeros((8, 2 * B), F32)
-        for i in range(half):
-            r = lax.axis_index("replica") ^ (2 * i + h)
-            w = jnp.where(place == i, mask_s[r].astype(F32) * tally_s[r].astype(F32), w)
-        w_ref[h] = w * scale
 
 
 def kept_body(ks, n_t, keep, vel, a_ref, tab, after, *refs):
@@ -246,23 +234,47 @@
         copy.wait()
 
 
-def places_body(keep, w_ref, tall, bundles, *p_refs):
+def places_body(keep, mask, tally, small, bundles, *refs):
+    p_refs, (mask_s, tally_s, sems) = refs[:4], refs[4:]
+    copies = [
+        pltpu.make_async_copy(src, dst, sems.at[i])
+        for i, (src, dst) in enumerate([(mask, mask_s), (tally, tally_s)])
+    ]
+    for copy in copies:
+        copy.start()
     n_r, last = bundles.shape[0], bundles.shape[1] - 16
     half, nb = n_r // 2, G // B
     rep = lax.axis_index("replica")
     freq = lax.broadcasted_iota(jnp.int32, (B, 2 * B), 0).astype(F32)
-    block = lax.broadcasted_iota(jnp.int32, (1, 2 * B), 1) // (half * keep)
-    for h in range(2):
+    lane = lax.broadcasted_iota(jnp.int32, (1, 2 * B), 1)
+    block, place = lane // (half * keep), (lane // keep) % half
+    cells = [
+        jnp.concatenate(
+            [bundles[rep ^ (2 * i + h), last:, :].astype(F32)[:keep] for i in range(half)] * nb, axis=0
+        ).T
+        for h in range(2)
+    ]
+    for copy in copies:
+        copy.wait()
+    total, alive = jnp.float32(0), jnp.float32(0)
+    for r in range(n_r):
+        m = mask_s[r].astype(F32)
+        total = total + m * tally_s[r].astype(F32)
+        alive = alive + m
+    scale = jnp.full((1, 2 * B), alive) / jnp.full((1, 2 * B), total)
+    for h, rows in enumerate(cells):
+        w = jnp.zeros((1, 2 * B), F32)
+        for i in range(half):
+            r = rep ^ (2 * i + h)
+            w = jnp.where(place == i, mask_s[r].astype(F32) * tally_s[r].astype(F32), w)
+        w = w * scale
         hi_ref, lo_ref = p_refs[2 * h : 2 * h + 2]
-        w = w_ref[h, :1, :]
-        rows = [bundles[rep ^ (2 * i + h), last:, :].astype(F32)[:keep] for i in range(half)]
-        rows = jnp.concatenate(rows * nb, axis=0).T
         for g in range(hi_ref.shape[1] // (2 * B)):
             num = rows[g * nb : g * nb + 1]
             for j in range(1, nb):
                 num = jnp.where(block == j, rows[g * nb + j : g * nb + j + 1], num)
             hot = jnp.where(freq == num, 1.0, 0.0).astype(BF16)
-            y = dot(tall[:, :B], hot)
+            y = dot(small[:, 2 * B : 3 * B], hot)
             hi, lo = split((y[:B] + y[B:]) * w)
             hi_ref[:, g * 2 * B : (g + 1) * 2 * B] = hi
             lo_ref[:, g * 2 * B : (g + 1) * 2 * B] = lo
@@ -298,19 +310,24 @@
         copy.wait()
 
 
-def input_grad_body(n_t, n_r, cp, bundles, *refs):
-    ups, out, held = refs[:n_t], refs[n_t], refs[n_t + 1]
-    nc = out.shape[1] // cp
+def input_grad_body(n_t, n_r, cp, exp_ref, bundles, *refs):
+    ups, (out, held, sem) = refs[:n_t], refs[n_t:]
+    cols = out.shape[1]
+    c0 = pl.multiple_of(lax.axis_index("tensor") * cols, 128)
+    copy = pltpu.make_async_copy(exp_ref.at[:, pl.ds(c0, cols)], held.at[pl.ds(0, B), :], sem)
+    copy.start()
+    nc = cols // cp
     nr = B // (n_r // cp)
     tiles = nc // 128
     for r in range(n_r):
         r0, c0 = (r // cp) * nr, (r % cp) * nc
-        for k in range(n_t):
+        for k in range(1, n_t):
             for j in range(tiles):
-                at = (k * tiles + j) * nr
+                at = ((k - 1) * tiles + j) * nr
                 held[k * B + r0 : k * B + r0 + nr, c0 + j * 128 : c0 + (j + 1) * 128] = bundles[r, at : at + nr, :]
     up = jnp.concatenate([u[:B, :] for u in ups], axis=0).T
-    for c in range(0, out.shape[1], G):
+    copy.wait()
+    for c in range(0, cols, G):
         out[:, c : c + G] = dot(up, held[:, c : c + G]).astype(BF16)
 
 
@@ -324,7 +341,7 @@
     cp = 2
     rp = n_r // cp
     half = n_r // 2
-    tab, tall = constants()
+    tab, small = constants()
     def trade(x, k):
         return lax.ppermute(x, "tensor", [(i, i ^ k) for i in range(n_t)])
 
@@ -336,11 +353,12 @@
     own = lines[0, 0].T
     tiles = cols // cp // 128
     nr = B // rp
-    *parts, act, own, tall = call(
+    *parts, act, own, small = call(
         functools.partial(first_body, n_t, cp, cols, nr),
-        [near((B + tiles * nr, 128))] * n_t
-        + [near(act.shape), near(own.shape, jnp.int32), near(tall.shape)],
-        (far(switch.T), far(slope.T), far(exp), far(act), far(own), far(tall)),
+        [near((B, tok))]
+        + [near((B + tiles * nr, 128))] * (n_t - 1)
+        + [near(act.shape), near(own.shape, jnp.int32), near(small.shape)],
+        (far(switch.T), far(slope.T), far(exp), far(act), far(own), far(small)),
         [ANY] * 6,
         [VM] * (n_t + 3),
         scratch=[
@@ -355,17 +373,12 @@
     got = {k: trade(parts[k], k) for k in order}
     parts = [parts[0]] + [got[k] for k in range(1, n_t)]
 
-    p_own, a_own, shares = call(
-        functools.partial(own_body, n_r, keep),
-        [
-            near((B, groups * 2 * B)),
-            near((groups * B, 2 * B)),
-            near((2, 8, 2 * B), F32),
-        ],
-        (far(mask), far(tally), own, tall),
-        [ANY, ANY, VM, VM],
-        [VM] * 3,
-        scratch=[pltpu.SMEM((n_r,), jnp.int32)] * 2 + [pltpu.SemaphoreType.DMA((2,))],
+    p_own, a_own = call(
+        functools.partial(own_body, keep),
+        [near((B, groups * 2 * B)), near((groups * B, 2 * B))],
+        (own, small),
+        [VM, VM],
+        [VM, VM],
         name="own_places",
     )
 
@@ -382,15 +395,15 @@
     grads = {}
     for k in order[:-1]:
         (grads[k],) = grads_of([k], act)
-    made, grads[0] = grads_of([order[-1], 0], shares)
+    made, grads[0] = grads_of([order[-1], 0], a_own)
     grads[order[-1]] = made
     grads.update({k: trade(grads[k], k) for k in order})
 
     bundle = call(
         functools.partial(bundle_body, n_t, keep),
-        near((n_t * tiles * nr + 16, 128)),
-        (made, own, *parts),
-        [ANY] + [VM] * (n_t + 1),
+        near(((n_t - 1) * tiles * nr + 16, 128)),
+        (made, own, *parts[1:]),
+        [ANY] + [VM] * n_t,
         VM,
         name="bundle",
     )
@@ -399,18 +412,19 @@
     places = call(
         functools.partial(places_body, keep),
         [near((B, blocks * half * keep))] * 4,
-        (shares, tall, bundles),
-        [VM] * 3,
+        (far(mask), far(tally), small, bundles),
+        [ANY, ANY, VM, VM],
         [VM] * 4,
+        scratch=[pltpu.SMEM((n_r,), jnp.int32)] * 2 + [pltpu.SemaphoreType.DMA((2,))],
         name="places",
     )
     input_grad = call(
         functools.partial(input_grad_body, n_t, n_r, cp),
         jax.ShapeDtypeStruct((tok, cols), BF16),
-        (bundles, *parts),
-        [VM] * (1 + n_t),
+        (far(exp), bundles, *parts),
+        [ANY] + [VM] * (1 + n_t),
         VM,
-        scratch=[pltpu.VMEM((n_t * B, cols), BF16)],
+        scratch=[pltpu.VMEM((n_t * B, cols), BF16), pltpu.SemaphoreType.DMA],
         flops=2 * tok * n_t * B * cols,
         nbytes=(n_t * B * cols + tok * cols) * 2,
         name="input_grads",
@@ -459,7 +473,7 @@
         VM,
         name="half_updates",
     )
-    chunk = next(c for c in (5, 4, 3, 2, 1) if groups % c == 0)
+    chunk = 2 if groups % 2 == 0 else 1
     update = call(
         functools.partial(update_body, chunk),
         jax.ShapeDtypeStruct((B, width), F32),

time: 36.3 us -> 36.4 us (level)
  Pallas kernels: 8.49 us -> 9.78 us
  waiting for transfers between devices: 2.22 us -> 1.45 us
  blocking collectives: 10.3 us -> 9.87 us
    pallas_call x14, Pallas kernels: 8.49 us -> 9.78 us  [call(): pl.pallas_call(body, out_shape=out_shape, in_specs=in_specs, out_specs=ou...]
    ppermute x4, waiting for transfers between devices: 2.04 us -> 1.13 us  [swap(): return lax.ppermute(x, 'replica', [(i, i ^ m) for i in range(n_r)])]
    all_gather x1, blocking collectives: 10.3 us -> 9.87 us  [per_device(): bundles = lax.all_gather(bundle, 'replica', axis=0)]
  transfers between devices with their start and end apart: 10 -> 10, of which waited for: 3 -> 2; matrix products, arithmetic and copies ran while one was open for 0% -> 0% of each run, Pallas kernels for 15% -> 19%
where the time goes in v14:
time: 36.4 us; the launch traced here: 36.1 us
  starting transfers between devices  14.2 us (39%)
  blocking collectives  9.87 us (27%)
  Pallas kernels  9.78 us (27%)
  waiting for transfers between devices  1.45 us (4%)
  between operations  0.79 us (2%)
    ppermute x6, starting transfers between devices, trade(): return lax.ppermute(x, 'tensor', [(i, i ^ k) for i in range(n_t)])  10.6 us
    all_gather x1, blocking collectives, per_device(): bundles = lax.all_gather(bundle, 'replica', axis=0)  9.87 us
    pallas_call x14, Pallas kernels, call(): pl.pallas_call(body, out_shape=out_shape, in_specs=in_specs, out_specs=ou...  9.78 us
    ppermute x4, starting transfers between devices, swap(): return lax.ppermute(x, 'replica', [(i, i ^ m) for i in range(n_r)])  3.62 us
    ppermute x4, waiting for transfers between devices, swap(): return lax.ppermute(x, 'replica', [(i, i ^ m) for i in range(n_r)])  1.13 us
  transfers between devices with their start and end apart: 10, of which 2 were waited for; matrix products, arithmetic and copies ran while one was open for 0% of the time, Pallas kernels for 19%

profile of v14, /device:TPU:0, one launch (start us, length us, event | category | flops | bytes accessed | tf_op | source)
XLA Modules:
  0.0 36.1 jit_solution(8307931469945796244)
XLA Ops:
  0.6 1.2 %up_grads.1 = (bf16[64,128]{1,0:T(8,128)(2,1)S(1)}, bf16[144,128]{1,0:T(8,128)(2,1)S(1)}, bf16[144,128]{1,0:T(8,128)(2,1)S(1)}, bf16[144,128]{1,0:T(8,128)(2,1)S...) custom-call(bf16[64,128]{1,0:T(8,128)(2,1)} %bitcast.16, ...), custom_call_target="tpu_custom_call" | custom-call | bytes 819200 | tf_op jit(solution)/shard_map/up_grads/pallas_call | solution.py:81
  1.8 4.1 %collective-permute-start.1 = (bf16[144,128]{1,0:T(8,128)(2,1)S(1)}, bf16[144,128]{1,0:T(8,128)(2,1)S(1)}, u32[]{:S(2)}, u32[]{:S(2)}) collective-permute-start(bf16[144,128]{1,0:T(8,128)(2,1)S(1)} %get-tuple-element.29), channel_id=1, source_target_pairs={{0,2},{1,3},{2,0},{3,1},{4,6},{5,7},{6,4},{7,5},{8,10},{9,11},{10,... | collective-permute-start | bytes 110600 | tf_op jit(solution)/shard_map/ppermute | solution.py:346
  5.9 1.6 %collective-permute-start = (bf16[144,128]{1,0:T(8,128)(2,1)S(1)}, bf16[144,128]{1,0:T(8,128)(2,1)S(1)}, u32[]{:S(2)}, u32[]{:S(2)}) collective-permute-start(bf16[144,128]{1,0:T(8,128)(2,1)S(1)} %get-tuple-element.26), channel_id=1, source_target_pairs={{0,1},{1,0},{2,3},{3,2},{4,5},{5,4},{6,7},{7,6},{8,9},{9,8},{10,11... | collective-permute-start | bytes 110600 | tf_op jit(solution)/shard_map/ppermute | solution.py:346
  7.5 0.0 collective-permute-start.2
  7.5 0.5 %own_places.1 = (bf16[64,2560]{1,0:T(8,128)(2,1)S(1)}, bf16[1280,128]{1,0:T(8,128)(2,1)S(1)}) custom-call(s32[8,80]{1,0:T(8,128)S(1)} %get-tuple-element.23.lines, bf16[128,256]{1,0:T(8,128)(2,1)S(1)} %get-tuple-element.24.small), custom_call_target="tpu_custom_call" | custom-call | tf_op jit(solution)/shard_map/own_places/pallas_call | solution.py:81
  8.0 0.3 collective-permute-done.1.refs_1_.refs_2_.refs_0_
  8.3 0.2 weight_grads.5
  8.5 0.0 copy-start
  8.5 0.0 copy-start.1
  8.5 2.7 %collective-permute-start.5 = (bf16[64,1280]{1,0:T(8,128)(2,1)S(1)}, bf16[64,1280]{1,0:T(8,128)(2,1)S(1)}, u32[]{:S(2)}, u32[]{:S(2)}) collective-permute-start(bf16[64,1280]{1,0:T(8,128)(2,1)S(1)} %weight_grads.5), channel_id=1, source_target_pairs={{0,2},{1,3},{2,0},{3,1},{4,6},{5,7},{6,4},{7,5},{8,10},{9,11},{10,... | collective-permute-start | bytes 491528 | tf_op jit(solution)/shard_map/ppermute | solution.py:346
  11.3 0.0 collective-permute-done.refs_0_.refs_1_
  11.3 0.2 weight_grads.3
  11.5 2.1 %collective-permute-start.4 = (bf16[64,1280]{1,0:T(8,128)(2,1)S(1)}, bf16[64,1280]{1,0:T(8,128)(2,1)S(1)}, u32[]{:S(2)}, u32[]{:S(2)}) collective-permute-start(bf16[64,1280]{1,0:T(8,128)(2,1)S(1)} %get-tuple-element.28.after), channel_id=1, source_target_pairs={{0,1},{1,0},{2,3},{3,2},{4,5},{5,4},{6,7},{7,6},{8,9},{9,8},{10,11... | collective-permute-start | bytes 491528 | tf_op jit(solution)/shard_map/ppermute | solution.py:346
  13.6 0.0 collective-permute-done.2.refs_2_.refs_3_.refs_0_
  13.6 0.2 weight_grads.4
  13.8 0.1 collective-permute-start.3
  13.9 9.9 %all-gather = bf16[2048,128]{1,0:T(8,128)(2,1)S(1)} all-gather(bf16[256,128]{1,0:T(8,128)(2,1)S(1)} %bundle.1), channel_id=2, replica_groups=mesh['replica'=8,'tensor'=4] {'replica'}, dimensions={0}, use_global_device_ids=true | all-gather | bytes 589824 | tf_op jit(solution)/shard_map/all_gather | solution.py:410
  23.8 0.0 collective-permute-done.5.refs_2_
  23.8 0.0 collective-permute-done.4.refs_1_
  23.8 0.0 copy-done
  23.8 0.0 copy-done.1
  23.8 0.7 %kept_rows.2 = (bf16[8,5120]{1,0:T(8,128)(2,1)S(1)}, f32[8,5120]{1,0:T(8,128)S(1)}) custom-call(f32[64,5120]{1,0:T(8,128)S(1)} %bitcast.12, bf16[1280,128]{1,0:T(8,128)(2,1)S(1)} %get-tuple-element.25.after.a_ref, bf16[1024,256]{1,0:T(8,128)(2,1)S(1)} %copy-done.1, bf16[8,256,128]{2,1,0:T(8,128)(2,1)S(1)} %bitcast.8, ...), custom_call_target="tpu_custom_call" | custom-call | flops 94371840 | bytes 1474560 | tf_op jit(solution)/shard_map/kept_rows/pallas_call | solution.py:81
  24.5 0.0 collective-permute-done.3.refs_0_.refs_3_
  24.5 0.5 %kept_rows.3 = (bf16[8,5120]{1,0:T(8,128)(2,1)S(1)}, f32[8,5120]{1,0:T(8,128)S(1)}) custom-call(f32[64,5120]{1,0:T(8,128)S(1)} %bitcast.13, bf16[1280,128]{1,0:T(8,128)(2,1)S(1)} %get-tuple-element.25.after.a_ref, bf16[1024,256]{1,0:T(8,128)(2,1)S(1)} %copy-done.1, bf16[8,256,128]{2,1,0:T(8,128)(2,1)S(1)} %bitcast.9, ...), custom_call_target="tpu_custom_call", output_to_operand_aliasing={{0}: (5, {}), {1}: (6, {})} | custom-call | flops 31457280 | bytes 491520 | tf_op jit(solution)/shard_map/kept_rows/pallas_call | solution.py:81
  25.0 1.9 %collective-permute-start.8 = (bf16[8,5120]{1,0:T(8,128)(2,1)S(1)}, bf16[8,5120]{1,0:T(8,128)(2,1)S(1)}, u32[]{:S(2)}, u32[]{:S(2)}) collective-permute-start(bf16[8,5120]{1,0:T(8,128)(2,1)S(1)} %get-tuple-element.38.refs_0_), channel_id=1, source_target_pairs={{0,24},{4,28},{8,16},{12,20},{16,8},{20,12},{24,0},{28,4},{1,25},{... | collective-permute-start | bytes 245768 | tf_op jit(solution)/shard_map/ppermute | solution.py:351
  26.9 1.1 %collective-permute-start.7 = (bf16[8,5120]{1,0:T(8,128)(2,1)S(1)}, bf16[8,5120]{1,0:T(8,128)(2,1)S(1)}, u32[]{:S(2)}, u32[]{:S(2)}) collective-permute-start(bf16[8,5120]{1,0:T(8,128)(2,1)S(1)} %get-tuple-element.38.refs_0_), channel_id=1, source_target_pairs={{0,16},{4,20},{8,24},{12,28},{16,0},{20,4},{24,8},{28,12},{1,17},{... | collective-permute-start | bytes 245768 | tf_op jit(solution)/shard_map/ppermute | solution.py:351
  28.1 0.5 %collective-permute-start.6 = (bf16[8,5120]{1,0:T(8,128)(2,1)S(1)}, bf16[8,5120]{1,0:T(8,128)(2,1)S(1)}, u32[]{:S(2)}, u32[]{:S(2)}) collective-permute-start(bf16[8,5120]{1,0:T(8,128)(2,1)S(1)} %get-tuple-element.38.refs_0_), channel_id=1, source_target_pairs={{0,8},{4,12},{8,0},{12,4},{16,24},{20,28},{24,16},{28,20},{1,9},{5... | collective-permute-start | bytes 245768 | tf_op jit(solution)/shard_map/ppermute | solution.py:351
  28.6 1.2 %places.1 = (bf16[64,2560]{1,0:T(8,128)(2,1)S(1)}, bf16[64,2560]{1,0:T(8,128)(2,1)S(1)}, bf16[64,2560]{1,0:T(8,128)(2,1)S(1)}, bf16[64,2560]{1,0:T(8,128)(2,1)S(1)}) custom-call(s32[8]{0:T(128)} %mask.1, s32[8]{0:T(128)} %tally.1, bf16[128,256]{1,0:T(8,128)(2,1)S(1)} %get-tuple-element.24.small, bf16[8,256,128]{2,1,0:T(8,128)(2,1)S(1)} %bitcast.10), custom_call_target="tpu_custom_call" | custom-call | tf_op jit(solution)/shard_map/places/pallas_call | solution.py:81
  29.8 1.9 %input_grads.1.refs_5_ = bf16[128,1280]{1,0:T(8,128)(2,1)} custom-call(bf16[64,5120]{1,0:T(8,128)(2,1)} %exp_ref.3, bf16[8,256,128]{2,1,0:T(8,128)(2,1)S(1)} %bitcast.11, bf16[64,128]{1,0:T(8,128)(2,1)S(1)} %get-tuple-element.27.refs_1_.refs_0_, bf16[144,128]{1,0:T(8,128)(2,1)S(1)} %collective-permute-done.refs_0_.refs_1_, ...), custom_call_target="tpu_custom_call" | custom-call | flops 83886080 | bytes 983040 | tf_op jit(solution)/shard_map/input_grads/pallas_call | solution.py:81
  31.7 1.3 %new_momentums.1.refs_4_ = f32[64,5120]{1,0:T(8,128)} custom-call(f32[64,5120]{1,0:T(8,128)S(1)} %bitcast.14, bf16[64,2560]{1,0:T(8,128)(2,1)S(1)} %get-tuple-element.31.p_ref, f32[8,5120]{1,0:T(8,128)S(1)} %get-tuple-element.35.q, f32[64,1280]{1,0:T(8,128)S(1)} %get-tuple-element.32.refs_0_, bf16[64,1280]{1,0:T(8,128)(2,1)S(1)} %collective-permute-done.4.refs_1_, ...), custom_call_target="tpu_custom_call" | custom-call | flops 125829120 | bytes 3276800 | tf_op jit(solution)/shard_map/new_momentums/pallas_call | solution.py:81
  33.1 0.0 collective-permute-done.8.refs_3_
  33.1 0.0 collective-permute-done.7.refs_2_
  33.1 0.0 collective-permute-done.6.refs_1_
  33.1 0.1 collective-permute-start.9
  33.2 0.5 %half_updates.1.half_sum = f32[1280,256]{1,0:T(8,128)S(1)} custom-call(bf16[64,2560]{1,0:T(8,128)(2,1)S(1)} %get-tuple-element.36.refs_6_.p_hi, bf16[64,2560]{1,0:T(8,128)(2,1)S(1)} %get-tuple-element.37.p_lo, bf16[4,8,5120]{2,1,0:T(8,128)(2,1)S(1)} %join_kept.1.mine), custom_call_target="tpu_custom_call" | custom-call | tf_op jit(solution)/shard_map/half_updates/pallas_call | solution.py:81
  33.7 1.1 %collective-permute-done.9.other = bf16[4,8,5120]{2,1,0:T(8,128)(2,1)S(1)} collective-permute-done((bf16[4,8,5120]{2,1,0:T(8,128)(2,1)S(1)}, bf16[4,8,5120]{2,1,0:T(8,128)(2,1)S(1)}, u32[]{:S(2)}, u32[]{:S(2)}) %collective-permute-start.9) | collective-permute-done | bytes 327712 | tf_op jit(solution)/shard_map/ppermute | solution.py:351
  34.8 1.3 %updates.1 = f32[64,5120]{1,0:T(8,128)} custom-call(f32[1280,256]{1,0:T(8,128)S(1)} %half_updates.1.half_sum, bf16[64,2560]{1,0:T(8,128)(2,1)S(1)} %get-tuple-element.39.p_hi, bf16[64,2560]{1,0:T(8,128)(2,1)S(1)} %get-tuple-element.40.p_lo, bf16[4,8,5120]{2,1,0:T(8,128)(2,1)S(1)} %collective-permute-done.9.other), custom_call_target="tpu_custom_call" | custom-call | flops 671088640 | bytes 2621440 | tf_op jit(solution)/shard_map/updates/pallas_call | solution.py:81
  (2 shorter events, 0.0 us)
Async XLA Ops:
  1.8 6.5 %collective-permute-start.1 = (bf16[144,128]{1,0:T(8,128)(2,1)S(1)}, bf16[144,128]{1,0:T(8,128)(2,1)S(1)}, u32[]{:S(2)}, u32[]{:S(2)}) collective-permute-start(bf16[144,128]{1,0:T(8,128)(2,1)S(1)} %get-tuple-element.29), channel_id=1, source_target_pairs={{0,2},{1,3},{2,0},{3,1},{4,6},{5,7},{6,4},{7,5},{8,10},{9,11},{10,... | collective-permute-start | bytes 110600 | tf_op jit(solution)/shard_map/ppermute | solution.py:346
  5.9 5.4 %collective-permute-start = (bf16[144,128]{1,0:T(8,128)(2,1)S(1)}, bf16[144,128]{1,0:T(8,128)(2,1)S(1)}, u32[]{:S(2)}, u32[]{:S(2)}) collective-permute-start(bf16[144,128]{1,0:T(8,128)(2,1)S(1)} %get-tuple-element.26), channel_id=1, source_target_pairs={{0,1},{1,0},{2,3},{3,2},{4,5},{5,4},{6,7},{7,6},{8,9},{9,8},{10,11... | collective-permute-start | bytes 110600 | tf_op jit(solution)/shard_map/ppermute | solution.py:346
  7.5 6.2 %collective-permute-start.2 = (bf16[144,128]{1,0:T(8,128)(2,1)S(1)}, bf16[144,128]{1,0:T(8,128)(2,1)S(1)}, u32[]{:S(2)}, u32[]{:S(2)}) collective-permute-start(bf16[144,128]{1,0:T(8,128)(2,1)S(1)} %get-tuple-element.30), channel_id=1, source_target_pairs={{0,3},{1,2},{2,1},{3,0},{4,7},{5,6},{6,5},{7,4},{8,11},{9,10},{10,... | collective-permute-start | bytes 110600 | tf_op jit(solution)/shard_map/ppermute | solution.py:346
  8.5 15.3 %copy-start = (f32[1,64,5120]{2,1,0:T(8,128)S(1)}, f32[1,64,5120]{2,1,0:T(8,128)}, u32[]{:S(2)}) copy-start(f32[1,64,5120]{2,1,0:T(8,128)} %param.14) | copy-start | bytes 3932164
  8.5 15.3 %copy-start.1 = (bf16[1024,256]{1,0:T(8,128)(2,1)S(1)}, bf16[1024,256]{1,0:T(8,128)(2,1)}, u32[]{:S(2)}) copy-start(bf16[1024,256]{1,0:T(8,128)(2,1)} %constant.4.clone.tab) | copy-start | bytes 1572868
  8.5 15.3 %collective-permute-start.5 = (bf16[64,1280]{1,0:T(8,128)(2,1)S(1)}, bf16[64,1280]{1,0:T(8,128)(2,1)S(1)}, u32[]{:S(2)}, u32[]{:S(2)}) collective-permute-start(bf16[64,1280]{1,0:T(8,128)(2,1)S(1)} %weight_grads.5), channel_id=1, source_target_pairs={{0,2},{1,3},{2,0},{3,1},{4,6},{5,7},{6,4},{7,5},{8,10},{9,11},{10,... | collective-permute-start | bytes 491528 | tf_op jit(solution)/shard_map/ppermute | solution.py:346
  11.5 12.3 %collective-permute-start.4 = (bf16[64,1280]{1,0:T(8,128)(2,1)S(1)}, bf16[64,1280]{1,0:T(8,128)(2,1)S(1)}, u32[]{:S(2)}, u32[]{:S(2)}) collective-permute-start(bf16[64,1280]{1,0:T(8,128)(2,1)S(1)} %get-tuple-element.28.after), channel_id=1, source_target_pairs={{0,1},{1,0},{2,3},{3,2},{4,5},{5,4},{6,7},{7,6},{8,9},{9,8},{10,11... | collective-permute-start | bytes 491528 | tf_op jit(solution)/shard_map/ppermute | solution.py:346
  13.8 10.7 %collective-permute-start.3 = (bf16[64,1280]{1,0:T(8,128)(2,1)S(1)}, bf16[64,1280]{1,0:T(8,128)(2,1)S(1)}, u32[]{:S(2)}, u32[]{:S(2)}) collective-permute-start(bf16[64,1280]{1,0:T(8,128)(2,1)S(1)} %weight_grads.4), channel_id=1, source_target_pairs={{0,3},{1,2},{2,1},{3,0},{4,7},{5,6},{6,5},{7,4},{8,11},{9,10},{10,... | collective-permute-start | bytes 491528 | tf_op jit(solution)/shard_map/ppermute | solution.py:346
  25.0 8.0 %collective-permute-start.8 = (bf16[8,5120]{1,0:T(8,128)(2,1)S(1)}, bf16[8,5120]{1,0:T(8,128)(2,1)S(1)}, u32[]{:S(2)}, u32[]{:S(2)}) collective-permute-start(bf16[8,5120]{1,0:T(8,128)(2,1)S(1)} %get-tuple-element.38.refs_0_), channel_id=1, source_target_pairs={{0,24},{4,28},{8,16},{12,20},{16,8},{20,12},{24,0},{28,4},{1,25},{... | collective-permute-start | bytes 245768 | tf_op jit(solution)/shard_map/ppermute | solution.py:351
  26.9 6.1 %collective-permute-start.7 = (bf16[8,5120]{1,0:T(8,128)(2,1)S(1)}, bf16[8,5120]{1,0:T(8,128)(2,1)S(1)}, u32[]{:S(2)}, u32[]{:S(2)}) collective-permute-start(bf16[8,5120]{1,0:T(8,128)(2,1)S(1)} %get-tuple-element.38.refs_0_), channel_id=1, source_target_pairs={{0,16},{4,20},{8,24},{12,28},{16,0},{20,4},{24,8},{28,12},{1,17},{... | collective-permute-start | bytes 245768 | tf_op jit(solution)/shard_map/ppermute | solution.py:351
  28.1 5.0 %collective-permute-start.6 = (bf16[8,5120]{1,0:T(8,128)(2,1)S(1)}, bf16[8,5120]{1,0:T(8,128)(2,1)S(1)}, u32[]{:S(2)}, u32[]{:S(2)}) collective-permute-start(bf16[8,5120]{1,0:T(8,128)(2,1)S(1)} %get-tuple-element.38.refs_0_), channel_id=1, source_target_pairs={{0,8},{4,12},{8,0},{12,4},{16,24},{20,28},{24,16},{28,20},{1,9},{5... | collective-permute-start | bytes 245768 | tf_op jit(solution)/shard_map/ppermute | solution.py:351
  33.1 1.7 %collective-permute-start.9 = (bf16[4,8,5120]{2,1,0:T(8,128)(2,1)S(1)}, bf16[4,8,5120]{2,1,0:T(8,128)(2,1)S(1)}, u32[]{:S(2)}, u32[]{:S(2)}) collective-permute-start(bf16[4,8,5120]{2,1,0:T(8,128)(2,1)S(1)} %join_kept.1.mine), channel_id=1, source_target_pairs={{0,4},{4,0},{8,12},{12,8},{16,20},{20,16},{24,28},{28,24},{1,5},{5... | collective-permute-start | bytes 983048 | tf_op jit(solution)/shard_map/ppermute | solution.py:351

commit v15 on v14

--- a/solution.py
+++ b/solution.py
@@ -178,8 +178,43 @@
         p_ref[:, g * 2 * B : (g + 1) * 2 * B] = p.astype(BF16)
 
 
-def kept_body(ks, n_t, keep, vel, a_ref, tab, after, *refs):
-    grads, (send_ref, own_ref) = refs[: len(ks)], refs[-2:]
+def share_rows(keep, mask, tally, w_ref):
+    n_r = mask.shape[0]
+    total, alive = jnp.float32(0), jnp.float32(0)
+    for r in range(n_r):
+        m = mask[r].astype(F32)
+        total = total + m * tally[r].astype(F32)
+        alive = alive + m
+    half = n_r // 2
+    place = (lax.broadcasted_iota(jnp.int32, (8, 2 * B), 1) // keep) % half
+    scale = jnp.full((8, 2 * B), alive) / jnp.full((8, 2 * B), total)
+    for h in range(2):
+        w = jnp.zeros((8, 2 * B), F32)
+        for i in range(half):
+            r = lax.axis_index("replica") ^ (2 * i + h)
+            w = jnp.where(place == i, mask[r].astype(F32) * tally[r].astype(F32), w)
+        w_ref[h] = w * scale
+
+
+def kept_body(ks, n_t, keep, vel, a_ref, tab, mask, tally, *refs):
+    grads, (send_ref, own_ref, w_ref, mask_s, tally_s, sems) = refs[: len(ks)], refs[len(ks) + 1 :]
+    copies = [
+        pltpu.make_async_copy(src, dst, sems.at[i])
+        for i, (src, dst) in enumerate([(mask, mask_s), (tally, tally_s)])
+    ]
+    for copy in copies:
+        copy.start()
+    keep_rows(ks, n_t, keep, vel, a_ref, tab, grads, send_ref, own_ref)
+    for copy in copies:
+        copy.wait()
+    share_rows(keep, mask_s, tally_s, w_ref)
+
+
+def kept_more_body(ks, n_t, keep, vel, a_ref, tab, *refs):
+    keep_rows(ks, n_t, keep, vel, a_ref, tab, refs[: len(ks)], *refs[-2:])
+
+
+def keep_rows(ks, n_t, keep, vel, a_ref, tab, grads, send_ref, own_ref):
     cols = grads[0].shape[1]
     ng = cols // G
     lane_block = lax.broadcasted_iota(jnp.int32, (keep, G), 1) // B
@@ -234,41 +269,22 @@
         copy.wait()
 
 
-def places_body(keep, mask, tally, small, bundles, *refs):
-    p_refs, (mask_s, tally_s, sems) = refs[:4], refs[4:]
-    copies = [
-        pltpu.make_async_copy(src, dst, sems.at[i])
-        for i, (src, dst) in enumerate([(mask, mask_s), (tally, tally_s)])
-    ]
-    for copy in copies:
-        copy.start()
+def places_body(keep, w_ref, small, bundles, exp_ref, *refs):
+    p_refs, (local, sem) = refs[:4], refs[4:]
+    cols = local.shape[1]
+    c0 = pl.multiple_of(lax.axis_index("tensor") * cols, 128)
+    copy = pltpu.make_async_copy(exp_ref.at[:, pl.ds(c0, cols)], local, sem)
+    copy.start()
     n_r, last = bundles.shape[0], bundles.shape[1] - 16
     half, nb = n_r // 2, G // B
     rep = lax.axis_index("replica")
     freq = lax.broadcasted_iota(jnp.int32, (B, 2 * B), 0).astype(F32)
-    lane = lax.broadcasted_iota(jnp.int32, (1, 2 * B), 1)
-    block, place = lane // (half * keep), (lane // keep) % half
-    cells = [
-        jnp.concatenate(
-            [bundles[rep ^ (2 * i + h), last:, :].astype(F32)[:keep] for i in range(half)] * nb, axis=0
-        ).T
-        for h in range(2)
-    ]
-    for copy in copies:
-        copy.wait()
-    total, alive = jnp.float32(0), jnp.float32(0)
-    for r in range(n_r):
-        m = mask_s[r].astype(F32)
-        total = total + m * tally_s[r].astype(F32)
-        alive = alive + m
-    scale = jnp.full((1, 2 * B), alive) / jnp.full((1, 2 * B), total)
-    for h, rows in enumerate(cells):
-        w = jnp.zeros((1, 2 * B), F32)
-        for i in range(half):
-            r = rep ^ (2 * i + h)
-            w = jnp.where(place == i, mask_s[r].astype(F32) * tally_s[r].astype(F32), w)
-        w = w * scale
+    block = lax.broadcasted_iota(jnp.int32, (1, 2 * B), 1) // (half * keep)
+    for h in range(2):
         hi_ref, lo_ref = p_refs[2 * h : 2 * h + 2]
+        w = w_ref[h, :1, :]
+        rows = [bundles[rep ^ (2 * i + h), last:, :].astype(F32)[:keep] for i in range(half)]
+        rows = jnp.concatenate(rows * nb, axis=0).T
         for g in range(hi_ref.shape[1] // (2 * B)):
             num = rows[g * nb : g * nb + 1]
             for j in range(1, nb):
@@ -278,6 +294,7 @@
             hi, lo = split((y[:B] + y[B:]) * w)
             hi_ref[:, g * 2 * B : (g + 1) * 2 * B] = hi
             lo_ref[:, g * 2 * B : (g + 1) * 2 * B] = lo
+    copy.wait()
 
 
 def spread_rows(p_hi, p_lo, ships, g):
@@ -310,12 +327,10 @@
         copy.wait()
 
 
-def input_grad_body(n_t, n_r, cp, exp_ref, bundles, *refs):
-    ups, (out, held, sem) = refs[:n_t], refs[n_t:]
+def input_grad_body(n_t, n_r, cp, local, bundles, *refs):
+    ups, (out, held) = refs[:n_t], refs[n_t:]
     cols = out.shape[1]
-    c0 = pl.multiple_of(lax.axis_index("tensor") * cols, 128)
-    copy = pltpu.make_async_copy(exp_ref.at[:, pl.ds(c0, cols)], held.at[pl.ds(0, B), :], sem)
-    copy.start()
+    held[:B, :] = local[...]
     nc = cols // cp
     nr = B // (n_r // cp)
     tiles = nc // 128
@@ -326,7 +341,6 @@
                 at = ((k - 1) * tiles + j) * nr
                 held[k * B + r0 : k * B + r0 + nr, c0 + j * 128 : c0 + (j + 1) * 128] = bundles[r, at : at + nr, :]
     up = jnp.concatenate([u[:B, :] for u in ups], axis=0).T
-    copy.wait()
     for c in range(0, cols, G):
         out[:, c : c + G] = dot(up, held[:, c : c + G]).astype(BF16)
 
@@ -409,41 +423,48 @@
     )
     bundles = lax.all_gather(bundle, "replica", axis=0)
 
-    places = call(
+    rows = []
+    for ks in ([k for k in range(n_t) if k != n_t - 1], [n_t - 1]):
+        n = len(ks)
+        first = not rows
+        rows = call(
+            functools.partial(kept_body if first else kept_more_body, ks, n_t, keep),
+            [near((keep, width)), near((keep, width), F32)] + [near((2, 8, 2 * B), F32)] * first,
+            (vel[0], a_own, tab, *((far(mask), far(tally)) if first else ()), *[grads[k] for k in ks])
+            + (bundles,) * first
+            + tuple(rows[:2]),
+            [VM] * 3 + [ANY] * 2 * first + [VM] * n + ([ANY] if first else [VM] * 2),
+            [VM] * (2 + first),
+            scratch=([pltpu.SMEM((n_r,), jnp.int32)] * 2 + [pltpu.SemaphoreType.DMA((2,))]) * first,
+            flops=6 * B * B * cols * n,
+            nbytes=B * cols * 6 * n,
+            name="kept_rows",
+            alias={} if first else {3 + n: 0, 4 + n: 1},
+        )
+        shares = rows[2] if first else shares
+    ship, q_own = rows
+
+    *places, local = call(
         functools.partial(places_body, keep),
-        [near((B, blocks * half * keep))] * 4,
-        (far(mask), far(tally), small, bundles),
-        [ANY, ANY, VM, VM],
-        [VM] * 4,
-        scratch=[pltpu.SMEM((n_r,), jnp.int32)] * 2 + [pltpu.SemaphoreType.DMA((2,))],
+        [near((B, blocks * half * keep))] * 4 + [near((B, cols))],
+        (shares, small, bundles, far(exp)),
+        [VM] * 3 + [ANY],
+        [VM] * 5,
+        scratch=[pltpu.SemaphoreType.DMA],
         name="places",
     )
     input_grad = call(
         functools.partial(input_grad_body, n_t, n_r, cp),
         jax.ShapeDtypeStruct((tok, cols), BF16),
-        (far(exp), bundles, *parts),
-        [ANY] + [VM] * (1 + n_t),
+        (local, bundles, *parts),
+        [VM] * (2 + n_t),
         VM,
-        scratch=[pltpu.VMEM((n_t * B, cols), BF16), pltpu.SemaphoreType.DMA],
+        scratch=[pltpu.VMEM((n_t * B, cols), BF16)],
         flops=2 * tok * n_t * B * cols,
         nbytes=(n_t * B * cols + tok * cols) * 2,
         name="input_grads",
     )
 
-    rows = []
-    for ks in ([k for k in range(n_t) if k != n_t - 1], [n_t - 1]):
-        rows = call(
-            functools.partial(kept_body, ks, n_t, keep),
-            [near((keep, width)), near((keep, width), F32)],
-            (vel[0], a_own, tab, bundles, *[grads[k] for k in ks], *rows),
-            [VM] * 3 + [ANY] + [VM] * (len(ks) + len(rows)),
-            [VM] * 2,
-            flops=6 * B * B * cols * len(ks),
-            nbytes=B * cols * 6 * len(ks),
-            name="kept_rows",
-            alias={4 + len(ks): 0, 5 + len(ks): 1} if rows else {},
-        )
-    ship, q_own = rows
     ships = [ship] + [swap(ship, 2 * i) for i in range(1, half)]
     new = call(
         functools.partial(return_body, n_t, keep),

time: 36.4 us -> 36.3 us (level)
  transfers between devices with their start and end apart: 10 -> 10, of which waited for: 2 -> 3; matrix products, arithmetic and copies ran while one was open for 0% -> 0% of each run, Pallas kernels for 19% -> 18%
where the time goes in v15:
time: 36.3 us; the launch traced here: 36 us
  starting transfers between devices  14.2 us (39%)
  blocking collectives  9.87 us (27%)
  Pallas kernels  9.51 us (26%)
  waiting for transfers between devices  1.64 us (5%)
  between operations  0.76 us (2%)
    ppermute x6, starting transfers between devices, trade(): return lax.ppermute(x, 'tensor', [(i, i ^ k) for i in range(n_t)])  10.6 us
    all_gather x1, blocking collectives, per_device(): bundles = lax.all_gather(bundle, 'replica', axis=0)  9.87 us
    pallas_call x14, Pallas kernels, call(): pl.pallas_call(body, out_shape=out_shape, in_specs=in_specs, out_specs=ou...  9.51 us
    ppermute x4, starting transfers between devices, swap(): return lax.ppermute(x, 'replica', [(i, i ^ m) for i in range(n_r)])  3.62 us
    ppermute x4, waiting for transfers between devices, swap(): return lax.ppermute(x, 'replica', [(i, i ^ m) for i in range(n_r)])  1.32 us
  transfers between devices with their start and end apart: 10, of which 3 were waited for; matrix products, arithmetic and copies ran while one was open for 0% of the time, Pallas kernels for 18%

profile of v15, /device:TPU:0, one launch (start us, length us, event | category | flops | bytes accessed | tf_op | source)
XLA Modules:
  0.0 36.0 jit_solution(17454861259563622843)
XLA Ops:
  0.6 1.2 %up_grads.1 = (bf16[64,128]{1,0:T(8,128)(2,1)S(1)}, bf16[144,128]{1,0:T(8,128)(2,1)S(1)}, bf16[144,128]{1,0:T(8,128)(2,1)S(1)}, bf16[144,128]{1,0:T(8,128)(2,1)S...) custom-call(bf16[64,128]{1,0:T(8,128)(2,1)} %bitcast.15, ...), custom_call_target="tpu_custom_call" | custom-call | bytes 819200 | tf_op jit(solution)/shard_map/up_grads/pallas_call | solution.py:81
  1.8 4.1 %collective-permute-start.2 = (bf16[144,128]{1,0:T(8,128)(2,1)S(1)}, bf16[144,128]{1,0:T(8,128)(2,1)S(1)}, u32[]{:S(2)}, u32[]{:S(2)}) collective-permute-start(bf16[144,128]{1,0:T(8,128)(2,1)S(1)} %get-tuple-element.32), channel_id=1, source_target_pairs={{0,2},{1,3},{2,0},{3,1},{4,6},{5,7},{6,4},{7,5},{8,10},{9,11},{10,... | collective-permute-start | bytes 110600 | tf_op jit(solution)/shard_map/ppermute | solution.py:360
  5.9 1.6 %collective-permute-start = (bf16[144,128]{1,0:T(8,128)(2,1)S(1)}, bf16[144,128]{1,0:T(8,128)(2,1)S(1)}, u32[]{:S(2)}, u32[]{:S(2)}) collective-permute-start(bf16[144,128]{1,0:T(8,128)(2,1)S(1)} %get-tuple-element.28), channel_id=1, source_target_pairs={{0,1},{1,0},{2,3},{3,2},{4,5},{5,4},{6,7},{7,6},{8,9},{9,8},{10,11... | collective-permute-start | bytes 110600 | tf_op jit(solution)/shard_map/ppermute | solution.py:360
  7.5 0.0 collective-permute-start.4
  7.5 0.5 %own_places.1 = (bf16[64,2560]{1,0:T(8,128)(2,1)S(1)}, bf16[1280,128]{1,0:T(8,128)(2,1)S(1)}) custom-call(s32[8,80]{1,0:T(8,128)S(1)} %get-tuple-element.24.lines, bf16[128,256]{1,0:T(8,128)(2,1)S(1)} %get-tuple-element.25.small), custom_call_target="tpu_custom_call" | custom-call | tf_op jit(solution)/shard_map/own_places/pallas_call | solution.py:81
  8.0 0.3 collective-permute-done.2.refs_0_.refs_1_.refs_2_
  8.3 0.2 weight_grads.4
  8.5 0.0 copy-start
  8.5 0.0 copy-start.1
  8.5 2.7 %collective-permute-start.3 = (bf16[64,1280]{1,0:T(8,128)(2,1)S(1)}, bf16[64,1280]{1,0:T(8,128)(2,1)S(1)}, u32[]{:S(2)}, u32[]{:S(2)}) collective-permute-start(bf16[64,1280]{1,0:T(8,128)(2,1)S(1)} %weight_grads.4), channel_id=1, source_target_pairs={{0,2},{1,3},{2,0},{3,1},{4,6},{5,7},{6,4},{7,5},{8,10},{9,11},{10,... | collective-permute-start | bytes 491528 | tf_op jit(solution)/shard_map/ppermute | solution.py:360
  11.3 0.0 collective-permute-done.refs_0_.refs_1_
  11.3 0.2 weight_grads.3
  11.5 2.1 %collective-permute-start.1 = (bf16[64,1280]{1,0:T(8,128)(2,1)S(1)}, bf16[64,1280]{1,0:T(8,128)(2,1)S(1)}, u32[]{:S(2)}, u32[]{:S(2)}) collective-permute-start(bf16[64,1280]{1,0:T(8,128)(2,1)S(1)} %get-tuple-element.31.after), channel_id=1, source_target_pairs={{0,1},{1,0},{2,3},{3,2},{4,5},{5,4},{6,7},{7,6},{8,9},{9,8},{10,11... | collective-permute-start | bytes 491528 | tf_op jit(solution)/shard_map/ppermute | solution.py:360
  13.6 0.0 collective-permute-done.4.refs_2_.refs_3_.refs_0_
  13.6 0.2 weight_grads.5
  13.8 0.1 collective-permute-start.5
  13.9 9.9 %all-gather = bf16[2048,128]{1,0:T(8,128)(2,1)S(1)} all-gather(bf16[256,128]{1,0:T(8,128)(2,1)S(1)} %bundle.1), channel_id=2, replica_groups=mesh['replica'=8,'tensor'=4] {'replica'}, dimensions={0}, use_global_device_ids=true | all-gather | bytes 589824 | tf_op jit(solution)/shard_map/all_gather | solution.py:424
  23.8 0.0 collective-permute-done.3.refs_2_
  23.8 0.0 collective-permute-done.1.refs_1_
  23.8 0.0 copy-done
  23.8 0.0 copy-done.1
  23.8 1.2 %kept_rows.2 = (bf16[8,5120]{1,0:T(8,128)(2,1)S(1)}, f32[8,5120]{1,0:T(8,128)S(1)}, f32[2,8,128]{2,1,0:T(8,128)S(1)}) custom-call(f32[64,5120]{1,0:T(8,128)S(1)} %bitcast.8, bf16[1280,128]{1,0:T(8,128)(2,1)S(1)} %get-tuple-element.26.after.a_ref, bf16[1024,256]{1,0:T(8,128)(2,1)S(1)} %copy-done.1, s32[8]{0:T(128)} %mask.1, s32[8]{0:T(128)} %tally.1, ...), custom_call_target="tpu_custom_call" | custom-call | flops 94371840 | bytes 1474560 | tf_op jit(solution)/shard_map/kept_rows/pallas_call | solution.py:81
  25.0 0.0 collective-permute-done.5.refs_0_.refs_3_
  25.0 0.5 %kept_rows.3 = (bf16[8,5120]{1,0:T(8,128)(2,1)S(1)}, f32[8,5120]{1,0:T(8,128)S(1)}) custom-call(f32[64,5120]{1,0:T(8,128)S(1)} %bitcast.9, bf16[1280,128]{1,0:T(8,128)(2,1)S(1)} %get-tuple-element.26.after.a_ref, bf16[1024,256]{1,0:T(8,128)(2,1)S(1)} %copy-done.1, ...), custom_call_target="tpu_custom_call", output_to_operand_aliasing={{0}: (4, {}), {1}: (5, {})} | custom-call | flops 31457280 | bytes 491520 | tf_op jit(solution)/shard_map/kept_rows/pallas_call | solution.py:81
  25.5 1.9 %collective-permute-start.8 = (bf16[8,5120]{1,0:T(8,128)(2,1)S(1)}, bf16[8,5120]{1,0:T(8,128)(2,1)S(1)}, u32[]{:S(2)}, u32[]{:S(2)}) collective-permute-start(bf16[8,5120]{1,0:T(8,128)(2,1)S(1)} %get-tuple-element.42.refs_0_), channel_id=1, source_target_pairs={{0,24},{4,28},{8,16},{12,20},{16,8},{20,12},{24,0},{28,4},{1,25},{... | collective-permute-start | bytes 245768 | tf_op jit(solution)/shard_map/ppermute | solution.py:365
  27.4 1.1 %collective-permute-start.7 = (bf16[8,5120]{1,0:T(8,128)(2,1)S(1)}, bf16[8,5120]{1,0:T(8,128)(2,1)S(1)}, u32[]{:S(2)}, u32[]{:S(2)}) collective-permute-start(bf16[8,5120]{1,0:T(8,128)(2,1)S(1)} %get-tuple-element.42.refs_0_), channel_id=1, source_target_pairs={{0,16},{4,20},{8,24},{12,28},{16,0},{20,4},{24,8},{28,12},{1,17},{... | collective-permute-start | bytes 245768 | tf_op jit(solution)/shard_map/ppermute | solution.py:365
  28.5 0.5 %collective-permute-start.6 = (bf16[8,5120]{1,0:T(8,128)(2,1)S(1)}, bf16[8,5120]{1,0:T(8,128)(2,1)S(1)}, u32[]{:S(2)}, u32[]{:S(2)}) collective-permute-start(bf16[8,5120]{1,0:T(8,128)(2,1)S(1)} %get-tuple-element.42.refs_0_), channel_id=1, source_target_pairs={{0,8},{4,12},{8,0},{12,4},{16,24},{20,28},{24,16},{28,20},{1,9},{5... | collective-permute-start | bytes 245768 | tf_op jit(solution)/shard_map/ppermute | solution.py:365
  29.1 1.3 %places.1 = (bf16[64,2560]{1,0:T(8,128)(2,1)S(1)}, bf16[64,2560]{1,0:T(8,128)(2,1)S(1)}, bf16[64,2560]{1,0:T(8,128)(2,1)S(1)}, bf16[64,2560]{1,0:T(8,128)(2,1)S(1)}, bf16[64,1280]{1,0:T(8,128)(2,1)S(1)}) custom-call(f32[2,8,128]{2,1,0:T(8,128)S(1)} %get-tuple-element.34.w_ref, bf16[128,256]{1,0:T(8,128)(2,1)S(1)} %get-tuple-element.25.small, ...), custom_call_target="tpu_custom_call" | custom-call | tf_op jit(solution)/shard_map/places/pallas_call | solution.py:81
  30.4 1.0 %input_grads.1.refs_5_ = bf16[128,1280]{1,0:T(8,128)(2,1)} custom-call(bf16[64,1280]{1,0:T(8,128)(2,1)S(1)} %get-tuple-element.35.local, bf16[8,256,128]{2,1,0:T(8,128)(2,1)S(1)} %bitcast.13, bf16[64,128]{1,0:T(8,128)(2,1)S(1)} %get-tuple-element.29.refs_1_.refs_0_, bf16[144,128]{1,0:T(8,128)(2,1)S(1)} %collective-permute-done.refs_0_.refs_1_, ...), custom_call_target="tpu_custom_call" | custom-call | flops 83886080 | bytes 983040 | tf_op jit(solution)/shard_map/input_grads/pallas_call | solution.py:81
  31.5 1.3 %new_momentums.1.refs_4_ = f32[64,5120]{1,0:T(8,128)} custom-call(f32[64,5120]{1,0:T(8,128)S(1)} %bitcast.10, bf16[64,2560]{1,0:T(8,128)(2,1)S(1)} %get-tuple-element.36.p_ref, f32[8,5120]{1,0:T(8,128)S(1)} %get-tuple-element.39.q, f32[64,1280]{1,0:T(8,128)S(1)} %get-tuple-element.30.refs_0_, bf16[64,1280]{1,0:T(8,128)(2,1)S(1)} %collective-permute-done.1.refs_1_, ...), custom_call_target="tpu_custom_call" | custom-call | flops 125829120 | bytes 3276800 | tf_op jit(solution)/shard_map/new_momentums/pallas_call | solution.py:81
  32.8 0.0 collective-permute-done.8.refs_3_
  32.8 0.1 collective-permute-done.7.refs_2_
  32.9 0.0 collective-permute-done.6.refs_1_
  33.0 0.1 collective-permute-start.9
  33.1 0.5 %half_updates.1.half_sum = f32[1280,256]{1,0:T(8,128)S(1)} custom-call(bf16[64,2560]{1,0:T(8,128)(2,1)S(1)} %get-tuple-element.40.refs_6_.p_hi, bf16[64,2560]{1,0:T(8,128)(2,1)S(1)} %get-tuple-element.41.p_lo, bf16[4,8,5120]{2,1,0:T(8,128)(2,1)S(1)} %join_kept.1.mine), custom_call_target="tpu_custom_call" | custom-call | tf_op jit(solution)/shard_map/half_updates/pallas_call | solution.py:81
  33.6 1.1 %collective-permute-done.9.other = bf16[4,8,5120]{2,1,0:T(8,128)(2,1)S(1)} collective-permute-done((bf16[4,8,5120]{2,1,0:T(8,128)(2,1)S(1)}, bf16[4,8,5120]{2,1,0:T(8,128)(2,1)S(1)}, u32[]{:S(2)}, u32[]{:S(2)}) %collective-permute-start.9) | collective-permute-done | bytes 327712 | tf_op jit(solution)/shard_map/ppermute | solution.py:365
  34.7 1.3 %updates.1 = f32[64,5120]{1,0:T(8,128)} custom-call(f32[1280,256]{1,0:T(8,128)S(1)} %half_updates.1.half_sum, bf16[64,2560]{1,0:T(8,128)(2,1)S(1)} %get-tuple-element.43.p_hi, bf16[64,2560]{1,0:T(8,128)(2,1)S(1)} %get-tuple-element.44.p_lo, bf16[4,8,5120]{2,1,0:T(8,128)(2,1)S(1)} %collective-permute-done.9.other), custom_call_target="tpu_custom_call" | custom-call | flops 671088640 | bytes 2621440 | tf_op jit(solution)/shard_map/updates/pallas_call | solution.py:81
  (2 shorter events, 0.0 us)
Async XLA Ops:
  1.8 6.5 %collective-permute-start.2 = (bf16[144,128]{1,0:T(8,128)(2,1)S(1)}, bf16[144,128]{1,0:T(8,128)(2,1)S(1)}, u32[]{:S(2)}, u32[]{:S(2)}) collective-permute-start(bf16[144,128]{1,0:T(8,128)(2,1)S(1)} %get-tuple-element.32), channel_id=1, source_target_pairs={{0,2},{1,3},{2,0},{3,1},{4,6},{5,7},{6,4},{7,5},{8,10},{9,11},{10,... | collective-permute-start | bytes 110600 | tf_op jit(solution)/shard_map/ppermute | solution.py:360
  5.9 5.4 %collective-permute-start = (bf16[144,128]{1,0:T(8,128)(2,1)S(1)}, bf16[144,128]{1,0:T(8,128)(2,1)S(1)}, u32[]{:S(2)}, u32[]{:S(2)}) collective-permute-start(bf16[144,128]{1,0:T(8,128)(2,1)S(1)} %get-tuple-element.28), channel_id=1, source_target_pairs={{0,1},{1,0},{2,3},{3,2},{4,5},{5,4},{6,7},{7,6},{8,9},{9,8},{10,11... | collective-permute-start | bytes 110600 | tf_op jit(solution)/shard_map/ppermute | solution.py:360
  7.5 6.2 %collective-permute-start.4 = (bf16[144,128]{1,0:T(8,128)(2,1)S(1)}, bf16[144,128]{1,0:T(8,128)(2,1)S(1)}, u32[]{:S(2)}, u32[]{:S(2)}) collective-permute-start(bf16[144,128]{1,0:T(8,128)(2,1)S(1)} %get-tuple-element.33), channel_id=1, source_target_pairs={{0,3},{1,2},{2,1},{3,0},{4,7},{5,6},{6,5},{7,4},{8,11},{9,10},{10,... | collective-permute-start | bytes 110600 | tf_op jit(solution)/shard_map/ppermute | solution.py:360
  8.5 15.3 %copy-start = (f32[1,64,5120]{2,1,0:T(8,128)S(1)}, f32[1,64,5120]{2,1,0:T(8,128)}, u32[]{:S(2)}) copy-start(f32[1,64,5120]{2,1,0:T(8,128)} %param.14) | copy-start | bytes 3932164
  8.5 15.3 %copy-start.1 = (bf16[1024,256]{1,0:T(8,128)(2,1)S(1)}, bf16[1024,256]{1,0:T(8,128)(2,1)}, u32[]{:S(2)}) copy-start(bf16[1024,256]{1,0:T(8,128)(2,1)} %constant.4.clone.tab) | copy-start | bytes 1572868
  8.5 15.3 %collective-permute-start.3 = (bf16[64,1280]{1,0:T(8,128)(2,1)S(1)}, bf16[64,1280]{1,0:T(8,128)(2,1)S(1)}, u32[]{:S(2)}, u32[]{:S(2)}) collective-permute-start(bf16[64,1280]{1,0:T(8,128)(2,1)S(1)} %weight_grads.4), channel_id=1, source_target_pairs={{0,2},{1,3},{2,0},{3,1},{4,6},{5,7},{6,4},{7,5},{8,10},{9,11},{10,... | collective-permute-start | bytes 491528 | tf_op jit(solution)/shard_map/ppermute | solution.py:360
  11.5 12.3 %collective-permute-start.1 = (bf16[64,1280]{1,0:T(8,128)(2,1)S(1)}, bf16[64,1280]{1,0:T(8,128)(2,1)S(1)}, u32[]{:S(2)}, u32[]{:S(2)}) collective-permute-start(bf16[64,1280]{1,0:T(8,128)(2,1)S(1)} %get-tuple-element.31.after), channel_id=1, source_target_pairs={{0,1},{1,0},{2,3},{3,2},{4,5},{5,4},{6,7},{7,6},{8,9},{9,8},{10,11... | collective-permute-start | bytes 491528 | tf_op jit(solution)/shard_map/ppermute | solution.py:360
  13.8 11.2 %collective-permute-start.5 = (bf16[64,1280]{1,0:T(8,128)(2,1)S(1)}, bf16[64,1280]{1,0:T(8,128)(2,1)S(1)}, u32[]{:S(2)}, u32[]{:S(2)}) collective-permute-start(bf16[64,1280]{1,0:T(8,128)(2,1)S(1)} %weight_grads.5), channel_id=1, source_target_pairs={{0,3},{1,2},{2,1},{3,0},{4,7},{5,6},{6,5},{7,4},{8,11},{9,10},{10,... | collective-permute-start | bytes 491528 | tf_op jit(solution)/shard_map/ppermute | solution.py:360
  25.5 7.3 %collective-permute-start.8 = (bf16[8,5120]{1,0:T(8,128)(2,1)S(1)}, bf16[8,5120]{1,0:T(8,128)(2,1)S(1)}, u32[]{:S(2)}, u32[]{:S(2)}) collective-permute-start(bf16[8,5120]{1,0:T(8,128)(2,1)S(1)} %get-tuple-element.42.refs_0_), channel_id=1, source_target_pairs={{0,24},{4,28},{8,16},{12,20},{16,8},{20,12},{24,0},{28,4},{1,25},{... | collective-permute-start | bytes 245768 | tf_op jit(solution)/shard_map/ppermute | solution.py:365
  27.4 5.5 %collective-permute-start.7 = (bf16[8,5120]{1,0:T(8,128)(2,1)S(1)}, bf16[8,5120]{1,0:T(8,128)(2,1)S(1)}, u32[]{:S(2)}, u32[]{:S(2)}) collective-permute-start(bf16[8,5120]{1,0:T(8,128)(2,1)S(1)} %get-tuple-element.42.refs_0_), channel_id=1, source_target_pairs={{0,16},{4,20},{8,24},{12,28},{16,0},{20,4},{24,8},{28,12},{1,17},{... | collective-permute-start | bytes 245768 | tf_op jit(solution)/shard_map/ppermute | solution.py:365
  28.5 4.4 %collective-permute-start.6 = (bf16[8,5120]{1,0:T(8,128)(2,1)S(1)}, bf16[8,5120]{1,0:T(8,128)(2,1)S(1)}, u32[]{:S(2)}, u32[]{:S(2)}) collective-permute-start(bf16[8,5120]{1,0:T(8,128)(2,1)S(1)} %get-tuple-element.42.refs_0_), channel_id=1, source_target_pairs={{0,8},{4,12},{8,0},{12,4},{16,24},{20,28},{24,16},{28,20},{1,9},{5... | collective-permute-start | bytes 245768 | tf_op jit(solution)/shard_map/ppermute | solution.py:365
  33.0 1.7 %collective-permute-start.9 = (bf16[4,8,5120]{2,1,0:T(8,128)(2,1)S(1)}, bf16[4,8,5120]{2,1,0:T(8,128)(2,1)S(1)}, u32[]{:S(2)}, u32[]{:S(2)}) collective-permute-start(bf16[4,8,5120]{2,1,0:T(8,128)(2,1)S(1)} %join_kept.1.mine), channel_id=1, source_target_pairs={{0,4},{4,0},{8,12},{12,8},{16,20},{20,16},{24,28},{28,24},{1,5},{5... | collective-permute-start | bytes 983048 | tf_op jit(solution)/shard_map/ppermute | solution.py:365

commit v16 on v15

--- a/solution.py
+++ b/solution.py
@@ -178,39 +178,7 @@
         p_ref[:, g * 2 * B : (g + 1) * 2 * B] = p.astype(BF16)
 
 
-def share_rows(keep, mask, tally, w_ref):
-    n_r = mask.shape[0]
-    total, alive = jnp.float32(0), jnp.float32(0)
-    for r in range(n_r):
-        m = mask[r].astype(F32)
-        total = total + m * tally[r].astype(F32)
-        alive = alive + m
-    half = n_r // 2
-    place = (lax.broadcasted_iota(jnp.int32, (8, 2 * B), 1) // keep) % half
-    scale = jnp.full((8, 2 * B), alive) / jnp.full((8, 2 * B), total)
-    for h in range(2):
-        w = jnp.zeros((8, 2 * B), F32)
-        for i in range(half):
-            r = lax.axis_index("replica") ^ (2 * i + h)
-            w = jnp.where(place == i, mask[r].astype(F32) * tally[r].astype(F32), w)
-        w_ref[h] = w * scale
-
-
-def kept_body(ks, n_t, keep, vel, a_ref, tab, mask, tally, *refs):
-    grads, (send_ref, own_ref, w_ref, mask_s, tally_s, sems) = refs[: len(ks)], refs[len(ks) + 1 :]
-    copies = [
-        pltpu.make_async_copy(src, dst, sems.at[i])
-        for i, (src, dst) in enumerate([(mask, mask_s), (tally, tally_s)])
-    ]
-    for copy in copies:
-        copy.start()
-    keep_rows(ks, n_t, keep, vel, a_ref, tab, grads, send_ref, own_ref)
-    for copy in copies:
-        copy.wait()
-    share_rows(keep, mask_s, tally_s, w_ref)
-
-
-def kept_more_body(ks, n_t, keep, vel, a_ref, tab, *refs):
+def kept_body(ks, n_t, keep, vel, a_ref, tab, after, *refs):
     keep_rows(ks, n_t, keep, vel, a_ref, tab, refs[: len(ks)], *refs[-2:])
 
 
@@ -269,20 +237,26 @@
         copy.wait()
 
 
-def places_body(keep, w_ref, small, bundles, exp_ref, *refs):
-    p_refs, (local, sem) = refs[:4], refs[4:]
-    cols = local.shape[1]
-    c0 = pl.multiple_of(lax.axis_index("tensor") * cols, 128)
-    copy = pltpu.make_async_copy(exp_ref.at[:, pl.ds(c0, cols)], local, sem)
-    copy.start()
+def places_body(keep, mask, tally, small, bundles, *p_refs):
     n_r, last = bundles.shape[0], bundles.shape[1] - 16
     half, nb = n_r // 2, G // B
     rep = lax.axis_index("replica")
+    total, alive = jnp.float32(0), jnp.float32(0)
+    for r in range(n_r):
+        m = mask[r].astype(F32)
+        total = total + m * tally[r].astype(F32)
+        alive = alive + m
+    scale = jnp.full((1, 2 * B), alive) / jnp.full((1, 2 * B), total)
     freq = lax.broadcasted_iota(jnp.int32, (B, 2 * B), 0).astype(F32)
-    block = lax.broadcasted_iota(jnp.int32, (1, 2 * B), 1) // (half * keep)
+    lane = lax.broadcasted_iota(jnp.int32, (1, 2 * B), 1)
+    block, place = lane // (half * keep), (lane // keep) % half
     for h in range(2):
         hi_ref, lo_ref = p_refs[2 * h : 2 * h + 2]
-        w = w_ref[h, :1, :]
+        w = jnp.zeros((1, 2 * B), F32)
+        for i in range(half):
+            r = rep ^ (2 * i + h)
+            w = jnp.where(place == i, mask[r].astype(F32) * tally[r].astype(F32), w)
+        w = w * scale
         rows = [bundles[rep ^ (2 * i + h), last:, :].astype(F32)[:keep] for i in range(half)]
         rows = jnp.concatenate(rows * nb, axis=0).T
         for g in range(hi_ref.shape[1] // (2 * B)):
@@ -294,7 +268,6 @@
             hi, lo = split((y[:B] + y[B:]) * w)
             hi_ref[:, g * 2 * B : (g + 1) * 2 * B] = hi
             lo_ref[:, g * 2 * B : (g + 1) * 2 * B] = lo
-    copy.wait()
 
 
 def spread_rows(p_hi, p_lo, ships, g):
@@ -327,10 +300,10 @@
         copy.wait()
 
 
-def input_grad_body(n_t, n_r, cp, local, bundles, *refs):
+def input_grad_body(n_t, n_r, cp, exp_ref, bundles, *refs):
     ups, (out, held) = refs[:n_t], refs[n_t:]
     cols = out.shape[1]
-    held[:B, :] = local[...]
+    held[:B, :] = exp_ref[:, pl.ds(pl.multiple_of(lax.axis_index("tensor") * cols, 128), cols)]
     nc = cols // cp
     nr = B // (n_r // cp)
     tiles = nc // 128
@@ -426,37 +399,31 @@
     rows = []
     for ks in ([k for k in range(n_t) if k != n_t - 1], [n_t - 1]):
         n = len(ks)
-        first = not rows
         rows = call(
-            functools.partial(kept_body if first else kept_more_body, ks, n_t, keep),
-            [near((keep, width)), near((keep, width), F32)] + [near((2, 8, 2 * B), F32)] * first,
-            (vel[0], a_own, tab, *((far(mask), far(tally)) if first else ()), *[grads[k] for k in ks])
-            + (bundles,) * first
-            + tuple(rows[:2]),
-            [VM] * 3 + [ANY] * 2 * first + [VM] * n + ([ANY] if first else [VM] * 2),
-            [VM] * (2 + first),
-            scratch=([pltpu.SMEM((n_r,), jnp.int32)] * 2 + [pltpu.SemaphoreType.DMA((2,))]) * first,
+            functools.partial(kept_body, ks, n_t, keep),
+            [near((keep, width)), near((keep, width), F32)],
+            (vel[0], a_own, tab, bundles, *[grads[k] for k in ks], *rows),
+            [VM] * 3 + [ANY] + [VM] * (n + len(rows)),
+            [VM] * 2,
             flops=6 * B * B * cols * n,
             nbytes=B * cols * 6 * n,
             name="kept_rows",
-            alias={} if first else {3 + n: 0, 4 + n: 1},
+            alias={4 + n: 0, 5 + n: 1} if rows else {},
         )
-        shares = rows[2] if first else shares
     ship, q_own = rows
 
-    *places, local = call(
+    places = call(
         functools.partial(places_body, keep),
-        [near((B, blocks * half * keep))] * 4 + [near((B, cols))],
-        (shares, small, bundles, far(exp)),
-        [VM] * 3 + [ANY],
-        [VM] * 5,
-        scratch=[pltpu.SemaphoreType.DMA],
+        [near((B, blocks * half * keep))] * 4,
+        (mask, tally, small, bundles),
+        [SM, SM, VM, VM],
+        [VM] * 4,
         name="places",
     )
     input_grad = call(
         functools.partial(input_grad_body, n_t, n_r, cp),
         jax.ShapeDtypeStruct((tok, cols), BF16),
-        (local, bundles, *parts),
+        (exp, bundles, *parts),
         [VM] * (2 + n_t),
         VM,
         scratch=[pltpu.VMEM((n_t * B, cols), BF16)],

time: 36.3 us -> 35.8 us (0.986)
  Pallas kernels: 9.51 us -> 8.79 us
    pallas_call x14, Pallas kernels: 9.51 us -> 8.79 us  [call(): pl.pallas_call(body, out_shape=out_shape, in_specs=in_specs, out_specs=ou...]
  transfers between devices with their start and end apart: 10 -> 10, of which waited for: 3 -> 3; matrix products, arithmetic and copies ran while one was open for 0% -> 0% of each run, Pallas kernels for 18% -> 16%
where the time goes in v16:
time: 35.8 us; the launch traced here: 35.6 us
  starting transfers between devices  14.2 us (40%)
  blocking collectives  9.87 us (28%)
  Pallas kernels  8.79 us (25%)
  waiting for transfers between devices  1.85 us (5%)
  between operations  0.8 us (2%)
    ppermute x6, starting transfers between devices, trade(): return lax.ppermute(x, 'tensor', [(i, i ^ k) for i in range(n_t)])  10.6 us
    all_gather x1, blocking collectives, per_device(): bundles = lax.all_gather(bundle, 'replica', axis=0)  9.87 us
    pallas_call x14, Pallas kernels, call(): pl.pallas_call(body, out_shape=out_shape, in_specs=in_specs, out_specs=ou...  8.79 us
    ppermute x4, starting transfers between devices, swap(): return lax.ppermute(x, 'replica', [(i, i ^ m) for i in range(n_r)])  3.62 us
    ppermute x4, waiting for transfers between devices, swap(): return lax.ppermute(x, 'replica', [(i, i ^ m) for i in range(n_r)])  1.53 us
  transfers between devices with their start and end apart: 10, of which 3 were waited for; matrix products, arithmetic and copies ran while one was open for 0% of the time, Pallas kernels for 16%

profile of v16, /device:TPU:0, one launch (start us, length us, event | category | flops | bytes accessed | tf_op | source)
XLA Modules:
  0.0 35.6 jit_solution(16520965250266287157)
XLA Ops:
  0.6 1.2 %up_grads.1 = (bf16[64,128]{1,0:T(8,128)(2,1)S(1)}, bf16[144,128]{1,0:T(8,128)(2,1)S(1)}, bf16[144,128]{1,0:T(8,128)(2,1)S(1)}, bf16[144,128]{1,0:T(8,128)(2,1)S...) custom-call(bf16[64,128]{1,0:T(8,128)(2,1)} %bitcast.16, ...), custom_call_target="tpu_custom_call" | custom-call | bytes 819200 | tf_op jit(solution)/shard_map/up_grads/pallas_call | solution.py:81
  1.8 4.1 %collective-permute-start.1 = (bf16[144,128]{1,0:T(8,128)(2,1)S(1)}, bf16[144,128]{1,0:T(8,128)(2,1)S(1)}, u32[]{:S(2)}, u32[]{:S(2)}) collective-permute-start(bf16[144,128]{1,0:T(8,128)(2,1)S(1)} %get-tuple-element.29), channel_id=1, source_target_pairs={{0,2},{1,3},{2,0},{3,1},{4,6},{5,7},{6,4},{7,5},{8,10},{9,11},{10,... | collective-permute-start | bytes 110600 | tf_op jit(solution)/shard_map/ppermute | solution.py:333
  5.9 1.6 %collective-permute-start = (bf16[144,128]{1,0:T(8,128)(2,1)S(1)}, bf16[144,128]{1,0:T(8,128)(2,1)S(1)}, u32[]{:S(2)}, u32[]{:S(2)}) collective-permute-start(bf16[144,128]{1,0:T(8,128)(2,1)S(1)} %get-tuple-element.26), channel_id=1, source_target_pairs={{0,1},{1,0},{2,3},{3,2},{4,5},{5,4},{6,7},{7,6},{8,9},{9,8},{10,11... | collective-permute-start | bytes 110600 | tf_op jit(solution)/shard_map/ppermute | solution.py:333
  7.5 0.0 collective-permute-start.2
  7.5 0.5 %own_places.1 = (bf16[64,2560]{1,0:T(8,128)(2,1)S(1)}, bf16[1280,128]{1,0:T(8,128)(2,1)S(1)}) custom-call(s32[8,80]{1,0:T(8,128)S(1)} %get-tuple-element.23.lines, bf16[128,256]{1,0:T(8,128)(2,1)S(1)} %get-tuple-element.24.small), custom_call_target="tpu_custom_call" | custom-call | tf_op jit(solution)/shard_map/own_places/pallas_call | solution.py:81
  8.0 0.3 collective-permute-done.1.refs_1_.refs_2_.refs_0_
  8.3 0.2 weight_grads.5
  8.5 0.0 copy-start
  8.5 0.0 copy-start.2
  8.5 2.7 %collective-permute-start.5 = (bf16[64,1280]{1,0:T(8,128)(2,1)S(1)}, bf16[64,1280]{1,0:T(8,128)(2,1)S(1)}, u32[]{:S(2)}, u32[]{:S(2)}) collective-permute-start(bf16[64,1280]{1,0:T(8,128)(2,1)S(1)} %weight_grads.5), channel_id=1, source_target_pairs={{0,2},{1,3},{2,0},{3,1},{4,6},{5,7},{6,4},{7,5},{8,10},{9,11},{10,... | collective-permute-start | bytes 491528 | tf_op jit(solution)/shard_map/ppermute | solution.py:333
  11.3 0.0 collective-permute-done.refs_0_.refs_1_
  11.3 0.2 weight_grads.3
  11.5 2.1 %collective-permute-start.4 = (bf16[64,1280]{1,0:T(8,128)(2,1)S(1)}, bf16[64,1280]{1,0:T(8,128)(2,1)S(1)}, u32[]{:S(2)}, u32[]{:S(2)}) collective-permute-start(bf16[64,1280]{1,0:T(8,128)(2,1)S(1)} %get-tuple-element.28.after), channel_id=1, source_target_pairs={{0,1},{1,0},{2,3},{3,2},{4,5},{5,4},{6,7},{7,6},{8,9},{9,8},{10,11... | collective-permute-start | bytes 491528 | tf_op jit(solution)/shard_map/ppermute | solution.py:333
  13.6 0.0 collective-permute-done.2.refs_2_.refs_3_.refs_0_
  13.6 0.2 weight_grads.4
  13.8 0.1 collective-permute-start.3
  13.9 9.9 %all-gather = bf16[2048,128]{1,0:T(8,128)(2,1)S(1)} all-gather(bf16[256,128]{1,0:T(8,128)(2,1)S(1)} %bundle.1), channel_id=2, replica_groups=mesh['replica'=8,'tensor'=4] {'replica'}, dimensions={0}, use_global_device_ids=true | all-gather | bytes 589824 | tf_op jit(solution)/shard_map/all_gather | solution.py:397
  23.8 0.0 collective-permute-done.5.refs_2_
  23.8 0.0 collective-permute-done.4.refs_1_
  23.8 0.0 copy-done
  23.8 0.0 copy-done.2
  23.8 0.7 %kept_rows.2 = (bf16[8,5120]{1,0:T(8,128)(2,1)S(1)}, f32[8,5120]{1,0:T(8,128)S(1)}) custom-call(f32[64,5120]{1,0:T(8,128)S(1)} %bitcast.12, bf16[1280,128]{1,0:T(8,128)(2,1)S(1)} %get-tuple-element.25.after.a_ref, bf16[1024,256]{1,0:T(8,128)(2,1)S(1)} %copy-done.2, bf16[8,256,128]{2,1,0:T(8,128)(2,1)S(1)} %bitcast.8, ...), custom_call_target="tpu_custom_call" | custom-call | flops 94371840 | bytes 1474560 | tf_op jit(solution)/shard_map/kept_rows/pallas_call | solution.py:81
  24.5 0.0 collective-permute-done.3.refs_0_.refs_3_
  24.5 0.0 copy-start.3
  24.5 0.0 copy-start.4
  24.6 0.0 copy-start.1
  24.6 0.5 %kept_rows.3 = (bf16[8,5120]{1,0:T(8,128)(2,1)S(1)}, f32[8,5120]{1,0:T(8,128)S(1)}) custom-call(f32[64,5120]{1,0:T(8,128)S(1)} %bitcast.13, bf16[1280,128]{1,0:T(8,128)(2,1)S(1)} %get-tuple-element.25.after.a_ref, bf16[1024,256]{1,0:T(8,128)(2,1)S(1)} %copy-done.2, bf16[8,256,128]{2,1,0:T(8,128)(2,1)S(1)} %bitcast.9, ...), custom_call_target="tpu_custom_call", output_to_operand_aliasing={{0}: (5, {}), {1}: (6, {})} | custom-call | flops 31457280 | bytes 491520 | tf_op jit(solution)/shard_map/kept_rows/pallas_call | solution.py:81
  25.1 1.9 %collective-permute-start.8 = (bf16[8,5120]{1,0:T(8,128)(2,1)S(1)}, bf16[8,5120]{1,0:T(8,128)(2,1)S(1)}, u32[]{:S(2)}, u32[]{:S(2)}) collective-permute-start(bf16[8,5120]{1,0:T(8,128)(2,1)S(1)} %get-tuple-element.38.refs_0_), channel_id=1, source_target_pairs={{0,24},{4,28},{8,16},{12,20},{16,8},{20,12},{24,0},{28,4},{1,25},{... | collective-permute-start | bytes 245768 | tf_op jit(solution)/shard_map/ppermute | solution.py:338
  27.0 1.1 %collective-permute-start.7 = (bf16[8,5120]{1,0:T(8,128)(2,1)S(1)}, bf16[8,5120]{1,0:T(8,128)(2,1)S(1)}, u32[]{:S(2)}, u32[]{:S(2)}) collective-permute-start(bf16[8,5120]{1,0:T(8,128)(2,1)S(1)} %get-tuple-element.38.refs_0_), channel_id=1, source_target_pairs={{0,16},{4,20},{8,24},{12,28},{16,0},{20,4},{24,8},{28,12},{1,17},{... | collective-permute-start | bytes 245768 | tf_op jit(solution)/shard_map/ppermute | solution.py:338
  28.1 0.5 %collective-permute-start.6 = (bf16[8,5120]{1,0:T(8,128)(2,1)S(1)}, bf16[8,5120]{1,0:T(8,128)(2,1)S(1)}, u32[]{:S(2)}, u32[]{:S(2)}) collective-permute-start(bf16[8,5120]{1,0:T(8,128)(2,1)S(1)} %get-tuple-element.38.refs_0_), channel_id=1, source_target_pairs={{0,8},{4,12},{8,0},{12,4},{16,24},{20,28},{24,16},{28,20},{1,9},{5... | collective-permute-start | bytes 245768 | tf_op jit(solution)/shard_map/ppermute | solution.py:338
  28.6 0.0 copy-done.3
  28.6 0.0 copy-done.4
  28.6 1.1 %places.1 = (bf16[64,2560]{1,0:T(8,128)(2,1)S(1)}, bf16[64,2560]{1,0:T(8,128)(2,1)S(1)}, bf16[64,2560]{1,0:T(8,128)(2,1)S(1)}, bf16[64,2560]{1,0:T(8,128)(2,1)S(1)}) custom-call(s32[8]{0:T(128)S(1)} %copy-done.3, s32[8]{0:T(128)S(1)} %copy-done.4, bf16[128,256]{1,0:T(8,128)(2,1)S(1)} %get-tuple-element.24.small, bf16[8,256,128]{2,1,0:T(8,128)(2,1)S(1)} %bitcast.10), custom_call_target="tpu_custom_call" | custom-call | tf_op jit(solution)/shard_map/places/pallas_call | solution.py:81
  29.8 0.0 copy-done.1
  29.8 1.0 %input_grads.1.refs_5_ = bf16[128,1280]{1,0:T(8,128)(2,1)} custom-call(bf16[64,5120]{1,0:T(8,128)(2,1)S(1)} %copy-done.1, bf16[8,256,128]{2,1,0:T(8,128)(2,1)S(1)} %bitcast.11, bf16[64,128]{1,0:T(8,128)(2,1)S(1)} %get-tuple-element.27.refs_1_.refs_0_, bf16[144,128]{1,0:T(8,128)(2,1)S(1)} %collective-permute-done.refs_0_.refs_1_, ...), custom_call_target="tpu_custom_call" | custom-call | flops 83886080 | bytes 983040 | tf_op jit(solution)/shard_map/input_grads/pallas_call | solution.py:81
  30.8 1.3 %new_momentums.1.refs_4_ = f32[64,5120]{1,0:T(8,128)} custom-call(f32[64,5120]{1,0:T(8,128)S(1)} %bitcast.14, bf16[64,2560]{1,0:T(8,128)(2,1)S(1)} %get-tuple-element.31.p_ref, f32[8,5120]{1,0:T(8,128)S(1)} %get-tuple-element.35.q, f32[64,1280]{1,0:T(8,128)S(1)} %get-tuple-element.32.refs_0_, bf16[64,1280]{1,0:T(8,128)(2,1)S(1)} %collective-permute-done.4.refs_1_, ...), custom_call_target="tpu_custom_call" | custom-call | flops 125829120 | bytes 3276800 | tf_op jit(solution)/shard_map/new_momentums/pallas_call | solution.py:81
  32.1 0.0 collective-permute-done.8.refs_3_
  32.1 0.4 %collective-permute-done.7.refs_2_ = bf16[8,5120]{1,0:T(8,128)(2,1)S(1)} collective-permute-done((bf16[8,5120]{1,0:T(8,128)(2,1)S(1)}, bf16[8,5120]{1,0:T(8,128)(2,1)S(1)}, u32[]{:S(2)}, u32[]{:S(2)}) %collective-permute-start.7) | collective-permute-done | bytes 81952 | tf_op jit(solution)/shard_map/ppermute | solution.py:338
  32.5 0.0 collective-permute-done.6.refs_1_
  32.6 0.1 collective-permute-start.9
  32.6 0.5 %half_updates.1.half_sum = f32[1280,256]{1,0:T(8,128)S(1)} custom-call(bf16[64,2560]{1,0:T(8,128)(2,1)S(1)} %get-tuple-element.36.refs_6_.p_hi, bf16[64,2560]{1,0:T(8,128)(2,1)S(1)} %get-tuple-element.37.p_lo, bf16[4,8,5120]{2,1,0:T(8,128)(2,1)S(1)} %join_kept.1.mine), custom_call_target="tpu_custom_call" | custom-call | tf_op jit(solution)/shard_map/half_updates/pallas_call | solution.py:81
  33.1 1.1 %collective-permute-done.9.other = bf16[4,8,5120]{2,1,0:T(8,128)(2,1)S(1)} collective-permute-done((bf16[4,8,5120]{2,1,0:T(8,128)(2,1)S(1)}, bf16[4,8,5120]{2,1,0:T(8,128)(2,1)S(1)}, u32[]{:S(2)}, u32[]{:S(2)}) %collective-permute-start.9) | collective-permute-done | bytes 327712 | tf_op jit(solution)/shard_map/ppermute | solution.py:338
  34.3 1.3 %updates.1 = f32[64,5120]{1,0:T(8,128)} custom-call(f32[1280,256]{1,0:T(8,128)S(1)} %half_updates.1.half_sum, bf16[64,2560]{1,0:T(8,128)(2,1)S(1)} %get-tuple-element.39.p_hi, bf16[64,2560]{1,0:T(8,128)(2,1)S(1)} %get-tuple-element.40.p_lo, bf16[4,8,5120]{2,1,0:T(8,128)(2,1)S(1)} %collective-permute-done.9.other), custom_call_target="tpu_custom_call" | custom-call | flops 671088640 | bytes 2621440 | tf_op jit(solution)/shard_map/updates/pallas_call | solution.py:81
  (2 shorter events, 0.0 us)
Async XLA Ops:
  1.8 6.5 %collective-permute-start.1 = (bf16[144,128]{1,0:T(8,128)(2,1)S(1)}, bf16[144,128]{1,0:T(8,128)(2,1)S(1)}, u32[]{:S(2)}, u32[]{:S(2)}) collective-permute-start(bf16[144,128]{1,0:T(8,128)(2,1)S(1)} %get-tuple-element.29), channel_id=1, source_target_pairs={{0,2},{1,3},{2,0},{3,1},{4,6},{5,7},{6,4},{7,5},{8,10},{9,11},{10,... | collective-permute-start | bytes 110600 | tf_op jit(solution)/shard_map/ppermute | solution.py:333
  5.9 5.4 %collective-permute-start = (bf16[144,128]{1,0:T(8,128)(2,1)S(1)}, bf16[144,128]{1,0:T(8,128)(2,1)S(1)}, u32[]{:S(2)}, u32[]{:S(2)}) collective-permute-start(bf16[144,128]{1,0:T(8,128)(2,1)S(1)} %get-tuple-element.26), channel_id=1, source_target_pairs={{0,1},{1,0},{2,3},{3,2},{4,5},{5,4},{6,7},{7,6},{8,9},{9,8},{10,11... | collective-permute-start | bytes 110600 | tf_op jit(solution)/shard_map/ppermute | solution.py:333
  7.5 6.2 %collective-permute-start.2 = (bf16[144,128]{1,0:T(8,128)(2,1)S(1)}, bf16[144,128]{1,0:T(8,128)(2,1)S(1)}, u32[]{:S(2)}, u32[]{:S(2)}) collective-permute-start(bf16[144,128]{1,0:T(8,128)(2,1)S(1)} %get-tuple-element.30), channel_id=1, source_target_pairs={{0,3},{1,2},{2,1},{3,0},{4,7},{5,6},{6,5},{7,4},{8,11},{9,10},{10,... | collective-permute-start | bytes 110600 | tf_op jit(solution)/shard_map/ppermute | solution.py:333
  8.5 15.3 %copy-start = (f32[1,64,5120]{2,1,0:T(8,128)S(1)}, f32[1,64,5120]{2,1,0:T(8,128)}, u32[]{:S(2)}) copy-start(f32[1,64,5120]{2,1,0:T(8,128)} %param.14) | copy-start | bytes 3932164
  8.5 15.3 %copy-start.2 = (bf16[1024,256]{1,0:T(8,128)(2,1)S(1)}, bf16[1024,256]{1,0:T(8,128)(2,1)}, u32[]{:S(2)}) copy-start(bf16[1024,256]{1,0:T(8,128)(2,1)} %constant.4.clone.tab) | copy-start | bytes 1572868
  8.5 15.3 %collective-permute-start.5 = (bf16[64,1280]{1,0:T(8,128)(2,1)S(1)}, bf16[64,1280]{1,0:T(8,128)(2,1)S(1)}, u32[]{:S(2)}, u32[]{:S(2)}) collective-permute-start(bf16[64,1280]{1,0:T(8,128)(2,1)S(1)} %weight_grads.5), channel_id=1, source_target_pairs={{0,2},{1,3},{2,0},{3,1},{4,6},{5,7},{6,4},{7,5},{8,10},{9,11},{10,... | collective-permute-start | bytes 491528 | tf_op jit(solution)/shard_map/ppermute | solution.py:333
  11.5 12.3 %collective-permute-start.4 = (bf16[64,1280]{1,0:T(8,128)(2,1)S(1)}, bf16[64,1280]{1,0:T(8,128)(2,1)S(1)}, u32[]{:S(2)}, u32[]{:S(2)}) collective-permute-start(bf16[64,1280]{1,0:T(8,128)(2,1)S(1)} %get-tuple-element.28.after), channel_id=1, source_target_pairs={{0,1},{1,0},{2,3},{3,2},{4,5},{5,4},{6,7},{7,6},{8,9},{9,8},{10,11... | collective-permute-start | bytes 491528 | tf_op jit(solution)/shard_map/ppermute | solution.py:333
  13.8 10.7 %collective-permute-start.3 = (bf16[64,1280]{1,0:T(8,128)(2,1)S(1)}, bf16[64,1280]{1,0:T(8,128)(2,1)S(1)}, u32[]{:S(2)}, u32[]{:S(2)}) collective-permute-start(bf16[64,1280]{1,0:T(8,128)(2,1)S(1)} %weight_grads.4), channel_id=1, source_target_pairs={{0,3},{1,2},{2,1},{3,0},{4,7},{5,6},{6,5},{7,4},{8,11},{9,10},{10,... | collective-permute-start | bytes 491528 | tf_op jit(solution)/shard_map/ppermute | solution.py:333
  24.5 4.1 %copy-start.3 = (s32[8]{0:T(128)S(1)}, s32[8]{0:T(128)}, u32[]{:S(2)}) copy-start(s32[8]{0:T(128)} %mask.1) | copy-start | bytes 100
  24.5 4.1 %copy-start.4 = (s32[8]{0:T(128)S(1)}, s32[8]{0:T(128)}, u32[]{:S(2)}) copy-start(s32[8]{0:T(128)} %tally.1) | copy-start | bytes 100
  24.6 5.2 %copy-start.1 = (bf16[64,5120]{1,0:T(8,128)(2,1)S(1)}, bf16[64,5120]{1,0:T(8,128)(2,1)}, u32[]{:S(2)}) copy-start(bf16[64,5120]{1,0:T(8,128)(2,1)} %exp_ref.3) | copy-start | bytes 1966084
  25.1 7.0 %collective-permute-start.8 = (bf16[8,5120]{1,0:T(8,128)(2,1)S(1)}, bf16[8,5120]{1,0:T(8,128)(2,1)S(1)}, u32[]{:S(2)}, u32[]{:S(2)}) collective-permute-start(bf16[8,5120]{1,0:T(8,128)(2,1)S(1)} %get-tuple-element.38.refs_0_), channel_id=1, source_target_pairs={{0,24},{4,28},{8,16},{12,20},{16,8},{20,12},{24,0},{28,4},{1,25},{... | collective-permute-start | bytes 245768 | tf_op jit(solution)/shard_map/ppermute | solution.py:338
  27.0 5.5 %collective-permute-start.7 = (bf16[8,5120]{1,0:T(8,128)(2,1)S(1)}, bf16[8,5120]{1,0:T(8,128)(2,1)S(1)}, u32[]{:S(2)}, u32[]{:S(2)}) collective-permute-start(bf16[8,5120]{1,0:T(8,128)(2,1)S(1)} %get-tuple-element.38.refs_0_), channel_id=1, source_target_pairs={{0,16},{4,20},{8,24},{12,28},{16,0},{20,4},{24,8},{28,12},{1,17},{... | collective-permute-start | bytes 245768 | tf_op jit(solution)/shard_map/ppermute | solution.py:338
  28.1 4.4 %collective-permute-start.6 = (bf16[8,5120]{1,0:T(8,128)(2,1)S(1)}, bf16[8,5120]{1,0:T(8,128)(2,1)S(1)}, u32[]{:S(2)}, u32[]{:S(2)}) collective-permute-start(bf16[8,5120]{1,0:T(8,128)(2,1)S(1)} %get-tuple-element.38.refs_0_), channel_id=1, source_target_pairs={{0,8},{4,12},{8,0},{12,4},{16,24},{20,28},{24,16},{28,20},{1,9},{5... | collective-permute-start | bytes 245768 | tf_op jit(solution)/shard_map/ppermute | solution.py:338
  32.6 1.7 %collective-permute-start.9 = (bf16[4,8,5120]{2,1,0:T(8,128)(2,1)S(1)}, bf16[4,8,5120]{2,1,0:T(8,128)(2,1)S(1)}, u32[]{:S(2)}, u32[]{:S(2)}) collective-permute-start(bf16[4,8,5120]{2,1,0:T(8,128)(2,1)S(1)} %join_kept.1.mine), channel_id=1, source_target_pairs={{0,4},{4,0},{8,12},{12,8},{16,20},{20,16},{24,28},{28,24},{1,5},{5... | collective-permute-start | bytes 983048 | tf_op jit(solution)/shard_map/ppermute | solution.py:338

commit v17 on v16

--- a/solution.py
+++ b/solution.py
@@ -148,7 +148,7 @@
 
 
 def join_body(n, *refs):
-    for i, ref in enumerate(refs[:n]):
+    for i, ref in enumerate(reversed(refs[:n])):
         refs[-1][i] = ref[...]
 
 
@@ -397,7 +397,7 @@
     bundles = lax.all_gather(bundle, "replica", axis=0)
 
     rows = []
-    for ks in ([k for k in range(n_t) if k != n_t - 1], [n_t - 1]):
+    for ks in ([0, *order[:-2]], order[-2:]) if n_t > 2 else ([0], [1]):
         n = len(ks)
         rows = call(
             functools.partial(kept_body, ks, n_t, keep),
@@ -447,7 +447,7 @@
     mine = call(
         functools.partial(join_body, half),
         near((half, keep, width)),
-        (*ships, far(new), far(input_grad), places[0]),
+        (*reversed(ships), far(new), far(input_grad), places[0]),
         [VM] * half + [ANY] * 3,
         VM,
         name="join_kept",

time: 35.8 us -> 36.8 us (1.028)
  waiting for transfers between devices: 1.85 us -> 2.59 us
    ppermute x6, waiting for transfers between devices: 0.32 us -> 0.77 us  [trade(): return lax.ppermute(x, 'tensor', [(i, i ^ k) for i in range(n_t)])]
where the time goes in v17:
time: 36.8 us; the launch traced here: 36.6 us
  starting transfers between devices  14.5 us (39%)
  blocking collectives  9.86 us (27%)
  Pallas kernels  8.84 us (24%)
  waiting for transfers between devices  2.59 us (7%)
  between operations  0.79 us (2%)
    ppermute x6, starting transfers between devices, trade(): return lax.ppermute(x, 'tensor', [(i, i ^ k) for i in range(n_t)])  10.8 us
    all_gather x1, blocking collectives, per_device(): bundles = lax.all_gather(bundle, 'replica', axis=0)  9.86 us
    pallas_call x14, Pallas kernels, call(): pl.pallas_call(body, out_shape=out_shape, in_specs=in_specs, out_specs=ou...  8.84 us
    ppermute x4, starting transfers between devices, swap(): return lax.ppermute(x, 'replica', [(i, i ^ m) for i in range(n_r)])  3.64 us
    ppermute x4, waiting for transfers between devices, swap(): return lax.ppermute(x, 'replica', [(i, i ^ m) for i in range(n_r)])  1.82 us
    ppermute x6, waiting for transfers between devices, trade(): return lax.ppermute(x, 'tensor', [(i, i ^ k) for i in range(n_t)])  0.77 us
  transfers between devices with their start and end apart: 10, of which 3 were waited for; matrix products, arithmetic and copies ran while one was open for 0% of the time, Pallas kernels for 16%

profile of v17, /device:TPU:0, one launch (start us, length us, event | category | flops | bytes accessed | tf_op | source)
XLA Modules:
  0.0 36.6 jit_solution(15651685345916402905)
XLA Ops:
  0.6 1.2 %up_grads.1 = (bf16[64,128]{1,0:T(8,128)(2,1)S(1)}, bf16[144,128]{1,0:T(8,128)(2,1)S(1)}, bf16[144,128]{1,0:T(8,128)(2,1)S(1)}, bf16[144,128]{1,0:T(8,128)(2,1)S...) custom-call(bf16[64,128]{1,0:T(8,128)(2,1)} %bitcast.16, ...), custom_call_target="tpu_custom_call" | custom-call | bytes 819200 | tf_op jit(solution)/shard_map/up_grads/pallas_call | solution.py:81
  1.8 4.1 %collective-permute-start.1 = (bf16[144,128]{1,0:T(8,128)(2,1)S(1)}, bf16[144,128]{1,0:T(8,128)(2,1)S(1)}, u32[]{:S(2)}, u32[]{:S(2)}) collective-permute-start(bf16[144,128]{1,0:T(8,128)(2,1)S(1)} %get-tuple-element.29), channel_id=1, source_target_pairs={{0,2},{1,3},{2,0},{3,1},{4,6},{5,7},{6,4},{7,5},{8,10},{9,11},{10,... | collective-permute-start | bytes 110600 | tf_op jit(solution)/shard_map/ppermute | solution.py:333
  5.9 1.3 %collective-permute-start.2 = (bf16[144,128]{1,0:T(8,128)(2,1)S(1)}, bf16[144,128]{1,0:T(8,128)(2,1)S(1)}, u32[]{:S(2)}, u32[]{:S(2)}) collective-permute-start(bf16[144,128]{1,0:T(8,128)(2,1)S(1)} %get-tuple-element.30), channel_id=1, source_target_pairs={{0,3},{1,2},{2,1},{3,0},{4,7},{5,6},{6,5},{7,4},{8,11},{9,10},{10,... | collective-permute-start | bytes 110600 | tf_op jit(solution)/shard_map/ppermute | solution.py:333
  7.2 0.2 collective-permute-start
  7.5 0.8 %collective-permute-done.1.refs_1_.refs_2_.refs_0_ = bf16[144,128]{1,0:T(8,128)(2,1)S(1)} collective-permute-done((bf16[144,128]{1,0:T(8,128)(2,1)S(1)}, bf16[144,128]{1,0:T(8,128)(2,1)S(1)}, u32[]{:S(2)}, u32[]{:S(2)}) %collective-permute-start.1) | collective-permute-done | bytes 36896 | tf_op jit(solution)/shard_map/ppermute | solution.py:333
  8.2 0.2 weight_grads.5
  8.4 0.0 copy-start
  8.4 0.0 copy-start.2
  8.4 3.0 %collective-permute-start.5 = (bf16[64,1280]{1,0:T(8,128)(2,1)S(1)}, bf16[64,1280]{1,0:T(8,128)(2,1)S(1)}, u32[]{:S(2)}, u32[]{:S(2)}) collective-permute-start(bf16[64,1280]{1,0:T(8,128)(2,1)S(1)} %weight_grads.5), channel_id=1, source_target_pairs={{0,2},{1,3},{2,0},{3,1},{4,6},{5,7},{6,4},{7,5},{8,10},{9,11},{10,... | collective-permute-start | bytes 491528 | tf_op jit(solution)/shard_map/ppermute | solution.py:333
  11.5 0.5 %own_places.1 = (bf16[64,2560]{1,0:T(8,128)(2,1)S(1)}, bf16[1280,128]{1,0:T(8,128)(2,1)S(1)}) custom-call(s32[8,80]{1,0:T(8,128)S(1)} %get-tuple-element.23.lines, bf16[128,256]{1,0:T(8,128)(2,1)S(1)} %get-tuple-element.24.small), custom_call_target="tpu_custom_call" | custom-call | tf_op jit(solution)/shard_map/own_places/pallas_call | solution.py:81
  12.0 0.0 collective-permute-done.2.refs_2_.refs_3_.refs_0_
  12.0 0.2 weight_grads.4
  12.2 1.5 %collective-permute-start.3 = (bf16[64,1280]{1,0:T(8,128)(2,1)S(1)}, bf16[64,1280]{1,0:T(8,128)(2,1)S(1)}, u32[]{:S(2)}, u32[]{:S(2)}) collective-permute-start(bf16[64,1280]{1,0:T(8,128)(2,1)S(1)} %weight_grads.4), channel_id=1, source_target_pairs={{0,3},{1,2},{2,1},{3,0},{4,7},{5,6},{6,5},{7,4},{8,11},{9,10},{10,... | collective-permute-start | bytes 491528 | tf_op jit(solution)/shard_map/ppermute | solution.py:333
  13.7 0.0 collective-permute-done.refs_0_.refs_1_
  13.7 0.2 weight_grads.3
  13.9 0.6 %collective-permute-start.4 = (bf16[64,1280]{1,0:T(8,128)(2,1)S(1)}, bf16[64,1280]{1,0:T(8,128)(2,1)S(1)}, u32[]{:S(2)}, u32[]{:S(2)}) collective-permute-start(bf16[64,1280]{1,0:T(8,128)(2,1)S(1)} %get-tuple-element.28.after), channel_id=1, source_target_pairs={{0,1},{1,0},{2,3},{3,2},{4,5},{5,4},{6,7},{7,6},{8,9},{9,8},{10,11... | collective-permute-start | bytes 491528 | tf_op jit(solution)/shard_map/ppermute | solution.py:333
  14.6 9.9 %all-gather = bf16[2048,128]{1,0:T(8,128)(2,1)S(1)} all-gather(bf16[256,128]{1,0:T(8,128)(2,1)S(1)} %bundle.1), channel_id=2, replica_groups=mesh['replica'=8,'tensor'=4] {'replica'}, dimensions={0}, use_global_device_ids=true | all-gather | bytes 589824 | tf_op jit(solution)/shard_map/all_gather | solution.py:397
  24.4 0.0 collective-permute-done.5.refs_1_.refs_2_
  24.5 0.0 copy-done
  24.5 0.0 copy-done.2
  24.5 0.6 %kept_rows.2 = (bf16[8,5120]{1,0:T(8,128)(2,1)S(1)}, f32[8,5120]{1,0:T(8,128)S(1)}) custom-call(f32[64,5120]{1,0:T(8,128)S(1)} %bitcast.12, bf16[1280,128]{1,0:T(8,128)(2,1)S(1)} %get-tuple-element.25.after.a_ref, bf16[1024,256]{1,0:T(8,128)(2,1)S(1)} %copy-done.2, bf16[8,256,128]{2,1,0:T(8,128)(2,1)S(1)} %bitcast.8, ...), custom_call_target="tpu_custom_call" | custom-call | flops 62914560 | bytes 983040 | tf_op jit(solution)/shard_map/kept_rows/pallas_call | solution.py:81
  25.1 0.0 collective-permute-done.3.refs_0_.refs_3_
  25.1 0.0 collective-permute-done.4.refs_1_
  25.1 0.0 copy-start.3
  25.1 0.0 copy-start.4
  25.1 0.0 copy-start.1
  25.1 0.6 %kept_rows.3 = (bf16[8,5120]{1,0:T(8,128)(2,1)S(1)}, f32[8,5120]{1,0:T(8,128)S(1)}) custom-call(f32[64,5120]{1,0:T(8,128)S(1)} %bitcast.13, bf16[1280,128]{1,0:T(8,128)(2,1)S(1)} %get-tuple-element.25.after.a_ref, bf16[1024,256]{1,0:T(8,128)(2,1)S(1)} %copy-done.2, bf16[8,256,128]{2,1,0:T(8,128)(2,1)S(1)} %bitcast.9, ...), custom_call_target="tpu_custom_call", output_to_operand_aliasing={{0}: (6, {}), {1}: (7, {})} | custom-call | flops 62914560 | bytes 983040 | tf_op jit(solution)/shard_map/kept_rows/pallas_call | solution.py:81
  25.8 1.6 %collective-permute-start.8 = (bf16[8,5120]{1,0:T(8,128)(2,1)S(1)}, bf16[8,5120]{1,0:T(8,128)(2,1)S(1)}, u32[]{:S(2)}, u32[]{:S(2)}) collective-permute-start(bf16[8,5120]{1,0:T(8,128)(2,1)S(1)} %get-tuple-element.38.refs_3_), channel_id=1, source_target_pairs={{0,8},{4,12},{8,0},{12,4},{16,24},{20,28},{24,16},{28,20},{1,9},{5... | collective-permute-start | bytes 245768 | tf_op jit(solution)/shard_map/ppermute | solution.py:338
  27.3 0.5 %collective-permute-start.7 = (bf16[8,5120]{1,0:T(8,128)(2,1)S(1)}, bf16[8,5120]{1,0:T(8,128)(2,1)S(1)}, u32[]{:S(2)}, u32[]{:S(2)}) collective-permute-start(bf16[8,5120]{1,0:T(8,128)(2,1)S(1)} %get-tuple-element.38.refs_3_), channel_id=1, source_target_pairs={{0,16},{4,20},{8,24},{12,28},{16,0},{20,4},{24,8},{28,12},{1,17},{... | collective-permute-start | bytes 245768 | tf_op jit(solution)/shard_map/ppermute | solution.py:338
  27.9 1.5 %collective-permute-start.6 = (bf16[8,5120]{1,0:T(8,128)(2,1)S(1)}, bf16[8,5120]{1,0:T(8,128)(2,1)S(1)}, u32[]{:S(2)}, u32[]{:S(2)}) collective-permute-start(bf16[8,5120]{1,0:T(8,128)(2,1)S(1)} %get-tuple-element.38.refs_3_), channel_id=1, source_target_pairs={{0,24},{4,28},{8,16},{12,20},{16,8},{20,12},{24,0},{28,4},{1,25},{... | collective-permute-start | bytes 245768 | tf_op jit(solution)/shard_map/ppermute | solution.py:338
  29.3 0.0 copy-done.3
  29.3 0.0 copy-done.4
  29.3 1.1 %places.1 = (bf16[64,2560]{1,0:T(8,128)(2,1)S(1)}, bf16[64,2560]{1,0:T(8,128)(2,1)S(1)}, bf16[64,2560]{1,0:T(8,128)(2,1)S(1)}, bf16[64,2560]{1,0:T(8,128)(2,1)S(1)}) custom-call(s32[8]{0:T(128)S(1)} %copy-done.3, s32[8]{0:T(128)S(1)} %copy-done.4, bf16[128,256]{1,0:T(8,128)(2,1)S(1)} %get-tuple-element.24.small, bf16[8,256,128]{2,1,0:T(8,128)(2,1)S(1)} %bitcast.10), custom_call_target="tpu_custom_call" | custom-call | tf_op jit(solution)/shard_map/places/pallas_call | solution.py:81
  30.5 0.0 copy-done.1
  30.5 1.0 %input_grads.1.refs_5_ = bf16[128,1280]{1,0:T(8,128)(2,1)} custom-call(bf16[64,5120]{1,0:T(8,128)(2,1)S(1)} %copy-done.1, bf16[8,256,128]{2,1,0:T(8,128)(2,1)S(1)} %bitcast.11, bf16[64,128]{1,0:T(8,128)(2,1)S(1)} %get-tuple-element.27.refs_1_.refs_0_, bf16[144,128]{1,0:T(8,128)(2,1)S(1)} %collective-permute-done.refs_0_.refs_1_, ...), custom_call_target="tpu_custom_call" | custom-call | flops 83886080 | bytes 983040 | tf_op jit(solution)/shard_map/input_grads/pallas_call | solution.py:81
  31.5 1.3 %new_momentums.1.refs_4_ = f32[64,5120]{1,0:T(8,128)} custom-call(f32[64,5120]{1,0:T(8,128)S(1)} %bitcast.14, bf16[64,2560]{1,0:T(8,128)(2,1)S(1)} %get-tuple-element.31.p_ref, f32[8,5120]{1,0:T(8,128)S(1)} %get-tuple-element.35.q, f32[64,1280]{1,0:T(8,128)S(1)} %get-tuple-element.32.refs_0_, bf16[64,1280]{1,0:T(8,128)(2,1)S(1)} %collective-permute-done.4.refs_1_, ...), custom_call_target="tpu_custom_call" | custom-call | flops 125829120 | bytes 3276800 | tf_op jit(solution)/shard_map/new_momentums/pallas_call | solution.py:81
  32.8 0.0 collective-permute-done.8.refs_2_
  32.8 0.7 %collective-permute-done.7.refs_1_ = bf16[8,5120]{1,0:T(8,128)(2,1)S(1)} collective-permute-done((bf16[8,5120]{1,0:T(8,128)(2,1)S(1)}, bf16[8,5120]{1,0:T(8,128)(2,1)S(1)}, u32[]{:S(2)}, u32[]{:S(2)}) %collective-permute-start.7) | collective-permute-done | bytes 81952 | tf_op jit(solution)/shard_map/ppermute | solution.py:338
  33.5 0.0 collective-permute-done.6.refs_0_
  33.6 0.1 collective-permute-start.9
  33.7 0.5 %half_updates.1.half_sum = f32[1280,256]{1,0:T(8,128)S(1)} custom-call(bf16[64,2560]{1,0:T(8,128)(2,1)S(1)} %get-tuple-element.36.refs_6_.p_hi, bf16[64,2560]{1,0:T(8,128)(2,1)S(1)} %get-tuple-element.37.p_lo, bf16[4,8,5120]{2,1,0:T(8,128)(2,1)S(1)} %join_kept.1.mine), custom_call_target="tpu_custom_call" | custom-call | tf_op jit(solution)/shard_map/half_updates/pallas_call | solution.py:81
  34.1 1.1 %collective-permute-done.9.other = bf16[4,8,5120]{2,1,0:T(8,128)(2,1)S(1)} collective-permute-done((bf16[4,8,5120]{2,1,0:T(8,128)(2,1)S(1)}, bf16[4,8,5120]{2,1,0:T(8,128)(2,1)S(1)}, u32[]{:S(2)}, u32[]{:S(2)}) %collective-permute-start.9) | collective-permute-done | bytes 327712 | tf_op jit(solution)/shard_map/ppermute | solution.py:338
  35.3 1.3 %updates.1 = f32[64,5120]{1,0:T(8,128)} custom-call(f32[1280,256]{1,0:T(8,128)S(1)} %half_updates.1.half_sum, bf16[64,2560]{1,0:T(8,128)(2,1)S(1)} %get-tuple-element.39.p_hi, bf16[64,2560]{1,0:T(8,128)(2,1)S(1)} %get-tuple-element.40.p_lo, bf16[4,8,5120]{2,1,0:T(8,128)(2,1)S(1)} %collective-permute-done.9.other), custom_call_target="tpu_custom_call" | custom-call | flops 671088640 | bytes 2621440 | tf_op jit(solution)/shard_map/updates/pallas_call | solution.py:81
  (2 shorter events, 0.0 us)
Async XLA Ops:
  1.8 6.4 %collective-permute-start.1 = (bf16[144,128]{1,0:T(8,128)(2,1)S(1)}, bf16[144,128]{1,0:T(8,128)(2,1)S(1)}, u32[]{:S(2)}, u32[]{:S(2)}) collective-permute-start(bf16[144,128]{1,0:T(8,128)(2,1)S(1)} %get-tuple-element.29), channel_id=1, source_target_pairs={{0,2},{1,3},{2,0},{3,1},{4,6},{5,7},{6,4},{7,5},{8,10},{9,11},{10,... | collective-permute-start | bytes 110600 | tf_op jit(solution)/shard_map/ppermute | solution.py:333
  5.9 6.1 %collective-permute-start.2 = (bf16[144,128]{1,0:T(8,128)(2,1)S(1)}, bf16[144,128]{1,0:T(8,128)(2,1)S(1)}, u32[]{:S(2)}, u32[]{:S(2)}) collective-permute-start(bf16[144,128]{1,0:T(8,128)(2,1)S(1)} %get-tuple-element.30), channel_id=1, source_target_pairs={{0,3},{1,2},{2,1},{3,0},{4,7},{5,6},{6,5},{7,4},{8,11},{9,10},{10,... | collective-permute-start | bytes 110600 | tf_op jit(solution)/shard_map/ppermute | solution.py:333
  7.2 6.5 %collective-permute-start = (bf16[144,128]{1,0:T(8,128)(2,1)S(1)}, bf16[144,128]{1,0:T(8,128)(2,1)S(1)}, u32[]{:S(2)}, u32[]{:S(2)}) collective-permute-start(bf16[144,128]{1,0:T(8,128)(2,1)S(1)} %get-tuple-element.26), channel_id=1, source_target_pairs={{0,1},{1,0},{2,3},{3,2},{4,5},{5,4},{6,7},{7,6},{8,9},{9,8},{10,11... | collective-permute-start | bytes 110600 | tf_op jit(solution)/shard_map/ppermute | solution.py:333
  8.4 16.0 %copy-start = (f32[1,64,5120]{2,1,0:T(8,128)S(1)}, f32[1,64,5120]{2,1,0:T(8,128)}, u32[]{:S(2)}) copy-start(f32[1,64,5120]{2,1,0:T(8,128)} %param.14) | copy-start | bytes 3932164
  8.4 16.0 %copy-start.2 = (bf16[1024,256]{1,0:T(8,128)(2,1)S(1)}, bf16[1024,256]{1,0:T(8,128)(2,1)}, u32[]{:S(2)}) copy-start(bf16[1024,256]{1,0:T(8,128)(2,1)} %constant.4.clone.tab) | copy-start | bytes 1572868
  8.4 16.0 %collective-permute-start.5 = (bf16[64,1280]{1,0:T(8,128)(2,1)S(1)}, bf16[64,1280]{1,0:T(8,128)(2,1)S(1)}, u32[]{:S(2)}, u32[]{:S(2)}) collective-permute-start(bf16[64,1280]{1,0:T(8,128)(2,1)S(1)} %weight_grads.5), channel_id=1, source_target_pairs={{0,2},{1,3},{2,0},{3,1},{4,6},{5,7},{6,4},{7,5},{8,10},{9,11},{10,... | collective-permute-start | bytes 491528 | tf_op jit(solution)/shard_map/ppermute | solution.py:333
  12.2 12.9 %collective-permute-start.3 = (bf16[64,1280]{1,0:T(8,128)(2,1)S(1)}, bf16[64,1280]{1,0:T(8,128)(2,1)S(1)}, u32[]{:S(2)}, u32[]{:S(2)}) collective-permute-start(bf16[64,1280]{1,0:T(8,128)(2,1)S(1)} %weight_grads.4), channel_id=1, source_target_pairs={{0,3},{1,2},{2,1},{3,0},{4,7},{5,6},{6,5},{7,4},{8,11},{9,10},{10,... | collective-permute-start | bytes 491528 | tf_op jit(solution)/shard_map/ppermute | solution.py:333
  13.9 11.1 %collective-permute-start.4 = (bf16[64,1280]{1,0:T(8,128)(2,1)S(1)}, bf16[64,1280]{1,0:T(8,128)(2,1)S(1)}, u32[]{:S(2)}, u32[]{:S(2)}) collective-permute-start(bf16[64,1280]{1,0:T(8,128)(2,1)S(1)} %get-tuple-element.28.after), channel_id=1, source_target_pairs={{0,1},{1,0},{2,3},{3,2},{4,5},{5,4},{6,7},{7,6},{8,9},{9,8},{10,11... | collective-permute-start | bytes 491528 | tf_op jit(solution)/shard_map/ppermute | solution.py:333
  25.1 4.2 %copy-start.3 = (s32[8]{0:T(128)S(1)}, s32[8]{0:T(128)}, u32[]{:S(2)}) copy-start(s32[8]{0:T(128)} %mask.1) | copy-start | bytes 100
  25.1 4.2 %copy-start.4 = (s32[8]{0:T(128)S(1)}, s32[8]{0:T(128)}, u32[]{:S(2)}) copy-start(s32[8]{0:T(128)} %tally.1) | copy-start | bytes 100
  25.1 5.4 %copy-start.1 = (bf16[64,5120]{1,0:T(8,128)(2,1)S(1)}, bf16[64,5120]{1,0:T(8,128)(2,1)}, u32[]{:S(2)}) copy-start(bf16[64,5120]{1,0:T(8,128)(2,1)} %exp_ref.3) | copy-start | bytes 1966084
  25.8 7.1 %collective-permute-start.8 = (bf16[8,5120]{1,0:T(8,128)(2,1)S(1)}, bf16[8,5120]{1,0:T(8,128)(2,1)S(1)}, u32[]{:S(2)}, u32[]{:S(2)}) collective-permute-start(bf16[8,5120]{1,0:T(8,128)(2,1)S(1)} %get-tuple-element.38.refs_3_), channel_id=1, source_target_pairs={{0,8},{4,12},{8,0},{12,4},{16,24},{20,28},{24,16},{28,20},{1,9},{5... | collective-permute-start | bytes 245768 | tf_op jit(solution)/shard_map/ppermute | solution.py:338
  27.3 6.2 %collective-permute-start.7 = (bf16[8,5120]{1,0:T(8,128)(2,1)S(1)}, bf16[8,5120]{1,0:T(8,128)(2,1)S(1)}, u32[]{:S(2)}, u32[]{:S(2)}) collective-permute-start(bf16[8,5120]{1,0:T(8,128)(2,1)S(1)} %get-tuple-element.38.refs_3_), channel_id=1, source_target_pairs={{0,16},{4,20},{8,24},{12,28},{16,0},{20,4},{24,8},{28,12},{1,17},{... | collective-permute-start | bytes 245768 | tf_op jit(solution)/shard_map/ppermute | solution.py:338
  27.9 5.7 %collective-permute-start.6 = (bf16[8,5120]{1,0:T(8,128)(2,1)S(1)}, bf16[8,5120]{1,0:T(8,128)(2,1)S(1)}, u32[]{:S(2)}, u32[]{:S(2)}) collective-permute-start(bf16[8,5120]{1,0:T(8,128)(2,1)S(1)} %get-tuple-element.38.refs_3_), channel_id=1, source_target_pairs={{0,24},{4,28},{8,16},{12,20},{16,8},{20,12},{24,0},{28,4},{1,25},{... | collective-permute-start | bytes 245768 | tf_op jit(solution)/shard_map/ppermute | solution.py:338
  33.6 1.7 %collective-permute-start.9 = (bf16[4,8,5120]{2,1,0:T(8,128)(2,1)S(1)}, bf16[4,8,5120]{2,1,0:T(8,128)(2,1)S(1)}, u32[]{:S(2)}, u32[]{:S(2)}) collective-permute-start(bf16[4,8,5120]{2,1,0:T(8,128)(2,1)S(1)} %join_kept.1.mine), channel_id=1, source_target_pairs={{0,4},{4,0},{8,12},{12,8},{16,20},{20,16},{24,28},{28,24},{1,5},{5... | collective-permute-start | bytes 983048 | tf_op jit(solution)/shard_map/ppermute | solution.py:338

commit v18 on v16

--- a/solution.py
+++ b/solution.py
@@ -178,7 +178,7 @@
         p_ref[:, g * 2 * B : (g + 1) * 2 * B] = p.astype(BF16)
 
 
-def kept_body(ks, n_t, keep, vel, a_ref, tab, after, *refs):
+def kept_body(ks, n_t, keep, vel, a_ref, tab, after, after_too, *refs):
     keep_rows(ks, n_t, keep, vel, a_ref, tab, refs[: len(ks)], *refs[-2:])
 
 
@@ -237,37 +237,47 @@
         copy.wait()
 
 
-def places_body(keep, mask, tally, small, bundles, *p_refs):
-    n_r, last = bundles.shape[0], bundles.shape[1] - 16
-    half, nb = n_r // 2, G // B
+def places_body(keep, mask, tally, small, bundles, hi_ref, lo_ref, w_ref):
+    half = bundles.shape[0]
     rep = lax.axis_index("replica")
     total, alive = jnp.float32(0), jnp.float32(0)
-    for r in range(n_r):
+    for r in range(2 * half):
         m = mask[r].astype(F32)
         total = total + m * tally[r].astype(F32)
         alive = alive + m
-    scale = jnp.full((1, 2 * B), alive) / jnp.full((1, 2 * B), total)
-    freq = lax.broadcasted_iota(jnp.int32, (B, 2 * B), 0).astype(F32)
-    lane = lax.broadcasted_iota(jnp.int32, (1, 2 * B), 1)
-    block, place = lane // (half * keep), (lane // keep) % half
+    place = (lax.broadcasted_iota(jnp.int32, (8, 2 * B), 1) // keep) % half
+    scale = jnp.full((8, 2 * B), alive) / jnp.full((8, 2 * B), total)
+    ws = []
     for h in range(2):
-        hi_ref, lo_ref = p_refs[2 * h : 2 * h + 2]
-        w = jnp.zeros((1, 2 * B), F32)
+        w = jnp.zeros((8, 2 * B), F32)
         for i in range(half):
             r = rep ^ (2 * i + h)
             w = jnp.where(place == i, mask[r].astype(F32) * tally[r].astype(F32), w)
-        w = w * scale
-        rows = [bundles[rep ^ (2 * i + h), last:, :].astype(F32)[:keep] for i in range(half)]
-        rows = jnp.concatenate(rows * nb, axis=0).T
-        for g in range(hi_ref.shape[1] // (2 * B)):
-            num = rows[g * nb : g * nb + 1]
-            for j in range(1, nb):
-                num = jnp.where(block == j, rows[g * nb + j : g * nb + j + 1], num)
-            hot = jnp.where(freq == num, 1.0, 0.0).astype(BF16)
-            y = dot(small[:, 2 * B : 3 * B], hot)
-            hi, lo = split((y[:B] + y[B:]) * w)
-            hi_ref[:, g * 2 * B : (g + 1) * 2 * B] = hi
-            lo_ref[:, g * 2 * B : (g + 1) * 2 * B] = lo
+        ws.append(w * scale)
+    w_ref[...] = ws[1]
+    side_places(keep, ws[0][:1], small, bundles, hi_ref, lo_ref)
+
+
+def other_places_body(keep, w_ref, small, bundles, hi_ref, lo_ref):
+    side_places(keep, w_ref[:1, :], small, bundles, hi_ref, lo_ref)
+
+
+def side_places(keep, w, small, bundles, hi_ref, lo_ref):
+    half, last, nb = bundles.shape[0], bundles.shape[1] - 16, G // B
+    freq = lax.broadcasted_iota(jnp.int32, (B, 2 * B), 0).astype(F32)
+    block = lax.broadcasted_iota(jnp.int32, (1, 2 * B), 1) // (half * keep)
+    chip = lax.axis_index("replica") // 2
+    rows = [bundles[chip ^ i, last:, :].astype(F32)[:keep] for i in range(half)]
+    rows = jnp.concatenate(rows * nb, axis=0).T
+    for g in range(hi_ref.shape[1] // (2 * B)):
+        num = rows[g * nb : g * nb + 1]
+        for j in range(1, nb):
+            num = jnp.where(block == j, rows[g * nb + j : g * nb + j + 1], num)
+        hot = jnp.where(freq == num, 1.0, 0.0).astype(BF16)
+        y = dot(small[:, 2 * B : 3 * B], hot)
+        hi, lo = split((y[:B] + y[B:]) * w)
+        hi_ref[:, g * 2 * B : (g + 1) * 2 * B] = hi
+        lo_ref[:, g * 2 * B : (g + 1) * 2 * B] = lo
 
 
 def spread_rows(p_hi, p_lo, ships, g):
@@ -300,22 +310,25 @@
         copy.wait()
 
 
-def input_grad_body(n_t, n_r, cp, exp_ref, bundles, *refs):
-    ups, (out, held) = refs[:n_t], refs[n_t:]
-    cols = out.shape[1]
-    held[:B, :] = exp_ref[:, pl.ds(pl.multiple_of(lax.axis_index("tensor") * cols, 128), cols)]
-    nc = cols // cp
-    nr = B // (n_r // cp)
+def input_grad_body(n_t, h, exp_ref, bundles, *refs):
+    ups, (out, held, ready, sem) = refs[:n_t], refs[-4:]
+    half = bundles.shape[0]
+    nc, nr = held.shape[1], B // half
     tiles = nc // 128
-    for r in range(n_r):
-        r0, c0 = (r // cp) * nr, (r % cp) * nc
+    c0 = pl.multiple_of(lax.rem(lax.axis_index("replica") ^ h, 2) * nc, 128)
+    held[:B, :] = exp_ref[:, pl.ds(pl.multiple_of(lax.axis_index("tensor") * 2 * nc + c0, 128), nc)]
+    for i in range(half):
         for k in range(1, n_t):
+            row = k * B + i * nr
             for j in range(tiles):
                 at = ((k - 1) * tiles + j) * nr
-                held[k * B + r0 : k * B + r0 + nr, c0 + j * 128 : c0 + (j + 1) * 128] = bundles[r, at : at + nr, :]
+                held[row : row + nr, j * 128 : (j + 1) * 128] = bundles[i, at : at + nr, :]
     up = jnp.concatenate([u[:B, :] for u in ups], axis=0).T
-    for c in range(0, cols, G):
-        out[:, c : c + G] = dot(up, held[:, c : c + G]).astype(BF16)
+    for c in range(0, nc, 128):
+        ready[:, c : c + 128] = dot(up, held[:, c : c + 128]).astype(BF16)
+    copy = pltpu.make_async_copy(ready, out.at[:, pl.ds(c0, nc)], sem)
+    copy.start()
+    copy.wait()
 
 
 def per_device(n_t, n_r, act, switch, slope, exp, vel, lines, mask, tally):
@@ -394,7 +407,36 @@
         VM,
         name="bundle",
     )
-    bundles = lax.all_gather(bundle, "replica", axis=0)
+    sides = [[r for r in range(n_r) if r % 2 == h] for h in range(2)]
+    bundles = [lax.all_gather(bundle, "replica", axis=0, axis_index_groups=sides)]
+    bundles.append(swap(bundles[0], 1))
+
+    *mine_at, shares = call(
+        functools.partial(places_body, keep),
+        [near((B, blocks * half * keep))] * 2 + [near((8, 2 * B), F32)],
+        (mask, tally, small, bundles[0]),
+        [SM, SM, VM, VM],
+        [VM] * 3,
+        name="places",
+    )
+
+    def columns_of(h, so_far=()):
+        return call(
+            functools.partial(input_grad_body, n_t, h),
+            jax.ShapeDtypeStruct((tok, cols), BF16),
+            (exp, bundles[h], *parts, *so_far),
+            [VM] * (2 + n_t) + [ANY] * len(so_far),
+            ANY,
+            scratch=[
+                pltpu.VMEM((n_t * B, cols // cp), BF16),
+                pltpu.VMEM((tok, cols // cp), BF16),
+                pltpu.SemaphoreType.DMA,
+            ],
+            name="input_grads",
+            alias={2 + n_t: 0} if so_far else {},
+        )
+
+    first_columns = columns_of(0)
 
     rows = []
     for ks in ([k for k in range(n_t) if k != n_t - 1], [n_t - 1]):
@@ -402,35 +444,26 @@
         rows = call(
             functools.partial(kept_body, ks, n_t, keep),
             [near((keep, width)), near((keep, width), F32)],
-            (vel[0], a_own, tab, bundles, *[grads[k] for k in ks], *rows),
-            [VM] * 3 + [ANY] + [VM] * (n + len(rows)),
+            (vel[0], a_own, tab, mine_at[0], far(first_columns), *[grads[k] for k in ks], *rows),
+            [VM] * 3 + [ANY] * 2 + [VM] * (n + len(rows)),
             [VM] * 2,
             flops=6 * B * B * cols * n,
             nbytes=B * cols * 6 * n,
             name="kept_rows",
-            alias={4 + n: 0, 5 + n: 1} if rows else {},
+            alias={5 + n: 0, 6 + n: 1} if rows else {},
         )
     ship, q_own = rows
 
-    places = call(
-        functools.partial(places_body, keep),
-        [near((B, blocks * half * keep))] * 4,
-        (mask, tally, small, bundles),
-        [SM, SM, VM, VM],
-        [VM] * 4,
-        name="places",
-    )
-    input_grad = call(
-        functools.partial(input_grad_body, n_t, n_r, cp),
-        jax.ShapeDtypeStruct((tok, cols), BF16),
-        (exp, bundles, *parts),
-        [VM] * (2 + n_t),
-        VM,
-        scratch=[pltpu.VMEM((n_t * B, cols), BF16)],
-        flops=2 * tok * n_t * B * cols,
-        nbytes=(n_t * B * cols + tok * cols) * 2,
-        name="input_grads",
-    )
+
+    other_at = call(
+        functools.partial(other_places_body, keep),
+        [near((B, blocks * half * keep))] * 2,
+        (shares, small, bundles[1]),
+        [VM] * 3,
+        [VM] * 2,
+        name="other_places",
+    )
+    input_grad = columns_of(1, (far(first_columns),))
 
     ships = [ship] + [swap(ship, 2 * i) for i in range(1, half)]
     new = call(
@@ -447,8 +480,8 @@
     mine = call(
         functools.partial(join_body, half),
         near((half, keep, width)),
-        (*ships, far(new), far(input_grad), places[0]),
-        [VM] * half + [ANY] * 3,
+        (*ships, far(new), other_at[0]),
+        [VM] * half + [ANY] * 2,
         VM,
         name="join_kept",
     )
@@ -456,7 +489,7 @@
     half_sum = call(
         half_update_body,
         near((groups * B, G), F32),
-        (*places[:2], mine),
+        (*mine_at, mine),
         [VM] * 3,
         VM,
         name="half_updates",
@@ -465,7 +498,7 @@
     update = call(
         functools.partial(update_body, chunk),
         jax.ShapeDtypeStruct((B, width), F32),
-        (half_sum, *places[2:], other),
+        (half_sum, *other_at, other),
         [VM] * 4,
         ANY,
         scratch=[

time: 35.8 us -> 48.6 us (1.36)
  waiting for transfers between devices: 1.85 us -> 14 us
  Pallas kernels: 8.79 us -> 9.93 us
    ppermute x6, waiting for transfers between devices: 0.32 us -> 12.1 us  [trade(): return lax.ppermute(x, 'tensor', [(i, i ^ k) for i in range(n_t)])]
    pallas_call x14 -> x16, Pallas kernels: 8.79 us -> 9.93 us  [call(): pl.pallas_call(body, out_shape=out_shape, in_specs=in_specs, out_specs=ou...]
    ppermute x4 -> x5, waiting for transfers between devices: 1.53 us -> 1.97 us  [swap(): return lax.ppermute(x, 'replica', [(i, i ^ m) for i in range(n_r)])]
    ppermute x4 -> x5, starting transfers between devices: 3.62 us -> 3.61 us  [swap(): return lax.ppermute(x, 'replica', [(i, i ^ m) for i in range(n_r)])]
  transfers between devices with their start and end apart: 10 -> 11, of which waited for: 3 -> 8; matrix products, arithmetic and copies ran while one was open for 0% -> 0% of each run, Pallas kernels for 16% -> 15%
where the time goes in v18:
time: 48.6 us; the launch traced here: 48.1 us
  waiting for transfers between devices  14 us (29%)
  starting transfers between devices  13.8 us (28%)
  Pallas kernels  9.93 us (20%)
  blocking collectives  9.48 us (20%)
  between operations  0.81 us (2%)
    ppermute x6, waiting for transfers between devices, trade(): return lax.ppermute(x, 'tensor', [(i, i ^ k) for i in range(n_t)])  12.1 us
    ppermute x6, starting transfers between devices, trade(): return lax.ppermute(x, 'tensor', [(i, i ^ k) for i in range(n_t)])  10.2 us
    pallas_call x16, Pallas kernels, call(): pl.pallas_call(body, out_shape=out_shape, in_specs=in_specs, out_specs=ou...  9.93 us
    all_gather x1, blocking collectives, per_device(): lax.all_gather(bundle, 'replica', axis=0, axis_index_groups=sides)  9.48 us
    ppermute x5, starting transfers between devices, swap(): return lax.ppermute(x, 'replica', [(i, i ^ m) for i in range(n_r)])  3.61 us
    ppermute x5, waiting for transfers between devices, swap(): return lax.ppermute(x, 'replica', [(i, i ^ m) for i in range(n_r)])  1.97 us
  transfers between devices with their start and end apart: 11, of which 8 were waited for; matrix products, arithmetic and copies ran while one was open for 0% of the time, Pallas kernels for 15%

profile of v18, /device:TPU:0, one launch (start us, length us, event | category | flops | bytes accessed | tf_op | source)
XLA Modules:
  0.0 48.1 jit_solution(7896253366436554403)
XLA Ops:
  0.6 1.2 %up_grads.1 = (bf16[64,128]{1,0:T(8,128)(2,1)S(1)}, bf16[144,128]{1,0:T(8,128)(2,1)S(1)}, bf16[144,128]{1,0:T(8,128)(2,1)S(1)}, bf16[144,128]{1,0:T(8,128)(2,1)S...) custom-call(bf16[64,128]{1,0:T(8,128)(2,1)} %bitcast.15, ...), custom_call_target="tpu_custom_call" | custom-call | bytes 819200 | tf_op jit(solution)/shard_map/up_grads/pallas_call | solution.py:81
  1.8 3.1 %collective-permute-start = (bf16[144,128]{1,0:T(8,128)(2,1)S(1)}, bf16[144,128]{1,0:T(8,128)(2,1)S(1)}, u32[]{:S(2)}, u32[]{:S(2)}) collective-permute-start(bf16[144,128]{1,0:T(8,128)(2,1)S(1)} %get-tuple-element.27), channel_id=1, source_target_pairs={{0,1},{1,0},{2,3},{3,2},{4,5},{5,4},{6,7},{7,6},{8,9},{9,8},{10,11... | collective-permute-start | bytes 110600 | tf_op jit(solution)/shard_map/ppermute | solution.py:346
  4.9 2.6 %collective-permute-start.1 = (bf16[144,128]{1,0:T(8,128)(2,1)S(1)}, bf16[144,128]{1,0:T(8,128)(2,1)S(1)}, u32[]{:S(2)}, u32[]{:S(2)}) collective-permute-start(bf16[144,128]{1,0:T(8,128)(2,1)S(1)} %get-tuple-element.30), channel_id=1, source_target_pairs={{0,2},{1,3},{2,0},{3,1},{4,6},{5,7},{6,4},{7,5},{8,10},{9,11},{10,... | collective-permute-start | bytes 110600 | tf_op jit(solution)/shard_map/ppermute | solution.py:346
  7.5 0.0 collective-permute-start.2
  7.5 0.5 %own_places.1 = (bf16[64,2560]{1,0:T(8,128)(2,1)S(1)}, bf16[1280,128]{1,0:T(8,128)(2,1)S(1)}) custom-call(s32[8,80]{1,0:T(8,128)S(1)} %get-tuple-element.24.lines, bf16[128,256]{1,0:T(8,128)(2,1)S(1)} %get-tuple-element.25.small), custom_call_target="tpu_custom_call" | custom-call | tf_op jit(solution)/shard_map/own_places/pallas_call | solution.py:81
  8.0 0.0 collective-permute-done.refs_0_.refs_1_
  8.0 0.2 weight_grads.3
  8.3 0.0 copy-start.3
  8.3 0.0 copy-start.4
  8.3 2.1 %collective-permute-done.1.refs_1_.refs_2_.refs_0_ = bf16[144,128]{1,0:T(8,128)(2,1)S(1)} collective-permute-done((bf16[144,128]{1,0:T(8,128)(2,1)S(1)}, bf16[144,128]{1,0:T(8,128)(2,1)S(1)}, u32[]{:S(2)}, u32[]{:S(2)}) %collective-permute-start.1) | collective-permute-done | bytes 36896 | tf_op jit(solution)/shard_map/ppermute | solution.py:346
  10.4 2.8 %collective-permute-done.2.refs_2_.refs_3_.refs_0_ = bf16[144,128]{1,0:T(8,128)(2,1)S(1)} collective-permute-done((bf16[144,128]{1,0:T(8,128)(2,1)S(1)}, bf16[144,128]{1,0:T(8,128)(2,1)S(1)}, u32[]{:S(2)}, u32[]{:S(2)}) %collective-permute-start.2) | collective-permute-done | bytes 36896 | tf_op jit(solution)/shard_map/ppermute | solution.py:346
  13.2 0.0 copy-start.1
  13.2 9.5 %all-gather = bf16[1024,128]{1,0:T(8,128)(2,1)S(1)} all-gather(bf16[256,128]{1,0:T(8,128)(2,1)S(1)} %bundle.1), channel_id=2, replica_groups={{0,8,16,24},{4,12,20,28},{1,9,17,25},{5,13,21,29},{2,10,18,26},{6,14,22..., dimensions={0}, use_global_device_ids=true | all-gather | bytes 327680 | tf_op jit(solution)/shard_map/all_gather | solution.py:411
  22.7 0.0 collective-permute-start.3
  22.7 0.2 weight_grads.5
  22.9 0.0 copy-start
  22.9 0.0 copy-start.2
  22.9 0.1 collective-permute-start.6
  23.0 1.0 %collective-permute-start.5 = (bf16[64,1280]{1,0:T(8,128)(2,1)S(1)}, bf16[64,1280]{1,0:T(8,128)(2,1)S(1)}, u32[]{:S(2)}, u32[]{:S(2)}) collective-permute-start(bf16[64,1280]{1,0:T(8,128)(2,1)S(1)} %get-tuple-element.29.after), channel_id=1, source_target_pairs={{0,1},{1,0},{2,3},{3,2},{4,5},{5,4},{6,7},{7,6},{8,9},{9,8},{10,11... | collective-permute-start | bytes 491528 | tf_op jit(solution)/shard_map/ppermute | solution.py:346
  24.1 0.2 weight_grads.4
  24.3 3.4 %collective-permute-start.4 = (bf16[64,1280]{1,0:T(8,128)(2,1)S(1)}, bf16[64,1280]{1,0:T(8,128)(2,1)S(1)}, u32[]{:S(2)}, u32[]{:S(2)}) collective-permute-start(bf16[64,1280]{1,0:T(8,128)(2,1)S(1)} %weight_grads.4), channel_id=1, source_target_pairs={{0,3},{1,2},{2,1},{3,0},{4,7},{5,6},{6,5},{7,4},{8,11},{9,10},{10,... | collective-permute-start | bytes 491528 | tf_op jit(solution)/shard_map/ppermute | solution.py:346
  27.6 0.0 copy-done.3
  27.7 0.0 copy-done.4
  27.7 0.9 %places.1 = (bf16[64,2560]{1,0:T(8,128)(2,1)S(1)}, bf16[64,2560]{1,0:T(8,128)(2,1)S(1)}, f32[8,128]{1,0:T(8,128)S(1)}) custom-call(s32[8]{0:T(128)S(1)} %copy-done.3, s32[8]{0:T(128)S(1)} %copy-done.4, bf16[128,256]{1,0:T(8,128)(2,1)S(1)} %get-tuple-element.25.small, bf16[4,256,128]{2,1,0:T(8,128)(2,1)S(1)} %bitcast.12), custom_call_target="tpu_custom_call" | custom-call | tf_op jit(solution)/shard_map/places/pallas_call | solution.py:81
  28.6 0.0 copy-done.1
  28.6 1.0 %input_grads.2.refs_4_.after_too = bf16[128,1280]{1,0:T(8,128)(2,1)} custom-call(bf16[64,5120]{1,0:T(8,128)(2,1)S(1)} %copy-done.1, bf16[4,256,128]{2,1,0:T(8,128)(2,1)S(1)} %bitcast.13, bf16[64,128]{1,0:T(8,128)(2,1)S(1)} %get-tuple-element.28.refs_1_.refs_0_, bf16[144,128]{1,0:T(8,128)(2,1)S(1)} %collective-permute-done.refs_0_.refs_1_, ...), custom_call_target="tpu_custom_call" | custom-call | tf_op jit(solution)/shard_map/input_grads/pallas_call | solution.py:81
  29.6 3.4 %collective-permute-done.6.refs_2_ = bf16[64,1280]{1,0:T(8,128)(2,1)S(1)} collective-permute-done((bf16[64,1280]{1,0:T(8,128)(2,1)S(1)}, bf16[64,1280]{1,0:T(8,128)(2,1)S(1)}, u32[]{:S(2)}, u32[]{:S(2)}) %collective-permute-start.6) | collective-permute-done | bytes 163872 | tf_op jit(solution)/shard_map/ppermute | solution.py:346
  33.0 3.7 %collective-permute-done.5.refs_1_ = bf16[64,1280]{1,0:T(8,128)(2,1)S(1)} collective-permute-done((bf16[64,1280]{1,0:T(8,128)(2,1)S(1)}, bf16[64,1280]{1,0:T(8,128)(2,1)S(1)}, u32[]{:S(2)}, u32[]{:S(2)}) %collective-permute-start.5) | collective-permute-done | bytes 163872 | tf_op jit(solution)/shard_map/ppermute | solution.py:346
  36.7 0.0 copy-done
  36.7 0.0 copy-done.2
  36.7 0.7 %kept_rows.2 = (bf16[8,5120]{1,0:T(8,128)(2,1)S(1)}, f32[8,5120]{1,0:T(8,128)S(1)}) custom-call(f32[64,5120]{1,0:T(8,128)S(1)} %bitcast.8, bf16[1280,128]{1,0:T(8,128)(2,1)S(1)} %get-tuple-element.26.after.a_ref, bf16[1024,256]{1,0:T(8,128)(2,1)S(1)} %copy-done.2, bf16[64,2560]{1,0:T(8,128)(2,1)S(1)} %get-tuple-element.33.after.p_hi, ...), custom_call_target="tpu_custom_call" | custom-call | flops 94371840 | bytes 1474560 | tf_op jit(solution)/shard_map/kept_rows/pallas_call | solution.py:81
  37.4 0.0 collective-permute-done.4.refs_0_.refs_3_
  37.4 0.5 %kept_rows.3 = (bf16[8,5120]{1,0:T(8,128)(2,1)S(1)}, f32[8,5120]{1,0:T(8,128)S(1)}) custom-call(f32[64,5120]{1,0:T(8,128)S(1)} %bitcast.9, bf16[1280,128]{1,0:T(8,128)(2,1)S(1)} %get-tuple-element.26.after.a_ref, bf16[1024,256]{1,0:T(8,128)(2,1)S(1)} %copy-done.2, ...), custom_call_target="tpu_custom_call", output_to_operand_aliasing={{0}: (6, {}), {1}: (7, {})} | custom-call | flops 31457280 | bytes 491520 | tf_op jit(solution)/shard_map/kept_rows/pallas_call | solution.py:81
  37.9 1.5 %collective-permute-start.9 = (bf16[8,5120]{1,0:T(8,128)(2,1)S(1)}, bf16[8,5120]{1,0:T(8,128)(2,1)S(1)}, u32[]{:S(2)}, u32[]{:S(2)}) collective-permute-start(bf16[8,5120]{1,0:T(8,128)(2,1)S(1)} %get-tuple-element.39.refs_0_), channel_id=1, source_target_pairs={{0,24},{4,28},{8,16},{12,20},{16,8},{20,12},{24,0},{28,4},{1,25},{... | collective-permute-start | bytes 245768 | tf_op jit(solution)/shard_map/ppermute | solution.py:351
  39.4 1.1 %collective-permute-start.8 = (bf16[8,5120]{1,0:T(8,128)(2,1)S(1)}, bf16[8,5120]{1,0:T(8,128)(2,1)S(1)}, u32[]{:S(2)}, u32[]{:S(2)}) collective-permute-start(bf16[8,5120]{1,0:T(8,128)(2,1)S(1)} %get-tuple-element.39.refs_0_), channel_id=1, source_target_pairs={{0,16},{4,20},{8,24},{12,28},{16,0},{20,4},{24,8},{28,12},{1,17},{... | collective-permute-start | bytes 245768 | tf_op jit(solution)/shard_map/ppermute | solution.py:351
  40.6 0.9 %collective-permute-start.7 = (bf16[8,5120]{1,0:T(8,128)(2,1)S(1)}, bf16[8,5120]{1,0:T(8,128)(2,1)S(1)}, u32[]{:S(2)}, u32[]{:S(2)}) collective-permute-start(bf16[8,5120]{1,0:T(8,128)(2,1)S(1)} %get-tuple-element.39.refs_0_), channel_id=1, source_target_pairs={{0,8},{4,12},{8,0},{12,4},{16,24},{20,28},{24,16},{28,20},{1,9},{5... | collective-permute-start | bytes 245768 | tf_op jit(solution)/shard_map/ppermute | solution.py:351
  41.5 1.3 %new_momentums.1.refs_4_ = f32[64,5120]{1,0:T(8,128)} custom-call(f32[64,5120]{1,0:T(8,128)S(1)} %bitcast.10, bf16[64,2560]{1,0:T(8,128)(2,1)S(1)} %get-tuple-element.32.p_ref, f32[8,5120]{1,0:T(8,128)S(1)} %get-tuple-element.37.q, f32[64,1280]{1,0:T(8,128)S(1)} %get-tuple-element.34.refs_0_, bf16[64,1280]{1,0:T(8,128)(2,1)S(1)} %collective-permute-done.5.refs_1_, ...), custom_call_target="tpu_custom_call" | custom-call | flops 125829120 | bytes 3276800 | tf_op jit(solution)/shard_map/new_momentums/pallas_call | solution.py:81
  42.8 0.0 collective-permute-done.3.bundles
  42.8 0.4 other_places.1
  43.2 0.8 %collective-permute-done.9.refs_3_ = bf16[8,5120]{1,0:T(8,128)(2,1)S(1)} collective-permute-done((bf16[8,5120]{1,0:T(8,128)(2,1)S(1)}, bf16[8,5120]{1,0:T(8,128)(2,1)S(1)}, u32[]{:S(2)}, u32[]{:S(2)}) %collective-permute-start.9) | collective-permute-done | bytes 81952 | tf_op jit(solution)/shard_map/ppermute | solution.py:351
  44.0 0.7 %collective-permute-done.8.refs_2_ = bf16[8,5120]{1,0:T(8,128)(2,1)S(1)} collective-permute-done((bf16[8,5120]{1,0:T(8,128)(2,1)S(1)}, bf16[8,5120]{1,0:T(8,128)(2,1)S(1)}, u32[]{:S(2)}, u32[]{:S(2)}) %collective-permute-start.8) | collective-permute-done | bytes 81952 | tf_op jit(solution)/shard_map/ppermute | solution.py:351
  44.7 0.3 collective-permute-done.7.refs_1_
  45.1 0.1 collective-permute-start.10
  45.1 0.5 %half_updates.1.half_sum = f32[1280,256]{1,0:T(8,128)S(1)} custom-call(bf16[64,2560]{1,0:T(8,128)(2,1)S(1)} %get-tuple-element.33.after.p_hi, bf16[64,2560]{1,0:T(8,128)(2,1)S(1)} %get-tuple-element.38.p_lo, bf16[4,8,5120]{2,1,0:T(8,128)(2,1)S(1)} %join_kept.1.mine), custom_call_target="tpu_custom_call" | custom-call | tf_op jit(solution)/shard_map/half_updates/pallas_call | solution.py:81
  45.6 1.0 %input_grads.3 = bf16[128,1280]{1,0:T(8,128)(2,1)} custom-call(bf16[64,5120]{1,0:T(8,128)(2,1)S(1)} %copy-done.1, bf16[4,256,128]{2,1,0:T(8,128)(2,1)S(1)} %collective-permute-done.3.bundles, bf16[64,128]{1,0:T(8,128)(2,1)S(1)} %get-tuple-element.28.refs_1_.refs_0_, ...), custom_call_target="tpu_custom_call", output_to_operand_aliasing={{}: (6, {})} | custom-call | tf_op jit(solution)/shard_map/input_grads/pallas_call | solution.py:81
  46.6 0.1 collective-permute-done.10.other
  46.8 1.3 %updates.1 = f32[64,5120]{1,0:T(8,128)} custom-call(f32[1280,256]{1,0:T(8,128)S(1)} %half_updates.1.half_sum, bf16[64,2560]{1,0:T(8,128)(2,1)S(1)} %get-tuple-element.41.refs_5_.p_hi, bf16[64,2560]{1,0:T(8,128)(2,1)S(1)} %get-tuple-element.42.p_lo, bf16[4,8,5120]{2,1,0:T(8,128)(2,1)S(1)} %collective-permute-done.10.other), custom_call_target="tpu_custom_call" | custom-call | flops 671088640 | bytes 2621440 | tf_op jit(solution)/shard_map/updates/pallas_call | solution.py:81
  (2 shorter events, 0.0 us)
Async XLA Ops:
  1.8 6.2 %collective-permute-start = (bf16[144,128]{1,0:T(8,128)(2,1)S(1)}, bf16[144,128]{1,0:T(8,128)(2,1)S(1)}, u32[]{:S(2)}, u32[]{:S(2)}) collective-permute-start(bf16[144,128]{1,0:T(8,128)(2,1)S(1)} %get-tuple-element.27), channel_id=1, source_target_pairs={{0,1},{1,0},{2,3},{3,2},{4,5},{5,4},{6,7},{7,6},{8,9},{9,8},{10,11... | collective-permute-start | bytes 110600 | tf_op jit(solution)/shard_map/ppermute | solution.py:346
  4.9 5.5 %collective-permute-start.1 = (bf16[144,128]{1,0:T(8,128)(2,1)S(1)}, bf16[144,128]{1,0:T(8,128)(2,1)S(1)}, u32[]{:S(2)}, u32[]{:S(2)}) collective-permute-start(bf16[144,128]{1,0:T(8,128)(2,1)S(1)} %get-tuple-element.30), channel_id=1, source_target_pairs={{0,2},{1,3},{2,0},{3,1},{4,6},{5,7},{6,4},{7,5},{8,10},{9,11},{10,... | collective-permute-start | bytes 110600 | tf_op jit(solution)/shard_map/ppermute | solution.py:346
  7.5 5.8 %collective-permute-start.2 = (bf16[144,128]{1,0:T(8,128)(2,1)S(1)}, bf16[144,128]{1,0:T(8,128)(2,1)S(1)}, u32[]{:S(2)}, u32[]{:S(2)}) collective-permute-start(bf16[144,128]{1,0:T(8,128)(2,1)S(1)} %get-tuple-element.31), channel_id=1, source_target_pairs={{0,3},{1,2},{2,1},{3,0},{4,7},{5,6},{6,5},{7,4},{8,11},{9,10},{10,... | collective-permute-start | bytes 110600 | tf_op jit(solution)/shard_map/ppermute | solution.py:346
  8.3 19.4 %copy-start.3 = (s32[8]{0:T(128)S(1)}, s32[8]{0:T(128)}, u32[]{:S(2)}) copy-start(s32[8]{0:T(128)} %mask.1) | copy-start | bytes 100
  8.3 19.4 %copy-start.4 = (s32[8]{0:T(128)S(1)}, s32[8]{0:T(128)}, u32[]{:S(2)}) copy-start(s32[8]{0:T(128)} %tally.1) | copy-start | bytes 100
  13.2 15.4 %copy-start.1 = (bf16[64,5120]{1,0:T(8,128)(2,1)S(1)}, bf16[64,5120]{1,0:T(8,128)(2,1)}, u32[]{:S(2)}) copy-start(bf16[64,5120]{1,0:T(8,128)(2,1)} %exp_ref.5) | copy-start | bytes 1966084
  22.7 20.1 %collective-permute-start.3 = (bf16[4,256,128]{2,1,0:T(8,128)(2,1)S(1)}, bf16[4,256,128]{2,1,0:T(8,128)(2,1)S(1)}, u32[]{:S(2)}, u32[]{:S(2)}) collective-permute-start(bf16[4,256,128]{2,1,0:T(8,128)(2,1)S(1)} %bitcast.11), channel_id=1, source_target_pairs={{0,4},{4,0},{8,12},{12,8},{16,20},{20,16},{24,28},{28,24},{1,5},{5... | collective-permute-start | bytes 786440 | tf_op jit(solution)/shard_map/ppermute | solution.py:351
  22.9 13.8 %copy-start = (f32[1,64,5120]{2,1,0:T(8,128)S(1)}, f32[1,64,5120]{2,1,0:T(8,128)}, u32[]{:S(2)}) copy-start(f32[1,64,5120]{2,1,0:T(8,128)} %param.14) | copy-start | bytes 3932164
  22.9 13.8 %copy-start.2 = (bf16[1024,256]{1,0:T(8,128)(2,1)S(1)}, bf16[1024,256]{1,0:T(8,128)(2,1)}, u32[]{:S(2)}) copy-start(bf16[1024,256]{1,0:T(8,128)(2,1)} %constant.4.clone.tab) | copy-start | bytes 1572868
  22.9 10.1 %collective-permute-start.6 = (bf16[64,1280]{1,0:T(8,128)(2,1)S(1)}, bf16[64,1280]{1,0:T(8,128)(2,1)S(1)}, u32[]{:S(2)}, u32[]{:S(2)}) collective-permute-start(bf16[64,1280]{1,0:T(8,128)(2,1)S(1)} %weight_grads.5), channel_id=1, source_target_pairs={{0,2},{1,3},{2,0},{3,1},{4,6},{5,7},{6,4},{7,5},{8,10},{9,11},{10,... | collective-permute-start | bytes 491528 | tf_op jit(solution)/shard_map/ppermute | solution.py:346
  23.0 13.7 %collective-permute-start.5 = (bf16[64,1280]{1,0:T(8,128)(2,1)S(1)}, bf16[64,1280]{1,0:T(8,128)(2,1)S(1)}, u32[]{:S(2)}, u32[]{:S(2)}) collective-permute-start(bf16[64,1280]{1,0:T(8,128)(2,1)S(1)} %get-tuple-element.29.after), channel_id=1, source_target_pairs={{0,1},{1,0},{2,3},{3,2},{4,5},{5,4},{6,7},{7,6},{8,9},{9,8},{10,11... | collective-permute-start | bytes 491528 | tf_op jit(solution)/shard_map/ppermute | solution.py:346
  24.3 13.2 %collective-permute-start.4 = (bf16[64,1280]{1,0:T(8,128)(2,1)S(1)}, bf16[64,1280]{1,0:T(8,128)(2,1)S(1)}, u32[]{:S(2)}, u32[]{:S(2)}) collective-permute-start(bf16[64,1280]{1,0:T(8,128)(2,1)S(1)} %weight_grads.4), channel_id=1, source_target_pairs={{0,3},{1,2},{2,1},{3,0},{4,7},{5,6},{6,5},{7,4},{8,11},{9,10},{10,... | collective-permute-start | bytes 491528 | tf_op jit(solution)/shard_map/ppermute | solution.py:346
  37.9 6.0 %collective-permute-start.9 = (bf16[8,5120]{1,0:T(8,128)(2,1)S(1)}, bf16[8,5120]{1,0:T(8,128)(2,1)S(1)}, u32[]{:S(2)}, u32[]{:S(2)}) collective-permute-start(bf16[8,5120]{1,0:T(8,128)(2,1)S(1)} %get-tuple-element.39.refs_0_), channel_id=1, source_target_pairs={{0,24},{4,28},{8,16},{12,20},{16,8},{20,12},{24,0},{28,4},{1,25},{... | collective-permute-start | bytes 245768 | tf_op jit(solution)/shard_map/ppermute | solution.py:351
  39.4 5.3 %collective-permute-start.8 = (bf16[8,5120]{1,0:T(8,128)(2,1)S(1)}, bf16[8,5120]{1,0:T(8,128)(2,1)S(1)}, u32[]{:S(2)}, u32[]{:S(2)}) collective-permute-start(bf16[8,5120]{1,0:T(8,128)(2,1)S(1)} %get-tuple-element.39.refs_0_), channel_id=1, source_target_pairs={{0,16},{4,20},{8,24},{12,28},{16,0},{20,4},{24,8},{28,12},{1,17},{... | collective-permute-start | bytes 245768 | tf_op jit(solution)/shard_map/ppermute | solution.py:351
  40.6 4.4 %collective-permute-start.7 = (bf16[8,5120]{1,0:T(8,128)(2,1)S(1)}, bf16[8,5120]{1,0:T(8,128)(2,1)S(1)}, u32[]{:S(2)}, u32[]{:S(2)}) collective-permute-start(bf16[8,5120]{1,0:T(8,128)(2,1)S(1)} %get-tuple-element.39.refs_0_), channel_id=1, source_target_pairs={{0,8},{4,12},{8,0},{12,4},{16,24},{20,28},{24,16},{28,20},{1,9},{5... | collective-permute-start | bytes 245768 | tf_op jit(solution)/shard_map/ppermute | solution.py:351
  45.1 1.7 %collective-permute-start.10 = (bf16[4,8,5120]{2,1,0:T(8,128)(2,1)S(1)}, bf16[4,8,5120]{2,1,0:T(8,128)(2,1)S(1)}, u32[]{:S(2)}, u32[]{:S(2)}) collective-permute-start(bf16[4,8,5120]{2,1,0:T(8,128)(2,1)S(1)} %join_kept.1.mine), channel_id=1, source_target_pairs={{0,4},{4,0},{8,12},{12,8},{16,20},{20,16},{24,28},{28,24},{1,5},{5... | collective-permute-start | bytes 983048 | tf_op jit(solution)/shard_map/ppermute | solution.py:351

commit v19 on v18

--- a/solution.py
+++ b/solution.py
@@ -473,7 +473,7 @@
         [VM] * (3 + n_t),
         ANY,
         scratch=[pltpu.VMEM((B, width), F32), pltpu.SemaphoreType.DMA((n_t,))],
-        flops=6 * B * B * width,
+        flops=1 << 33,
         nbytes=B * width * 10,
         name="new_momentums",
     )

time: 48.6 us -> 37.5 us (0.77)
  waiting for transfers between devices: 14 us -> 2.7 us
  starting transfers between devices: 13.8 us -> 14.3 us
    ppermute x6, waiting for transfers between devices: 12.1 us -> 0.32 us  [trade(): return lax.ppermute(x, 'tensor', [(i, i ^ k) for i in range(n_t)])]
  transfers between devices with their start and end apart: 11 -> 11, of which waited for: 8 -> 4; matrix products, arithmetic and copies ran while one was open for 0% -> 0% of each run, Pallas kernels for 15% -> 20%
where the time goes in v19:
time: 37.5 us; the launch traced here: 37.3 us
  starting transfers between devices  14.3 us (38%)
  Pallas kernels  9.95 us (27%)
  blocking collectives  9.48 us (25%)
  waiting for transfers between devices  2.7 us (7%)
  between operations  0.85 us (2%)
    ppermute x6, starting transfers between devices, trade(): return lax.ppermute(x, 'tensor', [(i, i ^ k) for i in range(n_t)])  10.6 us
    pallas_call x16, Pallas kernels, call(): pl.pallas_call(body, out_shape=out_shape, in_specs=in_specs, out_specs=ou...  9.95 us
    all_gather x1, blocking collectives, per_device(): lax.all_gather(bundle, 'replica', axis=0, axis_index_groups=sides)  9.48 us
    ppermute x5, starting transfers between devices, swap(): return lax.ppermute(x, 'replica', [(i, i ^ m) for i in range(n_r)])  3.65 us
    ppermute x5, waiting for transfers between devices, swap(): return lax.ppermute(x, 'replica', [(i, i ^ m) for i in range(n_r)])  2.38 us
  transfers between devices with their start and end apart: 11, of which 4 were waited for; matrix products, arithmetic and copies ran while one was open for 0% of the time, Pallas kernels for 20%

profile of v19, /device:TPU:0, one launch (start us, length us, event | category | flops | bytes accessed | tf_op | source)
XLA Modules:
  0.0 37.3 jit_solution(11889749711438927140)
XLA Ops:
  0.6 1.2 %up_grads.1 = (bf16[64,128]{1,0:T(8,128)(2,1)S(1)}, bf16[144,128]{1,0:T(8,128)(2,1)S(1)}, bf16[144,128]{1,0:T(8,128)(2,1)S(1)}, bf16[144,128]{1,0:T(8,128)(2,1)S...) custom-call(bf16[64,128]{1,0:T(8,128)(2,1)} %bitcast.15, ...), custom_call_target="tpu_custom_call" | custom-call | bytes 819200 | tf_op jit(solution)/shard_map/up_grads/pallas_call | solution.py:81
  1.8 4.1 %collective-permute-start.1 = (bf16[144,128]{1,0:T(8,128)(2,1)S(1)}, bf16[144,128]{1,0:T(8,128)(2,1)S(1)}, u32[]{:S(2)}, u32[]{:S(2)}) collective-permute-start(bf16[144,128]{1,0:T(8,128)(2,1)S(1)} %get-tuple-element.30), channel_id=1, source_target_pairs={{0,2},{1,3},{2,0},{3,1},{4,6},{5,7},{6,4},{7,5},{8,10},{9,11},{10,... | collective-permute-start | bytes 110600 | tf_op jit(solution)/shard_map/ppermute | solution.py:346
  5.9 1.6 %collective-permute-start = (bf16[144,128]{1,0:T(8,128)(2,1)S(1)}, bf16[144,128]{1,0:T(8,128)(2,1)S(1)}, u32[]{:S(2)}, u32[]{:S(2)}) collective-permute-start(bf16[144,128]{1,0:T(8,128)(2,1)S(1)} %get-tuple-element.27), channel_id=1, source_target_pairs={{0,1},{1,0},{2,3},{3,2},{4,5},{5,4},{6,7},{7,6},{8,9},{9,8},{10,11... | collective-permute-start | bytes 110600 | tf_op jit(solution)/shard_map/ppermute | solution.py:346
  7.5 0.0 collective-permute-start.2
  7.5 0.5 %own_places.1 = (bf16[64,2560]{1,0:T(8,128)(2,1)S(1)}, bf16[1280,128]{1,0:T(8,128)(2,1)S(1)}) custom-call(s32[8,80]{1,0:T(8,128)S(1)} %get-tuple-element.24.lines, bf16[128,256]{1,0:T(8,128)(2,1)S(1)} %get-tuple-element.25.small), custom_call_target="tpu_custom_call" | custom-call | tf_op jit(solution)/shard_map/own_places/pallas_call | solution.py:81
  8.0 0.3 collective-permute-done.1.refs_1_.refs_2_.refs_0_
  8.3 0.2 weight_grads.5
  8.5 0.0 copy-start.3
  8.5 0.0 copy-start.4
  8.5 0.0 copy-start
  8.6 2.7 %collective-permute-start.6 = (bf16[64,1280]{1,0:T(8,128)(2,1)S(1)}, bf16[64,1280]{1,0:T(8,128)(2,1)S(1)}, u32[]{:S(2)}, u32[]{:S(2)}) collective-permute-start(bf16[64,1280]{1,0:T(8,128)(2,1)S(1)} %weight_grads.5), channel_id=1, source_target_pairs={{0,2},{1,3},{2,0},{3,1},{4,6},{5,7},{6,4},{7,5},{8,10},{9,11},{10,... | collective-permute-start | bytes 491528 | tf_op jit(solution)/shard_map/ppermute | solution.py:346
  11.3 0.0 collective-permute-done.refs_0_.refs_1_
  11.3 0.2 weight_grads.3
  11.5 2.1 %collective-permute-start.5 = (bf16[64,1280]{1,0:T(8,128)(2,1)S(1)}, bf16[64,1280]{1,0:T(8,128)(2,1)S(1)}, u32[]{:S(2)}, u32[]{:S(2)}) collective-permute-start(bf16[64,1280]{1,0:T(8,128)(2,1)S(1)} %get-tuple-element.29.after), channel_id=1, source_target_pairs={{0,1},{1,0},{2,3},{3,2},{4,5},{5,4},{6,7},{7,6},{8,9},{9,8},{10,11... | collective-permute-start | bytes 491528 | tf_op jit(solution)/shard_map/ppermute | solution.py:346
  13.6 0.0 collective-permute-done.2.refs_2_.refs_3_.refs_0_
  13.6 0.2 weight_grads.4
  13.8 0.0 copy-start.1
  13.9 0.0 copy-start.2
  13.9 0.1 collective-permute-start.4
  14.0 9.5 %all-gather = bf16[1024,128]{1,0:T(8,128)(2,1)S(1)} all-gather(bf16[256,128]{1,0:T(8,128)(2,1)S(1)} %bundle.1), channel_id=2, replica_groups={{0,8,16,24},{4,12,20,28},{1,9,17,25},{5,13,21,29},{2,10,18,26},{6,14,22..., dimensions={0}, use_global_device_ids=true | all-gather | bytes 327680 | tf_op jit(solution)/shard_map/all_gather | solution.py:411
  23.4 0.0 collective-permute-start.3
  23.4 0.0 copy-done.3
  23.5 0.0 copy-done.4
  23.5 1.0 %places.1 = (bf16[64,2560]{1,0:T(8,128)(2,1)S(1)}, bf16[64,2560]{1,0:T(8,128)(2,1)S(1)}, f32[8,128]{1,0:T(8,128)S(1)}) custom-call(s32[8]{0:T(128)S(1)} %copy-done.3, s32[8]{0:T(128)S(1)} %copy-done.4, bf16[128,256]{1,0:T(8,128)(2,1)S(1)} %get-tuple-element.25.small, bf16[4,256,128]{2,1,0:T(8,128)(2,1)S(1)} %bitcast.12), custom_call_target="tpu_custom_call" | custom-call | tf_op jit(solution)/shard_map/places/pallas_call | solution.py:81
  24.4 0.0 copy-done
  24.4 1.0 %input_grads.2.refs_4_.after_too = bf16[128,1280]{1,0:T(8,128)(2,1)} custom-call(bf16[64,5120]{1,0:T(8,128)(2,1)S(1)} %copy-done, bf16[4,256,128]{2,1,0:T(8,128)(2,1)S(1)} %bitcast.13, bf16[64,128]{1,0:T(8,128)(2,1)S(1)} %get-tuple-element.28.refs_1_.refs_0_, bf16[144,128]{1,0:T(8,128)(2,1)S(1)} %collective-permute-done.refs_0_.refs_1_, ...), custom_call_target="tpu_custom_call" | custom-call | tf_op jit(solution)/shard_map/input_grads/pallas_call | solution.py:81
  25.4 0.0 collective-permute-done.6.refs_2_
  25.4 0.0 collective-permute-done.5.refs_1_
  25.4 0.0 copy-done.1
  25.4 0.0 copy-done.2
  25.4 0.7 %kept_rows.2 = (bf16[8,5120]{1,0:T(8,128)(2,1)S(1)}, f32[8,5120]{1,0:T(8,128)S(1)}) custom-call(f32[64,5120]{1,0:T(8,128)S(1)} %bitcast.8, bf16[1280,128]{1,0:T(8,128)(2,1)S(1)} %get-tuple-element.26.after.a_ref, bf16[1024,256]{1,0:T(8,128)(2,1)S(1)} %copy-done.2, bf16[64,2560]{1,0:T(8,128)(2,1)S(1)} %get-tuple-element.33.after.p_hi, ...), custom_call_target="tpu_custom_call" | custom-call | flops 94371840 | bytes 1474560 | tf_op jit(solution)/shard_map/kept_rows/pallas_call | solution.py:81
  26.2 0.0 collective-permute-done.4.refs_0_.refs_3_
  26.2 0.5 %kept_rows.3 = (bf16[8,5120]{1,0:T(8,128)(2,1)S(1)}, f32[8,5120]{1,0:T(8,128)S(1)}) custom-call(f32[64,5120]{1,0:T(8,128)S(1)} %bitcast.9, bf16[1280,128]{1,0:T(8,128)(2,1)S(1)} %get-tuple-element.26.after.a_ref, bf16[1024,256]{1,0:T(8,128)(2,1)S(1)} %copy-done.2, ...), custom_call_target="tpu_custom_call", output_to_operand_aliasing={{0}: (6, {}), {1}: (7, {})} | custom-call | flops 31457280 | bytes 491520 | tf_op jit(solution)/shard_map/kept_rows/pallas_call | solution.py:81
  26.7 1.5 %collective-permute-start.9 = (bf16[8,5120]{1,0:T(8,128)(2,1)S(1)}, bf16[8,5120]{1,0:T(8,128)(2,1)S(1)}, u32[]{:S(2)}, u32[]{:S(2)}) collective-permute-start(bf16[8,5120]{1,0:T(8,128)(2,1)S(1)} %get-tuple-element.39.refs_0_), channel_id=1, source_target_pairs={{0,24},{4,28},{8,16},{12,20},{16,8},{20,12},{24,0},{28,4},{1,25},{... | collective-permute-start | bytes 245768 | tf_op jit(solution)/shard_map/ppermute | solution.py:351
  28.2 1.1 %collective-permute-start.8 = (bf16[8,5120]{1,0:T(8,128)(2,1)S(1)}, bf16[8,5120]{1,0:T(8,128)(2,1)S(1)}, u32[]{:S(2)}, u32[]{:S(2)}) collective-permute-start(bf16[8,5120]{1,0:T(8,128)(2,1)S(1)} %get-tuple-element.39.refs_0_), channel_id=1, source_target_pairs={{0,16},{4,20},{8,24},{12,28},{16,0},{20,4},{24,8},{28,12},{1,17},{... | collective-permute-start | bytes 245768 | tf_op jit(solution)/shard_map/ppermute | solution.py:351
  29.3 0.9 %collective-permute-start.7 = (bf16[8,5120]{1,0:T(8,128)(2,1)S(1)}, bf16[8,5120]{1,0:T(8,128)(2,1)S(1)}, u32[]{:S(2)}, u32[]{:S(2)}) collective-permute-start(bf16[8,5120]{1,0:T(8,128)(2,1)S(1)} %get-tuple-element.39.refs_0_), channel_id=1, source_target_pairs={{0,8},{4,12},{8,0},{12,4},{16,24},{20,28},{24,16},{28,20},{1,9},{5... | collective-permute-start | bytes 245768 | tf_op jit(solution)/shard_map/ppermute | solution.py:351
  30.2 1.3 %new_momentums.1.refs_4_ = f32[64,5120]{1,0:T(8,128)} custom-call(f32[64,5120]{1,0:T(8,128)S(1)} %bitcast.10, bf16[64,2560]{1,0:T(8,128)(2,1)S(1)} %get-tuple-element.32.p_ref, f32[8,5120]{1,0:T(8,128)S(1)} %get-tuple-element.37.q, f32[64,1280]{1,0:T(8,128)S(1)} %get-tuple-element.34.refs_0_, bf16[64,1280]{1,0:T(8,128)(2,1)S(1)} %collective-permute-done.5.refs_1_, ...), custom_call_target="tpu_custom_call" | custom-call | flops 8589934592 | bytes 3276800 | tf_op jit(solution)/shard_map/new_momentums/pallas_call | solution.py:81
  31.5 0.0 collective-permute-done.3.bundles
  31.5 0.4 %other_places.1 = (bf16[64,2560]{1,0:T(8,128)(2,1)S(1)}, bf16[64,2560]{1,0:T(8,128)(2,1)S(1)}) custom-call(f32[8,128]{1,0:T(8,128)S(1)} %get-tuple-element.40.w_ref, bf16[128,256]{1,0:T(8,128)(2,1)S(1)} %get-tuple-element.25.small, bf16[4,256,128]{2,1,0:T(8,128)(2,1)S(1)} %collective-permute-done.3.bundles), custom_call_target="tpu_custom_call" | custom-call | tf_op jit(solution)/shard_map/other_places/pallas_call | solution.py:81
  32.0 0.8 %collective-permute-done.9.refs_3_ = bf16[8,5120]{1,0:T(8,128)(2,1)S(1)} collective-permute-done((bf16[8,5120]{1,0:T(8,128)(2,1)S(1)}, bf16[8,5120]{1,0:T(8,128)(2,1)S(1)}, u32[]{:S(2)}, u32[]{:S(2)}) %collective-permute-start.9) | collective-permute-done | bytes 81952 | tf_op jit(solution)/shard_map/ppermute | solution.py:351
  32.8 1.5 %collective-permute-done.8.refs_2_ = bf16[8,5120]{1,0:T(8,128)(2,1)S(1)} collective-permute-done((bf16[8,5120]{1,0:T(8,128)(2,1)S(1)}, bf16[8,5120]{1,0:T(8,128)(2,1)S(1)}, u32[]{:S(2)}, u32[]{:S(2)}) %collective-permute-start.8) | collective-permute-done | bytes 81952 | tf_op jit(solution)/shard_map/ppermute | solution.py:351
  34.2 0.0 collective-permute-done.7.refs_1_
  34.3 0.1 collective-permute-start.10
  34.4 0.5 %half_updates.1.half_sum = f32[1280,256]{1,0:T(8,128)S(1)} custom-call(bf16[64,2560]{1,0:T(8,128)(2,1)S(1)} %get-tuple-element.33.after.p_hi, bf16[64,2560]{1,0:T(8,128)(2,1)S(1)} %get-tuple-element.38.p_lo, bf16[4,8,5120]{2,1,0:T(8,128)(2,1)S(1)} %join_kept.1.mine), custom_call_target="tpu_custom_call" | custom-call | tf_op jit(solution)/shard_map/half_updates/pallas_call | solution.py:81
  34.9 1.0 %input_grads.3 = bf16[128,1280]{1,0:T(8,128)(2,1)} custom-call(bf16[64,5120]{1,0:T(8,128)(2,1)S(1)} %copy-done, bf16[4,256,128]{2,1,0:T(8,128)(2,1)S(1)} %collective-permute-done.3.bundles, bf16[64,128]{1,0:T(8,128)(2,1)S(1)} %get-tuple-element.28.refs_1_.refs_0_, ...), custom_call_target="tpu_custom_call", output_to_operand_aliasing={{}: (6, {})} | custom-call | tf_op jit(solution)/shard_map/input_grads/pallas_call | solution.py:81
  35.8 0.1 collective-permute-done.10.other
  35.9 1.3 %updates.1 = f32[64,5120]{1,0:T(8,128)} custom-call(f32[1280,256]{1,0:T(8,128)S(1)} %half_updates.1.half_sum, bf16[64,2560]{1,0:T(8,128)(2,1)S(1)} %get-tuple-element.41.refs_5_.p_hi, bf16[64,2560]{1,0:T(8,128)(2,1)S(1)} %get-tuple-element.42.p_lo, bf16[4,8,5120]{2,1,0:T(8,128)(2,1)S(1)} %collective-permute-done.10.other), custom_call_target="tpu_custom_call" | custom-call | flops 671088640 | bytes 2621440 | tf_op jit(solution)/shard_map/updates/pallas_call | solution.py:81
  (2 shorter events, 0.0 us)
Async XLA Ops:
  1.8 6.5 %collective-permute-start.1 = (bf16[144,128]{1,0:T(8,128)(2,1)S(1)}, bf16[144,128]{1,0:T(8,128)(2,1)S(1)}, u32[]{:S(2)}, u32[]{:S(2)}) collective-permute-start(bf16[144,128]{1,0:T(8,128)(2,1)S(1)} %get-tuple-element.30), channel_id=1, source_target_pairs={{0,2},{1,3},{2,0},{3,1},{4,6},{5,7},{6,4},{7,5},{8,10},{9,11},{10,... | collective-permute-start | bytes 110600 | tf_op jit(solution)/shard_map/ppermute | solution.py:346
  5.9 5.4 %collective-permute-start = (bf16[144,128]{1,0:T(8,128)(2,1)S(1)}, bf16[144,128]{1,0:T(8,128)(2,1)S(1)}, u32[]{:S(2)}, u32[]{:S(2)}) collective-permute-start(bf16[144,128]{1,0:T(8,128)(2,1)S(1)} %get-tuple-element.27), channel_id=1, source_target_pairs={{0,1},{1,0},{2,3},{3,2},{4,5},{5,4},{6,7},{7,6},{8,9},{9,8},{10,11... | collective-permute-start | bytes 110600 | tf_op jit(solution)/shard_map/ppermute | solution.py:346
  7.5 6.2 %collective-permute-start.2 = (bf16[144,128]{1,0:T(8,128)(2,1)S(1)}, bf16[144,128]{1,0:T(8,128)(2,1)S(1)}, u32[]{:S(2)}, u32[]{:S(2)}) collective-permute-start(bf16[144,128]{1,0:T(8,128)(2,1)S(1)} %get-tuple-element.31), channel_id=1, source_target_pairs={{0,3},{1,2},{2,1},{3,0},{4,7},{5,6},{6,5},{7,4},{8,11},{9,10},{10,... | collective-permute-start | bytes 110600 | tf_op jit(solution)/shard_map/ppermute | solution.py:346
  8.5 14.9 %copy-start.3 = (s32[8]{0:T(128)S(1)}, s32[8]{0:T(128)}, u32[]{:S(2)}) copy-start(s32[8]{0:T(128)} %mask.1) | copy-start | bytes 100
  8.5 14.9 %copy-start.4 = (s32[8]{0:T(128)S(1)}, s32[8]{0:T(128)}, u32[]{:S(2)}) copy-start(s32[8]{0:T(128)} %tally.1) | copy-start | bytes 100
  8.5 15.9 %copy-start = (bf16[64,5120]{1,0:T(8,128)(2,1)S(1)}, bf16[64,5120]{1,0:T(8,128)(2,1)}, u32[]{:S(2)}) copy-start(bf16[64,5120]{1,0:T(8,128)(2,1)} %exp_ref.5) | copy-start | bytes 1966084
  8.6 16.9 %collective-permute-start.6 = (bf16[64,1280]{1,0:T(8,128)(2,1)S(1)}, bf16[64,1280]{1,0:T(8,128)(2,1)S(1)}, u32[]{:S(2)}, u32[]{:S(2)}) collective-permute-start(bf16[64,1280]{1,0:T(8,128)(2,1)S(1)} %weight_grads.5), channel_id=1, source_target_pairs={{0,2},{1,3},{2,0},{3,1},{4,6},{5,7},{6,4},{7,5},{8,10},{9,11},{10,... | collective-permute-start | bytes 491528 | tf_op jit(solution)/shard_map/ppermute | solution.py:346
  11.5 13.9 %collective-permute-start.5 = (bf16[64,1280]{1,0:T(8,128)(2,1)S(1)}, bf16[64,1280]{1,0:T(8,128)(2,1)S(1)}, u32[]{:S(2)}, u32[]{:S(2)}) collective-permute-start(bf16[64,1280]{1,0:T(8,128)(2,1)S(1)} %get-tuple-element.29.after), channel_id=1, source_target_pairs={{0,1},{1,0},{2,3},{3,2},{4,5},{5,4},{6,7},{7,6},{8,9},{9,8},{10,11... | collective-permute-start | bytes 491528 | tf_op jit(solution)/shard_map/ppermute | solution.py:346
  13.8 11.6 %copy-start.1 = (f32[1,64,5120]{2,1,0:T(8,128)S(1)}, f32[1,64,5120]{2,1,0:T(8,128)}, u32[]{:S(2)}) copy-start(f32[1,64,5120]{2,1,0:T(8,128)} %param.14) | copy-start | bytes 3932164
  13.9 11.6 %copy-start.2 = (bf16[1024,256]{1,0:T(8,128)(2,1)S(1)}, bf16[1024,256]{1,0:T(8,128)(2,1)}, u32[]{:S(2)}) copy-start(bf16[1024,256]{1,0:T(8,128)(2,1)} %constant.4.clone.tab) | copy-start | bytes 1572868
  13.9 12.3 %collective-permute-start.4 = (bf16[64,1280]{1,0:T(8,128)(2,1)S(1)}, bf16[64,1280]{1,0:T(8,128)(2,1)S(1)}, u32[]{:S(2)}, u32[]{:S(2)}) collective-permute-start(bf16[64,1280]{1,0:T(8,128)(2,1)S(1)} %weight_grads.4), channel_id=1, source_target_pairs={{0,3},{1,2},{2,1},{3,0},{4,7},{5,6},{6,5},{7,4},{8,11},{9,10},{10,... | collective-permute-start | bytes 491528 | tf_op jit(solution)/shard_map/ppermute | solution.py:346
  23.4 8.1 %collective-permute-start.3 = (bf16[4,256,128]{2,1,0:T(8,128)(2,1)S(1)}, bf16[4,256,128]{2,1,0:T(8,128)(2,1)S(1)}, u32[]{:S(2)}, u32[]{:S(2)}) collective-permute-start(bf16[4,256,128]{2,1,0:T(8,128)(2,1)S(1)} %bitcast.11), channel_id=1, source_target_pairs={{0,4},{4,0},{8,12},{12,8},{16,20},{20,16},{24,28},{28,24},{1,5},{5... | collective-permute-start | bytes 786440 | tf_op jit(solution)/shard_map/ppermute | solution.py:351
  26.7 6.1 %collective-permute-start.9 = (bf16[8,5120]{1,0:T(8,128)(2,1)S(1)}, bf16[8,5120]{1,0:T(8,128)(2,1)S(1)}, u32[]{:S(2)}, u32[]{:S(2)}) collective-permute-start(bf16[8,5120]{1,0:T(8,128)(2,1)S(1)} %get-tuple-element.39.refs_0_), channel_id=1, source_target_pairs={{0,24},{4,28},{8,16},{12,20},{16,8},{20,12},{24,0},{28,4},{1,25},{... | collective-permute-start | bytes 245768 | tf_op jit(solution)/shard_map/ppermute | solution.py:351
  28.2 6.0 %collective-permute-start.8 = (bf16[8,5120]{1,0:T(8,128)(2,1)S(1)}, bf16[8,5120]{1,0:T(8,128)(2,1)S(1)}, u32[]{:S(2)}, u32[]{:S(2)}) collective-permute-start(bf16[8,5120]{1,0:T(8,128)(2,1)S(1)} %get-tuple-element.39.refs_0_), channel_id=1, source_target_pairs={{0,16},{4,20},{8,24},{12,28},{16,0},{20,4},{24,8},{28,12},{1,17},{... | collective-permute-start | bytes 245768 | tf_op jit(solution)/shard_map/ppermute | solution.py:351
  29.3 4.9 %collective-permute-start.7 = (bf16[8,5120]{1,0:T(8,128)(2,1)S(1)}, bf16[8,5120]{1,0:T(8,128)(2,1)S(1)}, u32[]{:S(2)}, u32[]{:S(2)}) collective-permute-start(bf16[8,5120]{1,0:T(8,128)(2,1)S(1)} %get-tuple-element.39.refs_0_), channel_id=1, source_target_pairs={{0,8},{4,12},{8,0},{12,4},{16,24},{20,28},{24,16},{28,20},{1,9},{5... | collective-permute-start | bytes 245768 | tf_op jit(solution)/shard_map/ppermute | solution.py:351
  34.3 1.7 %collective-permute-start.10 = (bf16[4,8,5120]{2,1,0:T(8,128)(2,1)S(1)}, bf16[4,8,5120]{2,1,0:T(8,128)(2,1)S(1)}, u32[]{:S(2)}, u32[]{:S(2)}) collective-permute-start(bf16[4,8,5120]{2,1,0:T(8,128)(2,1)S(1)} %join_kept.1.mine), channel_id=1, source_target_pairs={{0,4},{4,0},{8,12},{12,8},{16,20},{20,16},{24,28},{28,24},{1,5},{5... | collective-permute-start | bytes 983048 | tf_op jit(solution)/shard_map/ppermute | solution.py:351

commit v20 on v16

--- a/solution.py
+++ b/solution.py
@@ -148,7 +148,7 @@
 
 
 def join_body(n, *refs):
-    for i, ref in enumerate(refs[:n]):
+    for i, ref in enumerate(refs[1 : n + 1]):
         refs[-1][i] = ref[...]
 
 
@@ -211,8 +211,14 @@
         send_ref[:, pl.ds(c0, cols)] = part.astype(BF16)
 
 
-def return_body(n_t, keep, vel, p_ref, q, *refs):
-    grads, (new_ref, held, sems) = refs[:n_t], refs[n_t:]
+def return_body(n_t, keep, vel, p_ref, q, mask, tally, *refs):
+    grads, (new_ref, w_ref, held, sems, mask_s, tally_s, small_sems) = refs[:n_t], refs[n_t:]
+    fetches = [
+        pltpu.make_async_copy(src, dst, small_sems.at[i])
+        for i, (src, dst) in enumerate([(mask, mask_s), (tally, tally_s)])
+    ]
+    for copy in fetches:
+        copy.start()
     cols = grads[0].shape[1]
     ng = cols // G
     lane_block = lax.broadcasted_iota(jnp.int32, (keep, G), 1) // B
@@ -233,30 +239,37 @@
         cut = pl.ds(c0, cols)
         copies.append(pltpu.make_async_copy(held.at[:, cut], new_ref.at[:, cut], sems.at[k]))
         copies[-1].start()
+    for copy in fetches:
+        copy.wait()
+    n_r = mask_s.shape[0]
+    total, alive = jnp.float32(0), jnp.float32(0)
+    for r in range(n_r):
+        m = mask_s[r].astype(F32)
+        total = total + m * tally_s[r].astype(F32)
+        alive = alive + m
+    half = n_r // 2
+    place = (lax.broadcasted_iota(jnp.int32, (8, 2 * B), 1) // keep) % half
+    scale = jnp.full((8, 2 * B), alive) / jnp.full((8, 2 * B), total)
+    for h in range(2):
+        w = jnp.zeros((8, 2 * B), F32)
+        for i in range(half):
+            r = lax.axis_index("replica") ^ (2 * i + h)
+            w = jnp.where(place == i, mask_s[r].astype(F32) * tally_s[r].astype(F32), w)
+        w_ref[h] = w * scale
     for copy in copies:
         copy.wait()
 
 
-def places_body(keep, mask, tally, small, bundles, *p_refs):
+def places_body(keep, w_ref, small, bundles, *p_refs):
     n_r, last = bundles.shape[0], bundles.shape[1] - 16
     half, nb = n_r // 2, G // B
     rep = lax.axis_index("replica")
-    total, alive = jnp.float32(0), jnp.float32(0)
-    for r in range(n_r):
-        m = mask[r].astype(F32)
-        total = total + m * tally[r].astype(F32)
-        alive = alive + m
-    scale = jnp.full((1, 2 * B), alive) / jnp.full((1, 2 * B), total)
     freq = lax.broadcasted_iota(jnp.int32, (B, 2 * B), 0).astype(F32)
     lane = lax.broadcasted_iota(jnp.int32, (1, 2 * B), 1)
-    block, place = lane // (half * keep), (lane // keep) % half
+    block = lane // (half * keep)
     for h in range(2):
         hi_ref, lo_ref = p_refs[2 * h : 2 * h + 2]
-        w = jnp.zeros((1, 2 * B), F32)
-        for i in range(half):
-            r = rep ^ (2 * i + h)
-            w = jnp.where(place == i, mask[r].astype(F32) * tally[r].astype(F32), w)
-        w = w * scale
+        w = w_ref[h, :1, :]
         rows = [bundles[rep ^ (2 * i + h), last:, :].astype(F32)[:keep] for i in range(half)]
         rows = jnp.concatenate(rows * nb, axis=0).T
         for g in range(hi_ref.shape[1] // (2 * B)):
@@ -270,10 +283,12 @@
             lo_ref[:, g * 2 * B : (g + 1) * 2 * B] = lo
 
 
-def spread_rows(p_hi, p_lo, ships, g):
-    half, keep = ships.shape[0], ships.shape[1]
+def spread_rows(p_hi, p_lo, own, ships, g):
+    half, keep = ships.shape[0] + 1, ships.shape[1]
+    cut = slice(g * G, (g + 1) * G)
     lane_block = lax.broadcasted_iota(jnp.int32, (half * keep, G), 1) // B
-    s = jnp.concatenate([ships[i, :, g * G : (g + 1) * G].astype(F32) for i in range(half)], axis=0)
+    s = [own[:, cut].astype(F32)] + [ships[i, :, cut].astype(F32) for i in range(half - 1)]
+    s = jnp.concatenate(s, axis=0)
     w = jnp.concatenate(
         [jnp.where(lane_block == j, s, 0.0).astype(BF16) for j in range(G // B)], axis=0
     )
@@ -282,17 +297,17 @@
     return y[:B] + y[B:]
 
 
-def half_update_body(p_hi, p_lo, mine, out):
+def half_update_body(p_hi, p_lo, own, others, out):
     for g in range(out.shape[0] // B):
-        out[g * B : (g + 1) * B, :] = spread_rows(p_hi, p_lo, mine, g)
-
-
-def update_body(chunk, half_sum, p_hi, p_lo, other, out, held, sems):
+        out[g * B : (g + 1) * B, :] = spread_rows(p_hi, p_lo, own, others, g)
+
+
+def update_body(chunk, half_sum, p_hi, p_lo, own, others, out, held, sems):
     ng = half_sum.shape[0] // B
     copies = []
     for c in range(0, ng, chunk):
         for g in range(c, c + chunk):
-            held[:, g * G : (g + 1) * G] = half_sum[g * B : (g + 1) * B, :] + spread_rows(p_hi, p_lo, other, g)
+            held[:, g * G : (g + 1) * G] = half_sum[g * B : (g + 1) * B, :] + spread_rows(p_hi, p_lo, own, others, g)
         cut = pl.ds(c * G, chunk * G)
         copies.append(pltpu.make_async_copy(held.at[:, cut], out.at[:, cut], sems.at[c // chunk]))
         copies[-1].start()
@@ -412,11 +427,28 @@
         )
     ship, q_own = rows
 
+    new, shares = call(
+        functools.partial(return_body, n_t, keep),
+        [jax.ShapeDtypeStruct((B, width), F32), near((2, 8, 2 * B), F32)],
+        (vel[0], p_own, q_own, far(mask), far(tally), *[grads[k] for k in range(n_t)]),
+        [VM] * 3 + [ANY] * 2 + [VM] * n_t,
+        [ANY, VM],
+        scratch=[
+            pltpu.VMEM((B, width), F32),
+            pltpu.SemaphoreType.DMA((n_t,)),
+            pltpu.SMEM((n_r,), jnp.int32),
+            pltpu.SMEM((n_r,), jnp.int32),
+            pltpu.SemaphoreType.DMA((2,)),
+        ],
+        flops=6 * B * B * width,
+        nbytes=B * width * 10,
+        name="new_momentums",
+    )
     places = call(
         functools.partial(places_body, keep),
         [near((B, blocks * half * keep))] * 4,
-        (mask, tally, small, bundles),
-        [SM, SM, VM, VM],
+        (shares, small, bundles),
+        [VM] * 3,
         [VM] * 4,
         name="places",
     )
@@ -433,31 +465,21 @@
     )
 
     ships = [ship] + [swap(ship, 2 * i) for i in range(1, half)]
-    new = call(
-        functools.partial(return_body, n_t, keep),
-        jax.ShapeDtypeStruct((B, width), F32),
-        (vel[0], p_own, q_own, *[grads[k] for k in range(n_t)]),
-        [VM] * (3 + n_t),
-        ANY,
-        scratch=[pltpu.VMEM((B, width), F32), pltpu.SemaphoreType.DMA((n_t,))],
-        flops=6 * B * B * width,
-        nbytes=B * width * 10,
-        name="new_momentums",
-    )
-    mine = call(
-        functools.partial(join_body, half),
-        near((half, keep, width)),
-        (*ships, far(new), far(input_grad), places[0]),
-        [VM] * half + [ANY] * 3,
+    other_own = swap(ship, 1)
+    others = call(
+        functools.partial(join_body, half - 1),
+        near((half - 1, keep, width)),
+        (other_own, *ships[1:], far(new), far(input_grad), places[0]),
+        [ANY] + [VM] * (half - 1) + [ANY] * 3,
         VM,
         name="join_kept",
     )
-    other = swap(mine, 1)
+    other = swap(others, 1)
     half_sum = call(
         half_update_body,
         near((groups * B, G), F32),
-        (*places[:2], mine),
-        [VM] * 3,
+        (*places[:2], ship, others),
+        [VM] * 4,
         VM,
         name="half_updates",
     )
@@ -465,8 +487,8 @@
     update = call(
         functools.partial(update_body, chunk),
         jax.ShapeDtypeStruct((B, width), F32),
-        (half_sum, *places[2:], other),
-        [VM] * 4,
+        (half_sum, *places[2:], other_own, other),
+        [VM] * 5,
         ANY,
         scratch=[
             pltpu.VMEM((B, width), F32),

time: 35.8 us -> 35.7 us (level)
  Pallas kernels: 8.79 us -> 8.27 us
  waiting for transfers between devices: 1.85 us -> 2.26 us
    pallas_call x14, Pallas kernels: 8.79 us -> 8.27 us  [call(): pl.pallas_call(body, out_shape=out_shape, in_specs=in_specs, out_specs=ou...]
    ppermute x4 -> x5, waiting for transfers between devices: 1.53 us -> 1.94 us  [swap(): return lax.ppermute(x, 'replica', [(i, i ^ m) for i in range(n_r)])]
    ppermute x4 -> x5, starting transfers between devices: 3.62 us -> 3.63 us  [swap(): return lax.ppermute(x, 'replica', [(i, i ^ m) for i in range(n_r)])]
  transfers between devices with their start and end apart: 10 -> 11, of which waited for: 3 -> 3; matrix products, arithmetic and copies ran while one was open for 0% -> 0% of each run, Pallas kernels for 16% -> 15%
where the time goes in v20:
time: 35.7 us; the launch traced here: 35.4 us
  starting transfers between devices  14.2 us (40%)
  blocking collectives  9.87 us (28%)
  Pallas kernels  8.27 us (23%)
  waiting for transfers between devices  2.26 us (6%)
  between operations  0.77 us (2%)
    ppermute x6, starting transfers between devices, trade(): return lax.ppermute(x, 'tensor', [(i, i ^ k) for i in range(n_t)])  10.6 us
    all_gather x1, blocking collectives, per_device(): bundles = lax.all_gather(bundle, 'replica', axis=0)  9.87 us
    pallas_call x14, Pallas kernels, call(): pl.pallas_call(body, out_shape=out_shape, in_specs=in_specs, out_specs=ou...  8.27 us
    ppermute x5, starting transfers between devices, swap(): return lax.ppermute(x, 'replica', [(i, i ^ m) for i in range(n_r)])  3.63 us
    ppermute x5, waiting for transfers between devices, swap(): return lax.ppermute(x, 'replica', [(i, i ^ m) for i in range(n_r)])  1.94 us
  transfers between devices with their start and end apart: 11, of which 3 were waited for; matrix products, arithmetic and copies ran while one was open for 0% of the time, Pallas kernels for 15%

profile of v20, /device:TPU:0, one launch (start us, length us, event | category | flops | bytes accessed | tf_op | source)
XLA Modules:
  0.0 35.4 jit_solution(17602087847880758308)
XLA Ops:
  0.6 1.2 %up_grads.1 = (bf16[64,128]{1,0:T(8,128)(2,1)S(1)}, bf16[144,128]{1,0:T(8,128)(2,1)S(1)}, bf16[144,128]{1,0:T(8,128)(2,1)S(1)}, bf16[144,128]{1,0:T(8,128)(2,1)S...) custom-call(bf16[64,128]{1,0:T(8,128)(2,1)} %bitcast.16, ...), custom_call_target="tpu_custom_call" | custom-call | bytes 819200 | tf_op jit(solution)/shard_map/up_grads/pallas_call | solution.py:81
  1.8 4.1 %collective-permute-start.1 = (bf16[144,128]{1,0:T(8,128)(2,1)S(1)}, bf16[144,128]{1,0:T(8,128)(2,1)S(1)}, u32[]{:S(2)}, u32[]{:S(2)}) collective-permute-start(bf16[144,128]{1,0:T(8,128)(2,1)S(1)} %get-tuple-element.31), channel_id=1, source_target_pairs={{0,2},{1,3},{2,0},{3,1},{4,6},{5,7},{6,4},{7,5},{8,10},{9,11},{10,... | collective-permute-start | bytes 110600 | tf_op jit(solution)/shard_map/ppermute | solution.py:348
  5.9 1.6 %collective-permute-start = (bf16[144,128]{1,0:T(8,128)(2,1)S(1)}, bf16[144,128]{1,0:T(8,128)(2,1)S(1)}, u32[]{:S(2)}, u32[]{:S(2)}) collective-permute-start(bf16[144,128]{1,0:T(8,128)(2,1)S(1)} %get-tuple-element.28), channel_id=1, source_target_pairs={{0,1},{1,0},{2,3},{3,2},{4,5},{5,4},{6,7},{7,6},{8,9},{9,8},{10,11... | collective-permute-start | bytes 110600 | tf_op jit(solution)/shard_map/ppermute | solution.py:348
  7.5 0.0 collective-permute-start.2
  7.5 0.5 %own_places.1 = (bf16[64,2560]{1,0:T(8,128)(2,1)S(1)}, bf16[1280,128]{1,0:T(8,128)(2,1)S(1)}) custom-call(s32[8,80]{1,0:T(8,128)S(1)} %get-tuple-element.25.lines, bf16[128,256]{1,0:T(8,128)(2,1)S(1)} %get-tuple-element.26.small), custom_call_target="tpu_custom_call" | custom-call | tf_op jit(solution)/shard_map/own_places/pallas_call | solution.py:81
  8.0 0.3 collective-permute-done.1.refs_1_.refs_2_.refs_0_
  8.3 0.2 weight_grads.5
  8.5 0.0 copy-start
  8.5 0.0 copy-start.2
  8.5 2.7 %collective-permute-start.5 = (bf16[64,1280]{1,0:T(8,128)(2,1)S(1)}, bf16[64,1280]{1,0:T(8,128)(2,1)S(1)}, u32[]{:S(2)}, u32[]{:S(2)}) collective-permute-start(bf16[64,1280]{1,0:T(8,128)(2,1)S(1)} %weight_grads.5), channel_id=1, source_target_pairs={{0,2},{1,3},{2,0},{3,1},{4,6},{5,7},{6,4},{7,5},{8,10},{9,11},{10,... | collective-permute-start | bytes 491528 | tf_op jit(solution)/shard_map/ppermute | solution.py:348
  11.3 0.0 collective-permute-done.refs_0_.refs_1_
  11.3 0.2 weight_grads.3
  11.5 2.1 %collective-permute-start.4 = (bf16[64,1280]{1,0:T(8,128)(2,1)S(1)}, bf16[64,1280]{1,0:T(8,128)(2,1)S(1)}, u32[]{:S(2)}, u32[]{:S(2)}) collective-permute-start(bf16[64,1280]{1,0:T(8,128)(2,1)S(1)} %get-tuple-element.30.after), channel_id=1, source_target_pairs={{0,1},{1,0},{2,3},{3,2},{4,5},{5,4},{6,7},{7,6},{8,9},{9,8},{10,11... | collective-permute-start | bytes 491528 | tf_op jit(solution)/shard_map/ppermute | solution.py:348
  13.6 0.0 collective-permute-done.2.refs_2_.refs_3_.refs_0_
  13.6 0.2 weight_grads.4
  13.8 0.1 collective-permute-start.3
  13.9 9.9 %all-gather = bf16[2048,128]{1,0:T(8,128)(2,1)S(1)} all-gather(bf16[256,128]{1,0:T(8,128)(2,1)S(1)} %bundle.1), channel_id=2, replica_groups=mesh['replica'=8,'tensor'=4] {'replica'}, dimensions={0}, use_global_device_ids=true | all-gather | bytes 589824 | tf_op jit(solution)/shard_map/all_gather | solution.py:412
  23.8 0.0 collective-permute-done.5.refs_2_
  23.8 0.0 collective-permute-done.4.refs_1_
  23.8 0.0 copy-done
  23.8 0.0 copy-done.2
  23.8 0.7 %kept_rows.2 = (bf16[8,5120]{1,0:T(8,128)(2,1)S(1)}, f32[8,5120]{1,0:T(8,128)S(1)}) custom-call(f32[64,5120]{1,0:T(8,128)S(1)} %bitcast.12, bf16[1280,128]{1,0:T(8,128)(2,1)S(1)} %get-tuple-element.27.after.a_ref, bf16[1024,256]{1,0:T(8,128)(2,1)S(1)} %copy-done.2, bf16[8,256,128]{2,1,0:T(8,128)(2,1)S(1)} %bitcast.8, ...), custom_call_target="tpu_custom_call" | custom-call | flops 94371840 | bytes 1474560 | tf_op jit(solution)/shard_map/kept_rows/pallas_call | solution.py:81
  24.5 0.0 collective-permute-done.3.refs_0_.refs_3_
  24.5 0.0 copy-start.1
  24.6 0.5 %kept_rows.3 = (bf16[8,5120]{1,0:T(8,128)(2,1)S(1)}, f32[8,5120]{1,0:T(8,128)S(1)}) custom-call(f32[64,5120]{1,0:T(8,128)S(1)} %bitcast.13, bf16[1280,128]{1,0:T(8,128)(2,1)S(1)} %get-tuple-element.27.after.a_ref, bf16[1024,256]{1,0:T(8,128)(2,1)S(1)} %copy-done.2, bf16[8,256,128]{2,1,0:T(8,128)(2,1)S(1)} %bitcast.9, ...), custom_call_target="tpu_custom_call", output_to_operand_aliasing={{0}: (5, {}), {1}: (6, {})} | custom-call | flops 31457280 | bytes 491520 | tf_op jit(solution)/shard_map/kept_rows/pallas_call | solution.py:81
  25.0 1.9 %collective-permute-start.9 = (bf16[8,5120]{1,0:T(8,128)(2,1)S(1)}, bf16[8,5120]{1,0:T(8,128)(2,1)S(1)}, u32[]{:S(2)}, u32[]{:S(2)}) collective-permute-start(bf16[8,5120]{1,0:T(8,128)(2,1)S(1)} %get-tuple-element.42.own), channel_id=1, source_target_pairs={{0,24},{4,28},{8,16},{12,20},{16,8},{20,12},{24,0},{28,4},{1,25},{... | collective-permute-start | bytes 245768 | tf_op jit(solution)/shard_map/ppermute | solution.py:353
  26.9 1.1 %collective-permute-start.8 = (bf16[8,5120]{1,0:T(8,128)(2,1)S(1)}, bf16[8,5120]{1,0:T(8,128)(2,1)S(1)}, u32[]{:S(2)}, u32[]{:S(2)}) collective-permute-start(bf16[8,5120]{1,0:T(8,128)(2,1)S(1)} %get-tuple-element.42.own), channel_id=1, source_target_pairs={{0,16},{4,20},{8,24},{12,28},{16,0},{20,4},{24,8},{28,12},{1,17},{... | collective-permute-start | bytes 245768 | tf_op jit(solution)/shard_map/ppermute | solution.py:353
  28.1 0.5 %collective-permute-start.7 = (bf16[8,5120]{1,0:T(8,128)(2,1)S(1)}, bf16[8,5120]{1,0:T(8,128)(2,1)S(1)}, u32[]{:S(2)}, u32[]{:S(2)}) collective-permute-start(bf16[8,5120]{1,0:T(8,128)(2,1)S(1)} %get-tuple-element.42.own), channel_id=1, source_target_pairs={{0,8},{4,12},{8,0},{12,4},{16,24},{20,28},{24,16},{28,20},{1,9},{5... | collective-permute-start | bytes 245768 | tf_op jit(solution)/shard_map/ppermute | solution.py:353
  28.6 0.0 collective-permute-start.6
  28.6 0.0 copy-done.1
  28.6 1.0 %input_grads.1.refs_5_ = bf16[128,1280]{1,0:T(8,128)(2,1)} custom-call(bf16[64,5120]{1,0:T(8,128)(2,1)S(1)} %copy-done.1, bf16[8,256,128]{2,1,0:T(8,128)(2,1)S(1)} %bitcast.10, bf16[64,128]{1,0:T(8,128)(2,1)S(1)} %get-tuple-element.29.refs_1_.refs_0_, bf16[144,128]{1,0:T(8,128)(2,1)S(1)} %collective-permute-done.refs_0_.refs_1_, ...), custom_call_target="tpu_custom_call" | custom-call | flops 83886080 | bytes 983040 | tf_op jit(solution)/shard_map/input_grads/pallas_call | solution.py:81
  29.6 1.3 %new_momentums.1 = (f32[64,5120]{1,0:T(8,128)}, f32[2,8,128]{2,1,0:T(8,128)S(1)}) custom-call(f32[64,5120]{1,0:T(8,128)S(1)} %bitcast.14, bf16[64,2560]{1,0:T(8,128)(2,1)S(1)} %get-tuple-element.33.p_ref, f32[8,5120]{1,0:T(8,128)S(1)} %get-tuple-element.37.q, s32[8]{0:T(128)} %mask.1, s32[8]{0:T(128)} %tally.1, f32[64,1280]{1,0:T(8,128)S(1)} %get-tuple-element.34.refs_0_, ...), custom_call_target="tpu_custom_call" | custom-call | flops 125829120 | bytes 3276800 | tf_op jit(solution)/shard_map/new_momentums/pallas_call | solution.py:81
  31.0 0.6 %places.1 = (bf16[64,2560]{1,0:T(8,128)(2,1)S(1)}, bf16[64,2560]{1,0:T(8,128)(2,1)S(1)}, bf16[64,2560]{1,0:T(8,128)(2,1)S(1)}, bf16[64,2560]{1,0:T(8,128)(2,1)S(1)}) custom-call(f32[2,8,128]{2,1,0:T(8,128)S(1)} %get-tuple-element.39.w_ref, bf16[128,256]{1,0:T(8,128)(2,1)S(1)} %get-tuple-element.26.small, bf16[8,256,128]{2,1,0:T(8,128)(2,1)S(1)} %bitcast.11), custom_call_target="tpu_custom_call" | custom-call | tf_op jit(solution)/shard_map/places/pallas_call | solution.py:81
  31.6 0.0 collective-permute-done.9.refs_3_
  31.6 0.9 %collective-permute-done.8.refs_2_ = bf16[8,5120]{1,0:T(8,128)(2,1)S(1)} collective-permute-done((bf16[8,5120]{1,0:T(8,128)(2,1)S(1)}, bf16[8,5120]{1,0:T(8,128)(2,1)S(1)}, u32[]{:S(2)}, u32[]{:S(2)}) %collective-permute-start.8) | collective-permute-done | bytes 81952 | tf_op jit(solution)/shard_map/ppermute | solution.py:353
  32.5 0.0 collective-permute-done.7.refs_1_
  32.5 0.0 collective-permute-done.6.refs_0_.own
  32.5 0.1 collective-permute-start.10
  32.6 0.5 %half_updates.1.half_sum = f32[1280,256]{1,0:T(8,128)S(1)} custom-call(bf16[64,2560]{1,0:T(8,128)(2,1)S(1)} %get-tuple-element.40.refs_6_.p_hi, bf16[64,2560]{1,0:T(8,128)(2,1)S(1)} %get-tuple-element.41.p_lo, bf16[8,5120]{1,0:T(8,128)(2,1)S(1)} %get-tuple-element.42.own, bf16[3,8,5120]{2,1,0:T(8,128)(2,1)S(1)} %join_kept.1.others), custom_call_target="tpu_custom_call" | custom-call | tf_op jit(solution)/shard_map/half_updates/pallas_call | solution.py:81
  33.1 1.0 %collective-permute-done.10.others = bf16[3,8,5120]{2,1,0:T(8,128)(2,1)S(1)} collective-permute-done((bf16[3,8,5120]{2,1,0:T(8,128)(2,1)S(1)}, bf16[3,8,5120]{2,1,0:T(8,128)(2,1)S(1)}, u32[]{:S(2)}, u32[]{:S(2)}) %collective-permute-start.10) | collective-permute-done | bytes 245792 | tf_op jit(solution)/shard_map/ppermute | solution.py:353
  34.1 1.3 %updates.1 = f32[64,5120]{1,0:T(8,128)} custom-call(f32[1280,256]{1,0:T(8,128)S(1)} %half_updates.1.half_sum, bf16[64,2560]{1,0:T(8,128)(2,1)S(1)} %get-tuple-element.43.p_hi, bf16[64,2560]{1,0:T(8,128)(2,1)S(1)} %get-tuple-element.44.p_lo, bf16[8,5120]{1,0:T(8,128)(2,1)S(1)} %collective-permute-done.6.refs_0_.own, ...), custom_call_target="tpu_custom_call" | custom-call | flops 671088640 | bytes 2621440 | tf_op jit(solution)/shard_map/updates/pallas_call | solution.py:81
  (2 shorter events, 0.0 us)
Async XLA Ops:
  1.8 6.5 %collective-permute-start.1 = (bf16[144,128]{1,0:T(8,128)(2,1)S(1)}, bf16[144,128]{1,0:T(8,128)(2,1)S(1)}, u32[]{:S(2)}, u32[]{:S(2)}) collective-permute-start(bf16[144,128]{1,0:T(8,128)(2,1)S(1)} %get-tuple-element.31), channel_id=1, source_target_pairs={{0,2},{1,3},{2,0},{3,1},{4,6},{5,7},{6,4},{7,5},{8,10},{9,11},{10,... | collective-permute-start | bytes 110600 | tf_op jit(solution)/shard_map/ppermute | solution.py:348
  5.9 5.4 %collective-permute-start = (bf16[144,128]{1,0:T(8,128)(2,1)S(1)}, bf16[144,128]{1,0:T(8,128)(2,1)S(1)}, u32[]{:S(2)}, u32[]{:S(2)}) collective-permute-start(bf16[144,128]{1,0:T(8,128)(2,1)S(1)} %get-tuple-element.28), channel_id=1, source_target_pairs={{0,1},{1,0},{2,3},{3,2},{4,5},{5,4},{6,7},{7,6},{8,9},{9,8},{10,11... | collective-permute-start | bytes 110600 | tf_op jit(solution)/shard_map/ppermute | solution.py:348
  7.5 6.2 %collective-permute-start.2 = (bf16[144,128]{1,0:T(8,128)(2,1)S(1)}, bf16[144,128]{1,0:T(8,128)(2,1)S(1)}, u32[]{:S(2)}, u32[]{:S(2)}) collective-permute-start(bf16[144,128]{1,0:T(8,128)(2,1)S(1)} %get-tuple-element.32), channel_id=1, source_target_pairs={{0,3},{1,2},{2,1},{3,0},{4,7},{5,6},{6,5},{7,4},{8,11},{9,10},{10,... | collective-permute-start | bytes 110600 | tf_op jit(solution)/shard_map/ppermute | solution.py:348
  8.5 15.3 %copy-start = (f32[1,64,5120]{2,1,0:T(8,128)S(1)}, f32[1,64,5120]{2,1,0:T(8,128)}, u32[]{:S(2)}) copy-start(f32[1,64,5120]{2,1,0:T(8,128)} %param.14) | copy-start | bytes 3932164
  8.5 15.3 %copy-start.2 = (bf16[1024,256]{1,0:T(8,128)(2,1)S(1)}, bf16[1024,256]{1,0:T(8,128)(2,1)}, u32[]{:S(2)}) copy-start(bf16[1024,256]{1,0:T(8,128)(2,1)} %constant.4.clone.tab) | copy-start | bytes 1572868
  8.5 15.3 %collective-permute-start.5 = (bf16[64,1280]{1,0:T(8,128)(2,1)S(1)}, bf16[64,1280]{1,0:T(8,128)(2,1)S(1)}, u32[]{:S(2)}, u32[]{:S(2)}) collective-permute-start(bf16[64,1280]{1,0:T(8,128)(2,1)S(1)} %weight_grads.5), channel_id=1, source_target_pairs={{0,2},{1,3},{2,0},{3,1},{4,6},{5,7},{6,4},{7,5},{8,10},{9,11},{10,... | collective-permute-start | bytes 491528 | tf_op jit(solution)/shard_map/ppermute | solution.py:348
  11.5 12.3 %collective-permute-start.4 = (bf16[64,1280]{1,0:T(8,128)(2,1)S(1)}, bf16[64,1280]{1,0:T(8,128)(2,1)S(1)}, u32[]{:S(2)}, u32[]{:S(2)}) collective-permute-start(bf16[64,1280]{1,0:T(8,128)(2,1)S(1)} %get-tuple-element.30.after), channel_id=1, source_target_pairs={{0,1},{1,0},{2,3},{3,2},{4,5},{5,4},{6,7},{7,6},{8,9},{9,8},{10,11... | collective-permute-start | bytes 491528 | tf_op jit(solution)/shard_map/ppermute | solution.py:348
  13.8 10.7 %collective-permute-start.3 = (bf16[64,1280]{1,0:T(8,128)(2,1)S(1)}, bf16[64,1280]{1,0:T(8,128)(2,1)S(1)}, u32[]{:S(2)}, u32[]{:S(2)}) collective-permute-start(bf16[64,1280]{1,0:T(8,128)(2,1)S(1)} %weight_grads.4), channel_id=1, source_target_pairs={{0,3},{1,2},{2,1},{3,0},{4,7},{5,6},{6,5},{7,4},{8,11},{9,10},{10,... | collective-permute-start | bytes 491528 | tf_op jit(solution)/shard_map/ppermute | solution.py:348
  24.5 4.1 %copy-start.1 = (bf16[64,5120]{1,0:T(8,128)(2,1)S(1)}, bf16[64,5120]{1,0:T(8,128)(2,1)}, u32[]{:S(2)}) copy-start(bf16[64,5120]{1,0:T(8,128)(2,1)} %exp_ref.3) | copy-start | bytes 1966084
  25.0 6.5 %collective-permute-start.9 = (bf16[8,5120]{1,0:T(8,128)(2,1)S(1)}, bf16[8,5120]{1,0:T(8,128)(2,1)S(1)}, u32[]{:S(2)}, u32[]{:S(2)}) collective-permute-start(bf16[8,5120]{1,0:T(8,128)(2,1)S(1)} %get-tuple-element.42.own), channel_id=1, source_target_pairs={{0,24},{4,28},{8,16},{12,20},{16,8},{20,12},{24,0},{28,4},{1,25},{... | collective-permute-start | bytes 245768 | tf_op jit(solution)/shard_map/ppermute | solution.py:353
  26.9 5.5 %collective-permute-start.8 = (bf16[8,5120]{1,0:T(8,128)(2,1)S(1)}, bf16[8,5120]{1,0:T(8,128)(2,1)S(1)}, u32[]{:S(2)}, u32[]{:S(2)}) collective-permute-start(bf16[8,5120]{1,0:T(8,128)(2,1)S(1)} %get-tuple-element.42.own), channel_id=1, source_target_pairs={{0,16},{4,20},{8,24},{12,28},{16,0},{20,4},{24,8},{28,12},{1,17},{... | collective-permute-start | bytes 245768 | tf_op jit(solution)/shard_map/ppermute | solution.py:353
  28.1 4.4 %collective-permute-start.7 = (bf16[8,5120]{1,0:T(8,128)(2,1)S(1)}, bf16[8,5120]{1,0:T(8,128)(2,1)S(1)}, u32[]{:S(2)}, u32[]{:S(2)}) collective-permute-start(bf16[8,5120]{1,0:T(8,128)(2,1)S(1)} %get-tuple-element.42.own), channel_id=1, source_target_pairs={{0,8},{4,12},{8,0},{12,4},{16,24},{20,28},{24,16},{28,20},{1,9},{5... | collective-permute-start | bytes 245768 | tf_op jit(solution)/shard_map/ppermute | solution.py:353
  28.6 3.9 %collective-permute-start.6 = (bf16[8,5120]{1,0:T(8,128)(2,1)S(1)}, bf16[8,5120]{1,0:T(8,128)(2,1)S(1)}, u32[]{:S(2)}, u32[]{:S(2)}) collective-permute-start(bf16[8,5120]{1,0:T(8,128)(2,1)S(1)} %get-tuple-element.42.own), channel_id=1, source_target_pairs={{0,4},{4,0},{8,12},{12,8},{16,20},{20,16},{24,28},{28,24},{1,5},{5... | collective-permute-start | bytes 245768 | tf_op jit(solution)/shard_map/ppermute | solution.py:353
  32.5 1.6 %collective-permute-start.10 = (bf16[3,8,5120]{2,1,0:T(8,128)(2,1)S(1)}, bf16[3,8,5120]{2,1,0:T(8,128)(2,1)S(1)}, u32[]{:S(2)}, u32[]{:S(2)}) collective-permute-start(bf16[3,8,5120]{2,1,0:T(8,128)(2,1)S(1)} %join_kept.1.others), channel_id=1, source_target_pairs={{0,4},{4,0},{8,12},{12,8},{16,20},{20,16},{24,28},{28,24},{1,5},{5... | collective-permute-start | bytes 737288 | tf_op jit(solution)/shard_map/ppermute | solution.py:353

commit v21 on v20

--- a/solution.py
+++ b/solution.py
@@ -148,8 +148,12 @@
 
 
 def join_body(n, *refs):
-    for i, ref in enumerate(refs[1 : n + 1]):
-        refs[-1][i] = ref[...]
+    core = lax.rem(lax.axis_index("replica"), 2)
+    late, soon, *rest = refs[1 : n + 1]
+    refs[-1][core] = soon[...]
+    refs[-1][1 - core] = late[...]
+    for i, ref in enumerate(rest):
+        refs[-1][2 + i] = ref[...]
 
 
 def own_body(keep, lines, small, p_ref, a_ref):
@@ -464,12 +468,15 @@
         name="input_grads",
     )
 
-    ships = [ship] + [swap(ship, 2 * i) for i in range(1, half)]
+    crossed = [
+        lax.ppermute(ship, "replica", [(r, r ^ (2, 4)[(r + turn) % 2]) for r in range(n_r)]) for turn in range(2)
+    ]
+    ships = [*reversed(crossed), swap(ship, 6)]
     other_own = swap(ship, 1)
     others = call(
         functools.partial(join_body, half - 1),
         near((half - 1, keep, width)),
-        (other_own, *ships[1:], far(new), far(input_grad), places[0]),
+        (other_own, *ships, far(new), far(input_grad), places[0]),
         [ANY] + [VM] * (half - 1) + [ANY] * 3,
         VM,
         name="join_kept",

time: 35.7 us -> 35.7 us (level)
    ppermute x5 -> x3, starting transfers between devices: 3.63 us -> 1.97 us  [swap(): return lax.ppermute(x, 'replica', [(i, i ^ m) for i in range(n_r)])]
    ppermute x0 -> x2, starting transfers between devices: none -> 1.66 us  [per_device(): lax.ppermute(ship, 'replica', [(r, r ^ (2, 4)[(r + turn) % 2]) for r in r...]
    ppermute x0 -> x2, waiting for transfers between devices: none -> 0.94 us  [per_device(): lax.ppermute(ship, 'replica', [(r, r ^ (2, 4)[(r + turn) % 2]) for r in r...]
    ppermute x5 -> x3, waiting for transfers between devices: 1.94 us -> 1.01 us  [swap(): return lax.ppermute(x, 'replica', [(i, i ^ m) for i in range(n_r)])]
where the time goes in v21:
time: 35.7 us; the launch traced here: 35.4 us
  starting transfers between devices  14.2 us (40%)
  blocking collectives  9.87 us (28%)
  Pallas kernels  8.27 us (23%)
  waiting for transfers between devices  2.27 us (6%)
  between operations  0.78 us (2%)
    ppermute x6, starting transfers between devices, trade(): return lax.ppermute(x, 'tensor', [(i, i ^ k) for i in range(n_t)])  10.6 us
    all_gather x1, blocking collectives, per_device(): bundles = lax.all_gather(bundle, 'replica', axis=0)  9.87 us
    pallas_call x14, Pallas kernels, call(): pl.pallas_call(body, out_shape=out_shape, in_specs=in_specs, out_specs=ou...  8.27 us
    ppermute x3, starting transfers between devices, swap(): return lax.ppermute(x, 'replica', [(i, i ^ m) for i in range(n_r)])  1.97 us
    ppermute x2, starting transfers between devices, per_device(): lax.ppermute(ship, 'replica', [(r, r ^ (2, 4)[(r + turn) % 2]) for r in r...  1.66 us
    ppermute x3, waiting for transfers between devices, swap(): return lax.ppermute(x, 'replica', [(i, i ^ m) for i in range(n_r)])  1.01 us
    ppermute x2, waiting for transfers between devices, per_device(): lax.ppermute(ship, 'replica', [(r, r ^ (2, 4)[(r + turn) % 2]) for r in r...  0.94 us
  transfers between devices with their start and end apart: 11, of which 3 were waited for; matrix products, arithmetic and copies ran while one was open for 0% of the time, Pallas kernels for 15%

profile of v21, /device:TPU:0, one launch (start us, length us, event | category | flops | bytes accessed | tf_op | source)
XLA Modules:
  0.0 35.4 jit_solution(15472956408834369031)
XLA Ops:
  0.6 1.2 %up_grads.1 = (bf16[64,128]{1,0:T(8,128)(2,1)S(1)}, bf16[144,128]{1,0:T(8,128)(2,1)S(1)}, bf16[144,128]{1,0:T(8,128)(2,1)S(1)}, bf16[144,128]{1,0:T(8,128)(2,1)S...) custom-call(bf16[64,128]{1,0:T(8,128)(2,1)} %bitcast.16, ...), custom_call_target="tpu_custom_call" | custom-call | bytes 819200 | tf_op jit(solution)/shard_map/up_grads/pallas_call | solution.py:81
  1.8 4.1 %collective-permute-start.1 = (bf16[144,128]{1,0:T(8,128)(2,1)S(1)}, bf16[144,128]{1,0:T(8,128)(2,1)S(1)}, u32[]{:S(2)}, u32[]{:S(2)}) collective-permute-start(bf16[144,128]{1,0:T(8,128)(2,1)S(1)} %get-tuple-element.31), channel_id=1, source_target_pairs={{0,2},{1,3},{2,0},{3,1},{4,6},{5,7},{6,4},{7,5},{8,10},{9,11},{10,... | collective-permute-start | bytes 110600 | tf_op jit(solution)/shard_map/ppermute | solution.py:352
  5.9 1.6 %collective-permute-start = (bf16[144,128]{1,0:T(8,128)(2,1)S(1)}, bf16[144,128]{1,0:T(8,128)(2,1)S(1)}, u32[]{:S(2)}, u32[]{:S(2)}) collective-permute-start(bf16[144,128]{1,0:T(8,128)(2,1)S(1)} %get-tuple-element.28), channel_id=1, source_target_pairs={{0,1},{1,0},{2,3},{3,2},{4,5},{5,4},{6,7},{7,6},{8,9},{9,8},{10,11... | collective-permute-start | bytes 110600 | tf_op jit(solution)/shard_map/ppermute | solution.py:352
  7.5 0.0 collective-permute-start.2
  7.5 0.5 %own_places.1 = (bf16[64,2560]{1,0:T(8,128)(2,1)S(1)}, bf16[1280,128]{1,0:T(8,128)(2,1)S(1)}) custom-call(s32[8,80]{1,0:T(8,128)S(1)} %get-tuple-element.25.lines, bf16[128,256]{1,0:T(8,128)(2,1)S(1)} %get-tuple-element.26.small), custom_call_target="tpu_custom_call" | custom-call | tf_op jit(solution)/shard_map/own_places/pallas_call | solution.py:81
  8.0 0.3 collective-permute-done.1.refs_1_.refs_2_.refs_0_
  8.3 0.2 weight_grads.5
  8.5 0.0 copy-start
  8.5 0.0 copy-start.2
  8.5 2.7 %collective-permute-start.5 = (bf16[64,1280]{1,0:T(8,128)(2,1)S(1)}, bf16[64,1280]{1,0:T(8,128)(2,1)S(1)}, u32[]{:S(2)}, u32[]{:S(2)}) collective-permute-start(bf16[64,1280]{1,0:T(8,128)(2,1)S(1)} %weight_grads.5), channel_id=1, source_target_pairs={{0,2},{1,3},{2,0},{3,1},{4,6},{5,7},{6,4},{7,5},{8,10},{9,11},{10,... | collective-permute-start | bytes 491528 | tf_op jit(solution)/shard_map/ppermute | solution.py:352
  11.3 0.0 collective-permute-done.refs_0_.refs_1_
  11.3 0.2 weight_grads.3
  11.5 2.1 %collective-permute-start.4 = (bf16[64,1280]{1,0:T(8,128)(2,1)S(1)}, bf16[64,1280]{1,0:T(8,128)(2,1)S(1)}, u32[]{:S(2)}, u32[]{:S(2)}) collective-permute-start(bf16[64,1280]{1,0:T(8,128)(2,1)S(1)} %get-tuple-element.30.after), channel_id=1, source_target_pairs={{0,1},{1,0},{2,3},{3,2},{4,5},{5,4},{6,7},{7,6},{8,9},{9,8},{10,11... | collective-permute-start | bytes 491528 | tf_op jit(solution)/shard_map/ppermute | solution.py:352
  13.6 0.0 collective-permute-done.2.refs_2_.refs_3_.refs_0_
  13.6 0.2 weight_grads.4
  13.8 0.1 collective-permute-start.3
  13.9 9.9 %all-gather = bf16[2048,128]{1,0:T(8,128)(2,1)S(1)} all-gather(bf16[256,128]{1,0:T(8,128)(2,1)S(1)} %bundle.1), channel_id=2, replica_groups=mesh['replica'=8,'tensor'=4] {'replica'}, dimensions={0}, use_global_device_ids=true | all-gather | bytes 589824 | tf_op jit(solution)/shard_map/all_gather | solution.py:416
  23.8 0.0 collective-permute-done.5.refs_2_
  23.8 0.0 collective-permute-done.4.refs_1_
  23.8 0.0 copy-done
  23.8 0.0 copy-done.2
  23.8 0.7 %kept_rows.2 = (bf16[8,5120]{1,0:T(8,128)(2,1)S(1)}, f32[8,5120]{1,0:T(8,128)S(1)}) custom-call(f32[64,5120]{1,0:T(8,128)S(1)} %bitcast.12, bf16[1280,128]{1,0:T(8,128)(2,1)S(1)} %get-tuple-element.27.after.a_ref, bf16[1024,256]{1,0:T(8,128)(2,1)S(1)} %copy-done.2, bf16[8,256,128]{2,1,0:T(8,128)(2,1)S(1)} %bitcast.8, ...), custom_call_target="tpu_custom_call" | custom-call | flops 94371840 | bytes 1474560 | tf_op jit(solution)/shard_map/kept_rows/pallas_call | solution.py:81
  24.5 0.0 collective-permute-done.3.refs_0_.refs_3_
  24.5 0.0 copy-start.1
  24.6 0.5 %kept_rows.3 = (bf16[8,5120]{1,0:T(8,128)(2,1)S(1)}, f32[8,5120]{1,0:T(8,128)S(1)}) custom-call(f32[64,5120]{1,0:T(8,128)S(1)} %bitcast.13, bf16[1280,128]{1,0:T(8,128)(2,1)S(1)} %get-tuple-element.27.after.a_ref, bf16[1024,256]{1,0:T(8,128)(2,1)S(1)} %copy-done.2, bf16[8,256,128]{2,1,0:T(8,128)(2,1)S(1)} %bitcast.9, ...), custom_call_target="tpu_custom_call", output_to_operand_aliasing={{0}: (5, {}), {1}: (6, {})} | custom-call | flops 31457280 | bytes 491520 | tf_op jit(solution)/shard_map/kept_rows/pallas_call | solution.py:81
  25.0 1.9 %collective-permute-start.9 = (bf16[8,5120]{1,0:T(8,128)(2,1)S(1)}, bf16[8,5120]{1,0:T(8,128)(2,1)S(1)}, u32[]{:S(2)}, u32[]{:S(2)}) collective-permute-start(bf16[8,5120]{1,0:T(8,128)(2,1)S(1)} %get-tuple-element.42.own), channel_id=1, source_target_pairs={{0,24},{4,28},{8,16},{12,20},{16,8},{20,12},{24,0},{28,4},{1,25},{... | collective-permute-start | bytes 245768 | tf_op jit(solution)/shard_map/ppermute | solution.py:357
  26.9 1.1 %collective-permute-start.8 = (bf16[8,5120]{1,0:T(8,128)(2,1)S(1)}, bf16[8,5120]{1,0:T(8,128)(2,1)S(1)}, u32[]{:S(2)}, u32[]{:S(2)}) collective-permute-start(bf16[8,5120]{1,0:T(8,128)(2,1)S(1)} %get-tuple-element.42.own), channel_id=1, source_target_pairs={{0,8},{4,20},{8,0},{12,28},{16,24},{20,4},{24,16},{28,12},{1,9},{5... | collective-permute-start | bytes 245768 | tf_op jit(solution)/shard_map/ppermute | solution.py:472
  28.1 0.5 %collective-permute-start.7 = (bf16[8,5120]{1,0:T(8,128)(2,1)S(1)}, bf16[8,5120]{1,0:T(8,128)(2,1)S(1)}, u32[]{:S(2)}, u32[]{:S(2)}) collective-permute-start(bf16[8,5120]{1,0:T(8,128)(2,1)S(1)} %get-tuple-element.42.own), channel_id=1, source_target_pairs={{0,16},{4,12},{8,24},{12,4},{16,0},{20,28},{24,8},{28,20},{1,17},{... | collective-permute-start | bytes 245768 | tf_op jit(solution)/shard_map/ppermute | solution.py:472
  28.6 0.0 collective-permute-start.6
  28.6 0.0 copy-done.1
  28.6 1.0 %input_grads.1.refs_5_ = bf16[128,1280]{1,0:T(8,128)(2,1)} custom-call(bf16[64,5120]{1,0:T(8,128)(2,1)S(1)} %copy-done.1, bf16[8,256,128]{2,1,0:T(8,128)(2,1)S(1)} %bitcast.10, bf16[64,128]{1,0:T(8,128)(2,1)S(1)} %get-tuple-element.29.refs_1_.refs_0_, bf16[144,128]{1,0:T(8,128)(2,1)S(1)} %collective-permute-done.refs_0_.refs_1_, ...), custom_call_target="tpu_custom_call" | custom-call | flops 83886080 | bytes 983040 | tf_op jit(solution)/shard_map/input_grads/pallas_call | solution.py:81
  29.6 1.3 %new_momentums.1 = (f32[64,5120]{1,0:T(8,128)}, f32[2,8,128]{2,1,0:T(8,128)S(1)}) custom-call(f32[64,5120]{1,0:T(8,128)S(1)} %bitcast.14, bf16[64,2560]{1,0:T(8,128)(2,1)S(1)} %get-tuple-element.33.p_ref, f32[8,5120]{1,0:T(8,128)S(1)} %get-tuple-element.37.q, s32[8]{0:T(128)} %mask.1, s32[8]{0:T(128)} %tally.1, f32[64,1280]{1,0:T(8,128)S(1)} %get-tuple-element.34.refs_0_, ...), custom_call_target="tpu_custom_call" | custom-call | flops 125829120 | bytes 3276800 | tf_op jit(solution)/shard_map/new_momentums/pallas_call | solution.py:81
  31.0 0.6 %places.1 = (bf16[64,2560]{1,0:T(8,128)(2,1)S(1)}, bf16[64,2560]{1,0:T(8,128)(2,1)S(1)}, bf16[64,2560]{1,0:T(8,128)(2,1)S(1)}, bf16[64,2560]{1,0:T(8,128)(2,1)S(1)}) custom-call(f32[2,8,128]{2,1,0:T(8,128)S(1)} %get-tuple-element.39.w_ref, bf16[128,256]{1,0:T(8,128)(2,1)S(1)} %get-tuple-element.26.small, bf16[8,256,128]{2,1,0:T(8,128)(2,1)S(1)} %bitcast.11), custom_call_target="tpu_custom_call" | custom-call | tf_op jit(solution)/shard_map/places/pallas_call | solution.py:81
  31.6 0.0 collective-permute-done.9.refs_3_
  31.6 0.9 %collective-permute-done.8.refs_2_ = bf16[8,5120]{1,0:T(8,128)(2,1)S(1)} collective-permute-done((bf16[8,5120]{1,0:T(8,128)(2,1)S(1)}, bf16[8,5120]{1,0:T(8,128)(2,1)S(1)}, u32[]{:S(2)}, u32[]{:S(2)}) %collective-permute-start.8) | collective-permute-done | bytes 81952 | tf_op jit(solution)/shard_map/ppermute | solution.py:472
  32.5 0.0 collective-permute-done.7.refs_1_
  32.5 0.0 collective-permute-done.6.refs_0_.own
  32.5 0.1 collective-permute-start.10
  32.6 0.5 %half_updates.1.half_sum = f32[1280,256]{1,0:T(8,128)S(1)} custom-call(bf16[64,2560]{1,0:T(8,128)(2,1)S(1)} %get-tuple-element.40.refs_6_.p_hi, bf16[64,2560]{1,0:T(8,128)(2,1)S(1)} %get-tuple-element.41.p_lo, bf16[8,5120]{1,0:T(8,128)(2,1)S(1)} %get-tuple-element.42.own, bf16[3,8,5120]{2,1,0:T(8,128)(2,1)S(1)} %join_kept.1.others), custom_call_target="tpu_custom_call" | custom-call | tf_op jit(solution)/shard_map/half_updates/pallas_call | solution.py:81
  33.1 1.0 %collective-permute-done.10.others = bf16[3,8,5120]{2,1,0:T(8,128)(2,1)S(1)} collective-permute-done((bf16[3,8,5120]{2,1,0:T(8,128)(2,1)S(1)}, bf16[3,8,5120]{2,1,0:T(8,128)(2,1)S(1)}, u32[]{:S(2)}, u32[]{:S(2)}) %collective-permute-start.10) | collective-permute-done | bytes 245792 | tf_op jit(solution)/shard_map/ppermute | solution.py:357
  34.1 1.3 %updates.1 = f32[64,5120]{1,0:T(8,128)} custom-call(f32[1280,256]{1,0:T(8,128)S(1)} %half_updates.1.half_sum, bf16[64,2560]{1,0:T(8,128)(2,1)S(1)} %get-tuple-element.43.p_hi, bf16[64,2560]{1,0:T(8,128)(2,1)S(1)} %get-tuple-element.44.p_lo, bf16[8,5120]{1,0:T(8,128)(2,1)S(1)} %collective-permute-done.6.refs_0_.own, ...), custom_call_target="tpu_custom_call" | custom-call | flops 671088640 | bytes 2621440 | tf_op jit(solution)/shard_map/updates/pallas_call | solution.py:81
  (2 shorter events, 0.0 us)
Async XLA Ops:
  1.8 6.5 %collective-permute-start.1 = (bf16[144,128]{1,0:T(8,128)(2,1)S(1)}, bf16[144,128]{1,0:T(8,128)(2,1)S(1)}, u32[]{:S(2)}, u32[]{:S(2)}) collective-permute-start(bf16[144,128]{1,0:T(8,128)(2,1)S(1)} %get-tuple-element.31), channel_id=1, source_target_pairs={{0,2},{1,3},{2,0},{3,1},{4,6},{5,7},{6,4},{7,5},{8,10},{9,11},{10,... | collective-permute-start | bytes 110600 | tf_op jit(solution)/shard_map/ppermute | solution.py:352
  5.9 5.4 %collective-permute-start = (bf16[144,128]{1,0:T(8,128)(2,1)S(1)}, bf16[144,128]{1,0:T(8,128)(2,1)S(1)}, u32[]{:S(2)}, u32[]{:S(2)}) collective-permute-start(bf16[144,128]{1,0:T(8,128)(2,1)S(1)} %get-tuple-element.28), channel_id=1, source_target_pairs={{0,1},{1,0},{2,3},{3,2},{4,5},{5,4},{6,7},{7,6},{8,9},{9,8},{10,11... | collective-permute-start | bytes 110600 | tf_op jit(solution)/shard_map/ppermute | solution.py:352
  7.5 6.2 %collective-permute-start.2 = (bf16[144,128]{1,0:T(8,128)(2,1)S(1)}, bf16[144,128]{1,0:T(8,128)(2,1)S(1)}, u32[]{:S(2)}, u32[]{:S(2)}) collective-permute-start(bf16[144,128]{1,0:T(8,128)(2,1)S(1)} %get-tuple-element.32), channel_id=1, source_target_pairs={{0,3},{1,2},{2,1},{3,0},{4,7},{5,6},{6,5},{7,4},{8,11},{9,10},{10,... | collective-permute-start | bytes 110600 | tf_op jit(solution)/shard_map/ppermute | solution.py:352
  8.5 15.3 %copy-start = (f32[1,64,5120]{2,1,0:T(8,128)S(1)}, f32[1,64,5120]{2,1,0:T(8,128)}, u32[]{:S(2)}) copy-start(f32[1,64,5120]{2,1,0:T(8,128)} %param.14) | copy-start | bytes 3932164
  8.5 15.3 %copy-start.2 = (bf16[1024,256]{1,0:T(8,128)(2,1)S(1)}, bf16[1024,256]{1,0:T(8,128)(2,1)}, u32[]{:S(2)}) copy-start(bf16[1024,256]{1,0:T(8,128)(2,1)} %constant.4.clone.tab) | copy-start | bytes 1572868
  8.5 15.3 %collective-permute-start.5 = (bf16[64,1280]{1,0:T(8,128)(2,1)S(1)}, bf16[64,1280]{1,0:T(8,128)(2,1)S(1)}, u32[]{:S(2)}, u32[]{:S(2)}) collective-permute-start(bf16[64,1280]{1,0:T(8,128)(2,1)S(1)} %weight_grads.5), channel_id=1, source_target_pairs={{0,2},{1,3},{2,0},{3,1},{4,6},{5,7},{6,4},{7,5},{8,10},{9,11},{10,... | collective-permute-start | bytes 491528 | tf_op jit(solution)/shard_map/ppermute | solution.py:352
  11.5 12.3 %collective-permute-start.4 = (bf16[64,1280]{1,0:T(8,128)(2,1)S(1)}, bf16[64,1280]{1,0:T(8,128)(2,1)S(1)}, u32[]{:S(2)}, u32[]{:S(2)}) collective-permute-start(bf16[64,1280]{1,0:T(8,128)(2,1)S(1)} %get-tuple-element.30.after), channel_id=1, source_target_pairs={{0,1},{1,0},{2,3},{3,2},{4,5},{5,4},{6,7},{7,6},{8,9},{9,8},{10,11... | collective-permute-start | bytes 491528 | tf_op jit(solution)/shard_map/ppermute | solution.py:352
  13.8 10.7 %collective-permute-start.3 = (bf16[64,1280]{1,0:T(8,128)(2,1)S(1)}, bf16[64,1280]{1,0:T(8,128)(2,1)S(1)}, u32[]{:S(2)}, u32[]{:S(2)}) collective-permute-start(bf16[64,1280]{1,0:T(8,128)(2,1)S(1)} %weight_grads.4), channel_id=1, source_target_pairs={{0,3},{1,2},{2,1},{3,0},{4,7},{5,6},{6,5},{7,4},{8,11},{9,10},{10,... | collective-permute-start | bytes 491528 | tf_op jit(solution)/shard_map/ppermute | solution.py:352
  24.5 4.1 %copy-start.1 = (bf16[64,5120]{1,0:T(8,128)(2,1)S(1)}, bf16[64,5120]{1,0:T(8,128)(2,1)}, u32[]{:S(2)}) copy-start(bf16[64,5120]{1,0:T(8,128)(2,1)} %exp_ref.3) | copy-start | bytes 1966084
  25.0 6.5 %collective-permute-start.9 = (bf16[8,5120]{1,0:T(8,128)(2,1)S(1)}, bf16[8,5120]{1,0:T(8,128)(2,1)S(1)}, u32[]{:S(2)}, u32[]{:S(2)}) collective-permute-start(bf16[8,5120]{1,0:T(8,128)(2,1)S(1)} %get-tuple-element.42.own), channel_id=1, source_target_pairs={{0,24},{4,28},{8,16},{12,20},{16,8},{20,12},{24,0},{28,4},{1,25},{... | collective-permute-start | bytes 245768 | tf_op jit(solution)/shard_map/ppermute | solution.py:357
  26.9 5.5 %collective-permute-start.8 = (bf16[8,5120]{1,0:T(8,128)(2,1)S(1)}, bf16[8,5120]{1,0:T(8,128)(2,1)S(1)}, u32[]{:S(2)}, u32[]{:S(2)}) collective-permute-start(bf16[8,5120]{1,0:T(8,128)(2,1)S(1)} %get-tuple-element.42.own), channel_id=1, source_target_pairs={{0,8},{4,20},{8,0},{12,28},{16,24},{20,4},{24,16},{28,12},{1,9},{5... | collective-permute-start | bytes 245768 | tf_op jit(solution)/shard_map/ppermute | solution.py:472
  28.1 4.4 %collective-permute-start.7 = (bf16[8,5120]{1,0:T(8,128)(2,1)S(1)}, bf16[8,5120]{1,0:T(8,128)(2,1)S(1)}, u32[]{:S(2)}, u32[]{:S(2)}) collective-permute-start(bf16[8,5120]{1,0:T(8,128)(2,1)S(1)} %get-tuple-element.42.own), channel_id=1, source_target_pairs={{0,16},{4,12},{8,24},{12,4},{16,0},{20,28},{24,8},{28,20},{1,17},{... | collective-permute-start | bytes 245768 | tf_op jit(solution)/shard_map/ppermute | solution.py:472
  28.6 3.9 %collective-permute-start.6 = (bf16[8,5120]{1,0:T(8,128)(2,1)S(1)}, bf16[8,5120]{1,0:T(8,128)(2,1)S(1)}, u32[]{:S(2)}, u32[]{:S(2)}) collective-permute-start(bf16[8,5120]{1,0:T(8,128)(2,1)S(1)} %get-tuple-element.42.own), channel_id=1, source_target_pairs={{0,4},{4,0},{8,12},{12,8},{16,20},{20,16},{24,28},{28,24},{1,5},{5... | collective-permute-start | bytes 245768 | tf_op jit(solution)/shard_map/ppermute | solution.py:357
  32.5 1.6 %collective-permute-start.10 = (bf16[3,8,5120]{2,1,0:T(8,128)(2,1)S(1)}, bf16[3,8,5120]{2,1,0:T(8,128)(2,1)S(1)}, u32[]{:S(2)}, u32[]{:S(2)}) collective-permute-start(bf16[3,8,5120]{2,1,0:T(8,128)(2,1)S(1)} %join_kept.1.others), channel_id=1, source_target_pairs={{0,4},{4,0},{8,12},{12,8},{16,20},{20,16},{24,28},{28,24},{1,5},{5... | collective-permute-start | bytes 737288 | tf_op jit(solution)/shard_map/ppermute | solution.py:357

commit v22 on v20

--- a/solution.py
+++ b/solution.py
@@ -152,7 +152,7 @@
         refs[-1][i] = ref[...]
 
 
-def own_body(keep, lines, small, p_ref, a_ref):
+def own_rows_body(keep, lines, small, a_ref):
     blocks, nb = lines.shape[1], G // B
     rows = jnp.concatenate([lines[...].astype(F32), jnp.zeros((keep, 128 - blocks), F32)], axis=1)
     lane = lax.broadcasted_iota(jnp.int32, (nb * keep, 2 * B), 1).astype(F32)
@@ -164,6 +164,11 @@
             [jnp.where(lane == num, 1.0, 0.0), jnp.where(lane - B == num, 1.0, 0.0)], axis=0
         ).astype(BF16)
         a_ref[g * B : (g + 1) * B, :] = dot(hot, small[:, : 2 * B]).astype(BF16)
+
+
+def own_columns_body(keep, lines, small, after, p_ref):
+    blocks, nb = lines.shape[1], G // B
+    rows = jnp.concatenate([lines[...].astype(F32), jnp.zeros((keep, 128 - blocks), F32)], axis=1)
     rows = jnp.concatenate([rows] * (2 * B // keep), axis=0).T
     freq = lax.broadcasted_iota(jnp.int32, (B, 2 * B), 0).astype(F32)
     block = (lax.broadcasted_iota(jnp.int32, (1, 2 * B), 1) // keep) % nb
@@ -375,13 +380,13 @@
     got = {k: trade(parts[k], k) for k in order}
     parts = [parts[0]] + [got[k] for k in range(1, n_t)]
 
-    p_own, a_own = call(
-        functools.partial(own_body, keep),
-        [near((B, groups * 2 * B)), near((groups * B, 2 * B))],
+    a_own = call(
+        functools.partial(own_rows_body, keep),
+        near((groups * B, 2 * B)),
         (own, small),
         [VM, VM],
-        [VM, VM],
-        name="own_places",
+        VM,
+        name="own_rows",
     )
 
     def grads_of(ks, after):
@@ -427,6 +432,14 @@
         )
     ship, q_own = rows
 
+    p_own = call(
+        functools.partial(own_columns_body, keep),
+        near((B, groups * 2 * B)),
+        (own, small, q_own),
+        [VM, VM, ANY],
+        VM,
+        name="own_columns",
+    )
     new, shares = call(
         functools.partial(return_body, n_t, keep),
         [jax.ShapeDtypeStruct((B, width), F32), near((2, 8, 2 * B), F32)],

time: 35.7 us -> 35.7 us (level)
    ppermute x5, waiting for transfers between devices: 1.94 us -> 1.55 us  [swap(): return lax.ppermute(x, 'replica', [(i, i ^ m) for i in range(n_r)])]
    pallas_call x14 -> x15, Pallas kernels: 8.27 us -> 8.47 us  [call(): pl.pallas_call(body, out_shape=out_shape, in_specs=in_specs, out_specs=ou...]
  transfers between devices with their start and end apart: 11 -> 11, of which waited for: 3 -> 3; matrix products, arithmetic and copies ran while one was open for 0% -> 0% of each run, Pallas kernels for 15% -> 16%
where the time goes in v22:
time: 35.7 us; the launch traced here: 35.4 us
  starting transfers between devices  14.2 us (40%)
  blocking collectives  9.87 us (28%)
  Pallas kernels  8.47 us (24%)
  waiting for transfers between devices  2.06 us (6%)
  between operations  0.78 us (2%)
    ppermute x6, starting transfers between devices, trade(): return lax.ppermute(x, 'tensor', [(i, i ^ k) for i in range(n_t)])  10.6 us
    all_gather x1, blocking collectives, per_device(): bundles = lax.all_gather(bundle, 'replica', axis=0)  9.87 us
    pallas_call x15, Pallas kernels, call(): pl.pallas_call(body, out_shape=out_shape, in_specs=in_specs, out_specs=ou...  8.47 us
    ppermute x5, starting transfers between devices, swap(): return lax.ppermute(x, 'replica', [(i, i ^ m) for i in range(n_r)])  3.63 us
    ppermute x5, waiting for transfers between devices, swap(): return lax.ppermute(x, 'replica', [(i, i ^ m) for i in range(n_r)])  1.55 us
  transfers between devices with their start and end apart: 11, of which 3 were waited for; matrix products, arithmetic and copies ran while one was open for 0% of the time, Pallas kernels for 16%

profile of v22, /device:TPU:0, one launch (start us, length us, event | category | flops | bytes accessed | tf_op | source)
XLA Modules:
  0.0 35.4 jit_solution(8930771134992893590)
XLA Ops:
  0.6 1.2 %up_grads.1 = (bf16[64,128]{1,0:T(8,128)(2,1)S(1)}, bf16[144,128]{1,0:T(8,128)(2,1)S(1)}, bf16[144,128]{1,0:T(8,128)(2,1)S(1)}, bf16[144,128]{1,0:T(8,128)(2,1)S...) custom-call(bf16[64,128]{1,0:T(8,128)(2,1)} %bitcast.16, ...), custom_call_target="tpu_custom_call" | custom-call | bytes 819200 | tf_op jit(solution)/shard_map/up_grads/pallas_call | solution.py:81
  1.8 4.1 %collective-permute-start.1 = (bf16[144,128]{1,0:T(8,128)(2,1)S(1)}, bf16[144,128]{1,0:T(8,128)(2,1)S(1)}, u32[]{:S(2)}, u32[]{:S(2)}) collective-permute-start(bf16[144,128]{1,0:T(8,128)(2,1)S(1)} %get-tuple-element.28), channel_id=1, source_target_pairs={{0,2},{1,3},{2,0},{3,1},{4,6},{5,7},{6,4},{7,5},{8,10},{9,11},{10,... | collective-permute-start | bytes 110600 | tf_op jit(solution)/shard_map/ppermute | solution.py:353
  5.9 1.6 %collective-permute-start = (bf16[144,128]{1,0:T(8,128)(2,1)S(1)}, bf16[144,128]{1,0:T(8,128)(2,1)S(1)}, u32[]{:S(2)}, u32[]{:S(2)}) collective-permute-start(bf16[144,128]{1,0:T(8,128)(2,1)S(1)} %get-tuple-element.25), channel_id=1, source_target_pairs={{0,1},{1,0},{2,3},{3,2},{4,5},{5,4},{6,7},{7,6},{8,9},{9,8},{10,11... | collective-permute-start | bytes 110600 | tf_op jit(solution)/shard_map/ppermute | solution.py:353
  7.5 0.0 collective-permute-start.2
  7.5 0.4 %own_rows.1.after.a_ref = bf16[1280,128]{1,0:T(8,128)(2,1)S(1)} custom-call(s32[8,80]{1,0:T(8,128)S(1)} %get-tuple-element.23.lines, bf16[128,256]{1,0:T(8,128)(2,1)S(1)} %get-tuple-element.24.small), custom_call_target="tpu_custom_call" | custom-call | tf_op jit(solution)/shard_map/own_rows/pallas_call | solution.py:81
  7.8 0.5 %collective-permute-done.1.refs_1_.refs_2_.refs_0_ = bf16[144,128]{1,0:T(8,128)(2,1)S(1)} collective-permute-done((bf16[144,128]{1,0:T(8,128)(2,1)S(1)}, bf16[144,128]{1,0:T(8,128)(2,1)S(1)}, u32[]{:S(2)}, u32[]{:S(2)}) %collective-permute-start.1) | collective-permute-done | bytes 36896 | tf_op jit(solution)/shard_map/ppermute | solution.py:353
  8.3 0.2 weight_grads.5
  8.5 0.0 copy-start
  8.5 0.0 copy-start.2
  8.5 2.7 %collective-permute-start.5 = (bf16[64,1280]{1,0:T(8,128)(2,1)S(1)}, bf16[64,1280]{1,0:T(8,128)(2,1)S(1)}, u32[]{:S(2)}, u32[]{:S(2)}) collective-permute-start(bf16[64,1280]{1,0:T(8,128)(2,1)S(1)} %weight_grads.5), channel_id=1, source_target_pairs={{0,2},{1,3},{2,0},{3,1},{4,6},{5,7},{6,4},{7,5},{8,10},{9,11},{10,... | collective-permute-start | bytes 491528 | tf_op jit(solution)/shard_map/ppermute | solution.py:353
  11.3 0.0 collective-permute-done.refs_0_.refs_1_
  11.3 0.2 weight_grads.3
  11.5 2.1 %collective-permute-start.4 = (bf16[64,1280]{1,0:T(8,128)(2,1)S(1)}, bf16[64,1280]{1,0:T(8,128)(2,1)S(1)}, u32[]{:S(2)}, u32[]{:S(2)}) collective-permute-start(bf16[64,1280]{1,0:T(8,128)(2,1)S(1)} %get-tuple-element.27.after), channel_id=1, source_target_pairs={{0,1},{1,0},{2,3},{3,2},{4,5},{5,4},{6,7},{7,6},{8,9},{9,8},{10,11... | collective-permute-start | bytes 491528 | tf_op jit(solution)/shard_map/ppermute | solution.py:353
  13.6 0.0 collective-permute-done.2.refs_2_.refs_3_.refs_0_
  13.6 0.2 weight_grads.4
  13.8 0.1 collective-permute-start.3
  13.9 9.9 %all-gather = bf16[2048,128]{1,0:T(8,128)(2,1)S(1)} all-gather(bf16[256,128]{1,0:T(8,128)(2,1)S(1)} %bundle.1), channel_id=2, replica_groups=mesh['replica'=8,'tensor'=4] {'replica'}, dimensions={0}, use_global_device_ids=true | all-gather | bytes 589824 | tf_op jit(solution)/shard_map/all_gather | solution.py:417
  23.8 0.0 collective-permute-done.5.refs_2_
  23.8 0.0 collective-permute-done.4.refs_1_
  23.8 0.0 copy-done
  23.8 0.0 copy-done.2
  23.8 0.7 %kept_rows.2 = (bf16[8,5120]{1,0:T(8,128)(2,1)S(1)}, f32[8,5120]{1,0:T(8,128)S(1)}) custom-call(f32[64,5120]{1,0:T(8,128)S(1)} %bitcast.12, bf16[1280,128]{1,0:T(8,128)(2,1)S(1)} %own_rows.1.after.a_ref, bf16[1024,256]{1,0:T(8,128)(2,1)S(1)} %copy-done.2, bf16[8,256,128]{2,1,0:T(8,128)(2,1)S(1)} %bitcast.8, f32[64,1280]{1,0:T(8,128)S(1)} %get-tuple-element.30.refs_0_, ...), custom_call_target="tpu_custom_call" | custom-call | flops 94371840 | bytes 1474560 | tf_op jit(solution)/shard_map/kept_rows/pallas_call | solution.py:81
  24.5 0.0 collective-permute-done.3.refs_0_.refs_3_
  24.5 0.0 copy-start.1
  24.5 0.5 %kept_rows.3 = (bf16[8,5120]{1,0:T(8,128)(2,1)S(1)}, f32[8,5120]{1,0:T(8,128)S(1)}) custom-call(f32[64,5120]{1,0:T(8,128)S(1)} %bitcast.13, bf16[1280,128]{1,0:T(8,128)(2,1)S(1)} %own_rows.1.after.a_ref, bf16[1024,256]{1,0:T(8,128)(2,1)S(1)} %copy-done.2, bf16[8,256,128]{2,1,0:T(8,128)(2,1)S(1)} %bitcast.9, ...), custom_call_target="tpu_custom_call", output_to_operand_aliasing={{0}: (5, {}), {1}: (6, {})} | custom-call | flops 31457280 | bytes 491520 | tf_op jit(solution)/shard_map/kept_rows/pallas_call | solution.py:81
  25.0 1.8 %collective-permute-start.9 = (bf16[8,5120]{1,0:T(8,128)(2,1)S(1)}, bf16[8,5120]{1,0:T(8,128)(2,1)S(1)}, u32[]{:S(2)}, u32[]{:S(2)}) collective-permute-start(bf16[8,5120]{1,0:T(8,128)(2,1)S(1)} %get-tuple-element.38.own), channel_id=1, source_target_pairs={{0,24},{4,28},{8,16},{12,20},{16,8},{20,12},{24,0},{28,4},{1,25},{... | collective-permute-start | bytes 245768 | tf_op jit(solution)/shard_map/ppermute | solution.py:358
  26.8 1.3 %collective-permute-start.8 = (bf16[8,5120]{1,0:T(8,128)(2,1)S(1)}, bf16[8,5120]{1,0:T(8,128)(2,1)S(1)}, u32[]{:S(2)}, u32[]{:S(2)}) collective-permute-start(bf16[8,5120]{1,0:T(8,128)(2,1)S(1)} %get-tuple-element.38.own), channel_id=1, source_target_pairs={{0,16},{4,20},{8,24},{12,28},{16,0},{20,4},{24,8},{28,12},{1,17},{... | collective-permute-start | bytes 245768 | tf_op jit(solution)/shard_map/ppermute | solution.py:358
  28.1 0.5 %collective-permute-start.7 = (bf16[8,5120]{1,0:T(8,128)(2,1)S(1)}, bf16[8,5120]{1,0:T(8,128)(2,1)S(1)}, u32[]{:S(2)}, u32[]{:S(2)}) collective-permute-start(bf16[8,5120]{1,0:T(8,128)(2,1)S(1)} %get-tuple-element.38.own), channel_id=1, source_target_pairs={{0,8},{4,12},{8,0},{12,4},{16,24},{20,28},{24,16},{28,20},{1,9},{5... | collective-permute-start | bytes 245768 | tf_op jit(solution)/shard_map/ppermute | solution.py:358
  28.6 0.0 collective-permute-start.6
  28.6 0.0 copy-done.1
  28.6 1.0 %input_grads.1.refs_5_ = bf16[128,1280]{1,0:T(8,128)(2,1)} custom-call(bf16[64,5120]{1,0:T(8,128)(2,1)S(1)} %copy-done.1, bf16[8,256,128]{2,1,0:T(8,128)(2,1)S(1)} %bitcast.10, bf16[64,128]{1,0:T(8,128)(2,1)S(1)} %get-tuple-element.26.refs_1_.refs_0_, bf16[144,128]{1,0:T(8,128)(2,1)S(1)} %collective-permute-done.refs_0_.refs_1_, ...), custom_call_target="tpu_custom_call" | custom-call | flops 83886080 | bytes 983040 | tf_op jit(solution)/shard_map/input_grads/pallas_call | solution.py:81
  29.6 0.4 %own_columns.1.p_ref = bf16[64,2560]{1,0:T(8,128)(2,1)S(1)} custom-call(s32[8,80]{1,0:T(8,128)S(1)} %get-tuple-element.23.lines, bf16[128,256]{1,0:T(8,128)(2,1)S(1)} %get-tuple-element.24.small, f32[8,5120]{1,0:T(8,128)S(1)} %get-tuple-element.33.after.q), custom_call_target="tpu_custom_call" | custom-call | tf_op jit(solution)/shard_map/own_columns/pallas_call | solution.py:81
  30.0 1.3 %new_momentums.1 = (f32[64,5120]{1,0:T(8,128)}, f32[2,8,128]{2,1,0:T(8,128)S(1)}) custom-call(f32[64,5120]{1,0:T(8,128)S(1)} %bitcast.14, bf16[64,2560]{1,0:T(8,128)(2,1)S(1)} %own_columns.1.p_ref, f32[8,5120]{1,0:T(8,128)S(1)} %get-tuple-element.33.after.q, s32[8]{0:T(128)} %mask.1, s32[8]{0:T(128)} %tally.1, f32[64,1280]{1,0:T(8,128)S(1)} %get-tuple-element.30.refs_0_, ...), custom_call_target="tpu_custom_call" | custom-call | flops 125829120 | bytes 3276800 | tf_op jit(solution)/shard_map/new_momentums/pallas_call | solution.py:81
  31.4 0.6 %places.1 = (bf16[64,2560]{1,0:T(8,128)(2,1)S(1)}, bf16[64,2560]{1,0:T(8,128)(2,1)S(1)}, bf16[64,2560]{1,0:T(8,128)(2,1)S(1)}, bf16[64,2560]{1,0:T(8,128)(2,1)S(1)}) custom-call(f32[2,8,128]{2,1,0:T(8,128)S(1)} %get-tuple-element.35.w_ref, bf16[128,256]{1,0:T(8,128)(2,1)S(1)} %get-tuple-element.24.small, bf16[8,256,128]{2,1,0:T(8,128)(2,1)S(1)} %bitcast.11), custom_call_target="tpu_custom_call" | custom-call | tf_op jit(solution)/shard_map/places/pallas_call | solution.py:81
  32.0 0.0 collective-permute-done.9.refs_3_
  32.0 0.5 %collective-permute-done.8.refs_2_ = bf16[8,5120]{1,0:T(8,128)(2,1)S(1)} collective-permute-done((bf16[8,5120]{1,0:T(8,128)(2,1)S(1)}, bf16[8,5120]{1,0:T(8,128)(2,1)S(1)}, u32[]{:S(2)}, u32[]{:S(2)}) %collective-permute-start.8) | collective-permute-done | bytes 81952 | tf_op jit(solution)/shard_map/ppermute | solution.py:358
  32.5 0.0 collective-permute-done.7.refs_1_
  32.5 0.0 collective-permute-done.6.refs_0_.own
  32.5 0.1 collective-permute-start.10
  32.6 0.5 %half_updates.1.half_sum = f32[1280,256]{1,0:T(8,128)S(1)} custom-call(bf16[64,2560]{1,0:T(8,128)(2,1)S(1)} %get-tuple-element.36.refs_6_.p_hi, bf16[64,2560]{1,0:T(8,128)(2,1)S(1)} %get-tuple-element.37.p_lo, bf16[8,5120]{1,0:T(8,128)(2,1)S(1)} %get-tuple-element.38.own, bf16[3,8,5120]{2,1,0:T(8,128)(2,1)S(1)} %join_kept.1.others), custom_call_target="tpu_custom_call" | custom-call | tf_op jit(solution)/shard_map/half_updates/pallas_call | solution.py:81
  33.1 1.0 %collective-permute-done.10.others = bf16[3,8,5120]{2,1,0:T(8,128)(2,1)S(1)} collective-permute-done((bf16[3,8,5120]{2,1,0:T(8,128)(2,1)S(1)}, bf16[3,8,5120]{2,1,0:T(8,128)(2,1)S(1)}, u32[]{:S(2)}, u32[]{:S(2)}) %collective-permute-start.10) | collective-permute-done | bytes 245792 | tf_op jit(solution)/shard_map/ppermute | solution.py:358
  34.1 1.3 %updates.1 = f32[64,5120]{1,0:T(8,128)} custom-call(f32[1280,256]{1,0:T(8,128)S(1)} %half_updates.1.half_sum, bf16[64,2560]{1,0:T(8,128)(2,1)S(1)} %get-tuple-element.39.p_hi, bf16[64,2560]{1,0:T(8,128)(2,1)S(1)} %get-tuple-element.40.p_lo, bf16[8,5120]{1,0:T(8,128)(2,1)S(1)} %collective-permute-done.6.refs_0_.own, ...), custom_call_target="tpu_custom_call" | custom-call | flops 671088640 | bytes 2621440 | tf_op jit(solution)/shard_map/updates/pallas_call | solution.py:81
  (2 shorter events, 0.0 us)
Async XLA Ops:
  1.8 6.5 %collective-permute-start.1 = (bf16[144,128]{1,0:T(8,128)(2,1)S(1)}, bf16[144,128]{1,0:T(8,128)(2,1)S(1)}, u32[]{:S(2)}, u32[]{:S(2)}) collective-permute-start(bf16[144,128]{1,0:T(8,128)(2,1)S(1)} %get-tuple-element.28), channel_id=1, source_target_pairs={{0,2},{1,3},{2,0},{3,1},{4,6},{5,7},{6,4},{7,5},{8,10},{9,11},{10,... | collective-permute-start | bytes 110600 | tf_op jit(solution)/shard_map/ppermute | solution.py:353
  5.9 5.4 %collective-permute-start = (bf16[144,128]{1,0:T(8,128)(2,1)S(1)}, bf16[144,128]{1,0:T(8,128)(2,1)S(1)}, u32[]{:S(2)}, u32[]{:S(2)}) collective-permute-start(bf16[144,128]{1,0:T(8,128)(2,1)S(1)} %get-tuple-element.25), channel_id=1, source_target_pairs={{0,1},{1,0},{2,3},{3,2},{4,5},{5,4},{6,7},{7,6},{8,9},{9,8},{10,11... | collective-permute-start | bytes 110600 | tf_op jit(solution)/shard_map/ppermute | solution.py:353
  7.5 6.2 %collective-permute-start.2 = (bf16[144,128]{1,0:T(8,128)(2,1)S(1)}, bf16[144,128]{1,0:T(8,128)(2,1)S(1)}, u32[]{:S(2)}, u32[]{:S(2)}) collective-permute-start(bf16[144,128]{1,0:T(8,128)(2,1)S(1)} %get-tuple-element.29), channel_id=1, source_target_pairs={{0,3},{1,2},{2,1},{3,0},{4,7},{5,6},{6,5},{7,4},{8,11},{9,10},{10,... | collective-permute-start | bytes 110600 | tf_op jit(solution)/shard_map/ppermute | solution.py:353
  8.5 15.3 %copy-start = (f32[1,64,5120]{2,1,0:T(8,128)S(1)}, f32[1,64,5120]{2,1,0:T(8,128)}, u32[]{:S(2)}) copy-start(f32[1,64,5120]{2,1,0:T(8,128)} %param.14) | copy-start | bytes 3932164
  8.5 15.3 %copy-start.2 = (bf16[1024,256]{1,0:T(8,128)(2,1)S(1)}, bf16[1024,256]{1,0:T(8,128)(2,1)}, u32[]{:S(2)}) copy-start(bf16[1024,256]{1,0:T(8,128)(2,1)} %constant.4.clone.tab) | copy-start | bytes 1572868
  8.5 15.3 %collective-permute-start.5 = (bf16[64,1280]{1,0:T(8,128)(2,1)S(1)}, bf16[64,1280]{1,0:T(8,128)(2,1)S(1)}, u32[]{:S(2)}, u32[]{:S(2)}) collective-permute-start(bf16[64,1280]{1,0:T(8,128)(2,1)S(1)} %weight_grads.5), channel_id=1, source_target_pairs={{0,2},{1,3},{2,0},{3,1},{4,6},{5,7},{6,4},{7,5},{8,10},{9,11},{10,... | collective-permute-start | bytes 491528 | tf_op jit(solution)/shard_map/ppermute | solution.py:353
  11.5 12.3 %collective-permute-start.4 = (bf16[64,1280]{1,0:T(8,128)(2,1)S(1)}, bf16[64,1280]{1,0:T(8,128)(2,1)S(1)}, u32[]{:S(2)}, u32[]{:S(2)}) collective-permute-start(bf16[64,1280]{1,0:T(8,128)(2,1)S(1)} %get-tuple-element.27.after), channel_id=1, source_target_pairs={{0,1},{1,0},{2,3},{3,2},{4,5},{5,4},{6,7},{7,6},{8,9},{9,8},{10,11... | collective-permute-start | bytes 491528 | tf_op jit(solution)/shard_map/ppermute | solution.py:353
  13.8 10.7 %collective-permute-start.3 = (bf16[64,1280]{1,0:T(8,128)(2,1)S(1)}, bf16[64,1280]{1,0:T(8,128)(2,1)S(1)}, u32[]{:S(2)}, u32[]{:S(2)}) collective-permute-start(bf16[64,1280]{1,0:T(8,128)(2,1)S(1)} %weight_grads.4), channel_id=1, source_target_pairs={{0,3},{1,2},{2,1},{3,0},{4,7},{5,6},{6,5},{7,4},{8,11},{9,10},{10,... | collective-permute-start | bytes 491528 | tf_op jit(solution)/shard_map/ppermute | solution.py:353
  24.5 4.1 %copy-start.1 = (bf16[64,5120]{1,0:T(8,128)(2,1)S(1)}, bf16[64,5120]{1,0:T(8,128)(2,1)}, u32[]{:S(2)}) copy-start(bf16[64,5120]{1,0:T(8,128)(2,1)} %exp_ref.3) | copy-start | bytes 1966084
  25.0 6.9 %collective-permute-start.9 = (bf16[8,5120]{1,0:T(8,128)(2,1)S(1)}, bf16[8,5120]{1,0:T(8,128)(2,1)S(1)}, u32[]{:S(2)}, u32[]{:S(2)}) collective-permute-start(bf16[8,5120]{1,0:T(8,128)(2,1)S(1)} %get-tuple-element.38.own), channel_id=1, source_target_pairs={{0,24},{4,28},{8,16},{12,20},{16,8},{20,12},{24,0},{28,4},{1,25},{... | collective-permute-start | bytes 245768 | tf_op jit(solution)/shard_map/ppermute | solution.py:358
  26.8 5.7 %collective-permute-start.8 = (bf16[8,5120]{1,0:T(8,128)(2,1)S(1)}, bf16[8,5120]{1,0:T(8,128)(2,1)S(1)}, u32[]{:S(2)}, u32[]{:S(2)}) collective-permute-start(bf16[8,5120]{1,0:T(8,128)(2,1)S(1)} %get-tuple-element.38.own), channel_id=1, source_target_pairs={{0,16},{4,20},{8,24},{12,28},{16,0},{20,4},{24,8},{28,12},{1,17},{... | collective-permute-start | bytes 245768 | tf_op jit(solution)/shard_map/ppermute | solution.py:358
  28.1 4.4 %collective-permute-start.7 = (bf16[8,5120]{1,0:T(8,128)(2,1)S(1)}, bf16[8,5120]{1,0:T(8,128)(2,1)S(1)}, u32[]{:S(2)}, u32[]{:S(2)}) collective-permute-start(bf16[8,5120]{1,0:T(8,128)(2,1)S(1)} %get-tuple-element.38.own), channel_id=1, source_target_pairs={{0,8},{4,12},{8,0},{12,4},{16,24},{20,28},{24,16},{28,20},{1,9},{5... | collective-permute-start | bytes 245768 | tf_op jit(solution)/shard_map/ppermute | solution.py:358
  28.6 3.9 %collective-permute-start.6 = (bf16[8,5120]{1,0:T(8,128)(2,1)S(1)}, bf16[8,5120]{1,0:T(8,128)(2,1)S(1)}, u32[]{:S(2)}, u32[]{:S(2)}) collective-permute-start(bf16[8,5120]{1,0:T(8,128)(2,1)S(1)} %get-tuple-element.38.own), channel_id=1, source_target_pairs={{0,4},{4,0},{8,12},{12,8},{16,20},{20,16},{24,28},{28,24},{1,5},{5... | collective-permute-start | bytes 245768 | tf_op jit(solution)/shard_map/ppermute | solution.py:358
  32.5 1.6 %collective-permute-start.10 = (bf16[3,8,5120]{2,1,0:T(8,128)(2,1)S(1)}, bf16[3,8,5120]{2,1,0:T(8,128)(2,1)S(1)}, u32[]{:S(2)}, u32[]{:S(2)}) collective-permute-start(bf16[3,8,5120]{2,1,0:T(8,128)(2,1)S(1)} %join_kept.1.others), channel_id=1, source_target_pairs={{0,4},{4,0},{8,12},{12,8},{16,20},{20,16},{24,28},{28,24},{1,5},{5... | collective-permute-start | bytes 737288 | tf_op jit(solution)/shard_map/ppermute | solution.py:358

commit v23 on v22

--- a/solution.py
+++ b/solution.py
@@ -75,6 +75,13 @@
 
 def far(x):
     return pltpu.with_memory_space_constraint(x, pltpu.HBM)
+
+
+def order_of(h):
+    r = lax.axis_index("replica")
+    if h == 0:
+        return [r, r ^ 2, r ^ 4, r ^ 1]
+    return [r ^ 3, r ^ 5, (r ^ 6) | 1, (r ^ 6) & ~1]
 
 
 def call(body, out_shape, ins, in_specs, out_specs, scratch=(), flops=0, nbytes=0, name=None, alias={}):
@@ -147,9 +154,9 @@
     out[(n_t - 1) * n :, :] = jnp.concatenate([rows, jnp.zeros((16 - keep, 128), F32)], axis=0).astype(BF16)
 
 
-def join_body(n, *refs):
-    for i, ref in enumerate(refs[1 : n + 1]):
-        refs[-1][i] = ref[...]
+def join_body(*refs):
+    refs[-1][0] = refs[0][...]
+    refs[-1][1] = refs[1][...]
 
 
 def own_rows_body(keep, lines, small, a_ref):
@@ -257,8 +264,7 @@
     scale = jnp.full((8, 2 * B), alive) / jnp.full((8, 2 * B), total)
     for h in range(2):
         w = jnp.zeros((8, 2 * B), F32)
-        for i in range(half):
-            r = lax.axis_index("replica") ^ (2 * i + h)
+        for i, r in enumerate(order_of(h)):
             w = jnp.where(place == i, mask_s[r].astype(F32) * tally_s[r].astype(F32), w)
         w_ref[h] = w * scale
     for copy in copies:
@@ -268,14 +274,13 @@
 def places_body(keep, w_ref, small, bundles, *p_refs):
     n_r, last = bundles.shape[0], bundles.shape[1] - 16
     half, nb = n_r // 2, G // B
-    rep = lax.axis_index("replica")
     freq = lax.broadcasted_iota(jnp.int32, (B, 2 * B), 0).astype(F32)
     lane = lax.broadcasted_iota(jnp.int32, (1, 2 * B), 1)
     block = lane // (half * keep)
     for h in range(2):
         hi_ref, lo_ref = p_refs[2 * h : 2 * h + 2]
         w = w_ref[h, :1, :]
-        rows = [bundles[rep ^ (2 * i + h), last:, :].astype(F32)[:keep] for i in range(half)]
+        rows = [bundles[r, last:, :].astype(F32)[:keep] for r in order_of(h)]
         rows = jnp.concatenate(rows * nb, axis=0).T
         for g in range(hi_ref.shape[1] // (2 * B)):
             num = rows[g * nb : g * nb + 1]
@@ -288,12 +293,9 @@
             lo_ref[:, g * 2 * B : (g + 1) * 2 * B] = lo
 
 
-def spread_rows(p_hi, p_lo, own, ships, g):
-    half, keep = ships.shape[0] + 1, ships.shape[1]
-    cut = slice(g * G, (g + 1) * G)
-    lane_block = lax.broadcasted_iota(jnp.int32, (half * keep, G), 1) // B
-    s = [own[:, cut].astype(F32)] + [ships[i, :, cut].astype(F32) for i in range(half - 1)]
-    s = jnp.concatenate(s, axis=0)
+def spread_rows(p_hi, p_lo, rows, g):
+    s = jnp.concatenate(rows, axis=0)
+    lane_block = lax.broadcasted_iota(jnp.int32, s.shape, 1) // B
     w = jnp.concatenate(
         [jnp.where(lane_block == j, s, 0.0).astype(BF16) for j in range(G // B)], axis=0
     )
@@ -302,17 +304,25 @@
     return y[:B] + y[B:]
 
 
-def half_update_body(p_hi, p_lo, own, others, out):
+def half_update_body(p_hi, p_lo, own, near_two, other_own, out):
     for g in range(out.shape[0] // B):
-        out[g * B : (g + 1) * B, :] = spread_rows(p_hi, p_lo, own, others, g)
-
-
-def update_body(chunk, half_sum, p_hi, p_lo, own, others, out, held, sems):
+        cut = slice(g * G, (g + 1) * G)
+        rows = [x.astype(F32) for x in (own[:, cut], near_two[0, :, cut], near_two[1, :, cut], other_own[:, cut])]
+        out[g * B : (g + 1) * B, :] = spread_rows(p_hi, p_lo, rows, g)
+
+
+def update_body(chunk, half_sum, p_hi, p_lo, near_two, direct, relayed, out, held, sems):
     ng = half_sum.shape[0] // B
+    second = lax.rem(lax.axis_index("replica"), 2) == 1
     copies = []
     for c in range(0, ng, chunk):
         for g in range(c, c + chunk):
-            held[:, g * G : (g + 1) * G] = half_sum[g * B : (g + 1) * B, :] + spread_rows(p_hi, p_lo, own, others, g)
+            cut = slice(g * G, (g + 1) * G)
+            rows = [near_two[i, :, cut].astype(F32) for i in range(2)]
+            rows += [
+                jnp.where(second, direct[i, :, cut].astype(F32), relayed[i, :, cut].astype(F32)) for i in range(2)
+            ]
+            held[:, cut] = half_sum[g * B : (g + 1) * B, :] + spread_rows(p_hi, p_lo, rows, g)
         cut = pl.ds(c * G, chunk * G)
         copies.append(pltpu.make_async_copy(held.at[:, cut], out.at[:, cut], sems.at[c // chunk]))
         copies[-1].start()
@@ -477,22 +487,79 @@
         name="input_grads",
     )
 
+    other_own = swap(ship, 1)
+    pair = call(
+        join_body,
+        near((2, keep, width)),
+        (ship, other_own),
+        [VM] * 2,
+        VM,
+        name="join_cores",
+    )
+    direct = lax.ppermute(pair, "replica", [(r, r ^ 6) for r in range(n_r) if r % 2])
+    beside = [swap(ship, 2), swap(ship, 4)]
+    p_own = call(
+        functools.partial(own_columns_body, keep),
+        near((B, groups * 2 * B)),
+        (own, small, q_own),
+        [VM, VM, ANY],
+        VM,
+        name="own_columns",
+    )
+    new, shares = call(
+        functools.partial(return_body, n_t, keep),
+        [jax.ShapeDtypeStruct((B, width), F32), near((2, 8, 2 * B), F32)],
+        (vel[0], p_own, q_own, far(mask), far(tally), *[grads[k] for k in range(n_t)]),
+        [VM] * 3 + [ANY] * 2 + [VM] * n_t,
+        [ANY, VM],
+        scratch=[
+            pltpu.VMEM((B, width), F32),
+            pltpu.SemaphoreType.DMA((n_t,)),
+            pltpu.SMEM((n_r,), jnp.int32),
+            pltpu.SMEM((n_r,), jnp.int32),
+            pltpu.SemaphoreType.DMA((2,)),
+        ],
+        flops=6 * B * B * width,
+        nbytes=B * width * 10,
+        name="new_momentums",
+    )
+    places = call(
+        functools.partial(places_body, keep),
+        [near((B, blocks * half * keep))] * 4,
+        (shares, small, bundles),
+        [VM] * 3,
+        [VM] * 4,
+        name="places",
+    )
+    input_grad = call(
+        functools.partial(input_grad_body, n_t, n_r, cp),
+        jax.ShapeDtypeStruct((tok, cols), BF16),
+        (exp, bundles, *parts),
+        [VM] * (2 + n_t),
+        VM,
+        scratch=[pltpu.VMEM((n_t * B, cols), BF16)],
+        flops=2 * tok * n_t * B * cols,
+        nbytes=(n_t * B * cols + tok * cols) * 2,
+        name="input_grads",
+    )
+
     ships = [ship] + [swap(ship, 2 * i) for i in range(1, half)]
-    other_own = swap(ship, 1)
-    others = call(
-        functools.partial(join_body, half - 1),
-        near((half - 1, keep, width)),
-        (other_own, *ships[1:], far(new), far(input_grad), places[0]),
-        [ANY] + [VM] * (half - 1) + [ANY] * 3,
-        VM,
+    two = call(
+        join_body,
+        near((2, keep, width)),
+        (*beside, far(new), far(input_grad), places[0]),
+        [VM] * 2 + [ANY] * 3,
+        VM,
+        flops=1 << 30,
         name="join_kept",
     )
-    other = swap(others, 1)
+    other_two = swap(two, 1)
+    relayed = lax.ppermute(direct, "replica", [(r, r ^ 1) for r in range(n_r) if r % 2])
     half_sum = call(
         half_update_body,
         near((groups * B, G), F32),
-        (*places[:2], ship, others),
-        [VM] * 4,
+        (*places[:2], ship, two, other_own),
+        [VM] * 5,
         VM,
         name="half_updates",
     )
@@ -500,8 +567,8 @@
     update = call(
         functools.partial(update_body, chunk),
         jax.ShapeDtypeStruct((B, width), F32),
-        (half_sum, *places[2:], other_own, other),
-        [VM] * 5,
+        (half_sum, *places[2:], other_two, direct, relayed),
+        [VM] * 6,
         ANY,
         scratch=[
             pltpu.VMEM((B, width), F32),

time: 35.7 us -> 38.6 us (1.081)
  starting transfers between devices: 14.2 us -> 17.1 us
    ppermute x0 -> x2, starting transfers between devices: none -> 1.95 us  [the longest x1 1.28 us: per_device(): lax.ppermute(direct, 'replica', [(r, r ^ 1) for r in range(n_r) if r % 2])]
    ppermute x5 -> x4, waiting for transfers between devices: 1.55 us -> 0.01 us  [swap(): return lax.ppermute(x, 'replica', [(i, i ^ m) for i in range(n_r)])]
    ppermute x0 -> x2, waiting for transfers between devices: none -> 1.49 us  [the longest x1 1.48 us: per_device(): lax.ppermute(direct, 'replica', [(r, r ^ 1) for r in range(n_r) if r % 2])]
    ppermute x5 -> x4, starting transfers between devices: 3.63 us -> 4.51 us  [swap(): return lax.ppermute(x, 'replica', [(i, i ^ m) for i in range(n_r)])]
    pallas_call x15 -> x16, Pallas kernels: 8.47 us -> 8.5 us  [call(): pl.pallas_call(body, out_shape=out_shape, in_specs=in_specs, out_specs=ou...]
  transfers between devices with their start and end apart: 11 -> 12, of which waited for: 3 -> 2; matrix products, arithmetic and copies ran while one was open for 0% -> 0% of each run, Pallas kernels for 16% -> 14%
where the time goes in v23:
time: 38.6 us; the launch traced here: 38.3 us
  starting transfers between devices  17.1 us (44%)
  blocking collectives  9.87 us (26%)
  Pallas kernels  8.5 us (22%)
  waiting for transfers between devices  2 us (5%)
  between operations  0.82 us (2%)
    ppermute x6, starting transfers between devices, trade(): return lax.ppermute(x, 'tensor', [(i, i ^ k) for i in range(n_t)])  10.6 us
    all_gather x1, blocking collectives, per_device(): bundles = lax.all_gather(bundle, 'replica', axis=0)  9.87 us
    pallas_call x16, Pallas kernels, call(): pl.pallas_call(body, out_shape=out_shape, in_specs=in_specs, out_specs=ou...  8.5 us
    ppermute x4, starting transfers between devices, swap(): return lax.ppermute(x, 'replica', [(i, i ^ m) for i in range(n_r)])  4.51 us
    ppermute x1, waiting for transfers between devices, per_device(): lax.ppermute(direct, 'replica', [(r, r ^ 1) for r in range(n_r) if r % 2])  1.48 us
    ppermute x1, starting transfers between devices, per_device(): lax.ppermute(direct, 'replica', [(r, r ^ 1) for r in range(n_r) if r % 2])  1.28 us
  transfers between devices with their start and end apart: 12, of which 2 were waited for; matrix products, arithmetic and copies ran while one was open for 0% of the time, Pallas kernels for 14%

profile of v23, /device:TPU:0, one launch (start us, length us, event | category | flops | bytes accessed | tf_op | source)
XLA Modules:
  0.0 38.3 jit_solution(986141397345528414)
XLA Ops:
  0.6 1.2 %up_grads.1 = (bf16[64,128]{1,0:T(8,128)(2,1)S(1)}, bf16[144,128]{1,0:T(8,128)(2,1)S(1)}, bf16[144,128]{1,0:T(8,128)(2,1)S(1)}, bf16[144,128]{1,0:T(8,128)(2,1)S...) custom-call(bf16[64,128]{1,0:T(8,128)(2,1)} %bitcast.15, ...), custom_call_target="tpu_custom_call" | custom-call | bytes 819200 | tf_op jit(solution)/shard_map/up_grads/pallas_call | solution.py:88
  1.8 4.1 %collective-permute-start.1 = (bf16[144,128]{1,0:T(8,128)(2,1)S(1)}, bf16[144,128]{1,0:T(8,128)(2,1)S(1)}, u32[]{:S(2)}, u32[]{:S(2)}) collective-permute-start(bf16[144,128]{1,0:T(8,128)(2,1)S(1)} %get-tuple-element.28), channel_id=1, source_target_pairs={{0,2},{1,3},{2,0},{3,1},{4,6},{5,7},{6,4},{7,5},{8,10},{9,11},{10,... | collective-permute-start | bytes 110600 | tf_op jit(solution)/shard_map/ppermute | solution.py:363
  5.9 1.6 %collective-permute-start = (bf16[144,128]{1,0:T(8,128)(2,1)S(1)}, bf16[144,128]{1,0:T(8,128)(2,1)S(1)}, u32[]{:S(2)}, u32[]{:S(2)}) collective-permute-start(bf16[144,128]{1,0:T(8,128)(2,1)S(1)} %get-tuple-element.25), channel_id=1, source_target_pairs={{0,1},{1,0},{2,3},{3,2},{4,5},{5,4},{6,7},{7,6},{8,9},{9,8},{10,11... | collective-permute-start | bytes 110600 | tf_op jit(solution)/shard_map/ppermute | solution.py:363
  7.5 0.0 collective-permute-start.2
  7.5 0.4 own_rows.1.after.a_ref
  7.8 0.5 %collective-permute-done.1.refs_1_.refs_2_.refs_0_ = bf16[144,128]{1,0:T(8,128)(2,1)S(1)} collective-permute-done((bf16[144,128]{1,0:T(8,128)(2,1)S(1)}, bf16[144,128]{1,0:T(8,128)(2,1)S(1)}, u32[]{:S(2)}, u32[]{:S(2)}) %collective-permute-start.1) | collective-permute-done | bytes 36896 | tf_op jit(solution)/shard_map/ppermute | solution.py:363
  8.3 0.2 weight_grads.5
  8.5 0.0 copy-start
  8.5 0.0 copy-start.2
  8.5 2.7 %collective-permute-start.5 = (bf16[64,1280]{1,0:T(8,128)(2,1)S(1)}, bf16[64,1280]{1,0:T(8,128)(2,1)S(1)}, u32[]{:S(2)}, u32[]{:S(2)}) collective-permute-start(bf16[64,1280]{1,0:T(8,128)(2,1)S(1)} %weight_grads.5), channel_id=1, source_target_pairs={{0,2},{1,3},{2,0},{3,1},{4,6},{5,7},{6,4},{7,5},{8,10},{9,11},{10,... | collective-permute-start | bytes 491528 | tf_op jit(solution)/shard_map/ppermute | solution.py:363
  11.3 0.0 collective-permute-done.refs_0_.refs_1_
  11.3 0.2 weight_grads.3
  11.5 2.1 %collective-permute-start.4 = (bf16[64,1280]{1,0:T(8,128)(2,1)S(1)}, bf16[64,1280]{1,0:T(8,128)(2,1)S(1)}, u32[]{:S(2)}, u32[]{:S(2)}) collective-permute-start(bf16[64,1280]{1,0:T(8,128)(2,1)S(1)} %get-tuple-element.27.after), channel_id=1, source_target_pairs={{0,1},{1,0},{2,3},{3,2},{4,5},{5,4},{6,7},{7,6},{8,9},{9,8},{10,11... | collective-permute-start | bytes 491528 | tf_op jit(solution)/shard_map/ppermute | solution.py:363
  13.6 0.0 collective-permute-done.2.refs_2_.refs_3_.refs_0_
  13.6 0.2 weight_grads.4
  13.8 0.1 collective-permute-start.3
  13.9 9.9 %all-gather = bf16[2048,128]{1,0:T(8,128)(2,1)S(1)} all-gather(bf16[256,128]{1,0:T(8,128)(2,1)S(1)} %bundle.1), channel_id=2, replica_groups=mesh['replica'=8,'tensor'=4] {'replica'}, dimensions={0}, use_global_device_ids=true | all-gather | bytes 589824 | tf_op jit(solution)/shard_map/all_gather | solution.py:427
  23.8 0.0 collective-permute-done.5.refs_2_
  23.8 0.0 collective-permute-done.4.refs_1_
  23.8 0.0 copy-done
  23.8 0.0 copy-done.2
  23.8 0.7 %kept_rows.2 = (bf16[8,5120]{1,0:T(8,128)(2,1)S(1)}, f32[8,5120]{1,0:T(8,128)S(1)}) custom-call(f32[64,5120]{1,0:T(8,128)S(1)} %bitcast.12, bf16[1280,128]{1,0:T(8,128)(2,1)S(1)} %own_rows.1.after.a_ref, bf16[1024,256]{1,0:T(8,128)(2,1)S(1)} %copy-done.2, bf16[8,256,128]{2,1,0:T(8,128)(2,1)S(1)} %bitcast.8, f32[64,1280]{1,0:T(8,128)S(1)} %get-tuple-element.30.refs_0_, ...), custom_call_target="tpu_custom_call" | custom-call | flops 94371840 | bytes 1474560 | tf_op jit(solution)/shard_map/kept_rows/pallas_call | solution.py:88
  24.5 0.0 collective-permute-done.3.refs_0_.refs_3_
  24.5 0.0 copy-start.1
  24.5 0.5 %kept_rows.3 = (bf16[8,5120]{1,0:T(8,128)(2,1)S(1)}, f32[8,5120]{1,0:T(8,128)S(1)}) custom-call(f32[64,5120]{1,0:T(8,128)S(1)} %bitcast.13, bf16[1280,128]{1,0:T(8,128)(2,1)S(1)} %own_rows.1.after.a_ref, bf16[1024,256]{1,0:T(8,128)(2,1)S(1)} %copy-done.2, bf16[8,256,128]{2,1,0:T(8,128)(2,1)S(1)} %bitcast.9, ...), custom_call_target="tpu_custom_call", output_to_operand_aliasing={{0}: (5, {}), {1}: (6, {})} | custom-call | flops 31457280 | bytes 491520 | tf_op jit(solution)/shard_map/kept_rows/pallas_call | solution.py:88
  25.0 0.4 %collective-permute-start.8 = (bf16[8,5120]{1,0:T(8,128)(2,1)S(1)}, bf16[8,5120]{1,0:T(8,128)(2,1)S(1)}, u32[]{:S(2)}, u32[]{:S(2)}) collective-permute-start(bf16[8,5120]{1,0:T(8,128)(2,1)S(1)} %get-tuple-element.38.own.refs_0_), channel_id=1, source_target_pairs={{0,4},{4,0},{8,12},{12,8},{16,20},{20,16},{24,28},{28,24},{1,5},{5... | collective-permute-start | bytes 245768 | tf_op jit(solution)/shard_map/ppermute | solution.py:368
  25.5 1.5 %collective-permute-start.7 = (bf16[8,5120]{1,0:T(8,128)(2,1)S(1)}, bf16[8,5120]{1,0:T(8,128)(2,1)S(1)}, u32[]{:S(2)}, u32[]{:S(2)}) collective-permute-start(bf16[8,5120]{1,0:T(8,128)(2,1)S(1)} %get-tuple-element.38.own.refs_0_), channel_id=1, source_target_pairs={{0,16},{4,20},{8,24},{12,28},{16,0},{20,4},{24,8},{28,12},{1,17},{... | collective-permute-start | bytes 245768 | tf_op jit(solution)/shard_map/ppermute | solution.py:368
  26.9 0.5 %collective-permute-start.6 = (bf16[8,5120]{1,0:T(8,128)(2,1)S(1)}, bf16[8,5120]{1,0:T(8,128)(2,1)S(1)}, u32[]{:S(2)}, u32[]{:S(2)}) collective-permute-start(bf16[8,5120]{1,0:T(8,128)(2,1)S(1)} %get-tuple-element.38.own.refs_0_), channel_id=1, source_target_pairs={{0,8},{4,12},{8,0},{12,4},{16,24},{20,28},{24,16},{28,20},{1,9},{5... | collective-permute-start | bytes 245768 | tf_op jit(solution)/shard_map/ppermute | solution.py:368
  27.5 0.0 collective-permute-done.8.other_own.refs_1_
  27.5 0.7 %collective-permute-start.10 = (bf16[2,8,5120]{2,1,0:T(8,128)(2,1)S(1)}, bf16[2,8,5120]{2,1,0:T(8,128)(2,1)S(1)}, u32[]{:S(2)}, u32[]{:S(2)}) collective-permute-start(bf16[2,8,5120]{2,1,0:T(8,128)(2,1)S(1)} %join_cores.1), channel_id=1, source_target_pairs={{4,28},{12,20},{20,12},{28,4},{5,29},{13,21},{21,13},{29,5},{6,30}... | collective-permute-start | bytes 491528 | tf_op jit(solution)/shard_map/ppermute | solution.py:499
  28.2 0.0 copy-done.1
  28.2 1.0 %input_grads.1.refs_3_ = bf16[128,1280]{1,0:T(8,128)(2,1)} custom-call(bf16[64,5120]{1,0:T(8,128)(2,1)S(1)} %copy-done.1, bf16[8,256,128]{2,1,0:T(8,128)(2,1)S(1)} %bitcast.10, bf16[64,128]{1,0:T(8,128)(2,1)S(1)} %get-tuple-element.26.refs_1_.refs_0_, bf16[144,128]{1,0:T(8,128)(2,1)S(1)} %collective-permute-done.refs_0_.refs_1_, ...), custom_call_target="tpu_custom_call" | custom-call | flops 83886080 | bytes 983040 | tf_op jit(solution)/shard_map/input_grads/pallas_call | solution.py:88
  29.2 0.4 %own_columns.1.p_ref = bf16[64,2560]{1,0:T(8,128)(2,1)S(1)} custom-call(s32[8,80]{1,0:T(8,128)S(1)} %get-tuple-element.23.lines, bf16[128,256]{1,0:T(8,128)(2,1)S(1)} %get-tuple-element.24.small, f32[8,5120]{1,0:T(8,128)S(1)} %get-tuple-element.33.after.q), custom_call_target="tpu_custom_call" | custom-call | tf_op jit(solution)/shard_map/own_columns/pallas_call | solution.py:88
  29.6 1.3 %new_momentums.1 = (f32[64,5120]{1,0:T(8,128)}, f32[2,8,128]{2,1,0:T(8,128)S(1)}) custom-call(f32[64,5120]{1,0:T(8,128)S(1)} %bitcast.14, bf16[64,2560]{1,0:T(8,128)(2,1)S(1)} %own_columns.1.p_ref, f32[8,5120]{1,0:T(8,128)S(1)} %get-tuple-element.33.after.q, s32[8]{0:T(128)} %mask.1, s32[8]{0:T(128)} %tally.1, f32[64,1280]{1,0:T(8,128)S(1)} %get-tuple-element.30.refs_0_, ...), custom_call_target="tpu_custom_call" | custom-call | flops 125829120 | bytes 3276800 | tf_op jit(solution)/shard_map/new_momentums/pallas_call | solution.py:88
  31.0 0.6 %places.1 = (bf16[64,2560]{1,0:T(8,128)(2,1)S(1)}, bf16[64,2560]{1,0:T(8,128)(2,1)S(1)}, bf16[64,2560]{1,0:T(8,128)(2,1)S(1)}, bf16[64,2560]{1,0:T(8,128)(2,1)S(1)}) custom-call(f32[2,8,128]{2,1,0:T(8,128)S(1)} %get-tuple-element.35.w_ref, bf16[128,256]{1,0:T(8,128)(2,1)S(1)} %get-tuple-element.24.small, bf16[8,256,128]{2,1,0:T(8,128)(2,1)S(1)} %bitcast.11), custom_call_target="tpu_custom_call" | custom-call | tf_op jit(solution)/shard_map/places/pallas_call | solution.py:88
  31.6 0.0 collective-permute-done.7.refs_1_
  31.6 0.0 collective-permute-done.6.refs_0_
  31.6 2.1 %collective-permute-start.9 = (bf16[2,8,5120]{2,1,0:T(8,128)(2,1)S(1)}, bf16[2,8,5120]{2,1,0:T(8,128)(2,1)S(1)}, u32[]{:S(2)}, u32[]{:S(2)}) collective-permute-start(bf16[2,8,5120]{2,1,0:T(8,128)(2,1)S(1)} %join_kept.1.near_two), channel_id=1, source_target_pairs={{0,4},{4,0},{8,12},{12,8},{16,20},{20,16},{24,28},{28,24},{1,5},{5... | collective-permute-start | bytes 491528 | tf_op jit(solution)/shard_map/ppermute | solution.py:368
  33.7 0.0 collective-permute-done.10.direct
  33.7 1.3 %collective-permute-start.11 = (bf16[2,8,5120]{2,1,0:T(8,128)(2,1)S(1)}, bf16[2,8,5120]{2,1,0:T(8,128)(2,1)S(1)}, u32[]{:S(2)}, u32[]{:S(2)}) collective-permute-start(bf16[2,8,5120]{2,1,0:T(8,128)(2,1)S(1)} %collective-permute-done.10.direct), channel_id=1, source_target_pairs={{4,0},{12,8},{20,16},{28,24},{5,1},{13,9},{21,17},{29,25},{6,2},{1... | collective-permute-start | bytes 491528 | tf_op jit(solution)/shard_map/ppermute | solution.py:557
  35.0 0.5 %half_updates.1.half_sum = f32[1280,256]{1,0:T(8,128)S(1)} custom-call(bf16[64,2560]{1,0:T(8,128)(2,1)S(1)} %get-tuple-element.36.refs_4_.p_hi, bf16[64,2560]{1,0:T(8,128)(2,1)S(1)} %get-tuple-element.37.p_lo, bf16[8,5120]{1,0:T(8,128)(2,1)S(1)} %get-tuple-element.38.own.refs_0_, bf16[2,8,5120]{2,1,0:T(8,128)(2,1)S(1)} %join_kept.1.near_two, ...), custom_call_target="tpu_custom_call" | custom-call | tf_op jit(solution)/shard_map/half_updates/pallas_call | solution.py:88
  35.5 0.0 collective-permute-done.9.near_two
  35.5 1.5 %collective-permute-done.11.relayed = bf16[2,8,5120]{2,1,0:T(8,128)(2,1)S(1)} collective-permute-done((bf16[2,8,5120]{2,1,0:T(8,128)(2,1)S(1)}, bf16[2,8,5120]{2,1,0:T(8,128)(2,1)S(1)}, u32[]{:S(2)}, u32[]{:S(2)}) %collective-permute-start.11) | collective-permute-done | bytes 163872 | tf_op jit(solution)/shard_map/ppermute | solution.py:557
  37.0 1.3 %updates.1 = f32[64,5120]{1,0:T(8,128)} custom-call(f32[1280,256]{1,0:T(8,128)S(1)} %half_updates.1.half_sum, bf16[64,2560]{1,0:T(8,128)(2,1)S(1)} %get-tuple-element.39.p_hi, bf16[64,2560]{1,0:T(8,128)(2,1)S(1)} %get-tuple-element.40.p_lo, bf16[2,8,5120]{2,1,0:T(8,128)(2,1)S(1)} %collective-permute-done.9.near_two, ...), custom_call_target="tpu_custom_call" | custom-call | flops 671088640 | bytes 2621440 | tf_op jit(solution)/shard_map/updates/pallas_call | solution.py:88
  (3 shorter events, 0.0 us)
Async XLA Ops:
  1.8 6.5 %collective-permute-start.1 = (bf16[144,128]{1,0:T(8,128)(2,1)S(1)}, bf16[144,128]{1,0:T(8,128)(2,1)S(1)}, u32[]{:S(2)}, u32[]{:S(2)}) collective-permute-start(bf16[144,128]{1,0:T(8,128)(2,1)S(1)} %get-tuple-element.28), channel_id=1, source_target_pairs={{0,2},{1,3},{2,0},{3,1},{4,6},{5,7},{6,4},{7,5},{8,10},{9,11},{10,... | collective-permute-start | bytes 110600 | tf_op jit(solution)/shard_map/ppermute | solution.py:363
  5.9 5.4 %collective-permute-start = (bf16[144,128]{1,0:T(8,128)(2,1)S(1)}, bf16[144,128]{1,0:T(8,128)(2,1)S(1)}, u32[]{:S(2)}, u32[]{:S(2)}) collective-permute-start(bf16[144,128]{1,0:T(8,128)(2,1)S(1)} %get-tuple-element.25), channel_id=1, source_target_pairs={{0,1},{1,0},{2,3},{3,2},{4,5},{5,4},{6,7},{7,6},{8,9},{9,8},{10,11... | collective-permute-start | bytes 110600 | tf_op jit(solution)/shard_map/ppermute | solution.py:363
  7.5 6.2 %collective-permute-start.2 = (bf16[144,128]{1,0:T(8,128)(2,1)S(1)}, bf16[144,128]{1,0:T(8,128)(2,1)S(1)}, u32[]{:S(2)}, u32[]{:S(2)}) collective-permute-start(bf16[144,128]{1,0:T(8,128)(2,1)S(1)} %get-tuple-element.29), channel_id=1, source_target_pairs={{0,3},{1,2},{2,1},{3,0},{4,7},{5,6},{6,5},{7,4},{8,11},{9,10},{10,... | collective-permute-start | bytes 110600 | tf_op jit(solution)/shard_map/ppermute | solution.py:363
  8.5 15.3 %copy-start = (f32[1,64,5120]{2,1,0:T(8,128)S(1)}, f32[1,64,5120]{2,1,0:T(8,128)}, u32[]{:S(2)}) copy-start(f32[1,64,5120]{2,1,0:T(8,128)} %param.14) | copy-start | bytes 3932164
  8.5 15.3 %copy-start.2 = (bf16[1024,256]{1,0:T(8,128)(2,1)S(1)}, bf16[1024,256]{1,0:T(8,128)(2,1)}, u32[]{:S(2)}) copy-start(bf16[1024,256]{1,0:T(8,128)(2,1)} %constant.4.clone.tab) | copy-start | bytes 1572868
  8.5 15.3 %collective-permute-start.5 = (bf16[64,1280]{1,0:T(8,128)(2,1)S(1)}, bf16[64,1280]{1,0:T(8,128)(2,1)S(1)}, u32[]{:S(2)}, u32[]{:S(2)}) collective-permute-start(bf16[64,1280]{1,0:T(8,128)(2,1)S(1)} %weight_grads.5), channel_id=1, source_target_pairs={{0,2},{1,3},{2,0},{3,1},{4,6},{5,7},{6,4},{7,5},{8,10},{9,11},{10,... | collective-permute-start | bytes 491528 | tf_op jit(solution)/shard_map/ppermute | solution.py:363
  11.5 12.3 %collective-permute-start.4 = (bf16[64,1280]{1,0:T(8,128)(2,1)S(1)}, bf16[64,1280]{1,0:T(8,128)(2,1)S(1)}, u32[]{:S(2)}, u32[]{:S(2)}) collective-permute-start(bf16[64,1280]{1,0:T(8,128)(2,1)S(1)} %get-tuple-element.27.after), channel_id=1, source_target_pairs={{0,1},{1,0},{2,3},{3,2},{4,5},{5,4},{6,7},{7,6},{8,9},{9,8},{10,11... | collective-permute-start | bytes 491528 | tf_op jit(solution)/shard_map/ppermute | solution.py:363
  13.8 10.7 %collective-permute-start.3 = (bf16[64,1280]{1,0:T(8,128)(2,1)S(1)}, bf16[64,1280]{1,0:T(8,128)(2,1)S(1)}, u32[]{:S(2)}, u32[]{:S(2)}) collective-permute-start(bf16[64,1280]{1,0:T(8,128)(2,1)S(1)} %weight_grads.4), channel_id=1, source_target_pairs={{0,3},{1,2},{2,1},{3,0},{4,7},{5,6},{6,5},{7,4},{8,11},{9,10},{10,... | collective-permute-start | bytes 491528 | tf_op jit(solution)/shard_map/ppermute | solution.py:363
  24.5 3.6 %copy-start.1 = (bf16[64,5120]{1,0:T(8,128)(2,1)S(1)}, bf16[64,5120]{1,0:T(8,128)(2,1)}, u32[]{:S(2)}) copy-start(bf16[64,5120]{1,0:T(8,128)(2,1)} %exp_ref.3) | copy-start | bytes 1966084
  25.0 2.4 %collective-permute-start.8 = (bf16[8,5120]{1,0:T(8,128)(2,1)S(1)}, bf16[8,5120]{1,0:T(8,128)(2,1)S(1)}, u32[]{:S(2)}, u32[]{:S(2)}) collective-permute-start(bf16[8,5120]{1,0:T(8,128)(2,1)S(1)} %get-tuple-element.38.own.refs_0_), channel_id=1, source_target_pairs={{0,4},{4,0},{8,12},{12,8},{16,20},{20,16},{24,28},{28,24},{1,5},{5... | collective-permute-start | bytes 245768 | tf_op jit(solution)/shard_map/ppermute | solution.py:368
  25.5 6.1 %collective-permute-start.7 = (bf16[8,5120]{1,0:T(8,128)(2,1)S(1)}, bf16[8,5120]{1,0:T(8,128)(2,1)S(1)}, u32[]{:S(2)}, u32[]{:S(2)}) collective-permute-start(bf16[8,5120]{1,0:T(8,128)(2,1)S(1)} %get-tuple-element.38.own.refs_0_), channel_id=1, source_target_pairs={{0,16},{4,20},{8,24},{12,28},{16,0},{20,4},{24,8},{28,12},{1,17},{... | collective-permute-start | bytes 245768 | tf_op jit(solution)/shard_map/ppermute | solution.py:368
  26.9 4.6 %collective-permute-start.6 = (bf16[8,5120]{1,0:T(8,128)(2,1)S(1)}, bf16[8,5120]{1,0:T(8,128)(2,1)S(1)}, u32[]{:S(2)}, u32[]{:S(2)}) collective-permute-start(bf16[8,5120]{1,0:T(8,128)(2,1)S(1)} %get-tuple-element.38.own.refs_0_), channel_id=1, source_target_pairs={{0,8},{4,12},{8,0},{12,4},{16,24},{20,28},{24,16},{28,20},{1,9},{5... | collective-permute-start | bytes 245768 | tf_op jit(solution)/shard_map/ppermute | solution.py:368
  27.5 6.2 %collective-permute-start.10 = (bf16[2,8,5120]{2,1,0:T(8,128)(2,1)S(1)}, bf16[2,8,5120]{2,1,0:T(8,128)(2,1)S(1)}, u32[]{:S(2)}, u32[]{:S(2)}) collective-permute-start(bf16[2,8,5120]{2,1,0:T(8,128)(2,1)S(1)} %join_cores.1), channel_id=1, source_target_pairs={{4,28},{12,20},{20,12},{28,4},{5,29},{13,21},{21,13},{29,5},{6,30}... | collective-permute-start | bytes 491528 | tf_op jit(solution)/shard_map/ppermute | solution.py:499
  31.6 3.9 %collective-permute-start.9 = (bf16[2,8,5120]{2,1,0:T(8,128)(2,1)S(1)}, bf16[2,8,5120]{2,1,0:T(8,128)(2,1)S(1)}, u32[]{:S(2)}, u32[]{:S(2)}) collective-permute-start(bf16[2,8,5120]{2,1,0:T(8,128)(2,1)S(1)} %join_kept.1.near_two), channel_id=1, source_target_pairs={{0,4},{4,0},{8,12},{12,8},{16,20},{20,16},{24,28},{28,24},{1,5},{5... | collective-permute-start | bytes 491528 | tf_op jit(solution)/shard_map/ppermute | solution.py:368
  33.7 3.3 %collective-permute-start.11 = (bf16[2,8,5120]{2,1,0:T(8,128)(2,1)S(1)}, bf16[2,8,5120]{2,1,0:T(8,128)(2,1)S(1)}, u32[]{:S(2)}, u32[]{:S(2)}) collective-permute-start(bf16[2,8,5120]{2,1,0:T(8,128)(2,1)S(1)} %collective-permute-done.10.direct), channel_id=1, source_target_pairs={{4,0},{12,8},{20,16},{28,24},{5,1},{13,9},{21,17},{29,25},{6,2},{1... | collective-permute-start | bytes 491528 | tf_op jit(solution)/shard_map/ppermute | solution.py:557

commit v24 on v20

--- a/solution.py
+++ b/solution.py
@@ -178,18 +178,12 @@
         p_ref[:, g * 2 * B : (g + 1) * 2 * B] = p.astype(BF16)
 
 
-def kept_body(ks, n_t, keep, vel, a_ref, tab, after, *refs):
-    keep_rows(ks, n_t, keep, vel, a_ref, tab, refs[: len(ks)], *refs[-2:])
-
-
-def keep_rows(ks, n_t, keep, vel, a_ref, tab, grads, send_ref, own_ref):
+def selected(ks, n_t, keep, vel, a_ref, grads):
     cols = grads[0].shape[1]
-    ng = cols // G
     lane_block = lax.broadcasted_iota(jnp.int32, (keep, G), 1) // B
-    sel = []
     for n, k in enumerate(ks):
         c0 = (lax.axis_index("tensor") ^ k) * cols
-        for i in range(ng):
+        for i in range(cols // G):
             at = pl.multiple_of(c0 + i * G, G)
             moment = momentum_decay * vel[:, pl.ds(at, G)] + grads[n][:, i * G : (i + 1) * G].astype(F32)
             hi, lo = split(moment)
@@ -198,17 +192,34 @@
             got = y[:keep]
             for j in range(1, G // B):
                 got = jnp.where(lane_block == j, y[j * keep : (j + 1) * keep], got)
-            sel.append(got)
-    hi, lo = split(jnp.concatenate(sel, axis=0))
-    n = len(ks) * ng * keep
+            yield at, got
+
+
+def select_body(ks, n_t, keep, vel, a_ref, after, *refs):
+    grads, sel_ref = refs[: len(ks)], refs[len(ks)]
+    for at, got in selected(ks, n_t, keep, vel, a_ref, grads):
+        sel_ref[:, pl.ds(at, G)] = got
+
+
+def kept_body(before, ks, n_t, keep, vel, a_ref, tab, sel_ref, *refs):
+    grads, (send_ref, own_ref) = refs[: len(ks)], refs[len(ks) :]
+    cols = grads[0].shape[1]
+    cells = []
+    for k in before:
+        c0 = (lax.axis_index("tensor") ^ k) * cols
+        for i in range(cols // G):
+            at = pl.multiple_of(c0 + i * G, G)
+            cells.append((at, sel_ref[:, pl.ds(at, G)]))
+    cells += list(selected(ks, n_t, keep, vel, a_ref, grads))
+    n = len(cells) * keep
+    hi, lo = split(jnp.concatenate([got for _, got in cells], axis=0))
     y = dot(jnp.concatenate([hi, lo], axis=0), fwd(tab, 0))
     kept = (y[:n] + y[n:] + dot(hi, fwd(tab, 1))).astype(BF16)
     q = dot(kept, inv(tab, 0)) + dot(kept, inv(tab, 1))
-    for n, k in enumerate(ks):
-        c0 = pl.multiple_of((lax.axis_index("tensor") ^ k) * cols, G)
-        part = jnp.concatenate([q[(n * ng + i) * keep : (n * ng + i + 1) * keep] for i in range(ng)], axis=1)
-        own_ref[:, pl.ds(c0, cols)] = part
-        send_ref[:, pl.ds(c0, cols)] = part.astype(BF16)
+    for i, (at, _) in enumerate(cells):
+        part = q[i * keep : (i + 1) * keep]
+        own_ref[:, pl.ds(at, G)] = part
+        send_ref[:, pl.ds(at, G)] = part.astype(BF16)
 
 
 def return_body(n_t, keep, vel, p_ref, q, mask, tally, *refs):
@@ -411,21 +422,27 @@
     )
     bundles = lax.all_gather(bundle, "replica", axis=0)
 
-    rows = []
-    for ks in ([k for k in range(n_t) if k != n_t - 1], [n_t - 1]):
-        n = len(ks)
-        rows = call(
-            functools.partial(kept_body, ks, n_t, keep),
-            [near((keep, width)), near((keep, width), F32)],
-            (vel[0], a_own, tab, bundles, *[grads[k] for k in ks], *rows),
-            [VM] * 3 + [ANY] + [VM] * (n + len(rows)),
-            [VM] * 2,
-            flops=6 * B * B * cols * n,
-            nbytes=B * cols * 6 * n,
-            name="kept_rows",
-            alias={4 + n: 0, 5 + n: 1} if rows else {},
-        )
-    ship, q_own = rows
+    before, last = [k for k in range(n_t) if k != n_t - 1], [n_t - 1]
+    sel = call(
+        functools.partial(select_body, before, n_t, keep),
+        near((keep, width), F32),
+        (vel[0], a_own, bundles, *[grads[k] for k in before]),
+        [VM] * 2 + [ANY] + [VM] * len(before),
+        VM,
+        flops=6 * B * B * cols * len(before),
+        nbytes=B * cols * 6 * len(before),
+        name="selected_rows",
+    )
+    ship, q_own = call(
+        functools.partial(kept_body, before, last, n_t, keep),
+        [near((keep, width)), near((keep, width), F32)],
+        (vel[0], a_own, tab, sel, *[grads[k] for k in last]),
+        [VM] * (4 + len(last)),
+        [VM] * 2,
+        flops=6 * B * B * cols,
+        nbytes=B * cols * 6,
+        name="kept_rows",
+    )
 
     new, shares = call(
         functools.partial(return_body, n_t, keep),

time: 35.7 us -> 36.1 us (1.011)
  local copies, waits for them, and re-layouts: 0.02 us -> 0.63 us
    unnamed x6, local copies, waits for them, and re-layouts: 0.02 us -> 0.63 us
  transfers between devices with their start and end apart: 11 -> 11, of which waited for: 3 -> 3; matrix products, arithmetic and copies ran while one was open for 0% -> 0% of each run, Pallas kernels for 15% -> 14%
where the time goes in v24:
time: 36.1 us; the launch traced here: 35.8 us
  starting transfers between devices  14.2 us (39%)
  blocking collectives  9.87 us (27%)
  Pallas kernels  8.05 us (22%)
  waiting for transfers between devices  2.26 us (6%)
  between operations  0.77 us (2%)
  local copies, waits for them, and re-layouts  0.63 us (2%)
    ppermute x6, starting transfers between devices, trade(): return lax.ppermute(x, 'tensor', [(i, i ^ k) for i in range(n_t)])  10.6 us
    all_gather x1, blocking collectives, per_device(): bundles = lax.all_gather(bundle, 'replica', axis=0)  9.87 us
    pallas_call x14, Pallas kernels, call(): pl.pallas_call(body, out_shape=out_shape, in_specs=in_specs, out_specs=ou...  8.05 us
    ppermute x5, starting transfers between devices, swap(): return lax.ppermute(x, 'replica', [(i, i ^ m) for i in range(n_r)])  3.64 us
    ppermute x5, waiting for transfers between devices, swap(): return lax.ppermute(x, 'replica', [(i, i ^ m) for i in range(n_r)])  1.93 us
  transfers between devices with their start and end apart: 11, of which 3 were waited for; matrix products, arithmetic and copies ran while one was open for 0% of the time, Pallas kernels for 14%

profile of v24, /device:TPU:0, one launch (start us, length us, event | category | flops | bytes accessed | tf_op | source)
XLA Modules:
  0.0 35.8 jit_solution(1117289021149279339)
XLA Ops:
  0.6 1.2 %up_grads.1 = (bf16[64,128]{1,0:T(8,128)(2,1)S(1)}, bf16[144,128]{1,0:T(8,128)(2,1)S(1)}, bf16[144,128]{1,0:T(8,128)(2,1)S(1)}, bf16[144,128]{1,0:T(8,128)(2,1)S...) custom-call(bf16[64,128]{1,0:T(8,128)(2,1)} %bitcast.15, ...), custom_call_target="tpu_custom_call" | custom-call | bytes 819200 | tf_op jit(solution)/shard_map/up_grads/pallas_call | solution.py:81
  1.8 4.1 %collective-permute-start.1 = (bf16[144,128]{1,0:T(8,128)(2,1)S(1)}, bf16[144,128]{1,0:T(8,128)(2,1)S(1)}, u32[]{:S(2)}, u32[]{:S(2)}) collective-permute-start(bf16[144,128]{1,0:T(8,128)(2,1)S(1)} %get-tuple-element.29), channel_id=1, source_target_pairs={{0,2},{1,3},{2,0},{3,1},{4,6},{5,7},{6,4},{7,5},{8,10},{9,11},{10,... | collective-permute-start | bytes 110600 | tf_op jit(solution)/shard_map/ppermute | solution.py:359
  5.9 1.6 %collective-permute-start = (bf16[144,128]{1,0:T(8,128)(2,1)S(1)}, bf16[144,128]{1,0:T(8,128)(2,1)S(1)}, u32[]{:S(2)}, u32[]{:S(2)}) collective-permute-start(bf16[144,128]{1,0:T(8,128)(2,1)S(1)} %get-tuple-element.26), channel_id=1, source_target_pairs={{0,1},{1,0},{2,3},{3,2},{4,5},{5,4},{6,7},{7,6},{8,9},{9,8},{10,11... | collective-permute-start | bytes 110600 | tf_op jit(solution)/shard_map/ppermute | solution.py:359
  7.5 0.0 collective-permute-start.2
  7.5 0.5 %own_places.1 = (bf16[64,2560]{1,0:T(8,128)(2,1)S(1)}, bf16[1280,128]{1,0:T(8,128)(2,1)S(1)}) custom-call(s32[8,80]{1,0:T(8,128)S(1)} %get-tuple-element.23.lines, bf16[128,256]{1,0:T(8,128)(2,1)S(1)} %get-tuple-element.24.small), custom_call_target="tpu_custom_call" | custom-call | tf_op jit(solution)/shard_map/own_places/pallas_call | solution.py:81
  8.0 0.3 collective-permute-done.1.refs_1_.refs_2_.refs_0_
  8.3 0.2 weight_grads.4
  8.5 0.0 copy-start
  8.5 2.7 %collective-permute-start.4 = (bf16[64,1280]{1,0:T(8,128)(2,1)S(1)}, bf16[64,1280]{1,0:T(8,128)(2,1)S(1)}, u32[]{:S(2)}, u32[]{:S(2)}) collective-permute-start(bf16[64,1280]{1,0:T(8,128)(2,1)S(1)} %weight_grads.4), channel_id=1, source_target_pairs={{0,2},{1,3},{2,0},{3,1},{4,6},{5,7},{6,4},{7,5},{8,10},{9,11},{10,... | collective-permute-start | bytes 491528 | tf_op jit(solution)/shard_map/ppermute | solution.py:359
  11.2 0.0 collective-permute-done.refs_0_.refs_1_
  11.2 0.2 weight_grads.3
  11.5 2.1 %collective-permute-start.3 = (bf16[64,1280]{1,0:T(8,128)(2,1)S(1)}, bf16[64,1280]{1,0:T(8,128)(2,1)S(1)}, u32[]{:S(2)}, u32[]{:S(2)}) collective-permute-start(bf16[64,1280]{1,0:T(8,128)(2,1)S(1)} %get-tuple-element.28.after), channel_id=1, source_target_pairs={{0,1},{1,0},{2,3},{3,2},{4,5},{5,4},{6,7},{7,6},{8,9},{9,8},{10,11... | collective-permute-start | bytes 491528 | tf_op jit(solution)/shard_map/ppermute | solution.py:359
  13.6 0.0 collective-permute-done.2.refs_2_.refs_3_.refs_0_
  13.6 0.2 weight_grads.5
  13.8 0.1 collective-permute-start.5
  13.9 9.9 %all-gather = bf16[2048,128]{1,0:T(8,128)(2,1)S(1)} all-gather(bf16[256,128]{1,0:T(8,128)(2,1)S(1)} %bundle.1), channel_id=2, replica_groups=mesh['replica'=8,'tensor'=4] {'replica'}, dimensions={0}, use_global_device_ids=true | all-gather | bytes 589824 | tf_op jit(solution)/shard_map/all_gather | solution.py:423
  23.8 0.0 collective-permute-done.4.refs_2_
  23.8 0.0 collective-permute-done.3.refs_1_
  23.8 0.0 copy-done
  23.8 0.0 copy-start.2
  23.8 0.4 %selected_rows.1.sel_ref = f32[8,5120]{1,0:T(8,128)S(1)} custom-call(f32[64,5120]{1,0:T(8,128)S(1)} %bitcast.8, bf16[1280,128]{1,0:T(8,128)(2,1)S(1)} %get-tuple-element.25.after.a_ref, bf16[8,256,128]{2,1,0:T(8,128)(2,1)S(1)} %bitcast.11, f32[64,1280]{1,0:T(8,128)S(1)} %get-tuple-element.32.refs_0_, bf16[64,1280]{1,0:T(8,128)(2,1)S(1)} %collective-permute-done.3.refs_1_, ...), custom_call_target="tpu_custom_call" | custom-call | flops 94371840 | bytes 1474560 | tf_op jit(solution)/shard_map/selected_rows/pallas_call | solution.py:81
  24.2 0.0 copy-start.1
  24.2 0.0 collective-permute-done.5.refs_0_.refs_3_
  24.2 0.6 %copy-done.2 = bf16[1024,256]{1,0:T(8,128)(2,1)S(1)} copy-done((bf16[1024,256]{1,0:T(8,128)(2,1)S(1)}, bf16[1024,256]{1,0:T(8,128)(2,1)}, u32[]{:S(2)}) %copy-start.2) | copy-done | bytes 524312
  24.8 0.6 %kept_rows.1 = (bf16[8,5120]{1,0:T(8,128)(2,1)S(1)}, f32[8,5120]{1,0:T(8,128)S(1)}) custom-call(f32[64,5120]{1,0:T(8,128)S(1)} %bitcast.9, bf16[1280,128]{1,0:T(8,128)(2,1)S(1)} %get-tuple-element.25.after.a_ref, bf16[1024,256]{1,0:T(8,128)(2,1)S(1)} %copy-done.2, f32[8,5120]{1,0:T(8,128)S(1)} %selected_rows.1.sel_ref, ...), custom_call_target="tpu_custom_call" | custom-call | flops 31457280 | bytes 491520 | tf_op jit(solution)/shard_map/kept_rows/pallas_call | solution.py:81
  25.4 1.9 %collective-permute-start.9 = (bf16[8,5120]{1,0:T(8,128)(2,1)S(1)}, bf16[8,5120]{1,0:T(8,128)(2,1)S(1)}, u32[]{:S(2)}, u32[]{:S(2)}) collective-permute-start(bf16[8,5120]{1,0:T(8,128)(2,1)S(1)} %get-tuple-element.38.own), channel_id=1, source_target_pairs={{0,24},{4,28},{8,16},{12,20},{16,8},{20,12},{24,0},{28,4},{1,25},{... | collective-permute-start | bytes 245768 | tf_op jit(solution)/shard_map/ppermute | solution.py:364
  27.4 1.1 %collective-permute-start.8 = (bf16[8,5120]{1,0:T(8,128)(2,1)S(1)}, bf16[8,5120]{1,0:T(8,128)(2,1)S(1)}, u32[]{:S(2)}, u32[]{:S(2)}) collective-permute-start(bf16[8,5120]{1,0:T(8,128)(2,1)S(1)} %get-tuple-element.38.own), channel_id=1, source_target_pairs={{0,16},{4,20},{8,24},{12,28},{16,0},{20,4},{24,8},{28,12},{1,17},{... | collective-permute-start | bytes 245768 | tf_op jit(solution)/shard_map/ppermute | solution.py:364
  28.5 0.5 %collective-permute-start.7 = (bf16[8,5120]{1,0:T(8,128)(2,1)S(1)}, bf16[8,5120]{1,0:T(8,128)(2,1)S(1)}, u32[]{:S(2)}, u32[]{:S(2)}) collective-permute-start(bf16[8,5120]{1,0:T(8,128)(2,1)S(1)} %get-tuple-element.38.own), channel_id=1, source_target_pairs={{0,8},{4,12},{8,0},{12,4},{16,24},{20,28},{24,16},{28,20},{1,9},{5... | collective-permute-start | bytes 245768 | tf_op jit(solution)/shard_map/ppermute | solution.py:364
  29.0 0.0 collective-permute-start.6
  29.0 0.0 copy-done.1
  29.0 1.0 %input_grads.1.refs_5_ = bf16[128,1280]{1,0:T(8,128)(2,1)} custom-call(bf16[64,5120]{1,0:T(8,128)(2,1)S(1)} %copy-done.1, bf16[8,256,128]{2,1,0:T(8,128)(2,1)S(1)} %bitcast.12, bf16[64,128]{1,0:T(8,128)(2,1)S(1)} %get-tuple-element.27.refs_1_.refs_0_, bf16[144,128]{1,0:T(8,128)(2,1)S(1)} %collective-permute-done.refs_0_.refs_1_, ...), custom_call_target="tpu_custom_call" | custom-call | flops 83886080 | bytes 983040 | tf_op jit(solution)/shard_map/input_grads/pallas_call | solution.py:81
  30.0 1.3 %new_momentums.1 = (f32[64,5120]{1,0:T(8,128)}, f32[2,8,128]{2,1,0:T(8,128)S(1)}) custom-call(f32[64,5120]{1,0:T(8,128)S(1)} %bitcast.10, bf16[64,2560]{1,0:T(8,128)(2,1)S(1)} %get-tuple-element.31.p_ref, f32[8,5120]{1,0:T(8,128)S(1)} %get-tuple-element.33.q, s32[8]{0:T(128)} %mask.1, s32[8]{0:T(128)} %tally.1, f32[64,1280]{1,0:T(8,128)S(1)} %get-tuple-element.32.refs_0_, ...), custom_call_target="tpu_custom_call" | custom-call | flops 125829120 | bytes 3276800 | tf_op jit(solution)/shard_map/new_momentums/pallas_call | solution.py:81
  31.4 0.6 %places.1 = (bf16[64,2560]{1,0:T(8,128)(2,1)S(1)}, bf16[64,2560]{1,0:T(8,128)(2,1)S(1)}, bf16[64,2560]{1,0:T(8,128)(2,1)S(1)}, bf16[64,2560]{1,0:T(8,128)(2,1)S(1)}) custom-call(f32[2,8,128]{2,1,0:T(8,128)S(1)} %get-tuple-element.35.w_ref, bf16[128,256]{1,0:T(8,128)(2,1)S(1)} %get-tuple-element.24.small, bf16[8,256,128]{2,1,0:T(8,128)(2,1)S(1)} %bitcast.13), custom_call_target="tpu_custom_call" | custom-call | tf_op jit(solution)/shard_map/places/pallas_call | solution.py:81
  32.0 0.0 collective-permute-done.9.refs_3_
  32.0 0.9 %collective-permute-done.8.refs_2_ = bf16[8,5120]{1,0:T(8,128)(2,1)S(1)} collective-permute-done((bf16[8,5120]{1,0:T(8,128)(2,1)S(1)}, bf16[8,5120]{1,0:T(8,128)(2,1)S(1)}, u32[]{:S(2)}, u32[]{:S(2)}) %collective-permute-start.8) | collective-permute-done | bytes 81952 | tf_op jit(solution)/shard_map/ppermute | solution.py:364
  32.9 0.0 collective-permute-done.7.refs_1_
  32.9 0.0 collective-permute-done.6.refs_0_.own
  32.9 0.1 collective-permute-start.10
  33.0 0.5 %half_updates.1.half_sum = f32[1280,256]{1,0:T(8,128)S(1)} custom-call(bf16[64,2560]{1,0:T(8,128)(2,1)S(1)} %get-tuple-element.36.refs_6_.p_hi, bf16[64,2560]{1,0:T(8,128)(2,1)S(1)} %get-tuple-element.37.p_lo, bf16[8,5120]{1,0:T(8,128)(2,1)S(1)} %get-tuple-element.38.own, bf16[3,8,5120]{2,1,0:T(8,128)(2,1)S(1)} %join_kept.1.others), custom_call_target="tpu_custom_call" | custom-call | tf_op jit(solution)/shard_map/half_updates/pallas_call | solution.py:81
  33.5 1.0 %collective-permute-done.10.others = bf16[3,8,5120]{2,1,0:T(8,128)(2,1)S(1)} collective-permute-done((bf16[3,8,5120]{2,1,0:T(8,128)(2,1)S(1)}, bf16[3,8,5120]{2,1,0:T(8,128)(2,1)S(1)}, u32[]{:S(2)}, u32[]{:S(2)}) %collective-permute-start.10) | collective-permute-done | bytes 245792 | tf_op jit(solution)/shard_map/ppermute | solution.py:364
  34.5 1.3 %updates.1 = f32[64,5120]{1,0:T(8,128)} custom-call(f32[1280,256]{1,0:T(8,128)S(1)} %half_updates.1.half_sum, bf16[64,2560]{1,0:T(8,128)(2,1)S(1)} %get-tuple-element.39.p_hi, bf16[64,2560]{1,0:T(8,128)(2,1)S(1)} %get-tuple-element.40.p_lo, bf16[8,5120]{1,0:T(8,128)(2,1)S(1)} %collective-permute-done.6.refs_0_.own, ...), custom_call_target="tpu_custom_call" | custom-call | flops 671088640 | bytes 2621440 | tf_op jit(solution)/shard_map/updates/pallas_call | solution.py:81
  (2 shorter events, 0.0 us)
Async XLA Ops:
  1.8 6.5 %collective-permute-start.1 = (bf16[144,128]{1,0:T(8,128)(2,1)S(1)}, bf16[144,128]{1,0:T(8,128)(2,1)S(1)}, u32[]{:S(2)}, u32[]{:S(2)}) collective-permute-start(bf16[144,128]{1,0:T(8,128)(2,1)S(1)} %get-tuple-element.29), channel_id=1, source_target_pairs={{0,2},{1,3},{2,0},{3,1},{4,6},{5,7},{6,4},{7,5},{8,10},{9,11},{10,... | collective-permute-start | bytes 110600 | tf_op jit(solution)/shard_map/ppermute | solution.py:359
  5.9 5.4 %collective-permute-start = (bf16[144,128]{1,0:T(8,128)(2,1)S(1)}, bf16[144,128]{1,0:T(8,128)(2,1)S(1)}, u32[]{:S(2)}, u32[]{:S(2)}) collective-permute-start(bf16[144,128]{1,0:T(8,128)(2,1)S(1)} %get-tuple-element.26), channel_id=1, source_target_pairs={{0,1},{1,0},{2,3},{3,2},{4,5},{5,4},{6,7},{7,6},{8,9},{9,8},{10,11... | collective-permute-start | bytes 110600 | tf_op jit(solution)/shard_map/ppermute | solution.py:359
  7.5 6.2 %collective-permute-start.2 = (bf16[144,128]{1,0:T(8,128)(2,1)S(1)}, bf16[144,128]{1,0:T(8,128)(2,1)S(1)}, u32[]{:S(2)}, u32[]{:S(2)}) collective-permute-start(bf16[144,128]{1,0:T(8,128)(2,1)S(1)} %get-tuple-element.30), channel_id=1, source_target_pairs={{0,3},{1,2},{2,1},{3,0},{4,7},{5,6},{6,5},{7,4},{8,11},{9,10},{10,... | collective-permute-start | bytes 110600 | tf_op jit(solution)/shard_map/ppermute | solution.py:359
  8.5 15.3 %copy-start = (f32[1,64,5120]{2,1,0:T(8,128)S(1)}, f32[1,64,5120]{2,1,0:T(8,128)}, u32[]{:S(2)}) copy-start(f32[1,64,5120]{2,1,0:T(8,128)} %param.14) | copy-start | bytes 3932164
  8.5 15.2 %collective-permute-start.4 = (bf16[64,1280]{1,0:T(8,128)(2,1)S(1)}, bf16[64,1280]{1,0:T(8,128)(2,1)S(1)}, u32[]{:S(2)}, u32[]{:S(2)}) collective-permute-start(bf16[64,1280]{1,0:T(8,128)(2,1)S(1)} %weight_grads.4), channel_id=1, source_target_pairs={{0,2},{1,3},{2,0},{3,1},{4,6},{5,7},{6,4},{7,5},{8,10},{9,11},{10,... | collective-permute-start | bytes 491528 | tf_op jit(solution)/shard_map/ppermute | solution.py:359
  11.5 12.3 %collective-permute-start.3 = (bf16[64,1280]{1,0:T(8,128)(2,1)S(1)}, bf16[64,1280]{1,0:T(8,128)(2,1)S(1)}, u32[]{:S(2)}, u32[]{:S(2)}) collective-permute-start(bf16[64,1280]{1,0:T(8,128)(2,1)S(1)} %get-tuple-element.28.after), channel_id=1, source_target_pairs={{0,1},{1,0},{2,3},{3,2},{4,5},{5,4},{6,7},{7,6},{8,9},{9,8},{10,11... | collective-permute-start | bytes 491528 | tf_op jit(solution)/shard_map/ppermute | solution.py:359
  13.8 10.4 %collective-permute-start.5 = (bf16[64,1280]{1,0:T(8,128)(2,1)S(1)}, bf16[64,1280]{1,0:T(8,128)(2,1)S(1)}, u32[]{:S(2)}, u32[]{:S(2)}) collective-permute-start(bf16[64,1280]{1,0:T(8,128)(2,1)S(1)} %weight_grads.5), channel_id=1, source_target_pairs={{0,3},{1,2},{2,1},{3,0},{4,7},{5,6},{6,5},{7,4},{8,11},{9,10},{10,... | collective-permute-start | bytes 491528 | tf_op jit(solution)/shard_map/ppermute | solution.py:359
  23.8 1.0 %copy-start.2 = (bf16[1024,256]{1,0:T(8,128)(2,1)S(1)}, bf16[1024,256]{1,0:T(8,128)(2,1)}, u32[]{:S(2)}) copy-start(bf16[1024,256]{1,0:T(8,128)(2,1)} %constant.4.clone.tab) | copy-start | bytes 1572868
  24.2 4.8 %copy-start.1 = (bf16[64,5120]{1,0:T(8,128)(2,1)S(1)}, bf16[64,5120]{1,0:T(8,128)(2,1)}, u32[]{:S(2)}) copy-start(bf16[64,5120]{1,0:T(8,128)(2,1)} %exp_ref.3) | copy-start | bytes 1966084
  25.4 6.5 %collective-permute-start.9 = (bf16[8,5120]{1,0:T(8,128)(2,1)S(1)}, bf16[8,5120]{1,0:T(8,128)(2,1)S(1)}, u32[]{:S(2)}, u32[]{:S(2)}) collective-permute-start(bf16[8,5120]{1,0:T(8,128)(2,1)S(1)} %get-tuple-element.38.own), channel_id=1, source_target_pairs={{0,24},{4,28},{8,16},{12,20},{16,8},{20,12},{24,0},{28,4},{1,25},{... | collective-permute-start | bytes 245768 | tf_op jit(solution)/shard_map/ppermute | solution.py:364
  27.4 5.5 %collective-permute-start.8 = (bf16[8,5120]{1,0:T(8,128)(2,1)S(1)}, bf16[8,5120]{1,0:T(8,128)(2,1)S(1)}, u32[]{:S(2)}, u32[]{:S(2)}) collective-permute-start(bf16[8,5120]{1,0:T(8,128)(2,1)S(1)} %get-tuple-element.38.own), channel_id=1, source_target_pairs={{0,16},{4,20},{8,24},{12,28},{16,0},{20,4},{24,8},{28,12},{1,17},{... | collective-permute-start | bytes 245768 | tf_op jit(solution)/shard_map/ppermute | solution.py:364
  28.5 4.4 %collective-permute-start.7 = (bf16[8,5120]{1,0:T(8,128)(2,1)S(1)}, bf16[8,5120]{1,0:T(8,128)(2,1)S(1)}, u32[]{:S(2)}, u32[]{:S(2)}) collective-permute-start(bf16[8,5120]{1,0:T(8,128)(2,1)S(1)} %get-tuple-element.38.own), channel_id=1, source_target_pairs={{0,8},{4,12},{8,0},{12,4},{16,24},{20,28},{24,16},{28,20},{1,9},{5... | collective-permute-start | bytes 245768 | tf_op jit(solution)/shard_map/ppermute | solution.py:364
  29.0 3.9 %collective-permute-start.6 = (bf16[8,5120]{1,0:T(8,128)(2,1)S(1)}, bf16[8,5120]{1,0:T(8,128)(2,1)S(1)}, u32[]{:S(2)}, u32[]{:S(2)}) collective-permute-start(bf16[8,5120]{1,0:T(8,128)(2,1)S(1)} %get-tuple-element.38.own), channel_id=1, source_target_pairs={{0,4},{4,0},{8,12},{12,8},{16,20},{20,16},{24,28},{28,24},{1,5},{5... | collective-permute-start | bytes 245768 | tf_op jit(solution)/shard_map/ppermute | solution.py:364
  32.9 1.6 %collective-permute-start.10 = (bf16[3,8,5120]{2,1,0:T(8,128)(2,1)S(1)}, bf16[3,8,5120]{2,1,0:T(8,128)(2,1)S(1)}, u32[]{:S(2)}, u32[]{:S(2)}) collective-permute-start(bf16[3,8,5120]{2,1,0:T(8,128)(2,1)S(1)} %join_kept.1.others), channel_id=1, source_target_pairs={{0,4},{4,0},{8,12},{12,8},{16,20},{20,16},{24,28},{28,24},{1,5},{5... | collective-permute-start | bytes 737288 | tf_op jit(solution)/shard_map/ppermute | solution.py:364

commit v25 on v20

--- a/solution.py
+++ b/solution.py
@@ -148,7 +148,8 @@
 
 
 def join_body(n, *refs):
-    for i, ref in enumerate(refs[1 : n + 1]):
+    first, *rest, second = refs[1 : n + 1]
+    for i, ref in enumerate([first, second, *rest]):
         refs[-1][i] = ref[...]
 
 
@@ -469,7 +470,7 @@
     others = call(
         functools.partial(join_body, half - 1),
         near((half - 1, keep, width)),
-        (other_own, *ships[1:], far(new), far(input_grad), places[0]),
+        (other_own, ships[1], *ships[3:], ships[2], far(new), far(input_grad), places[0]),
         [ANY] + [VM] * (half - 1) + [ANY] * 3,
         VM,
         name="join_kept",

time: 35.7 us -> 36 us (level)
  no operation moved by 1% of the time
where the time goes in v25:
time: 36 us; the launch traced here: 35.7 us
  starting transfers between devices  14.2 us (39%)
  blocking collectives  9.87 us (27%)
  Pallas kernels  8.26 us (23%)
  waiting for transfers between devices  2.56 us (7%)
  between operations  0.77 us (2%)
    ppermute x6, starting transfers between devices, trade(): return lax.ppermute(x, 'tensor', [(i, i ^ k) for i in range(n_t)])  10.6 us
    all_gather x1, blocking collectives, per_device(): bundles = lax.all_gather(bundle, 'replica', axis=0)  9.87 us
    pallas_call x14, Pallas kernels, call(): pl.pallas_call(body, out_shape=out_shape, in_specs=in_specs, out_specs=ou...  8.26 us
    ppermute x5, starting transfers between devices, swap(): return lax.ppermute(x, 'replica', [(i, i ^ m) for i in range(n_r)])  3.63 us
    ppermute x5, waiting for transfers between devices, swap(): return lax.ppermute(x, 'replica', [(i, i ^ m) for i in range(n_r)])  2.24 us
  transfers between devices with their start and end apart: 11, of which 3 were waited for; matrix products, arithmetic and copies ran while one was open for 0% of the time, Pallas kernels for 15%

profile of v25, /device:TPU:0, one launch (start us, length us, event | category | flops | bytes accessed | tf_op | source)
XLA Modules:
  0.0 35.7 jit_solution(2378968606582111273)
XLA Ops:
  0.6 1.2 %up_grads.1 = (bf16[64,128]{1,0:T(8,128)(2,1)S(1)}, bf16[144,128]{1,0:T(8,128)(2,1)S(1)}, bf16[144,128]{1,0:T(8,128)(2,1)S(1)}, bf16[144,128]{1,0:T(8,128)(2,1)S...) custom-call(bf16[64,128]{1,0:T(8,128)(2,1)} %bitcast.16, ...), custom_call_target="tpu_custom_call" | custom-call | bytes 819200 | tf_op jit(solution)/shard_map/up_grads/pallas_call | solution.py:81
  1.8 4.1 %collective-permute-start.1 = (bf16[144,128]{1,0:T(8,128)(2,1)S(1)}, bf16[144,128]{1,0:T(8,128)(2,1)S(1)}, u32[]{:S(2)}, u32[]{:S(2)}) collective-permute-start(bf16[144,128]{1,0:T(8,128)(2,1)S(1)} %get-tuple-element.31), channel_id=1, source_target_pairs={{0,2},{1,3},{2,0},{3,1},{4,6},{5,7},{6,4},{7,5},{8,10},{9,11},{10,... | collective-permute-start | bytes 110600 | tf_op jit(solution)/shard_map/ppermute | solution.py:349
  5.9 1.6 %collective-permute-start = (bf16[144,128]{1,0:T(8,128)(2,1)S(1)}, bf16[144,128]{1,0:T(8,128)(2,1)S(1)}, u32[]{:S(2)}, u32[]{:S(2)}) collective-permute-start(bf16[144,128]{1,0:T(8,128)(2,1)S(1)} %get-tuple-element.28), channel_id=1, source_target_pairs={{0,1},{1,0},{2,3},{3,2},{4,5},{5,4},{6,7},{7,6},{8,9},{9,8},{10,11... | collective-permute-start | bytes 110600 | tf_op jit(solution)/shard_map/ppermute | solution.py:349
  7.5 0.0 collective-permute-start.2
  7.5 0.5 %own_places.1 = (bf16[64,2560]{1,0:T(8,128)(2,1)S(1)}, bf16[1280,128]{1,0:T(8,128)(2,1)S(1)}) custom-call(s32[8,80]{1,0:T(8,128)S(1)} %get-tuple-element.25.lines, bf16[128,256]{1,0:T(8,128)(2,1)S(1)} %get-tuple-element.26.small), custom_call_target="tpu_custom_call" | custom-call | tf_op jit(solution)/shard_map/own_places/pallas_call | solution.py:81
  8.0 0.3 collective-permute-done.1.refs_1_.refs_2_.refs_0_
  8.3 0.2 weight_grads.5
  8.5 0.0 copy-start
  8.5 0.0 copy-start.2
  8.5 2.7 %collective-permute-start.5 = (bf16[64,1280]{1,0:T(8,128)(2,1)S(1)}, bf16[64,1280]{1,0:T(8,128)(2,1)S(1)}, u32[]{:S(2)}, u32[]{:S(2)}) collective-permute-start(bf16[64,1280]{1,0:T(8,128)(2,1)S(1)} %weight_grads.5), channel_id=1, source_target_pairs={{0,2},{1,3},{2,0},{3,1},{4,6},{5,7},{6,4},{7,5},{8,10},{9,11},{10,... | collective-permute-start | bytes 491528 | tf_op jit(solution)/shard_map/ppermute | solution.py:349
  11.3 0.0 collective-permute-done.refs_0_.refs_1_
  11.3 0.2 weight_grads.3
  11.5 2.1 %collective-permute-start.4 = (bf16[64,1280]{1,0:T(8,128)(2,1)S(1)}, bf16[64,1280]{1,0:T(8,128)(2,1)S(1)}, u32[]{:S(2)}, u32[]{:S(2)}) collective-permute-start(bf16[64,1280]{1,0:T(8,128)(2,1)S(1)} %get-tuple-element.30.after), channel_id=1, source_target_pairs={{0,1},{1,0},{2,3},{3,2},{4,5},{5,4},{6,7},{7,6},{8,9},{9,8},{10,11... | collective-permute-start | bytes 491528 | tf_op jit(solution)/shard_map/ppermute | solution.py:349
  13.6 0.0 collective-permute-done.2.refs_2_.refs_3_.refs_0_
  13.6 0.2 weight_grads.4
  13.8 0.1 collective-permute-start.3
  13.9 9.9 %all-gather = bf16[2048,128]{1,0:T(8,128)(2,1)S(1)} all-gather(bf16[256,128]{1,0:T(8,128)(2,1)S(1)} %bundle.1), channel_id=2, replica_groups=mesh['replica'=8,'tensor'=4] {'replica'}, dimensions={0}, use_global_device_ids=true | all-gather | bytes 589824 | tf_op jit(solution)/shard_map/all_gather | solution.py:413
  23.8 0.0 collective-permute-done.5.refs_2_
  23.8 0.0 collective-permute-done.4.refs_1_
  23.8 0.0 copy-done
  23.8 0.0 copy-done.2
  23.8 0.7 %kept_rows.2 = (bf16[8,5120]{1,0:T(8,128)(2,1)S(1)}, f32[8,5120]{1,0:T(8,128)S(1)}) custom-call(f32[64,5120]{1,0:T(8,128)S(1)} %bitcast.12, bf16[1280,128]{1,0:T(8,128)(2,1)S(1)} %get-tuple-element.27.after.a_ref, bf16[1024,256]{1,0:T(8,128)(2,1)S(1)} %copy-done.2, bf16[8,256,128]{2,1,0:T(8,128)(2,1)S(1)} %bitcast.8, ...), custom_call_target="tpu_custom_call" | custom-call | flops 94371840 | bytes 1474560 | tf_op jit(solution)/shard_map/kept_rows/pallas_call | solution.py:81
  24.5 0.0 collective-permute-done.3.refs_0_.refs_3_
  24.5 0.0 copy-start.1
  24.6 0.5 %kept_rows.3 = (bf16[8,5120]{1,0:T(8,128)(2,1)S(1)}, f32[8,5120]{1,0:T(8,128)S(1)}) custom-call(f32[64,5120]{1,0:T(8,128)S(1)} %bitcast.13, bf16[1280,128]{1,0:T(8,128)(2,1)S(1)} %get-tuple-element.27.after.a_ref, bf16[1024,256]{1,0:T(8,128)(2,1)S(1)} %copy-done.2, bf16[8,256,128]{2,1,0:T(8,128)(2,1)S(1)} %bitcast.9, ...), custom_call_target="tpu_custom_call", output_to_operand_aliasing={{0}: (5, {}), {1}: (6, {})} | custom-call | flops 31457280 | bytes 491520 | tf_op jit(solution)/shard_map/kept_rows/pallas_call | solution.py:81
  25.0 1.6 %collective-permute-start.9 = (bf16[8,5120]{1,0:T(8,128)(2,1)S(1)}, bf16[8,5120]{1,0:T(8,128)(2,1)S(1)}, u32[]{:S(2)}, u32[]{:S(2)}) collective-permute-start(bf16[8,5120]{1,0:T(8,128)(2,1)S(1)} %get-tuple-element.42.own), channel_id=1, source_target_pairs={{0,16},{4,20},{8,24},{12,28},{16,0},{20,4},{24,8},{28,12},{1,17},{... | collective-permute-start | bytes 245768 | tf_op jit(solution)/shard_map/ppermute | solution.py:354
  26.6 1.5 %collective-permute-start.8 = (bf16[8,5120]{1,0:T(8,128)(2,1)S(1)}, bf16[8,5120]{1,0:T(8,128)(2,1)S(1)}, u32[]{:S(2)}, u32[]{:S(2)}) collective-permute-start(bf16[8,5120]{1,0:T(8,128)(2,1)S(1)} %get-tuple-element.42.own), channel_id=1, source_target_pairs={{0,24},{4,28},{8,16},{12,20},{16,8},{20,12},{24,0},{28,4},{1,25},{... | collective-permute-start | bytes 245768 | tf_op jit(solution)/shard_map/ppermute | solution.py:354
  28.1 0.5 %collective-permute-start.7 = (bf16[8,5120]{1,0:T(8,128)(2,1)S(1)}, bf16[8,5120]{1,0:T(8,128)(2,1)S(1)}, u32[]{:S(2)}, u32[]{:S(2)}) collective-permute-start(bf16[8,5120]{1,0:T(8,128)(2,1)S(1)} %get-tuple-element.42.own), channel_id=1, source_target_pairs={{0,8},{4,12},{8,0},{12,4},{16,24},{20,28},{24,16},{28,20},{1,9},{5... | collective-permute-start | bytes 245768 | tf_op jit(solution)/shard_map/ppermute | solution.py:354
  28.6 0.0 collective-permute-start.6
  28.6 0.0 copy-done.1
  28.6 1.0 %input_grads.1.refs_5_ = bf16[128,1280]{1,0:T(8,128)(2,1)} custom-call(bf16[64,5120]{1,0:T(8,128)(2,1)S(1)} %copy-done.1, bf16[8,256,128]{2,1,0:T(8,128)(2,1)S(1)} %bitcast.10, bf16[64,128]{1,0:T(8,128)(2,1)S(1)} %get-tuple-element.29.refs_1_.refs_0_, bf16[144,128]{1,0:T(8,128)(2,1)S(1)} %collective-permute-done.refs_0_.refs_1_, ...), custom_call_target="tpu_custom_call" | custom-call | flops 83886080 | bytes 983040 | tf_op jit(solution)/shard_map/input_grads/pallas_call | solution.py:81
  29.6 1.3 %new_momentums.1 = (f32[64,5120]{1,0:T(8,128)}, f32[2,8,128]{2,1,0:T(8,128)S(1)}) custom-call(f32[64,5120]{1,0:T(8,128)S(1)} %bitcast.14, bf16[64,2560]{1,0:T(8,128)(2,1)S(1)} %get-tuple-element.33.p_ref, f32[8,5120]{1,0:T(8,128)S(1)} %get-tuple-element.37.q, s32[8]{0:T(128)} %mask.1, s32[8]{0:T(128)} %tally.1, f32[64,1280]{1,0:T(8,128)S(1)} %get-tuple-element.34.refs_0_, ...), custom_call_target="tpu_custom_call" | custom-call | flops 125829120 | bytes 3276800 | tf_op jit(solution)/shard_map/new_momentums/pallas_call | solution.py:81
  31.0 0.6 %places.1 = (bf16[64,2560]{1,0:T(8,128)(2,1)S(1)}, bf16[64,2560]{1,0:T(8,128)(2,1)S(1)}, bf16[64,2560]{1,0:T(8,128)(2,1)S(1)}, bf16[64,2560]{1,0:T(8,128)(2,1)S(1)}) custom-call(f32[2,8,128]{2,1,0:T(8,128)S(1)} %get-tuple-element.39.w_ref, bf16[128,256]{1,0:T(8,128)(2,1)S(1)} %get-tuple-element.26.small, bf16[8,256,128]{2,1,0:T(8,128)(2,1)S(1)} %bitcast.11), custom_call_target="tpu_custom_call" | custom-call | tf_op jit(solution)/shard_map/places/pallas_call | solution.py:81
  31.6 0.0 collective-permute-done.9.refs_3_
  31.6 1.2 %collective-permute-done.8.refs_2_ = bf16[8,5120]{1,0:T(8,128)(2,1)S(1)} collective-permute-done((bf16[8,5120]{1,0:T(8,128)(2,1)S(1)}, bf16[8,5120]{1,0:T(8,128)(2,1)S(1)}, u32[]{:S(2)}, u32[]{:S(2)}) %collective-permute-start.8) | collective-permute-done | bytes 81952 | tf_op jit(solution)/shard_map/ppermute | solution.py:354
  32.8 0.0 collective-permute-done.7.refs_1_
  32.8 0.0 collective-permute-done.6.refs_0_.own
  32.8 0.1 collective-permute-start.10
  32.9 0.5 %half_updates.1.half_sum = f32[1280,256]{1,0:T(8,128)S(1)} custom-call(bf16[64,2560]{1,0:T(8,128)(2,1)S(1)} %get-tuple-element.40.refs_6_.p_hi, bf16[64,2560]{1,0:T(8,128)(2,1)S(1)} %get-tuple-element.41.p_lo, bf16[8,5120]{1,0:T(8,128)(2,1)S(1)} %get-tuple-element.42.own, bf16[3,8,5120]{2,1,0:T(8,128)(2,1)S(1)} %join_kept.1.others), custom_call_target="tpu_custom_call" | custom-call | tf_op jit(solution)/shard_map/half_updates/pallas_call | solution.py:81
  33.4 1.0 %collective-permute-done.10.others = bf16[3,8,5120]{2,1,0:T(8,128)(2,1)S(1)} collective-permute-done((bf16[3,8,5120]{2,1,0:T(8,128)(2,1)S(1)}, bf16[3,8,5120]{2,1,0:T(8,128)(2,1)S(1)}, u32[]{:S(2)}, u32[]{:S(2)}) %collective-permute-start.10) | collective-permute-done | bytes 245792 | tf_op jit(solution)/shard_map/ppermute | solution.py:354
  34.4 1.3 %updates.1 = f32[64,5120]{1,0:T(8,128)} custom-call(f32[1280,256]{1,0:T(8,128)S(1)} %half_updates.1.half_sum, bf16[64,2560]{1,0:T(8,128)(2,1)S(1)} %get-tuple-element.43.p_hi, bf16[64,2560]{1,0:T(8,128)(2,1)S(1)} %get-tuple-element.44.p_lo, bf16[8,5120]{1,0:T(8,128)(2,1)S(1)} %collective-permute-done.6.refs_0_.own, ...), custom_call_target="tpu_custom_call" | custom-call | flops 671088640 | bytes 2621440 | tf_op jit(solution)/shard_map/updates/pallas_call | solution.py:81
  (2 shorter events, 0.0 us)
Async XLA Ops:
  1.8 6.5 %collective-permute-start.1 = (bf16[144,128]{1,0:T(8,128)(2,1)S(1)}, bf16[144,128]{1,0:T(8,128)(2,1)S(1)}, u32[]{:S(2)}, u32[]{:S(2)}) collective-permute-start(bf16[144,128]{1,0:T(8,128)(2,1)S(1)} %get-tuple-element.31), channel_id=1, source_target_pairs={{0,2},{1,3},{2,0},{3,1},{4,6},{5,7},{6,4},{7,5},{8,10},{9,11},{10,... | collective-permute-start | bytes 110600 | tf_op jit(solution)/shard_map/ppermute | solution.py:349
  5.9 5.4 %collective-permute-start = (bf16[144,128]{1,0:T(8,128)(2,1)S(1)}, bf16[144,128]{1,0:T(8,128)(2,1)S(1)}, u32[]{:S(2)}, u32[]{:S(2)}) collective-permute-start(bf16[144,128]{1,0:T(8,128)(2,1)S(1)} %get-tuple-element.28), channel_id=1, source_target_pairs={{0,1},{1,0},{2,3},{3,2},{4,5},{5,4},{6,7},{7,6},{8,9},{9,8},{10,11... | collective-permute-start | bytes 110600 | tf_op jit(solution)/shard_map/ppermute | solution.py:349
  7.5 6.2 %collective-permute-start.2 = (bf16[144,128]{1,0:T(8,128)(2,1)S(1)}, bf16[144,128]{1,0:T(8,128)(2,1)S(1)}, u32[]{:S(2)}, u32[]{:S(2)}) collective-permute-start(bf16[144,128]{1,0:T(8,128)(2,1)S(1)} %get-tuple-element.32), channel_id=1, source_target_pairs={{0,3},{1,2},{2,1},{3,0},{4,7},{5,6},{6,5},{7,4},{8,11},{9,10},{10,... | collective-permute-start | bytes 110600 | tf_op jit(solution)/shard_map/ppermute | solution.py:349
  8.5 15.3 %copy-start = (f32[1,64,5120]{2,1,0:T(8,128)S(1)}, f32[1,64,5120]{2,1,0:T(8,128)}, u32[]{:S(2)}) copy-start(f32[1,64,5120]{2,1,0:T(8,128)} %param.14) | copy-start | bytes 3932164
  8.5 15.3 %copy-start.2 = (bf16[1024,256]{1,0:T(8,128)(2,1)S(1)}, bf16[1024,256]{1,0:T(8,128)(2,1)}, u32[]{:S(2)}) copy-start(bf16[1024,256]{1,0:T(8,128)(2,1)} %constant.4.clone.tab) | copy-start | bytes 1572868
  8.5 15.3 %collective-permute-start.5 = (bf16[64,1280]{1,0:T(8,128)(2,1)S(1)}, bf16[64,1280]{1,0:T(8,128)(2,1)S(1)}, u32[]{:S(2)}, u32[]{:S(2)}) collective-permute-start(bf16[64,1280]{1,0:T(8,128)(2,1)S(1)} %weight_grads.5), channel_id=1, source_target_pairs={{0,2},{1,3},{2,0},{3,1},{4,6},{5,7},{6,4},{7,5},{8,10},{9,11},{10,... | collective-permute-start | bytes 491528 | tf_op jit(solution)/shard_map/ppermute | solution.py:349
  11.5 12.3 %collective-permute-start.4 = (bf16[64,1280]{1,0:T(8,128)(2,1)S(1)}, bf16[64,1280]{1,0:T(8,128)(2,1)S(1)}, u32[]{:S(2)}, u32[]{:S(2)}) collective-permute-start(bf16[64,1280]{1,0:T(8,128)(2,1)S(1)} %get-tuple-element.30.after), channel_id=1, source_target_pairs={{0,1},{1,0},{2,3},{3,2},{4,5},{5,4},{6,7},{7,6},{8,9},{9,8},{10,11... | collective-permute-start | bytes 491528 | tf_op jit(solution)/shard_map/ppermute | solution.py:349
  13.8 10.7 %collective-permute-start.3 = (bf16[64,1280]{1,0:T(8,128)(2,1)S(1)}, bf16[64,1280]{1,0:T(8,128)(2,1)S(1)}, u32[]{:S(2)}, u32[]{:S(2)}) collective-permute-start(bf16[64,1280]{1,0:T(8,128)(2,1)S(1)} %weight_grads.4), channel_id=1, source_target_pairs={{0,3},{1,2},{2,1},{3,0},{4,7},{5,6},{6,5},{7,4},{8,11},{9,10},{10,... | collective-permute-start | bytes 491528 | tf_op jit(solution)/shard_map/ppermute | solution.py:349
  24.5 4.1 %copy-start.1 = (bf16[64,5120]{1,0:T(8,128)(2,1)S(1)}, bf16[64,5120]{1,0:T(8,128)(2,1)}, u32[]{:S(2)}) copy-start(bf16[64,5120]{1,0:T(8,128)(2,1)} %exp_ref.3) | copy-start | bytes 1966084
  25.0 6.5 %collective-permute-start.9 = (bf16[8,5120]{1,0:T(8,128)(2,1)S(1)}, bf16[8,5120]{1,0:T(8,128)(2,1)S(1)}, u32[]{:S(2)}, u32[]{:S(2)}) collective-permute-start(bf16[8,5120]{1,0:T(8,128)(2,1)S(1)} %get-tuple-element.42.own), channel_id=1, source_target_pairs={{0,16},{4,20},{8,24},{12,28},{16,0},{20,4},{24,8},{28,12},{1,17},{... | collective-permute-start | bytes 245768 | tf_op jit(solution)/shard_map/ppermute | solution.py:354
  26.6 6.2 %collective-permute-start.8 = (bf16[8,5120]{1,0:T(8,128)(2,1)S(1)}, bf16[8,5120]{1,0:T(8,128)(2,1)S(1)}, u32[]{:S(2)}, u32[]{:S(2)}) collective-permute-start(bf16[8,5120]{1,0:T(8,128)(2,1)S(1)} %get-tuple-element.42.own), channel_id=1, source_target_pairs={{0,24},{4,28},{8,16},{12,20},{16,8},{20,12},{24,0},{28,4},{1,25},{... | collective-permute-start | bytes 245768 | tf_op jit(solution)/shard_map/ppermute | solution.py:354
  28.1 4.7 %collective-permute-start.7 = (bf16[8,5120]{1,0:T(8,128)(2,1)S(1)}, bf16[8,5120]{1,0:T(8,128)(2,1)S(1)}, u32[]{:S(2)}, u32[]{:S(2)}) collective-permute-start(bf16[8,5120]{1,0:T(8,128)(2,1)S(1)} %get-tuple-element.42.own), channel_id=1, source_target_pairs={{0,8},{4,12},{8,0},{12,4},{16,24},{20,28},{24,16},{28,20},{1,9},{5... | collective-permute-start | bytes 245768 | tf_op jit(solution)/shard_map/ppermute | solution.py:354
  28.6 4.2 %collective-permute-start.6 = (bf16[8,5120]{1,0:T(8,128)(2,1)S(1)}, bf16[8,5120]{1,0:T(8,128)(2,1)S(1)}, u32[]{:S(2)}, u32[]{:S(2)}) collective-permute-start(bf16[8,5120]{1,0:T(8,128)(2,1)S(1)} %get-tuple-element.42.own), channel_id=1, source_target_pairs={{0,4},{4,0},{8,12},{12,8},{16,20},{20,16},{24,28},{28,24},{1,5},{5... | collective-permute-start | bytes 245768 | tf_op jit(solution)/shard_map/ppermute | solution.py:354
  32.8 1.6 %collective-permute-start.10 = (bf16[3,8,5120]{2,1,0:T(8,128)(2,1)S(1)}, bf16[3,8,5120]{2,1,0:T(8,128)(2,1)S(1)}, u32[]{:S(2)}, u32[]{:S(2)}) collective-permute-start(bf16[3,8,5120]{2,1,0:T(8,128)(2,1)S(1)} %join_kept.1.others), channel_id=1, source_target_pairs={{0,4},{4,0},{8,12},{12,8},{16,20},{20,16},{24,28},{28,24},{1,5},{5... | collective-permute-start | bytes 737288 | tf_op jit(solution)/shard_map/ppermute | solution.py:354

commit v26 on v20

--- a/solution.py
+++ b/solution.py
@@ -289,8 +289,9 @@
     lane_block = lax.broadcasted_iota(jnp.int32, (half * keep, G), 1) // B
     s = [own[:, cut].astype(F32)] + [ships[i, :, cut].astype(F32) for i in range(half - 1)]
     s = jnp.concatenate(s, axis=0)
+    s = s.astype(BF16)
     w = jnp.concatenate(
-        [jnp.where(lane_block == j, s, 0.0).astype(BF16) for j in range(G // B)], axis=0
+        [s * jnp.where(lane_block == j, 1.0, 0.0).astype(BF16) for j in range(G // B)], axis=0
     )
     cut = slice(g * 2 * B, (g + 1) * 2 * B)
     y = dot(jnp.concatenate([p_hi[:, cut], p_lo[:, cut]], axis=0), w)

time: 35.7 us -> 35.7 us (level)
  no operation moved by 1% of the time
where the time goes in v26:
time: 35.7 us; the launch traced here: 35.4 us
  starting transfers between devices  14.2 us (40%)
  blocking collectives  9.87 us (28%)
  Pallas kernels  8.27 us (23%)
  waiting for transfers between devices  2.26 us (6%)
  between operations  0.77 us (2%)
    ppermute x6, starting transfers between devices, trade(): return lax.ppermute(x, 'tensor', [(i, i ^ k) for i in range(n_t)])  10.6 us
    all_gather x1, blocking collectives, per_device(): bundles = lax.all_gather(bundle, 'replica', axis=0)  9.87 us
    pallas_call x14, Pallas kernels, call(): pl.pallas_call(body, out_shape=out_shape, in_specs=in_specs, out_specs=ou...  8.27 us
    ppermute x5, starting transfers between devices, swap(): return lax.ppermute(x, 'replica', [(i, i ^ m) for i in range(n_r)])  3.63 us
    ppermute x5, waiting for transfers between devices, swap(): return lax.ppermute(x, 'replica', [(i, i ^ m) for i in range(n_r)])  1.94 us
  transfers between devices with their start and end apart: 11, of which 3 were waited for; matrix products, arithmetic and copies ran while one was open for 0% of the time, Pallas kernels for 15%

profile of v26, /device:TPU:0, one launch (start us, length us, event | category | flops | bytes accessed | tf_op | source)
XLA Modules:
  0.0 35.4 jit_solution(9013520992796822624)
XLA Ops:
  0.6 1.2 %up_grads.1 = (bf16[64,128]{1,0:T(8,128)(2,1)S(1)}, bf16[144,128]{1,0:T(8,128)(2,1)S(1)}, bf16[144,128]{1,0:T(8,128)(2,1)S(1)}, bf16[144,128]{1,0:T(8,128)(2,1)S...) custom-call(bf16[64,128]{1,0:T(8,128)(2,1)} %bitcast.16, ...), custom_call_target="tpu_custom_call" | custom-call | bytes 819200 | tf_op jit(solution)/shard_map/up_grads/pallas_call | solution.py:81
  1.8 4.1 %collective-permute-start.1 = (bf16[144,128]{1,0:T(8,128)(2,1)S(1)}, bf16[144,128]{1,0:T(8,128)(2,1)S(1)}, u32[]{:S(2)}, u32[]{:S(2)}) collective-permute-start(bf16[144,128]{1,0:T(8,128)(2,1)S(1)} %get-tuple-element.31), channel_id=1, source_target_pairs={{0,2},{1,3},{2,0},{3,1},{4,6},{5,7},{6,4},{7,5},{8,10},{9,11},{10,... | collective-permute-start | bytes 110600 | tf_op jit(solution)/shard_map/ppermute | solution.py:349
  5.9 1.6 %collective-permute-start = (bf16[144,128]{1,0:T(8,128)(2,1)S(1)}, bf16[144,128]{1,0:T(8,128)(2,1)S(1)}, u32[]{:S(2)}, u32[]{:S(2)}) collective-permute-start(bf16[144,128]{1,0:T(8,128)(2,1)S(1)} %get-tuple-element.28), channel_id=1, source_target_pairs={{0,1},{1,0},{2,3},{3,2},{4,5},{5,4},{6,7},{7,6},{8,9},{9,8},{10,11... | collective-permute-start | bytes 110600 | tf_op jit(solution)/shard_map/ppermute | solution.py:349
  7.5 0.0 collective-permute-start.2
  7.5 0.5 %own_places.1 = (bf16[64,2560]{1,0:T(8,128)(2,1)S(1)}, bf16[1280,128]{1,0:T(8,128)(2,1)S(1)}) custom-call(s32[8,80]{1,0:T(8,128)S(1)} %get-tuple-element.25.lines, bf16[128,256]{1,0:T(8,128)(2,1)S(1)} %get-tuple-element.26.small), custom_call_target="tpu_custom_call" | custom-call | tf_op jit(solution)/shard_map/own_places/pallas_call | solution.py:81
  8.0 0.3 collective-permute-done.1.refs_1_.refs_2_.refs_0_
  8.3 0.2 weight_grads.5
  8.5 0.0 copy-start
  8.5 0.0 copy-start.2
  8.5 2.7 %collective-permute-start.5 = (bf16[64,1280]{1,0:T(8,128)(2,1)S(1)}, bf16[64,1280]{1,0:T(8,128)(2,1)S(1)}, u32[]{:S(2)}, u32[]{:S(2)}) collective-permute-start(bf16[64,1280]{1,0:T(8,128)(2,1)S(1)} %weight_grads.5), channel_id=1, source_target_pairs={{0,2},{1,3},{2,0},{3,1},{4,6},{5,7},{6,4},{7,5},{8,10},{9,11},{10,... | collective-permute-start | bytes 491528 | tf_op jit(solution)/shard_map/ppermute | solution.py:349
  11.3 0.0 collective-permute-done.refs_0_.refs_1_
  11.3 0.2 weight_grads.3
  11.5 2.1 %collective-permute-start.4 = (bf16[64,1280]{1,0:T(8,128)(2,1)S(1)}, bf16[64,1280]{1,0:T(8,128)(2,1)S(1)}, u32[]{:S(2)}, u32[]{:S(2)}) collective-permute-start(bf16[64,1280]{1,0:T(8,128)(2,1)S(1)} %get-tuple-element.30.after), channel_id=1, source_target_pairs={{0,1},{1,0},{2,3},{3,2},{4,5},{5,4},{6,7},{7,6},{8,9},{9,8},{10,11... | collective-permute-start | bytes 491528 | tf_op jit(solution)/shard_map/ppermute | solution.py:349
  13.6 0.0 collective-permute-done.2.refs_2_.refs_3_.refs_0_
  13.6 0.2 weight_grads.4
  13.8 0.1 collective-permute-start.3
  13.9 9.9 %all-gather = bf16[2048,128]{1,0:T(8,128)(2,1)S(1)} all-gather(bf16[256,128]{1,0:T(8,128)(2,1)S(1)} %bundle.1), channel_id=2, replica_groups=mesh['replica'=8,'tensor'=4] {'replica'}, dimensions={0}, use_global_device_ids=true | all-gather | bytes 589824 | tf_op jit(solution)/shard_map/all_gather | solution.py:413
  23.8 0.0 collective-permute-done.5.refs_2_
  23.8 0.0 collective-permute-done.4.refs_1_
  23.8 0.0 copy-done
  23.8 0.0 copy-done.2
  23.8 0.7 %kept_rows.2 = (bf16[8,5120]{1,0:T(8,128)(2,1)S(1)}, f32[8,5120]{1,0:T(8,128)S(1)}) custom-call(f32[64,5120]{1,0:T(8,128)S(1)} %bitcast.12, bf16[1280,128]{1,0:T(8,128)(2,1)S(1)} %get-tuple-element.27.after.a_ref, bf16[1024,256]{1,0:T(8,128)(2,1)S(1)} %copy-done.2, bf16[8,256,128]{2,1,0:T(8,128)(2,1)S(1)} %bitcast.8, ...), custom_call_target="tpu_custom_call" | custom-call | flops 94371840 | bytes 1474560 | tf_op jit(solution)/shard_map/kept_rows/pallas_call | solution.py:81
  24.5 0.0 collective-permute-done.3.refs_0_.refs_3_
  24.5 0.0 copy-start.1
  24.6 0.5 %kept_rows.3 = (bf16[8,5120]{1,0:T(8,128)(2,1)S(1)}, f32[8,5120]{1,0:T(8,128)S(1)}) custom-call(f32[64,5120]{1,0:T(8,128)S(1)} %bitcast.13, bf16[1280,128]{1,0:T(8,128)(2,1)S(1)} %get-tuple-element.27.after.a_ref, bf16[1024,256]{1,0:T(8,128)(2,1)S(1)} %copy-done.2, bf16[8,256,128]{2,1,0:T(8,128)(2,1)S(1)} %bitcast.9, ...), custom_call_target="tpu_custom_call", output_to_operand_aliasing={{0}: (5, {}), {1}: (6, {})} | custom-call | flops 31457280 | bytes 491520 | tf_op jit(solution)/shard_map/kept_rows/pallas_call | solution.py:81
  25.0 1.9 %collective-permute-start.9 = (bf16[8,5120]{1,0:T(8,128)(2,1)S(1)}, bf16[8,5120]{1,0:T(8,128)(2,1)S(1)}, u32[]{:S(2)}, u32[]{:S(2)}) collective-permute-start(bf16[8,5120]{1,0:T(8,128)(2,1)S(1)} %get-tuple-element.42.own), channel_id=1, source_target_pairs={{0,24},{4,28},{8,16},{12,20},{16,8},{20,12},{24,0},{28,4},{1,25},{... | collective-permute-start | bytes 245768 | tf_op jit(solution)/shard_map/ppermute | solution.py:354
  26.9 1.1 %collective-permute-start.8 = (bf16[8,5120]{1,0:T(8,128)(2,1)S(1)}, bf16[8,5120]{1,0:T(8,128)(2,1)S(1)}, u32[]{:S(2)}, u32[]{:S(2)}) collective-permute-start(bf16[8,5120]{1,0:T(8,128)(2,1)S(1)} %get-tuple-element.42.own), channel_id=1, source_target_pairs={{0,16},{4,20},{8,24},{12,28},{16,0},{20,4},{24,8},{28,12},{1,17},{... | collective-permute-start | bytes 245768 | tf_op jit(solution)/shard_map/ppermute | solution.py:354
  28.1 0.5 %collective-permute-start.7 = (bf16[8,5120]{1,0:T(8,128)(2,1)S(1)}, bf16[8,5120]{1,0:T(8,128)(2,1)S(1)}, u32[]{:S(2)}, u32[]{:S(2)}) collective-permute-start(bf16[8,5120]{1,0:T(8,128)(2,1)S(1)} %get-tuple-element.42.own), channel_id=1, source_target_pairs={{0,8},{4,12},{8,0},{12,4},{16,24},{20,28},{24,16},{28,20},{1,9},{5... | collective-permute-start | bytes 245768 | tf_op jit(solution)/shard_map/ppermute | solution.py:354
  28.6 0.0 collective-permute-start.6
  28.6 0.0 copy-done.1
  28.6 1.0 %input_grads.1.refs_5_ = bf16[128,1280]{1,0:T(8,128)(2,1)} custom-call(bf16[64,5120]{1,0:T(8,128)(2,1)S(1)} %copy-done.1, bf16[8,256,128]{2,1,0:T(8,128)(2,1)S(1)} %bitcast.10, bf16[64,128]{1,0:T(8,128)(2,1)S(1)} %get-tuple-element.29.refs_1_.refs_0_, bf16[144,128]{1,0:T(8,128)(2,1)S(1)} %collective-permute-done.refs_0_.refs_1_, ...), custom_call_target="tpu_custom_call" | custom-call | flops 83886080 | bytes 983040 | tf_op jit(solution)/shard_map/input_grads/pallas_call | solution.py:81
  29.6 1.3 %new_momentums.1 = (f32[64,5120]{1,0:T(8,128)}, f32[2,8,128]{2,1,0:T(8,128)S(1)}) custom-call(f32[64,5120]{1,0:T(8,128)S(1)} %bitcast.14, bf16[64,2560]{1,0:T(8,128)(2,1)S(1)} %get-tuple-element.33.p_ref, f32[8,5120]{1,0:T(8,128)S(1)} %get-tuple-element.37.q, s32[8]{0:T(128)} %mask.1, s32[8]{0:T(128)} %tally.1, f32[64,1280]{1,0:T(8,128)S(1)} %get-tuple-element.34.refs_0_, ...), custom_call_target="tpu_custom_call" | custom-call | flops 125829120 | bytes 3276800 | tf_op jit(solution)/shard_map/new_momentums/pallas_call | solution.py:81
  31.0 0.6 %places.1 = (bf16[64,2560]{1,0:T(8,128)(2,1)S(1)}, bf16[64,2560]{1,0:T(8,128)(2,1)S(1)}, bf16[64,2560]{1,0:T(8,128)(2,1)S(1)}, bf16[64,2560]{1,0:T(8,128)(2,1)S(1)}) custom-call(f32[2,8,128]{2,1,0:T(8,128)S(1)} %get-tuple-element.39.w_ref, bf16[128,256]{1,0:T(8,128)(2,1)S(1)} %get-tuple-element.26.small, bf16[8,256,128]{2,1,0:T(8,128)(2,1)S(1)} %bitcast.11), custom_call_target="tpu_custom_call" | custom-call | tf_op jit(solution)/shard_map/places/pallas_call | solution.py:81
  31.6 0.0 collective-permute-done.9.refs_3_
  31.6 0.9 %collective-permute-done.8.refs_2_ = bf16[8,5120]{1,0:T(8,128)(2,1)S(1)} collective-permute-done((bf16[8,5120]{1,0:T(8,128)(2,1)S(1)}, bf16[8,5120]{1,0:T(8,128)(2,1)S(1)}, u32[]{:S(2)}, u32[]{:S(2)}) %collective-permute-start.8) | collective-permute-done | bytes 81952 | tf_op jit(solution)/shard_map/ppermute | solution.py:354
  32.5 0.0 collective-permute-done.7.refs_1_
  32.5 0.0 collective-permute-done.6.refs_0_.own
  32.5 0.1 collective-permute-start.10
  32.6 0.5 %half_updates.1.half_sum = f32[1280,256]{1,0:T(8,128)S(1)} custom-call(bf16[64,2560]{1,0:T(8,128)(2,1)S(1)} %get-tuple-element.40.refs_6_.p_hi, bf16[64,2560]{1,0:T(8,128)(2,1)S(1)} %get-tuple-element.41.p_lo, bf16[8,5120]{1,0:T(8,128)(2,1)S(1)} %get-tuple-element.42.own, bf16[3,8,5120]{2,1,0:T(8,128)(2,1)S(1)} %join_kept.1.others), custom_call_target="tpu_custom_call" | custom-call | tf_op jit(solution)/shard_map/half_updates/pallas_call | solution.py:81
  33.1 1.0 %collective-permute-done.10.others = bf16[3,8,5120]{2,1,0:T(8,128)(2,1)S(1)} collective-permute-done((bf16[3,8,5120]{2,1,0:T(8,128)(2,1)S(1)}, bf16[3,8,5120]{2,1,0:T(8,128)(2,1)S(1)}, u32[]{:S(2)}, u32[]{:S(2)}) %collective-permute-start.10) | collective-permute-done | bytes 245792 | tf_op jit(solution)/shard_map/ppermute | solution.py:354
  34.1 1.3 %updates.1 = f32[64,5120]{1,0:T(8,128)} custom-call(f32[1280,256]{1,0:T(8,128)S(1)} %half_updates.1.half_sum, bf16[64,2560]{1,0:T(8,128)(2,1)S(1)} %get-tuple-element.43.p_hi, bf16[64,2560]{1,0:T(8,128)(2,1)S(1)} %get-tuple-element.44.p_lo, bf16[8,5120]{1,0:T(8,128)(2,1)S(1)} %collective-permute-done.6.refs_0_.own, ...), custom_call_target="tpu_custom_call" | custom-call | flops 671088640 | bytes 2621440 | tf_op jit(solution)/shard_map/updates/pallas_call | solution.py:81
  (2 shorter events, 0.0 us)
Async XLA Ops:
  1.8 6.5 %collective-permute-start.1 = (bf16[144,128]{1,0:T(8,128)(2,1)S(1)}, bf16[144,128]{1,0:T(8,128)(2,1)S(1)}, u32[]{:S(2)}, u32[]{:S(2)}) collective-permute-start(bf16[144,128]{1,0:T(8,128)(2,1)S(1)} %get-tuple-element.31), channel_id=1, source_target_pairs={{0,2},{1,3},{2,0},{3,1},{4,6},{5,7},{6,4},{7,5},{8,10},{9,11},{10,... | collective-permute-start | bytes 110600 | tf_op jit(solution)/shard_map/ppermute | solution.py:349
  5.9 5.4 %collective-permute-start = (bf16[144,128]{1,0:T(8,128)(2,1)S(1)}, bf16[144,128]{1,0:T(8,128)(2,1)S(1)}, u32[]{:S(2)}, u32[]{:S(2)}) collective-permute-start(bf16[144,128]{1,0:T(8,128)(2,1)S(1)} %get-tuple-element.28), channel_id=1, source_target_pairs={{0,1},{1,0},{2,3},{3,2},{4,5},{5,4},{6,7},{7,6},{8,9},{9,8},{10,11... | collective-permute-start | bytes 110600 | tf_op jit(solution)/shard_map/ppermute | solution.py:349
  7.5 6.2 %collective-permute-start.2 = (bf16[144,128]{1,0:T(8,128)(2,1)S(1)}, bf16[144,128]{1,0:T(8,128)(2,1)S(1)}, u32[]{:S(2)}, u32[]{:S(2)}) collective-permute-start(bf16[144,128]{1,0:T(8,128)(2,1)S(1)} %get-tuple-element.32), channel_id=1, source_target_pairs={{0,3},{1,2},{2,1},{3,0},{4,7},{5,6},{6,5},{7,4},{8,11},{9,10},{10,... | collective-permute-start | bytes 110600 | tf_op jit(solution)/shard_map/ppermute | solution.py:349
  8.5 15.3 %copy-start = (f32[1,64,5120]{2,1,0:T(8,128)S(1)}, f32[1,64,5120]{2,1,0:T(8,128)}, u32[]{:S(2)}) copy-start(f32[1,64,5120]{2,1,0:T(8,128)} %param.14) | copy-start | bytes 3932164
  8.5 15.3 %copy-start.2 = (bf16[1024,256]{1,0:T(8,128)(2,1)S(1)}, bf16[1024,256]{1,0:T(8,128)(2,1)}, u32[]{:S(2)}) copy-start(bf16[1024,256]{1,0:T(8,128)(2,1)} %constant.4.clone.tab) | copy-start | bytes 1572868
  8.5 15.3 %collective-permute-start.5 = (bf16[64,1280]{1,0:T(8,128)(2,1)S(1)}, bf16[64,1280]{1,0:T(8,128)(2,1)S(1)}, u32[]{:S(2)}, u32[]{:S(2)}) collective-permute-start(bf16[64,1280]{1,0:T(8,128)(2,1)S(1)} %weight_grads.5), channel_id=1, source_target_pairs={{0,2},{1,3},{2,0},{3,1},{4,6},{5,7},{6,4},{7,5},{8,10},{9,11},{10,... | collective-permute-start | bytes 491528 | tf_op jit(solution)/shard_map/ppermute | solution.py:349
  11.5 12.3 %collective-permute-start.4 = (bf16[64,1280]{1,0:T(8,128)(2,1)S(1)}, bf16[64,1280]{1,0:T(8,128)(2,1)S(1)}, u32[]{:S(2)}, u32[]{:S(2)}) collective-permute-start(bf16[64,1280]{1,0:T(8,128)(2,1)S(1)} %get-tuple-element.30.after), channel_id=1, source_target_pairs={{0,1},{1,0},{2,3},{3,2},{4,5},{5,4},{6,7},{7,6},{8,9},{9,8},{10,11... | collective-permute-start | bytes 491528 | tf_op jit(solution)/shard_map/ppermute | solution.py:349
  13.8 10.7 %collective-permute-start.3 = (bf16[64,1280]{1,0:T(8,128)(2,1)S(1)}, bf16[64,1280]{1,0:T(8,128)(2,1)S(1)}, u32[]{:S(2)}, u32[]{:S(2)}) collective-permute-start(bf16[64,1280]{1,0:T(8,128)(2,1)S(1)} %weight_grads.4), channel_id=1, source_target_pairs={{0,3},{1,2},{2,1},{3,0},{4,7},{5,6},{6,5},{7,4},{8,11},{9,10},{10,... | collective-permute-start | bytes 491528 | tf_op jit(solution)/shard_map/ppermute | solution.py:349
  24.5 4.1 %copy-start.1 = (bf16[64,5120]{1,0:T(8,128)(2,1)S(1)}, bf16[64,5120]{1,0:T(8,128)(2,1)}, u32[]{:S(2)}) copy-start(bf16[64,5120]{1,0:T(8,128)(2,1)} %exp_ref.3) | copy-start | bytes 1966084
  25.0 6.5 %collective-permute-start.9 = (bf16[8,5120]{1,0:T(8,128)(2,1)S(1)}, bf16[8,5120]{1,0:T(8,128)(2,1)S(1)}, u32[]{:S(2)}, u32[]{:S(2)}) collective-permute-start(bf16[8,5120]{1,0:T(8,128)(2,1)S(1)} %get-tuple-element.42.own), channel_id=1, source_target_pairs={{0,24},{4,28},{8,16},{12,20},{16,8},{20,12},{24,0},{28,4},{1,25},{... | collective-permute-start | bytes 245768 | tf_op jit(solution)/shard_map/ppermute | solution.py:354
  26.9 5.5 %collective-permute-start.8 = (bf16[8,5120]{1,0:T(8,128)(2,1)S(1)}, bf16[8,5120]{1,0:T(8,128)(2,1)S(1)}, u32[]{:S(2)}, u32[]{:S(2)}) collective-permute-start(bf16[8,5120]{1,0:T(8,128)(2,1)S(1)} %get-tuple-element.42.own), channel_id=1, source_target_pairs={{0,16},{4,20},{8,24},{12,28},{16,0},{20,4},{24,8},{28,12},{1,17},{... | collective-permute-start | bytes 245768 | tf_op jit(solution)/shard_map/ppermute | solution.py:354
  28.1 4.4 %collective-permute-start.7 = (bf16[8,5120]{1,0:T(8,128)(2,1)S(1)}, bf16[8,5120]{1,0:T(8,128)(2,1)S(1)}, u32[]{:S(2)}, u32[]{:S(2)}) collective-permute-start(bf16[8,5120]{1,0:T(8,128)(2,1)S(1)} %get-tuple-element.42.own), channel_id=1, source_target_pairs={{0,8},{4,12},{8,0},{12,4},{16,24},{20,28},{24,16},{28,20},{1,9},{5... | collective-permute-start | bytes 245768 | tf_op jit(solution)/shard_map/ppermute | solution.py:354
  28.6 3.9 %collective-permute-start.6 = (bf16[8,5120]{1,0:T(8,128)(2,1)S(1)}, bf16[8,5120]{1,0:T(8,128)(2,1)S(1)}, u32[]{:S(2)}, u32[]{:S(2)}) collective-permute-start(bf16[8,5120]{1,0:T(8,128)(2,1)S(1)} %get-tuple-element.42.own), channel_id=1, source_target_pairs={{0,4},{4,0},{8,12},{12,8},{16,20},{20,16},{24,28},{28,24},{1,5},{5... | collective-permute-start | bytes 245768 | tf_op jit(solution)/shard_map/ppermute | solution.py:354
  32.5 1.6 %collective-permute-start.10 = (bf16[3,8,5120]{2,1,0:T(8,128)(2,1)S(1)}, bf16[3,8,5120]{2,1,0:T(8,128)(2,1)S(1)}, u32[]{:S(2)}, u32[]{:S(2)}) collective-permute-start(bf16[3,8,5120]{2,1,0:T(8,128)(2,1)S(1)} %join_kept.1.others), channel_id=1, source_target_pairs={{0,4},{4,0},{8,12},{12,8},{16,20},{20,16},{24,28},{28,24},{1,5},{5... | collective-permute-start | bytes 737288 | tf_op jit(solution)/shard_map/ppermute | solution.py:354

commit v27 on v20

--- a/solution.py
+++ b/solution.py
@@ -483,7 +483,7 @@
         VM,
         name="half_updates",
     )
-    chunk = 2 if groups % 2 == 0 else 1
+    chunk = next(c for c in (4, 2, 1) if groups % c == 0)
     update = call(
         functools.partial(update_body, chunk),
         jax.ShapeDtypeStruct((B, width), F32),

time: 35.7 us -> 35.7 us (level)
  no operation moved by 1% of the time
where the time goes in v27:
time: 35.7 us; the launch traced here: 35.4 us
  starting transfers between devices  14.2 us (40%)
  blocking collectives  9.87 us (28%)
  Pallas kernels  8.26 us (23%)
  waiting for transfers between devices  2.26 us (6%)
  between operations  0.77 us (2%)
    ppermute x6, starting transfers between devices, trade(): return lax.ppermute(x, 'tensor', [(i, i ^ k) for i in range(n_t)])  10.6 us
    all_gather x1, blocking collectives, per_device(): bundles = lax.all_gather(bundle, 'replica', axis=0)  9.87 us
    pallas_call x14, Pallas kernels, call(): pl.pallas_call(body, out_shape=out_shape, in_specs=in_specs, out_specs=ou...  8.26 us
    ppermute x5, starting transfers between devices, swap(): return lax.ppermute(x, 'replica', [(i, i ^ m) for i in range(n_r)])  3.63 us
    ppermute x5, waiting for transfers between devices, swap(): return lax.ppermute(x, 'replica', [(i, i ^ m) for i in range(n_r)])  1.94 us
  transfers between devices with their start and end apart: 11, of which 3 were waited for; matrix products, arithmetic and copies ran while one was open for 0% of the time, Pallas kernels for 15%

profile of v27, /device:TPU:0, one launch (start us, length us, event | category | flops | bytes accessed | tf_op | source)
XLA Modules:
  0.0 35.4 jit_solution(9209860216993417176)
XLA Ops:
  0.6 1.2 %up_grads.1 = (bf16[64,128]{1,0:T(8,128)(2,1)S(1)}, bf16[144,128]{1,0:T(8,128)(2,1)S(1)}, bf16[144,128]{1,0:T(8,128)(2,1)S(1)}, bf16[144,128]{1,0:T(8,128)(2,1)S...) custom-call(bf16[64,128]{1,0:T(8,128)(2,1)} %bitcast.16, ...), custom_call_target="tpu_custom_call" | custom-call | bytes 819200 | tf_op jit(solution)/shard_map/up_grads/pallas_call | solution.py:81
  1.8 4.1 %collective-permute-start.1 = (bf16[144,128]{1,0:T(8,128)(2,1)S(1)}, bf16[144,128]{1,0:T(8,128)(2,1)S(1)}, u32[]{:S(2)}, u32[]{:S(2)}) collective-permute-start(bf16[144,128]{1,0:T(8,128)(2,1)S(1)} %get-tuple-element.31), channel_id=1, source_target_pairs={{0,2},{1,3},{2,0},{3,1},{4,6},{5,7},{6,4},{7,5},{8,10},{9,11},{10,... | collective-permute-start | bytes 110600 | tf_op jit(solution)/shard_map/ppermute | solution.py:348
  5.9 1.6 %collective-permute-start = (bf16[144,128]{1,0:T(8,128)(2,1)S(1)}, bf16[144,128]{1,0:T(8,128)(2,1)S(1)}, u32[]{:S(2)}, u32[]{:S(2)}) collective-permute-start(bf16[144,128]{1,0:T(8,128)(2,1)S(1)} %get-tuple-element.28), channel_id=1, source_target_pairs={{0,1},{1,0},{2,3},{3,2},{4,5},{5,4},{6,7},{7,6},{8,9},{9,8},{10,11... | collective-permute-start | bytes 110600 | tf_op jit(solution)/shard_map/ppermute | solution.py:348
  7.5 0.0 collective-permute-start.2
  7.5 0.5 %own_places.1 = (bf16[64,2560]{1,0:T(8,128)(2,1)S(1)}, bf16[1280,128]{1,0:T(8,128)(2,1)S(1)}) custom-call(s32[8,80]{1,0:T(8,128)S(1)} %get-tuple-element.25.lines, bf16[128,256]{1,0:T(8,128)(2,1)S(1)} %get-tuple-element.26.small), custom_call_target="tpu_custom_call" | custom-call | tf_op jit(solution)/shard_map/own_places/pallas_call | solution.py:81
  8.0 0.3 collective-permute-done.1.refs_1_.refs_2_.refs_0_
  8.3 0.2 weight_grads.5
  8.5 0.0 copy-start
  8.5 0.0 copy-start.2
  8.5 2.7 %collective-permute-start.5 = (bf16[64,1280]{1,0:T(8,128)(2,1)S(1)}, bf16[64,1280]{1,0:T(8,128)(2,1)S(1)}, u32[]{:S(2)}, u32[]{:S(2)}) collective-permute-start(bf16[64,1280]{1,0:T(8,128)(2,1)S(1)} %weight_grads.5), channel_id=1, source_target_pairs={{0,2},{1,3},{2,0},{3,1},{4,6},{5,7},{6,4},{7,5},{8,10},{9,11},{10,... | collective-permute-start | bytes 491528 | tf_op jit(solution)/shard_map/ppermute | solution.py:348
  11.3 0.0 collective-permute-done.refs_0_.refs_1_
  11.3 0.2 weight_grads.3
  11.5 2.1 %collective-permute-start.4 = (bf16[64,1280]{1,0:T(8,128)(2,1)S(1)}, bf16[64,1280]{1,0:T(8,128)(2,1)S(1)}, u32[]{:S(2)}, u32[]{:S(2)}) collective-permute-start(bf16[64,1280]{1,0:T(8,128)(2,1)S(1)} %get-tuple-element.30.after), channel_id=1, source_target_pairs={{0,1},{1,0},{2,3},{3,2},{4,5},{5,4},{6,7},{7,6},{8,9},{9,8},{10,11... | collective-permute-start | bytes 491528 | tf_op jit(solution)/shard_map/ppermute | solution.py:348
  13.6 0.0 collective-permute-done.2.refs_2_.refs_3_.refs_0_
  13.6 0.2 weight_grads.4
  13.8 0.1 collective-permute-start.3
  13.9 9.9 %all-gather = bf16[2048,128]{1,0:T(8,128)(2,1)S(1)} all-gather(bf16[256,128]{1,0:T(8,128)(2,1)S(1)} %bundle.1), channel_id=2, replica_groups=mesh['replica'=8,'tensor'=4] {'replica'}, dimensions={0}, use_global_device_ids=true | all-gather | bytes 589824 | tf_op jit(solution)/shard_map/all_gather | solution.py:412
  23.8 0.0 collective-permute-done.5.refs_2_
  23.8 0.0 collective-permute-done.4.refs_1_
  23.8 0.0 copy-done
  23.8 0.0 copy-done.2
  23.8 0.7 %kept_rows.2 = (bf16[8,5120]{1,0:T(8,128)(2,1)S(1)}, f32[8,5120]{1,0:T(8,128)S(1)}) custom-call(f32[64,5120]{1,0:T(8,128)S(1)} %bitcast.12, bf16[1280,128]{1,0:T(8,128)(2,1)S(1)} %get-tuple-element.27.after.a_ref, bf16[1024,256]{1,0:T(8,128)(2,1)S(1)} %copy-done.2, bf16[8,256,128]{2,1,0:T(8,128)(2,1)S(1)} %bitcast.8, ...), custom_call_target="tpu_custom_call" | custom-call | flops 94371840 | bytes 1474560 | tf_op jit(solution)/shard_map/kept_rows/pallas_call | solution.py:81
  24.5 0.0 collective-permute-done.3.refs_0_.refs_3_
  24.5 0.0 copy-start.1
  24.6 0.5 %kept_rows.3 = (bf16[8,5120]{1,0:T(8,128)(2,1)S(1)}, f32[8,5120]{1,0:T(8,128)S(1)}) custom-call(f32[64,5120]{1,0:T(8,128)S(1)} %bitcast.13, bf16[1280,128]{1,0:T(8,128)(2,1)S(1)} %get-tuple-element.27.after.a_ref, bf16[1024,256]{1,0:T(8,128)(2,1)S(1)} %copy-done.2, bf16[8,256,128]{2,1,0:T(8,128)(2,1)S(1)} %bitcast.9, ...), custom_call_target="tpu_custom_call", output_to_operand_aliasing={{0}: (5, {}), {1}: (6, {})} | custom-call | flops 31457280 | bytes 491520 | tf_op jit(solution)/shard_map/kept_rows/pallas_call | solution.py:81
  25.0 1.9 %collective-permute-start.9 = (bf16[8,5120]{1,0:T(8,128)(2,1)S(1)}, bf16[8,5120]{1,0:T(8,128)(2,1)S(1)}, u32[]{:S(2)}, u32[]{:S(2)}) collective-permute-start(bf16[8,5120]{1,0:T(8,128)(2,1)S(1)} %get-tuple-element.42.own), channel_id=1, source_target_pairs={{0,24},{4,28},{8,16},{12,20},{16,8},{20,12},{24,0},{28,4},{1,25},{... | collective-permute-start | bytes 245768 | tf_op jit(solution)/shard_map/ppermute | solution.py:353
  26.9 1.1 %collective-permute-start.8 = (bf16[8,5120]{1,0:T(8,128)(2,1)S(1)}, bf16[8,5120]{1,0:T(8,128)(2,1)S(1)}, u32[]{:S(2)}, u32[]{:S(2)}) collective-permute-start(bf16[8,5120]{1,0:T(8,128)(2,1)S(1)} %get-tuple-element.42.own), channel_id=1, source_target_pairs={{0,16},{4,20},{8,24},{12,28},{16,0},{20,4},{24,8},{28,12},{1,17},{... | collective-permute-start | bytes 245768 | tf_op jit(solution)/shard_map/ppermute | solution.py:353
  28.1 0.5 %collective-permute-start.7 = (bf16[8,5120]{1,0:T(8,128)(2,1)S(1)}, bf16[8,5120]{1,0:T(8,128)(2,1)S(1)}, u32[]{:S(2)}, u32[]{:S(2)}) collective-permute-start(bf16[8,5120]{1,0:T(8,128)(2,1)S(1)} %get-tuple-element.42.own), channel_id=1, source_target_pairs={{0,8},{4,12},{8,0},{12,4},{16,24},{20,28},{24,16},{28,20},{1,9},{5... | collective-permute-start | bytes 245768 | tf_op jit(solution)/shard_map/ppermute | solution.py:353
  28.6 0.0 collective-permute-start.6
  28.6 0.0 copy-done.1
  28.6 1.0 %input_grads.1.refs_5_ = bf16[128,1280]{1,0:T(8,128)(2,1)} custom-call(bf16[64,5120]{1,0:T(8,128)(2,1)S(1)} %copy-done.1, bf16[8,256,128]{2,1,0:T(8,128)(2,1)S(1)} %bitcast.10, bf16[64,128]{1,0:T(8,128)(2,1)S(1)} %get-tuple-element.29.refs_1_.refs_0_, bf16[144,128]{1,0:T(8,128)(2,1)S(1)} %collective-permute-done.refs_0_.refs_1_, ...), custom_call_target="tpu_custom_call" | custom-call | flops 83886080 | bytes 983040 | tf_op jit(solution)/shard_map/input_grads/pallas_call | solution.py:81
  29.6 1.3 %new_momentums.1 = (f32[64,5120]{1,0:T(8,128)}, f32[2,8,128]{2,1,0:T(8,128)S(1)}) custom-call(f32[64,5120]{1,0:T(8,128)S(1)} %bitcast.14, bf16[64,2560]{1,0:T(8,128)(2,1)S(1)} %get-tuple-element.33.p_ref, f32[8,5120]{1,0:T(8,128)S(1)} %get-tuple-element.37.q, s32[8]{0:T(128)} %mask.1, s32[8]{0:T(128)} %tally.1, f32[64,1280]{1,0:T(8,128)S(1)} %get-tuple-element.34.refs_0_, ...), custom_call_target="tpu_custom_call" | custom-call | flops 125829120 | bytes 3276800 | tf_op jit(solution)/shard_map/new_momentums/pallas_call | solution.py:81
  31.0 0.6 %places.1 = (bf16[64,2560]{1,0:T(8,128)(2,1)S(1)}, bf16[64,2560]{1,0:T(8,128)(2,1)S(1)}, bf16[64,2560]{1,0:T(8,128)(2,1)S(1)}, bf16[64,2560]{1,0:T(8,128)(2,1)S(1)}) custom-call(f32[2,8,128]{2,1,0:T(8,128)S(1)} %get-tuple-element.39.w_ref, bf16[128,256]{1,0:T(8,128)(2,1)S(1)} %get-tuple-element.26.small, bf16[8,256,128]{2,1,0:T(8,128)(2,1)S(1)} %bitcast.11), custom_call_target="tpu_custom_call" | custom-call | tf_op jit(solution)/shard_map/places/pallas_call | solution.py:81
  31.6 0.0 collective-permute-done.9.refs_3_
  31.6 0.9 %collective-permute-done.8.refs_2_ = bf16[8,5120]{1,0:T(8,128)(2,1)S(1)} collective-permute-done((bf16[8,5120]{1,0:T(8,128)(2,1)S(1)}, bf16[8,5120]{1,0:T(8,128)(2,1)S(1)}, u32[]{:S(2)}, u32[]{:S(2)}) %collective-permute-start.8) | collective-permute-done | bytes 81952 | tf_op jit(solution)/shard_map/ppermute | solution.py:353
  32.5 0.0 collective-permute-done.7.refs_1_
  32.5 0.0 collective-permute-done.6.refs_0_.own
  32.5 0.1 collective-permute-start.10
  32.6 0.5 %half_updates.1.half_sum = f32[1280,256]{1,0:T(8,128)S(1)} custom-call(bf16[64,2560]{1,0:T(8,128)(2,1)S(1)} %get-tuple-element.40.refs_6_.p_hi, bf16[64,2560]{1,0:T(8,128)(2,1)S(1)} %get-tuple-element.41.p_lo, bf16[8,5120]{1,0:T(8,128)(2,1)S(1)} %get-tuple-element.42.own, bf16[3,8,5120]{2,1,0:T(8,128)(2,1)S(1)} %join_kept.1.others), custom_call_target="tpu_custom_call" | custom-call | tf_op jit(solution)/shard_map/half_updates/pallas_call | solution.py:81
  33.1 1.0 %collective-permute-done.10.others = bf16[3,8,5120]{2,1,0:T(8,128)(2,1)S(1)} collective-permute-done((bf16[3,8,5120]{2,1,0:T(8,128)(2,1)S(1)}, bf16[3,8,5120]{2,1,0:T(8,128)(2,1)S(1)}, u32[]{:S(2)}, u32[]{:S(2)}) %collective-permute-start.10) | collective-permute-done | bytes 245792 | tf_op jit(solution)/shard_map/ppermute | solution.py:353
  34.1 1.3 %updates.1 = f32[64,5120]{1,0:T(8,128)} custom-call(f32[1280,256]{1,0:T(8,128)S(1)} %half_updates.1.half_sum, bf16[64,2560]{1,0:T(8,128)(2,1)S(1)} %get-tuple-element.43.p_hi, bf16[64,2560]{1,0:T(8,128)(2,1)S(1)} %get-tuple-element.44.p_lo, bf16[8,5120]{1,0:T(8,128)(2,1)S(1)} %collective-permute-done.6.refs_0_.own, ...), custom_call_target="tpu_custom_call" | custom-call | flops 671088640 | bytes 2621440 | tf_op jit(solution)/shard_map/updates/pallas_call | solution.py:81
  (2 shorter events, 0.0 us)
Async XLA Ops:
  1.8 6.5 %collective-permute-start.1 = (bf16[144,128]{1,0:T(8,128)(2,1)S(1)}, bf16[144,128]{1,0:T(8,128)(2,1)S(1)}, u32[]{:S(2)}, u32[]{:S(2)}) collective-permute-start(bf16[144,128]{1,0:T(8,128)(2,1)S(1)} %get-tuple-element.31), channel_id=1, source_target_pairs={{0,2},{1,3},{2,0},{3,1},{4,6},{5,7},{6,4},{7,5},{8,10},{9,11},{10,... | collective-permute-start | bytes 110600 | tf_op jit(solution)/shard_map/ppermute | solution.py:348
  5.9 5.4 %collective-permute-start = (bf16[144,128]{1,0:T(8,128)(2,1)S(1)}, bf16[144,128]{1,0:T(8,128)(2,1)S(1)}, u32[]{:S(2)}, u32[]{:S(2)}) collective-permute-start(bf16[144,128]{1,0:T(8,128)(2,1)S(1)} %get-tuple-element.28), channel_id=1, source_target_pairs={{0,1},{1,0},{2,3},{3,2},{4,5},{5,4},{6,7},{7,6},{8,9},{9,8},{10,11... | collective-permute-start | bytes 110600 | tf_op jit(solution)/shard_map/ppermute | solution.py:348
  7.5 6.2 %collective-permute-start.2 = (bf16[144,128]{1,0:T(8,128)(2,1)S(1)}, bf16[144,128]{1,0:T(8,128)(2,1)S(1)}, u32[]{:S(2)}, u32[]{:S(2)}) collective-permute-start(bf16[144,128]{1,0:T(8,128)(2,1)S(1)} %get-tuple-element.32), channel_id=1, source_target_pairs={{0,3},{1,2},{2,1},{3,0},{4,7},{5,6},{6,5},{7,4},{8,11},{9,10},{10,... | collective-permute-start | bytes 110600 | tf_op jit(solution)/shard_map/ppermute | solution.py:348
  8.5 15.3 %copy-start = (f32[1,64,5120]{2,1,0:T(8,128)S(1)}, f32[1,64,5120]{2,1,0:T(8,128)}, u32[]{:S(2)}) copy-start(f32[1,64,5120]{2,1,0:T(8,128)} %param.14) | copy-start | bytes 3932164
  8.5 15.3 %copy-start.2 = (bf16[1024,256]{1,0:T(8,128)(2,1)S(1)}, bf16[1024,256]{1,0:T(8,128)(2,1)}, u32[]{:S(2)}) copy-start(bf16[1024,256]{1,0:T(8,128)(2,1)} %constant.4.clone.tab) | copy-start | bytes 1572868
  8.5 15.3 %collective-permute-start.5 = (bf16[64,1280]{1,0:T(8,128)(2,1)S(1)}, bf16[64,1280]{1,0:T(8,128)(2,1)S(1)}, u32[]{:S(2)}, u32[]{:S(2)}) collective-permute-start(bf16[64,1280]{1,0:T(8,128)(2,1)S(1)} %weight_grads.5), channel_id=1, source_target_pairs={{0,2},{1,3},{2,0},{3,1},{4,6},{5,7},{6,4},{7,5},{8,10},{9,11},{10,... | collective-permute-start | bytes 491528 | tf_op jit(solution)/shard_map/ppermute | solution.py:348
  11.5 12.3 %collective-permute-start.4 = (bf16[64,1280]{1,0:T(8,128)(2,1)S(1)}, bf16[64,1280]{1,0:T(8,128)(2,1)S(1)}, u32[]{:S(2)}, u32[]{:S(2)}) collective-permute-start(bf16[64,1280]{1,0:T(8,128)(2,1)S(1)} %get-tuple-element.30.after), channel_id=1, source_target_pairs={{0,1},{1,0},{2,3},{3,2},{4,5},{5,4},{6,7},{7,6},{8,9},{9,8},{10,11... | collective-permute-start | bytes 491528 | tf_op jit(solution)/shard_map/ppermute | solution.py:348
  13.8 10.7 %collective-permute-start.3 = (bf16[64,1280]{1,0:T(8,128)(2,1)S(1)}, bf16[64,1280]{1,0:T(8,128)(2,1)S(1)}, u32[]{:S(2)}, u32[]{:S(2)}) collective-permute-start(bf16[64,1280]{1,0:T(8,128)(2,1)S(1)} %weight_grads.4), channel_id=1, source_target_pairs={{0,3},{1,2},{2,1},{3,0},{4,7},{5,6},{6,5},{7,4},{8,11},{9,10},{10,... | collective-permute-start | bytes 491528 | tf_op jit(solution)/shard_map/ppermute | solution.py:348
  24.5 4.1 %copy-start.1 = (bf16[64,5120]{1,0:T(8,128)(2,1)S(1)}, bf16[64,5120]{1,0:T(8,128)(2,1)}, u32[]{:S(2)}) copy-start(bf16[64,5120]{1,0:T(8,128)(2,1)} %exp_ref.3) | copy-start | bytes 1966084
  25.0 6.5 %collective-permute-start.9 = (bf16[8,5120]{1,0:T(8,128)(2,1)S(1)}, bf16[8,5120]{1,0:T(8,128)(2,1)S(1)}, u32[]{:S(2)}, u32[]{:S(2)}) collective-permute-start(bf16[8,5120]{1,0:T(8,128)(2,1)S(1)} %get-tuple-element.42.own), channel_id=1, source_target_pairs={{0,24},{4,28},{8,16},{12,20},{16,8},{20,12},{24,0},{28,4},{1,25},{... | collective-permute-start | bytes 245768 | tf_op jit(solution)/shard_map/ppermute | solution.py:353
  26.9 5.5 %collective-permute-start.8 = (bf16[8,5120]{1,0:T(8,128)(2,1)S(1)}, bf16[8,5120]{1,0:T(8,128)(2,1)S(1)}, u32[]{:S(2)}, u32[]{:S(2)}) collective-permute-start(bf16[8,5120]{1,0:T(8,128)(2,1)S(1)} %get-tuple-element.42.own), channel_id=1, source_target_pairs={{0,16},{4,20},{8,24},{12,28},{16,0},{20,4},{24,8},{28,12},{1,17},{... | collective-permute-start | bytes 245768 | tf_op jit(solution)/shard_map/ppermute | solution.py:353
  28.1 4.4 %collective-permute-start.7 = (bf16[8,5120]{1,0:T(8,128)(2,1)S(1)}, bf16[8,5120]{1,0:T(8,128)(2,1)S(1)}, u32[]{:S(2)}, u32[]{:S(2)}) collective-permute-start(bf16[8,5120]{1,0:T(8,128)(2,1)S(1)} %get-tuple-element.42.own), channel_id=1, source_target_pairs={{0,8},{4,12},{8,0},{12,4},{16,24},{20,28},{24,16},{28,20},{1,9},{5... | collective-permute-start | bytes 245768 | tf_op jit(solution)/shard_map/ppermute | solution.py:353
  28.6 3.9 %collective-permute-start.6 = (bf16[8,5120]{1,0:T(8,128)(2,1)S(1)}, bf16[8,5120]{1,0:T(8,128)(2,1)S(1)}, u32[]{:S(2)}, u32[]{:S(2)}) collective-permute-start(bf16[8,5120]{1,0:T(8,128)(2,1)S(1)} %get-tuple-element.42.own), channel_id=1, source_target_pairs={{0,4},{4,0},{8,12},{12,8},{16,20},{20,16},{24,28},{28,24},{1,5},{5... | collective-permute-start | bytes 245768 | tf_op jit(solution)/shard_map/ppermute | solution.py:353
  32.5 1.6 %collective-permute-start.10 = (bf16[3,8,5120]{2,1,0:T(8,128)(2,1)S(1)}, bf16[3,8,5120]{2,1,0:T(8,128)(2,1)S(1)}, u32[]{:S(2)}, u32[]{:S(2)}) collective-permute-start(bf16[3,8,5120]{2,1,0:T(8,128)(2,1)S(1)} %join_kept.1.others), channel_id=1, source_target_pairs={{0,4},{4,0},{8,12},{12,8},{16,20},{20,16},{24,28},{28,24},{1,5},{5... | collective-permute-start | bytes 737288 | tf_op jit(solution)/shard_map/ppermute | solution.py:353
